TPU v7x, 32 devices: a whole 2x2x4 slice. The times are simulated.
32 devices in a mesh: dp: 4 (over y, x), rows: 8 (over z, core).
Axes of the slice: x: 2, y: 2, z: 4, core: 2. Of those that a mesh axis runs over, the one named last changes fastest.
Arguments:
- events: bfloat16 [16384, 512], P(('dp', 'rows')), may hold values from -6 to 6
- cotangent: bfloat16 [16384, 512], P(('dp', 'rows')), may hold values from -6 to 6
- lengths: int32 [32], P(('dp', 'rows')), may hold values from 128 to 512
- event_slot: int32 [32, 512], P(('dp', 'rows')), may hold values from 0 to 511, as said below
- slot_row: int32 [32, 32, 16], P(('dp', 'rows')), may hold values from 0 to 511, as said below
- slot_count: int32 [32, 32], P(('dp', 'rows')), may hold values from 1 to 16, as said below
- w_in: bfloat16 [512, 2048], replicated, may hold values from -0.25 to 0.25
- w_out: bfloat16 [512, 512], replicated, may hold values from -0.25 to 0.25
- item_table: float32 [16384, 512], P(('dp', 'rows')), may hold values from -6 to 6
- accumulator: float32 [16384], P(('dp', 'rows')), may hold values from 0.5 to 8
Outputs:
- grad_in: float32 [512, 2048], P('rows')
- grad_out: float32 [512, 512], P('rows')
- table_new: float32 [16384, 512], P(('dp', 'rows'))
- accum_new: float32 [16384], P(('dp', 'rows'))
Inputs may be any that keep to these rules, and one draw needn't show every extreme that they name: `event_slot`: slot s of a history belongs to shard s // 16, place s % 16; events only name slots whose place is below that history's slot_count for the shard, and every such slot is named by at least one event of the history. `slot_row`: within one history and shard the used slots name distinct rows; unused slots hold 0. `slot_count`: for one shard drawn from the seed every history uses all 16 slots, and some history uses all 16 slots of the last shard.
All inputs are finite; a program needn't handle non-finite values.
Results may differ from a plain program's by a relative error of at most 0.0081.
Values sent between devices are 32-bit elements; how exact they have to be, the bound alone decides.
No kernel may reach another device: no remote copies, remote signals or barrier semaphores. Data moves between devices by JAX's collectives and lax.ppermute only.
A program may use at most 64 MiB of HBM per device.

v0:
```python
import functools

import jax
import jax.numpy as jnp
from jax import lax
from jax.experimental import pallas as pl
from jax.experimental.pallas import tpu as pltpu
from jax.sharding import PartitionSpec as P

HEADS = 4

norm_eps = 1e-05
adagrad_eps = 1e-10
learning_rate = 0.1

f32, bf16 = jnp.float32, jnp.bfloat16
VMEM_BYTES = 56 * 1024 * 1024
STEP = 256
LANES = 128
ID_ROWS = 8


def dot_nn(a, b):
    return lax.dot_general(a, b, (((1,), (0,)), ((), ())), preferred_element_type=f32)


def dot_nt(a, b):
    return lax.dot_general(a, b, (((1,), (1,)), ((), ())), preferred_element_type=f32)


def dot_tn(a, b):
    return lax.dot_general(a, b, (((0,), (0,)), ((), ())), preferred_element_type=f32)


def standardize(x):
    centered = x - jnp.mean(x, axis=-1, keepdims=True)
    inv = lax.rsqrt(jnp.mean(centered * centered, axis=-1, keepdims=True) + norm_eps)
    return centered * inv, inv


def masked_rows(cot, start, length):
    row = start + lax.broadcasted_iota(jnp.int32, cot.shape, 0)
    return jnp.where(row < length, cot.astype(f32), 0.0)


def owner_order(width, rows, dp):
    chips = rows // 2
    piece = width // (rows * dp)
    at = lax.broadcasted_iota(jnp.int32, (width, 1), 0)
    side, rest = at // (width // 2), at % (width // 2)
    part, rest = rest // (chips * piece), rest % (chips * piece)
    chip, row = rest // piece, rest % piece
    core = lax.rem(lax.axis_index("rows"), 2)
    core = jnp.where(side == 0, core, 1 - core)
    wanted = ((chip * 2 + core) * dp + part) * piece + row
    return jnp.where(lax.broadcasted_iota(jnp.int32, (width, width), 1) == wanted, 1.0, 0.0).astype(bf16)


def forward_kernel(rows_size, dp_size, len_ref, ev_ref, cot_ref, win_ref, wout_ref,
                   keep_ref, send_ref, hid_ref, dsilu_ref, gatt_ref, gpre_ref, normed_t_ref,
                   normed_ref, user_ref, duser_ref, att_ref, mixed_ref, masked_ref):
    tokens, width = ev_ref.shape
    hd = width // HEADS
    length = len_ref[0]
    inv_len = 1.0 / length.astype(f32)
    scale = hd ** -0.5
    steps = tokens // STEP

    for i in range(steps):
        rows = pl.ds(i * STEP, STEP)
        xhat, _ = standardize(ev_ref[rows, :].astype(f32))
        normed_ref[rows, :] = xhat.astype(bf16)
        masked_ref[rows, :] = masked_rows(cot_ref[rows, :], i * STEP, length).astype(bf16)

    def project(i, c):
        rows = pl.ds(i * STEP, STEP)
        pre = dot_nn(normed_ref[rows, :], win_ref[:, c * width:(c + 1) * width])
        sig = 0.5 + 0.5 * jnp.tanh(0.5 * pre)
        hid = pre * sig
        dsilu = sig * (1.0 + (pre - hid))
        if c == 0:
            user_ref[rows, :] = hid.astype(bf16)
            duser_ref[rows, :] = dsilu
        else:
            cols = slice((c - 1) * width, c * width)
            hid_ref[rows, cols] = hid.astype(bf16)
            dsilu_ref[rows, cols] = dsilu.astype(bf16)

    for c in range(4):
        for i in range(steps):
            project(i, c)

    tri = lax.broadcasted_iota(jnp.int32, (STEP, STEP), 0) >= lax.broadcasted_iota(jnp.int32, (STEP, STEP), 1)
    for h in range(HEADS):
        v_cols = slice(h * hd, (h + 1) * hd)
        q_cols = slice(width + h * hd, width + (h + 1) * hd)
        k_cols = slice(2 * width + h * hd, 2 * width + (h + 1) * hd)
        for i in range(steps):
            rows = pl.ds(i * STEP, STEP)
            query = hid_ref[rows, q_cols]
            total = None
            for j in range(i + 1):
                keys = pl.ds(j * STEP, STEP)
                half = dot_nt(query, hid_ref[keys, k_cols]) * (0.5 * scale)
                weights = (half + half * jnp.tanh(half)) * inv_len
                if i == j:
                    weights = jnp.where(tri, weights, 0.0)
                part = dot_nn(weights.astype(bf16), hid_ref[keys, v_cols])
                total = part if total is None else total + part
            att_ref[rows, v_cols] = total

    for i in range(steps):
        rows = pl.ds(i * STEP, STEP)
        ahat, inv = standardize(att_ref[rows, :])
        user = user_ref[rows, :].astype(f32)
        mixed_ref[rows, :] = (ahat * user).astype(bf16)
        grad_mixed = dot_nt(masked_ref[rows, :], wout_ref[...])
        gpre_ref[rows, :] = (grad_mixed * ahat * duser_ref[rows, :]).astype(bf16)
        e = grad_mixed * user
        gatt_ref[rows, :] = (inv * (e - jnp.mean(e, axis=-1, keepdims=True)
                                    - ahat * jnp.mean(e * ahat, axis=-1, keepdims=True))).astype(bf16)

    order = owner_order(width, rows_size, dp_size)
    normed_t_ref[...] = dot_nt(order, normed_ref[...]).astype(bf16)
    mixed_t = dot_nt(order, mixed_ref[...]).astype(bf16)
    half = width // 2
    for ref, start in ((send_ref, half), (keep_ref, 0)):
        ref[:, :width] = dot_nn(mixed_t[start:start + half], masked_ref[...])
        ref[:, width:] = dot_nn(normed_t_ref[start:start + half, :], gpre_ref[...])


def attention_kernel(len_ref, hid_ref, dsilu_ref, gatt_ref, normed_t_ref, keep_ref, send_ref, gpre_ref):
    tokens, width = gatt_ref.shape
    hd = width // HEADS
    inv_len = 1.0 / len_ref[0].astype(f32)
    scale = hd ** -0.5
    steps = tokens // STEP

    tri = lax.broadcasted_iota(jnp.int32, (STEP, STEP), 0) <= lax.broadcasted_iota(jnp.int32, (STEP, STEP), 1)
    for h in range(HEADS):
        v_cols = slice(h * hd, (h + 1) * hd)
        q_cols = slice(width + h * hd, width + (h + 1) * hd)
        k_cols = slice(2 * width + h * hd, 2 * width + (h + 1) * hd)
        grad_q = [None] * steps
        for j in range(steps):
            keys = pl.ds(j * STEP, STEP)
            key, value = hid_ref[keys, k_cols], hid_ref[keys, v_cols]
            grad_k = grad_v = None
            for i in range(j, steps):
                rows = pl.ds(i * STEP, STEP)
                query, gatt = hid_ref[rows, q_cols], gatt_ref[rows, v_cols]
                half = dot_nt(key, query) * (0.5 * scale)
                sig2 = 1.0 + jnp.tanh(half)
                silu = half * sig2
                dsilu = sig2 * ((1.0 + half) + (half - silu))
                weights = silu * inv_len
                gscore = dot_nt(value, gatt) * dsilu * (0.5 * inv_len * scale)
                if i == j:
                    weights = jnp.where(tri, weights, 0.0)
                    gscore = jnp.where(tri, gscore, 0.0)
                weights, gscore = weights.astype(bf16), gscore.astype(bf16)
                pv, pk, pq = dot_nn(weights, gatt), dot_nn(gscore, query), dot_tn(gscore, key)
                grad_v = pv if grad_v is None else grad_v + pv
                grad_k = pk if grad_k is None else grad_k + pk
                grad_q[i] = pq if grad_q[i] is None else grad_q[i] + pq
            gpre_ref[keys, v_cols] = (grad_v * dsilu_ref[keys, v_cols].astype(f32)).astype(bf16)
            gpre_ref[keys, k_cols] = (grad_k * dsilu_ref[keys, k_cols].astype(f32)).astype(bf16)
        for i in range(steps):
            rows = pl.ds(i * STEP, STEP)
            gpre_ref[rows, q_cols] = (grad_q[i] * dsilu_ref[rows, q_cols].astype(f32)).astype(bf16)

    half = width // 2
    for ref, start in ((send_ref, half), (keep_ref, 0)):
        ref[...] = dot_nn(normed_t_ref[start:start + half, :], gpre_ref[...])


def events_kernel(len_ref, ev_ref, cot_ref, win_ref, slot_ref, slot_row_ref, gpre_u_ref, gpre_ref,
                  send_ref, hi_ref, lo_ref, rows_ref):
    tokens, width = ev_ref.shape
    owners, capacity = slot_row_ref.shape
    length = len_ref[0]
    for i in range(tokens // STEP):
        rows = pl.ds(i * STEP, STEP)
        xhat, inv = standardize(ev_ref[rows, :].astype(f32))
        grad_normed = dot_nt(gpre_u_ref[rows, :], win_ref[:, :width]) + dot_nt(gpre_ref[rows, :], win_ref[:, width:])
        grad = masked_rows(cot_ref[rows, :], i * STEP, length) + inv * (
            grad_normed - jnp.mean(grad_normed, axis=-1, keepdims=True)
            - xhat * jnp.mean(grad_normed * xhat, axis=-1, keepdims=True))
        high = grad.astype(bf16)
        hi_ref[rows, :] = high
        lo_ref[rows, :] = (grad - high.astype(f32)).astype(bf16)

    rows_ref[...] = one_hot_rows(slot_ref[...], rows_ref.shape[0], hi_ref, lo_ref)
    me = lax.axis_index(("dp", "rows"))
    lane = lax.broadcasted_iota(jnp.int32, (capacity, LANES), 1)
    place = lax.broadcasted_iota(jnp.int32, (capacity, LANES), 0) + lax.rem(me, LANES // capacity) * capacity
    spread = jnp.where(lane == place, 1.0, 0.0).astype(bf16)
    ids = slot_row_ref[...]
    ids = 16.0 * dot_nn((ids // 16).astype(bf16), spread) + dot_nn((ids % 16).astype(bf16), spread)
    tiles = width // LANES
    for o in range(owners):
        for t in range(tiles):
            send_ref[o, t * capacity:(t + 1) * capacity, :] = rows_ref[o * capacity:(o + 1) * capacity, t * LANES:(t + 1) * LANES]
        send_ref[o, tiles * capacity:, :] = jnp.broadcast_to(ids[o:o + 1, :], (ID_ROWS, LANES))


def one_hot_rows(ids, rows, hi_ref, lo_ref):
    named = lax.broadcasted_iota(jnp.int32, (rows, ids.shape[1]), 0) == ids
    onehot = jnp.where(named, 1.0, 0.0).astype(bf16)
    return dot_nn(onehot, hi_ref[...]) + dot_nn(onehot, lo_ref[...])


def table_kernel(recv_ref, table_ref, accum_ref, table_new_ref, accum_new_ref, rows_ref, hi_ref, lo_ref):
    owners = recv_ref.shape[0]
    rows, width = table_ref.shape
    tiles = width // LANES
    capacity = (recv_ref.shape[1] - ID_ROWS) // tiles
    for o in range(owners):
        for t in range(tiles):
            rows_ref[o * capacity:(o + 1) * capacity, t * LANES:(t + 1) * LANES] = recv_ref[o, t * capacity:(t + 1) * capacity, :]
    group = LANES // capacity
    ids = [sum(recv_ref[o, tiles * capacity:, :] for o in range(g, g + group)) for g in range(0, owners, group)]
    ids = jnp.concatenate(ids, axis=1)[:1, :].astype(jnp.int32)
    high = rows_ref[...].astype(bf16)
    hi_ref[...] = high
    lo_ref[...] = (rows_ref[...] - high.astype(f32)).astype(bf16)
    grad = one_hot_rows(ids, rows, hi_ref, lo_ref)
    accum = jnp.transpose(jnp.broadcast_to(accum_ref[...].reshape(1, rows), (8, rows)))[:, :1]
    accum_new = accum + jnp.mean(grad * grad, axis=-1, keepdims=True)
    accum_new_ref[...] = jnp.transpose(jnp.broadcast_to(accum_new, (rows, LANES)))[:1, :].reshape(rows)
    table_new_ref[...] = table_ref[...] - learning_rate * grad / (jnp.sqrt(accum_new) + adagrad_eps)


def split_first_kernel(keep_ref, recv_ref, send_a_ref, keep_a_ref, send_b_ref, keep_b_ref):
    d = lax.axis_index("dp")
    x, y = lax.rem(d, 2), d // 2
    half = keep_ref.shape[-1] // 2
    lo, hi = slice(0, half), slice(half, 2 * half)
    for s in range(2):
        send_a_ref[s] = keep_ref[s, 1 - x, :, lo] + recv_ref[s, 1 - x, :, lo]
        send_b_ref[s] = keep_ref[1 - y, s, :, hi] + recv_ref[1 - y, s, :, hi]
        keep_a_ref[s] = keep_ref[s, x, :, lo] + recv_ref[s, x, :, lo]
        keep_b_ref[s] = keep_ref[y, s, :, hi] + recv_ref[y, s, :, hi]


def split_second_kernel(keep_a_ref, recv_a_ref, keep_b_ref, recv_b_ref, send_a_ref, next_a_ref, send_b_ref, next_b_ref):
    d = lax.axis_index("dp")
    x, y = lax.rem(d, 2), d // 2
    send_a_ref[...] = keep_a_ref[1 - y] + recv_a_ref[1 - y]
    send_b_ref[...] = keep_b_ref[1 - x] + recv_b_ref[1 - x]
    next_a_ref[...] = keep_a_ref[y] + recv_a_ref[y]
    next_b_ref[...] = keep_b_ref[x] + recv_b_ref[x]


def chips_kernel(keep_a_ref, recv_a_ref, keep_b_ref, recv_b_ref, *out_refs):
    chips = len(out_refs)
    chip = lax.axis_index("rows") // 2
    half = keep_a_ref.shape[-1]
    for k, out_ref in enumerate(out_refs):
        at = lax.rem(chip + k, chips)
        out_ref[:, :half] = keep_a_ref[at] + recv_a_ref[at]
        out_ref[:, half:] = keep_b_ref[at] + recv_b_ref[at]


def total_kernel(tokens, *refs):
    total = refs[0][...]
    for ref in refs[1:-1]:
        total = total + ref[...]
    refs[-1][...] = total * (1.0 / tokens)


def gather_kernel(*refs):
    *pieces, grad_in_ref, grad_out_ref = refs
    dp = len(pieces) // 2
    d = lax.axis_index("dp")
    width = grad_out_ref.shape[-1]
    for k in range(dp):
        at = jnp.bitwise_xor(d, k)
        grad_out_ref[at] = pieces[k][:, :width]
        grad_in_ref[at, :, :width] = pieces[k][:, width:]
        grad_in_ref[at, :, width:] = pieces[dp + k][...]


def vmem():
    return pl.BlockSpec(memory_space=pltpu.VMEM)


def smem():
    return pl.BlockSpec(memory_space=pltpu.SMEM)


def shape(*dims, dtype=f32):
    return jax.ShapeDtypeStruct(dims, dtype)


def call(kernel, name, out_shape, args, scalars=0, scratch=()):
    return pl.pallas_call(
        kernel,
        name=name,
        in_specs=[smem()] * scalars + [vmem()] * (len(args) - scalars),
        out_specs=[vmem()] * len(out_shape),
        out_shape=out_shape,
        scratch_shapes=[pltpu.VMEM(dims, dtype) for dims, dtype in scratch],
        compiler_params=pltpu.CompilerParams(vmem_limit_bytes=VMEM_BYTES),
    )(*args)


def body(rows_size, dp_size, events, cotangent, lengths, event_slot, slot_row, slot_count, w_in, w_out, item_table, accumulator):
    tokens, width = events.shape
    owners, capacity = slot_row.shape[1:]
    chips = rows_size // 2
    piece = width // (rows_size * dp_size)
    flip = lambda bit, size: [(i, i ^ bit) for i in range(size)]
    other_core = lambda v: lax.ppermute(v, "rows", flip(1, rows_size))
    over_dp = lambda v, bit: lax.ppermute(v, "dp", flip(bit, dp_size))
    over_chips = lambda v, k: lax.ppermute(v, "rows", [(i, (i + 2 * k) % rows_size) for i in range(rows_size)])

    def summed(keep, recv):
        cols = keep.shape[1]
        views = [v.reshape(2, 2, chips * piece, cols) for v in (keep, recv)]
        send_a, keep_a, send_b, keep_b = call(
            split_first_kernel, "split_first", [shape(2, chips * piece, cols // 2)] * 4, views)
        recv_a, recv_b = over_dp(send_a, 1), over_dp(send_b, 2)
        send_a, keep_a, send_b, keep_b = call(
            split_second_kernel, "split_second", [shape(chips * piece, cols // 2)] * 4, [keep_a, recv_a, keep_b, recv_b])
        recv_a, recv_b = over_dp(send_a, 2), over_dp(send_b, 1)
        views = [v.reshape(chips, piece, cols // 2) for v in (keep_a, recv_a, keep_b, recv_b)]
        blocks = call(chips_kernel, "by_chip", [shape(piece, cols)] * chips, views)
        blocks = [blocks[0]] + [over_chips(blocks[k], k) for k in range(1, chips)]
        (total,) = call(functools.partial(total_kernel, tokens), "total", [shape(piece, cols)], blocks)
        return [total] + [over_dp(total, k) for k in range(1, dp_size)]

    sides = lambda cols: [shape(width // 2, cols)] * 2
    keep1, send1, hid, dsilu, gatt, gpre_u, normed_t = call(
        functools.partial(forward_kernel, rows_size, dp_size), "forward_part",
        sides(2 * width) + [
            shape(tokens, 3 * width, dtype=bf16),
            shape(tokens, 3 * width, dtype=bf16),
            shape(tokens, width, dtype=bf16),
            shape(tokens, width, dtype=bf16),
            shape(width, tokens, dtype=bf16),
        ],
        (lengths, events, cotangent, w_in, w_out), 1,
        [((tokens, width), bf16), ((tokens, width), bf16), ((tokens, width), f32), ((tokens, width), f32),
         ((tokens, width), bf16), ((tokens, width), bf16)])
    recv1 = other_core(send1)
    keep2, send2, gpre = call(
        attention_kernel, "attention_part", sides(3 * width) + [shape(tokens, 3 * width, dtype=bf16)],
        (lengths, hid, dsilu, gatt, normed_t), 1)
    recv2 = other_core(send2)
    pay_rows = capacity * (width // LANES) + ID_ROWS
    (send,) = call(
        events_kernel, "events_part", [shape(owners, pay_rows, LANES)],
        (lengths, events, cotangent, w_in, event_slot, slot_row[0], gpre_u, gpre), 1,
        [((tokens, width), bf16), ((tokens, width), bf16), ((owners * capacity, width), f32)])
    recv = lax.all_to_all(send, ("dp", "rows"), split_axis=0, concat_axis=0, tiled=True)
    pieces = summed(keep1, recv1) + summed(keep2, recv2)
    grad_in, grad_out = call(
        gather_kernel, "gather", [shape(dp_size, piece, 4 * width), shape(dp_size, piece, width)], pieces)
    slots = owners * capacity
    table_new, accum_new = call(
        table_kernel, "table_part", [shape(*item_table.shape), shape(*accumulator.shape)],
        (recv, item_table, accumulator), 0,
        [((slots, width), f32), ((slots, width), bf16), ((slots, width), bf16)])
    return grad_in.reshape(-1, 4 * width), grad_out.reshape(-1, width), table_new, accum_new


def solution(mesh):
    whole = P(("dp", "rows"))
    in_specs = (whole,) * 6 + (P(), P(), whole, whole)
    out_specs = (P("rows"), P("rows"), whole, whole)
    run = functools.partial(body, mesh.shape["rows"], mesh.shape["dp"])
    return jax.shard_map(run, mesh=mesh, in_specs=in_specs, out_specs=out_specs, check_vma=False)
```

profile of v0, /device:TPU:0, one launch (start us, length us, event | category | flops | bytes accessed | tf_op | source)
XLA Modules:
  0.0 116.1 jit_solution(17326744574369298987)
XLA Ops:
  1.3 9.2 %forward_part.1 = (f32[256,1024]{1,0:T(8,128)}, f32[256,1024]{1,0:T(8,128)}, bf16[512,1536]{1,0:T(8,128)(2,1)}, bf16[512,1536]{1,0:T(8,128)(2,1)}, bf16[512,512]...) custom-call(s32[1]{0:T(128)S(6)} %copy.14.len_ref, bf16[512,512]{1,0:T(8,128)(2,1)} %ev_ref.3, ...), custom_call_target="tpu_custom_call" | custom-call | tf_op jit(solution)/shard_map/forward_part/pallas_call | solution.py:297
  10.5 8.4 %attention_part.1 = (f32[256,1536]{1,0:T(8,128)}, f32[256,1536]{1,0:T(8,128)}, bf16[512,1536]{1,0:T(8,128)(2,1)}) custom-call(s32[1]{0:T(128)S(6)} %copy.14.len_ref, bf16[512,1536]{1,0:T(8,128)(2,1)} %get-tuple-element.56.hid_ref, bf16[512,1536]{1,0:T(8,128)(2,1)} %get-tuple-element.57.dsilu_ref, bf16[512,512]{1,0:T(8,128)(2,1)} %get-tuple-element.58.gatt_ref, ...), custom_call_target="tpu_custom_call" | custom-call | tf_op jit(solution)/shard_map/attention_part/pallas_call | solution.py:297
  19.0 0.5 collective-permute-start.11
  19.4 0.7 copy.13
  20.1 5.7 %events_part.1 = f32[32,72,128]{2,1,0:T(8,128)} custom-call(s32[1]{0:T(128)S(6)} %copy.14.len_ref, bf16[512,512]{1,0:T(8,128)(2,1)} %ev_ref.3, bf16[512,512]{1,0:T(8,128)(2,1)} %cot_ref.3, bf16[512,2048]{1,0:T(8,128)(2,1)} %win_ref.3, s32[1,512]{1,0:T(1,128)} %slot_ref.1, s32[32,16]{1,0:T(8,128)} %bitcast.27, bf16[512,512]{1,0:T(8,128)(2,1)} %get-tuple-element.76.gpre_u_ref, ...), custom_call_target="tpu_custom_call" | custom-call | tf_op jit(solution)/shard_map/events_part/pallas_call | solution.py:297
  25.8 7.2 %all-to-all-start = ((f32[32,72,128]{2,1,0:T(8,128)}), f32[32,72,128]{2,1,0:T(8,128)S(1)}, u32[]{:S(2)}, u32[]{:S(2)}) async-start(f32[32,72,128]{2,1,0:T(8,128)} %events_part.1), calls=%async_computation | async-start | bytes 2359296 | tf_op jit(solution)/shard_map/all_to_all | solution.py:356
  33.0 0.1 collective-permute-start
  33.2 1.1 copy-done.1
  34.3 3.2 %split_first.3 = (f32[2,64,768]{2,1,0:T(8,128)}, f32[2,64,768]{2,1,0:T(8,128)}, f32[2,64,768]{2,1,0:T(8,128)}, f32[2,64,768]{2,1,0:T(8,128)}) custom-call(f32[2,2,64,1536]{3,2,1,0:T(8,128)} %bitcast.15, f32[2,2,64,1536]{3,2,1,0:T(8,128)} %bitcast.16), custom_call_target="tpu_custom_call" | custom-call | tf_op jit(solution)/shard_map/split_first/pallas_call | solution.py:297
  37.5 1.7 %collective-permute-start.12 = (f32[2,64,768]{2,1,0:T(8,128)}, f32[2,64,768]{2,1,0:T(8,128)S(1)}, u32[]{:S(2)}, u32[]{:S(2)}) collective-permute-start(f32[2,64,768]{2,1,0:T(8,128)} %get-tuple-element.63), channel_id=1, source_target_pairs={{0,8},{8,0},{16,24},{24,16},{1,9},{9,1},{17,25},{25,17},{2,10},{10... | collective-permute-start | bytes 1179656 | tf_op jit(solution)/shard_map/ppermute | solution.py:315
  39.2 1.5 %collective-permute-start.13 = (f32[2,64,768]{2,1,0:T(8,128)}, f32[2,64,768]{2,1,0:T(8,128)S(1)}, u32[]{:S(2)}, u32[]{:S(2)}) collective-permute-start(f32[2,64,768]{2,1,0:T(8,128)} %get-tuple-element.65), channel_id=1, source_target_pairs={{0,16},{8,24},{16,0},{24,8},{1,17},{9,25},{17,1},{25,9},{2,18},{10... | collective-permute-start | bytes 1179656 | tf_op jit(solution)/shard_map/ppermute | solution.py:315
  40.6 1.0 copy-done.2
  41.6 2.6 %split_first.2 = (f32[2,64,512]{2,1,0:T(8,128)}, f32[2,64,512]{2,1,0:T(8,128)}, f32[2,64,512]{2,1,0:T(8,128)}, f32[2,64,512]{2,1,0:T(8,128)}) custom-call(f32[2,2,64,1024]{3,2,1,0:T(8,128)} %bitcast.17, f32[2,2,64,1024]{3,2,1,0:T(8,128)} %bitcast.18), custom_call_target="tpu_custom_call" | custom-call | tf_op jit(solution)/shard_map/split_first/pallas_call | solution.py:297
  44.3 0.6 collective-permute-start.1
  44.8 0.3 collective-permute-start.2
  45.2 17.1 %collective-permute-done.1.recv_a_ref = f32[2,64,512]{2,1,0:T(8,128)S(1)} collective-permute-done((f32[2,64,512]{2,1,0:T(8,128)}, f32[2,64,512]{2,1,0:T(8,128)S(1)}, u32[]{:S(2)}, u32[]{:S(2)}) %collective-permute-start.1) | collective-permute-done | bytes 262176 | tf_op jit(solution)/shard_map/ppermute | solution.py:315
  62.2 0.9 collective-permute-done.2.recv_b_ref
  63.1 0.7 copy-done.6
  63.8 2.0 %split_second.2 = (f32[64,512]{1,0:T(8,128)}, f32[64,512]{1,0:T(8,128)}, f32[64,512]{1,0:T(8,128)}, f32[64,512]{1,0:T(8,128)}) custom-call(f32[2,64,512]{2,1,0:T(8,128)} %get-tuple-element.44.keep_a_ref, f32[2,64,512]{2,1,0:T(8,128)} %copy-done.5, f32[2,64,512]{2,1,0:T(8,128)} %get-tuple-element.46.keep_b_ref, f32[2,64,512]{2,1,0:T(8,128)} %copy-done.6), custom_call_target="tpu_custom_call" | custom-call | tf_op jit(solution)/shard_map/split_second/pallas_call | solution.py:297
  65.9 0.0 copy-start.3
  65.9 0.0 copy-start.4
  65.9 0.7 copy-done.3
  66.6 0.1 copy-done.4
  66.7 2.3 %split_second.3 = (f32[64,768]{1,0:T(8,128)}, f32[64,768]{1,0:T(8,128)}, f32[64,768]{1,0:T(8,128)}, f32[64,768]{1,0:T(8,128)}) custom-call(f32[2,64,768]{2,1,0:T(8,128)} %get-tuple-element.62.keep_a_ref, f32[2,64,768]{2,1,0:T(8,128)} %copy-done.3, f32[2,64,768]{2,1,0:T(8,128)} %get-tuple-element.64.keep_b_ref, f32[2,64,768]{2,1,0:T(8,128)} %copy-done.4), custom_call_target="tpu_custom_call" | custom-call | tf_op jit(solution)/shard_map/split_second/pallas_call | solution.py:297
  69.1 1.1 collective-permute-start.14
  70.2 1.0 collective-permute-start.15
  71.2 0.5 collective-permute-start.3
  71.7 1.4 %collective-permute-start.4 = (f32[64,512]{1,0:T(8,128)S(1)}, f32[64,512]{1,0:T(8,128)S(1)}, u32[]{:S(2)}, u32[]{:S(2)}) collective-permute-start(f32[64,512]{1,0:T(8,128)S(1)} %copy-done.24), channel_id=1, source_target_pairs={{0,8},{8,0},{16,24},{24,16},{1,9},{9,1},{17,25},{25,17},{2,10},{10... | collective-permute-start | bytes 393224 | tf_op jit(solution)/shard_map/ppermute | solution.py:315
  73.1 4.9 %collective-permute-done.3 = f32[64,512]{1,0:T(8,128)S(1)} collective-permute-done((f32[64,512]{1,0:T(8,128)S(1)}, f32[64,512]{1,0:T(8,128)S(1)}, u32[]{:S(2)}, u32[]{:S(2)}) %collective-permute-start.3) | collective-permute-done | bytes 131104 | tf_op jit(solution)/shard_map/ppermute | solution.py:315
  78.0 1.2 %collective-permute-done.4 = f32[64,512]{1,0:T(8,128)S(1)} collective-permute-done((f32[64,512]{1,0:T(8,128)S(1)}, f32[64,512]{1,0:T(8,128)S(1)}, u32[]{:S(2)}, u32[]{:S(2)}) %collective-permute-start.4) | collective-permute-done | bytes 131104 | tf_op jit(solution)/shard_map/ppermute | solution.py:315
  79.2 0.7 copy-done.10
  79.9 1.8 %by_chip.2 = (f32[16,1024]{1,0:T(8,128)}, f32[16,1024]{1,0:T(8,128)}, f32[16,1024]{1,0:T(8,128)}, f32[16,1024]{1,0:T(8,128)}) custom-call(f32[4,16,512]{2,1,0:T(8,128)} %bitcast.23, f32[4,16,512]{2,1,0:T(8,128)} %bitcast.25, f32[4,16,512]{2,1,0:T(8,128)} %bitcast.24, f32[4,16,512]{2,1,0:T(8,128)} %bitcast.26), custom_call_target="tpu_custom_call" | custom-call | tf_op jit(solution)/shard_map/by_chip/pallas_call | solution.py:297
  81.7 1.7 %collective-permute-start.5 = (f32[16,1024]{1,0:T(8,128)}, f32[16,1024]{1,0:T(8,128)S(1)}, u32[]{:S(2)}, u32[]{:S(2)}) collective-permute-start(f32[16,1024]{1,0:T(8,128)} %get-tuple-element.53), channel_id=1, source_target_pairs={{0,2},{1,3},{2,4},{3,5},{4,6},{5,7},{6,0},{7,1},{8,10},{9,11},{10,... | collective-permute-start | bytes 196616 | tf_op jit(solution)/shard_map/ppermute | solution.py:316
  83.4 2.3 %collective-permute-start.6 = (f32[16,1024]{1,0:T(8,128)}, f32[16,1024]{1,0:T(8,128)S(1)}, u32[]{:S(2)}, u32[]{:S(2)}) collective-permute-start(f32[16,1024]{1,0:T(8,128)} %get-tuple-element.54), channel_id=1, source_target_pairs={{0,4},{1,5},{2,6},{3,7},{4,0},{5,1},{6,2},{7,3},{8,12},{9,13},{10,... | collective-permute-start | bytes 196616 | tf_op jit(solution)/shard_map/ppermute | solution.py:316
  85.7 1.3 %collective-permute-start.7 = (f32[16,1024]{1,0:T(8,128)}, f32[16,1024]{1,0:T(8,128)S(1)}, u32[]{:S(2)}, u32[]{:S(2)}) collective-permute-start(f32[16,1024]{1,0:T(8,128)} %get-tuple-element.55), channel_id=1, source_target_pairs={{0,6},{1,7},{2,0},{3,1},{4,2},{5,3},{6,4},{7,5},{8,14},{9,15},{10,... | collective-permute-start | bytes 196616 | tf_op jit(solution)/shard_map/ppermute | solution.py:316
  87.0 0.0 collective-permute-done.14
  87.0 0.0 copy-start.8
  87.1 0.7 copy-done.7
  87.7 0.1 copy-done.8
  87.8 2.0 %by_chip.3 = (f32[16,1536]{1,0:T(8,128)}, f32[16,1536]{1,0:T(8,128)}, f32[16,1536]{1,0:T(8,128)}, f32[16,1536]{1,0:T(8,128)}) custom-call(f32[4,16,768]{2,1,0:T(8,128)} %bitcast.19, f32[4,16,768]{2,1,0:T(8,128)} %bitcast.21, f32[4,16,768]{2,1,0:T(8,128)} %bitcast.20, f32[4,16,768]{2,1,0:T(8,128)} %bitcast.22), custom_call_target="tpu_custom_call" | custom-call | tf_op jit(solution)/shard_map/by_chip/pallas_call | solution.py:297
  89.8 0.7 collective-permute-start.16
  90.5 0.6 collective-permute-start.17
  91.1 2.6 %collective-permute-start.18 = (f32[16,1536]{1,0:T(8,128)}, f32[16,1536]{1,0:T(8,128)S(1)}, u32[]{:S(2)}, u32[]{:S(2)}) collective-permute-start(f32[16,1536]{1,0:T(8,128)} %get-tuple-element.73), channel_id=1, source_target_pairs={{0,6},{1,7},{2,0},{3,1},{4,2},{5,3},{6,4},{7,5},{8,14},{9,15},{10,... | collective-permute-start | bytes 294920 | tf_op jit(solution)/shard_map/ppermute | solution.py:316
  93.7 0.6 copy-done.19
  94.3 0.0 copy-done.20
  94.3 1.6 %total.2.refs_0_ = f32[16,1024]{1,0:T(8,128)} custom-call(f32[16,1024]{1,0:T(8,128)} %get-tuple-element.52.refs_0_, f32[16,1024]{1,0:T(8,128)} %copy-done.18, f32[16,1024]{1,0:T(8,128)} %copy-done.19, f32[16,1024]{1,0:T(8,128)} %copy-done.20), custom_call_target="tpu_custom_call" | custom-call | tf_op jit(solution)/shard_map/total/pallas_call | solution.py:297
  95.9 1.4 %collective-permute-start.8 = (f32[16,1024]{1,0:T(8,128)}, f32[16,1024]{1,0:T(8,128)S(1)}, u32[]{:S(2)}, u32[]{:S(2)}) collective-permute-start(f32[16,1024]{1,0:T(8,128)} %total.2.refs_0_), channel_id=1, source_target_pairs={{0,8},{8,0},{16,24},{24,16},{1,9},{9,1},{17,25},{25,17},{2,10},{10... | collective-permute-start | bytes 196616 | tf_op jit(solution)/shard_map/ppermute | solution.py:315
  97.2 2.0 %collective-permute-done.17.refs_2_ = f32[16,1536]{1,0:T(8,128)S(1)} collective-permute-done((f32[16,1536]{1,0:T(8,128)}, f32[16,1536]{1,0:T(8,128)S(1)}, u32[]{:S(2)}, u32[]{:S(2)}) %collective-permute-start.17) | collective-permute-done | bytes 98336 | tf_op jit(solution)/shard_map/ppermute | solution.py:316
  99.2 0.6 copy-done.15
  99.8 0.0 copy-done.16
  99.9 1.7 %total.3.refs_4_ = f32[16,1536]{1,0:T(8,128)} custom-call(f32[16,1536]{1,0:T(8,128)} %get-tuple-element.70.refs_0_, f32[16,1536]{1,0:T(8,128)} %copy-done.14, f32[16,1536]{1,0:T(8,128)} %copy-done.15, f32[16,1536]{1,0:T(8,128)} %copy-done.16), custom_call_target="tpu_custom_call" | custom-call | tf_op jit(solution)/shard_map/total/pallas_call | solution.py:297
  101.6 1.2 %collective-permute-start.19 = (f32[16,1536]{1,0:T(8,128)}, f32[16,1536]{1,0:T(8,128)S(1)}, u32[]{:S(2)}, u32[]{:S(2)}) collective-permute-start(f32[16,1536]{1,0:T(8,128)} %total.3.refs_4_), channel_id=1, source_target_pairs={{0,8},{8,0},{16,24},{24,16},{1,9},{9,1},{17,25},{25,17},{2,10},{10... | collective-permute-start | bytes 294920 | tf_op jit(solution)/shard_map/ppermute | solution.py:315
  102.7 1.5 %collective-permute-start.20 = (f32[16,1536]{1,0:T(8,128)}, f32[16,1536]{1,0:T(8,128)S(1)}, u32[]{:S(2)}, u32[]{:S(2)}) collective-permute-start(f32[16,1536]{1,0:T(8,128)} %total.3.refs_4_), channel_id=1, source_target_pairs={{0,16},{8,24},{16,0},{24,8},{1,17},{9,25},{17,1},{25,9},{2,18},{10... | collective-permute-start | bytes 294920 | tf_op jit(solution)/shard_map/ppermute | solution.py:315
  104.2 0.8 collective-permute-start.21
  105.1 0.7 collective-permute-start.9
  105.8 1.9 %collective-permute-start.10 = (f32[16,1024]{1,0:T(8,128)}, f32[16,1024]{1,0:T(8,128)S(1)}, u32[]{:S(2)}, u32[]{:S(2)}) collective-permute-start(f32[16,1024]{1,0:T(8,128)} %total.2.refs_0_), channel_id=1, source_target_pairs={{0,24},{8,16},{16,8},{24,0},{1,25},{9,17},{17,9},{25,1},{2,26},{10... | collective-permute-start | bytes 196616 | tf_op jit(solution)/shard_map/ppermute | solution.py:315
  107.7 1.1 copy-done
  108.8 4.0 %table_part.1 = (f32[512,512]{1,0:T(8,128)}, f32[512]{0:T(512)}) custom-call(f32[32,72,128]{2,1,0:T(8,128)} %copy-done, f32[512,512]{1,0:T(8,128)} %table_ref.1, f32[512]{0:T(512)} %accum_ref.1), custom_call_target="tpu_custom_call" | custom-call | tf_op jit(solution)/shard_map/table_part/pallas_call | solution.py:297
  112.8 0.6 copy-done.21
  113.4 0.0 copy-done.22
  113.4 0.0 copy-done.11
  113.4 0.0 copy-done.12
  113.4 0.6 copy-done.13
  114.1 2.1 %gather.1 = (f32[4,16,2048]{2,1,0:T(8,128)}, f32[4,16,512]{2,1,0:T(8,128)}) custom-call(f32[16,1024]{1,0:T(8,128)} %total.2.refs_0_, f32[16,1024]{1,0:T(8,128)} %copy-done.17, f32[16,1024]{1,0:T(8,128)} %copy-done.21, f32[16,1024]{1,0:T(8,128)} %copy-done.22, f32[16,1536]{1,0:T(8,128)} %total.3.refs_4_, f32[16,1536]{1,0:T(8,128)} %copy-done.11, ...), custom_call_target="tpu_custom_call" | custom-call | tf_op jit(solution)/shard_map/gather/pallas_call | solution.py:297
  (48 shorter events, 0.1 us)
Async XLA Ops:
  10.5 8.9 %copy-start.23 = (s32[1,32,16]{1,2,0:T(8,128)S(1)}, s32[1,32,16]{1,2,0:T(8,128)}, u32[]{:S(2)}) copy-start(s32[1,32,16]{1,2,0:T(8,128)} %param.14) | copy-start | bytes 6148
  19.0 14.2 %collective-permute-start.11 = (f32[256,1536]{1,0:T(8,128)}, f32[256,1536]{1,0:T(8,128)S(1)}, u32[]{:S(2)}, u32[]{:S(2)}) collective-permute-start(f32[256,1536]{1,0:T(8,128)} %get-tuple-element.61), channel_id=1, source_target_pairs={{0,1},{1,0},{2,3},{3,2},{4,5},{5,4},{6,7},{7,6},{8,9},{9,8},{10,11... | collective-permute-start | bytes 4718600 | tf_op jit(solution)/shard_map/ppermute | solution.py:314
  25.8 81.9 %all-to-all-start = ((f32[32,72,128]{2,1,0:T(8,128)}), f32[32,72,128]{2,1,0:T(8,128)S(1)}, u32[]{:S(2)}, u32[]{:S(2)}) async-start(f32[32,72,128]{2,1,0:T(8,128)} %events_part.1), calls=%async_computation | async-start | bytes 2359296 | tf_op jit(solution)/shard_map/all_to_all | solution.py:356
  33.0 7.6 %collective-permute-start = (f32[256,1024]{1,0:T(8,128)}, f32[256,1024]{1,0:T(8,128)S(1)}, u32[]{:S(2)}, u32[]{:S(2)}) collective-permute-start(f32[256,1024]{1,0:T(8,128)} %get-tuple-element.43), channel_id=1, source_target_pairs={{0,1},{1,0},{2,3},{3,2},{4,5},{5,4},{6,7},{7,6},{8,9},{9,8},{10,11... | collective-permute-start | bytes 3145736 | tf_op jit(solution)/shard_map/ppermute | solution.py:314
  33.1 1.1 copy-start.1
  37.5 28.4 %collective-permute-start.12 = (f32[2,64,768]{2,1,0:T(8,128)}, f32[2,64,768]{2,1,0:T(8,128)S(1)}, u32[]{:S(2)}, u32[]{:S(2)}) collective-permute-start(f32[2,64,768]{2,1,0:T(8,128)} %get-tuple-element.63), channel_id=1, source_target_pairs={{0,8},{8,0},{16,24},{24,16},{1,9},{9,1},{17,25},{25,17},{2,10},{10... | collective-permute-start | bytes 1179656 | tf_op jit(solution)/shard_map/ppermute | solution.py:315
  39.2 26.7 %collective-permute-start.13 = (f32[2,64,768]{2,1,0:T(8,128)}, f32[2,64,768]{2,1,0:T(8,128)S(1)}, u32[]{:S(2)}, u32[]{:S(2)}) collective-permute-start(f32[2,64,768]{2,1,0:T(8,128)} %get-tuple-element.65), channel_id=1, source_target_pairs={{0,16},{8,24},{16,0},{24,8},{1,17},{9,25},{17,1},{25,9},{2,18},{10... | collective-permute-start | bytes 1179656 | tf_op jit(solution)/shard_map/ppermute | solution.py:315
  40.6 1.0 copy-start.2
  44.3 18.0 %collective-permute-start.1 = (f32[2,64,512]{2,1,0:T(8,128)}, f32[2,64,512]{2,1,0:T(8,128)S(1)}, u32[]{:S(2)}, u32[]{:S(2)}) collective-permute-start(f32[2,64,512]{2,1,0:T(8,128)} %get-tuple-element.45), channel_id=1, source_target_pairs={{0,8},{8,0},{16,24},{24,16},{1,9},{9,1},{17,25},{25,17},{2,10},{10... | collective-permute-start | bytes 786440 | tf_op jit(solution)/shard_map/ppermute | solution.py:315
  44.8 18.3 %collective-permute-start.2 = (f32[2,64,512]{2,1,0:T(8,128)}, f32[2,64,512]{2,1,0:T(8,128)S(1)}, u32[]{:S(2)}, u32[]{:S(2)}) collective-permute-start(f32[2,64,512]{2,1,0:T(8,128)} %get-tuple-element.47), channel_id=1, source_target_pairs={{0,16},{8,24},{16,0},{24,8},{1,17},{9,25},{17,1},{25,9},{2,18},{10... | collective-permute-start | bytes 786440 | tf_op jit(solution)/shard_map/ppermute | solution.py:315
  62.2 0.9 copy-start.5
  63.1 0.7 copy-start.6
  65.8 5.3 %copy-start.25 = (f32[64,512]{1,0:T(8,128)S(1)}, f32[64,512]{1,0:T(8,128)}, u32[]{:S(2)}) copy-start(f32[64,512]{1,0:T(8,128)} %get-tuple-element.49) | copy-start | bytes 393220
  65.8 5.9 %copy-start.24 = (f32[64,512]{1,0:T(8,128)S(1)}, f32[64,512]{1,0:T(8,128)}, u32[]{:S(2)}) copy-start(f32[64,512]{1,0:T(8,128)} %get-tuple-element.51) | copy-start | bytes 393220
  65.9 0.7 copy-start.3
  65.9 0.9 copy-start.4
  69.1 18.0 %collective-permute-start.14 = (f32[64,768]{1,0:T(8,128)}, f32[64,768]{1,0:T(8,128)S(1)}, u32[]{:S(2)}, u32[]{:S(2)}) collective-permute-start(f32[64,768]{1,0:T(8,128)} %get-tuple-element.67), channel_id=1, source_target_pairs={{0,16},{8,24},{16,0},{24,8},{1,17},{9,25},{17,1},{25,9},{2,18},{10... | collective-permute-start | bytes 589832 | tf_op jit(solution)/shard_map/ppermute | solution.py:315
  70.2 16.8 %collective-permute-start.15 = (f32[64,768]{1,0:T(8,128)}, f32[64,768]{1,0:T(8,128)S(1)}, u32[]{:S(2)}, u32[]{:S(2)}) collective-permute-start(f32[64,768]{1,0:T(8,128)} %get-tuple-element.69), channel_id=1, source_target_pairs={{0,8},{8,0},{16,24},{24,16},{1,9},{9,1},{17,25},{25,17},{2,10},{10... | collective-permute-start | bytes 589832 | tf_op jit(solution)/shard_map/ppermute | solution.py:315
  71.2 6.8 %collective-permute-start.3 = (f32[64,512]{1,0:T(8,128)S(1)}, f32[64,512]{1,0:T(8,128)S(1)}, u32[]{:S(2)}, u32[]{:S(2)}) collective-permute-start(f32[64,512]{1,0:T(8,128)S(1)} %copy-done.25), channel_id=1, source_target_pairs={{0,16},{8,24},{16,0},{24,8},{1,17},{9,25},{17,1},{25,9},{2,18},{10... | collective-permute-start | bytes 393224 | tf_op jit(solution)/shard_map/ppermute | solution.py:315
  71.7 7.5 %collective-permute-start.4 = (f32[64,512]{1,0:T(8,128)S(1)}, f32[64,512]{1,0:T(8,128)S(1)}, u32[]{:S(2)}, u32[]{:S(2)}) collective-permute-start(f32[64,512]{1,0:T(8,128)S(1)} %copy-done.24), channel_id=1, source_target_pairs={{0,8},{8,0},{16,24},{24,16},{1,9},{9,1},{17,25},{25,17},{2,10},{10... | collective-permute-start | bytes 393224 | tf_op jit(solution)/shard_map/ppermute | solution.py:315
  78.0 1.2 %copy-start.9 = (f32[64,512]{1,0:T(8,128)}, f32[64,512]{1,0:T(8,128)S(1)}, u32[]{:S(2)}) copy-start(f32[64,512]{1,0:T(8,128)S(1)} %collective-permute-done.3) | copy-start | bytes 393220
  79.2 0.7 copy-start.10
  81.7 9.4 %collective-permute-start.5 = (f32[16,1024]{1,0:T(8,128)}, f32[16,1024]{1,0:T(8,128)S(1)}, u32[]{:S(2)}, u32[]{:S(2)}) collective-permute-start(f32[16,1024]{1,0:T(8,128)} %get-tuple-element.53), channel_id=1, source_target_pairs={{0,2},{1,3},{2,4},{3,5},{4,6},{5,7},{6,0},{7,1},{8,10},{9,11},{10,... | collective-permute-start | bytes 196616 | tf_op jit(solution)/shard_map/ppermute | solution.py:316
  83.4 10.3 %collective-permute-start.6 = (f32[16,1024]{1,0:T(8,128)}, f32[16,1024]{1,0:T(8,128)S(1)}, u32[]{:S(2)}, u32[]{:S(2)}) collective-permute-start(f32[16,1024]{1,0:T(8,128)} %get-tuple-element.54), channel_id=1, source_target_pairs={{0,4},{1,5},{2,6},{3,7},{4,0},{5,1},{6,2},{7,3},{8,12},{9,13},{10,... | collective-permute-start | bytes 196616 | tf_op jit(solution)/shard_map/ppermute | solution.py:316
  85.7 7.9 %collective-permute-start.7 = (f32[16,1024]{1,0:T(8,128)}, f32[16,1024]{1,0:T(8,128)S(1)}, u32[]{:S(2)}, u32[]{:S(2)}) collective-permute-start(f32[16,1024]{1,0:T(8,128)} %get-tuple-element.55), channel_id=1, source_target_pairs={{0,6},{1,7},{2,0},{3,1},{4,2},{5,3},{6,4},{7,5},{8,14},{9,15},{10,... | collective-permute-start | bytes 196616 | tf_op jit(solution)/shard_map/ppermute | solution.py:316
  87.0 0.7 copy-start.7
  87.0 0.7 copy-start.8
  89.8 7.5 %collective-permute-start.16 = (f32[16,1536]{1,0:T(8,128)}, f32[16,1536]{1,0:T(8,128)S(1)}, u32[]{:S(2)}, u32[]{:S(2)}) collective-permute-start(f32[16,1536]{1,0:T(8,128)} %get-tuple-element.71), channel_id=1, source_target_pairs={{0,2},{1,3},{2,4},{3,5},{4,6},{5,7},{6,0},{7,1},{8,10},{9,11},{10,... | collective-permute-start | bytes 294920 | tf_op jit(solution)/shard_map/ppermute | solution.py:316
  90.5 8.7 %collective-permute-start.17 = (f32[16,1536]{1,0:T(8,128)}, f32[16,1536]{1,0:T(8,128)S(1)}, u32[]{:S(2)}, u32[]{:S(2)}) collective-permute-start(f32[16,1536]{1,0:T(8,128)} %get-tuple-element.72), channel_id=1, source_target_pairs={{0,4},{1,5},{2,6},{3,7},{4,0},{5,1},{6,2},{7,3},{8,12},{9,13},{10,... | collective-permute-start | bytes 294920 | tf_op jit(solution)/shard_map/ppermute | solution.py:316
  91.1 2.6 %copy-start.18 = (f32[16,1024]{1,0:T(8,128)}, f32[16,1024]{1,0:T(8,128)S(1)}, u32[]{:S(2)}) copy-start(f32[16,1024]{1,0:T(8,128)S(1)} %collective-permute-done.5.refs_1_) | copy-start | bytes 196612
  91.1 8.2 %collective-permute-start.18 = (f32[16,1536]{1,0:T(8,128)}, f32[16,1536]{1,0:T(8,128)S(1)}, u32[]{:S(2)}, u32[]{:S(2)}) collective-permute-start(f32[16,1536]{1,0:T(8,128)} %get-tuple-element.73), channel_id=1, source_target_pairs={{0,6},{1,7},{2,0},{3,1},{4,2},{5,3},{6,4},{7,5},{8,14},{9,15},{10,... | collective-permute-start | bytes 294920 | tf_op jit(solution)/shard_map/ppermute | solution.py:316
  93.7 0.6 copy-start.19
  93.7 0.6 copy-start.20
  95.9 9.9 %collective-permute-start.8 = (f32[16,1024]{1,0:T(8,128)}, f32[16,1024]{1,0:T(8,128)S(1)}, u32[]{:S(2)}, u32[]{:S(2)}) collective-permute-start(f32[16,1024]{1,0:T(8,128)} %total.2.refs_0_), channel_id=1, source_target_pairs={{0,8},{8,0},{16,24},{24,16},{1,9},{9,1},{17,25},{25,17},{2,10},{10... | collective-permute-start | bytes 196616 | tf_op jit(solution)/shard_map/ppermute | solution.py:315
  97.2 2.0 %copy-start.14 = (f32[16,1536]{1,0:T(8,128)}, f32[16,1536]{1,0:T(8,128)S(1)}, u32[]{:S(2)}) copy-start(f32[16,1536]{1,0:T(8,128)S(1)} %collective-permute-done.16.refs_1_) | copy-start | bytes 294916
  99.2 0.6 copy-start.15
  99.2 0.7 copy-start.16
  101.6 11.2 %collective-permute-start.19 = (f32[16,1536]{1,0:T(8,128)}, f32[16,1536]{1,0:T(8,128)S(1)}, u32[]{:S(2)}, u32[]{:S(2)}) collective-permute-start(f32[16,1536]{1,0:T(8,128)} %total.3.refs_4_), channel_id=1, source_target_pairs={{0,8},{8,0},{16,24},{24,16},{1,9},{9,1},{17,25},{25,17},{2,10},{10... | collective-permute-start | bytes 294920 | tf_op jit(solution)/shard_map/ppermute | solution.py:315
  102.7 10.0 %collective-permute-start.20 = (f32[16,1536]{1,0:T(8,128)}, f32[16,1536]{1,0:T(8,128)S(1)}, u32[]{:S(2)}, u32[]{:S(2)}) collective-permute-start(f32[16,1536]{1,0:T(8,128)} %total.3.refs_4_), channel_id=1, source_target_pairs={{0,16},{8,24},{16,0},{24,8},{1,17},{9,25},{17,1},{25,9},{2,18},{10... | collective-permute-start | bytes 294920 | tf_op jit(solution)/shard_map/ppermute | solution.py:315
  104.2 8.5 %collective-permute-start.21 = (f32[16,1536]{1,0:T(8,128)}, f32[16,1536]{1,0:T(8,128)S(1)}, u32[]{:S(2)}, u32[]{:S(2)}) collective-permute-start(f32[16,1536]{1,0:T(8,128)} %total.3.refs_4_), channel_id=1, source_target_pairs={{0,24},{8,16},{16,8},{24,0},{1,25},{9,17},{17,9},{25,1},{2,26},{10... | collective-permute-start | bytes 294920 | tf_op jit(solution)/shard_map/ppermute | solution.py:315
  105.1 7.7 %collective-permute-start.9 = (f32[16,1024]{1,0:T(8,128)}, f32[16,1024]{1,0:T(8,128)S(1)}, u32[]{:S(2)}, u32[]{:S(2)}) collective-permute-start(f32[16,1024]{1,0:T(8,128)} %total.2.refs_0_), channel_id=1, source_target_pairs={{0,16},{8,24},{16,0},{24,8},{1,17},{9,25},{17,1},{25,9},{2,18},{10... | collective-permute-start | bytes 196616 | tf_op jit(solution)/shard_map/ppermute | solution.py:315
  105.8 7.0 %copy-start.17 = (f32[16,1024]{1,0:T(8,128)}, f32[16,1024]{1,0:T(8,128)S(1)}, u32[]{:S(2)}) copy-start(f32[16,1024]{1,0:T(8,128)S(1)} %collective-permute-done.8.refs_1_) | copy-start | bytes 196612
  105.8 6.9 %collective-permute-start.10 = (f32[16,1024]{1,0:T(8,128)}, f32[16,1024]{1,0:T(8,128)S(1)}, u32[]{:S(2)}, u32[]{:S(2)}) collective-permute-start(f32[16,1024]{1,0:T(8,128)} %total.2.refs_0_), channel_id=1, source_target_pairs={{0,24},{8,16},{16,8},{24,0},{1,25},{9,17},{17,9},{25,1},{2,26},{10... | collective-permute-start | bytes 196616 | tf_op jit(solution)/shard_map/ppermute | solution.py:315
  107.7 1.1 copy-start
  112.7 0.6 copy-start.21
  112.7 0.6 copy-start.22
  112.8 0.7 copy-start.11
  112.8 0.7 copy-start.12
  113.4 0.6 copy-start.13
where the time goes:
time: 117 us; the launch traced here: 116 us
  Pallas kernels  46.7 us (40%)
  starting transfers between devices  32.6 us (28%)
  waiting for transfers between devices  26 us (22%)
  local copies, waits for them, and re-layouts  9.4 us (8%)
  between operations  1.46 us (1%)
    pallas_call x13, Pallas kernels, call(): pl.pallas_call(kernel, name=name, in_specs=[smem()] * scalars + [vmem()]...  46.7 us
    ppermute x14, waiting for transfers between devices, body(): over_dp = lambda v, bit: lax.ppermute(v, 'dp', flip(bit, dp_size))  24 us
    ppermute x14, starting transfers between devices, body(): over_dp = lambda v, bit: lax.ppermute(v, 'dp', flip(bit, dp_size))  15.6 us
    unnamed x53, local copies, waits for them, and re-layouts  9.4 us
    ppermute x6, starting transfers between devices, body(): lax.ppermute(v, 'rows', [(i, (i + 2 * k) % rows_size) for i in range(rows...  9.21 us
    all_to_all x1, starting transfers between devices, body(): lax.all_to_all(send, ('dp', 'rows'), split_axis=0, concat_axis=0, tiled=T...  7.16 us
  transfers between devices with their start and end apart: 23, of which 5 were waited for; matrix products, arithmetic and copies ran while one was open for 1% of the time, Pallas kernels for 23%

commit v1 on v0

v1 whole, which is shorter than its diff:
```python
import functools

import jax
import jax.numpy as jnp
from jax import lax
from jax.experimental import pallas as pl
from jax.experimental.pallas import tpu as pltpu
from jax.sharding import PartitionSpec as P

HEADS = 4

norm_eps = 1e-05
adagrad_eps = 1e-10
learning_rate = 0.1

f32, bf16 = jnp.float32, jnp.bfloat16
VMEM_BYTES = 32 * 1024 * 1024
STEP = 256
LANES = 128
ID_ROWS = 8


def dot_nn(a, b):
    return lax.dot_general(a, b, (((1,), (0,)), ((), ())), preferred_element_type=f32)


def dot_nt(a, b):
    return lax.dot_general(a, b, (((1,), (1,)), ((), ())), preferred_element_type=f32)


def dot_tn(a, b):
    return lax.dot_general(a, b, (((0,), (0,)), ((), ())), preferred_element_type=f32)


def standardize(x):
    centered = x - jnp.mean(x, axis=-1, keepdims=True)
    inv = lax.rsqrt(jnp.mean(centered * centered, axis=-1, keepdims=True) + norm_eps)
    return centered * inv, inv


def masked_rows(cot, start, length):
    row = start + lax.broadcasted_iota(jnp.int32, cot.shape, 0)
    return jnp.where(row < length, cot.astype(f32), 0.0)


def owner_order(width, rows, dp):
    chips = rows // 2
    piece = width // (rows * dp)
    at = lax.broadcasted_iota(jnp.int32, (width, 1), 0)
    side, rest = at // (width // 2), at % (width // 2)
    part, rest = rest // (chips * piece), rest % (chips * piece)
    chip, row = rest // piece, rest % piece
    core = lax.rem(lax.axis_index("rows"), 2)
    core = jnp.where(side == 0, core, 1 - core)
    wanted = ((chip * 2 + core) * dp + part) * piece + row
    return jnp.where(lax.broadcasted_iota(jnp.int32, (width, width), 1) == wanted, 1.0, 0.0).astype(bf16)


def forward_kernel(rows_size, dp_size, len_ref, ev_hbm, cot_hbm, win_hbm, wout_hbm,
                   keep_ref, send_ref, hid_ref, dsilu_ref, gatt_ref, gpre_ref, normed_t_ref,
                   ev_ref, cot_ref, win_ref, normed_ref, user_ref, duser_ref, att_ref, mixed_ref, masked_ref, dval_ref, weights_ref,
                   wout_ref, arrived):
    tokens, width = ev_ref.shape
    copies = [pltpu.make_async_copy(ev_hbm, ev_ref, arrived.at[0])]
    for c in range(4):
        cols = pl.ds(c * width, width)
        copies.append(pltpu.make_async_copy(win_hbm.at[:, cols], win_ref.at[:, cols], arrived.at[1 + c]))
    copies.append(pltpu.make_async_copy(cot_hbm, cot_ref, arrived.at[5]))
    copies.append(pltpu.make_async_copy(wout_hbm, wout_ref, arrived.at[6]))
    for copy in copies:
        copy.start()
    hd = width // HEADS
    length = len_ref[0]
    inv_len = 1.0 / length.astype(f32)
    scale = hd ** -0.5
    steps = tokens // STEP

    copies[0].wait()
    for i in range(steps):
        rows = pl.ds(i * STEP, STEP)
        xhat, _ = standardize(ev_ref[rows, :].astype(f32))
        normed_ref[rows, :] = xhat.astype(bf16)

    def project(i, c):
        rows = pl.ds(i * STEP, STEP)
        pre = dot_nn(normed_ref[rows, :], win_ref[:, c * width:(c + 1) * width])
        sig = 0.5 + 0.5 * jnp.tanh(0.5 * pre)
        hid = pre * sig
        dsilu = sig * (1.0 + (pre - hid))
        if c == 0:
            user_ref[rows, :] = hid.astype(bf16)
            duser_ref[rows, :] = dsilu
        else:
            cols = slice((c - 1) * width, c * width)
            hid_ref[rows, cols] = hid.astype(bf16)
            if c == 1:
                dval_ref[rows, :] = dsilu
            else:
                dsilu_ref[rows, (c - 2) * width:(c - 1) * width] = dsilu.astype(bf16)

    for c in range(4):
        copies[1 + c].wait()
        for i in range(steps):
            project(i, c)

    tri = lax.broadcasted_iota(jnp.int32, (STEP, STEP), 0) >= lax.broadcasted_iota(jnp.int32, (STEP, STEP), 1)
    for h in range(HEADS):
        v_cols = slice(h * hd, (h + 1) * hd)
        q_cols = slice(width + h * hd, width + (h + 1) * hd)
        k_cols = slice(2 * width + h * hd, 2 * width + (h + 1) * hd)
        for i in range(steps):
            rows = pl.ds(i * STEP, STEP)
            query = hid_ref[rows, q_cols]
            total = None
            for j in range(i + 1):
                keys = pl.ds(j * STEP, STEP)
                half = dot_nt(query, hid_ref[keys, k_cols]) * (0.5 * scale)
                weights = (half + half * jnp.tanh(half)) * inv_len
                if i == j:
                    weights = jnp.where(tri, weights, 0.0)
                weights = weights.astype(bf16)
                weights_ref[h, rows, keys] = weights
                part = dot_nn(weights, hid_ref[keys, v_cols])
                total = part if total is None else total + part
            att_ref[rows, v_cols] = total

    copies[5].wait()
    copies[6].wait()
    for i in range(steps):
        rows = pl.ds(i * STEP, STEP)
        masked_ref[rows, :] = masked_rows(cot_ref[rows, :], i * STEP, length).astype(bf16)
        ahat, inv = standardize(att_ref[rows, :])
        user = user_ref[rows, :].astype(f32)
        mixed_ref[rows, :] = (ahat * user).astype(bf16)
        grad_mixed = dot_nt(masked_ref[rows, :], wout_ref[...])
        gpre_ref[rows, :width] = (grad_mixed * ahat * duser_ref[rows, :]).astype(bf16)
        e = grad_mixed * user
        gatt_ref[rows, :] = (inv * (e - jnp.mean(e, axis=-1, keepdims=True)
                                    - ahat * jnp.mean(e * ahat, axis=-1, keepdims=True))).astype(bf16)

    for h in range(HEADS):
        v_cols = slice(h * hd, (h + 1) * hd)
        for j in range(steps):
            keys, rest = pl.ds(j * STEP, STEP), pl.ds(j * STEP, tokens - j * STEP)
            grad_v = dot_tn(weights_ref[h, rest, keys], gatt_ref[rest, v_cols])
            gpre_ref[keys, width + h * hd:width + (h + 1) * hd] = (grad_v * dval_ref[keys, v_cols]).astype(bf16)

    order = owner_order(width, rows_size, dp_size)
    normed_t_ref[...] = dot_nt(order, normed_ref[...]).astype(bf16)
    mixed_t = dot_nt(order, mixed_ref[...]).astype(bf16)
    half = width // 2
    for ref, start in ((send_ref, half), (keep_ref, 0)):
        ref[:, :width] = dot_nn(mixed_t[start:start + half], masked_ref[...])
        ref[:, width:] = dot_nn(normed_t_ref[start:start + half, :], gpre_ref[...])


def attention_kernel(len_ref, hid_ref, dsilu_ref, gatt_ref, normed_t_ref, keep_ref, send_ref, gpre_ref):
    tokens, width = gatt_ref.shape
    hd = width // HEADS
    inv_len = 1.0 / len_ref[0].astype(f32)
    scale = hd ** -0.5
    steps = tokens // STEP

    tri = lax.broadcasted_iota(jnp.int32, (STEP, STEP), 0) <= lax.broadcasted_iota(jnp.int32, (STEP, STEP), 1)
    for h in range(HEADS):
        v_cols = slice(h * hd, (h + 1) * hd)
        q_cols = slice(width + h * hd, width + (h + 1) * hd)
        k_cols = slice(2 * width + h * hd, 2 * width + (h + 1) * hd)
        grad_q = [None] * steps
        for j in range(steps):
            keys = pl.ds(j * STEP, STEP)
            key, value = hid_ref[keys, k_cols], hid_ref[keys, v_cols]
            grad_k = None
            for i in range(j, steps):
                rows = pl.ds(i * STEP, STEP)
                query, gatt = hid_ref[rows, q_cols], gatt_ref[rows, v_cols]
                half = dot_nt(key, query) * (0.5 * scale)
                sig2 = 1.0 + jnp.tanh(half)
                silu = half * sig2
                dsilu = sig2 * ((1.0 + half) + (half - silu))
                gscore = dot_nt(value, gatt) * dsilu * (0.5 * inv_len * scale)
                if i == j:
                    gscore = jnp.where(tri, gscore, 0.0)
                gscore = gscore.astype(bf16)
                pk, pq = dot_nn(gscore, query), dot_tn(gscore, key)
                grad_k = pk if grad_k is None else grad_k + pk
                grad_q[i] = pq if grad_q[i] is None else grad_q[i] + pq
            gpre_ref[keys, q_cols] = (grad_k * dsilu_ref[keys, q_cols].astype(f32)).astype(bf16)
        for i in range(steps):
            rows = pl.ds(i * STEP, STEP)
            gpre_ref[rows, v_cols] = (grad_q[i] * dsilu_ref[rows, v_cols].astype(f32)).astype(bf16)

    half = width // 2
    for ref, start in ((send_ref, half), (keep_ref, 0)):
        ref[...] = dot_nn(normed_t_ref[start:start + half, :], gpre_ref[...])


def events_kernel(len_ref, ev_ref, cot_ref, win_ref, slot_ref, slot_row_ref, gpre_uv_ref, gpre_qk_ref,
                  send_ref, hi_ref, lo_ref, rows_ref):
    tokens, width = ev_ref.shape
    capacity, owners = slot_row_ref.shape
    length = len_ref[0]
    for i in range(tokens // STEP):
        rows = pl.ds(i * STEP, STEP)
        xhat, inv = standardize(ev_ref[rows, :].astype(f32))
        grad_normed = dot_nt(gpre_uv_ref[rows, :], win_ref[:, :2 * width]) + dot_nt(gpre_qk_ref[rows, :], win_ref[:, 2 * width:])
        grad = masked_rows(cot_ref[rows, :], i * STEP, length) + inv * (
            grad_normed - jnp.mean(grad_normed, axis=-1, keepdims=True)
            - xhat * jnp.mean(grad_normed * xhat, axis=-1, keepdims=True))
        high = grad.astype(bf16)
        hi_ref[rows, :] = high
        lo_ref[rows, :] = (grad - high.astype(f32)).astype(bf16)

    rows_ref[...] = one_hot_rows(slot_ref[...], rows_ref.shape[0], hi_ref, lo_ref)
    me = lax.axis_index(("dp", "rows"))
    lane = lax.broadcasted_iota(jnp.int32, (capacity, LANES), 1)
    place = lax.broadcasted_iota(jnp.int32, (capacity, LANES), 0) + lax.rem(me, LANES // capacity) * capacity
    spread = jnp.where(lane == place, 1.0, 0.0).astype(bf16)
    ids = slot_row_ref[...]
    ids = 16.0 * dot_tn((ids // 16).astype(bf16), spread) + dot_tn((ids % 16).astype(bf16), spread)
    tiles = width // LANES
    for o in range(owners):
        for t in range(tiles):
            send_ref[o, t * capacity:(t + 1) * capacity, :] = rows_ref[o * capacity:(o + 1) * capacity, t * LANES:(t + 1) * LANES]
        send_ref[o, tiles * capacity:, :] = jnp.broadcast_to(ids[o:o + 1, :], (ID_ROWS, LANES))


def one_hot_rows(ids, rows, hi_ref, lo_ref):
    named = lax.broadcasted_iota(jnp.int32, (rows, ids.shape[1]), 0) == ids
    onehot = jnp.where(named, 1.0, 0.0).astype(bf16)
    return dot_nn(onehot, hi_ref[...]) + dot_nn(onehot, lo_ref[...])


def table_kernel(recv_ref, table_ref, accum_ref, table_new_ref, accum_new_ref, rows_ref, hi_ref, lo_ref):
    owners = recv_ref.shape[0]
    rows, width = table_ref.shape
    tiles = width // LANES
    capacity = (recv_ref.shape[1] - ID_ROWS) // tiles
    for o in range(owners):
        for t in range(tiles):
            rows_ref[o * capacity:(o + 1) * capacity, t * LANES:(t + 1) * LANES] = recv_ref[o, t * capacity:(t + 1) * capacity, :]
    group = LANES // capacity
    ids = [sum(recv_ref[o, tiles * capacity:, :] for o in range(g, g + group)) for g in range(0, owners, group)]
    ids = jnp.concatenate(ids, axis=1)[:1, :].astype(jnp.int32)
    high = rows_ref[...].astype(bf16)
    hi_ref[...] = high
    lo_ref[...] = (rows_ref[...] - high.astype(f32)).astype(bf16)
    grad = one_hot_rows(ids, rows, hi_ref, lo_ref)
    accum = jnp.transpose(jnp.broadcast_to(accum_ref[...].reshape(1, rows), (8, rows)))[:, :1]
    accum_new = accum + jnp.mean(grad * grad, axis=-1, keepdims=True)
    accum_new_ref[...] = jnp.transpose(jnp.broadcast_to(accum_new, (rows, LANES)))[:1, :].reshape(rows)
    table_new_ref[...] = table_ref[...] - learning_rate * grad / (jnp.sqrt(accum_new) + adagrad_eps)


def vmem():
    return pl.BlockSpec(memory_space=pltpu.VMEM)


def shape(*dims, dtype=f32):
    return jax.ShapeDtypeStruct(dims, dtype)


def call(kernel, name, out_shape, args, scalars=0, scratch=(), flops=0, far=0):
    place = [None] * scalars + [pltpu.HBM] * far + [pltpu.VMEM] * (len(args) - scalars - far)
    args = [a if p is None else pltpu.with_memory_space_constraint(a, p) for a, p in zip(args, place)]
    return pl.pallas_call(
        kernel,
        name=name,
        in_specs=[pl.BlockSpec(memory_space=p or pltpu.SMEM) for p in place],
        out_specs=[vmem()] * len(out_shape),
        out_shape=out_shape,
        scratch_shapes=[pltpu.VMEM(dims, dtype) for dims, dtype in scratch] + [pltpu.SemaphoreType.DMA((7,))] * (far > 0),
        compiler_params=pltpu.CompilerParams(vmem_limit_bytes=VMEM_BYTES),
        cost_estimate=pl.CostEstimate(flops=flops, bytes_accessed=1 << 20, transcendentals=0),
    )(*args)


def body(rows_size, dp_size, events, cotangent, lengths, event_slot, slot_row, slot_count, w_in, w_out, item_table, accumulator):
    tokens, width = events.shape
    owners, capacity = slot_row.shape[1:]
    chips = rows_size // 2
    piece = width // (rows_size * dp_size)
    cores = [(i, i ^ 1) for i in range(rows_size)]
    lines = [list(range(c, rows_size, 2)) for c in range(2)]

    def exchange(v, axis, groups=None):
        return lax.all_to_all(v, axis, split_axis=0, concat_axis=0, axis_index_groups=groups, tiled=True)

    def after(value, *others):
        return lax.optimization_barrier((value, *others))[0]

    def over_dp(both):
        return exchange(both.reshape(dp_size, chips * piece, both.shape[1]), "dp")

    def over_chips(parts):
        return exchange(jnp.sum(parts, axis=0).reshape(chips, piece, -1), "rows", lines)

    def gathered(parts):
        part = jnp.sum(parts, axis=0) * (1.0 / tokens)
        return exchange(jnp.broadcast_to(part, (dp_size, *part.shape)), "dp").reshape(dp_size * piece, -1)

    local = lambda *dims, dtype=f32: pltpu.VMEM(dims, dtype)
    sides = lambda cols: [local(width // 2, cols)] * 2
    keep1, send1, hid, dsilu, gatt, gpre_uv, normed_t, events, cotangent, w_in = call(
        functools.partial(forward_kernel, rows_size, dp_size), "forward_part",
        sides(3 * width) + [
            local(tokens, 3 * width, dtype=bf16),
            local(tokens, 2 * width, dtype=bf16),
            local(tokens, width, dtype=bf16),
            local(tokens, 2 * width, dtype=bf16),
            local(width, tokens, dtype=bf16),
            local(tokens, width, dtype=bf16),
            local(tokens, width, dtype=bf16),
            local(*w_in.shape, dtype=bf16),
        ],
        (lengths, events, cotangent, w_in, w_out), 1,
        [((tokens, width), bf16), ((tokens, width), bf16), ((tokens, width), f32), ((tokens, width), f32),
         ((tokens, width), bf16), ((tokens, width), bf16), ((tokens, width), f32), ((HEADS, tokens, tokens), bf16),
         (w_out.shape, bf16)],
        flops=100_000_000_000, far=4)
    recv1 = lax.ppermute(send1, "rows", cores)
    keep2, send2, gpre_qk = call(
        attention_kernel, "attention_part", sides(2 * width) + [local(tokens, 2 * width, dtype=bf16)],
        (lengths, hid, dsilu, gatt, normed_t), 1, flops=100_000_000_000)
    recv2 = lax.ppermute(send2, "rows", cores)
    pay_rows = capacity * (width // LANES) + ID_ROWS
    both1 = keep1 + recv1
    gpre_uv = after(gpre_uv, both1)
    parts1 = over_dp(both1)
    (send,) = call(
        events_kernel, "events_part", [local(owners, pay_rows, LANES)],
        (lengths, events, cotangent, w_in, event_slot, slot_row[0].T, gpre_uv, gpre_qk), 1,
        [((tokens, width), bf16), ((tokens, width), bf16), ((owners * capacity, width), f32)], flops=100_000_000_000)
    recv = exchange(send, ("dp", "rows"))
    both2 = after(keep2, send) + recv2
    parts2 = over_dp(both2)
    parts1 = over_chips(after(parts1, both2))
    parts2 = over_chips(after(parts2, parts1))
    first = gathered(parts1)
    second = gathered(parts2)
    grad_in = jnp.concatenate([first[:, width:], second], axis=1)
    slots = owners * capacity
    table_new, accum_new = call(
        table_kernel, "table_part", [shape(*item_table.shape), shape(*accumulator.shape)],
        (recv, item_table, accumulator), 0,
        [((slots, width), f32), ((slots, width), bf16), ((slots, width), bf16)], flops=10_000_000_000)
    return grad_in, first[:, :width], table_new, accum_new


def solution(mesh):
    whole = P(("dp", "rows"))
    in_specs = (whole,) * 6 + (P(), P(), whole, whole)
    out_specs = (P("rows"), P("rows"), whole, whole)
    run = functools.partial(body, mesh.shape["rows"], mesh.shape["dp"])
    return jax.shard_map(run, mesh=mesh, in_specs=in_specs, out_specs=out_specs, check_vma=False)
```

time: 117 us -> 140 us (1.20)
  waiting for transfers between devices: 26 us -> 60.8 us
  Pallas kernels: 46.7 us -> 18 us
  blocking collectives: 0 us -> 26.6 us
  starting transfers between devices: 32.6 us -> 19.2 us
  other arithmetic: 0 us -> 6.19 us
  local copies, waits for them, and re-layouts: 9.4 us -> 7.11 us
    all_to_all x1 -> x5, waiting for transfers between devices: 0.01 us -> 60.8 us  [exchange(): lax.all_to_all(v, axis, split_axis=0, concat_axis=0, axis_index_groups=gr...]
    pallas_call x13 -> x4, Pallas kernels: 46.7 us -> 18 us  [call(): pl.pallas_call(kernel, name=name, in_specs=[pl.BlockSpec(memory_space=p o...]
    all_to_all x0 -> x2, blocking collectives: none -> 26.6 us  [exchange(): lax.all_to_all(v, axis, split_axis=0, concat_axis=0, axis_index_groups=gr...]
    ppermute x22 -> x2, waiting for transfers between devices: 26 us -> 0.01 us  [the longest x1 0.01 us: body(): recv1 = lax.ppermute(send1, 'rows', cores)]
    ppermute x22 -> x2, starting transfers between devices: 25.4 us -> 0.64 us  [the longest x1 0.52 us: body(): recv1 = lax.ppermute(send1, 'rows', cores)]
    all_to_all x1 -> x5, starting transfers between devices: 7.16 us -> 18.6 us  [exchange(): lax.all_to_all(v, axis, split_axis=0, concat_axis=0, axis_index_groups=gr...]
    unnamed x53 -> x24, local copies, waits for them, and re-layouts: 9.4 us -> 4.93 us
    add x0 -> x2, other arithmetic: none -> 3.7 us  [the longest x1 2.33 us: body(): both2 = after(keep2, send) + recv2]
  transfers between devices with their start and end apart: 23 -> 7, of which waited for: 5 -> 5; matrix products, arithmetic and copies ran while one was open for 1% -> 3% of each run, Pallas kernels for 23% -> 7%
where the time goes in v1:
time: 140 us; the launch traced here: 139 us
  waiting for transfers between devices  60.8 us (43%)
  blocking collectives  26.6 us (19%)
  starting transfers between devices  19.2 us (14%)
  Pallas kernels  18 us (13%)
  local copies, waits for them, and re-layouts  7.11 us (5%)
  other arithmetic  6.19 us (4%)
  between operations  1.48 us (1%)
    all_to_all x5, waiting for transfers between devices, exchange(): lax.all_to_all(v, axis, split_axis=0, concat_axis=0, axis_index_groups=gr...  60.8 us
    all_to_all x2, blocking collectives, exchange(): lax.all_to_all(v, axis, split_axis=0, concat_axis=0, axis_index_groups=gr...  26.6 us
    all_to_all x5, starting transfers between devices, exchange(): lax.all_to_all(v, axis, split_axis=0, concat_axis=0, axis_index_groups=gr...  18.6 us
    pallas_call x4, Pallas kernels, call(): pl.pallas_call(kernel, name=name, in_specs=[pl.BlockSpec(memory_space=p o...  18 us
    unnamed x24, local copies, waits for them, and re-layouts  4.93 us
  transfers between devices with their start and end apart: 7, of which 5 were waited for; matrix products, arithmetic and copies ran while one was open for 3% of the time, Pallas kernels for 7%

profile of v1, /device:TPU:0, one launch (start us, length us, event | category | flops | bytes accessed | tf_op | source)
XLA Modules:
  0.0 139.3 jit_solution(8051778401756071448)
XLA Ops:
  1.3 8.3 %forward_part.1 = (f32[256,1536]{1,0:T(8,128)S(1)}, f32[256,1536]{1,0:T(8,128)S(1)}, bf16[512,1536]{1,0:T(8,128)(2,1)S(1)}, bf16[512,1024]{1,0:T(8,128)(2,1)S(1)...) custom-call(s32[1]{0:T(128)S(6)} %copy.13.len_ref, ...), custom_call_target="tpu_custom_call" | custom-call | flops 99999997952 | bytes 1048576 | tf_op jit(solution)/shard_map/forward_part/pallas_call | solution.py:266
  9.5 0.0 copy-start.4
  9.6 0.0 copy-start.8
  9.6 0.0 copy-start.10
  9.6 0.5 collective-permute-start
  10.1 4.1 %attention_part.1 = (f32[256,1024]{1,0:T(8,128)S(1)}, f32[256,1024]{1,0:T(8,128)S(1)}, bf16[512,1024]{1,0:T(8,128)(2,1)S(1)}) custom-call(s32[1]{0:T(128)S(6)} %copy.13.len_ref, bf16[512,1536]{1,0:T(8,128)(2,1)S(1)} %get-tuple-element.25.hid_ref, bf16[512,1024]{1,0:T(8,128)(2,1)S(1)} %get-tuple-element.26.dsilu_ref, ...), custom_call_target="tpu_custom_call" | custom-call | flops 99999997952 | bytes 1048576 | tf_op jit(solution)/shard_map/attention_part/pallas_call | solution.py:266
  14.2 0.0 copy-done.4
  14.2 0.0 copy-done.8
  14.2 0.0 copy-done.10
  14.3 0.0 copy-start.6
  14.3 0.1 collective-permute-start.1
  14.4 0.0 collective-permute-done
  14.4 1.4 add.6
  15.8 0.0 copy-done.6
  15.8 0.0 copy-start.1
  15.8 0.0 copy-start.2
  15.8 5.3 %all-to-all-start = ((f32[4,64,1536]{2,1,0:T(8,128)}), f32[4,64,1536]{2,1,0:T(8,128)}, u32[]{:S(2)}, u32[]{:S(2)}) async-start(f32[4,64,1536]{2,1,0:T(8,128)} %bitcast.10), calls=%async_computation | async-start | bytes 3145728 | tf_op jit(solution)/shard_map/all_to_all | solution.py:287
  21.1 0.0 copy-done.1
  21.1 0.0 copy-done.2
  21.1 0.0 copy-start.5
  21.1 1.6 %copy-done.5 = bf16[512,2048]{1,0:T(8,128)(2,1)S(1)} copy-done((bf16[512,2048]{1,0:T(8,128)(2,1)S(1)}, bf16[512,2048]{1,0:T(8,128)(2,1)}, u32[]{:S(2)}) %copy-start.5) | copy-done | bytes 2097176
  22.7 0.0 copy-start.7
  22.7 1.2 copy-done.7
  23.9 0.0 copy-start.9
  23.9 1.0 copy-done.9
  24.9 0.0 copy-start.11
  24.9 1.0 copy-done.11
  26.0 3.2 %events_part.1 = f32[32,72,128]{2,1,0:T(8,128)} custom-call(s32[1]{0:T(128)S(6)} %copy.13.len_ref, bf16[512,512]{1,0:T(8,128)(2,1)S(1)} %copy-done.9, bf16[512,512]{1,0:T(8,128)(2,1)S(1)} %copy-done.11, bf16[512,2048]{1,0:T(8,128)(2,1)S(1)} %copy-done.5, s32[1,512]{1,0:T(1,128)S(1)} %copy-done.2, s32[16,32]{1,0:T(8,128)S(1)} %bitcast.9, ...), custom_call_target="tpu_custom_call" | custom-call | flops 99999997952 | bytes 1048576 | tf_op jit(solution)/shard_map/events_part/pallas_call | solution.py:266
  29.2 0.0 collective-permute-done.1
  29.2 2.3 %add.7 = f32[256,1024]{1,0:T(8,128)} add(f32[256,1024]{1,0:T(8,128)S(1)} %get-tuple-element.36, f32[256,1024]{1,0:T(8,128)} %collective-permute-done.1) | non-fusion elementwise | flops 262144 | bytes 3145728 | tf_op jit(solution)/shard_map/add | solution.py:335
  31.5 9.9 %all-to-all-done = f32[4,64,1536]{2,1,0:T(8,128)} async-done(((f32[4,64,1536]{2,1,0:T(8,128)}), f32[4,64,1536]{2,1,0:T(8,128)}, u32[]{:S(2)}, u32[]{:S(2)}) %all-to-all-start) | async-done | bytes 1572896 | tf_op jit(solution)/shard_map/all_to_all | solution.py:287
  41.5 1.5 %reduce_sum.36 = f32[64,1536]{1,0:T(8,128)S(1)} reduce(f32[4,64,1536]{2,1,0:T(8,128)} %all-to-all-done, f32[]{:T(128)} %constant.2.clone.1), dimensions={0}, to_apply=%region_0.0 | reduce | flops 294912 | bytes 1966084 | tf_op jit(solution)/shard_map/reduce_sum | solution.py:296
  43.0 15.8 %all_to_all.35 = f32[4,16,1536]{2,1,0:T(8,128)S(1)} all-to-all(f32[4,16,1536]{2,1,0:T(8,128)S(1)} %bitcast.13), channel_id=1, replica_groups={{0,2,4,6},{1,3,5,7},{8,10,12,14},{9,11,13,15},{16,18,20,22},{17,19,21,2..., dimensions={0} | all-to-all | bytes 786432 | tf_op jit(solution)/shard_map/all_to_all | solution.py:287
  58.8 3.5 %all-to-all-start.3 = ((f32[4,64,1024]{2,1,0:T(8,128)}), f32[4,64,1024]{2,1,0:T(8,128)S(1)}, u32[]{:S(2)}, u32[]{:S(2)}) async-start(f32[4,64,1024]{2,1,0:T(8,128)} %bitcast.5), calls=%async_computation.3 | async-start | bytes 2097152 | tf_op jit(solution)/shard_map/all_to_all | solution.py:287
  62.4 12.3 %all-to-all-done.3 = f32[4,64,1024]{2,1,0:T(8,128)S(1)} async-done(((f32[4,64,1024]{2,1,0:T(8,128)}), f32[4,64,1024]{2,1,0:T(8,128)S(1)}, u32[]{:S(2)}, u32[]{:S(2)}) %all-to-all-start.3) | async-done | bytes 1048608 | tf_op jit(solution)/shard_map/all_to_all | solution.py:287
  74.6 0.8 broadcast_in_dim.6
  75.4 3.5 %all-to-all-start.2 = ((f32[4,16,1536]{2,1,0:T(8,128)}), f32[4,16,1536]{2,1,0:T(8,128)S(1)}, u32[]{:S(2)}, u32[]{:S(2)}) async-start(f32[4,16,1536]{2,1,0:T(8,128)} %broadcast_in_dim.6), calls=%async_computation.2 | async-start | bytes 786432 | tf_op jit(solution)/shard_map/all_to_all | solution.py:287
  78.9 0.1 reduce_sum.38
  79.0 5.9 %all-to-all-done.2 = f32[4,16,1536]{2,1,0:T(8,128)S(1)} async-done(((f32[4,16,1536]{2,1,0:T(8,128)}), f32[4,16,1536]{2,1,0:T(8,128)S(1)}, u32[]{:S(2)}, u32[]{:S(2)}) %all-to-all-start.2) | async-done | bytes 393248 | tf_op jit(solution)/shard_map/all_to_all | solution.py:287
  84.9 10.8 %all_to_all.36 = f32[4,16,1024]{2,1,0:T(8,128)S(1)} all-to-all(f32[4,16,1024]{2,1,0:T(8,128)S(1)} %bitcast.14), channel_id=1, replica_groups={{0,2,4,6},{1,3,5,7},{8,10,12,14},{9,11,13,15},{16,18,20,22},{17,19,21,2..., dimensions={0} | all-to-all | bytes 524288 | tf_op jit(solution)/shard_map/all_to_all | solution.py:287
  95.6 2.9 %all-to-all-start.6 = ((f32[32,72,128]{2,1,0:T(8,128)}), f32[32,72,128]{2,1,0:T(8,128)S(1)}, u32[]{:S(2)}, u32[]{:S(2)}) async-start(f32[32,72,128]{2,1,0:T(8,128)} %events_part.1), calls=%async_computation.6 | async-start | bytes 2359296 | tf_op jit(solution)/shard_map/all_to_all | solution.py:287
  98.5 0.0 copy-start
  98.6 0.0 copy-start.3
  98.6 0.7 slice.9
  99.3 29.6 %all-to-all-done.6.recv_ref = f32[32,72,128]{2,1,0:T(8,128)S(1)} async-done(((f32[32,72,128]{2,1,0:T(8,128)}), f32[32,72,128]{2,1,0:T(8,128)S(1)}, u32[]{:S(2)}, u32[]{:S(2)}) %all-to-all-start.6) | async-done | bytes 1179680 | tf_op jit(solution)/shard_map/all_to_all | solution.py:287
  128.9 0.7 broadcast_in_dim.7
  129.7 3.4 %all-to-all-start.5 = ((f32[4,16,1024]{2,1,0:T(8,128)}), f32[4,16,1024]{2,1,0:T(8,128)S(1)}, u32[]{:S(2)}, u32[]{:S(2)}) async-start(f32[4,16,1024]{2,1,0:T(8,128)} %broadcast_in_dim.7), calls=%async_computation.5 | async-start | bytes 524288 | tf_op jit(solution)/shard_map/all_to_all | solution.py:287
  133.1 0.0 copy-done
  133.1 0.0 copy-done.3
  133.1 2.4 %table_part.1 = (f32[512,512]{1,0:T(8,128)}, f32[512]{0:T(512)}) custom-call(f32[32,72,128]{2,1,0:T(8,128)S(1)} %all-to-all-done.6.recv_ref, f32[512,512]{1,0:T(8,128)S(1)} %copy-done, f32[512]{0:T(512)S(1)} %copy-done.3), custom_call_target="tpu_custom_call" | custom-call | flops 10000000000 | bytes 1048576 | tf_op jit(solution)/shard_map/table_part/pallas_call | solution.py:266
  135.5 3.0 %all-to-all-done.5 = f32[4,16,1024]{2,1,0:T(8,128)S(1)} async-done(((f32[4,16,1024]{2,1,0:T(8,128)}), f32[4,16,1024]{2,1,0:T(8,128)S(1)}, u32[]{:S(2)}, u32[]{:S(2)}) %all-to-all-start.5) | async-done | bytes 262176 | tf_op jit(solution)/shard_map/all_to_all | solution.py:287
  138.5 0.8 pad_maximum_fusion
  (5 shorter events, 0.1 us)
Async XLA Ops:
  9.5 4.7 %copy-start.4 = (bf16[512,2048]{1,0:T(8,128)(2,1)}, bf16[512,2048]{1,0:T(8,128)(2,1)S(1)}, u32[]{:S(2)}) copy-start(bf16[512,2048]{1,0:T(8,128)(2,1)S(1)} %get-tuple-element.32.win_ref) | copy-start | bytes 6291460
  9.6 4.7 %copy-start.8 = (bf16[512,512]{1,0:T(8,128)(2,1)}, bf16[512,512]{1,0:T(8,128)(2,1)S(1)}, u32[]{:S(2)}) copy-start(bf16[512,512]{1,0:T(8,128)(2,1)S(1)} %get-tuple-element.30.ev_ref) | copy-start | bytes 1572868
  9.6 4.7 %copy-start.10 = (bf16[512,512]{1,0:T(8,128)(2,1)}, bf16[512,512]{1,0:T(8,128)(2,1)S(1)}, u32[]{:S(2)}) copy-start(bf16[512,512]{1,0:T(8,128)(2,1)S(1)} %get-tuple-element.31.cot_ref) | copy-start | bytes 1572868
  9.6 4.8 %collective-permute-start = (f32[256,1536]{1,0:T(8,128)S(1)}, f32[256,1536]{1,0:T(8,128)S(1)}, u32[]{:S(2)}, u32[]{:S(2)}) collective-permute-start(f32[256,1536]{1,0:T(8,128)S(1)} %get-tuple-element.24), channel_id=1, source_target_pairs={{0,1},{1,0},{2,3},{3,2},{4,5},{5,4},{6,7},{7,6},{8,9},{9,8},{10,11... | collective-permute-start | bytes 4718600 | tf_op jit(solution)/shard_map/ppermute | solution.py:321
  14.3 1.5 %copy-start.6 = (bf16[512,1024]{1,0:T(8,128)(2,1)}, bf16[512,1024]{1,0:T(8,128)(2,1)S(1)}, u32[]{:S(2)}) copy-start(bf16[512,1024]{1,0:T(8,128)(2,1)S(1)} %get-tuple-element.35.gpre_qk_ref) | copy-start | bytes 3145732
  14.3 14.9 %collective-permute-start.1 = (f32[256,1024]{1,0:T(8,128)S(1)}, f32[256,1024]{1,0:T(8,128)}, u32[]{:S(2)}, u32[]{:S(2)}) collective-permute-start(f32[256,1024]{1,0:T(8,128)S(1)} %get-tuple-element.37), channel_id=1, source_target_pairs={{0,1},{1,0},{2,3},{3,2},{4,5},{5,4},{6,7},{7,6},{8,9},{9,8},{10,11... | collective-permute-start | bytes 3145736 | tf_op jit(solution)/shard_map/ppermute | solution.py:325
  15.8 5.3 %copy-start.1 = (s32[1,32,16]{1,2,0:T(8,128)S(1)}, s32[1,32,16]{1,2,0:T(8,128)}, u32[]{:S(2)}) copy-start(s32[1,32,16]{1,2,0:T(8,128)} %param.14) | copy-start | bytes 6148
  15.8 5.3 %copy-start.2 = (s32[1,512]{1,0:T(1,128)S(1)}, s32[1,512]{1,0:T(1,128)}, u32[]{:S(2)}) copy-start(s32[1,512]{1,0:T(1,128)} %slot_ref.1) | copy-start | bytes 6148
  15.8 25.7 %all-to-all-start = ((f32[4,64,1536]{2,1,0:T(8,128)}), f32[4,64,1536]{2,1,0:T(8,128)}, u32[]{:S(2)}, u32[]{:S(2)}) async-start(f32[4,64,1536]{2,1,0:T(8,128)} %bitcast.10), calls=%async_computation | async-start | bytes 3145728 | tf_op jit(solution)/shard_map/all_to_all | solution.py:287
  21.1 1.6 %copy-start.5 = (bf16[512,2048]{1,0:T(8,128)(2,1)S(1)}, bf16[512,2048]{1,0:T(8,128)(2,1)}, u32[]{:S(2)}) copy-start(bf16[512,2048]{1,0:T(8,128)(2,1)} %copy-done.4) | copy-start | bytes 6291460
  22.7 1.2 copy-start.7
  23.9 1.0 copy-start.9
  24.9 1.0 copy-start.11
  58.8 15.8 %all-to-all-start.3 = ((f32[4,64,1024]{2,1,0:T(8,128)}), f32[4,64,1024]{2,1,0:T(8,128)S(1)}, u32[]{:S(2)}, u32[]{:S(2)}) async-start(f32[4,64,1024]{2,1,0:T(8,128)} %bitcast.5), calls=%async_computation.3 | async-start | bytes 2097152 | tf_op jit(solution)/shard_map/all_to_all | solution.py:287
  75.4 9.4 %all-to-all-start.2 = ((f32[4,16,1536]{2,1,0:T(8,128)}), f32[4,16,1536]{2,1,0:T(8,128)S(1)}, u32[]{:S(2)}, u32[]{:S(2)}) async-start(f32[4,16,1536]{2,1,0:T(8,128)} %broadcast_in_dim.6), calls=%async_computation.2 | async-start | bytes 786432 | tf_op jit(solution)/shard_map/all_to_all | solution.py:287
  95.6 33.3 %all-to-all-start.6 = ((f32[32,72,128]{2,1,0:T(8,128)}), f32[32,72,128]{2,1,0:T(8,128)S(1)}, u32[]{:S(2)}, u32[]{:S(2)}) async-start(f32[32,72,128]{2,1,0:T(8,128)} %events_part.1), calls=%async_computation.6 | async-start | bytes 2359296 | tf_op jit(solution)/shard_map/all_to_all | solution.py:287
  98.5 34.5 %copy-start = (f32[512,512]{1,0:T(8,128)S(1)}, f32[512,512]{1,0:T(8,128)}, u32[]{:S(2)}) copy-start(f32[512,512]{1,0:T(8,128)} %table_ref.1) | copy-start | bytes 3145732
  98.6 34.5 %copy-start.3 = (f32[512]{0:T(512)S(1)}, f32[512]{0:T(512)}, u32[]{:S(2)}) copy-start(f32[512]{0:T(512)} %accum_ref.1) | copy-start | bytes 6148
  129.7 8.9 %all-to-all-start.5 = ((f32[4,16,1024]{2,1,0:T(8,128)}), f32[4,16,1024]{2,1,0:T(8,128)S(1)}, u32[]{:S(2)}, u32[]{:S(2)}) async-start(f32[4,16,1024]{2,1,0:T(8,128)} %broadcast_in_dim.7), calls=%async_computation.5 | async-start | bytes 524288 | tf_op jit(solution)/shard_map/all_to_all | solution.py:287

commit v2 on v1

--- a/solution.py
+++ b/solution.py
@@ -14,7 +14,7 @@
 learning_rate = 0.1
 
 f32, bf16 = jnp.float32, jnp.bfloat16
-VMEM_BYTES = 32 * 1024 * 1024
+VMEM_BYTES = 16 * 1024 * 1024
 STEP = 256
 LANES = 128
 ID_ROWS = 8
@@ -252,6 +252,60 @@
     table_new_ref[...] = table_ref[...] - learning_rate * grad / (jnp.sqrt(accum_new) + adagrad_eps)
 
 
+def split_first_kernel(keep_ref, recv_ref, send_a_ref, keep_a_ref, send_b_ref, keep_b_ref):
+    d = lax.axis_index("dp")
+    x, y = lax.rem(d, 2), d // 2
+    half = keep_ref.shape[-1] // 2
+    lo, hi = slice(0, half), slice(half, 2 * half)
+    for s in range(2):
+        send_a_ref[s] = keep_ref[s, 1 - x, :, lo] + recv_ref[s, 1 - x, :, lo]
+        send_b_ref[s] = keep_ref[1 - y, s, :, hi] + recv_ref[1 - y, s, :, hi]
+        keep_a_ref[s] = keep_ref[s, x, :, lo] + recv_ref[s, x, :, lo]
+        keep_b_ref[s] = keep_ref[y, s, :, hi] + recv_ref[y, s, :, hi]
+
+
+def split_second_kernel(keep_a_ref, recv_a_ref, keep_b_ref, recv_b_ref, send_a_ref, next_a_ref, send_b_ref, next_b_ref):
+    d = lax.axis_index("dp")
+    x, y = lax.rem(d, 2), d // 2
+    send_a_ref[...] = keep_a_ref[1 - y] + recv_a_ref[1 - y]
+    send_b_ref[...] = keep_b_ref[1 - x] + recv_b_ref[1 - x]
+    next_a_ref[...] = keep_a_ref[y] + recv_a_ref[y]
+    next_b_ref[...] = keep_b_ref[x] + recv_b_ref[x]
+
+
+def chips_kernel(keep_a_ref, recv_a_ref, keep_b_ref, recv_b_ref, *out_refs):
+    chips = len(out_refs)
+    chip = lax.axis_index("rows") // 2
+    half = keep_a_ref.shape[-1]
+    for k, out_ref in enumerate(out_refs):
+        at = lax.rem(chip + k, chips)
+        out_ref[:, :half] = keep_a_ref[at] + recv_a_ref[at]
+        out_ref[:, half:] = keep_b_ref[at] + recv_b_ref[at]
+
+
+def total_kernel(tokens, *refs):
+    *pieces, out_ref = refs
+    half = len(pieces) // 2
+    start = 0
+    for group in (pieces[:half], pieces[half:]):
+        total = group[0][...]
+        for ref in group[1:]:
+            total = total + ref[...]
+        end = start + total.shape[-1]
+        out_ref[:, start:end] = total * (1.0 / tokens)
+        start = end
+
+
+def gather_kernel(*refs):
+    *pieces, grad_in_ref, grad_out_ref = refs
+    d = lax.axis_index("dp")
+    width = grad_out_ref.shape[-1]
+    for k, piece in enumerate(pieces):
+        at = jnp.bitwise_xor(d, k)
+        grad_out_ref[at] = piece[:, :width]
+        grad_in_ref[at] = piece[:, width:]
+
+
 def vmem():
     return pl.BlockSpec(memory_space=pltpu.VMEM)
 
@@ -268,10 +322,10 @@
         name=name,
         in_specs=[pl.BlockSpec(memory_space=p or pltpu.SMEM) for p in place],
         out_specs=[vmem()] * len(out_shape),
-        out_shape=out_shape,
+        out_shape=list(out_shape),
         scratch_shapes=[pltpu.VMEM(dims, dtype) for dims, dtype in scratch] + [pltpu.SemaphoreType.DMA((7,))] * (far > 0),
         compiler_params=pltpu.CompilerParams(vmem_limit_bytes=VMEM_BYTES),
-        cost_estimate=pl.CostEstimate(flops=flops, bytes_accessed=1 << 20, transcendentals=0),
+        cost_estimate=pl.CostEstimate(flops=flops, bytes_accessed=1 << 16, transcendentals=0),
     )(*args)
 
 
@@ -281,23 +335,28 @@
     chips = rows_size // 2
     piece = width // (rows_size * dp_size)
     cores = [(i, i ^ 1) for i in range(rows_size)]
-    lines = [list(range(c, rows_size, 2)) for c in range(2)]
-
-    def exchange(v, axis, groups=None):
-        return lax.all_to_all(v, axis, split_axis=0, concat_axis=0, axis_index_groups=groups, tiled=True)
-
-    def after(value, *others):
-        return lax.optimization_barrier((value, *others))[0]
-
-    def over_dp(both):
-        return exchange(both.reshape(dp_size, chips * piece, both.shape[1]), "dp")
-
-    def over_chips(parts):
-        return exchange(jnp.sum(parts, axis=0).reshape(chips, piece, -1), "rows", lines)
-
-    def gathered(parts):
-        part = jnp.sum(parts, axis=0) * (1.0 / tokens)
-        return exchange(jnp.broadcast_to(part, (dp_size, *part.shape)), "dp").reshape(dp_size * piece, -1)
+    over_dp = lambda v, bit: lax.ppermute(v, "dp", [(i, i ^ bit) for i in range(dp_size)])
+    over_chips = lambda v, k: lax.ppermute(v, "rows", [(i, (i + 2 * k) % rows_size) for i in range(rows_size)])
+    after = lambda value, *others: lax.optimization_barrier((value, *others))[0]
+    strip = chips * piece
+
+    def split_first(keep, recv):
+        cols = keep.shape[1]
+        views = [v.reshape(2, 2, strip, cols) for v in (keep, recv)]
+        return call(split_first_kernel, "split_first", [local(2, strip, cols // 2)] * 4, views)
+
+    def split_second(send_a, keep_a, send_b, keep_b):
+        recv_a, recv_b = over_dp(send_a, 1), over_dp(send_b, 2)
+        return call(split_second_kernel, "split_second", [local(strip, keep_a.shape[-1])] * 4, (keep_a, recv_a, keep_b, recv_b))
+
+    def by_chip(send_a, keep_a, send_b, keep_b):
+        cols = keep_a.shape[-1]
+        recv_a, recv_b = over_dp(send_a, 2), over_dp(send_b, 1)
+        views = [v.reshape(chips, piece, cols) for v in (keep_a, recv_a, keep_b, recv_b)]
+        return call(chips_kernel, "by_chip", [local(piece, 2 * cols)] * chips, views)
+
+    def meet(blocks):
+        return [blocks[0]] + [over_chips(blocks[k], k) for k in range(1, chips)]
 
     local = lambda *dims, dtype=f32: pltpu.VMEM(dims, dtype)
     sides = lambda cols: [local(width // 2, cols)] * 2
@@ -324,27 +383,31 @@
         (lengths, hid, dsilu, gatt, normed_t), 1, flops=100_000_000_000)
     recv2 = lax.ppermute(send2, "rows", cores)
     pay_rows = capacity * (width // LANES) + ID_ROWS
-    both1 = keep1 + recv1
-    gpre_uv = after(gpre_uv, both1)
-    parts1 = over_dp(both1)
+    first = list(split_first(keep1, after(recv1, keep2)))
+    gpre_uv = after(gpre_uv, *first)
     (send,) = call(
         events_kernel, "events_part", [local(owners, pay_rows, LANES)],
         (lengths, events, cotangent, w_in, event_slot, slot_row[0].T, gpre_uv, gpre_qk), 1,
         [((tokens, width), bf16), ((tokens, width), bf16), ((owners * capacity, width), f32)], flops=100_000_000_000)
-    recv = exchange(send, ("dp", "rows"))
-    both2 = after(keep2, send) + recv2
-    parts2 = over_dp(both2)
-    parts1 = over_chips(after(parts1, both2))
-    parts2 = over_chips(after(parts2, parts1))
-    first = gathered(parts1)
-    second = gathered(parts2)
-    grad_in = jnp.concatenate([first[:, width:], second], axis=1)
+    recv = lax.all_to_all(send, ("dp", "rows"), split_axis=0, concat_axis=0, tiled=True)
+    first[1] = after(first[1], send)
+    first = list(split_second(*first))
+    second = list(split_first(after(keep2, *first), recv2))
+    first[1] = after(first[1], *second)
+    first = by_chip(*first)
+    second[1] = after(second[1], *first)
+    second = list(split_second(*second))
+    second = by_chip(*second)
+    (total,) = call(functools.partial(total_kernel, tokens), "total", [local(piece, 5 * width)], meet(first) + meet(second))
+    pieces = [total] + [over_dp(total, k) for k in range(1, dp_size)]
+    grad_in, grad_out = call(
+        gather_kernel, "gather", [shape(dp_size, piece, 4 * width), shape(dp_size, piece, width)], pieces)
     slots = owners * capacity
     table_new, accum_new = call(
         table_kernel, "table_part", [shape(*item_table.shape), shape(*accumulator.shape)],
         (recv, item_table, accumulator), 0,
-        [((slots, width), f32), ((slots, width), bf16), ((slots, width), bf16)], flops=10_000_000_000)
-    return grad_in, first[:, :width], table_new, accum_new
+        [((slots, width), f32), ((slots, width), bf16), ((slots, width), bf16)])
+    return grad_in.reshape(-1, 4 * width), grad_out.reshape(-1, width), table_new, accum_new
 
 
 def solution(mesh):

time: 140 us -> 94.1 us (0.67)
  blocking collectives: 26.6 us -> 0 us
  waiting for transfers between devices: 60.8 us -> 41 us
  starting transfers between devices: 19.2 us -> 30.1 us
  other arithmetic: 6.19 us -> 0 us
  local copies, waits for them, and re-layouts: 7.11 us -> 1.52 us
  Pallas kernels: 18 us -> 19.9 us
    all_to_all x5 -> x1, waiting for transfers between devices: 60.8 us -> 0.01 us  [body(): lax.all_to_all(send, ('dp', 'rows'), split_axis=0, concat_axis=0, tiled=T...]
    ppermute x0 -> x17, waiting for transfers between devices: none -> 41 us  [the longest x11 34.9 us: body(): lax.ppermute(v, 'dp', [(i, i ^ bit) for i in range(dp_size)])]
    all_to_all x2 -> x0, blocking collectives: 26.6 us -> none  [exchange(): lax.all_to_all(v, axis, split_axis=0, concat_axis=0, axis_index_groups=gr...]
    ppermute x0 -> x17, starting transfers between devices: none -> 22.3 us  [the longest x11 11.7 us: body(): lax.ppermute(v, 'dp', [(i, i ^ bit) for i in range(dp_size)])]
    all_to_all x5 -> x1, starting transfers between devices: 18.6 us -> 6.95 us  [body(): lax.all_to_all(send, ('dp', 'rows'), split_axis=0, concat_axis=0, tiled=T...]
    add x2 -> x0, other arithmetic: 3.7 us -> none  [the longest x1 2.33 us: body(): both2 = after(keep2, send) + recv2]
    unnamed x24 -> x12, local copies, waits for them, and re-layouts: 4.93 us -> 1.52 us
    pallas_call x4 -> x12, Pallas kernels: 18 us -> 19.9 us  [call(): pl.pallas_call(kernel, name=name, in_specs=[pl.BlockSpec(memory_space=p o...]
  transfers between devices with their start and end apart: 7 -> 20, of which waited for: 5 -> 8; matrix products, arithmetic and copies ran while one was open for 3% -> 0% of each run, Pallas kernels for 7% -> 6%
where the time goes in v2:
time: 94.1 us; the launch traced here: 93.9 us
  waiting for transfers between devices  41 us (44%)
  starting transfers between devices  30.1 us (32%)
  Pallas kernels  19.9 us (21%)
  local copies, waits for them, and re-layouts  1.52 us (2%)
  between operations  1.43 us (2%)
    ppermute x11, waiting for transfers between devices, body(): lax.ppermute(v, 'dp', [(i, i ^ bit) for i in range(dp_size)])  34.9 us
    pallas_call x12, Pallas kernels, call(): pl.pallas_call(kernel, name=name, in_specs=[pl.BlockSpec(memory_space=p o...  19.9 us
    ppermute x11, starting transfers between devices, body(): lax.ppermute(v, 'dp', [(i, i ^ bit) for i in range(dp_size)])  11.7 us
    ppermute x6, starting transfers between devices, body(): lax.ppermute(v, 'rows', [(i, (i + 2 * k) % rows_size) for i in range(rows...  10.5 us
    all_to_all x1, starting transfers between devices, body(): lax.all_to_all(send, ('dp', 'rows'), split_axis=0, concat_axis=0, tiled=T...  6.95 us
    ppermute x6, waiting for transfers between devices, body(): lax.ppermute(v, 'rows', [(i, (i + 2 * k) % rows_size) for i in range(rows...  6.13 us
  transfers between devices with their start and end apart: 20, of which 8 were waited for; matrix products, arithmetic and copies ran while one was open for 0% of the time, Pallas kernels for 6%

profile of v2, /device:TPU:0, one launch (start us, length us, event | category | flops | bytes accessed | tf_op | source)
XLA Modules:
  0.0 93.9 jit_solution(6675509563868364924)
XLA Ops:
  1.3 8.4 %forward_part.1 = (f32[256,1536]{1,0:T(8,128)S(1)}, f32[256,1536]{1,0:T(8,128)S(1)}, bf16[512,1536]{1,0:T(8,128)(2,1)S(1)}, bf16[512,1024]{1,0:T(8,128)(2,1)S(1)...) custom-call(s32[1]{0:T(128)S(6)} %copy.13.len_ref, ...), custom_call_target="tpu_custom_call" | custom-call | flops 99999997952 | bytes 65536 | tf_op jit(solution)/shard_map/forward_part/pallas_call | solution.py:320
  9.6 0.5 collective-permute-start
  10.2 4.2 %attention_part.1 = (f32[256,1024]{1,0:T(8,128)S(1)}, f32[256,1024]{1,0:T(8,128)S(1)}, bf16[512,1024]{1,0:T(8,128)(2,1)S(1)}) custom-call(s32[1]{0:T(128)S(6)} %copy.13.len_ref, bf16[512,1536]{1,0:T(8,128)(2,1)S(1)} %get-tuple-element.53.hid_ref, bf16[512,1024]{1,0:T(8,128)(2,1)S(1)} %get-tuple-element.54.dsilu_ref, ...), custom_call_target="tpu_custom_call" | custom-call | flops 99999997952 | bytes 65536 | tf_op jit(solution)/shard_map/attention_part/pallas_call | solution.py:320
  14.3 0.0 copy-start.2
  14.3 0.0 collective-permute-done
  14.4 0.0 copy-start.4
  14.4 0.0 copy-start.5
  14.4 0.2 split_first.2
  14.6 0.7 copy-done.2
  15.3 0.0 copy-start.3
  15.3 0.7 copy-done.3
  16.0 0.0 copy-done.4
  16.1 0.0 copy-done.5
  16.1 3.5 %events_part.1 = f32[32,72,128]{2,1,0:T(8,128)} custom-call(s32[1]{0:T(128)S(6)} %copy.13.len_ref, bf16[512,512]{1,0:T(8,128)(2,1)S(1)} %get-tuple-element.60.ev_ref, bf16[512,512]{1,0:T(8,128)(2,1)S(1)} %get-tuple-element.61.cot_ref, bf16[512,2048]{1,0:T(8,128)(2,1)S(1)} %get-tuple-element.62.win_ref, s32[1,512]{1,0:T(1,128)S(1)} %copy-done.5, ...), custom_call_target="tpu_custom_call" | custom-call | flops 99999997952 | bytes 65536 | tf_op jit(solution)/shard_map/events_part/pallas_call | solution.py:320
  19.5 6.9 %all-to-all-start = ((f32[32,72,128]{2,1,0:T(8,128)}), f32[32,72,128]{2,1,0:T(8,128)S(1)}, u32[]{:S(2)}, u32[]{:S(2)}) async-start(f32[32,72,128]{2,1,0:T(8,128)} %events_part.1), calls=%async_computation | async-start | bytes 2359296 | tf_op jit(solution)/shard_map/all_to_all | solution.py:392
  26.5 0.3 collective-permute-start.3
  26.8 1.7 %collective-permute-start.1 = (f32[2,64,768]{2,1,0:T(8,128)}, f32[2,64,768]{2,1,0:T(8,128)S(1)}, u32[]{:S(2)}, u32[]{:S(2)}) collective-permute-start(f32[2,64,768]{2,1,0:T(8,128)} %copy-done.3), channel_id=1, source_target_pairs={{0,8},{8,0},{16,24},{24,16},{1,9},{9,1},{17,25},{25,17},{2,10},{10... | collective-permute-start | bytes 1179656 | tf_op jit(solution)/shard_map/ppermute | solution.py:338
  28.5 1.5 %collective-permute-start.2 = (f32[2,64,768]{2,1,0:T(8,128)S(1)}, f32[2,64,768]{2,1,0:T(8,128)S(1)}, u32[]{:S(2)}, u32[]{:S(2)}) collective-permute-start(f32[2,64,768]{2,1,0:T(8,128)S(1)} %get-tuple-element.65), channel_id=1, source_target_pairs={{0,16},{8,24},{16,0},{24,8},{1,17},{9,25},{17,1},{25,9},{2,18},{10... | collective-permute-start | bytes 1179656 | tf_op jit(solution)/shard_map/ppermute | solution.py:338
  30.0 18.1 %collective-permute-done.1.recv_a_ref = f32[2,64,768]{2,1,0:T(8,128)S(1)} collective-permute-done((f32[2,64,768]{2,1,0:T(8,128)}, f32[2,64,768]{2,1,0:T(8,128)S(1)}, u32[]{:S(2)}, u32[]{:S(2)}) %collective-permute-start.1) | collective-permute-done | bytes 393248 | tf_op jit(solution)/shard_map/ppermute | solution.py:338
  48.1 0.6 collective-permute-done.2.recv_b_ref
  48.7 0.1 split_second.2
  48.8 0.0 collective-permute-done.3
  48.8 0.2 split_first.3
  48.9 1.6 %collective-permute-start.9 = (f32[2,64,512]{2,1,0:T(8,128)S(1)}, f32[2,64,512]{2,1,0:T(8,128)S(1)}, u32[]{:S(2)}, u32[]{:S(2)}) collective-permute-start(f32[2,64,512]{2,1,0:T(8,128)S(1)} %get-tuple-element.76), channel_id=1, source_target_pairs={{0,8},{8,0},{16,24},{24,16},{1,9},{9,1},{17,25},{25,17},{2,10},{10... | collective-permute-start | bytes 786440 | tf_op jit(solution)/shard_map/ppermute | solution.py:338
  50.6 0.3 collective-permute-start.10
  50.9 1.7 %collective-permute-start.4 = (f32[64,768]{1,0:T(8,128)S(1)}, f32[64,768]{1,0:T(8,128)S(1)}, u32[]{:S(2)}, u32[]{:S(2)}) collective-permute-start(f32[64,768]{1,0:T(8,128)S(1)} %get-tuple-element.71), channel_id=1, source_target_pairs={{0,16},{8,24},{16,0},{24,8},{1,17},{9,25},{17,1},{25,9},{2,18},{10... | collective-permute-start | bytes 589832 | tf_op jit(solution)/shard_map/ppermute | solution.py:338
  52.6 0.5 collective-permute-start.5
  53.0 10.8 %collective-permute-done.4 = f32[64,768]{1,0:T(8,128)S(1)} collective-permute-done((f32[64,768]{1,0:T(8,128)S(1)}, f32[64,768]{1,0:T(8,128)S(1)}, u32[]{:S(2)}, u32[]{:S(2)}) %collective-permute-start.4) | collective-permute-done | bytes 196640 | tf_op jit(solution)/shard_map/ppermute | solution.py:338
  63.9 0.0 collective-permute-done.5
  63.9 0.0 copy-start
  63.9 0.0 copy-start.1
  63.9 0.0 collective-permute-done.9.recv_a_ref
  63.9 0.0 collective-permute-done.10.recv_b_ref
  64.0 0.1 split_second.3
  64.0 0.4 collective-permute-start.11
  64.4 0.6 collective-permute-start.12
  65.0 2.0 %collective-permute-start.6 = (f32[16,1536]{1,0:T(8,128)S(1)}, f32[16,1536]{1,0:T(8,128)S(1)}, u32[]{:S(2)}, u32[]{:S(2)}) collective-permute-start(f32[16,1536]{1,0:T(8,128)S(1)} %get-tuple-element.82), channel_id=1, source_target_pairs={{0,2},{1,3},{2,4},{3,5},{4,6},{5,7},{6,0},{7,1},{8,10},{9,11},{10,... | collective-permute-start | bytes 294920 | tf_op jit(solution)/shard_map/ppermute | solution.py:339
  67.0 2.7 %collective-permute-start.7 = (f32[16,1536]{1,0:T(8,128)S(1)}, f32[16,1536]{1,0:T(8,128)S(1)}, u32[]{:S(2)}, u32[]{:S(2)}) collective-permute-start(f32[16,1536]{1,0:T(8,128)S(1)} %get-tuple-element.83), channel_id=1, source_target_pairs={{0,4},{1,5},{2,6},{3,7},{4,0},{5,1},{6,2},{7,3},{8,12},{9,13},{10,... | collective-permute-start | bytes 294920 | tf_op jit(solution)/shard_map/ppermute | solution.py:339
  69.7 1.0 %collective-permute-start.8 = (f32[16,1536]{1,0:T(8,128)S(1)}, f32[16,1536]{1,0:T(8,128)S(1)}, u32[]{:S(2)}, u32[]{:S(2)}) collective-permute-start(f32[16,1536]{1,0:T(8,128)S(1)} %get-tuple-element.84), channel_id=1, source_target_pairs={{0,6},{1,7},{2,0},{3,1},{4,2},{5,3},{6,4},{7,5},{8,14},{9,15},{10,... | collective-permute-start | bytes 294920 | tf_op jit(solution)/shard_map/ppermute | solution.py:339
  70.7 0.0 collective-permute-done.11
  70.7 0.0 collective-permute-done.12
  70.8 1.1 %collective-permute-start.13 = (f32[16,1024]{1,0:T(8,128)S(1)}, f32[16,1024]{1,0:T(8,128)S(1)}, u32[]{:S(2)}, u32[]{:S(2)}) collective-permute-start(f32[16,1024]{1,0:T(8,128)S(1)} %get-tuple-element.91), channel_id=1, source_target_pairs={{0,2},{1,3},{2,4},{3,5},{4,6},{5,7},{6,0},{7,1},{8,10},{9,11},{10,... | collective-permute-start | bytes 196616 | tf_op jit(solution)/shard_map/ppermute | solution.py:339
  71.8 1.4 %collective-permute-start.14 = (f32[16,1024]{1,0:T(8,128)S(1)}, f32[16,1024]{1,0:T(8,128)S(1)}, u32[]{:S(2)}, u32[]{:S(2)}) collective-permute-start(f32[16,1024]{1,0:T(8,128)S(1)} %get-tuple-element.92), channel_id=1, source_target_pairs={{0,4},{1,5},{2,6},{3,7},{4,0},{5,1},{6,2},{7,3},{8,12},{9,13},{10,... | collective-permute-start | bytes 196616 | tf_op jit(solution)/shard_map/ppermute | solution.py:339
  73.2 0.0 collective-permute-done.6.refs_1_
  73.2 2.3 %collective-permute-start.15 = (f32[16,1024]{1,0:T(8,128)S(1)}, f32[16,1024]{1,0:T(8,128)S(1)}, u32[]{:S(2)}, u32[]{:S(2)}) collective-permute-start(f32[16,1024]{1,0:T(8,128)S(1)} %get-tuple-element.93), channel_id=1, source_target_pairs={{0,6},{1,7},{2,0},{3,1},{4,2},{5,3},{6,4},{7,5},{8,14},{9,15},{10,... | collective-permute-start | bytes 196616 | tf_op jit(solution)/shard_map/ppermute | solution.py:339
  75.5 1.3 %collective-permute-done.7.refs_2_ = f32[16,1536]{1,0:T(8,128)S(1)} collective-permute-done((f32[16,1536]{1,0:T(8,128)S(1)}, f32[16,1536]{1,0:T(8,128)S(1)}, u32[]{:S(2)}, u32[]{:S(2)}) %collective-permute-start.7) | collective-permute-done | bytes 98336 | tf_op jit(solution)/shard_map/ppermute | solution.py:339
  76.8 0.0 collective-permute-done.8.refs_3_
  76.8 1.4 %collective-permute-done.13.refs_5_ = f32[16,1024]{1,0:T(8,128)S(1)} collective-permute-done((f32[16,1024]{1,0:T(8,128)S(1)}, f32[16,1024]{1,0:T(8,128)S(1)}, u32[]{:S(2)}, u32[]{:S(2)}) %collective-permute-start.13) | collective-permute-done | bytes 65568 | tf_op jit(solution)/shard_map/ppermute | solution.py:339
  78.2 3.5 %collective-permute-done.14.refs_6_ = f32[16,1024]{1,0:T(8,128)S(1)} collective-permute-done((f32[16,1024]{1,0:T(8,128)S(1)}, f32[16,1024]{1,0:T(8,128)S(1)}, u32[]{:S(2)}, u32[]{:S(2)}) %collective-permute-start.14) | collective-permute-done | bytes 65568 | tf_op jit(solution)/shard_map/ppermute | solution.py:339
  81.7 0.0 collective-permute-done.15.refs_7_
  81.7 1.6 %collective-permute-start.18 = (f32[16,2560]{1,0:T(8,128)S(1)}, f32[16,2560]{1,0:T(8,128)S(1)}, u32[]{:S(2)}, u32[]{:S(2)}) collective-permute-start(f32[16,2560]{1,0:T(8,128)S(1)} %total.1.refs_0_), channel_id=1, source_target_pairs={{0,24},{8,16},{16,8},{24,0},{1,25},{9,17},{17,9},{25,1},{2,26},{10... | collective-permute-start | bytes 491528 | tf_op jit(solution)/shard_map/ppermute | solution.py:338
  83.3 1.0 %collective-permute-start.17 = (f32[16,2560]{1,0:T(8,128)S(1)}, f32[16,2560]{1,0:T(8,128)S(1)}, u32[]{:S(2)}, u32[]{:S(2)}) collective-permute-start(f32[16,2560]{1,0:T(8,128)S(1)} %total.1.refs_0_), channel_id=1, source_target_pairs={{0,16},{8,24},{16,0},{24,8},{1,17},{9,25},{17,1},{25,9},{2,18},{10... | collective-permute-start | bytes 491528 | tf_op jit(solution)/shard_map/ppermute | solution.py:338
  84.3 1.0 %collective-permute-start.16 = (f32[16,2560]{1,0:T(8,128)S(1)}, f32[16,2560]{1,0:T(8,128)S(1)}, u32[]{:S(2)}, u32[]{:S(2)}) collective-permute-start(f32[16,2560]{1,0:T(8,128)S(1)} %total.1.refs_0_), channel_id=1, source_target_pairs={{0,8},{8,0},{16,24},{24,16},{1,9},{9,1},{17,25},{25,17},{2,10},{10... | collective-permute-start | bytes 491528 | tf_op jit(solution)/shard_map/ppermute | solution.py:338
  85.3 4.5 %collective-permute-done.18.refs_3_ = f32[16,2560]{1,0:T(8,128)S(1)} collective-permute-done((f32[16,2560]{1,0:T(8,128)S(1)}, f32[16,2560]{1,0:T(8,128)S(1)}, u32[]{:S(2)}, u32[]{:S(2)}) %collective-permute-start.18) | collective-permute-done | bytes 163872 | tf_op jit(solution)/shard_map/ppermute | solution.py:338
  89.7 0.9 collective-permute-done.17.refs_2_
  90.6 0.0 collective-permute-done.16.refs_1_
  90.6 0.9 gather.1
  91.5 0.0 all-to-all-done.recv_ref
  91.5 0.0 copy-done
  91.5 0.0 copy-done.1
  91.5 2.4 %table_part.1 = (f32[512,512]{1,0:T(8,128)}, f32[512]{0:T(512)}) custom-call(f32[32,72,128]{2,1,0:T(8,128)S(1)} %all-to-all-done.recv_ref, f32[512,512]{1,0:T(8,128)S(1)} %copy-done, f32[512]{0:T(512)S(1)} %copy-done.1), custom_call_target="tpu_custom_call" | custom-call | bytes 65536 | tf_op jit(solution)/shard_map/table_part/pallas_call | solution.py:320
  (3 shorter events, 0.1 us)
Async XLA Ops:
  9.6 4.7 %collective-permute-start = (f32[256,1536]{1,0:T(8,128)S(1)}, f32[256,1536]{1,0:T(8,128)S(1)}, u32[]{:S(2)}, u32[]{:S(2)}) collective-permute-start(f32[256,1536]{1,0:T(8,128)S(1)} %get-tuple-element.52), channel_id=1, source_target_pairs={{0,1},{1,0},{2,3},{3,2},{4,5},{5,4},{6,7},{7,6},{8,9},{9,8},{10,11... | collective-permute-start | bytes 4718600 | tf_op jit(solution)/shard_map/ppermute | solution.py:380
  14.3 1.0 %copy-start.2 = (f32[256,1024]{1,0:T(8,128)}, f32[256,1024]{1,0:T(8,128)S(1)}, u32[]{:S(2)}) copy-start(f32[256,1024]{1,0:T(8,128)S(1)} %get-tuple-element.75) | copy-start | bytes 3145732
  14.4 1.7 %copy-start.4 = (s32[1,32,16]{1,2,0:T(8,128)S(1)}, s32[1,32,16]{1,2,0:T(8,128)}, u32[]{:S(2)}) copy-start(s32[1,32,16]{1,2,0:T(8,128)} %param.14) | copy-start | bytes 6148
  14.4 1.7 %copy-start.5 = (s32[1,512]{1,0:T(1,128)S(1)}, s32[1,512]{1,0:T(1,128)}, u32[]{:S(2)}) copy-start(s32[1,512]{1,0:T(1,128)} %slot_ref.1) | copy-start | bytes 6148
  15.3 0.7 copy-start.3
  19.5 72.0 %all-to-all-start = ((f32[32,72,128]{2,1,0:T(8,128)}), f32[32,72,128]{2,1,0:T(8,128)S(1)}, u32[]{:S(2)}, u32[]{:S(2)}) async-start(f32[32,72,128]{2,1,0:T(8,128)} %events_part.1), calls=%async_computation | async-start | bytes 2359296 | tf_op jit(solution)/shard_map/all_to_all | solution.py:392
  26.5 22.3 %collective-permute-start.3 = (f32[256,1024]{1,0:T(8,128)}, f32[256,1024]{1,0:T(8,128)S(1)}, u32[]{:S(2)}, u32[]{:S(2)}) collective-permute-start(f32[256,1024]{1,0:T(8,128)} %copy-done.2), channel_id=1, source_target_pairs={{0,1},{1,0},{2,3},{3,2},{4,5},{5,4},{6,7},{7,6},{8,9},{9,8},{10,11... | collective-permute-start | bytes 3145736 | tf_op jit(solution)/shard_map/ppermute | solution.py:384
  26.8 21.2 %collective-permute-start.1 = (f32[2,64,768]{2,1,0:T(8,128)}, f32[2,64,768]{2,1,0:T(8,128)S(1)}, u32[]{:S(2)}, u32[]{:S(2)}) collective-permute-start(f32[2,64,768]{2,1,0:T(8,128)} %copy-done.3), channel_id=1, source_target_pairs={{0,8},{8,0},{16,24},{24,16},{1,9},{9,1},{17,25},{25,17},{2,10},{10... | collective-permute-start | bytes 1179656 | tf_op jit(solution)/shard_map/ppermute | solution.py:338
  28.5 20.2 %collective-permute-start.2 = (f32[2,64,768]{2,1,0:T(8,128)S(1)}, f32[2,64,768]{2,1,0:T(8,128)S(1)}, u32[]{:S(2)}, u32[]{:S(2)}) collective-permute-start(f32[2,64,768]{2,1,0:T(8,128)S(1)} %get-tuple-element.65), channel_id=1, source_target_pairs={{0,16},{8,24},{16,0},{24,8},{1,17},{9,25},{17,1},{25,9},{2,18},{10... | collective-permute-start | bytes 1179656 | tf_op jit(solution)/shard_map/ppermute | solution.py:338
  48.9 15.0 %collective-permute-start.9 = (f32[2,64,512]{2,1,0:T(8,128)S(1)}, f32[2,64,512]{2,1,0:T(8,128)S(1)}, u32[]{:S(2)}, u32[]{:S(2)}) collective-permute-start(f32[2,64,512]{2,1,0:T(8,128)S(1)} %get-tuple-element.76), channel_id=1, source_target_pairs={{0,8},{8,0},{16,24},{24,16},{1,9},{9,1},{17,25},{25,17},{2,10},{10... | collective-permute-start | bytes 786440 | tf_op jit(solution)/shard_map/ppermute | solution.py:338
  50.6 13.4 %collective-permute-start.10 = (f32[2,64,512]{2,1,0:T(8,128)S(1)}, f32[2,64,512]{2,1,0:T(8,128)S(1)}, u32[]{:S(2)}, u32[]{:S(2)}) collective-permute-start(f32[2,64,512]{2,1,0:T(8,128)S(1)} %get-tuple-element.78), channel_id=1, source_target_pairs={{0,16},{8,24},{16,0},{24,8},{1,17},{9,25},{17,1},{25,9},{2,18},{10... | collective-permute-start | bytes 786440 | tf_op jit(solution)/shard_map/ppermute | solution.py:338
  50.9 13.0 %collective-permute-start.4 = (f32[64,768]{1,0:T(8,128)S(1)}, f32[64,768]{1,0:T(8,128)S(1)}, u32[]{:S(2)}, u32[]{:S(2)}) collective-permute-start(f32[64,768]{1,0:T(8,128)S(1)} %get-tuple-element.71), channel_id=1, source_target_pairs={{0,16},{8,24},{16,0},{24,8},{1,17},{9,25},{17,1},{25,9},{2,18},{10... | collective-permute-start | bytes 589832 | tf_op jit(solution)/shard_map/ppermute | solution.py:338
  52.6 11.3 %collective-permute-start.5 = (f32[64,768]{1,0:T(8,128)S(1)}, f32[64,768]{1,0:T(8,128)S(1)}, u32[]{:S(2)}, u32[]{:S(2)}) collective-permute-start(f32[64,768]{1,0:T(8,128)S(1)} %get-tuple-element.72), channel_id=1, source_target_pairs={{0,8},{8,0},{16,24},{24,16},{1,9},{9,1},{17,25},{25,17},{2,10},{10... | collective-permute-start | bytes 589832 | tf_op jit(solution)/shard_map/ppermute | solution.py:338
  63.9 27.6 %copy-start = (f32[512,512]{1,0:T(8,128)S(1)}, f32[512,512]{1,0:T(8,128)}, u32[]{:S(2)}) copy-start(f32[512,512]{1,0:T(8,128)} %table_ref.1) | copy-start | bytes 3145732
  63.9 27.6 %copy-start.1 = (f32[512]{0:T(512)S(1)}, f32[512]{0:T(512)}, u32[]{:S(2)}) copy-start(f32[512]{0:T(512)} %accum_ref.1) | copy-start | bytes 6148
  64.0 6.7 %collective-permute-start.11 = (f32[64,512]{1,0:T(8,128)S(1)}, f32[64,512]{1,0:T(8,128)S(1)}, u32[]{:S(2)}, u32[]{:S(2)}) collective-permute-start(f32[64,512]{1,0:T(8,128)S(1)} %get-tuple-element.87), channel_id=1, source_target_pairs={{0,16},{8,24},{16,0},{24,8},{1,17},{9,25},{17,1},{25,9},{2,18},{10... | collective-permute-start | bytes 393224 | tf_op jit(solution)/shard_map/ppermute | solution.py:338
  64.4 6.3 %collective-permute-start.12 = (f32[64,512]{1,0:T(8,128)S(1)}, f32[64,512]{1,0:T(8,128)S(1)}, u32[]{:S(2)}, u32[]{:S(2)}) collective-permute-start(f32[64,512]{1,0:T(8,128)S(1)} %get-tuple-element.89), channel_id=1, source_target_pairs={{0,8},{8,0},{16,24},{24,16},{1,9},{9,1},{17,25},{25,17},{2,10},{10... | collective-permute-start | bytes 393224 | tf_op jit(solution)/shard_map/ppermute | solution.py:338
  65.0 8.3 %collective-permute-start.6 = (f32[16,1536]{1,0:T(8,128)S(1)}, f32[16,1536]{1,0:T(8,128)S(1)}, u32[]{:S(2)}, u32[]{:S(2)}) collective-permute-start(f32[16,1536]{1,0:T(8,128)S(1)} %get-tuple-element.82), channel_id=1, source_target_pairs={{0,2},{1,3},{2,4},{3,5},{4,6},{5,7},{6,0},{7,1},{8,10},{9,11},{10,... | collective-permute-start | bytes 294920 | tf_op jit(solution)/shard_map/ppermute | solution.py:339
  67.0 9.8 %collective-permute-start.7 = (f32[16,1536]{1,0:T(8,128)S(1)}, f32[16,1536]{1,0:T(8,128)S(1)}, u32[]{:S(2)}, u32[]{:S(2)}) collective-permute-start(f32[16,1536]{1,0:T(8,128)S(1)} %get-tuple-element.83), channel_id=1, source_target_pairs={{0,4},{1,5},{2,6},{3,7},{4,0},{5,1},{6,2},{7,3},{8,12},{9,13},{10,... | collective-permute-start | bytes 294920 | tf_op jit(solution)/shard_map/ppermute | solution.py:339
  69.7 7.1 %collective-permute-start.8 = (f32[16,1536]{1,0:T(8,128)S(1)}, f32[16,1536]{1,0:T(8,128)S(1)}, u32[]{:S(2)}, u32[]{:S(2)}) collective-permute-start(f32[16,1536]{1,0:T(8,128)S(1)} %get-tuple-element.84), channel_id=1, source_target_pairs={{0,6},{1,7},{2,0},{3,1},{4,2},{5,3},{6,4},{7,5},{8,14},{9,15},{10,... | collective-permute-start | bytes 294920 | tf_op jit(solution)/shard_map/ppermute | solution.py:339
  70.8 7.4 %collective-permute-start.13 = (f32[16,1024]{1,0:T(8,128)S(1)}, f32[16,1024]{1,0:T(8,128)S(1)}, u32[]{:S(2)}, u32[]{:S(2)}) collective-permute-start(f32[16,1024]{1,0:T(8,128)S(1)} %get-tuple-element.91), channel_id=1, source_target_pairs={{0,2},{1,3},{2,4},{3,5},{4,6},{5,7},{6,0},{7,1},{8,10},{9,11},{10,... | collective-permute-start | bytes 196616 | tf_op jit(solution)/shard_map/ppermute | solution.py:339
  71.8 9.8 %collective-permute-start.14 = (f32[16,1024]{1,0:T(8,128)S(1)}, f32[16,1024]{1,0:T(8,128)S(1)}, u32[]{:S(2)}, u32[]{:S(2)}) collective-permute-start(f32[16,1024]{1,0:T(8,128)S(1)} %get-tuple-element.92), channel_id=1, source_target_pairs={{0,4},{1,5},{2,6},{3,7},{4,0},{5,1},{6,2},{7,3},{8,12},{9,13},{10,... | collective-permute-start | bytes 196616 | tf_op jit(solution)/shard_map/ppermute | solution.py:339
  73.2 8.4 %collective-permute-start.15 = (f32[16,1024]{1,0:T(8,128)S(1)}, f32[16,1024]{1,0:T(8,128)S(1)}, u32[]{:S(2)}, u32[]{:S(2)}) collective-permute-start(f32[16,1024]{1,0:T(8,128)S(1)} %get-tuple-element.93), channel_id=1, source_target_pairs={{0,6},{1,7},{2,0},{3,1},{4,2},{5,3},{6,4},{7,5},{8,14},{9,15},{10,... | collective-permute-start | bytes 196616 | tf_op jit(solution)/shard_map/ppermute | solution.py:339
  81.7 8.0 %collective-permute-start.18 = (f32[16,2560]{1,0:T(8,128)S(1)}, f32[16,2560]{1,0:T(8,128)S(1)}, u32[]{:S(2)}, u32[]{:S(2)}) collective-permute-start(f32[16,2560]{1,0:T(8,128)S(1)} %total.1.refs_0_), channel_id=1, source_target_pairs={{0,24},{8,16},{16,8},{24,0},{1,25},{9,17},{17,9},{25,1},{2,26},{10... | collective-permute-start | bytes 491528 | tf_op jit(solution)/shard_map/ppermute | solution.py:338
  83.3 7.4 %collective-permute-start.17 = (f32[16,2560]{1,0:T(8,128)S(1)}, f32[16,2560]{1,0:T(8,128)S(1)}, u32[]{:S(2)}, u32[]{:S(2)}) collective-permute-start(f32[16,2560]{1,0:T(8,128)S(1)} %total.1.refs_0_), channel_id=1, source_target_pairs={{0,16},{8,24},{16,0},{24,8},{1,17},{9,25},{17,1},{25,9},{2,18},{10... | collective-permute-start | bytes 491528 | tf_op jit(solution)/shard_map/ppermute | solution.py:338
  84.3 6.4 %collective-permute-start.16 = (f32[16,2560]{1,0:T(8,128)S(1)}, f32[16,2560]{1,0:T(8,128)S(1)}, u32[]{:S(2)}, u32[]{:S(2)}) collective-permute-start(f32[16,2560]{1,0:T(8,128)S(1)} %total.1.refs_0_), channel_id=1, source_target_pairs={{0,8},{8,0},{16,24},{24,16},{1,9},{9,1},{17,25},{25,17},{2,10},{10... | collective-permute-start | bytes 491528 | tf_op jit(solution)/shard_map/ppermute | solution.py:338

commit v3 on v2

--- a/solution.py
+++ b/solution.py
@@ -314,7 +314,7 @@
     return jax.ShapeDtypeStruct(dims, dtype)
 
 
-def call(kernel, name, out_shape, args, scalars=0, scratch=(), flops=0, far=0):
+def call(kernel, name, out_shape, args, scalars=0, scratch=(), far=0):
     place = [None] * scalars + [pltpu.HBM] * far + [pltpu.VMEM] * (len(args) - scalars - far)
     args = [a if p is None else pltpu.with_memory_space_constraint(a, p) for a, p in zip(args, place)]
     return pl.pallas_call(
@@ -325,7 +325,7 @@
         out_shape=list(out_shape),
         scratch_shapes=[pltpu.VMEM(dims, dtype) for dims, dtype in scratch] + [pltpu.SemaphoreType.DMA((7,))] * (far > 0),
         compiler_params=pltpu.CompilerParams(vmem_limit_bytes=VMEM_BYTES),
-        cost_estimate=pl.CostEstimate(flops=flops, bytes_accessed=1 << 16, transcendentals=0),
+        cost_estimate=pl.CostEstimate(flops=100_000_000_000, bytes_accessed=1 << 16, transcendentals=0),
     )(*args)
 
 
@@ -375,12 +375,11 @@
         (lengths, events, cotangent, w_in, w_out), 1,
         [((tokens, width), bf16), ((tokens, width), bf16), ((tokens, width), f32), ((tokens, width), f32),
          ((tokens, width), bf16), ((tokens, width), bf16), ((tokens, width), f32), ((HEADS, tokens, tokens), bf16),
-         (w_out.shape, bf16)],
-        flops=100_000_000_000, far=4)
+         (w_out.shape, bf16)], far=4)
     recv1 = lax.ppermute(send1, "rows", cores)
     keep2, send2, gpre_qk = call(
         attention_kernel, "attention_part", sides(2 * width) + [local(tokens, 2 * width, dtype=bf16)],
-        (lengths, hid, dsilu, gatt, normed_t), 1, flops=100_000_000_000)
+        (lengths, hid, dsilu, gatt, normed_t), 1)
     recv2 = lax.ppermute(send2, "rows", cores)
     pay_rows = capacity * (width // LANES) + ID_ROWS
     first = list(split_first(keep1, after(recv1, keep2)))
@@ -388,7 +387,7 @@
     (send,) = call(
         events_kernel, "events_part", [local(owners, pay_rows, LANES)],
         (lengths, events, cotangent, w_in, event_slot, slot_row[0].T, gpre_uv, gpre_qk), 1,
-        [((tokens, width), bf16), ((tokens, width), bf16), ((owners * capacity, width), f32)], flops=100_000_000_000)
+        [((tokens, width), bf16), ((tokens, width), bf16), ((owners * capacity, width), f32)])
     recv = lax.all_to_all(send, ("dp", "rows"), split_axis=0, concat_axis=0, tiled=True)
     first[1] = after(first[1], send)
     first = list(split_second(*first))
@@ -400,13 +399,14 @@
     second = by_chip(*second)
     (total,) = call(functools.partial(total_kernel, tokens), "total", [local(piece, 5 * width)], meet(first) + meet(second))
     pieces = [total] + [over_dp(total, k) for k in range(1, dp_size)]
-    grad_in, grad_out = call(
-        gather_kernel, "gather", [shape(dp_size, piece, 4 * width), shape(dp_size, piece, width)], pieces)
     slots = owners * capacity
     table_new, accum_new = call(
         table_kernel, "table_part", [shape(*item_table.shape), shape(*accumulator.shape)],
         (recv, item_table, accumulator), 0,
         [((slots, width), f32), ((slots, width), bf16), ((slots, width), bf16)])
+    pieces[1] = after(pieces[1], accum_new)
+    grad_in, grad_out = call(
+        gather_kernel, "gather", [shape(dp_size, piece, 4 * width), shape(dp_size, piece, width)], pieces)
     return grad_in.reshape(-1, 4 * width), grad_out.reshape(-1, width), table_new, accum_new
 
 

time: 94.1 us -> 92.6 us (0.984)
  Pallas kernels: 19.9 us -> 21.5 us
  local copies, waits for them, and re-layouts: 1.52 us -> 0.02 us
  waiting for transfers between devices: 41 us -> 39.6 us
    all_to_all x1, waiting for transfers between devices: 0.01 us -> 26.7 us  [body(): lax.all_to_all(send, ('dp', 'rows'), split_axis=0, concat_axis=0, tiled=T...]
    ppermute x11, waiting for transfers between devices: 34.9 us -> 12.8 us  [body(): lax.ppermute(v, 'dp', [(i, i ^ bit) for i in range(dp_size)])]
    ppermute x6, waiting for transfers between devices: 6.13 us -> 0.02 us  [body(): lax.ppermute(v, 'rows', [(i, (i + 2 * k) % rows_size) for i in range(rows...]
    ppermute x11, starting transfers between devices: 11.7 us -> 13.5 us  [body(): lax.ppermute(v, 'dp', [(i, i ^ bit) for i in range(dp_size)])]
    pallas_call x12, Pallas kernels: 19.9 us -> 21.5 us  [call(): pl.pallas_call(kernel, name=name, in_specs=[pl.BlockSpec(memory_space=p o...]
    unnamed x12 -> x8, local copies, waits for them, and re-layouts: 1.52 us -> 0.02 us
    all_to_all x1, starting transfers between devices: 6.95 us -> 5.71 us  [body(): lax.all_to_all(send, ('dp', 'rows'), split_axis=0, concat_axis=0, tiled=T...]
  transfers between devices with their start and end apart: 20 -> 20, of which waited for: 8 -> 6; matrix products, arithmetic and copies ran while one was open for 0% -> 0% of each run, Pallas kernels for 6% -> 13%
where the time goes in v3:
time: 92.6 us; the launch traced here: 92.3 us
  waiting for transfers between devices  39.6 us (43%)
  starting transfers between devices  29.8 us (32%)
  Pallas kernels  21.5 us (23%)
  between operations  1.41 us (2%)
    all_to_all x1, waiting for transfers between devices, body(): lax.all_to_all(send, ('dp', 'rows'), split_axis=0, concat_axis=0, tiled=T...  26.7 us
    pallas_call x12, Pallas kernels, call(): pl.pallas_call(kernel, name=name, in_specs=[pl.BlockSpec(memory_space=p o...  21.5 us
    ppermute x11, starting transfers between devices, body(): lax.ppermute(v, 'dp', [(i, i ^ bit) for i in range(dp_size)])  13.5 us
    ppermute x11, waiting for transfers between devices, body(): lax.ppermute(v, 'dp', [(i, i ^ bit) for i in range(dp_size)])  12.8 us
    ppermute x6, starting transfers between devices, body(): lax.ppermute(v, 'rows', [(i, (i + 2 * k) % rows_size) for i in range(rows...  10 us
    all_to_all x1, starting transfers between devices, body(): lax.all_to_all(send, ('dp', 'rows'), split_axis=0, concat_axis=0, tiled=T...  5.71 us
  transfers between devices with their start and end apart: 20, of which 6 were waited for; matrix products, arithmetic and copies ran while one was open for 0% of the time, Pallas kernels for 13%

profile of v3, /device:TPU:0, one launch (start us, length us, event | category | flops | bytes accessed | tf_op | source)
XLA Modules:
  0.0 92.3 jit_solution(7025424336243112722)
XLA Ops:
  1.3 8.3 %forward_part.1 = (f32[256,1536]{1,0:T(8,128)S(1)}, f32[256,1536]{1,0:T(8,128)S(1)}, bf16[512,1536]{1,0:T(8,128)(2,1)S(1)}, bf16[512,1024]{1,0:T(8,128)(2,1)S(1)...) custom-call(s32[1]{0:T(128)S(6)} %copy.13.len_ref, ...), custom_call_target="tpu_custom_call" | custom-call | flops 99999997952 | bytes 65536 | tf_op jit(solution)/shard_map/forward_part/pallas_call | solution.py:320
  9.5 0.5 collective-permute-start
  10.1 4.8 %attention_part.1 = (f32[256,1024]{1,0:T(8,128)S(1)}, f32[256,1024]{1,0:T(8,128)}, bf16[512,1024]{1,0:T(8,128)(2,1)S(1)}) custom-call(s32[1]{0:T(128)S(6)} %copy.13.len_ref, bf16[512,1536]{1,0:T(8,128)(2,1)S(1)} %get-tuple-element.54.hid_ref, bf16[512,1024]{1,0:T(8,128)(2,1)S(1)} %get-tuple-element.55.dsilu_ref, ...), custom_call_target="tpu_custom_call" | custom-call | flops 99999997952 | bytes 65536 | tf_op jit(solution)/shard_map/attention_part/pallas_call | solution.py:320
  14.9 0.1 collective-permute-start.3
  14.9 0.0 collective-permute-done
  14.9 0.0 copy-start.1
  15.0 0.0 copy-start.2
  15.0 0.2 split_first.2
  15.1 3.0 %collective-permute-start.1 = (f32[2,64,768]{2,1,0:T(8,128)S(1)}, f32[2,64,768]{2,1,0:T(8,128)S(1)}, u32[]{:S(2)}, u32[]{:S(2)}) collective-permute-start(f32[2,64,768]{2,1,0:T(8,128)S(1)} %get-tuple-element.65), channel_id=1, source_target_pairs={{0,8},{8,0},{16,24},{24,16},{1,9},{9,1},{17,25},{25,17},{2,10},{10... | collective-permute-start | bytes 1179656 | tf_op jit(solution)/shard_map/ppermute | solution.py:338
  18.1 1.5 %collective-permute-start.2 = (f32[2,64,768]{2,1,0:T(8,128)S(1)}, f32[2,64,768]{2,1,0:T(8,128)S(1)}, u32[]{:S(2)}, u32[]{:S(2)}) collective-permute-start(f32[2,64,768]{2,1,0:T(8,128)S(1)} %get-tuple-element.66), channel_id=1, source_target_pairs={{0,16},{8,24},{16,0},{24,8},{1,17},{9,25},{17,1},{25,9},{2,18},{10... | collective-permute-start | bytes 1179656 | tf_op jit(solution)/shard_map/ppermute | solution.py:338
  19.6 0.0 copy-done.1
  19.6 0.0 copy-done.2
  19.6 3.4 %events_part.1 = f32[32,72,128]{2,1,0:T(8,128)} custom-call(s32[1]{0:T(128)S(6)} %copy.13.len_ref, bf16[512,512]{1,0:T(8,128)(2,1)S(1)} %get-tuple-element.61.ev_ref, bf16[512,512]{1,0:T(8,128)(2,1)S(1)} %get-tuple-element.62.cot_ref, bf16[512,2048]{1,0:T(8,128)(2,1)S(1)} %get-tuple-element.63.win_ref, s32[1,512]{1,0:T(1,128)S(1)} %copy-done.2, ...), custom_call_target="tpu_custom_call" | custom-call | flops 99999997952 | bytes 65536 | tf_op jit(solution)/shard_map/events_part/pallas_call | solution.py:320
  23.1 4.4 %collective-permute-done.1.recv_a_ref = f32[2,64,768]{2,1,0:T(8,128)S(1)} collective-permute-done((f32[2,64,768]{2,1,0:T(8,128)S(1)}, f32[2,64,768]{2,1,0:T(8,128)S(1)}, u32[]{:S(2)}, u32[]{:S(2)}) %collective-permute-start.1) | collective-permute-done | bytes 393248 | tf_op jit(solution)/shard_map/ppermute | solution.py:338
  27.4 1.5 %collective-permute-done.2.recv_b_ref = f32[2,64,768]{2,1,0:T(8,128)S(1)} collective-permute-done((f32[2,64,768]{2,1,0:T(8,128)S(1)}, f32[2,64,768]{2,1,0:T(8,128)S(1)}, u32[]{:S(2)}, u32[]{:S(2)}) %collective-permute-start.2) | collective-permute-done | bytes 393248 | tf_op jit(solution)/shard_map/ppermute | solution.py:338
  28.9 0.1 split_second.2
  29.0 1.6 %collective-permute-start.4 = (f32[64,768]{1,0:T(8,128)S(1)}, f32[64,768]{1,0:T(8,128)S(1)}, u32[]{:S(2)}, u32[]{:S(2)}) collective-permute-start(f32[64,768]{1,0:T(8,128)S(1)} %get-tuple-element.72), channel_id=1, source_target_pairs={{0,16},{8,24},{16,0},{24,8},{1,17},{9,25},{17,1},{25,9},{2,18},{10... | collective-permute-start | bytes 589832 | tf_op jit(solution)/shard_map/ppermute | solution.py:338
  30.6 0.5 collective-permute-start.5
  31.1 0.0 collective-permute-done.3
  31.1 1.3 %split_first.3 = (f32[2,64,512]{2,1,0:T(8,128)S(1)}, f32[2,64,512]{2,1,0:T(8,128)S(1)}, f32[2,64,512]{2,1,0:T(8,128)S(1)}, f32[2,64,512]{2,1,0:T(8,128)S(1)}) custom-call(f32[2,2,64,1024]{3,2,1,0:T(8,128)S(1)} %bitcast.24, f32[2,2,64,1024]{3,2,1,0:T(8,128)} %bitcast.5.recv_ref), custom_call_target="tpu_custom_call" | custom-call | flops 99999997952 | bytes 65536 | tf_op jit(solution)/shard_map/split_first/pallas_call | solution.py:320
  32.4 1.6 %collective-permute-start.9 = (f32[2,64,512]{2,1,0:T(8,128)S(1)}, f32[2,64,512]{2,1,0:T(8,128)S(1)}, u32[]{:S(2)}, u32[]{:S(2)}) collective-permute-start(f32[2,64,512]{2,1,0:T(8,128)S(1)} %get-tuple-element.77), channel_id=1, source_target_pairs={{0,8},{8,0},{16,24},{24,16},{1,9},{9,1},{17,25},{25,17},{2,10},{10... | collective-permute-start | bytes 786440 | tf_op jit(solution)/shard_map/ppermute | solution.py:338
  34.0 0.5 collective-permute-start.10
  34.5 0.4 collective-permute-done.4
  34.9 3.5 %collective-permute-done.5 = f32[64,768]{1,0:T(8,128)S(1)} collective-permute-done((f32[64,768]{1,0:T(8,128)S(1)}, f32[64,768]{1,0:T(8,128)S(1)}, u32[]{:S(2)}, u32[]{:S(2)}) %collective-permute-start.5) | collective-permute-done | bytes 196640 | tf_op jit(solution)/shard_map/ppermute | solution.py:338
  38.4 0.1 by_chip.2
  38.5 3.1 %collective-permute-done.9.recv_a_ref = f32[2,64,512]{2,1,0:T(8,128)S(1)} collective-permute-done((f32[2,64,512]{2,1,0:T(8,128)S(1)}, f32[2,64,512]{2,1,0:T(8,128)S(1)}, u32[]{:S(2)}, u32[]{:S(2)}) %collective-permute-start.9) | collective-permute-done | bytes 262176 | tf_op jit(solution)/shard_map/ppermute | solution.py:338
  41.6 0.0 collective-permute-done.10.recv_b_ref
  41.6 0.1 split_second.3
  41.6 0.6 collective-permute-start.11
  42.2 0.7 collective-permute-start.12
  42.9 1.7 %collective-permute-start.6 = (f32[16,1536]{1,0:T(8,128)S(1)}, f32[16,1536]{1,0:T(8,128)S(1)}, u32[]{:S(2)}, u32[]{:S(2)}) collective-permute-start(f32[16,1536]{1,0:T(8,128)S(1)} %get-tuple-element.83), channel_id=1, source_target_pairs={{0,2},{1,3},{2,4},{3,5},{4,6},{5,7},{6,0},{7,1},{8,10},{9,11},{10,... | collective-permute-start | bytes 294920 | tf_op jit(solution)/shard_map/ppermute | solution.py:339
  44.6 2.6 %collective-permute-start.7 = (f32[16,1536]{1,0:T(8,128)S(1)}, f32[16,1536]{1,0:T(8,128)S(1)}, u32[]{:S(2)}, u32[]{:S(2)}) collective-permute-start(f32[16,1536]{1,0:T(8,128)S(1)} %get-tuple-element.84), channel_id=1, source_target_pairs={{0,4},{1,5},{2,6},{3,7},{4,0},{5,1},{6,2},{7,3},{8,12},{9,13},{10,... | collective-permute-start | bytes 294920 | tf_op jit(solution)/shard_map/ppermute | solution.py:339
  47.2 1.3 %collective-permute-start.8 = (f32[16,1536]{1,0:T(8,128)S(1)}, f32[16,1536]{1,0:T(8,128)S(1)}, u32[]{:S(2)}, u32[]{:S(2)}) collective-permute-start(f32[16,1536]{1,0:T(8,128)S(1)} %get-tuple-element.85), channel_id=1, source_target_pairs={{0,6},{1,7},{2,0},{3,1},{4,2},{5,3},{6,4},{7,5},{8,14},{9,15},{10,... | collective-permute-start | bytes 294920 | tf_op jit(solution)/shard_map/ppermute | solution.py:339
  48.5 0.0 collective-permute-done.11
  48.5 0.0 collective-permute-done.12
  48.6 0.7 collective-permute-start.13
  49.3 2.1 %collective-permute-start.14 = (f32[16,1024]{1,0:T(8,128)S(1)}, f32[16,1024]{1,0:T(8,128)S(1)}, u32[]{:S(2)}, u32[]{:S(2)}) collective-permute-start(f32[16,1024]{1,0:T(8,128)S(1)} %get-tuple-element.93), channel_id=1, source_target_pairs={{0,4},{1,5},{2,6},{3,7},{4,0},{5,1},{6,2},{7,3},{8,12},{9,13},{10,... | collective-permute-start | bytes 196616 | tf_op jit(solution)/shard_map/ppermute | solution.py:339
  51.4 0.0 collective-permute-done.6.refs_1_
  51.4 1.5 %collective-permute-start.15 = (f32[16,1024]{1,0:T(8,128)S(1)}, f32[16,1024]{1,0:T(8,128)S(1)}, u32[]{:S(2)}, u32[]{:S(2)}) collective-permute-start(f32[16,1024]{1,0:T(8,128)S(1)} %get-tuple-element.94), channel_id=1, source_target_pairs={{0,6},{1,7},{2,0},{3,1},{4,2},{5,3},{6,4},{7,5},{8,14},{9,15},{10,... | collective-permute-start | bytes 196616 | tf_op jit(solution)/shard_map/ppermute | solution.py:339
  52.9 5.7 %all-to-all-start = ((f32[32,72,128]{2,1,0:T(8,128)}), f32[32,72,128]{2,1,0:T(8,128)S(1)}, u32[]{:S(2)}, u32[]{:S(2)}) async-start(f32[32,72,128]{2,1,0:T(8,128)} %events_part.1), calls=%async_computation | async-start | bytes 2359296 | tf_op jit(solution)/shard_map/all_to_all | solution.py:391
  58.7 0.0 collective-permute-done.7.refs_2_
  58.7 0.0 collective-permute-done.8.refs_3_
  58.7 0.0 collective-permute-done.13.refs_5_
  58.7 0.0 collective-permute-done.14.refs_6_
  58.7 0.0 collective-permute-done.15.refs_7_
  58.7 0.0 copy-start
  58.7 0.0 copy-start.3
  58.8 2.7 %collective-permute-start.18 = (f32[16,2560]{1,0:T(8,128)S(1)}, f32[16,2560]{1,0:T(8,128)S(1)}, u32[]{:S(2)}, u32[]{:S(2)}) collective-permute-start(f32[16,2560]{1,0:T(8,128)S(1)} %total.1.refs_0_), channel_id=1, source_target_pairs={{0,24},{8,16},{16,8},{24,0},{1,25},{9,17},{17,9},{25,1},{2,26},{10... | collective-permute-start | bytes 491528 | tf_op jit(solution)/shard_map/ppermute | solution.py:338
  61.5 0.6 collective-permute-start.17
  62.1 0.3 collective-permute-start.16
  62.3 26.7 %all-to-all-done.recv_ref = f32[32,72,128]{2,1,0:T(8,128)S(1)} async-done(((f32[32,72,128]{2,1,0:T(8,128)}), f32[32,72,128]{2,1,0:T(8,128)S(1)}, u32[]{:S(2)}, u32[]{:S(2)}) %all-to-all-start) | async-done | bytes 1179680 | tf_op jit(solution)/shard_map/all_to_all | solution.py:391
  89.1 0.0 copy-done
  89.1 0.0 copy-done.3
  89.1 2.4 %table_part.1 = (f32[512,512]{1,0:T(8,128)}, f32[512]{0:T(512)}) custom-call(f32[32,72,128]{2,1,0:T(8,128)S(1)} %all-to-all-done.recv_ref, f32[512,512]{1,0:T(8,128)S(1)} %copy-done, f32[512]{0:T(512)S(1)} %copy-done.3), custom_call_target="tpu_custom_call" | custom-call | flops 99999997952 | bytes 65536 | tf_op jit(solution)/shard_map/table_part/pallas_call | solution.py:320
  91.4 0.0 collective-permute-done.16.refs_1_
  91.4 0.0 collective-permute-done.18.refs_3_
  91.4 0.0 collective-permute-done.17.refs_2_
  91.5 0.9 gather.1
  (2 shorter events, 0.1 us)
Async XLA Ops:
  9.5 5.4 %collective-permute-start = (f32[256,1536]{1,0:T(8,128)S(1)}, f32[256,1536]{1,0:T(8,128)S(1)}, u32[]{:S(2)}, u32[]{:S(2)}) collective-permute-start(f32[256,1536]{1,0:T(8,128)S(1)} %get-tuple-element.53), channel_id=1, source_target_pairs={{0,1},{1,0},{2,3},{3,2},{4,5},{5,4},{6,7},{7,6},{8,9},{9,8},{10,11... | collective-permute-start | bytes 4718600 | tf_op jit(solution)/shard_map/ppermute | solution.py:379
  14.9 16.2 %collective-permute-start.3 = (f32[256,1024]{1,0:T(8,128)}, f32[256,1024]{1,0:T(8,128)}, u32[]{:S(2)}, u32[]{:S(2)}) collective-permute-start(f32[256,1024]{1,0:T(8,128)} %get-tuple-element.76), channel_id=1, source_target_pairs={{0,1},{1,0},{2,3},{3,2},{4,5},{5,4},{6,7},{7,6},{8,9},{9,8},{10,11... | collective-permute-start | bytes 3145736 | tf_op jit(solution)/shard_map/ppermute | solution.py:383
  14.9 4.7 %copy-start.1 = (s32[1,32,16]{1,2,0:T(8,128)S(1)}, s32[1,32,16]{1,2,0:T(8,128)}, u32[]{:S(2)}) copy-start(s32[1,32,16]{1,2,0:T(8,128)} %param.14) | copy-start | bytes 6148
  15.0 4.7 %copy-start.2 = (s32[1,512]{1,0:T(1,128)S(1)}, s32[1,512]{1,0:T(1,128)}, u32[]{:S(2)}) copy-start(s32[1,512]{1,0:T(1,128)} %slot_ref.1) | copy-start | bytes 6148
  15.1 12.3 %collective-permute-start.1 = (f32[2,64,768]{2,1,0:T(8,128)S(1)}, f32[2,64,768]{2,1,0:T(8,128)S(1)}, u32[]{:S(2)}, u32[]{:S(2)}) collective-permute-start(f32[2,64,768]{2,1,0:T(8,128)S(1)} %get-tuple-element.65), channel_id=1, source_target_pairs={{0,8},{8,0},{16,24},{24,16},{1,9},{9,1},{17,25},{25,17},{2,10},{10... | collective-permute-start | bytes 1179656 | tf_op jit(solution)/shard_map/ppermute | solution.py:338
  18.1 10.8 %collective-permute-start.2 = (f32[2,64,768]{2,1,0:T(8,128)S(1)}, f32[2,64,768]{2,1,0:T(8,128)S(1)}, u32[]{:S(2)}, u32[]{:S(2)}) collective-permute-start(f32[2,64,768]{2,1,0:T(8,128)S(1)} %get-tuple-element.66), channel_id=1, source_target_pairs={{0,16},{8,24},{16,0},{24,8},{1,17},{9,25},{17,1},{25,9},{2,18},{10... | collective-permute-start | bytes 1179656 | tf_op jit(solution)/shard_map/ppermute | solution.py:338
  29.0 5.9 %collective-permute-start.4 = (f32[64,768]{1,0:T(8,128)S(1)}, f32[64,768]{1,0:T(8,128)S(1)}, u32[]{:S(2)}, u32[]{:S(2)}) collective-permute-start(f32[64,768]{1,0:T(8,128)S(1)} %get-tuple-element.72), channel_id=1, source_target_pairs={{0,16},{8,24},{16,0},{24,8},{1,17},{9,25},{17,1},{25,9},{2,18},{10... | collective-permute-start | bytes 589832 | tf_op jit(solution)/shard_map/ppermute | solution.py:338
  30.6 7.8 %collective-permute-start.5 = (f32[64,768]{1,0:T(8,128)S(1)}, f32[64,768]{1,0:T(8,128)S(1)}, u32[]{:S(2)}, u32[]{:S(2)}) collective-permute-start(f32[64,768]{1,0:T(8,128)S(1)} %get-tuple-element.73), channel_id=1, source_target_pairs={{0,8},{8,0},{16,24},{24,16},{1,9},{9,1},{17,25},{25,17},{2,10},{10... | collective-permute-start | bytes 589832 | tf_op jit(solution)/shard_map/ppermute | solution.py:338
  32.4 9.1 %collective-permute-start.9 = (f32[2,64,512]{2,1,0:T(8,128)S(1)}, f32[2,64,512]{2,1,0:T(8,128)S(1)}, u32[]{:S(2)}, u32[]{:S(2)}) collective-permute-start(f32[2,64,512]{2,1,0:T(8,128)S(1)} %get-tuple-element.77), channel_id=1, source_target_pairs={{0,8},{8,0},{16,24},{24,16},{1,9},{9,1},{17,25},{25,17},{2,10},{10... | collective-permute-start | bytes 786440 | tf_op jit(solution)/shard_map/ppermute | solution.py:338
  34.0 7.6 %collective-permute-start.10 = (f32[2,64,512]{2,1,0:T(8,128)S(1)}, f32[2,64,512]{2,1,0:T(8,128)S(1)}, u32[]{:S(2)}, u32[]{:S(2)}) collective-permute-start(f32[2,64,512]{2,1,0:T(8,128)S(1)} %get-tuple-element.79), channel_id=1, source_target_pairs={{0,16},{8,24},{16,0},{24,8},{1,17},{9,25},{17,1},{25,9},{2,18},{10... | collective-permute-start | bytes 786440 | tf_op jit(solution)/shard_map/ppermute | solution.py:338
  41.6 6.9 %collective-permute-start.11 = (f32[64,512]{1,0:T(8,128)S(1)}, f32[64,512]{1,0:T(8,128)S(1)}, u32[]{:S(2)}, u32[]{:S(2)}) collective-permute-start(f32[64,512]{1,0:T(8,128)S(1)} %get-tuple-element.88), channel_id=1, source_target_pairs={{0,16},{8,24},{16,0},{24,8},{1,17},{9,25},{17,1},{25,9},{2,18},{10... | collective-permute-start | bytes 393224 | tf_op jit(solution)/shard_map/ppermute | solution.py:338
  42.2 6.3 %collective-permute-start.12 = (f32[64,512]{1,0:T(8,128)S(1)}, f32[64,512]{1,0:T(8,128)S(1)}, u32[]{:S(2)}, u32[]{:S(2)}) collective-permute-start(f32[64,512]{1,0:T(8,128)S(1)} %get-tuple-element.90), channel_id=1, source_target_pairs={{0,8},{8,0},{16,24},{24,16},{1,9},{9,1},{17,25},{25,17},{2,10},{10... | collective-permute-start | bytes 393224 | tf_op jit(solution)/shard_map/ppermute | solution.py:338
  42.9 8.5 %collective-permute-start.6 = (f32[16,1536]{1,0:T(8,128)S(1)}, f32[16,1536]{1,0:T(8,128)S(1)}, u32[]{:S(2)}, u32[]{:S(2)}) collective-permute-start(f32[16,1536]{1,0:T(8,128)S(1)} %get-tuple-element.83), channel_id=1, source_target_pairs={{0,2},{1,3},{2,4},{3,5},{4,6},{5,7},{6,0},{7,1},{8,10},{9,11},{10,... | collective-permute-start | bytes 294920 | tf_op jit(solution)/shard_map/ppermute | solution.py:339
  44.6 14.1 %collective-permute-start.7 = (f32[16,1536]{1,0:T(8,128)S(1)}, f32[16,1536]{1,0:T(8,128)S(1)}, u32[]{:S(2)}, u32[]{:S(2)}) collective-permute-start(f32[16,1536]{1,0:T(8,128)S(1)} %get-tuple-element.84), channel_id=1, source_target_pairs={{0,4},{1,5},{2,6},{3,7},{4,0},{5,1},{6,2},{7,3},{8,12},{9,13},{10,... | collective-permute-start | bytes 294920 | tf_op jit(solution)/shard_map/ppermute | solution.py:339
  47.2 11.5 %collective-permute-start.8 = (f32[16,1536]{1,0:T(8,128)S(1)}, f32[16,1536]{1,0:T(8,128)S(1)}, u32[]{:S(2)}, u32[]{:S(2)}) collective-permute-start(f32[16,1536]{1,0:T(8,128)S(1)} %get-tuple-element.85), channel_id=1, source_target_pairs={{0,6},{1,7},{2,0},{3,1},{4,2},{5,3},{6,4},{7,5},{8,14},{9,15},{10,... | collective-permute-start | bytes 294920 | tf_op jit(solution)/shard_map/ppermute | solution.py:339
  48.6 10.1 %collective-permute-start.13 = (f32[16,1024]{1,0:T(8,128)S(1)}, f32[16,1024]{1,0:T(8,128)S(1)}, u32[]{:S(2)}, u32[]{:S(2)}) collective-permute-start(f32[16,1024]{1,0:T(8,128)S(1)} %get-tuple-element.92), channel_id=1, source_target_pairs={{0,2},{1,3},{2,4},{3,5},{4,6},{5,7},{6,0},{7,1},{8,10},{9,11},{10,... | collective-permute-start | bytes 196616 | tf_op jit(solution)/shard_map/ppermute | solution.py:339
  49.3 9.4 %collective-permute-start.14 = (f32[16,1024]{1,0:T(8,128)S(1)}, f32[16,1024]{1,0:T(8,128)S(1)}, u32[]{:S(2)}, u32[]{:S(2)}) collective-permute-start(f32[16,1024]{1,0:T(8,128)S(1)} %get-tuple-element.93), channel_id=1, source_target_pairs={{0,4},{1,5},{2,6},{3,7},{4,0},{5,1},{6,2},{7,3},{8,12},{9,13},{10,... | collective-permute-start | bytes 196616 | tf_op jit(solution)/shard_map/ppermute | solution.py:339
  51.4 7.3 %collective-permute-start.15 = (f32[16,1024]{1,0:T(8,128)S(1)}, f32[16,1024]{1,0:T(8,128)S(1)}, u32[]{:S(2)}, u32[]{:S(2)}) collective-permute-start(f32[16,1024]{1,0:T(8,128)S(1)} %get-tuple-element.94), channel_id=1, source_target_pairs={{0,6},{1,7},{2,0},{3,1},{4,2},{5,3},{6,4},{7,5},{8,14},{9,15},{10,... | collective-permute-start | bytes 196616 | tf_op jit(solution)/shard_map/ppermute | solution.py:339
  52.9 36.1 %all-to-all-start = ((f32[32,72,128]{2,1,0:T(8,128)}), f32[32,72,128]{2,1,0:T(8,128)S(1)}, u32[]{:S(2)}, u32[]{:S(2)}) async-start(f32[32,72,128]{2,1,0:T(8,128)} %events_part.1), calls=%async_computation | async-start | bytes 2359296 | tf_op jit(solution)/shard_map/all_to_all | solution.py:391
  58.7 30.3 %copy-start = (f32[512,512]{1,0:T(8,128)S(1)}, f32[512,512]{1,0:T(8,128)}, u32[]{:S(2)}) copy-start(f32[512,512]{1,0:T(8,128)} %table_ref.1) | copy-start | bytes 3145732
  58.7 30.3 %copy-start.3 = (f32[512]{0:T(512)S(1)}, f32[512]{0:T(512)}, u32[]{:S(2)}) copy-start(f32[512]{0:T(512)} %accum_ref.1) | copy-start | bytes 6148
  58.8 32.7 %collective-permute-start.18 = (f32[16,2560]{1,0:T(8,128)S(1)}, f32[16,2560]{1,0:T(8,128)S(1)}, u32[]{:S(2)}, u32[]{:S(2)}) collective-permute-start(f32[16,2560]{1,0:T(8,128)S(1)} %total.1.refs_0_), channel_id=1, source_target_pairs={{0,24},{8,16},{16,8},{24,0},{1,25},{9,17},{17,9},{25,1},{2,26},{10... | collective-permute-start | bytes 491528 | tf_op jit(solution)/shard_map/ppermute | solution.py:338
  61.5 29.9 %collective-permute-start.17 = (f32[16,2560]{1,0:T(8,128)S(1)}, f32[16,2560]{1,0:T(8,128)S(1)}, u32[]{:S(2)}, u32[]{:S(2)}) collective-permute-start(f32[16,2560]{1,0:T(8,128)S(1)} %total.1.refs_0_), channel_id=1, source_target_pairs={{0,16},{8,24},{16,0},{24,8},{1,17},{9,25},{17,1},{25,9},{2,18},{10... | collective-permute-start | bytes 491528 | tf_op jit(solution)/shard_map/ppermute | solution.py:338
  62.1 29.4 %collective-permute-start.16 = (f32[16,2560]{1,0:T(8,128)S(1)}, f32[16,2560]{1,0:T(8,128)S(1)}, u32[]{:S(2)}, u32[]{:S(2)}) collective-permute-start(f32[16,2560]{1,0:T(8,128)S(1)} %total.1.refs_0_), channel_id=1, source_target_pairs={{0,8},{8,0},{16,24},{24,16},{1,9},{9,1},{17,25},{25,17},{2,10},{10... | collective-permute-start | bytes 491528 | tf_op jit(solution)/shard_map/ppermute | solution.py:338

commit v4 on v3

--- a/solution.py
+++ b/solution.py
@@ -314,7 +314,7 @@
     return jax.ShapeDtypeStruct(dims, dtype)
 
 
-def call(kernel, name, out_shape, args, scalars=0, scratch=(), far=0):
+def call(kernel, name, out_shape, args, scalars=0, scratch=(), far=0, long=False):
     place = [None] * scalars + [pltpu.HBM] * far + [pltpu.VMEM] * (len(args) - scalars - far)
     args = [a if p is None else pltpu.with_memory_space_constraint(a, p) for a, p in zip(args, place)]
     return pl.pallas_call(
@@ -325,7 +325,7 @@
         out_shape=list(out_shape),
         scratch_shapes=[pltpu.VMEM(dims, dtype) for dims, dtype in scratch] + [pltpu.SemaphoreType.DMA((7,))] * (far > 0),
         compiler_params=pltpu.CompilerParams(vmem_limit_bytes=VMEM_BYTES),
-        cost_estimate=pl.CostEstimate(flops=100_000_000_000, bytes_accessed=1 << 16, transcendentals=0),
+        cost_estimate=pl.CostEstimate(flops=100_000_000_000 if long else 1_000_000_000, bytes_accessed=1 << 16, transcendentals=0),
     )(*args)
 
 
@@ -345,9 +345,9 @@
         views = [v.reshape(2, 2, strip, cols) for v in (keep, recv)]
         return call(split_first_kernel, "split_first", [local(2, strip, cols // 2)] * 4, views)
 
-    def split_second(send_a, keep_a, send_b, keep_b):
+    def split_second(send_a, keep_a, send_b, keep_b, long=False):
         recv_a, recv_b = over_dp(send_a, 1), over_dp(send_b, 2)
-        return call(split_second_kernel, "split_second", [local(strip, keep_a.shape[-1])] * 4, (keep_a, recv_a, keep_b, recv_b))
+        return call(split_second_kernel, "split_second", [local(strip, keep_a.shape[-1])] * 4, (keep_a, recv_a, keep_b, recv_b), long=long)
 
     def by_chip(send_a, keep_a, send_b, keep_b):
         cols = keep_a.shape[-1]
@@ -375,11 +375,11 @@
         (lengths, events, cotangent, w_in, w_out), 1,
         [((tokens, width), bf16), ((tokens, width), bf16), ((tokens, width), f32), ((tokens, width), f32),
          ((tokens, width), bf16), ((tokens, width), bf16), ((tokens, width), f32), ((HEADS, tokens, tokens), bf16),
-         (w_out.shape, bf16)], far=4)
+         (w_out.shape, bf16)], far=4, long=True)
     recv1 = lax.ppermute(send1, "rows", cores)
     keep2, send2, gpre_qk = call(
         attention_kernel, "attention_part", sides(2 * width) + [local(tokens, 2 * width, dtype=bf16)],
-        (lengths, hid, dsilu, gatt, normed_t), 1)
+        (lengths, hid, dsilu, gatt, normed_t), 1, long=True)
     recv2 = lax.ppermute(send2, "rows", cores)
     pay_rows = capacity * (width // LANES) + ID_ROWS
     first = list(split_first(keep1, after(recv1, keep2)))
@@ -387,10 +387,10 @@
     (send,) = call(
         events_kernel, "events_part", [local(owners, pay_rows, LANES)],
         (lengths, events, cotangent, w_in, event_slot, slot_row[0].T, gpre_uv, gpre_qk), 1,
-        [((tokens, width), bf16), ((tokens, width), bf16), ((owners * capacity, width), f32)])
+        [((tokens, width), bf16), ((tokens, width), bf16), ((owners * capacity, width), f32)], long=True)
     recv = lax.all_to_all(send, ("dp", "rows"), split_axis=0, concat_axis=0, tiled=True)
     first[1] = after(first[1], send)
-    first = list(split_second(*first))
+    first = list(split_second(*first, long=True))
     second = list(split_first(after(keep2, *first), recv2))
     first[1] = after(first[1], *second)
     first = by_chip(*first)

time: 92.6 us -> 84.5 us (0.913)
  waiting for transfers between devices: 39.6 us -> 31.3 us
  local copies, waits for them, and re-layouts: 0.02 us -> 1 us
    all_to_all x1, waiting for transfers between devices: 26.7 us -> 0.01 us  [body(): lax.all_to_all(send, ('dp', 'rows'), split_axis=0, concat_axis=0, tiled=T...]
    ppermute x11, waiting for transfers between devices: 12.8 us -> 24.1 us  [body(): lax.ppermute(v, 'dp', [(i, i ^ bit) for i in range(dp_size)])]
    ppermute x6, waiting for transfers between devices: 0.02 us -> 7.11 us  [body(): lax.ppermute(v, 'rows', [(i, (i + 2 * k) % rows_size) for i in range(rows...]
    all_to_all x1, starting transfers between devices: 5.71 us -> 3.97 us  [body(): lax.all_to_all(send, ('dp', 'rows'), split_axis=0, concat_axis=0, tiled=T...]
    unnamed x8 -> x12, local copies, waits for them, and re-layouts: 0.02 us -> 1 us
  transfers between devices with their start and end apart: 20 -> 20, of which waited for: 6 -> 13; matrix products, arithmetic and copies ran while one was open for 0% -> 0% of each run, Pallas kernels for 13% -> 15%
where the time goes in v4:
time: 84.5 us; the launch traced here: 84.2 us
  waiting for transfers between devices  31.3 us (37%)
  starting transfers between devices  29.1 us (34%)
  Pallas kernels  21.5 us (25%)
  between operations  1.36 us (2%)
  local copies, waits for them, and re-layouts  1 us (1%)
    ppermute x11, waiting for transfers between devices, body(): lax.ppermute(v, 'dp', [(i, i ^ bit) for i in range(dp_size)])  24.1 us
    pallas_call x12, Pallas kernels, call(): pl.pallas_call(kernel, name=name, in_specs=[pl.BlockSpec(memory_space=p o...  21.5 us
    ppermute x11, starting transfers between devices, body(): lax.ppermute(v, 'dp', [(i, i ^ bit) for i in range(dp_size)])  14.4 us
    ppermute x6, starting transfers between devices, body(): lax.ppermute(v, 'rows', [(i, (i + 2 * k) % rows_size) for i in range(rows...  10.2 us
    ppermute x6, waiting for transfers between devices, body(): lax.ppermute(v, 'rows', [(i, (i + 2 * k) % rows_size) for i in range(rows...  7.11 us
    all_to_all x1, starting transfers between devices, body(): lax.all_to_all(send, ('dp', 'rows'), split_axis=0, concat_axis=0, tiled=T...  3.97 us
  transfers between devices with their start and end apart: 20, of which 13 were waited for; matrix products, arithmetic and copies ran while one was open for 0% of the time, Pallas kernels for 15%

profile of v4, /device:TPU:0, one launch (start us, length us, event | category | flops | bytes accessed | tf_op | source)
XLA Modules:
  0.0 84.2 jit_solution(9280234263546168080)
XLA Ops:
  1.3 8.3 %forward_part.1 = (f32[256,1536]{1,0:T(8,128)S(1)}, f32[256,1536]{1,0:T(8,128)S(1)}, bf16[512,1536]{1,0:T(8,128)(2,1)S(1)}, bf16[512,1024]{1,0:T(8,128)(2,1)S(1)...) custom-call(s32[1]{0:T(128)S(6)} %copy.13.len_ref, ...), custom_call_target="tpu_custom_call" | custom-call | flops 99999997952 | bytes 65536 | tf_op jit(solution)/shard_map/forward_part/pallas_call | solution.py:320
  9.5 0.5 collective-permute-start
  10.1 4.8 %attention_part.1 = (f32[256,1024]{1,0:T(8,128)S(1)}, f32[256,1024]{1,0:T(8,128)}, bf16[512,1024]{1,0:T(8,128)(2,1)S(1)}) custom-call(s32[1]{0:T(128)S(6)} %copy.13.len_ref, bf16[512,1536]{1,0:T(8,128)(2,1)S(1)} %get-tuple-element.54.hid_ref, bf16[512,1024]{1,0:T(8,128)(2,1)S(1)} %get-tuple-element.55.dsilu_ref, ...), custom_call_target="tpu_custom_call" | custom-call | flops 99999997952 | bytes 65536 | tf_op jit(solution)/shard_map/attention_part/pallas_call | solution.py:320
  14.9 0.0 copy-start.4
  14.9 1.0 %copy-done.4 = f32[256,1024]{1,0:T(8,128)} copy-done((f32[256,1024]{1,0:T(8,128)}, f32[256,1024]{1,0:T(8,128)S(1)}, u32[]{:S(2)}) %copy-start.4) | copy-done | bytes 1048600
  15.9 0.1 collective-permute-start.3
  15.9 0.0 collective-permute-done
  15.9 0.0 copy-start.1
  15.9 0.0 copy-start.2
  15.9 0.2 split_first.2
  16.1 3.0 %collective-permute-start.1 = (f32[2,64,768]{2,1,0:T(8,128)S(1)}, f32[2,64,768]{2,1,0:T(8,128)S(1)}, u32[]{:S(2)}, u32[]{:S(2)}) collective-permute-start(f32[2,64,768]{2,1,0:T(8,128)S(1)} %get-tuple-element.65), channel_id=1, source_target_pairs={{0,8},{8,0},{16,24},{24,16},{1,9},{9,1},{17,25},{25,17},{2,10},{10... | collective-permute-start | bytes 1179656 | tf_op jit(solution)/shard_map/ppermute | solution.py:338
  19.1 1.5 %collective-permute-start.2 = (f32[2,64,768]{2,1,0:T(8,128)S(1)}, f32[2,64,768]{2,1,0:T(8,128)S(1)}, u32[]{:S(2)}, u32[]{:S(2)}) collective-permute-start(f32[2,64,768]{2,1,0:T(8,128)S(1)} %get-tuple-element.66), channel_id=1, source_target_pairs={{0,16},{8,24},{16,0},{24,8},{1,17},{9,25},{17,1},{25,9},{2,18},{10... | collective-permute-start | bytes 1179656 | tf_op jit(solution)/shard_map/ppermute | solution.py:338
  20.6 0.0 copy-done.1
  20.6 0.0 copy-done.2
  20.6 3.4 %events_part.1 = f32[32,72,128]{2,1,0:T(8,128)} custom-call(s32[1]{0:T(128)S(6)} %copy.13.len_ref, bf16[512,512]{1,0:T(8,128)(2,1)S(1)} %get-tuple-element.61.ev_ref, bf16[512,512]{1,0:T(8,128)(2,1)S(1)} %get-tuple-element.62.cot_ref, bf16[512,2048]{1,0:T(8,128)(2,1)S(1)} %get-tuple-element.63.win_ref, s32[1,512]{1,0:T(1,128)S(1)} %copy-done.2, ...), custom_call_target="tpu_custom_call" | custom-call | flops 99999997952 | bytes 65536 | tf_op jit(solution)/shard_map/events_part/pallas_call | solution.py:320
  24.0 4.0 %all-to-all-start = ((f32[32,72,128]{2,1,0:T(8,128)}), f32[32,72,128]{2,1,0:T(8,128)S(1)}, u32[]{:S(2)}, u32[]{:S(2)}) async-start(f32[32,72,128]{2,1,0:T(8,128)} %events_part.1), calls=%async_computation | async-start | bytes 2359296 | tf_op jit(solution)/shard_map/all_to_all | solution.py:391
  28.0 0.0 copy-start.5
  28.0 0.4 collective-permute-done.1.recv_a_ref
  28.4 1.5 %collective-permute-done.2.recv_b_ref = f32[2,64,768]{2,1,0:T(8,128)S(1)} collective-permute-done((f32[2,64,768]{2,1,0:T(8,128)S(1)}, f32[2,64,768]{2,1,0:T(8,128)S(1)}, u32[]{:S(2)}, u32[]{:S(2)}) %collective-permute-start.2) | collective-permute-done | bytes 393248 | tf_op jit(solution)/shard_map/ppermute | solution.py:338
  29.9 0.1 split_second.2
  30.0 1.7 %collective-permute-start.4 = (f32[64,768]{1,0:T(8,128)S(1)}, f32[64,768]{1,0:T(8,128)S(1)}, u32[]{:S(2)}, u32[]{:S(2)}) collective-permute-start(f32[64,768]{1,0:T(8,128)S(1)} %get-tuple-element.72), channel_id=1, source_target_pairs={{0,16},{8,24},{16,0},{24,8},{1,17},{9,25},{17,1},{25,9},{2,18},{10... | collective-permute-start | bytes 589832 | tf_op jit(solution)/shard_map/ppermute | solution.py:338
  31.6 0.4 collective-permute-start.5
  32.1 0.0 collective-permute-done.3
  32.1 0.0 copy-done.5
  32.1 1.3 %split_first.3 = (f32[2,64,512]{2,1,0:T(8,128)S(1)}, f32[2,64,512]{2,1,0:T(8,128)S(1)}, f32[2,64,512]{2,1,0:T(8,128)S(1)}, f32[2,64,512]{2,1,0:T(8,128)S(1)}) custom-call(f32[2,2,64,1024]{3,2,1,0:T(8,128)S(1)} %bitcast.24, f32[2,2,64,1024]{3,2,1,0:T(8,128)} %bitcast.5.recv_ref), custom_call_target="tpu_custom_call" | custom-call | flops 1000000000 | bytes 65536 | tf_op jit(solution)/shard_map/split_first/pallas_call | solution.py:320
  33.4 1.6 %collective-permute-start.9 = (f32[2,64,512]{2,1,0:T(8,128)S(1)}, f32[2,64,512]{2,1,0:T(8,128)S(1)}, u32[]{:S(2)}, u32[]{:S(2)}) collective-permute-start(f32[2,64,512]{2,1,0:T(8,128)S(1)} %get-tuple-element.77), channel_id=1, source_target_pairs={{0,8},{8,0},{16,24},{24,16},{1,9},{9,1},{17,25},{25,17},{2,10},{10... | collective-permute-start | bytes 786440 | tf_op jit(solution)/shard_map/ppermute | solution.py:338
  35.1 0.4 collective-permute-start.10
  35.5 8.4 %collective-permute-done.4 = f32[64,768]{1,0:T(8,128)S(1)} collective-permute-done((f32[64,768]{1,0:T(8,128)S(1)}, f32[64,768]{1,0:T(8,128)S(1)}, u32[]{:S(2)}, u32[]{:S(2)}) %collective-permute-start.4) | collective-permute-done | bytes 196640 | tf_op jit(solution)/shard_map/ppermute | solution.py:338
  43.9 0.1 collective-permute-done.5
  44.0 7.1 %collective-permute-done.9.recv_a_ref = f32[2,64,512]{2,1,0:T(8,128)S(1)} collective-permute-done((f32[2,64,512]{2,1,0:T(8,128)S(1)}, f32[2,64,512]{2,1,0:T(8,128)S(1)}, u32[]{:S(2)}, u32[]{:S(2)}) %collective-permute-start.9) | collective-permute-done | bytes 262176 | tf_op jit(solution)/shard_map/ppermute | solution.py:338
  51.2 0.5 collective-permute-done.10.recv_b_ref
  51.7 0.1 split_second.3
  51.8 1.0 %collective-permute-start.11 = (f32[64,512]{1,0:T(8,128)S(1)}, f32[64,512]{1,0:T(8,128)S(1)}, u32[]{:S(2)}, u32[]{:S(2)}) collective-permute-start(f32[64,512]{1,0:T(8,128)S(1)} %get-tuple-element.88), channel_id=1, source_target_pairs={{0,16},{8,24},{16,0},{24,8},{1,17},{9,25},{17,1},{25,9},{2,18},{10... | collective-permute-start | bytes 393224 | tf_op jit(solution)/shard_map/ppermute | solution.py:338
  52.8 1.1 %collective-permute-start.12 = (f32[64,512]{1,0:T(8,128)S(1)}, f32[64,512]{1,0:T(8,128)S(1)}, u32[]{:S(2)}, u32[]{:S(2)}) collective-permute-start(f32[64,512]{1,0:T(8,128)S(1)} %get-tuple-element.90), channel_id=1, source_target_pairs={{0,8},{8,0},{16,24},{24,16},{1,9},{9,1},{17,25},{25,17},{2,10},{10... | collective-permute-start | bytes 393224 | tf_op jit(solution)/shard_map/ppermute | solution.py:338
  53.9 1.9 %collective-permute-start.6 = (f32[16,1536]{1,0:T(8,128)S(1)}, f32[16,1536]{1,0:T(8,128)S(1)}, u32[]{:S(2)}, u32[]{:S(2)}) collective-permute-start(f32[16,1536]{1,0:T(8,128)S(1)} %get-tuple-element.83), channel_id=1, source_target_pairs={{0,2},{1,3},{2,4},{3,5},{4,6},{5,7},{6,0},{7,1},{8,10},{9,11},{10,... | collective-permute-start | bytes 294920 | tf_op jit(solution)/shard_map/ppermute | solution.py:339
  55.8 3.2 %collective-permute-start.7 = (f32[16,1536]{1,0:T(8,128)S(1)}, f32[16,1536]{1,0:T(8,128)S(1)}, u32[]{:S(2)}, u32[]{:S(2)}) collective-permute-start(f32[16,1536]{1,0:T(8,128)S(1)} %get-tuple-element.84), channel_id=1, source_target_pairs={{0,4},{1,5},{2,6},{3,7},{4,0},{5,1},{6,2},{7,3},{8,12},{9,13},{10,... | collective-permute-start | bytes 294920 | tf_op jit(solution)/shard_map/ppermute | solution.py:339
  58.9 0.7 collective-permute-start.8
  59.6 0.0 collective-permute-done.11
  59.6 0.0 collective-permute-done.12
  59.7 1.4 %collective-permute-start.13 = (f32[16,1024]{1,0:T(8,128)S(1)}, f32[16,1024]{1,0:T(8,128)S(1)}, u32[]{:S(2)}, u32[]{:S(2)}) collective-permute-start(f32[16,1024]{1,0:T(8,128)S(1)} %get-tuple-element.92), channel_id=1, source_target_pairs={{0,2},{1,3},{2,4},{3,5},{4,6},{5,7},{6,0},{7,1},{8,10},{9,11},{10,... | collective-permute-start | bytes 196616 | tf_op jit(solution)/shard_map/ppermute | solution.py:339
  61.1 2.4 %collective-permute-start.14 = (f32[16,1024]{1,0:T(8,128)S(1)}, f32[16,1024]{1,0:T(8,128)S(1)}, u32[]{:S(2)}, u32[]{:S(2)}) collective-permute-start(f32[16,1024]{1,0:T(8,128)S(1)} %get-tuple-element.93), channel_id=1, source_target_pairs={{0,4},{1,5},{2,6},{3,7},{4,0},{5,1},{6,2},{7,3},{8,12},{9,13},{10,... | collective-permute-start | bytes 196616 | tf_op jit(solution)/shard_map/ppermute | solution.py:339
  63.4 0.0 collective-permute-done.6.refs_1_
  63.4 0.7 collective-permute-start.15
  64.1 2.2 %collective-permute-done.7.refs_2_ = f32[16,1536]{1,0:T(8,128)S(1)} collective-permute-done((f32[16,1536]{1,0:T(8,128)S(1)}, f32[16,1536]{1,0:T(8,128)S(1)}, u32[]{:S(2)}, u32[]{:S(2)}) %collective-permute-start.7) | collective-permute-done | bytes 98336 | tf_op jit(solution)/shard_map/ppermute | solution.py:339
  66.3 0.3 collective-permute-done.8.refs_3_
  66.7 1.0 %collective-permute-done.13.refs_5_ = f32[16,1024]{1,0:T(8,128)S(1)} collective-permute-done((f32[16,1024]{1,0:T(8,128)S(1)}, f32[16,1024]{1,0:T(8,128)S(1)}, u32[]{:S(2)}, u32[]{:S(2)}) %collective-permute-start.13) | collective-permute-done | bytes 65568 | tf_op jit(solution)/shard_map/ppermute | solution.py:339
  67.7 3.6 %collective-permute-done.14.refs_6_ = f32[16,1024]{1,0:T(8,128)S(1)} collective-permute-done((f32[16,1024]{1,0:T(8,128)S(1)}, f32[16,1024]{1,0:T(8,128)S(1)}, u32[]{:S(2)}, u32[]{:S(2)}) %collective-permute-start.14) | collective-permute-done | bytes 65568 | tf_op jit(solution)/shard_map/ppermute | solution.py:339
  71.2 0.0 collective-permute-done.15.refs_7_
  71.2 0.0 copy-start
  71.2 0.0 copy-start.3
  71.3 1.5 %collective-permute-start.16 = (f32[16,2560]{1,0:T(8,128)S(1)}, f32[16,2560]{1,0:T(8,128)S(1)}, u32[]{:S(2)}, u32[]{:S(2)}) collective-permute-start(f32[16,2560]{1,0:T(8,128)S(1)} %total.1.refs_0_), channel_id=1, source_target_pairs={{0,8},{8,0},{16,24},{24,16},{1,9},{9,1},{17,25},{25,17},{2,10},{10... | collective-permute-start | bytes 491528 | tf_op jit(solution)/shard_map/ppermute | solution.py:338
  72.8 1.6 %collective-permute-start.18 = (f32[16,2560]{1,0:T(8,128)S(1)}, f32[16,2560]{1,0:T(8,128)S(1)}, u32[]{:S(2)}, u32[]{:S(2)}) collective-permute-start(f32[16,2560]{1,0:T(8,128)S(1)} %total.1.refs_0_), channel_id=1, source_target_pairs={{0,24},{8,16},{16,8},{24,0},{1,25},{9,17},{17,9},{25,1},{2,26},{10... | collective-permute-start | bytes 491528 | tf_op jit(solution)/shard_map/ppermute | solution.py:338
  74.3 0.5 collective-permute-start.17
  74.8 0.0 all-to-all-done.recv_ref
  74.8 0.0 copy-done
  74.8 0.0 copy-done.3
  74.9 2.4 %table_part.1 = (f32[512,512]{1,0:T(8,128)}, f32[512]{0:T(512)}) custom-call(f32[32,72,128]{2,1,0:T(8,128)S(1)} %all-to-all-done.recv_ref, f32[512,512]{1,0:T(8,128)S(1)} %copy-done, f32[512]{0:T(512)S(1)} %copy-done.3), custom_call_target="tpu_custom_call" | custom-call | flops 1000000000 | bytes 65536 | tf_op jit(solution)/shard_map/table_part/pallas_call | solution.py:320
  77.2 1.2 %collective-permute-done.16.refs_1_ = f32[16,2560]{1,0:T(8,128)S(1)} collective-permute-done((f32[16,2560]{1,0:T(8,128)S(1)}, f32[16,2560]{1,0:T(8,128)S(1)}, u32[]{:S(2)}, u32[]{:S(2)}) %collective-permute-start.16) | collective-permute-done | bytes 163872 | tf_op jit(solution)/shard_map/ppermute | solution.py:338
  78.4 3.5 %collective-permute-done.18.refs_3_ = f32[16,2560]{1,0:T(8,128)S(1)} collective-permute-done((f32[16,2560]{1,0:T(8,128)S(1)}, f32[16,2560]{1,0:T(8,128)S(1)}, u32[]{:S(2)}, u32[]{:S(2)}) %collective-permute-start.18) | collective-permute-done | bytes 163872 | tf_op jit(solution)/shard_map/ppermute | solution.py:338
  82.0 1.4 %collective-permute-done.17.refs_2_ = f32[16,2560]{1,0:T(8,128)S(1)} collective-permute-done((f32[16,2560]{1,0:T(8,128)S(1)}, f32[16,2560]{1,0:T(8,128)S(1)}, u32[]{:S(2)}, u32[]{:S(2)}) %collective-permute-start.17) | collective-permute-done | bytes 163872 | tf_op jit(solution)/shard_map/ppermute | solution.py:338
  83.3 0.9 %gather.1 = (f32[4,16,2048]{2,1,0:T(8,128)}, f32[4,16,512]{2,1,0:T(8,128)}) custom-call(f32[16,2560]{1,0:T(8,128)S(1)} %total.1.refs_0_, f32[16,2560]{1,0:T(8,128)S(1)} %collective-permute-done.16.refs_1_, f32[16,2560]{1,0:T(8,128)S(1)} %collective-permute-done.17.refs_2_, f32[16,2560]{1,0:T(8,128)S(1)} %collective-permute-done.18.refs_3_), custom_call_target="tpu_custom_call" | custom-call | flops 1000000000 | bytes 65536 | tf_op jit(solution)/shard_map/gather/pallas_call | solution.py:320
  (3 shorter events, 0.1 us)
Async XLA Ops:
  9.5 6.4 %collective-permute-start = (f32[256,1536]{1,0:T(8,128)S(1)}, f32[256,1536]{1,0:T(8,128)S(1)}, u32[]{:S(2)}, u32[]{:S(2)}) collective-permute-start(f32[256,1536]{1,0:T(8,128)S(1)} %get-tuple-element.53), channel_id=1, source_target_pairs={{0,1},{1,0},{2,3},{3,2},{4,5},{5,4},{6,7},{7,6},{8,9},{9,8},{10,11... | collective-permute-start | bytes 4718600 | tf_op jit(solution)/shard_map/ppermute | solution.py:379
  14.9 1.0 %copy-start.4 = (f32[256,1024]{1,0:T(8,128)}, f32[256,1024]{1,0:T(8,128)S(1)}, u32[]{:S(2)}) copy-start(f32[256,1024]{1,0:T(8,128)S(1)} %get-tuple-element.75) | copy-start | bytes 3145732
  15.9 16.2 %collective-permute-start.3 = (f32[256,1024]{1,0:T(8,128)}, f32[256,1024]{1,0:T(8,128)}, u32[]{:S(2)}, u32[]{:S(2)}) collective-permute-start(f32[256,1024]{1,0:T(8,128)} %get-tuple-element.76), channel_id=1, source_target_pairs={{0,1},{1,0},{2,3},{3,2},{4,5},{5,4},{6,7},{7,6},{8,9},{9,8},{10,11... | collective-permute-start | bytes 3145736 | tf_op jit(solution)/shard_map/ppermute | solution.py:383
  15.9 4.7 %copy-start.1 = (s32[1,32,16]{1,2,0:T(8,128)S(1)}, s32[1,32,16]{1,2,0:T(8,128)}, u32[]{:S(2)}) copy-start(s32[1,32,16]{1,2,0:T(8,128)} %param.14) | copy-start | bytes 6148
  15.9 4.7 %copy-start.2 = (s32[1,512]{1,0:T(1,128)S(1)}, s32[1,512]{1,0:T(1,128)}, u32[]{:S(2)}) copy-start(s32[1,512]{1,0:T(1,128)} %slot_ref.1) | copy-start | bytes 6148
  16.1 12.3 %collective-permute-start.1 = (f32[2,64,768]{2,1,0:T(8,128)S(1)}, f32[2,64,768]{2,1,0:T(8,128)S(1)}, u32[]{:S(2)}, u32[]{:S(2)}) collective-permute-start(f32[2,64,768]{2,1,0:T(8,128)S(1)} %get-tuple-element.65), channel_id=1, source_target_pairs={{0,8},{8,0},{16,24},{24,16},{1,9},{9,1},{17,25},{25,17},{2,10},{10... | collective-permute-start | bytes 1179656 | tf_op jit(solution)/shard_map/ppermute | solution.py:338
  19.1 10.8 %collective-permute-start.2 = (f32[2,64,768]{2,1,0:T(8,128)S(1)}, f32[2,64,768]{2,1,0:T(8,128)S(1)}, u32[]{:S(2)}, u32[]{:S(2)}) collective-permute-start(f32[2,64,768]{2,1,0:T(8,128)S(1)} %get-tuple-element.66), channel_id=1, source_target_pairs={{0,16},{8,24},{16,0},{24,8},{1,17},{9,25},{17,1},{25,9},{2,18},{10... | collective-permute-start | bytes 1179656 | tf_op jit(solution)/shard_map/ppermute | solution.py:338
  24.0 50.8 %all-to-all-start = ((f32[32,72,128]{2,1,0:T(8,128)}), f32[32,72,128]{2,1,0:T(8,128)S(1)}, u32[]{:S(2)}, u32[]{:S(2)}) async-start(f32[32,72,128]{2,1,0:T(8,128)} %events_part.1), calls=%async_computation | async-start | bytes 2359296 | tf_op jit(solution)/shard_map/all_to_all | solution.py:391
  28.0 4.1 %copy-start.5 = (f32[256,1024]{1,0:T(8,128)S(1)}, f32[256,1024]{1,0:T(8,128)}, u32[]{:S(2)}) copy-start(f32[256,1024]{1,0:T(8,128)} %copy-done.4) | copy-start | bytes 3145732
  30.0 13.9 %collective-permute-start.4 = (f32[64,768]{1,0:T(8,128)S(1)}, f32[64,768]{1,0:T(8,128)S(1)}, u32[]{:S(2)}, u32[]{:S(2)}) collective-permute-start(f32[64,768]{1,0:T(8,128)S(1)} %get-tuple-element.72), channel_id=1, source_target_pairs={{0,16},{8,24},{16,0},{24,8},{1,17},{9,25},{17,1},{25,9},{2,18},{10... | collective-permute-start | bytes 589832 | tf_op jit(solution)/shard_map/ppermute | solution.py:338
  31.6 12.4 %collective-permute-start.5 = (f32[64,768]{1,0:T(8,128)S(1)}, f32[64,768]{1,0:T(8,128)S(1)}, u32[]{:S(2)}, u32[]{:S(2)}) collective-permute-start(f32[64,768]{1,0:T(8,128)S(1)} %get-tuple-element.73), channel_id=1, source_target_pairs={{0,8},{8,0},{16,24},{24,16},{1,9},{9,1},{17,25},{25,17},{2,10},{10... | collective-permute-start | bytes 589832 | tf_op jit(solution)/shard_map/ppermute | solution.py:338
  33.4 17.8 %collective-permute-start.9 = (f32[2,64,512]{2,1,0:T(8,128)S(1)}, f32[2,64,512]{2,1,0:T(8,128)S(1)}, u32[]{:S(2)}, u32[]{:S(2)}) collective-permute-start(f32[2,64,512]{2,1,0:T(8,128)S(1)} %get-tuple-element.77), channel_id=1, source_target_pairs={{0,8},{8,0},{16,24},{24,16},{1,9},{9,1},{17,25},{25,17},{2,10},{10... | collective-permute-start | bytes 786440 | tf_op jit(solution)/shard_map/ppermute | solution.py:338
  35.1 16.7 %collective-permute-start.10 = (f32[2,64,512]{2,1,0:T(8,128)S(1)}, f32[2,64,512]{2,1,0:T(8,128)S(1)}, u32[]{:S(2)}, u32[]{:S(2)}) collective-permute-start(f32[2,64,512]{2,1,0:T(8,128)S(1)} %get-tuple-element.79), channel_id=1, source_target_pairs={{0,16},{8,24},{16,0},{24,8},{1,17},{9,25},{17,1},{25,9},{2,18},{10... | collective-permute-start | bytes 786440 | tf_op jit(solution)/shard_map/ppermute | solution.py:338
  51.8 7.8 %collective-permute-start.11 = (f32[64,512]{1,0:T(8,128)S(1)}, f32[64,512]{1,0:T(8,128)S(1)}, u32[]{:S(2)}, u32[]{:S(2)}) collective-permute-start(f32[64,512]{1,0:T(8,128)S(1)} %get-tuple-element.88), channel_id=1, source_target_pairs={{0,16},{8,24},{16,0},{24,8},{1,17},{9,25},{17,1},{25,9},{2,18},{10... | collective-permute-start | bytes 393224 | tf_op jit(solution)/shard_map/ppermute | solution.py:338
  52.8 6.8 %collective-permute-start.12 = (f32[64,512]{1,0:T(8,128)S(1)}, f32[64,512]{1,0:T(8,128)S(1)}, u32[]{:S(2)}, u32[]{:S(2)}) collective-permute-start(f32[64,512]{1,0:T(8,128)S(1)} %get-tuple-element.90), channel_id=1, source_target_pairs={{0,8},{8,0},{16,24},{24,16},{1,9},{9,1},{17,25},{25,17},{2,10},{10... | collective-permute-start | bytes 393224 | tf_op jit(solution)/shard_map/ppermute | solution.py:338
  53.9 9.5 %collective-permute-start.6 = (f32[16,1536]{1,0:T(8,128)S(1)}, f32[16,1536]{1,0:T(8,128)S(1)}, u32[]{:S(2)}, u32[]{:S(2)}) collective-permute-start(f32[16,1536]{1,0:T(8,128)S(1)} %get-tuple-element.83), channel_id=1, source_target_pairs={{0,2},{1,3},{2,4},{3,5},{4,6},{5,7},{6,0},{7,1},{8,10},{9,11},{10,... | collective-permute-start | bytes 294920 | tf_op jit(solution)/shard_map/ppermute | solution.py:339
  55.8 10.5 %collective-permute-start.7 = (f32[16,1536]{1,0:T(8,128)S(1)}, f32[16,1536]{1,0:T(8,128)S(1)}, u32[]{:S(2)}, u32[]{:S(2)}) collective-permute-start(f32[16,1536]{1,0:T(8,128)S(1)} %get-tuple-element.84), channel_id=1, source_target_pairs={{0,4},{1,5},{2,6},{3,7},{4,0},{5,1},{6,2},{7,3},{8,12},{9,13},{10,... | collective-permute-start | bytes 294920 | tf_op jit(solution)/shard_map/ppermute | solution.py:339
  58.9 7.7 %collective-permute-start.8 = (f32[16,1536]{1,0:T(8,128)S(1)}, f32[16,1536]{1,0:T(8,128)S(1)}, u32[]{:S(2)}, u32[]{:S(2)}) collective-permute-start(f32[16,1536]{1,0:T(8,128)S(1)} %get-tuple-element.85), channel_id=1, source_target_pairs={{0,6},{1,7},{2,0},{3,1},{4,2},{5,3},{6,4},{7,5},{8,14},{9,15},{10,... | collective-permute-start | bytes 294920 | tf_op jit(solution)/shard_map/ppermute | solution.py:339
  59.7 8.0 %collective-permute-start.13 = (f32[16,1024]{1,0:T(8,128)S(1)}, f32[16,1024]{1,0:T(8,128)S(1)}, u32[]{:S(2)}, u32[]{:S(2)}) collective-permute-start(f32[16,1024]{1,0:T(8,128)S(1)} %get-tuple-element.92), channel_id=1, source_target_pairs={{0,2},{1,3},{2,4},{3,5},{4,6},{5,7},{6,0},{7,1},{8,10},{9,11},{10,... | collective-permute-start | bytes 196616 | tf_op jit(solution)/shard_map/ppermute | solution.py:339
  61.1 10.2 %collective-permute-start.14 = (f32[16,1024]{1,0:T(8,128)S(1)}, f32[16,1024]{1,0:T(8,128)S(1)}, u32[]{:S(2)}, u32[]{:S(2)}) collective-permute-start(f32[16,1024]{1,0:T(8,128)S(1)} %get-tuple-element.93), channel_id=1, source_target_pairs={{0,4},{1,5},{2,6},{3,7},{4,0},{5,1},{6,2},{7,3},{8,12},{9,13},{10,... | collective-permute-start | bytes 196616 | tf_op jit(solution)/shard_map/ppermute | solution.py:339
  63.4 7.8 %collective-permute-start.15 = (f32[16,1024]{1,0:T(8,128)S(1)}, f32[16,1024]{1,0:T(8,128)S(1)}, u32[]{:S(2)}, u32[]{:S(2)}) collective-permute-start(f32[16,1024]{1,0:T(8,128)S(1)} %get-tuple-element.94), channel_id=1, source_target_pairs={{0,6},{1,7},{2,0},{3,1},{4,2},{5,3},{6,4},{7,5},{8,14},{9,15},{10,... | collective-permute-start | bytes 196616 | tf_op jit(solution)/shard_map/ppermute | solution.py:339
  71.2 3.6 %copy-start = (f32[512,512]{1,0:T(8,128)S(1)}, f32[512,512]{1,0:T(8,128)}, u32[]{:S(2)}) copy-start(f32[512,512]{1,0:T(8,128)} %table_ref.1) | copy-start | bytes 3145732
  71.2 3.6 %copy-start.3 = (f32[512]{0:T(512)S(1)}, f32[512]{0:T(512)}, u32[]{:S(2)}) copy-start(f32[512]{0:T(512)} %accum_ref.1) | copy-start | bytes 6148
  71.3 7.1 %collective-permute-start.16 = (f32[16,2560]{1,0:T(8,128)S(1)}, f32[16,2560]{1,0:T(8,128)S(1)}, u32[]{:S(2)}, u32[]{:S(2)}) collective-permute-start(f32[16,2560]{1,0:T(8,128)S(1)} %total.1.refs_0_), channel_id=1, source_target_pairs={{0,8},{8,0},{16,24},{24,16},{1,9},{9,1},{17,25},{25,17},{2,10},{10... | collective-permute-start | bytes 491528 | tf_op jit(solution)/shard_map/ppermute | solution.py:338
  72.8 9.2 %collective-permute-start.18 = (f32[16,2560]{1,0:T(8,128)S(1)}, f32[16,2560]{1,0:T(8,128)S(1)}, u32[]{:S(2)}, u32[]{:S(2)}) collective-permute-start(f32[16,2560]{1,0:T(8,128)S(1)} %total.1.refs_0_), channel_id=1, source_target_pairs={{0,24},{8,16},{16,8},{24,0},{1,25},{9,17},{17,9},{25,1},{2,26},{10... | collective-permute-start | bytes 491528 | tf_op jit(solution)/shard_map/ppermute | solution.py:338
  74.3 9.0 %collective-permute-start.17 = (f32[16,2560]{1,0:T(8,128)S(1)}, f32[16,2560]{1,0:T(8,128)S(1)}, u32[]{:S(2)}, u32[]{:S(2)}) collective-permute-start(f32[16,2560]{1,0:T(8,128)S(1)} %total.1.refs_0_), channel_id=1, source_target_pairs={{0,16},{8,24},{16,0},{24,8},{1,17},{9,25},{17,1},{25,9},{2,18},{10... | collective-permute-start | bytes 491528 | tf_op jit(solution)/shard_map/ppermute | solution.py:338

commit v5 on v1

--- a/solution.py
+++ b/solution.py
@@ -14,7 +14,7 @@
 learning_rate = 0.1
 
 f32, bf16 = jnp.float32, jnp.bfloat16
-VMEM_BYTES = 32 * 1024 * 1024
+MIB = 1024 * 1024
 STEP = 256
 LANES = 128
 ID_ROWS = 8
@@ -252,6 +252,101 @@
     table_new_ref[...] = table_ref[...] - learning_rate * grad / (jnp.sqrt(accum_new) + adagrad_eps)
 
 
+def place_on_dp():
+    d = lax.axis_index("dp")
+    return lax.rem(d, 2), d // 2
+
+
+def split_first(x, y, keep_ref, recv_ref):
+    half = keep_ref.shape[-1] // 2
+    part = lambda i, j, cols: keep_ref[i, j, :, cols] + recv_ref[i, j, :, cols]
+    lo, hi = slice(0, half), slice(half, 2 * half)
+    return ([part(s, 1 - x, lo) for s in range(2)], [part(1 - y, s, hi) for s in range(2)],
+            [part(s, x, lo) for s in range(2)], [part(y, s, hi) for s in range(2)])
+
+
+def first_kernel(keep_ref, recv_ref, to_x_ref, to_y_ref, keep_a_ref, keep_b_ref):
+    parts = split_first(*place_on_dp(), keep_ref, recv_ref)
+    for ref, pair in zip((to_x_ref, to_y_ref, keep_a_ref, keep_b_ref), parts):
+        for s in range(2):
+            ref[s] = pair[s]
+
+
+def second_kernel(keep_a_ref, from_x_ref, keep_b_ref, from_y_ref, keep_ref, recv_ref,
+                  to_x_ref, to_y_ref, next_a_ref, next_b_ref, keep2_a_ref, keep2_b_ref):
+    x, y = place_on_dp()
+    half = keep_a_ref.shape[-1]
+    to_y_ref[:, :half] = keep_a_ref[1 - y] + from_x_ref[1 - y]
+    to_x_ref[:, :half] = keep_b_ref[1 - x] + from_y_ref[1 - x]
+    next_a_ref[...] = keep_a_ref[y] + from_x_ref[y]
+    next_b_ref[...] = keep_b_ref[x] + from_y_ref[x]
+    send_x, send_y, keep2_a, keep2_b = split_first(x, y, keep_ref, recv_ref)
+    half2 = keep_ref.shape[-1] // 2
+    for s in range(2):
+        to_x_ref[:, half + s * half2:half + (s + 1) * half2] = send_x[s]
+        to_y_ref[:, half + s * half2:half + (s + 1) * half2] = send_y[s]
+        keep2_a_ref[s] = keep2_a[s]
+        keep2_b_ref[s] = keep2_b[s]
+
+
+def chip_parts(out_refs, keep_a, recv_a, keep_b, recv_b):
+    chips = len(out_refs)
+    chip = lax.axis_index("rows") // 2
+    half = out_refs[0].shape[-1] // 2
+    for k, out_ref in enumerate(out_refs):
+        at = lax.rem(chip + k, chips)
+        out_ref[:, :half] = keep_a(at) + recv_a(at)
+        out_ref[:, half:] = keep_b(at) + recv_b(at)
+
+
+def third_kernel(chips, next_a_ref, next_b_ref, from_x_ref, from_y_ref, keep2_a_ref, keep2_b_ref, *out_refs):
+    x, y = place_on_dp()
+    half, half2 = next_a_ref.shape[-1], keep2_a_ref.shape[-1]
+    lo = slice(0, half)
+    chip_parts(out_refs[:chips], lambda at: next_a_ref[at], lambda at: from_y_ref[at, :, lo],
+               lambda at: next_b_ref[at], lambda at: from_x_ref[at, :, lo])
+    to_x_ref, to_y_ref, next2_a_ref, next2_b_ref = out_refs[chips:]
+    blocks = [slice(half + s * half2, half + (s + 1) * half2) for s in range(2)]
+    sum_a = [keep2_a_ref[s] + from_x_ref[:, :, blocks[s]] for s in range(2)]
+    sum_b = [keep2_b_ref[s] + from_y_ref[:, :, blocks[s]] for s in range(2)]
+    to_y_ref[...] = jnp.where(y == 0, sum_a[1], sum_a[0])
+    next2_a_ref[...] = jnp.where(y == 0, sum_a[0], sum_a[1])
+    to_x_ref[...] = jnp.where(x == 0, sum_b[1], sum_b[0])
+    next2_b_ref[...] = jnp.where(x == 0, sum_b[0], sum_b[1])
+
+
+def sum_of(refs):
+    total = refs[0][...]
+    for ref in refs[1:]:
+        total = total + ref[...]
+    return total
+
+
+def fourth_kernel(chips, tokens, *refs):
+    blocks, (next2_a_ref, next2_b_ref, from_x_ref, from_y_ref) = refs[:chips], refs[chips:chips + 4]
+    total_ref, *out_refs = refs[chips + 4:]
+    total_ref[...] = sum_of(blocks) * (1.0 / tokens)
+    chip_parts(out_refs, lambda at: next2_a_ref[at], lambda at: from_y_ref[at],
+               lambda at: next2_b_ref[at], lambda at: from_x_ref[at])
+
+
+def total_kernel(tokens, *refs):
+    refs[-1][...] = sum_of(refs[:-1]) * (1.0 / tokens)
+
+
+def gather_kernel(*refs):
+    *pieces, grad_in_ref, grad_out_ref = refs
+    dp = len(pieces) // 2
+    d = lax.axis_index("dp")
+    width = grad_out_ref.shape[-1]
+    for k in range(dp):
+        at = jnp.bitwise_xor(d, k)
+        first = pieces[k].shape[-1]
+        grad_out_ref[at] = pieces[k][:, :width]
+        grad_in_ref[at, :, :first - width] = pieces[k][:, width:]
+        grad_in_ref[at, :, first - width:] = pieces[dp + k][...]
+
+
 def vmem():
     return pl.BlockSpec(memory_space=pltpu.VMEM)
 
@@ -260,7 +355,7 @@
     return jax.ShapeDtypeStruct(dims, dtype)
 
 
-def call(kernel, name, out_shape, args, scalars=0, scratch=(), flops=0, far=0):
+def call(kernel, name, out_shape, args, scalars=0, scratch=(), far=0, long=False, grant=4):
     place = [None] * scalars + [pltpu.HBM] * far + [pltpu.VMEM] * (len(args) - scalars - far)
     args = [a if p is None else pltpu.with_memory_space_constraint(a, p) for a, p in zip(args, place)]
     return pl.pallas_call(
@@ -268,10 +363,10 @@
         name=name,
         in_specs=[pl.BlockSpec(memory_space=p or pltpu.SMEM) for p in place],
         out_specs=[vmem()] * len(out_shape),
-        out_shape=out_shape,
+        out_shape=list(out_shape),
         scratch_shapes=[pltpu.VMEM(dims, dtype) for dims, dtype in scratch] + [pltpu.SemaphoreType.DMA((7,))] * (far > 0),
-        compiler_params=pltpu.CompilerParams(vmem_limit_bytes=VMEM_BYTES),
-        cost_estimate=pl.CostEstimate(flops=flops, bytes_accessed=1 << 20, transcendentals=0),
+        compiler_params=pltpu.CompilerParams(vmem_limit_bytes=grant * MIB),
+        cost_estimate=pl.CostEstimate(flops=100_000_000_000 if long else 1_000_000_000, bytes_accessed=1 << 16, transcendentals=0),
     )(*args)
 
 
@@ -281,24 +376,19 @@
     chips = rows_size // 2
     piece = width // (rows_size * dp_size)
     cores = [(i, i ^ 1) for i in range(rows_size)]
-    lines = [list(range(c, rows_size, 2)) for c in range(2)]
-
-    def exchange(v, axis, groups=None):
-        return lax.all_to_all(v, axis, split_axis=0, concat_axis=0, axis_index_groups=groups, tiled=True)
-
-    def after(value, *others):
-        return lax.optimization_barrier((value, *others))[0]
-
-    def over_dp(both):
-        return exchange(both.reshape(dp_size, chips * piece, both.shape[1]), "dp")
-
-    def over_chips(parts):
-        return exchange(jnp.sum(parts, axis=0).reshape(chips, piece, -1), "rows", lines)
-
-    def gathered(parts):
-        part = jnp.sum(parts, axis=0) * (1.0 / tokens)
-        return exchange(jnp.broadcast_to(part, (dp_size, *part.shape)), "dp").reshape(dp_size * piece, -1)
-
+    over_dp = lambda v, bit: lax.ppermute(v, "dp", [(i, i ^ bit) for i in range(dp_size)])
+    over_chips = lambda v, k: lax.ppermute(v, "rows", [(i, (i + 2 * k) % rows_size) for i in range(rows_size)])
+    after = lambda value, *others: lax.optimization_barrier((value, *others))[0]
+    strip = chips * piece
+
+    def to_chips(blocks):
+        return [blocks[0]] + [over_chips(blocks[k], k) for k in range(1, chips)]
+
+    def gathered(total):
+        return [total] + [over_dp(total, k) for k in range(1, dp_size)]
+
+    by_dp = lambda v: v.reshape(2, 2, strip, v.shape[-1])
+    by_chip = lambda v: v.reshape(*v.shape[:-2], chips, piece, v.shape[-1])
     local = lambda *dims, dtype=f32: pltpu.VMEM(dims, dtype)
     sides = lambda cols: [local(width // 2, cols)] * 2
     keep1, send1, hid, dsilu, gatt, gpre_uv, normed_t, events, cotangent, w_in = call(
@@ -316,35 +406,51 @@
         (lengths, events, cotangent, w_in, w_out), 1,
         [((tokens, width), bf16), ((tokens, width), bf16), ((tokens, width), f32), ((tokens, width), f32),
          ((tokens, width), bf16), ((tokens, width), bf16), ((tokens, width), f32), ((HEADS, tokens, tokens), bf16),
-         (w_out.shape, bf16)],
-        flops=100_000_000_000, far=4)
+         (w_out.shape, bf16)], far=4, long=True, grant=16)
     recv1 = lax.ppermute(send1, "rows", cores)
     keep2, send2, gpre_qk = call(
         attention_kernel, "attention_part", sides(2 * width) + [local(tokens, 2 * width, dtype=bf16)],
-        (lengths, hid, dsilu, gatt, normed_t), 1, flops=100_000_000_000)
+        (lengths, hid, dsilu, gatt, normed_t), 1, long=True, grant=10)
     recv2 = lax.ppermute(send2, "rows", cores)
     pay_rows = capacity * (width // LANES) + ID_ROWS
-    both1 = keep1 + recv1
-    gpre_uv = after(gpre_uv, both1)
-    parts1 = over_dp(both1)
+    half1, half2 = 3 * width // 2, width
+    to_x, to_y, keep_a, keep_b = call(
+        first_kernel, "first_sums", [local(2, strip, half1)] * 4, (by_dp(keep1), by_dp(after(recv1, keep2))))
+    gpre_uv = after(gpre_uv, to_x, to_y)
     (send,) = call(
         events_kernel, "events_part", [local(owners, pay_rows, LANES)],
         (lengths, events, cotangent, w_in, event_slot, slot_row[0].T, gpre_uv, gpre_qk), 1,
-        [((tokens, width), bf16), ((tokens, width), bf16), ((owners * capacity, width), f32)], flops=100_000_000_000)
-    recv = exchange(send, ("dp", "rows"))
-    both2 = after(keep2, send) + recv2
-    parts2 = over_dp(both2)
-    parts1 = over_chips(after(parts1, both2))
-    parts2 = over_chips(after(parts2, parts1))
-    first = gathered(parts1)
-    second = gathered(parts2)
-    grad_in = jnp.concatenate([first[:, width:], second], axis=1)
+        [((tokens, width), bf16), ((tokens, width), bf16), ((owners * capacity, width), f32)], long=True, grant=10)
+    recv = lax.all_to_all(send, ("dp", "rows"), split_axis=0, concat_axis=0, tiled=True)
+    from_x, from_y = over_dp(to_x, 1), over_dp(to_y, 2)
+    to_x, to_y, next_a, next_b, keep2_a, keep2_b = call(
+        second_kernel, "second_sums",
+        [local(strip, half1 + 2 * half2)] * 2 + [local(strip, half1)] * 2 + [local(2, strip, half2)] * 2,
+        (after(keep_a, send), from_x, keep_b, from_y, by_dp(keep2), by_dp(recv2)), long=True)
+    from_x, from_y = over_dp(to_x, 1), over_dp(to_y, 2)
+    *blocks, to_x, to_y, next2_a, next2_b = call(
+        functools.partial(third_kernel, chips), "third_sums",
+        [local(piece, 2 * half1)] * chips + [local(chips, piece, half2)] * 4,
+        [by_chip(v) for v in (next_a, next_b, from_x, from_y, keep2_a, keep2_b)])
+    from_x, from_y = over_dp(to_x, 1), over_dp(to_y, 2)
+    total, *blocks = call(
+        functools.partial(fourth_kernel, chips, tokens), "fourth_sums",
+        [local(piece, 2 * half1)] + [local(piece, 2 * half2)] * chips,
+        to_chips(blocks) + [next2_a, next2_b, from_x, from_y])
+    pieces = gathered(total)
+    blocks = to_chips(blocks)
+    blocks[0] = after(blocks[0], *pieces)
+    (total,) = call(functools.partial(total_kernel, tokens), "last_sums", [local(piece, 2 * half2)], blocks)
+    pieces += gathered(total)
     slots = owners * capacity
     table_new, accum_new = call(
         table_kernel, "table_part", [shape(*item_table.shape), shape(*accumulator.shape)],
         (recv, item_table, accumulator), 0,
-        [((slots, width), f32), ((slots, width), bf16), ((slots, width), bf16)], flops=10_000_000_000)
-    return grad_in, first[:, :width], table_new, accum_new
+        [((slots, width), f32), ((slots, width), bf16), ((slots, width), bf16)], grant=10)
+    pieces[-1] = after(pieces[-1], accum_new)
+    grad_in, grad_out = call(
+        gather_kernel, "gather", [shape(dp_size, piece, 4 * width), shape(dp_size, piece, width)], pieces)
+    return grad_in.reshape(-1, 4 * width), grad_out.reshape(-1, width), table_new, accum_new
 
 
 def solution(mesh):

time: 140 us -> 86.1 us (0.61)
  waiting for transfers between devices: 60.8 us -> 25.7 us
  blocking collectives: 26.6 us -> 0 us
  starting transfers between devices: 19.2 us -> 32.3 us
  other arithmetic: 6.19 us -> 0 us
  Pallas kernels: 18 us -> 21.6 us
  local copies, waits for them, and re-layouts: 7.11 us -> 4.76 us
    all_to_all x5 -> x1, waiting for transfers between devices: 60.8 us -> 0.01 us  [body(): lax.all_to_all(send, ('dp', 'rows'), split_axis=0, concat_axis=0, tiled=T...]
    ppermute x0 -> x18, starting transfers between devices: none -> 27.7 us  [the longest x12 16 us: body(): lax.ppermute(v, 'dp', [(i, i ^ bit) for i in range(dp_size)])]
    all_to_all x2 -> x0, blocking collectives: 26.6 us -> none  [exchange(): lax.all_to_all(v, axis, split_axis=0, concat_axis=0, axis_index_groups=gr...]
    ppermute x0 -> x18, waiting for transfers between devices: none -> 25.7 us  [the longest x12 17.9 us: body(): lax.ppermute(v, 'dp', [(i, i ^ bit) for i in range(dp_size)])]
    all_to_all x5 -> x1, starting transfers between devices: 18.6 us -> 3.97 us  [body(): lax.all_to_all(send, ('dp', 'rows'), split_axis=0, concat_axis=0, tiled=T...]
    add x2 -> x0, other arithmetic: 3.7 us -> none  [the longest x1 2.33 us: body(): both2 = after(keep2, send) + recv2]
    pallas_call x4 -> x10, Pallas kernels: 18 us -> 21.6 us  [call(): pl.pallas_call(kernel, name=name, in_specs=[pl.BlockSpec(memory_space=p o...]
    reduce_sum x4 -> x0, other arithmetic: 1.65 us -> none  [the longest x2 1.61 us: over_chips(): jnp.sum(parts, axis=0).reshape(chips, piece, -1)]
  transfers between devices with their start and end apart: 7 -> 21, of which waited for: 5 -> 10; matrix products, arithmetic and copies ran while one was open for 3% -> 0% of each run, Pallas kernels for 7% -> 15%
where the time goes in v5:
time: 86.1 us; the launch traced here: 85.7 us
  starting transfers between devices  32.3 us (38%)
  waiting for transfers between devices  25.7 us (30%)
  Pallas kernels  21.6 us (25%)
  local copies, waits for them, and re-layouts  4.76 us (6%)
  between operations  1.37 us (2%)
    pallas_call x10, Pallas kernels, call(): pl.pallas_call(kernel, name=name, in_specs=[pl.BlockSpec(memory_space=p o...  21.6 us
    ppermute x12, waiting for transfers between devices, body(): lax.ppermute(v, 'dp', [(i, i ^ bit) for i in range(dp_size)])  17.9 us
    ppermute x12, starting transfers between devices, body(): lax.ppermute(v, 'dp', [(i, i ^ bit) for i in range(dp_size)])  16 us
    ppermute x6, starting transfers between devices, body(): lax.ppermute(v, 'rows', [(i, (i + 2 * k) % rows_size) for i in range(rows...  11.7 us
    ppermute x6, waiting for transfers between devices, body(): lax.ppermute(v, 'rows', [(i, (i + 2 * k) % rows_size) for i in range(rows...  7.8 us
    unnamed x20, local copies, waits for them, and re-layouts  4.76 us
    all_to_all x1, starting transfers between devices, body(): lax.all_to_all(send, ('dp', 'rows'), split_axis=0, concat_axis=0, tiled=T...  3.97 us
  transfers between devices with their start and end apart: 21, of which 10 were waited for; matrix products, arithmetic and copies ran while one was open for 0% of the time, Pallas kernels for 15%

profile of v5, /device:TPU:0, one launch (start us, length us, event | category | flops | bytes accessed | tf_op | source)
XLA Modules:
  0.0 85.7 jit_solution(14993432771116706920)
XLA Ops:
  1.3 8.3 %forward_part.1 = (f32[256,1536]{1,0:T(8,128)S(1)}, f32[256,1536]{1,0:T(8,128)S(1)}, bf16[512,1536]{1,0:T(8,128)(2,1)S(1)}, bf16[512,1024]{1,0:T(8,128)(2,1)S(1)...) custom-call(s32[1]{0:T(128)S(6)} %copy.13.len_ref, ...), custom_call_target="tpu_custom_call" | custom-call | flops 99999997952 | bytes 65536 | tf_op jit(solution)/shard_map/forward_part/pallas_call | solution.py:361
  9.5 0.5 collective-permute-start
  10.1 4.1 %attention_part.1 = (f32[256,1024]{1,0:T(8,128)S(1)}, f32[256,1024]{1,0:T(8,128)S(1)}, bf16[512,1024]{1,0:T(8,128)(2,1)S(1)}) custom-call(s32[1]{0:T(128)S(6)} %copy.13.len_ref, bf16[512,1536]{1,0:T(8,128)(2,1)S(1)} %get-tuple-element.51.hid_ref, bf16[512,1024]{1,0:T(8,128)(2,1)S(1)} %get-tuple-element.52.dsilu_ref, ...), custom_call_target="tpu_custom_call" | custom-call | flops 99999997952 | bytes 65536 | tf_op jit(solution)/shard_map/attention_part/pallas_call | solution.py:361
  14.2 0.0 copy-start.4
  14.2 0.1 collective-permute-start.3
  14.3 0.0 collective-permute-done
  14.3 0.0 copy-start.1
  14.3 0.0 copy-start.2
  14.3 1.1 %first_sums.1 = (f32[2,64,768]{2,1,0:T(8,128)}, f32[2,64,768]{2,1,0:T(8,128)}, f32[2,64,768]{2,1,0:T(8,128)S(1)}, f32[2,64,768]{2,1,0:T(8,128)S(1)}) custom-call(f32[2,2,64,1536]{3,2,1,0:T(8,128)S(1)} %bitcast.20, f32[2,2,64,1536]{3,2,1,0:T(8,128)S(1)} %bitcast.15), custom_call_target="tpu_custom_call" | custom-call | flops 1000000000 | bytes 65536 | tf_op jit(solution)/shard_map/first_sums/pallas_call | solution.py:361
  15.4 0.0 copy-done.4
  15.4 0.7 copy-done.6
  16.2 0.8 copy-done.8
  16.9 2.9 %collective-permute-start.1 = (f32[2,64,768]{2,1,0:T(8,128)}, f32[2,64,768]{2,1,0:T(8,128)}, u32[]{:S(2)}, u32[]{:S(2)}) collective-permute-start(f32[2,64,768]{2,1,0:T(8,128)} %get-tuple-element.62), channel_id=1, source_target_pairs={{0,8},{8,0},{16,24},{24,16},{1,9},{9,1},{17,25},{25,17},{2,10},{10... | collective-permute-start | bytes 1179656 | tf_op jit(solution)/shard_map/ppermute | solution.py:379
  19.8 1.5 %collective-permute-start.2 = (f32[2,64,768]{2,1,0:T(8,128)}, f32[2,64,768]{2,1,0:T(8,128)}, u32[]{:S(2)}, u32[]{:S(2)}) collective-permute-start(f32[2,64,768]{2,1,0:T(8,128)} %get-tuple-element.63), channel_id=1, source_target_pairs={{0,16},{8,24},{16,0},{24,8},{1,17},{9,25},{17,1},{25,9},{2,18},{10... | collective-permute-start | bytes 1179656 | tf_op jit(solution)/shard_map/ppermute | solution.py:379
  21.4 0.0 copy-done.1
  21.4 0.0 copy-done.2
  21.4 3.4 %events_part.1 = f32[32,72,128]{2,1,0:T(8,128)} custom-call(s32[1]{0:T(128)S(6)} %copy.13.len_ref, bf16[512,512]{1,0:T(8,128)(2,1)S(1)} %get-tuple-element.58.ev_ref, bf16[512,512]{1,0:T(8,128)(2,1)S(1)} %get-tuple-element.59.cot_ref, bf16[512,2048]{1,0:T(8,128)(2,1)S(1)} %get-tuple-element.60.win_ref, s32[1,512]{1,0:T(1,128)S(1)} %copy-done.2, ...), custom_call_target="tpu_custom_call" | custom-call | flops 99999997952 | bytes 65536 | tf_op jit(solution)/shard_map/events_part/pallas_call | solution.py:361
  24.8 4.0 %all-to-all-start = ((f32[32,72,128]{2,1,0:T(8,128)}), f32[32,72,128]{2,1,0:T(8,128)S(1)}, u32[]{:S(2)}, u32[]{:S(2)}) async-start(f32[32,72,128]{2,1,0:T(8,128)} %events_part.1), calls=%async_computation | async-start | bytes 2359296 | tf_op jit(solution)/shard_map/all_to_all | solution.py:424
  28.8 0.0 collective-permute-done.3
  28.8 0.7 collective-permute-done.1.from_x_ref
  29.5 1.5 %collective-permute-done.2.from_y_ref = f32[2,64,768]{2,1,0:T(8,128)} collective-permute-done((f32[2,64,768]{2,1,0:T(8,128)}, f32[2,64,768]{2,1,0:T(8,128)}, u32[]{:S(2)}, u32[]{:S(2)}) %collective-permute-start.2) | collective-permute-done | bytes 393248 | tf_op jit(solution)/shard_map/ppermute | solution.py:379
  31.0 1.2 %copy-done.5 = f32[256,1024]{1,0:T(8,128)S(1)} copy-done((f32[256,1024]{1,0:T(8,128)S(1)}, f32[256,1024]{1,0:T(8,128)}, u32[]{:S(2)}) %copy-start.5) | copy-done | bytes 1048600
  32.2 1.0 %copy-done.7 = f32[2,64,768]{2,1,0:T(8,128)S(1)} copy-done((f32[2,64,768]{2,1,0:T(8,128)S(1)}, f32[2,64,768]{2,1,0:T(8,128)}, u32[]{:S(2)}) %copy-start.7) | copy-done | bytes 393240
  33.2 1.0 %copy-done.9 = f32[2,64,768]{2,1,0:T(8,128)S(1)} copy-done((f32[2,64,768]{2,1,0:T(8,128)S(1)}, f32[2,64,768]{2,1,0:T(8,128)}, u32[]{:S(2)}) %copy-start.9) | copy-done | bytes 393240
  34.2 1.3 %second_sums.1 = (f32[64,1792]{1,0:T(8,128)S(1)}, f32[64,1792]{1,0:T(8,128)S(1)}, f32[64,768]{1,0:T(8,128)S(1)}, f32[64,768]{1,0:T(8,128)S(1)}, f32[2,64,512]{2,1,0:T(8,128)S(1)}, /*index=5*/f32[2,64,512]{2,1,0:T(8,128)S(1)}) custom-call(f32[2,64,768]{2,1,0:T(8,128)S(1)} %copy-done.7, f32[2,64,768]{2,1,0:T(8,128)} %collective-permute-done.1.from_x_ref, ...), custom_call_target="tpu_custom_call" | custom-call | flops 99999997952 | bytes 65536 | tf_op jit(solution)/shard_map/second_sums/pallas_call | solution.py:361
  35.5 0.4 collective-permute-start.4
  35.9 1.7 %collective-permute-start.5 = (f32[64,1792]{1,0:T(8,128)S(1)}, f32[64,1792]{1,0:T(8,128)S(1)}, u32[]{:S(2)}, u32[]{:S(2)}) collective-permute-start(f32[64,1792]{1,0:T(8,128)S(1)} %get-tuple-element.72), channel_id=1, source_target_pairs={{0,16},{8,24},{16,0},{24,8},{1,17},{9,25},{17,1},{25,9},{2,18},{10... | collective-permute-start | bytes 1376264 | tf_op jit(solution)/shard_map/ppermute | solution.py:379
  37.6 15.0 %collective-permute-done.4 = f32[64,1792]{1,0:T(8,128)S(1)} collective-permute-done((f32[64,1792]{1,0:T(8,128)S(1)}, f32[64,1792]{1,0:T(8,128)S(1)}, u32[]{:S(2)}, u32[]{:S(2)}) %collective-permute-start.4) | collective-permute-done | bytes 458784 | tf_op jit(solution)/shard_map/ppermute | solution.py:379
  52.6 0.3 collective-permute-done.5
  53.0 0.1 third_sums.1
  53.1 1.4 %collective-permute-start.9 = (f32[4,16,512]{2,1,0:T(8,128)S(1)}, f32[4,16,512]{2,1,0:T(8,128)S(1)}, u32[]{:S(2)}, u32[]{:S(2)}) collective-permute-start(f32[4,16,512]{2,1,0:T(8,128)S(1)} %get-tuple-element.81), channel_id=1, source_target_pairs={{0,8},{8,0},{16,24},{24,16},{1,9},{9,1},{17,25},{25,17},{2,10},{10... | collective-permute-start | bytes 393224 | tf_op jit(solution)/shard_map/ppermute | solution.py:379
  54.4 1.0 %collective-permute-start.10 = (f32[4,16,512]{2,1,0:T(8,128)S(1)}, f32[4,16,512]{2,1,0:T(8,128)S(1)}, u32[]{:S(2)}, u32[]{:S(2)}) collective-permute-start(f32[4,16,512]{2,1,0:T(8,128)S(1)} %get-tuple-element.82), channel_id=1, source_target_pairs={{0,16},{8,24},{16,0},{24,8},{1,17},{9,25},{17,1},{25,9},{2,18},{10... | collective-permute-start | bytes 393224 | tf_op jit(solution)/shard_map/ppermute | solution.py:379
  55.4 2.6 %collective-permute-start.6 = (f32[16,1536]{1,0:T(8,128)S(1)}, f32[16,1536]{1,0:T(8,128)S(1)}, u32[]{:S(2)}, u32[]{:S(2)}) collective-permute-start(f32[16,1536]{1,0:T(8,128)S(1)} %get-tuple-element.76), channel_id=1, source_target_pairs={{0,2},{1,3},{2,4},{3,5},{4,6},{5,7},{6,0},{7,1},{8,10},{9,11},{10,... | collective-permute-start | bytes 294920 | tf_op jit(solution)/shard_map/ppermute | solution.py:380
  58.0 2.2 %collective-permute-start.7 = (f32[16,1536]{1,0:T(8,128)S(1)}, f32[16,1536]{1,0:T(8,128)S(1)}, u32[]{:S(2)}, u32[]{:S(2)}) collective-permute-start(f32[16,1536]{1,0:T(8,128)S(1)} %get-tuple-element.77), channel_id=1, source_target_pairs={{0,4},{1,5},{2,6},{3,7},{4,0},{5,1},{6,2},{7,3},{8,12},{9,13},{10,... | collective-permute-start | bytes 294920 | tf_op jit(solution)/shard_map/ppermute | solution.py:380
  60.2 1.5 %collective-permute-start.8 = (f32[16,1536]{1,0:T(8,128)S(1)}, f32[16,1536]{1,0:T(8,128)S(1)}, u32[]{:S(2)}, u32[]{:S(2)}) collective-permute-start(f32[16,1536]{1,0:T(8,128)S(1)} %get-tuple-element.78), channel_id=1, source_target_pairs={{0,6},{1,7},{2,0},{3,1},{4,2},{5,3},{6,4},{7,5},{8,14},{9,15},{10,... | collective-permute-start | bytes 294920 | tf_op jit(solution)/shard_map/ppermute | solution.py:380
  61.7 1.7 %collective-permute-done.6.refs_1_ = f32[16,1536]{1,0:T(8,128)S(1)} collective-permute-done((f32[16,1536]{1,0:T(8,128)S(1)}, f32[16,1536]{1,0:T(8,128)S(1)}, u32[]{:S(2)}, u32[]{:S(2)}) %collective-permute-start.6) | collective-permute-done | bytes 98336 | tf_op jit(solution)/shard_map/ppermute | solution.py:380
  63.4 2.8 %collective-permute-done.7.refs_2_ = f32[16,1536]{1,0:T(8,128)S(1)} collective-permute-done((f32[16,1536]{1,0:T(8,128)S(1)}, f32[16,1536]{1,0:T(8,128)S(1)}, u32[]{:S(2)}, u32[]{:S(2)}) %collective-permute-start.7) | collective-permute-done | bytes 98336 | tf_op jit(solution)/shard_map/ppermute | solution.py:380
  66.2 0.0 collective-permute-done.8.refs_3_
  66.2 0.0 collective-permute-done.9.refs_6_
  66.2 0.0 collective-permute-done.10.refs_7_
  66.3 1.6 %collective-permute-start.13 = (f32[16,1536]{1,0:T(8,128)S(1)}, f32[16,1536]{1,0:T(8,128)S(1)}, u32[]{:S(2)}, u32[]{:S(2)}) collective-permute-start(f32[16,1536]{1,0:T(8,128)S(1)} %get-tuple-element.83.refs_0_), channel_id=1, source_target_pairs={{0,24},{8,16},{16,8},{24,0},{1,25},{9,17},{17,9},{25,1},{2,26},{10... | collective-permute-start | bytes 294920 | tf_op jit(solution)/shard_map/ppermute | solution.py:379
  67.8 0.7 collective-permute-start.12
  68.5 1.3 %collective-permute-start.11 = (f32[16,1536]{1,0:T(8,128)S(1)}, f32[16,1536]{1,0:T(8,128)S(1)}, u32[]{:S(2)}, u32[]{:S(2)}) collective-permute-start(f32[16,1536]{1,0:T(8,128)S(1)} %get-tuple-element.83.refs_0_), channel_id=1, source_target_pairs={{0,8},{8,0},{16,24},{24,16},{1,9},{9,1},{17,25},{25,17},{2,10},{10... | collective-permute-start | bytes 294920 | tf_op jit(solution)/shard_map/ppermute | solution.py:379
  69.8 2.1 %collective-permute-start.14 = (f32[16,1024]{1,0:T(8,128)S(1)}, f32[16,1024]{1,0:T(8,128)S(1)}, u32[]{:S(2)}, u32[]{:S(2)}) collective-permute-start(f32[16,1024]{1,0:T(8,128)S(1)} %get-tuple-element.86), channel_id=1, source_target_pairs={{0,2},{1,3},{2,4},{3,5},{4,6},{5,7},{6,0},{7,1},{8,10},{9,11},{10,... | collective-permute-start | bytes 196616 | tf_op jit(solution)/shard_map/ppermute | solution.py:380
  71.9 1.7 %collective-permute-start.15 = (f32[16,1024]{1,0:T(8,128)S(1)}, f32[16,1024]{1,0:T(8,128)S(1)}, u32[]{:S(2)}, u32[]{:S(2)}) collective-permute-start(f32[16,1024]{1,0:T(8,128)S(1)} %get-tuple-element.87), channel_id=1, source_target_pairs={{0,4},{1,5},{2,6},{3,7},{4,0},{5,1},{6,2},{7,3},{8,12},{9,13},{10,... | collective-permute-start | bytes 196616 | tf_op jit(solution)/shard_map/ppermute | solution.py:380
  73.6 0.0 collective-permute-done.13.refs_3_
  73.6 1.6 %collective-permute-start.16 = (f32[16,1024]{1,0:T(8,128)S(1)}, f32[16,1024]{1,0:T(8,128)S(1)}, u32[]{:S(2)}, u32[]{:S(2)}) collective-permute-start(f32[16,1024]{1,0:T(8,128)S(1)} %get-tuple-element.88), channel_id=1, source_target_pairs={{0,6},{1,7},{2,0},{3,1},{4,2},{5,3},{6,4},{7,5},{8,14},{9,15},{10,... | collective-permute-start | bytes 196616 | tf_op jit(solution)/shard_map/ppermute | solution.py:380
  75.2 0.0 collective-permute-done.12.refs_2_
  75.2 0.0 collective-permute-done.11.refs_1_
  75.2 0.0 copy-start.3
  75.2 1.1 %collective-permute-done.14.refs_1_ = f32[16,1024]{1,0:T(8,128)S(1)} collective-permute-done((f32[16,1024]{1,0:T(8,128)S(1)}, f32[16,1024]{1,0:T(8,128)S(1)}, u32[]{:S(2)}, u32[]{:S(2)}) %collective-permute-start.14) | collective-permute-done | bytes 65568 | tf_op jit(solution)/shard_map/ppermute | solution.py:380
  76.3 2.1 %collective-permute-done.15.refs_2_ = f32[16,1024]{1,0:T(8,128)S(1)} collective-permute-done((f32[16,1024]{1,0:T(8,128)S(1)}, f32[16,1024]{1,0:T(8,128)S(1)}, u32[]{:S(2)}, u32[]{:S(2)}) %collective-permute-start.15) | collective-permute-done | bytes 65568 | tf_op jit(solution)/shard_map/ppermute | solution.py:380
  78.4 0.1 collective-permute-done.16.refs_3_
  78.5 1.5 %collective-permute-start.19 = (f32[16,1024]{1,0:T(8,128)S(1)}, f32[16,1024]{1,0:T(8,128)S(1)}, u32[]{:S(2)}, u32[]{:S(2)}) collective-permute-start(f32[16,1024]{1,0:T(8,128)S(1)} %last_sums.1.refs_4_), channel_id=1, source_target_pairs={{0,24},{8,16},{16,8},{24,0},{1,25},{9,17},{17,9},{25,1},{2,26},{10... | collective-permute-start | bytes 196616 | tf_op jit(solution)/shard_map/ppermute | solution.py:379
  80.0 0.5 collective-permute-start.18
  80.5 1.5 %collective-permute-start.17 = (f32[16,1024]{1,0:T(8,128)S(1)}, f32[16,1024]{1,0:T(8,128)S(1)}, u32[]{:S(2)}, u32[]{:S(2)}) collective-permute-start(f32[16,1024]{1,0:T(8,128)S(1)} %last_sums.1.refs_4_), channel_id=1, source_target_pairs={{0,8},{8,0},{16,24},{24,16},{1,9},{9,1},{17,25},{25,17},{2,10},{10... | collective-permute-start | bytes 196616 | tf_op jit(solution)/shard_map/ppermute | solution.py:379
  82.1 0.0 all-to-all-done.recv_ref
  82.1 0.0 copy-done
  82.1 0.0 copy-done.3
  82.1 2.4 %table_part.1 = (f32[512,512]{1,0:T(8,128)}, f32[512]{0:T(512)}) custom-call(f32[32,72,128]{2,1,0:T(8,128)S(1)} %all-to-all-done.recv_ref, f32[512,512]{1,0:T(8,128)S(1)} %copy-done, f32[512]{0:T(512)S(1)} %copy-done.3), custom_call_target="tpu_custom_call" | custom-call | flops 1000000000 | bytes 65536 | tf_op jit(solution)/shard_map/table_part/pallas_call | solution.py:361
  84.5 0.0 collective-permute-done.19.refs_7_
  84.5 0.0 collective-permute-done.18.refs_6_
  84.5 0.3 collective-permute-done.17.refs_5_
  84.8 0.9 %gather.1 = (f32[4,16,2048]{2,1,0:T(8,128)}, f32[4,16,512]{2,1,0:T(8,128)}) custom-call(f32[16,1536]{1,0:T(8,128)S(1)} %get-tuple-element.83.refs_0_, f32[16,1536]{1,0:T(8,128)S(1)} %collective-permute-done.11.refs_1_, f32[16,1536]{1,0:T(8,128)S(1)} %collective-permute-done.12.refs_2_, f32[16,1536]{1,0:T(8,128)S(1)} %collective-permute-done.13.refs_3_, ...), custom_call_target="tpu_custom_call" | custom-call | flops 1000000000 | bytes 65536 | tf_op jit(solution)/shard_map/gather/pallas_call | solution.py:361
  (8 shorter events, 0.1 us)
Async XLA Ops:
  9.5 4.8 %collective-permute-start = (f32[256,1536]{1,0:T(8,128)S(1)}, f32[256,1536]{1,0:T(8,128)S(1)}, u32[]{:S(2)}, u32[]{:S(2)}) collective-permute-start(f32[256,1536]{1,0:T(8,128)S(1)} %get-tuple-element.50), channel_id=1, source_target_pairs={{0,1},{1,0},{2,3},{3,2},{4,5},{5,4},{6,7},{7,6},{8,9},{9,8},{10,11... | collective-permute-start | bytes 4718600 | tf_op jit(solution)/shard_map/ppermute | solution.py:410
  14.2 1.2 %copy-start.4 = (f32[256,1024]{1,0:T(8,128)}, f32[256,1024]{1,0:T(8,128)S(1)}, u32[]{:S(2)}) copy-start(f32[256,1024]{1,0:T(8,128)S(1)} %get-tuple-element.55) | copy-start | bytes 3145732
  14.2 14.6 %collective-permute-start.3 = (f32[256,1024]{1,0:T(8,128)S(1)}, f32[256,1024]{1,0:T(8,128)S(1)}, u32[]{:S(2)}, u32[]{:S(2)}) collective-permute-start(f32[256,1024]{1,0:T(8,128)S(1)} %get-tuple-element.68), channel_id=1, source_target_pairs={{0,1},{1,0},{2,3},{3,2},{4,5},{5,4},{6,7},{7,6},{8,9},{9,8},{10,11... | collective-permute-start | bytes 3145736 | tf_op jit(solution)/shard_map/ppermute | solution.py:414
  14.3 7.0 %copy-start.1 = (s32[1,32,16]{1,2,0:T(8,128)S(1)}, s32[1,32,16]{1,2,0:T(8,128)}, u32[]{:S(2)}) copy-start(s32[1,32,16]{1,2,0:T(8,128)} %param.14) | copy-start | bytes 6148
  14.3 7.0 %copy-start.2 = (s32[1,512]{1,0:T(1,128)S(1)}, s32[1,512]{1,0:T(1,128)}, u32[]{:S(2)}) copy-start(s32[1,512]{1,0:T(1,128)} %slot_ref.1) | copy-start | bytes 6148
  15.4 0.7 copy-start.6
  16.2 0.8 copy-start.8
  16.9 12.6 %collective-permute-start.1 = (f32[2,64,768]{2,1,0:T(8,128)}, f32[2,64,768]{2,1,0:T(8,128)}, u32[]{:S(2)}, u32[]{:S(2)}) collective-permute-start(f32[2,64,768]{2,1,0:T(8,128)} %get-tuple-element.62), channel_id=1, source_target_pairs={{0,8},{8,0},{16,24},{24,16},{1,9},{9,1},{17,25},{25,17},{2,10},{10... | collective-permute-start | bytes 1179656 | tf_op jit(solution)/shard_map/ppermute | solution.py:379
  19.8 11.1 %collective-permute-start.2 = (f32[2,64,768]{2,1,0:T(8,128)}, f32[2,64,768]{2,1,0:T(8,128)}, u32[]{:S(2)}, u32[]{:S(2)}) collective-permute-start(f32[2,64,768]{2,1,0:T(8,128)} %get-tuple-element.63), channel_id=1, source_target_pairs={{0,16},{8,24},{16,0},{24,8},{1,17},{9,25},{17,1},{25,9},{2,18},{10... | collective-permute-start | bytes 1179656 | tf_op jit(solution)/shard_map/ppermute | solution.py:379
  24.8 57.3 %all-to-all-start = ((f32[32,72,128]{2,1,0:T(8,128)}), f32[32,72,128]{2,1,0:T(8,128)S(1)}, u32[]{:S(2)}, u32[]{:S(2)}) async-start(f32[32,72,128]{2,1,0:T(8,128)} %events_part.1), calls=%async_computation | async-start | bytes 2359296 | tf_op jit(solution)/shard_map/all_to_all | solution.py:424
  31.0 1.2 %copy-start.5 = (f32[256,1024]{1,0:T(8,128)S(1)}, f32[256,1024]{1,0:T(8,128)}, u32[]{:S(2)}) copy-start(f32[256,1024]{1,0:T(8,128)} %copy-done.4) | copy-start | bytes 3145732
  32.2 1.0 %copy-start.7 = (f32[2,64,768]{2,1,0:T(8,128)S(1)}, f32[2,64,768]{2,1,0:T(8,128)}, u32[]{:S(2)}) copy-start(f32[2,64,768]{2,1,0:T(8,128)} %copy-done.6) | copy-start | bytes 1179652
  33.2 1.0 %copy-start.9 = (f32[2,64,768]{2,1,0:T(8,128)S(1)}, f32[2,64,768]{2,1,0:T(8,128)}, u32[]{:S(2)}) copy-start(f32[2,64,768]{2,1,0:T(8,128)} %copy-done.8) | copy-start | bytes 1179652
  35.5 17.1 %collective-permute-start.4 = (f32[64,1792]{1,0:T(8,128)S(1)}, f32[64,1792]{1,0:T(8,128)S(1)}, u32[]{:S(2)}, u32[]{:S(2)}) collective-permute-start(f32[64,1792]{1,0:T(8,128)S(1)} %get-tuple-element.71), channel_id=1, source_target_pairs={{0,8},{8,0},{16,24},{24,16},{1,9},{9,1},{17,25},{25,17},{2,10},{10... | collective-permute-start | bytes 1376264 | tf_op jit(solution)/shard_map/ppermute | solution.py:379
  35.9 17.1 %collective-permute-start.5 = (f32[64,1792]{1,0:T(8,128)S(1)}, f32[64,1792]{1,0:T(8,128)S(1)}, u32[]{:S(2)}, u32[]{:S(2)}) collective-permute-start(f32[64,1792]{1,0:T(8,128)S(1)} %get-tuple-element.72), channel_id=1, source_target_pairs={{0,16},{8,24},{16,0},{24,8},{1,17},{9,25},{17,1},{25,9},{2,18},{10... | collective-permute-start | bytes 1376264 | tf_op jit(solution)/shard_map/ppermute | solution.py:379
  53.1 13.1 %collective-permute-start.9 = (f32[4,16,512]{2,1,0:T(8,128)S(1)}, f32[4,16,512]{2,1,0:T(8,128)S(1)}, u32[]{:S(2)}, u32[]{:S(2)}) collective-permute-start(f32[4,16,512]{2,1,0:T(8,128)S(1)} %get-tuple-element.81), channel_id=1, source_target_pairs={{0,8},{8,0},{16,24},{24,16},{1,9},{9,1},{17,25},{25,17},{2,10},{10... | collective-permute-start | bytes 393224 | tf_op jit(solution)/shard_map/ppermute | solution.py:379
  54.4 11.8 %collective-permute-start.10 = (f32[4,16,512]{2,1,0:T(8,128)S(1)}, f32[4,16,512]{2,1,0:T(8,128)S(1)}, u32[]{:S(2)}, u32[]{:S(2)}) collective-permute-start(f32[4,16,512]{2,1,0:T(8,128)S(1)} %get-tuple-element.82), channel_id=1, source_target_pairs={{0,16},{8,24},{16,0},{24,8},{1,17},{9,25},{17,1},{25,9},{2,18},{10... | collective-permute-start | bytes 393224 | tf_op jit(solution)/shard_map/ppermute | solution.py:379
  55.4 8.0 %collective-permute-start.6 = (f32[16,1536]{1,0:T(8,128)S(1)}, f32[16,1536]{1,0:T(8,128)S(1)}, u32[]{:S(2)}, u32[]{:S(2)}) collective-permute-start(f32[16,1536]{1,0:T(8,128)S(1)} %get-tuple-element.76), channel_id=1, source_target_pairs={{0,2},{1,3},{2,4},{3,5},{4,6},{5,7},{6,0},{7,1},{8,10},{9,11},{10,... | collective-permute-start | bytes 294920 | tf_op jit(solution)/shard_map/ppermute | solution.py:380
  58.0 8.2 %collective-permute-start.7 = (f32[16,1536]{1,0:T(8,128)S(1)}, f32[16,1536]{1,0:T(8,128)S(1)}, u32[]{:S(2)}, u32[]{:S(2)}) collective-permute-start(f32[16,1536]{1,0:T(8,128)S(1)} %get-tuple-element.77), channel_id=1, source_target_pairs={{0,4},{1,5},{2,6},{3,7},{4,0},{5,1},{6,2},{7,3},{8,12},{9,13},{10,... | collective-permute-start | bytes 294920 | tf_op jit(solution)/shard_map/ppermute | solution.py:380
  60.2 6.0 %collective-permute-start.8 = (f32[16,1536]{1,0:T(8,128)S(1)}, f32[16,1536]{1,0:T(8,128)S(1)}, u32[]{:S(2)}, u32[]{:S(2)}) collective-permute-start(f32[16,1536]{1,0:T(8,128)S(1)} %get-tuple-element.78), channel_id=1, source_target_pairs={{0,6},{1,7},{2,0},{3,1},{4,2},{5,3},{6,4},{7,5},{8,14},{9,15},{10,... | collective-permute-start | bytes 294920 | tf_op jit(solution)/shard_map/ppermute | solution.py:380
  66.3 7.4 %collective-permute-start.13 = (f32[16,1536]{1,0:T(8,128)S(1)}, f32[16,1536]{1,0:T(8,128)S(1)}, u32[]{:S(2)}, u32[]{:S(2)}) collective-permute-start(f32[16,1536]{1,0:T(8,128)S(1)} %get-tuple-element.83.refs_0_), channel_id=1, source_target_pairs={{0,24},{8,16},{16,8},{24,0},{1,25},{9,17},{17,9},{25,1},{2,26},{10... | collective-permute-start | bytes 294920 | tf_op jit(solution)/shard_map/ppermute | solution.py:379
  67.8 7.4 %collective-permute-start.12 = (f32[16,1536]{1,0:T(8,128)S(1)}, f32[16,1536]{1,0:T(8,128)S(1)}, u32[]{:S(2)}, u32[]{:S(2)}) collective-permute-start(f32[16,1536]{1,0:T(8,128)S(1)} %get-tuple-element.83.refs_0_), channel_id=1, source_target_pairs={{0,16},{8,24},{16,0},{24,8},{1,17},{9,25},{17,1},{25,9},{2,18},{10... | collective-permute-start | bytes 294920 | tf_op jit(solution)/shard_map/ppermute | solution.py:379
  68.5 6.7 %collective-permute-start.11 = (f32[16,1536]{1,0:T(8,128)S(1)}, f32[16,1536]{1,0:T(8,128)S(1)}, u32[]{:S(2)}, u32[]{:S(2)}) collective-permute-start(f32[16,1536]{1,0:T(8,128)S(1)} %get-tuple-element.83.refs_0_), channel_id=1, source_target_pairs={{0,8},{8,0},{16,24},{24,16},{1,9},{9,1},{17,25},{25,17},{2,10},{10... | collective-permute-start | bytes 294920 | tf_op jit(solution)/shard_map/ppermute | solution.py:379
  69.8 6.5 %collective-permute-start.14 = (f32[16,1024]{1,0:T(8,128)S(1)}, f32[16,1024]{1,0:T(8,128)S(1)}, u32[]{:S(2)}, u32[]{:S(2)}) collective-permute-start(f32[16,1024]{1,0:T(8,128)S(1)} %get-tuple-element.86), channel_id=1, source_target_pairs={{0,2},{1,3},{2,4},{3,5},{4,6},{5,7},{6,0},{7,1},{8,10},{9,11},{10,... | collective-permute-start | bytes 196616 | tf_op jit(solution)/shard_map/ppermute | solution.py:380
  71.9 6.5 %collective-permute-start.15 = (f32[16,1024]{1,0:T(8,128)S(1)}, f32[16,1024]{1,0:T(8,128)S(1)}, u32[]{:S(2)}, u32[]{:S(2)}) collective-permute-start(f32[16,1024]{1,0:T(8,128)S(1)} %get-tuple-element.87), channel_id=1, source_target_pairs={{0,4},{1,5},{2,6},{3,7},{4,0},{5,1},{6,2},{7,3},{8,12},{9,13},{10,... | collective-permute-start | bytes 196616 | tf_op jit(solution)/shard_map/ppermute | solution.py:380
  73.6 4.9 %collective-permute-start.16 = (f32[16,1024]{1,0:T(8,128)S(1)}, f32[16,1024]{1,0:T(8,128)S(1)}, u32[]{:S(2)}, u32[]{:S(2)}) collective-permute-start(f32[16,1024]{1,0:T(8,128)S(1)} %get-tuple-element.88), channel_id=1, source_target_pairs={{0,6},{1,7},{2,0},{3,1},{4,2},{5,3},{6,4},{7,5},{8,14},{9,15},{10,... | collective-permute-start | bytes 196616 | tf_op jit(solution)/shard_map/ppermute | solution.py:380
  75.2 6.9 %copy-start = (f32[512,512]{1,0:T(8,128)S(1)}, f32[512,512]{1,0:T(8,128)}, u32[]{:S(2)}) copy-start(f32[512,512]{1,0:T(8,128)} %table_ref.1) | copy-start | bytes 3145732
  75.2 6.9 %copy-start.3 = (f32[512]{0:T(512)S(1)}, f32[512]{0:T(512)}, u32[]{:S(2)}) copy-start(f32[512]{0:T(512)} %accum_ref.1) | copy-start | bytes 6148
  78.5 5.9 %collective-permute-start.19 = (f32[16,1024]{1,0:T(8,128)S(1)}, f32[16,1024]{1,0:T(8,128)S(1)}, u32[]{:S(2)}, u32[]{:S(2)}) collective-permute-start(f32[16,1024]{1,0:T(8,128)S(1)} %last_sums.1.refs_4_), channel_id=1, source_target_pairs={{0,24},{8,16},{16,8},{24,0},{1,25},{9,17},{17,9},{25,1},{2,26},{10... | collective-permute-start | bytes 196616 | tf_op jit(solution)/shard_map/ppermute | solution.py:379
  80.0 4.5 %collective-permute-start.18 = (f32[16,1024]{1,0:T(8,128)S(1)}, f32[16,1024]{1,0:T(8,128)S(1)}, u32[]{:S(2)}, u32[]{:S(2)}) collective-permute-start(f32[16,1024]{1,0:T(8,128)S(1)} %last_sums.1.refs_4_), channel_id=1, source_target_pairs={{0,16},{8,24},{16,0},{24,8},{1,17},{9,25},{17,1},{25,9},{2,18},{10... | collective-permute-start | bytes 196616 | tf_op jit(solution)/shard_map/ppermute | solution.py:379
  80.5 4.3 %collective-permute-start.17 = (f32[16,1024]{1,0:T(8,128)S(1)}, f32[16,1024]{1,0:T(8,128)S(1)}, u32[]{:S(2)}, u32[]{:S(2)}) collective-permute-start(f32[16,1024]{1,0:T(8,128)S(1)} %last_sums.1.refs_4_), channel_id=1, source_target_pairs={{0,8},{8,0},{16,24},{24,16},{1,9},{9,1},{17,25},{25,17},{2,10},{10... | collective-permute-start | bytes 196616 | tf_op jit(solution)/shard_map/ppermute | solution.py:379

commit v6 on v5

--- a/solution.py
+++ b/solution.py
@@ -355,9 +355,9 @@
     return jax.ShapeDtypeStruct(dims, dtype)
 
 
-def call(kernel, name, out_shape, args, scalars=0, scratch=(), far=0, long=False, grant=4):
+def call(kernel, name, out_shape, args, scalars=0, scratch=(), far=0, long=False, grant=4, tied=True):
     place = [None] * scalars + [pltpu.HBM] * far + [pltpu.VMEM] * (len(args) - scalars - far)
-    args = [a if p is None else pltpu.with_memory_space_constraint(a, p) for a, p in zip(args, place)]
+    args = [a if p is None or not tied else pltpu.with_memory_space_constraint(a, p) for a, p in zip(args, place)]
     return pl.pallas_call(
         kernel,
         name=name,
@@ -421,17 +421,18 @@
         events_kernel, "events_part", [local(owners, pay_rows, LANES)],
         (lengths, events, cotangent, w_in, event_slot, slot_row[0].T, gpre_uv, gpre_qk), 1,
         [((tokens, width), bf16), ((tokens, width), bf16), ((owners * capacity, width), f32)], long=True, grant=10)
-    recv = lax.all_to_all(send, ("dp", "rows"), split_axis=0, concat_axis=0, tiled=True)
     from_x, from_y = over_dp(to_x, 1), over_dp(to_y, 2)
     to_x, to_y, next_a, next_b, keep2_a, keep2_b = call(
         second_kernel, "second_sums",
-        [local(strip, half1 + 2 * half2)] * 2 + [local(strip, half1)] * 2 + [local(2, strip, half2)] * 2,
-        (after(keep_a, send), from_x, keep_b, from_y, by_dp(keep2), by_dp(recv2)), long=True)
+        [shape(strip, half1 + 2 * half2)] * 2 + [shape(strip, half1)] * 2 + [shape(2, strip, half2)] * 2,
+        (after(keep_a, send), from_x, keep_b, from_y, by_dp(keep2), by_dp(recv2)), grant=10)
+    send = after(send, to_x, to_y)
+    recv = lax.all_to_all(send, ("dp", "rows"), split_axis=0, concat_axis=0, tiled=True)
     from_x, from_y = over_dp(to_x, 1), over_dp(to_y, 2)
     *blocks, to_x, to_y, next2_a, next2_b = call(
         functools.partial(third_kernel, chips), "third_sums",
         [local(piece, 2 * half1)] * chips + [local(chips, piece, half2)] * 4,
-        [by_chip(v) for v in (next_a, next_b, from_x, from_y, keep2_a, keep2_b)])
+        [by_chip(v) for v in (next_a, next_b, from_x, from_y, keep2_a, keep2_b)], long=True, grant=10, tied=False)
     from_x, from_y = over_dp(to_x, 1), over_dp(to_y, 2)
     total, *blocks = call(
         functools.partial(fourth_kernel, chips, tokens), "fourth_sums",

time: 86.1 us -> 93.3 us (1.084)
  waiting for transfers between devices: 25.7 us -> 31.8 us
  starting transfers between devices: 32.3 us -> 37.1 us
  Pallas kernels: 21.6 us -> 19.6 us
  local copies, waits for them, and re-layouts: 4.76 us -> 3.22 us
    ppermute x6, waiting for transfers between devices: 7.8 us -> 15.5 us  [body(): lax.ppermute(v, 'rows', [(i, (i + 2 * k) % rows_size) for i in range(rows...]
    ppermute x12, starting transfers between devices: 16 us -> 21.7 us  [body(): lax.ppermute(v, 'dp', [(i, i ^ bit) for i in range(dp_size)])]
    pallas_call x10, Pallas kernels: 21.6 us -> 19.6 us  [call(): pl.pallas_call(kernel, name=name, in_specs=[pl.BlockSpec(memory_space=p o...]
    ppermute x6, starting transfers between devices: 11.7 us -> 9.82 us  [body(): lax.ppermute(v, 'rows', [(i, (i + 2 * k) % rows_size) for i in range(rows...]
    ppermute x12, waiting for transfers between devices: 17.9 us -> 16.3 us  [body(): lax.ppermute(v, 'dp', [(i, i ^ bit) for i in range(dp_size)])]
    unnamed x20 -> x16, local copies, waits for them, and re-layouts: 4.76 us -> 3.22 us
  transfers between devices with their start and end apart: 21 -> 21, of which waited for: 10 -> 11; matrix products, arithmetic and copies ran while one was open for 0% -> 0% of each run, Pallas kernels for 15% -> 11%
where the time goes in v6:
time: 93.3 us; the launch traced here: 93 us
  starting transfers between devices  37.1 us (40%)
  waiting for transfers between devices  31.8 us (34%)
  Pallas kernels  19.6 us (21%)
  local copies, waits for them, and re-layouts  3.22 us (3%)
  between operations  1.38 us (1%)
    ppermute x12, starting transfers between devices, body(): lax.ppermute(v, 'dp', [(i, i ^ bit) for i in range(dp_size)])  21.7 us
    pallas_call x10, Pallas kernels, call(): pl.pallas_call(kernel, name=name, in_specs=[pl.BlockSpec(memory_space=p o...  19.6 us
    ppermute x12, waiting for transfers between devices, body(): lax.ppermute(v, 'dp', [(i, i ^ bit) for i in range(dp_size)])  16.3 us
    ppermute x6, waiting for transfers between devices, body(): lax.ppermute(v, 'rows', [(i, (i + 2 * k) % rows_size) for i in range(rows...  15.5 us
    ppermute x6, starting transfers between devices, body(): lax.ppermute(v, 'rows', [(i, (i + 2 * k) % rows_size) for i in range(rows...  9.82 us
    all_to_all x1, starting transfers between devices, body(): lax.all_to_all(send, ('dp', 'rows'), split_axis=0, concat_axis=0, tiled=T...  4.89 us
    unnamed x16, local copies, waits for them, and re-layouts  3.22 us
  transfers between devices with their start and end apart: 21, of which 11 were waited for; matrix products, arithmetic and copies ran while one was open for 0% of the time, Pallas kernels for 11%

profile of v6, /device:TPU:0, one launch (start us, length us, event | category | flops | bytes accessed | tf_op | source)
XLA Modules:
  0.0 93.0 jit_solution(3052643239728439021)
XLA Ops:
  1.3 8.3 %forward_part.1 = (f32[256,1536]{1,0:T(8,128)S(1)}, f32[256,1536]{1,0:T(8,128)S(1)}, bf16[512,1536]{1,0:T(8,128)(2,1)S(1)}, bf16[512,1024]{1,0:T(8,128)(2,1)S(1)...) custom-call(s32[1]{0:T(128)S(6)} %copy.13.len_ref, ...), custom_call_target="tpu_custom_call" | custom-call | flops 99999997952 | bytes 65536 | tf_op jit(solution)/shard_map/forward_part/pallas_call | solution.py:361
  9.5 0.5 collective-permute-start
  10.1 4.1 %attention_part.1 = (f32[256,1024]{1,0:T(8,128)S(1)}, f32[256,1024]{1,0:T(8,128)S(1)}, bf16[512,1024]{1,0:T(8,128)(2,1)S(1)}) custom-call(s32[1]{0:T(128)S(6)} %copy.13.len_ref, bf16[512,1536]{1,0:T(8,128)(2,1)S(1)} %get-tuple-element.52.hid_ref, bf16[512,1024]{1,0:T(8,128)(2,1)S(1)} %get-tuple-element.53.dsilu_ref, ...), custom_call_target="tpu_custom_call" | custom-call | flops 99999997952 | bytes 65536 | tf_op jit(solution)/shard_map/attention_part/pallas_call | solution.py:361
  14.2 0.1 collective-permute-start.3
  14.3 0.0 collective-permute-done
  14.3 0.0 copy-start.1
  14.3 0.0 copy-start.2
  14.3 0.2 first_sums.1
  14.5 3.0 %collective-permute-start.1 = (f32[2,64,768]{2,1,0:T(8,128)S(1)}, f32[2,64,768]{2,1,0:T(8,128)S(1)}, u32[]{:S(2)}, u32[]{:S(2)}) collective-permute-start(f32[2,64,768]{2,1,0:T(8,128)S(1)} %get-tuple-element.63), channel_id=1, source_target_pairs={{0,8},{8,0},{16,24},{24,16},{1,9},{9,1},{17,25},{25,17},{2,10},{10... | collective-permute-start | bytes 1179656 | tf_op jit(solution)/shard_map/ppermute | solution.py:379
  17.5 1.5 %collective-permute-start.2 = (f32[2,64,768]{2,1,0:T(8,128)S(1)}, f32[2,64,768]{2,1,0:T(8,128)S(1)}, u32[]{:S(2)}, u32[]{:S(2)}) collective-permute-start(f32[2,64,768]{2,1,0:T(8,128)S(1)} %get-tuple-element.64), channel_id=1, source_target_pairs={{0,16},{8,24},{16,0},{24,8},{1,17},{9,25},{17,1},{25,9},{2,18},{10... | collective-permute-start | bytes 1179656 | tf_op jit(solution)/shard_map/ppermute | solution.py:379
  19.0 0.0 copy-done.1
  19.0 0.0 copy-done.2
  19.0 3.4 %events_part.1 = f32[32,72,128]{2,1,0:T(8,128)} custom-call(s32[1]{0:T(128)S(6)} %copy.13.len_ref, bf16[512,512]{1,0:T(8,128)(2,1)S(1)} %get-tuple-element.59.ev_ref, bf16[512,512]{1,0:T(8,128)(2,1)S(1)} %get-tuple-element.60.cot_ref, bf16[512,2048]{1,0:T(8,128)(2,1)S(1)} %get-tuple-element.61.win_ref, s32[1,512]{1,0:T(1,128)S(1)} %copy-done.2, ...), custom_call_target="tpu_custom_call" | custom-call | flops 99999997952 | bytes 65536 | tf_op jit(solution)/shard_map/events_part/pallas_call | solution.py:361
  22.4 0.0 collective-permute-done.3
  22.4 4.4 %collective-permute-done.1.from_x_ref = f32[2,64,768]{2,1,0:T(8,128)S(1)} collective-permute-done((f32[2,64,768]{2,1,0:T(8,128)S(1)}, f32[2,64,768]{2,1,0:T(8,128)S(1)}, u32[]{:S(2)}, u32[]{:S(2)}) %collective-permute-start.1) | collective-permute-done | bytes 393248 | tf_op jit(solution)/shard_map/ppermute | solution.py:379
  26.8 1.5 %collective-permute-done.2.from_y_ref = f32[2,64,768]{2,1,0:T(8,128)S(1)} collective-permute-done((f32[2,64,768]{2,1,0:T(8,128)S(1)}, f32[2,64,768]{2,1,0:T(8,128)S(1)}, u32[]{:S(2)}, u32[]{:S(2)}) %collective-permute-start.2) | collective-permute-done | bytes 393248 | tf_op jit(solution)/shard_map/ppermute | solution.py:379
  28.3 0.2 second_sums.1
  28.5 0.0 copy-start.4
  28.5 0.7 copy-done.4
  29.2 0.0 copy-start.6
  29.2 0.7 copy-done.6
  29.8 0.4 collective-permute-start.4
  30.2 1.7 %collective-permute-start.5 = (f32[64,1792]{1,0:T(8,128)S(1)}, f32[64,1792]{1,0:T(8,128)S(1)}, u32[]{:S(2)}, u32[]{:S(2)}) collective-permute-start(f32[64,1792]{1,0:T(8,128)S(1)} %get-tuple-element.73), channel_id=1, source_target_pairs={{0,16},{8,24},{16,0},{24,8},{1,17},{9,25},{17,1},{25,9},{2,18},{10... | collective-permute-start | bytes 1376264 | tf_op jit(solution)/shard_map/ppermute | solution.py:379
  31.9 4.9 %all-to-all-start = ((f32[32,72,128]{2,1,0:T(8,128)}), f32[32,72,128]{2,1,0:T(8,128)S(1)}, u32[]{:S(2)}, u32[]{:S(2)}) async-start(f32[32,72,128]{2,1,0:T(8,128)} %events_part.1), calls=%async_computation | async-start | bytes 2359296 | tf_op jit(solution)/shard_map/all_to_all | solution.py:430
  36.8 6.7 %collective-permute-done.4 = f32[64,1792]{1,0:T(8,128)S(1)} collective-permute-done((f32[64,1792]{1,0:T(8,128)S(1)}, f32[64,1792]{1,0:T(8,128)S(1)}, u32[]{:S(2)}, u32[]{:S(2)}) %collective-permute-start.4) | collective-permute-done | bytes 458784 | tf_op jit(solution)/shard_map/ppermute | solution.py:379
  43.5 2.3 %collective-permute-done.5 = f32[64,1792]{1,0:T(8,128)S(1)} collective-permute-done((f32[64,1792]{1,0:T(8,128)S(1)}, f32[64,1792]{1,0:T(8,128)S(1)}, u32[]{:S(2)}, u32[]{:S(2)}) %collective-permute-start.5) | collective-permute-done | bytes 458784 | tf_op jit(solution)/shard_map/ppermute | solution.py:379
  45.8 0.9 copy-done.5
  46.7 0.9 copy-done.7
  47.6 0.1 third_sums.1
  47.7 5.6 %collective-permute-start.9 = (f32[4,16,512]{2,1,0:T(8,128)S(1)}, f32[4,16,512]{2,1,0:T(8,128)S(1)}, u32[]{:S(2)}, u32[]{:S(2)}) collective-permute-start(f32[4,16,512]{2,1,0:T(8,128)S(1)} %get-tuple-element.82), channel_id=1, source_target_pairs={{0,8},{8,0},{16,24},{24,16},{1,9},{9,1},{17,25},{25,17},{2,10},{10... | collective-permute-start | bytes 393224 | tf_op jit(solution)/shard_map/ppermute | solution.py:379
  53.3 2.5 %collective-permute-start.10 = (f32[4,16,512]{2,1,0:T(8,128)S(1)}, f32[4,16,512]{2,1,0:T(8,128)S(1)}, u32[]{:S(2)}, u32[]{:S(2)}) collective-permute-start(f32[4,16,512]{2,1,0:T(8,128)S(1)} %get-tuple-element.83), channel_id=1, source_target_pairs={{0,16},{8,24},{16,0},{24,8},{1,17},{9,25},{17,1},{25,9},{2,18},{10... | collective-permute-start | bytes 393224 | tf_op jit(solution)/shard_map/ppermute | solution.py:379
  55.8 0.0 collective-permute-start.6
  55.8 4.6 %collective-permute-start.7 = (f32[16,1536]{1,0:T(8,128)S(1)}, f32[16,1536]{1,0:T(8,128)S(1)}, u32[]{:S(2)}, u32[]{:S(2)}) collective-permute-start(f32[16,1536]{1,0:T(8,128)S(1)} %get-tuple-element.78), channel_id=1, source_target_pairs={{0,4},{1,5},{2,6},{3,7},{4,0},{5,1},{6,2},{7,3},{8,12},{9,13},{10,... | collective-permute-start | bytes 294920 | tf_op jit(solution)/shard_map/ppermute | solution.py:380
  60.4 0.0 collective-permute-start.8
  60.4 3.1 %collective-permute-done.6.refs_1_ = f32[16,1536]{1,0:T(8,128)S(1)} collective-permute-done((f32[16,1536]{1,0:T(8,128)S(1)}, f32[16,1536]{1,0:T(8,128)S(1)}, u32[]{:S(2)}, u32[]{:S(2)}) %collective-permute-start.6) | collective-permute-done | bytes 98336 | tf_op jit(solution)/shard_map/ppermute | solution.py:380
  63.6 9.1 %collective-permute-done.7.refs_2_ = f32[16,1536]{1,0:T(8,128)S(1)} collective-permute-done((f32[16,1536]{1,0:T(8,128)S(1)}, f32[16,1536]{1,0:T(8,128)S(1)}, u32[]{:S(2)}, u32[]{:S(2)}) %collective-permute-start.7) | collective-permute-done | bytes 98336 | tf_op jit(solution)/shard_map/ppermute | solution.py:380
  72.7 0.0 collective-permute-done.8.refs_3_
  72.7 0.0 collective-permute-done.9.refs_6_
  72.7 0.0 collective-permute-done.10.refs_7_
  72.7 0.1 fourth_sums.1
  72.7 2.5 %collective-permute-start.13 = (f32[16,1536]{1,0:T(8,128)S(1)}, f32[16,1536]{1,0:T(8,128)S(1)}, u32[]{:S(2)}, u32[]{:S(2)}) collective-permute-start(f32[16,1536]{1,0:T(8,128)S(1)} %get-tuple-element.84.refs_0_), channel_id=1, source_target_pairs={{0,24},{8,16},{16,8},{24,0},{1,25},{9,17},{17,9},{25,1},{2,26},{10... | collective-permute-start | bytes 294920 | tf_op jit(solution)/shard_map/ppermute | solution.py:379
  75.2 0.5 collective-permute-start.12
  75.7 0.6 collective-permute-start.11
  76.3 2.2 %collective-permute-start.14 = (f32[16,1024]{1,0:T(8,128)S(1)}, f32[16,1024]{1,0:T(8,128)S(1)}, u32[]{:S(2)}, u32[]{:S(2)}) collective-permute-start(f32[16,1024]{1,0:T(8,128)S(1)} %get-tuple-element.87), channel_id=1, source_target_pairs={{0,2},{1,3},{2,4},{3,5},{4,6},{5,7},{6,0},{7,1},{8,10},{9,11},{10,... | collective-permute-start | bytes 196616 | tf_op jit(solution)/shard_map/ppermute | solution.py:380
  78.5 1.3 %collective-permute-start.15 = (f32[16,1024]{1,0:T(8,128)S(1)}, f32[16,1024]{1,0:T(8,128)S(1)}, u32[]{:S(2)}, u32[]{:S(2)}) collective-permute-start(f32[16,1024]{1,0:T(8,128)S(1)} %get-tuple-element.88), channel_id=1, source_target_pairs={{0,4},{1,5},{2,6},{3,7},{4,0},{5,1},{6,2},{7,3},{8,12},{9,13},{10,... | collective-permute-start | bytes 196616 | tf_op jit(solution)/shard_map/ppermute | solution.py:380
  79.8 0.0 collective-permute-done.13.refs_3_
  79.8 1.7 %collective-permute-start.16 = (f32[16,1024]{1,0:T(8,128)S(1)}, f32[16,1024]{1,0:T(8,128)S(1)}, u32[]{:S(2)}, u32[]{:S(2)}) collective-permute-start(f32[16,1024]{1,0:T(8,128)S(1)} %get-tuple-element.89), channel_id=1, source_target_pairs={{0,6},{1,7},{2,0},{3,1},{4,2},{5,3},{6,4},{7,5},{8,14},{9,15},{10,... | collective-permute-start | bytes 196616 | tf_op jit(solution)/shard_map/ppermute | solution.py:380
  81.5 0.0 collective-permute-done.12.refs_2_
  81.5 0.0 collective-permute-done.11.refs_1_
  81.5 0.0 copy-start.3
  81.5 1.5 %collective-permute-done.14.refs_1_ = f32[16,1024]{1,0:T(8,128)S(1)} collective-permute-done((f32[16,1024]{1,0:T(8,128)S(1)}, f32[16,1024]{1,0:T(8,128)S(1)}, u32[]{:S(2)}, u32[]{:S(2)}) %collective-permute-start.14) | collective-permute-done | bytes 65568 | tf_op jit(solution)/shard_map/ppermute | solution.py:380
  83.0 1.5 %collective-permute-done.15.refs_2_ = f32[16,1024]{1,0:T(8,128)S(1)} collective-permute-done((f32[16,1024]{1,0:T(8,128)S(1)}, f32[16,1024]{1,0:T(8,128)S(1)}, u32[]{:S(2)}, u32[]{:S(2)}) %collective-permute-start.15) | collective-permute-done | bytes 65568 | tf_op jit(solution)/shard_map/ppermute | solution.py:380
  84.5 0.2 collective-permute-done.16.refs_3_
  84.7 2.6 %collective-permute-start.19 = (f32[16,1024]{1,0:T(8,128)S(1)}, f32[16,1024]{1,0:T(8,128)S(1)}, u32[]{:S(2)}, u32[]{:S(2)}) collective-permute-start(f32[16,1024]{1,0:T(8,128)S(1)} %last_sums.1.refs_4_), channel_id=1, source_target_pairs={{0,24},{8,16},{16,8},{24,0},{1,25},{9,17},{17,9},{25,1},{2,26},{10... | collective-permute-start | bytes 196616 | tf_op jit(solution)/shard_map/ppermute | solution.py:379
  87.3 0.6 collective-permute-start.18
  87.9 0.4 collective-permute-start.17
  88.3 0.0 all-to-all-done.recv_ref
  88.3 0.0 copy-done
  88.3 0.0 copy-done.3
  88.3 2.4 %table_part.1 = (f32[512,512]{1,0:T(8,128)}, f32[512]{0:T(512)}) custom-call(f32[32,72,128]{2,1,0:T(8,128)S(1)} %all-to-all-done.recv_ref, f32[512,512]{1,0:T(8,128)S(1)} %copy-done, f32[512]{0:T(512)S(1)} %copy-done.3), custom_call_target="tpu_custom_call" | custom-call | flops 1000000000 | bytes 65536 | tf_op jit(solution)/shard_map/table_part/pallas_call | solution.py:361
  90.7 0.0 collective-permute-done.19.refs_7_
  90.7 0.9 collective-permute-done.18.refs_6_
  91.6 0.6 collective-permute-done.17.refs_5_
  92.1 0.9 gather.1
  (4 shorter events, 0.0 us)
Async XLA Ops:
  9.5 4.8 %collective-permute-start = (f32[256,1536]{1,0:T(8,128)S(1)}, f32[256,1536]{1,0:T(8,128)S(1)}, u32[]{:S(2)}, u32[]{:S(2)}) collective-permute-start(f32[256,1536]{1,0:T(8,128)S(1)} %get-tuple-element.51), channel_id=1, source_target_pairs={{0,1},{1,0},{2,3},{3,2},{4,5},{5,4},{6,7},{7,6},{8,9},{9,8},{10,11... | collective-permute-start | bytes 4718600 | tf_op jit(solution)/shard_map/ppermute | solution.py:410
  14.2 8.2 %collective-permute-start.3 = (f32[256,1024]{1,0:T(8,128)S(1)}, f32[256,1024]{1,0:T(8,128)S(1)}, u32[]{:S(2)}, u32[]{:S(2)}) collective-permute-start(f32[256,1024]{1,0:T(8,128)S(1)} %get-tuple-element.69), channel_id=1, source_target_pairs={{0,1},{1,0},{2,3},{3,2},{4,5},{5,4},{6,7},{7,6},{8,9},{9,8},{10,11... | collective-permute-start | bytes 3145736 | tf_op jit(solution)/shard_map/ppermute | solution.py:414
  14.3 4.7 %copy-start.1 = (s32[1,32,16]{1,2,0:T(8,128)S(1)}, s32[1,32,16]{1,2,0:T(8,128)}, u32[]{:S(2)}) copy-start(s32[1,32,16]{1,2,0:T(8,128)} %param.14) | copy-start | bytes 6148
  14.3 4.7 %copy-start.2 = (s32[1,512]{1,0:T(1,128)S(1)}, s32[1,512]{1,0:T(1,128)}, u32[]{:S(2)}) copy-start(s32[1,512]{1,0:T(1,128)} %slot_ref.1) | copy-start | bytes 6148
  14.5 12.3 %collective-permute-start.1 = (f32[2,64,768]{2,1,0:T(8,128)S(1)}, f32[2,64,768]{2,1,0:T(8,128)S(1)}, u32[]{:S(2)}, u32[]{:S(2)}) collective-permute-start(f32[2,64,768]{2,1,0:T(8,128)S(1)} %get-tuple-element.63), channel_id=1, source_target_pairs={{0,8},{8,0},{16,24},{24,16},{1,9},{9,1},{17,25},{25,17},{2,10},{10... | collective-permute-start | bytes 1179656 | tf_op jit(solution)/shard_map/ppermute | solution.py:379
  17.5 10.8 %collective-permute-start.2 = (f32[2,64,768]{2,1,0:T(8,128)S(1)}, f32[2,64,768]{2,1,0:T(8,128)S(1)}, u32[]{:S(2)}, u32[]{:S(2)}) collective-permute-start(f32[2,64,768]{2,1,0:T(8,128)S(1)} %get-tuple-element.64), channel_id=1, source_target_pairs={{0,16},{8,24},{16,0},{24,8},{1,17},{9,25},{17,1},{25,9},{2,18},{10... | collective-permute-start | bytes 1179656 | tf_op jit(solution)/shard_map/ppermute | solution.py:379
  28.5 0.7 copy-start.4
  29.2 0.7 copy-start.6
  29.8 13.6 %collective-permute-start.4 = (f32[64,1792]{1,0:T(8,128)S(1)}, f32[64,1792]{1,0:T(8,128)S(1)}, u32[]{:S(2)}, u32[]{:S(2)}) collective-permute-start(f32[64,1792]{1,0:T(8,128)S(1)} %get-tuple-element.72), channel_id=1, source_target_pairs={{0,8},{8,0},{16,24},{24,16},{1,9},{9,1},{17,25},{25,17},{2,10},{10... | collective-permute-start | bytes 1376264 | tf_op jit(solution)/shard_map/ppermute | solution.py:379
  30.2 15.6 %collective-permute-start.5 = (f32[64,1792]{1,0:T(8,128)S(1)}, f32[64,1792]{1,0:T(8,128)S(1)}, u32[]{:S(2)}, u32[]{:S(2)}) collective-permute-start(f32[64,1792]{1,0:T(8,128)S(1)} %get-tuple-element.73), channel_id=1, source_target_pairs={{0,16},{8,24},{16,0},{24,8},{1,17},{9,25},{17,1},{25,9},{2,18},{10... | collective-permute-start | bytes 1376264 | tf_op jit(solution)/shard_map/ppermute | solution.py:379
  31.9 56.4 %all-to-all-start = ((f32[32,72,128]{2,1,0:T(8,128)}), f32[32,72,128]{2,1,0:T(8,128)S(1)}, u32[]{:S(2)}, u32[]{:S(2)}) async-start(f32[32,72,128]{2,1,0:T(8,128)} %events_part.1), calls=%async_computation | async-start | bytes 2359296 | tf_op jit(solution)/shard_map/all_to_all | solution.py:430
  45.8 0.9 copy-start.5
  46.7 0.9 copy-start.7
  47.7 24.9 %collective-permute-start.9 = (f32[4,16,512]{2,1,0:T(8,128)S(1)}, f32[4,16,512]{2,1,0:T(8,128)S(1)}, u32[]{:S(2)}, u32[]{:S(2)}) collective-permute-start(f32[4,16,512]{2,1,0:T(8,128)S(1)} %get-tuple-element.82), channel_id=1, source_target_pairs={{0,8},{8,0},{16,24},{24,16},{1,9},{9,1},{17,25},{25,17},{2,10},{10... | collective-permute-start | bytes 393224 | tf_op jit(solution)/shard_map/ppermute | solution.py:379
  53.3 19.4 %collective-permute-start.10 = (f32[4,16,512]{2,1,0:T(8,128)S(1)}, f32[4,16,512]{2,1,0:T(8,128)S(1)}, u32[]{:S(2)}, u32[]{:S(2)}) collective-permute-start(f32[4,16,512]{2,1,0:T(8,128)S(1)} %get-tuple-element.83), channel_id=1, source_target_pairs={{0,16},{8,24},{16,0},{24,8},{1,17},{9,25},{17,1},{25,9},{2,18},{10... | collective-permute-start | bytes 393224 | tf_op jit(solution)/shard_map/ppermute | solution.py:379
  55.8 7.8 %collective-permute-start.6 = (f32[16,1536]{1,0:T(8,128)S(1)}, f32[16,1536]{1,0:T(8,128)S(1)}, u32[]{:S(2)}, u32[]{:S(2)}) collective-permute-start(f32[16,1536]{1,0:T(8,128)S(1)} %get-tuple-element.77), channel_id=1, source_target_pairs={{0,2},{1,3},{2,4},{3,5},{4,6},{5,7},{6,0},{7,1},{8,10},{9,11},{10,... | collective-permute-start | bytes 294920 | tf_op jit(solution)/shard_map/ppermute | solution.py:380
  55.8 16.9 %collective-permute-start.7 = (f32[16,1536]{1,0:T(8,128)S(1)}, f32[16,1536]{1,0:T(8,128)S(1)}, u32[]{:S(2)}, u32[]{:S(2)}) collective-permute-start(f32[16,1536]{1,0:T(8,128)S(1)} %get-tuple-element.78), channel_id=1, source_target_pairs={{0,4},{1,5},{2,6},{3,7},{4,0},{5,1},{6,2},{7,3},{8,12},{9,13},{10,... | collective-permute-start | bytes 294920 | tf_op jit(solution)/shard_map/ppermute | solution.py:380
  60.4 12.2 %collective-permute-start.8 = (f32[16,1536]{1,0:T(8,128)S(1)}, f32[16,1536]{1,0:T(8,128)S(1)}, u32[]{:S(2)}, u32[]{:S(2)}) collective-permute-start(f32[16,1536]{1,0:T(8,128)S(1)} %get-tuple-element.79), channel_id=1, source_target_pairs={{0,6},{1,7},{2,0},{3,1},{4,2},{5,3},{6,4},{7,5},{8,14},{9,15},{10,... | collective-permute-start | bytes 294920 | tf_op jit(solution)/shard_map/ppermute | solution.py:380
  72.7 7.1 %collective-permute-start.13 = (f32[16,1536]{1,0:T(8,128)S(1)}, f32[16,1536]{1,0:T(8,128)S(1)}, u32[]{:S(2)}, u32[]{:S(2)}) collective-permute-start(f32[16,1536]{1,0:T(8,128)S(1)} %get-tuple-element.84.refs_0_), channel_id=1, source_target_pairs={{0,24},{8,16},{16,8},{24,0},{1,25},{9,17},{17,9},{25,1},{2,26},{10... | collective-permute-start | bytes 294920 | tf_op jit(solution)/shard_map/ppermute | solution.py:379
  75.2 6.3 %collective-permute-start.12 = (f32[16,1536]{1,0:T(8,128)S(1)}, f32[16,1536]{1,0:T(8,128)S(1)}, u32[]{:S(2)}, u32[]{:S(2)}) collective-permute-start(f32[16,1536]{1,0:T(8,128)S(1)} %get-tuple-element.84.refs_0_), channel_id=1, source_target_pairs={{0,16},{8,24},{16,0},{24,8},{1,17},{9,25},{17,1},{25,9},{2,18},{10... | collective-permute-start | bytes 294920 | tf_op jit(solution)/shard_map/ppermute | solution.py:379
  75.7 5.8 %collective-permute-start.11 = (f32[16,1536]{1,0:T(8,128)S(1)}, f32[16,1536]{1,0:T(8,128)S(1)}, u32[]{:S(2)}, u32[]{:S(2)}) collective-permute-start(f32[16,1536]{1,0:T(8,128)S(1)} %get-tuple-element.84.refs_0_), channel_id=1, source_target_pairs={{0,8},{8,0},{16,24},{24,16},{1,9},{9,1},{17,25},{25,17},{2,10},{10... | collective-permute-start | bytes 294920 | tf_op jit(solution)/shard_map/ppermute | solution.py:379
  76.3 6.7 %collective-permute-start.14 = (f32[16,1024]{1,0:T(8,128)S(1)}, f32[16,1024]{1,0:T(8,128)S(1)}, u32[]{:S(2)}, u32[]{:S(2)}) collective-permute-start(f32[16,1024]{1,0:T(8,128)S(1)} %get-tuple-element.87), channel_id=1, source_target_pairs={{0,2},{1,3},{2,4},{3,5},{4,6},{5,7},{6,0},{7,1},{8,10},{9,11},{10,... | collective-permute-start | bytes 196616 | tf_op jit(solution)/shard_map/ppermute | solution.py:380
  78.5 6.0 %collective-permute-start.15 = (f32[16,1024]{1,0:T(8,128)S(1)}, f32[16,1024]{1,0:T(8,128)S(1)}, u32[]{:S(2)}, u32[]{:S(2)}) collective-permute-start(f32[16,1024]{1,0:T(8,128)S(1)} %get-tuple-element.88), channel_id=1, source_target_pairs={{0,4},{1,5},{2,6},{3,7},{4,0},{5,1},{6,2},{7,3},{8,12},{9,13},{10,... | collective-permute-start | bytes 196616 | tf_op jit(solution)/shard_map/ppermute | solution.py:380
  79.8 4.9 %collective-permute-start.16 = (f32[16,1024]{1,0:T(8,128)S(1)}, f32[16,1024]{1,0:T(8,128)S(1)}, u32[]{:S(2)}, u32[]{:S(2)}) collective-permute-start(f32[16,1024]{1,0:T(8,128)S(1)} %get-tuple-element.89), channel_id=1, source_target_pairs={{0,6},{1,7},{2,0},{3,1},{4,2},{5,3},{6,4},{7,5},{8,14},{9,15},{10,... | collective-permute-start | bytes 196616 | tf_op jit(solution)/shard_map/ppermute | solution.py:380
  81.5 6.8 %copy-start = (f32[512,512]{1,0:T(8,128)S(1)}, f32[512,512]{1,0:T(8,128)}, u32[]{:S(2)}) copy-start(f32[512,512]{1,0:T(8,128)} %table_ref.1) | copy-start | bytes 3145732
  81.5 6.8 %copy-start.3 = (f32[512]{0:T(512)S(1)}, f32[512]{0:T(512)}, u32[]{:S(2)}) copy-start(f32[512]{0:T(512)} %accum_ref.1) | copy-start | bytes 6148
  84.7 5.9 %collective-permute-start.19 = (f32[16,1024]{1,0:T(8,128)S(1)}, f32[16,1024]{1,0:T(8,128)S(1)}, u32[]{:S(2)}, u32[]{:S(2)}) collective-permute-start(f32[16,1024]{1,0:T(8,128)S(1)} %last_sums.1.refs_4_), channel_id=1, source_target_pairs={{0,24},{8,16},{16,8},{24,0},{1,25},{9,17},{17,9},{25,1},{2,26},{10... | collective-permute-start | bytes 196616 | tf_op jit(solution)/shard_map/ppermute | solution.py:379
  87.3 4.3 %collective-permute-start.18 = (f32[16,1024]{1,0:T(8,128)S(1)}, f32[16,1024]{1,0:T(8,128)S(1)}, u32[]{:S(2)}, u32[]{:S(2)}) collective-permute-start(f32[16,1024]{1,0:T(8,128)S(1)} %last_sums.1.refs_4_), channel_id=1, source_target_pairs={{0,16},{8,24},{16,0},{24,8},{1,17},{9,25},{17,1},{25,9},{2,18},{10... | collective-permute-start | bytes 196616 | tf_op jit(solution)/shard_map/ppermute | solution.py:379
  87.9 4.3 %collective-permute-start.17 = (f32[16,1024]{1,0:T(8,128)S(1)}, f32[16,1024]{1,0:T(8,128)S(1)}, u32[]{:S(2)}, u32[]{:S(2)}) collective-permute-start(f32[16,1024]{1,0:T(8,128)S(1)} %last_sums.1.refs_4_), channel_id=1, source_target_pairs={{0,8},{8,0},{16,24},{24,16},{1,9},{9,1},{17,25},{25,17},{2,10},{10... | collective-permute-start | bytes 196616 | tf_op jit(solution)/shard_map/ppermute | solution.py:379

commit v7 on v5

--- a/solution.py
+++ b/solution.py
@@ -289,23 +289,24 @@
         keep2_b_ref[s] = keep2_b[s]
 
 
-def chip_parts(out_refs, keep_a, recv_a, keep_b, recv_b):
-    chips = len(out_refs)
-    chip = lax.axis_index("rows") // 2
-    half = out_refs[0].shape[-1] // 2
-    for k, out_ref in enumerate(out_refs):
-        at = lax.rem(chip + k, chips)
-        out_ref[:, :half] = keep_a(at) + recv_a(at)
-        out_ref[:, half:] = keep_b(at) + recv_b(at)
-
-
-def third_kernel(chips, next_a_ref, next_b_ref, from_x_ref, from_y_ref, keep2_a_ref, keep2_b_ref, *out_refs):
+def chip_bit(bit):
+    return (lax.axis_index("rows") // 2) // (1 << bit) % 2
+
+
+def halve(bit, send_ref, keep_ref, block):
+    mine = chip_bit(bit)
+    for i in range(send_ref.shape[0]):
+        send_ref[i] = block(2 * i + 1 - mine)
+        keep_ref[i] = block(2 * i + mine)
+
+
+def third_kernel(next_a_ref, next_b_ref, from_x_ref, from_y_ref, keep2_a_ref, keep2_b_ref,
+                 send_ref, keep_ref, to_x_ref, to_y_ref, next2_a_ref, next2_b_ref):
     x, y = place_on_dp()
     half, half2 = next_a_ref.shape[-1], keep2_a_ref.shape[-1]
     lo = slice(0, half)
-    chip_parts(out_refs[:chips], lambda at: next_a_ref[at], lambda at: from_y_ref[at, :, lo],
-               lambda at: next_b_ref[at], lambda at: from_x_ref[at, :, lo])
-    to_x_ref, to_y_ref, next2_a_ref, next2_b_ref = out_refs[chips:]
+    halve(0, send_ref, keep_ref, lambda at: jnp.concatenate(
+        [next_a_ref[at] + from_y_ref[at, :, lo], next_b_ref[at] + from_x_ref[at, :, lo]], axis=1))
     blocks = [slice(half + s * half2, half + (s + 1) * half2) for s in range(2)]
     sum_a = [keep2_a_ref[s] + from_x_ref[:, :, blocks[s]] for s in range(2)]
     sum_b = [keep2_b_ref[s] + from_y_ref[:, :, blocks[s]] for s in range(2)]
@@ -315,23 +316,32 @@
     next2_b_ref[...] = jnp.where(x == 0, sum_b[0], sum_b[1])
 
 
-def sum_of(refs):
-    total = refs[0][...]
-    for ref in refs[1:]:
-        total = total + ref[...]
-    return total
-
-
-def fourth_kernel(chips, tokens, *refs):
-    blocks, (next2_a_ref, next2_b_ref, from_x_ref, from_y_ref) = refs[:chips], refs[chips:chips + 4]
-    total_ref, *out_refs = refs[chips + 4:]
-    total_ref[...] = sum_of(blocks) * (1.0 / tokens)
-    chip_parts(out_refs, lambda at: next2_a_ref[at], lambda at: from_y_ref[at],
-               lambda at: next2_b_ref[at], lambda at: from_x_ref[at])
-
-
-def total_kernel(tokens, *refs):
-    refs[-1][...] = sum_of(refs[:-1]) * (1.0 / tokens)
+def chips_kernel(tokens, bit, bit2, first, *refs):
+    refs = list(refs)
+    take = lambda n: [refs.pop(0) for _ in range(n)]
+    inputs = take(2) if first else []
+    inputs2 = take(4 if bit2 == 0 else 2)
+    if first:
+        keep_in, recv_in = inputs
+        if bit is None:
+            (total_ref,) = take(1)
+            total_ref[...] = (keep_in[0] + recv_in[0]) * (1.0 / tokens)
+        else:
+            send_ref, keep_ref = take(2)
+            halve(bit, send_ref, keep_ref, lambda at: keep_in[at] + recv_in[at])
+    if bit2 is None:
+        keep_in, recv_in = inputs2
+        (total_ref,) = take(1)
+        total_ref[...] = (keep_in[0] + recv_in[0]) * (1.0 / tokens)
+    else:
+        send_ref, keep_ref = take(2)
+        if bit2 == 0:
+            next_a, next_b, from_x, from_y = inputs2
+            halve(0, send_ref, keep_ref, lambda at: jnp.concatenate(
+                [next_a[at] + from_y[at], next_b[at] + from_x[at]], axis=1))
+        else:
+            keep_in, recv_in = inputs2
+            halve(bit2, send_ref, keep_ref, lambda at: keep_in[at] + recv_in[at])
 
 
 def gather_kernel(*refs):
@@ -355,9 +365,10 @@
     return jax.ShapeDtypeStruct(dims, dtype)
 
 
-def call(kernel, name, out_shape, args, scalars=0, scratch=(), far=0, long=False, grant=4):
+def call(kernel, name, out_shape, args, scalars=0, scratch=(), far=0, long=False, grant=4, apart=(), either=()):
     place = [None] * scalars + [pltpu.HBM] * far + [pltpu.VMEM] * (len(args) - scalars - far)
-    args = [a if p is None else pltpu.with_memory_space_constraint(a, p) for a, p in zip(args, place)]
+    held = [None if i in either else pltpu.HBM if i in apart else p for i, p in enumerate(place)]
+    args = [a if p is None else pltpu.with_memory_space_constraint(a, p) for a, p in zip(args, held)]
     return pl.pallas_call(
         kernel,
         name=name,
@@ -377,18 +388,17 @@
     piece = width // (rows_size * dp_size)
     cores = [(i, i ^ 1) for i in range(rows_size)]
     over_dp = lambda v, bit: lax.ppermute(v, "dp", [(i, i ^ bit) for i in range(dp_size)])
-    over_chips = lambda v, k: lax.ppermute(v, "rows", [(i, (i + 2 * k) % rows_size) for i in range(rows_size)])
+    over_chips = lambda v, bit: lax.ppermute(v, "rows", [(i, i ^ (2 << bit)) for i in range(rows_size)])
     after = lambda value, *others: lax.optimization_barrier((value, *others))[0]
     strip = chips * piece
 
-    def to_chips(blocks):
-        return [blocks[0]] + [over_chips(blocks[k], k) for k in range(1, chips)]
-
     def gathered(total):
         return [total] + [over_dp(total, k) for k in range(1, dp_size)]
 
     by_dp = lambda v: v.reshape(2, 2, strip, v.shape[-1])
     by_chip = lambda v: v.reshape(*v.shape[:-2], chips, piece, v.shape[-1])
+    bits = chips.bit_length() - 1
+    far_off = lambda *dims, dtype=f32: pltpu.HBM(dims, dtype)
     local = lambda *dims, dtype=f32: pltpu.VMEM(dims, dtype)
     sides = lambda cols: [local(width // 2, cols)] * 2
     keep1, send1, hid, dsilu, gatt, gpre_uv, normed_t, events, cotangent, w_in = call(
@@ -409,13 +419,13 @@
          (w_out.shape, bf16)], far=4, long=True, grant=16)
     recv1 = lax.ppermute(send1, "rows", cores)
     keep2, send2, gpre_qk = call(
-        attention_kernel, "attention_part", sides(2 * width) + [local(tokens, 2 * width, dtype=bf16)],
+        attention_kernel, "attention_part", [far_off(width // 2, 2 * width)] * 2 + [local(tokens, 2 * width, dtype=bf16)],
         (lengths, hid, dsilu, gatt, normed_t), 1, long=True, grant=10)
     recv2 = lax.ppermute(send2, "rows", cores)
     pay_rows = capacity * (width // LANES) + ID_ROWS
     half1, half2 = 3 * width // 2, width
     to_x, to_y, keep_a, keep_b = call(
-        first_kernel, "first_sums", [local(2, strip, half1)] * 4, (by_dp(keep1), by_dp(after(recv1, keep2))))
+        first_kernel, "first_sums", [far_off(2, strip, half1)] * 4, (by_dp(keep1), by_dp(after(recv1, keep2))))
     gpre_uv = after(gpre_uv, to_x, to_y)
     (send,) = call(
         events_kernel, "events_part", [local(owners, pay_rows, LANES)],
@@ -426,22 +436,33 @@
     to_x, to_y, next_a, next_b, keep2_a, keep2_b = call(
         second_kernel, "second_sums",
         [local(strip, half1 + 2 * half2)] * 2 + [local(strip, half1)] * 2 + [local(2, strip, half2)] * 2,
-        (after(keep_a, send), from_x, keep_b, from_y, by_dp(keep2), by_dp(recv2)), long=True)
+        (after(keep_a, send), from_x, keep_b, from_y, by_dp(keep2), by_dp(recv2)), long=True, grant=10, apart=(0, 2, 4), either=(1, 3, 5))
     from_x, from_y = over_dp(to_x, 1), over_dp(to_y, 2)
-    *blocks, to_x, to_y, next2_a, next2_b = call(
-        functools.partial(third_kernel, chips), "third_sums",
-        [local(piece, 2 * half1)] * chips + [local(chips, piece, half2)] * 4,
+    send1, keep1, to_x, to_y, next_a, next_b = call(
+        third_kernel, "third_sums", [local(chips // 2, piece, 2 * half1)] * 2 + [local(chips, piece, half2)] * 4,
         [by_chip(v) for v in (next_a, next_b, from_x, from_y, keep2_a, keep2_b)])
-    from_x, from_y = over_dp(to_x, 1), over_dp(to_y, 2)
-    total, *blocks = call(
-        functools.partial(fourth_kernel, chips, tokens), "fourth_sums",
-        [local(piece, 2 * half1)] + [local(piece, 2 * half2)] * chips,
-        to_chips(blocks) + [next2_a, next2_b, from_x, from_y])
-    pieces = gathered(total)
-    blocks = to_chips(blocks)
-    blocks[0] = after(blocks[0], *pieces)
-    (total,) = call(functools.partial(total_kernel, tokens), "last_sums", [local(piece, 2 * half2)], blocks)
-    pieces += gathered(total)
+    first = [keep1, over_chips(send1, 0)]
+    second = [next_a, next_b, over_dp(to_x, 1), over_dp(to_y, 2)]
+    pieces, at = [], 1
+    while second is not None:
+        bit, bit2 = at if at < bits else None, at - 1 if at - 1 < bits else None
+        outs = []
+        if first is not None:
+            outs += [local(piece, 2 * half1)] if bit is None else [local(chips >> (bit + 1), piece, 2 * half1)] * 2
+        outs += [local(piece, 2 * half2)] if bit2 is None else [local(chips >> (bit2 + 1), piece, 2 * half2)] * 2
+        outs = list(call(
+            functools.partial(chips_kernel, tokens, bit, bit2, first is not None), "chip_sums", outs, (first or []) + second))
+        if first is not None:
+            if bit is None:
+                first, pieces = None, gathered(outs.pop(0))
+            else:
+                first = [outs[1], over_chips(outs[0], bit)]
+                outs = outs[2:]
+        if bit2 is None:
+            second, pieces = None, pieces + gathered(outs[0])
+        else:
+            second = [outs[1], over_chips(outs[0], bit2)]
+        at += 1
     slots = owners * capacity
     table_new, accum_new = call(
         table_kernel, "table_part", [shape(*item_table.shape), shape(*accumulator.shape)],

time: 86.1 us -> 85 us (0.987)
  waiting for transfers between devices: 25.7 us -> 32 us
  local copies, waits for them, and re-layouts: 4.76 us -> 0.01 us
  starting transfers between devices: 32.3 us -> 28.1 us
  Pallas kernels: 21.6 us -> 23.3 us
    ppermute x12, waiting for transfers between devices: 17.9 us -> 25.5 us  [body(): lax.ppermute(v, 'dp', [(i, i ^ bit) for i in range(dp_size)])]
    unnamed x20 -> x8, local copies, waits for them, and re-layouts: 4.76 us -> 0.01 us
    ppermute x6 -> x4, starting transfers between devices: 11.7 us -> 8.47 us  [body(): lax.ppermute(v, 'rows', [(i, i ^ 2 << bit) for i in range(rows_size)])]
    pallas_call x10 -> x11, Pallas kernels: 21.6 us -> 23.3 us  [call(): pl.pallas_call(kernel, name=name, in_specs=[pl.BlockSpec(memory_space=p o...]
    ppermute x6 -> x4, waiting for transfers between devices: 7.8 us -> 6.45 us  [body(): lax.ppermute(v, 'rows', [(i, i ^ 2 << bit) for i in range(rows_size)])]
    ppermute x12, starting transfers between devices: 16 us -> 15 us  [body(): lax.ppermute(v, 'dp', [(i, i ^ bit) for i in range(dp_size)])]
  transfers between devices with their start and end apart: 21 -> 19, of which waited for: 10 -> 10; matrix products, arithmetic and copies ran while one was open for 0% -> 0% of each run, Pallas kernels for 15% -> 17%
where the time goes in v7:
time: 85 us; the launch traced here: 84.7 us
  waiting for transfers between devices  32 us (38%)
  starting transfers between devices  28.1 us (33%)
  Pallas kernels  23.3 us (27%)
  between operations  1.36 us (2%)
    ppermute x12, waiting for transfers between devices, body(): lax.ppermute(v, 'dp', [(i, i ^ bit) for i in range(dp_size)])  25.5 us
    pallas_call x11, Pallas kernels, call(): pl.pallas_call(kernel, name=name, in_specs=[pl.BlockSpec(memory_space=p o...  23.3 us
    ppermute x12, starting transfers between devices, body(): lax.ppermute(v, 'dp', [(i, i ^ bit) for i in range(dp_size)])  15 us
    ppermute x4, starting transfers between devices, body(): lax.ppermute(v, 'rows', [(i, i ^ 2 << bit) for i in range(rows_size)])  8.47 us
    ppermute x4, waiting for transfers between devices, body(): lax.ppermute(v, 'rows', [(i, i ^ 2 << bit) for i in range(rows_size)])  6.45 us
    all_to_all x1, starting transfers between devices, body(): lax.all_to_all(send, ('dp', 'rows'), split_axis=0, concat_axis=0, tiled=T...  3.97 us
  transfers between devices with their start and end apart: 19, of which 10 were waited for; matrix products, arithmetic and copies ran while one was open for 0% of the time, Pallas kernels for 17%

profile of v7, /device:TPU:0, one launch (start us, length us, event | category | flops | bytes accessed | tf_op | source)
XLA Modules:
  0.0 84.7 jit_solution(12117043104767485253)
XLA Ops:
  1.3 8.3 %forward_part.1 = (f32[256,1536]{1,0:T(8,128)S(1)}, f32[256,1536]{1,0:T(8,128)S(1)}, bf16[512,1536]{1,0:T(8,128)(2,1)S(1)}, bf16[512,1024]{1,0:T(8,128)(2,1)S(1)...) custom-call(s32[1]{0:T(128)S(6)} %copy.13.len_ref, ...), custom_call_target="tpu_custom_call" | custom-call | flops 99999997952 | bytes 65536 | tf_op jit(solution)/shard_map/forward_part/pallas_call | solution.py:372
  9.5 0.5 collective-permute-start
  10.1 5.2 %attention_part.1 = (f32[256,1024]{1,0:T(8,128)}, f32[256,1024]{1,0:T(8,128)}, bf16[512,1024]{1,0:T(8,128)(2,1)S(1)}) custom-call(s32[1]{0:T(128)S(6)} %copy.13.len_ref, bf16[512,1536]{1,0:T(8,128)(2,1)S(1)} %get-tuple-element.50.hid_ref, bf16[512,1024]{1,0:T(8,128)(2,1)S(1)} %get-tuple-element.51.dsilu_ref, ...), custom_call_target="tpu_custom_call" | custom-call | flops 99999997952 | bytes 65536 | tf_op jit(solution)/shard_map/attention_part/pallas_call | solution.py:372
  15.3 0.1 collective-permute-start.3
  15.4 0.0 collective-permute-done
  15.4 0.0 copy-start.1
  15.4 0.0 copy-start.2
  15.4 1.3 %first_sums.1 = (f32[2,64,768]{2,1,0:T(8,128)}, f32[2,64,768]{2,1,0:T(8,128)}, f32[2,64,768]{2,1,0:T(8,128)}, f32[2,64,768]{2,1,0:T(8,128)}) custom-call(f32[2,2,64,1536]{3,2,1,0:T(8,128)S(1)} %bitcast.20, f32[2,2,64,1536]{3,2,1,0:T(8,128)S(1)} %bitcast.15), custom_call_target="tpu_custom_call" | custom-call | flops 1000000000 | bytes 65536 | tf_op jit(solution)/shard_map/first_sums/pallas_call | solution.py:372
  16.7 2.9 %collective-permute-start.1 = (f32[2,64,768]{2,1,0:T(8,128)}, f32[2,64,768]{2,1,0:T(8,128)S(1)}, u32[]{:S(2)}, u32[]{:S(2)}) collective-permute-start(f32[2,64,768]{2,1,0:T(8,128)} %get-tuple-element.61), channel_id=1, source_target_pairs={{0,8},{8,0},{16,24},{24,16},{1,9},{9,1},{17,25},{25,17},{2,10},{10... | collective-permute-start | bytes 1179656 | tf_op jit(solution)/shard_map/ppermute | solution.py:390
  19.6 1.5 %collective-permute-start.2 = (f32[2,64,768]{2,1,0:T(8,128)}, f32[2,64,768]{2,1,0:T(8,128)S(1)}, u32[]{:S(2)}, u32[]{:S(2)}) collective-permute-start(f32[2,64,768]{2,1,0:T(8,128)} %get-tuple-element.62), channel_id=1, source_target_pairs={{0,16},{8,24},{16,0},{24,8},{1,17},{9,25},{17,1},{25,9},{2,18},{10... | collective-permute-start | bytes 1179656 | tf_op jit(solution)/shard_map/ppermute | solution.py:390
  21.1 0.0 copy-done.1
  21.1 0.0 copy-done.2
  21.1 3.4 %events_part.1 = f32[32,72,128]{2,1,0:T(8,128)} custom-call(s32[1]{0:T(128)S(6)} %copy.13.len_ref, bf16[512,512]{1,0:T(8,128)(2,1)S(1)} %get-tuple-element.57.ev_ref, bf16[512,512]{1,0:T(8,128)(2,1)S(1)} %get-tuple-element.58.cot_ref, bf16[512,2048]{1,0:T(8,128)(2,1)S(1)} %get-tuple-element.59.win_ref, s32[1,512]{1,0:T(1,128)S(1)} %copy-done.2, ...), custom_call_target="tpu_custom_call" | custom-call | flops 99999997952 | bytes 65536 | tf_op jit(solution)/shard_map/events_part/pallas_call | solution.py:372
  24.5 4.0 %all-to-all-start = ((f32[32,72,128]{2,1,0:T(8,128)}), f32[32,72,128]{2,1,0:T(8,128)S(1)}, u32[]{:S(2)}, u32[]{:S(2)}) async-start(f32[32,72,128]{2,1,0:T(8,128)} %events_part.1), calls=%async_computation | async-start | bytes 2359296 | tf_op jit(solution)/shard_map/all_to_all | solution.py:434
  28.5 0.0 collective-permute-done.3
  28.5 0.6 collective-permute-done.1.from_x_ref
  29.1 1.5 %collective-permute-done.2.from_y_ref = f32[2,64,768]{2,1,0:T(8,128)S(1)} collective-permute-done((f32[2,64,768]{2,1,0:T(8,128)}, f32[2,64,768]{2,1,0:T(8,128)S(1)}, u32[]{:S(2)}, u32[]{:S(2)}) %collective-permute-start.2) | collective-permute-done | bytes 393248 | tf_op jit(solution)/shard_map/ppermute | solution.py:390
  30.6 1.7 %second_sums.1 = (f32[64,1792]{1,0:T(8,128)S(1)}, f32[64,1792]{1,0:T(8,128)S(1)}, f32[64,768]{1,0:T(8,128)S(1)}, f32[64,768]{1,0:T(8,128)S(1)}, f32[2,64,512]{2,1,0:T(8,128)S(1)}, /*index=5*/f32[2,64,512]{2,1,0:T(8,128)S(1)}) custom-call(f32[2,64,768]{2,1,0:T(8,128)} %get-tuple-element.65.keep_a_ref, f32[2,64,768]{2,1,0:T(8,128)S(1)} %collective-permute-done.1.from_x_ref, ...), custom_call_target="tpu_custom_call" | custom-call | flops 99999997952 | bytes 65536 | tf_op jit(solution)/shard_map/second_sums/pallas_call | solution.py:372
  32.2 0.4 collective-permute-start.4
  32.6 1.7 %collective-permute-start.5 = (f32[64,1792]{1,0:T(8,128)S(1)}, f32[64,1792]{1,0:T(8,128)S(1)}, u32[]{:S(2)}, u32[]{:S(2)}) collective-permute-start(f32[64,1792]{1,0:T(8,128)S(1)} %get-tuple-element.71), channel_id=1, source_target_pairs={{0,16},{8,24},{16,0},{24,8},{1,17},{9,25},{17,1},{25,9},{2,18},{10... | collective-permute-start | bytes 1376264 | tf_op jit(solution)/shard_map/ppermute | solution.py:390
  34.4 17.3 %collective-permute-done.4 = f32[64,1792]{1,0:T(8,128)S(1)} collective-permute-done((f32[64,1792]{1,0:T(8,128)S(1)}, f32[64,1792]{1,0:T(8,128)S(1)}, u32[]{:S(2)}, u32[]{:S(2)}) %collective-permute-start.4) | collective-permute-done | bytes 458784 | tf_op jit(solution)/shard_map/ppermute | solution.py:390
  51.7 0.6 collective-permute-done.5
  52.3 0.1 third_sums.1
  52.4 2.5 %collective-permute-start.6 = (f32[2,16,1536]{2,1,0:T(8,128)S(1)}, f32[2,16,1536]{2,1,0:T(8,128)S(1)}, u32[]{:S(2)}, u32[]{:S(2)}) collective-permute-start(f32[2,16,1536]{2,1,0:T(8,128)S(1)} %get-tuple-element.75), channel_id=1, source_target_pairs={{0,2},{1,3},{2,0},{3,1},{4,6},{5,7},{6,4},{7,5},{8,10},{9,11},{10,... | collective-permute-start | bytes 589832 | tf_op jit(solution)/shard_map/ppermute | solution.py:391
  54.9 0.5 collective-permute-start.7
  55.4 1.0 %collective-permute-start.8 = (f32[4,16,512]{2,1,0:T(8,128)S(1)}, f32[4,16,512]{2,1,0:T(8,128)S(1)}, u32[]{:S(2)}, u32[]{:S(2)}) collective-permute-start(f32[4,16,512]{2,1,0:T(8,128)S(1)} %get-tuple-element.79), channel_id=1, source_target_pairs={{0,16},{8,24},{16,0},{24,8},{1,17},{9,25},{17,1},{25,9},{2,18},{10... | collective-permute-start | bytes 393224 | tf_op jit(solution)/shard_map/ppermute | solution.py:390
  56.3 3.9 %collective-permute-done.7.refs_4_ = f32[4,16,512]{2,1,0:T(8,128)S(1)} collective-permute-done((f32[4,16,512]{2,1,0:T(8,128)S(1)}, f32[4,16,512]{2,1,0:T(8,128)S(1)}, u32[]{:S(2)}, u32[]{:S(2)}) %collective-permute-start.7) | collective-permute-done | bytes 131104 | tf_op jit(solution)/shard_map/ppermute | solution.py:390
  60.3 0.5 collective-permute-done.8.refs_5_
  60.7 0.1 collective-permute-done.6.refs_1_
  60.9 0.4 collective-permute-start.10
  61.3 3.3 %collective-permute-start.9 = (f32[1,16,1536]{2,1,0:T(8,128)S(1)}, f32[1,16,1536]{2,1,0:T(8,128)S(1)}, u32[]{:S(2)}, u32[]{:S(2)}) collective-permute-start(f32[1,16,1536]{2,1,0:T(8,128)S(1)} %get-tuple-element.81), channel_id=1, source_target_pairs={{0,4},{1,5},{2,6},{3,7},{4,0},{5,1},{6,2},{7,3},{8,12},{9,13},{10,... | collective-permute-start | bytes 294920 | tf_op jit(solution)/shard_map/ppermute | solution.py:391
  64.6 3.4 %collective-permute-done.9.refs_1_ = f32[1,16,1536]{2,1,0:T(8,128)S(1)} collective-permute-done((f32[1,16,1536]{2,1,0:T(8,128)S(1)}, f32[1,16,1536]{2,1,0:T(8,128)S(1)}, u32[]{:S(2)}, u32[]{:S(2)}) %collective-permute-start.9) | collective-permute-done | bytes 98336 | tf_op jit(solution)/shard_map/ppermute | solution.py:391
  68.0 0.0 collective-permute-done.10.refs_3_
  68.0 2.3 %collective-permute-start.14 = (f32[1,16,1024]{2,1,0:T(8,128)S(1)}, f32[1,16,1024]{2,1,0:T(8,128)S(1)}, u32[]{:S(2)}, u32[]{:S(2)}) collective-permute-start(f32[1,16,1024]{2,1,0:T(8,128)S(1)} %get-tuple-element.86), channel_id=1, source_target_pairs={{0,4},{1,5},{2,6},{3,7},{4,0},{5,1},{6,2},{7,3},{8,12},{9,13},{10,... | collective-permute-start | bytes 196616 | tf_op jit(solution)/shard_map/ppermute | solution.py:391
  70.3 2.9 %collective-permute-done.14.refs_1_ = f32[1,16,1024]{2,1,0:T(8,128)S(1)} collective-permute-done((f32[1,16,1024]{2,1,0:T(8,128)S(1)}, f32[1,16,1024]{2,1,0:T(8,128)S(1)}, u32[]{:S(2)}, u32[]{:S(2)}) %collective-permute-start.14) | collective-permute-done | bytes 65568 | tf_op jit(solution)/shard_map/ppermute | solution.py:391
  73.3 0.0 copy-start
  73.3 0.0 copy-start.3
  73.3 1.5 %collective-permute-start.17 = (f32[16,1024]{1,0:T(8,128)S(1)}, f32[16,1024]{1,0:T(8,128)S(1)}, u32[]{:S(2)}, u32[]{:S(2)}) collective-permute-start(f32[16,1024]{1,0:T(8,128)S(1)} %chip_sums.5.refs_4_), channel_id=1, source_target_pairs={{0,24},{8,16},{16,8},{24,0},{1,25},{9,17},{17,9},{25,1},{2,26},{10... | collective-permute-start | bytes 196616 | tf_op jit(solution)/shard_map/ppermute | solution.py:390
  74.8 1.5 %collective-permute-start.13 = (f32[16,1536]{1,0:T(8,128)S(1)}, f32[16,1536]{1,0:T(8,128)S(1)}, u32[]{:S(2)}, u32[]{:S(2)}) collective-permute-start(f32[16,1536]{1,0:T(8,128)S(1)} %get-tuple-element.84.refs_0_), channel_id=1, source_target_pairs={{0,24},{8,16},{16,8},{24,0},{1,25},{9,17},{17,9},{25,1},{2,26},{10... | collective-permute-start | bytes 294920 | tf_op jit(solution)/shard_map/ppermute | solution.py:390
  76.3 1.1 %collective-permute-start.12 = (f32[16,1536]{1,0:T(8,128)S(1)}, f32[16,1536]{1,0:T(8,128)S(1)}, u32[]{:S(2)}, u32[]{:S(2)}) collective-permute-start(f32[16,1536]{1,0:T(8,128)S(1)} %get-tuple-element.84.refs_0_), channel_id=1, source_target_pairs={{0,16},{8,24},{16,0},{24,8},{1,17},{9,25},{17,1},{25,9},{2,18},{10... | collective-permute-start | bytes 294920 | tf_op jit(solution)/shard_map/ppermute | solution.py:390
  77.4 0.8 %collective-permute-start.11 = (f32[16,1536]{1,0:T(8,128)S(1)}, f32[16,1536]{1,0:T(8,128)S(1)}, u32[]{:S(2)}, u32[]{:S(2)}) collective-permute-start(f32[16,1536]{1,0:T(8,128)S(1)} %get-tuple-element.84.refs_0_), channel_id=1, source_target_pairs={{0,8},{8,0},{16,24},{24,16},{1,9},{9,1},{17,25},{25,17},{2,10},{10... | collective-permute-start | bytes 294920 | tf_op jit(solution)/shard_map/ppermute | solution.py:390
  78.3 1.3 %collective-permute-start.16 = (f32[16,1024]{1,0:T(8,128)S(1)}, f32[16,1024]{1,0:T(8,128)S(1)}, u32[]{:S(2)}, u32[]{:S(2)}) collective-permute-start(f32[16,1024]{1,0:T(8,128)S(1)} %chip_sums.5.refs_4_), channel_id=1, source_target_pairs={{0,16},{8,24},{16,0},{24,8},{1,17},{9,25},{17,1},{25,9},{2,18},{10... | collective-permute-start | bytes 196616 | tf_op jit(solution)/shard_map/ppermute | solution.py:390
  79.6 0.0 collective-permute-done.17.refs_7_
  79.6 0.8 collective-permute-start.15
  80.3 0.0 all-to-all-done.recv_ref
  80.3 0.0 copy-done
  80.3 0.0 copy-done.3
  80.3 2.4 %table_part.1 = (f32[512,512]{1,0:T(8,128)}, f32[512]{0:T(512)}) custom-call(f32[32,72,128]{2,1,0:T(8,128)S(1)} %all-to-all-done.recv_ref, f32[512,512]{1,0:T(8,128)S(1)} %copy-done, f32[512]{0:T(512)S(1)} %copy-done.3), custom_call_target="tpu_custom_call" | custom-call | flops 1000000000 | bytes 65536 | tf_op jit(solution)/shard_map/table_part/pallas_call | solution.py:372
  82.7 0.0 collective-permute-done.13.refs_3_
  82.7 0.0 collective-permute-done.12.refs_2_
  82.7 0.0 collective-permute-done.11.refs_1_
  82.7 0.0 collective-permute-done.16.refs_6_
  82.7 1.1 %collective-permute-done.15.refs_5_ = f32[16,1024]{1,0:T(8,128)S(1)} collective-permute-done((f32[16,1024]{1,0:T(8,128)S(1)}, f32[16,1024]{1,0:T(8,128)S(1)}, u32[]{:S(2)}, u32[]{:S(2)}) %collective-permute-start.15) | collective-permute-done | bytes 65568 | tf_op jit(solution)/shard_map/ppermute | solution.py:390
  83.8 0.9 %gather.1 = (f32[4,16,2048]{2,1,0:T(8,128)}, f32[4,16,512]{2,1,0:T(8,128)}) custom-call(f32[16,1536]{1,0:T(8,128)S(1)} %get-tuple-element.84.refs_0_, f32[16,1536]{1,0:T(8,128)S(1)} %collective-permute-done.11.refs_1_, f32[16,1536]{1,0:T(8,128)S(1)} %collective-permute-done.12.refs_2_, f32[16,1536]{1,0:T(8,128)S(1)} %collective-permute-done.13.refs_3_, ...), custom_call_target="tpu_custom_call" | custom-call | flops 1000000000 | bytes 65536 | tf_op jit(solution)/shard_map/gather/pallas_call | solution.py:372
  (3 shorter events, 0.1 us)
Async XLA Ops:
  9.5 5.8 %collective-permute-start = (f32[256,1536]{1,0:T(8,128)S(1)}, f32[256,1536]{1,0:T(8,128)S(1)}, u32[]{:S(2)}, u32[]{:S(2)}) collective-permute-start(f32[256,1536]{1,0:T(8,128)S(1)} %get-tuple-element.49), channel_id=1, source_target_pairs={{0,1},{1,0},{2,3},{3,2},{4,5},{5,4},{6,7},{7,6},{8,9},{9,8},{10,11... | collective-permute-start | bytes 4718600 | tf_op jit(solution)/shard_map/ppermute | solution.py:420
  15.3 13.2 %collective-permute-start.3 = (f32[256,1024]{1,0:T(8,128)}, f32[256,1024]{1,0:T(8,128)S(1)}, u32[]{:S(2)}, u32[]{:S(2)}) collective-permute-start(f32[256,1024]{1,0:T(8,128)} %get-tuple-element.67), channel_id=1, source_target_pairs={{0,1},{1,0},{2,3},{3,2},{4,5},{5,4},{6,7},{7,6},{8,9},{9,8},{10,11... | collective-permute-start | bytes 3145736 | tf_op jit(solution)/shard_map/ppermute | solution.py:424
  15.4 5.8 %copy-start.1 = (s32[1,32,16]{1,2,0:T(8,128)S(1)}, s32[1,32,16]{1,2,0:T(8,128)}, u32[]{:S(2)}) copy-start(s32[1,32,16]{1,2,0:T(8,128)} %param.14) | copy-start | bytes 6148
  15.4 5.8 %copy-start.2 = (s32[1,512]{1,0:T(1,128)S(1)}, s32[1,512]{1,0:T(1,128)}, u32[]{:S(2)}) copy-start(s32[1,512]{1,0:T(1,128)} %slot_ref.1) | copy-start | bytes 6148
  16.7 12.4 %collective-permute-start.1 = (f32[2,64,768]{2,1,0:T(8,128)}, f32[2,64,768]{2,1,0:T(8,128)S(1)}, u32[]{:S(2)}, u32[]{:S(2)}) collective-permute-start(f32[2,64,768]{2,1,0:T(8,128)} %get-tuple-element.61), channel_id=1, source_target_pairs={{0,8},{8,0},{16,24},{24,16},{1,9},{9,1},{17,25},{25,17},{2,10},{10... | collective-permute-start | bytes 1179656 | tf_op jit(solution)/shard_map/ppermute | solution.py:390
  19.6 11.0 %collective-permute-start.2 = (f32[2,64,768]{2,1,0:T(8,128)}, f32[2,64,768]{2,1,0:T(8,128)S(1)}, u32[]{:S(2)}, u32[]{:S(2)}) collective-permute-start(f32[2,64,768]{2,1,0:T(8,128)} %get-tuple-element.62), channel_id=1, source_target_pairs={{0,16},{8,24},{16,0},{24,8},{1,17},{9,25},{17,1},{25,9},{2,18},{10... | collective-permute-start | bytes 1179656 | tf_op jit(solution)/shard_map/ppermute | solution.py:390
  24.5 55.8 %all-to-all-start = ((f32[32,72,128]{2,1,0:T(8,128)}), f32[32,72,128]{2,1,0:T(8,128)S(1)}, u32[]{:S(2)}, u32[]{:S(2)}) async-start(f32[32,72,128]{2,1,0:T(8,128)} %events_part.1), calls=%async_computation | async-start | bytes 2359296 | tf_op jit(solution)/shard_map/all_to_all | solution.py:434
  32.2 19.4 %collective-permute-start.4 = (f32[64,1792]{1,0:T(8,128)S(1)}, f32[64,1792]{1,0:T(8,128)S(1)}, u32[]{:S(2)}, u32[]{:S(2)}) collective-permute-start(f32[64,1792]{1,0:T(8,128)S(1)} %get-tuple-element.70), channel_id=1, source_target_pairs={{0,8},{8,0},{16,24},{24,16},{1,9},{9,1},{17,25},{25,17},{2,10},{10... | collective-permute-start | bytes 1376264 | tf_op jit(solution)/shard_map/ppermute | solution.py:390
  32.6 19.7 %collective-permute-start.5 = (f32[64,1792]{1,0:T(8,128)S(1)}, f32[64,1792]{1,0:T(8,128)S(1)}, u32[]{:S(2)}, u32[]{:S(2)}) collective-permute-start(f32[64,1792]{1,0:T(8,128)S(1)} %get-tuple-element.71), channel_id=1, source_target_pairs={{0,16},{8,24},{16,0},{24,8},{1,17},{9,25},{17,1},{25,9},{2,18},{10... | collective-permute-start | bytes 1376264 | tf_op jit(solution)/shard_map/ppermute | solution.py:390
  52.4 8.4 %collective-permute-start.6 = (f32[2,16,1536]{2,1,0:T(8,128)S(1)}, f32[2,16,1536]{2,1,0:T(8,128)S(1)}, u32[]{:S(2)}, u32[]{:S(2)}) collective-permute-start(f32[2,16,1536]{2,1,0:T(8,128)S(1)} %get-tuple-element.75), channel_id=1, source_target_pairs={{0,2},{1,3},{2,0},{3,1},{4,6},{5,7},{6,4},{7,5},{8,10},{9,11},{10,... | collective-permute-start | bytes 589832 | tf_op jit(solution)/shard_map/ppermute | solution.py:391
  54.9 5.4 %collective-permute-start.7 = (f32[4,16,512]{2,1,0:T(8,128)S(1)}, f32[4,16,512]{2,1,0:T(8,128)S(1)}, u32[]{:S(2)}, u32[]{:S(2)}) collective-permute-start(f32[4,16,512]{2,1,0:T(8,128)S(1)} %get-tuple-element.78), channel_id=1, source_target_pairs={{0,8},{8,0},{16,24},{24,16},{1,9},{9,1},{17,25},{25,17},{2,10},{10... | collective-permute-start | bytes 393224 | tf_op jit(solution)/shard_map/ppermute | solution.py:390
  55.4 5.4 %collective-permute-start.8 = (f32[4,16,512]{2,1,0:T(8,128)S(1)}, f32[4,16,512]{2,1,0:T(8,128)S(1)}, u32[]{:S(2)}, u32[]{:S(2)}) collective-permute-start(f32[4,16,512]{2,1,0:T(8,128)S(1)} %get-tuple-element.79), channel_id=1, source_target_pairs={{0,16},{8,24},{16,0},{24,8},{1,17},{9,25},{17,1},{25,9},{2,18},{10... | collective-permute-start | bytes 393224 | tf_op jit(solution)/shard_map/ppermute | solution.py:390
  60.9 7.1 %collective-permute-start.10 = (f32[2,16,1024]{2,1,0:T(8,128)S(1)}, f32[2,16,1024]{2,1,0:T(8,128)S(1)}, u32[]{:S(2)}, u32[]{:S(2)}) collective-permute-start(f32[2,16,1024]{2,1,0:T(8,128)S(1)} %get-tuple-element.83), channel_id=1, source_target_pairs={{0,2},{1,3},{2,0},{3,1},{4,6},{5,7},{6,4},{7,5},{8,10},{9,11},{10,... | collective-permute-start | bytes 393224 | tf_op jit(solution)/shard_map/ppermute | solution.py:391
  61.3 6.7 %collective-permute-start.9 = (f32[1,16,1536]{2,1,0:T(8,128)S(1)}, f32[1,16,1536]{2,1,0:T(8,128)S(1)}, u32[]{:S(2)}, u32[]{:S(2)}) collective-permute-start(f32[1,16,1536]{2,1,0:T(8,128)S(1)} %get-tuple-element.81), channel_id=1, source_target_pairs={{0,4},{1,5},{2,6},{3,7},{4,0},{5,1},{6,2},{7,3},{8,12},{9,13},{10,... | collective-permute-start | bytes 294920 | tf_op jit(solution)/shard_map/ppermute | solution.py:391
  68.0 5.2 %collective-permute-start.14 = (f32[1,16,1024]{2,1,0:T(8,128)S(1)}, f32[1,16,1024]{2,1,0:T(8,128)S(1)}, u32[]{:S(2)}, u32[]{:S(2)}) collective-permute-start(f32[1,16,1024]{2,1,0:T(8,128)S(1)} %get-tuple-element.86), channel_id=1, source_target_pairs={{0,4},{1,5},{2,6},{3,7},{4,0},{5,1},{6,2},{7,3},{8,12},{9,13},{10,... | collective-permute-start | bytes 196616 | tf_op jit(solution)/shard_map/ppermute | solution.py:391
  73.3 7.1 %copy-start = (f32[512,512]{1,0:T(8,128)S(1)}, f32[512,512]{1,0:T(8,128)}, u32[]{:S(2)}) copy-start(f32[512,512]{1,0:T(8,128)} %table_ref.1) | copy-start | bytes 3145732
  73.3 7.1 %copy-start.3 = (f32[512]{0:T(512)S(1)}, f32[512]{0:T(512)}, u32[]{:S(2)}) copy-start(f32[512]{0:T(512)} %accum_ref.1) | copy-start | bytes 6148
  73.3 6.3 %collective-permute-start.17 = (f32[16,1024]{1,0:T(8,128)S(1)}, f32[16,1024]{1,0:T(8,128)S(1)}, u32[]{:S(2)}, u32[]{:S(2)}) collective-permute-start(f32[16,1024]{1,0:T(8,128)S(1)} %chip_sums.5.refs_4_), channel_id=1, source_target_pairs={{0,24},{8,16},{16,8},{24,0},{1,25},{9,17},{17,9},{25,1},{2,26},{10... | collective-permute-start | bytes 196616 | tf_op jit(solution)/shard_map/ppermute | solution.py:390
  74.8 8.0 %collective-permute-start.13 = (f32[16,1536]{1,0:T(8,128)S(1)}, f32[16,1536]{1,0:T(8,128)S(1)}, u32[]{:S(2)}, u32[]{:S(2)}) collective-permute-start(f32[16,1536]{1,0:T(8,128)S(1)} %get-tuple-element.84.refs_0_), channel_id=1, source_target_pairs={{0,24},{8,16},{16,8},{24,0},{1,25},{9,17},{17,9},{25,1},{2,26},{10... | collective-permute-start | bytes 294920 | tf_op jit(solution)/shard_map/ppermute | solution.py:390
  76.3 6.4 %collective-permute-start.12 = (f32[16,1536]{1,0:T(8,128)S(1)}, f32[16,1536]{1,0:T(8,128)S(1)}, u32[]{:S(2)}, u32[]{:S(2)}) collective-permute-start(f32[16,1536]{1,0:T(8,128)S(1)} %get-tuple-element.84.refs_0_), channel_id=1, source_target_pairs={{0,16},{8,24},{16,0},{24,8},{1,17},{9,25},{17,1},{25,9},{2,18},{10... | collective-permute-start | bytes 294920 | tf_op jit(solution)/shard_map/ppermute | solution.py:390
  77.4 5.3 %collective-permute-start.11 = (f32[16,1536]{1,0:T(8,128)S(1)}, f32[16,1536]{1,0:T(8,128)S(1)}, u32[]{:S(2)}, u32[]{:S(2)}) collective-permute-start(f32[16,1536]{1,0:T(8,128)S(1)} %get-tuple-element.84.refs_0_), channel_id=1, source_target_pairs={{0,8},{8,0},{16,24},{24,16},{1,9},{9,1},{17,25},{25,17},{2,10},{10... | collective-permute-start | bytes 294920 | tf_op jit(solution)/shard_map/ppermute | solution.py:390
  78.3 4.5 %collective-permute-start.16 = (f32[16,1024]{1,0:T(8,128)S(1)}, f32[16,1024]{1,0:T(8,128)S(1)}, u32[]{:S(2)}, u32[]{:S(2)}) collective-permute-start(f32[16,1024]{1,0:T(8,128)S(1)} %chip_sums.5.refs_4_), channel_id=1, source_target_pairs={{0,16},{8,24},{16,0},{24,8},{1,17},{9,25},{17,1},{25,9},{2,18},{10... | collective-permute-start | bytes 196616 | tf_op jit(solution)/shard_map/ppermute | solution.py:390
  79.6 4.3 %collective-permute-start.15 = (f32[16,1024]{1,0:T(8,128)S(1)}, f32[16,1024]{1,0:T(8,128)S(1)}, u32[]{:S(2)}, u32[]{:S(2)}) collective-permute-start(f32[16,1024]{1,0:T(8,128)S(1)} %chip_sums.5.refs_4_), channel_id=1, source_target_pairs={{0,8},{8,0},{16,24},{24,16},{1,9},{9,1},{17,25},{25,17},{2,10},{10... | collective-permute-start | bytes 196616 | tf_op jit(solution)/shard_map/ppermute | solution.py:390

commit v8 on v7

--- a/solution.py
+++ b/solution.py
@@ -154,18 +154,27 @@
         ref[:, width:] = dot_nn(normed_t_ref[start:start + half, :], gpre_ref[...])
 
 
-def attention_kernel(len_ref, hid_ref, dsilu_ref, gatt_ref, normed_t_ref, keep_ref, send_ref, gpre_ref):
+def attention_kernel(heads, len_ref, hid_ref, dsilu_ref, gatt_ref, *refs):
+    *refs, gpre_ref = refs
     tokens, width = gatt_ref.shape
     hd = width // HEADS
     inv_len = 1.0 / len_ref[0].astype(f32)
     scale = hd ** -0.5
     steps = tokens // STEP
+    base = gpre_ref.shape[1] // 2
+    past = heads[0] * hd if refs else 0
+    if refs:
+        normed_t_ref, before_ref, keep_ref, send_ref = refs
+        gpre_ref[:, :past] = before_ref[:, :past]
+        gpre_ref[:, base:base + past] = before_ref[:, past:]
 
     tri = lax.broadcasted_iota(jnp.int32, (STEP, STEP), 0) <= lax.broadcasted_iota(jnp.int32, (STEP, STEP), 1)
-    for h in range(HEADS):
+    for h in heads:
         v_cols = slice(h * hd, (h + 1) * hd)
         q_cols = slice(width + h * hd, width + (h + 1) * hd)
         k_cols = slice(2 * width + h * hd, 2 * width + (h + 1) * hd)
+        at = past + (h - heads[0]) * hd
+        out_q, out_k = slice(at, at + hd), slice(base + at, base + at + hd)
         grad_q = [None] * steps
         for j in range(steps):
             keys = pl.ds(j * STEP, STEP)
@@ -185,14 +194,15 @@
                 pk, pq = dot_nn(gscore, query), dot_tn(gscore, key)
                 grad_k = pk if grad_k is None else grad_k + pk
                 grad_q[i] = pq if grad_q[i] is None else grad_q[i] + pq
-            gpre_ref[keys, q_cols] = (grad_k * dsilu_ref[keys, q_cols].astype(f32)).astype(bf16)
+            gpre_ref[keys, out_k] = (grad_k * dsilu_ref[keys, q_cols].astype(f32)).astype(bf16)
         for i in range(steps):
             rows = pl.ds(i * STEP, STEP)
-            gpre_ref[rows, v_cols] = (grad_q[i] * dsilu_ref[rows, v_cols].astype(f32)).astype(bf16)
-
-    half = width // 2
-    for ref, start in ((send_ref, half), (keep_ref, 0)):
-        ref[...] = dot_nn(normed_t_ref[start:start + half, :], gpre_ref[...])
+            gpre_ref[rows, out_q] = (grad_q[i] * dsilu_ref[rows, v_cols].astype(f32)).astype(bf16)
+
+    if refs:
+        half = width // 2
+        for ref, start in ((send_ref, half), (keep_ref, 0)):
+            ref[...] = dot_nn(normed_t_ref[start:start + half, :], gpre_ref[...])
 
 
 def events_kernel(len_ref, ev_ref, cot_ref, win_ref, slot_ref, slot_row_ref, gpre_uv_ref, gpre_qk_ref,
@@ -418,29 +428,34 @@
          ((tokens, width), bf16), ((tokens, width), bf16), ((tokens, width), f32), ((HEADS, tokens, tokens), bf16),
          (w_out.shape, bf16)], far=4, long=True, grant=16)
     recv1 = lax.ppermute(send1, "rows", cores)
+    heads = list(range(HEADS))
+    (gpre_some,) = call(
+        functools.partial(attention_kernel, heads[:HEADS // 2]), "attention_first", [local(tokens, width, dtype=bf16)],
+        (lengths, hid, dsilu, gatt), 1, long=True, grant=10)
+    half1, half2 = 3 * width // 2, width
+    to_x, to_y, keep_a, keep_b = call(
+        first_kernel, "first_sums", [local(2, strip, half1)] * 4, (by_dp(keep1), by_dp(after(recv1, gpre_some))))
     keep2, send2, gpre_qk = call(
-        attention_kernel, "attention_part", [far_off(width // 2, 2 * width)] * 2 + [local(tokens, 2 * width, dtype=bf16)],
-        (lengths, hid, dsilu, gatt, normed_t), 1, long=True, grant=10)
+        functools.partial(attention_kernel, heads[HEADS // 2:]), "attention_second",
+        [local(width // 2, 2 * width)] * 2 + [local(tokens, 2 * width, dtype=bf16)],
+        (lengths, hid, dsilu, after(gatt, to_x, to_y), normed_t, gpre_some), 1, long=True, grant=10)
     recv2 = lax.ppermute(send2, "rows", cores)
     pay_rows = capacity * (width // LANES) + ID_ROWS
-    half1, half2 = 3 * width // 2, width
-    to_x, to_y, keep_a, keep_b = call(
-        first_kernel, "first_sums", [far_off(2, strip, half1)] * 4, (by_dp(keep1), by_dp(after(recv1, keep2))))
-    gpre_uv = after(gpre_uv, to_x, to_y)
     (send,) = call(
         events_kernel, "events_part", [local(owners, pay_rows, LANES)],
         (lengths, events, cotangent, w_in, event_slot, slot_row[0].T, gpre_uv, gpre_qk), 1,
-        [((tokens, width), bf16), ((tokens, width), bf16), ((owners * capacity, width), f32)], long=True, grant=10)
-    recv = lax.all_to_all(send, ("dp", "rows"), split_axis=0, concat_axis=0, tiled=True)
+        [((tokens, width), bf16), ((tokens, width), bf16), ((owners * capacity, width), f32)], grant=10)
     from_x, from_y = over_dp(to_x, 1), over_dp(to_y, 2)
     to_x, to_y, next_a, next_b, keep2_a, keep2_b = call(
         second_kernel, "second_sums",
-        [local(strip, half1 + 2 * half2)] * 2 + [local(strip, half1)] * 2 + [local(2, strip, half2)] * 2,
-        (after(keep_a, send), from_x, keep_b, from_y, by_dp(keep2), by_dp(recv2)), long=True, grant=10, apart=(0, 2, 4), either=(1, 3, 5))
+        [local(strip, half1 + 2 * half2)] * 2 + [far_off(strip, half1)] * 2 + [far_off(2, strip, half2)] * 2,
+        (after(keep_a, send), from_x, keep_b, from_y, by_dp(keep2), by_dp(recv2)))
+    recv = lax.all_to_all(after(send, to_x, to_y), ("dp", "rows"), split_axis=0, concat_axis=0, tiled=True)
     from_x, from_y = over_dp(to_x, 1), over_dp(to_y, 2)
     send1, keep1, to_x, to_y, next_a, next_b = call(
         third_kernel, "third_sums", [local(chips // 2, piece, 2 * half1)] * 2 + [local(chips, piece, half2)] * 4,
-        [by_chip(v) for v in (next_a, next_b, from_x, from_y, keep2_a, keep2_b)])
+        [by_chip(v) for v in (next_a, next_b, from_x, from_y, keep2_a, keep2_b)],
+        long=True, grant=10, apart=(0, 1, 4, 5), either=(2, 3))
     first = [keep1, over_chips(send1, 0)]
     second = [next_a, next_b, over_dp(to_x, 1), over_dp(to_y, 2)]
     pieces, at = [], 1
@@ -450,6 +465,8 @@
         if first is not None:
             outs += [local(piece, 2 * half1)] if bit is None else [local(chips >> (bit + 1), piece, 2 * half1)] * 2
         outs += [local(piece, 2 * half2)] if bit2 is None else [local(chips >> (bit2 + 1), piece, 2 * half2)] * 2
+        if pieces:
+            second[0] = after(second[0], *pieces)
         outs = list(call(
             functools.partial(chips_kernel, tokens, bit, bit2, first is not None), "chip_sums", outs, (first or []) + second))
         if first is not None:

time: 85 us -> 89.3 us (1.051)
  starting transfers between devices: 28.1 us -> 33.7 us
  Pallas kernels: 23.3 us -> 21.9 us
    ppermute x12, starting transfers between devices: 15 us -> 18.4 us  [body(): lax.ppermute(v, 'dp', [(i, i ^ bit) for i in range(dp_size)])]
    ppermute x12, waiting for transfers between devices: 25.5 us -> 24.1 us  [body(): lax.ppermute(v, 'dp', [(i, i ^ bit) for i in range(dp_size)])]
    pallas_call x11 -> x12, Pallas kernels: 23.3 us -> 21.9 us  [call(): pl.pallas_call(kernel, name=name, in_specs=[pl.BlockSpec(memory_space=p o...]
    ppermute x1, waiting for transfers between devices: 0.01 us -> 1.19 us  [body(): recv1 = lax.ppermute(send1, 'rows', cores)]
    ppermute x4, starting transfers between devices: 8.47 us -> 9.47 us  [body(): lax.ppermute(v, 'rows', [(i, i ^ 2 << bit) for i in range(rows_size)])]
    all_to_all x1, starting transfers between devices: 3.97 us -> 4.89 us  [body(): lax.all_to_all(after(send, to_x, to_y), ('dp', 'rows'), split_axis=0, con...]
  transfers between devices with their start and end apart: 19 -> 19, of which waited for: 10 -> 15; matrix products, arithmetic and copies ran while one was open for 0% -> 0% of each run, Pallas kernels for 17% -> 10%
where the time goes in v8:
time: 89.3 us; the launch traced here: 89.1 us
  starting transfers between devices  33.7 us (38%)
  waiting for transfers between devices  32.1 us (36%)
  Pallas kernels  21.9 us (25%)
  between operations  1.36 us (2%)
    ppermute x12, waiting for transfers between devices, body(): lax.ppermute(v, 'dp', [(i, i ^ bit) for i in range(dp_size)])  24.1 us
    pallas_call x12, Pallas kernels, call(): pl.pallas_call(kernel, name=name, in_specs=[pl.BlockSpec(memory_space=p o...  21.9 us
    ppermute x12, starting transfers between devices, body(): lax.ppermute(v, 'dp', [(i, i ^ bit) for i in range(dp_size)])  18.4 us
    ppermute x4, starting transfers between devices, body(): lax.ppermute(v, 'rows', [(i, i ^ 2 << bit) for i in range(rows_size)])  9.47 us
    ppermute x4, waiting for transfers between devices, body(): lax.ppermute(v, 'rows', [(i, i ^ 2 << bit) for i in range(rows_size)])  6.84 us
    all_to_all x1, starting transfers between devices, body(): lax.all_to_all(after(send, to_x, to_y), ('dp', 'rows'), split_axis=0, con...  4.89 us
  transfers between devices with their start and end apart: 19, of which 15 were waited for; matrix products, arithmetic and copies ran while one was open for 0% of the time, Pallas kernels for 10%

profile of v8, /device:TPU:0, one launch (start us, length us, event | category | flops | bytes accessed | tf_op | source)
XLA Modules:
  0.0 89.1 jit_solution(9221237089022818894)
XLA Ops:
  1.3 8.3 %forward_part.1 = (f32[256,1536]{1,0:T(8,128)S(1)}, f32[256,1536]{1,0:T(8,128)S(1)}, bf16[512,1536]{1,0:T(8,128)(2,1)S(1)}, bf16[512,1024]{1,0:T(8,128)(2,1)S(1)...) custom-call(s32[1]{0:T(128)S(6)} %copy.13.len_ref, ...), custom_call_target="tpu_custom_call" | custom-call | flops 99999997952 | bytes 65536 | tf_op jit(solution)/shard_map/forward_part/pallas_call | solution.py:382
  9.5 0.5 collective-permute-start
  10.1 1.8 %attention_first.1.refs_1_ = bf16[512,512]{1,0:T(8,128)(2,1)S(1)} custom-call(s32[1]{0:T(128)S(6)} %copy.13.len_ref, bf16[512,1536]{1,0:T(8,128)(2,1)S(1)} %get-tuple-element.52.hid_ref, bf16[512,1024]{1,0:T(8,128)(2,1)S(1)} %get-tuple-element.53.dsilu_ref, bf16[512,512]{1,0:T(8,128)(2,1)S(1)} %get-tuple-element.63.gatt_ref), custom_call_target="tpu_custom_call" | custom-call | flops 99999997952 | bytes 65536 | tf_op jit(solution)/shard_map/attention_first/pallas_call | solution.py:382
  11.9 1.2 %collective-permute-done = f32[256,1536]{1,0:T(8,128)S(1)} collective-permute-done((f32[256,1536]{1,0:T(8,128)S(1)}, f32[256,1536]{1,0:T(8,128)S(1)}, u32[]{:S(2)}, u32[]{:S(2)}) %collective-permute-start) | collective-permute-done | bytes 1572896 | tf_op jit(solution)/shard_map/ppermute | solution.py:430
  13.1 0.2 first_sums.1
  13.3 0.0 copy-start
  13.3 0.0 copy-start.1
  13.3 2.5 %attention_second.1 = (f32[256,1024]{1,0:T(8,128)S(1)}, f32[256,1024]{1,0:T(8,128)S(1)}, bf16[512,1024]{1,0:T(8,128)(2,1)S(1)}) custom-call(s32[1]{0:T(128)S(6)} %copy.13.len_ref, bf16[512,1536]{1,0:T(8,128)(2,1)S(1)} %get-tuple-element.52.hid_ref, bf16[512,1024]{1,0:T(8,128)(2,1)S(1)} %get-tuple-element.53.dsilu_ref, ...), custom_call_target="tpu_custom_call" | custom-call | flops 99999997952 | bytes 65536 | tf_op jit(solution)/shard_map/attention_second/pallas_call | solution.py:382
  15.8 0.4 collective-permute-start.3
  16.2 2.6 %collective-permute-start.1 = (f32[2,64,768]{2,1,0:T(8,128)S(1)}, f32[2,64,768]{2,1,0:T(8,128)S(1)}, u32[]{:S(2)}, u32[]{:S(2)}) collective-permute-start(f32[2,64,768]{2,1,0:T(8,128)S(1)} %get-tuple-element.61), channel_id=1, source_target_pairs={{0,8},{8,0},{16,24},{24,16},{1,9},{9,1},{17,25},{25,17},{2,10},{10... | collective-permute-start | bytes 1179656 | tf_op jit(solution)/shard_map/ppermute | solution.py:400
  18.8 1.5 %collective-permute-start.2 = (f32[2,64,768]{2,1,0:T(8,128)S(1)}, f32[2,64,768]{2,1,0:T(8,128)S(1)}, u32[]{:S(2)}, u32[]{:S(2)}) collective-permute-start(f32[2,64,768]{2,1,0:T(8,128)S(1)} %get-tuple-element.62), channel_id=1, source_target_pairs={{0,16},{8,24},{16,0},{24,8},{1,17},{9,25},{17,1},{25,9},{2,18},{10... | collective-permute-start | bytes 1179656 | tf_op jit(solution)/shard_map/ppermute | solution.py:400
  20.4 0.0 copy-done
  20.4 0.0 copy-done.1
  20.4 3.4 %events_part.1 = f32[32,72,128]{2,1,0:T(8,128)} custom-call(s32[1]{0:T(128)S(6)} %copy.13.len_ref, bf16[512,512]{1,0:T(8,128)(2,1)S(1)} %get-tuple-element.57.ev_ref, bf16[512,512]{1,0:T(8,128)(2,1)S(1)} %get-tuple-element.58.cot_ref, bf16[512,2048]{1,0:T(8,128)(2,1)S(1)} %get-tuple-element.59.win_ref, s32[1,512]{1,0:T(1,128)S(1)} %copy-done.1, ...), custom_call_target="tpu_custom_call" | custom-call | flops 1000000000 | bytes 65536 | tf_op jit(solution)/shard_map/events_part/pallas_call | solution.py:382
  23.8 4.7 %collective-permute-done.1.from_x_ref = f32[2,64,768]{2,1,0:T(8,128)S(1)} collective-permute-done((f32[2,64,768]{2,1,0:T(8,128)S(1)}, f32[2,64,768]{2,1,0:T(8,128)S(1)}, u32[]{:S(2)}, u32[]{:S(2)}) %collective-permute-start.1) | collective-permute-done | bytes 393248 | tf_op jit(solution)/shard_map/ppermute | solution.py:400
  28.5 1.5 %collective-permute-done.2.from_y_ref = f32[2,64,768]{2,1,0:T(8,128)S(1)} collective-permute-done((f32[2,64,768]{2,1,0:T(8,128)S(1)}, f32[2,64,768]{2,1,0:T(8,128)S(1)}, u32[]{:S(2)}, u32[]{:S(2)}) %collective-permute-start.2) | collective-permute-done | bytes 393248 | tf_op jit(solution)/shard_map/ppermute | solution.py:400
  29.9 0.0 collective-permute-done.3
  29.9 1.0 %second_sums.1 = (f32[64,1792]{1,0:T(8,128)S(1)}, f32[64,1792]{1,0:T(8,128)S(1)}, f32[64,768]{1,0:T(8,128)}, f32[64,768]{1,0:T(8,128)}, f32[2,64,512]{2,1,0:T(8,128)}, /*index=5*/f32[2,64,512]{2,1,0:T(8,128)}) custom-call(f32[2,64,768]{2,1,0:T(8,128)S(1)} %get-tuple-element.66.keep_a_ref, f32[2,64,768]{2,1,0:T(8,128)S(1)} %collective-permute-done.1.from_x_ref, ...), custom_call_target="tpu_custom_call" | custom-call | flops 1000000000 | bytes 65536 | tf_op jit(solution)/shard_map/second_sums/pallas_call | solution.py:382
  31.0 0.3 collective-permute-start.4
  31.3 1.7 %collective-permute-start.5 = (f32[64,1792]{1,0:T(8,128)S(1)}, f32[64,1792]{1,0:T(8,128)S(1)}, u32[]{:S(2)}, u32[]{:S(2)}) collective-permute-start(f32[64,1792]{1,0:T(8,128)S(1)} %get-tuple-element.73), channel_id=1, source_target_pairs={{0,16},{8,24},{16,0},{24,8},{1,17},{9,25},{17,1},{25,9},{2,18},{10... | collective-permute-start | bytes 1376264 | tf_op jit(solution)/shard_map/ppermute | solution.py:400
  33.0 4.9 %all-to-all-start = ((f32[32,72,128]{2,1,0:T(8,128)}), f32[32,72,128]{2,1,0:T(8,128)S(1)}, u32[]{:S(2)}, u32[]{:S(2)}) async-start(f32[32,72,128]{2,1,0:T(8,128)} %events_part.1), calls=%async_computation | async-start | bytes 2359296 | tf_op jit(solution)/shard_map/all_to_all | solution.py:453
  38.0 7.9 %collective-permute-done.4 = f32[64,1792]{1,0:T(8,128)S(1)} collective-permute-done((f32[64,1792]{1,0:T(8,128)S(1)}, f32[64,1792]{1,0:T(8,128)S(1)}, u32[]{:S(2)}, u32[]{:S(2)}) %collective-permute-start.4) | collective-permute-done | bytes 458784 | tf_op jit(solution)/shard_map/ppermute | solution.py:400
  45.8 1.2 %collective-permute-done.5 = f32[64,1792]{1,0:T(8,128)S(1)} collective-permute-done((f32[64,1792]{1,0:T(8,128)S(1)}, f32[64,1792]{1,0:T(8,128)S(1)}, u32[]{:S(2)}, u32[]{:S(2)}) %collective-permute-start.5) | collective-permute-done | bytes 458784 | tf_op jit(solution)/shard_map/ppermute | solution.py:400
  47.0 1.3 %third_sums.1 = (f32[2,16,1536]{2,1,0:T(8,128)S(1)}, f32[2,16,1536]{2,1,0:T(8,128)S(1)}, f32[4,16,512]{2,1,0:T(8,128)S(1)}, f32[4,16,512]{2,1,0:T(8,128)S(1)}, f...) custom-call(f32[4,16,768]{2,1,0:T(8,128)} %bitcast.25, f32[4,16,768]{2,1,0:T(8,128)} %bitcast.26, ...), custom_call_target="tpu_custom_call" | custom-call | flops 99999997952 | bytes 65536 | tf_op jit(solution)/shard_map/third_sums/pallas_call | solution.py:382
  48.3 3.2 %collective-permute-start.6 = (f32[2,16,1536]{2,1,0:T(8,128)S(1)}, f32[2,16,1536]{2,1,0:T(8,128)S(1)}, u32[]{:S(2)}, u32[]{:S(2)}) collective-permute-start(f32[2,16,1536]{2,1,0:T(8,128)S(1)} %get-tuple-element.77), channel_id=1, source_target_pairs={{0,2},{1,3},{2,0},{3,1},{4,6},{5,7},{6,4},{7,5},{8,10},{9,11},{10,... | collective-permute-start | bytes 589832 | tf_op jit(solution)/shard_map/ppermute | solution.py:401
  51.5 2.6 %collective-permute-start.7 = (f32[4,16,512]{2,1,0:T(8,128)S(1)}, f32[4,16,512]{2,1,0:T(8,128)S(1)}, u32[]{:S(2)}, u32[]{:S(2)}) collective-permute-start(f32[4,16,512]{2,1,0:T(8,128)S(1)} %get-tuple-element.80), channel_id=1, source_target_pairs={{0,8},{8,0},{16,24},{24,16},{1,9},{9,1},{17,25},{25,17},{2,10},{10... | collective-permute-start | bytes 393224 | tf_op jit(solution)/shard_map/ppermute | solution.py:400
  54.1 2.5 %collective-permute-start.8 = (f32[4,16,512]{2,1,0:T(8,128)S(1)}, f32[4,16,512]{2,1,0:T(8,128)S(1)}, u32[]{:S(2)}, u32[]{:S(2)}) collective-permute-start(f32[4,16,512]{2,1,0:T(8,128)S(1)} %get-tuple-element.81), channel_id=1, source_target_pairs={{0,16},{8,24},{16,0},{24,8},{1,17},{9,25},{17,1},{25,9},{2,18},{10... | collective-permute-start | bytes 393224 | tf_op jit(solution)/shard_map/ppermute | solution.py:400
  56.6 1.0 %collective-permute-done.7.refs_4_ = f32[4,16,512]{2,1,0:T(8,128)S(1)} collective-permute-done((f32[4,16,512]{2,1,0:T(8,128)S(1)}, f32[4,16,512]{2,1,0:T(8,128)S(1)}, u32[]{:S(2)}, u32[]{:S(2)}) %collective-permute-start.7) | collective-permute-done | bytes 131104 | tf_op jit(solution)/shard_map/ppermute | solution.py:400
  57.6 2.2 %collective-permute-done.8.refs_5_ = f32[4,16,512]{2,1,0:T(8,128)S(1)} collective-permute-done((f32[4,16,512]{2,1,0:T(8,128)S(1)}, f32[4,16,512]{2,1,0:T(8,128)S(1)}, u32[]{:S(2)}, u32[]{:S(2)}) %collective-permute-start.8) | collective-permute-done | bytes 131104 | tf_op jit(solution)/shard_map/ppermute | solution.py:400
  59.8 2.1 %collective-permute-done.6.refs_1_ = f32[2,16,1536]{2,1,0:T(8,128)S(1)} collective-permute-done((f32[2,16,1536]{2,1,0:T(8,128)S(1)}, f32[2,16,1536]{2,1,0:T(8,128)S(1)}, u32[]{:S(2)}, u32[]{:S(2)}) %collective-permute-start.6) | collective-permute-done | bytes 196640 | tf_op jit(solution)/shard_map/ppermute | solution.py:401
  61.9 2.5 %collective-permute-start.10 = (f32[2,16,1024]{2,1,0:T(8,128)S(1)}, f32[2,16,1024]{2,1,0:T(8,128)S(1)}, u32[]{:S(2)}, u32[]{:S(2)}) collective-permute-start(f32[2,16,1024]{2,1,0:T(8,128)S(1)} %get-tuple-element.85), channel_id=1, source_target_pairs={{0,2},{1,3},{2,0},{3,1},{4,6},{5,7},{6,4},{7,5},{8,10},{9,11},{10,... | collective-permute-start | bytes 393224 | tf_op jit(solution)/shard_map/ppermute | solution.py:401
  64.5 2.2 %collective-permute-start.9 = (f32[1,16,1536]{2,1,0:T(8,128)S(1)}, f32[1,16,1536]{2,1,0:T(8,128)S(1)}, u32[]{:S(2)}, u32[]{:S(2)}) collective-permute-start(f32[1,16,1536]{2,1,0:T(8,128)S(1)} %get-tuple-element.83), channel_id=1, source_target_pairs={{0,4},{1,5},{2,6},{3,7},{4,0},{5,1},{6,2},{7,3},{8,12},{9,13},{10,... | collective-permute-start | bytes 294920 | tf_op jit(solution)/shard_map/ppermute | solution.py:401
  66.6 3.6 %collective-permute-done.9.refs_1_ = f32[1,16,1536]{2,1,0:T(8,128)S(1)} collective-permute-done((f32[1,16,1536]{2,1,0:T(8,128)S(1)}, f32[1,16,1536]{2,1,0:T(8,128)S(1)}, u32[]{:S(2)}, u32[]{:S(2)}) %collective-permute-start.9) | collective-permute-done | bytes 98336 | tf_op jit(solution)/shard_map/ppermute | solution.py:401
  70.3 0.9 %collective-permute-done.10.refs_3_ = f32[2,16,1024]{2,1,0:T(8,128)S(1)} collective-permute-done((f32[2,16,1024]{2,1,0:T(8,128)S(1)}, f32[2,16,1024]{2,1,0:T(8,128)S(1)}, u32[]{:S(2)}, u32[]{:S(2)}) %collective-permute-start.10) | collective-permute-done | bytes 131104 | tf_op jit(solution)/shard_map/ppermute | solution.py:401
  71.3 1.6 %collective-permute-start.11 = (f32[16,1536]{1,0:T(8,128)S(1)}, f32[16,1536]{1,0:T(8,128)S(1)}, u32[]{:S(2)}, u32[]{:S(2)}) collective-permute-start(f32[16,1536]{1,0:T(8,128)S(1)} %get-tuple-element.86.refs_0_), channel_id=1, source_target_pairs={{0,8},{8,0},{16,24},{24,16},{1,9},{9,1},{17,25},{25,17},{2,10},{10... | collective-permute-start | bytes 294920 | tf_op jit(solution)/shard_map/ppermute | solution.py:400
  72.8 1.5 %collective-permute-start.12 = (f32[16,1536]{1,0:T(8,128)S(1)}, f32[16,1536]{1,0:T(8,128)S(1)}, u32[]{:S(2)}, u32[]{:S(2)}) collective-permute-start(f32[16,1536]{1,0:T(8,128)S(1)} %get-tuple-element.86.refs_0_), channel_id=1, source_target_pairs={{0,16},{8,24},{16,0},{24,8},{1,17},{9,25},{17,1},{25,9},{2,18},{10... | collective-permute-start | bytes 294920 | tf_op jit(solution)/shard_map/ppermute | solution.py:400
  74.3 0.5 collective-permute-start.13
  74.8 1.6 %collective-permute-start.14 = (f32[1,16,1024]{2,1,0:T(8,128)S(1)}, f32[1,16,1024]{2,1,0:T(8,128)S(1)}, u32[]{:S(2)}, u32[]{:S(2)}) collective-permute-start(f32[1,16,1024]{2,1,0:T(8,128)S(1)} %get-tuple-element.89), channel_id=1, source_target_pairs={{0,4},{1,5},{2,6},{3,7},{4,0},{5,1},{6,2},{7,3},{8,12},{9,13},{10,... | collective-permute-start | bytes 196616 | tf_op jit(solution)/shard_map/ppermute | solution.py:401
  76.4 0.1 collective-permute-done.11.refs_1_
  76.5 2.0 %collective-permute-done.12.refs_2_ = f32[16,1536]{1,0:T(8,128)S(1)} collective-permute-done((f32[16,1536]{1,0:T(8,128)S(1)}, f32[16,1536]{1,0:T(8,128)S(1)}, u32[]{:S(2)}, u32[]{:S(2)}) %collective-permute-start.12) | collective-permute-done | bytes 98336 | tf_op jit(solution)/shard_map/ppermute | solution.py:400
  78.5 1.3 %collective-permute-done.13.refs_3_ = f32[16,1536]{1,0:T(8,128)S(1)} collective-permute-done((f32[16,1536]{1,0:T(8,128)S(1)}, f32[16,1536]{1,0:T(8,128)S(1)}, u32[]{:S(2)}, u32[]{:S(2)}) %collective-permute-start.13) | collective-permute-done | bytes 98336 | tf_op jit(solution)/shard_map/ppermute | solution.py:400
  79.8 0.0 copy-start.2
  79.8 0.0 copy-start.3
  79.8 0.2 collective-permute-done.14.refs_1_
  80.0 1.6 %collective-permute-start.15 = (f32[16,1024]{1,0:T(8,128)S(1)}, f32[16,1024]{1,0:T(8,128)S(1)}, u32[]{:S(2)}, u32[]{:S(2)}) collective-permute-start(f32[16,1024]{1,0:T(8,128)S(1)} %chip_sums.5.refs_4_), channel_id=1, source_target_pairs={{0,8},{8,0},{16,24},{24,16},{1,9},{9,1},{17,25},{25,17},{2,10},{10... | collective-permute-start | bytes 196616 | tf_op jit(solution)/shard_map/ppermute | solution.py:400
  81.6 1.5 %collective-permute-start.16 = (f32[16,1024]{1,0:T(8,128)S(1)}, f32[16,1024]{1,0:T(8,128)S(1)}, u32[]{:S(2)}, u32[]{:S(2)}) collective-permute-start(f32[16,1024]{1,0:T(8,128)S(1)} %chip_sums.5.refs_4_), channel_id=1, source_target_pairs={{0,16},{8,24},{16,0},{24,8},{1,17},{9,25},{17,1},{25,9},{2,18},{10... | collective-permute-start | bytes 196616 | tf_op jit(solution)/shard_map/ppermute | solution.py:400
  83.0 0.5 collective-permute-start.17
  83.6 0.0 all-to-all-done.recv_ref
  83.6 0.0 copy-done.2
  83.6 0.0 copy-done.3
  83.6 2.4 %table_part.1 = (f32[512,512]{1,0:T(8,128)}, f32[512]{0:T(512)}) custom-call(f32[32,72,128]{2,1,0:T(8,128)S(1)} %all-to-all-done.recv_ref, f32[512,512]{1,0:T(8,128)S(1)} %copy-done.2, f32[512]{0:T(512)S(1)} %copy-done.3), custom_call_target="tpu_custom_call" | custom-call | flops 1000000000 | bytes 65536 | tf_op jit(solution)/shard_map/table_part/pallas_call | solution.py:382
  85.9 2.3 %collective-permute-done.17.refs_7_ = f32[16,1024]{1,0:T(8,128)S(1)} collective-permute-done((f32[16,1024]{1,0:T(8,128)S(1)}, f32[16,1024]{1,0:T(8,128)S(1)}, u32[]{:S(2)}, u32[]{:S(2)}) %collective-permute-start.17) | collective-permute-done | bytes 65568 | tf_op jit(solution)/shard_map/ppermute | solution.py:400
  88.2 0.0 collective-permute-done.15.refs_5_
  88.2 0.0 collective-permute-done.16.refs_6_
  88.2 0.9 %gather.1 = (f32[4,16,2048]{2,1,0:T(8,128)}, f32[4,16,512]{2,1,0:T(8,128)}) custom-call(f32[16,1536]{1,0:T(8,128)S(1)} %get-tuple-element.86.refs_0_, f32[16,1536]{1,0:T(8,128)S(1)} %collective-permute-done.11.refs_1_, f32[16,1536]{1,0:T(8,128)S(1)} %collective-permute-done.12.refs_2_, f32[16,1536]{1,0:T(8,128)S(1)} %collective-permute-done.13.refs_3_, ...), custom_call_target="tpu_custom_call" | custom-call | flops 1000000000 | bytes 65536 | tf_op jit(solution)/shard_map/gather/pallas_call | solution.py:382
  (3 shorter events, 0.1 us)
Async XLA Ops:
  9.5 3.6 %collective-permute-start = (f32[256,1536]{1,0:T(8,128)S(1)}, f32[256,1536]{1,0:T(8,128)S(1)}, u32[]{:S(2)}, u32[]{:S(2)}) collective-permute-start(f32[256,1536]{1,0:T(8,128)S(1)} %get-tuple-element.51), channel_id=1, source_target_pairs={{0,1},{1,0},{2,3},{3,2},{4,5},{5,4},{6,7},{7,6},{8,9},{9,8},{10,11... | collective-permute-start | bytes 4718600 | tf_op jit(solution)/shard_map/ppermute | solution.py:430
  13.3 7.1 %copy-start = (s32[1,32,16]{1,2,0:T(8,128)S(1)}, s32[1,32,16]{1,2,0:T(8,128)}, u32[]{:S(2)}) copy-start(s32[1,32,16]{1,2,0:T(8,128)} %param.14) | copy-start | bytes 6148
  13.3 7.1 %copy-start.1 = (s32[1,512]{1,0:T(1,128)S(1)}, s32[1,512]{1,0:T(1,128)}, u32[]{:S(2)}) copy-start(s32[1,512]{1,0:T(1,128)} %slot_ref.1) | copy-start | bytes 6148
  15.8 14.2 %collective-permute-start.3 = (f32[256,1024]{1,0:T(8,128)S(1)}, f32[256,1024]{1,0:T(8,128)S(1)}, u32[]{:S(2)}, u32[]{:S(2)}) collective-permute-start(f32[256,1024]{1,0:T(8,128)S(1)} %get-tuple-element.69), channel_id=1, source_target_pairs={{0,1},{1,0},{2,3},{3,2},{4,5},{5,4},{6,7},{7,6},{8,9},{9,8},{10,11... | collective-permute-start | bytes 3145736 | tf_op jit(solution)/shard_map/ppermute | solution.py:442
  16.2 12.3 %collective-permute-start.1 = (f32[2,64,768]{2,1,0:T(8,128)S(1)}, f32[2,64,768]{2,1,0:T(8,128)S(1)}, u32[]{:S(2)}, u32[]{:S(2)}) collective-permute-start(f32[2,64,768]{2,1,0:T(8,128)S(1)} %get-tuple-element.61), channel_id=1, source_target_pairs={{0,8},{8,0},{16,24},{24,16},{1,9},{9,1},{17,25},{25,17},{2,10},{10... | collective-permute-start | bytes 1179656 | tf_op jit(solution)/shard_map/ppermute | solution.py:400
  18.8 11.1 %collective-permute-start.2 = (f32[2,64,768]{2,1,0:T(8,128)S(1)}, f32[2,64,768]{2,1,0:T(8,128)S(1)}, u32[]{:S(2)}, u32[]{:S(2)}) collective-permute-start(f32[2,64,768]{2,1,0:T(8,128)S(1)} %get-tuple-element.62), channel_id=1, source_target_pairs={{0,16},{8,24},{16,0},{24,8},{1,17},{9,25},{17,1},{25,9},{2,18},{10... | collective-permute-start | bytes 1179656 | tf_op jit(solution)/shard_map/ppermute | solution.py:400
  31.0 14.8 %collective-permute-start.4 = (f32[64,1792]{1,0:T(8,128)S(1)}, f32[64,1792]{1,0:T(8,128)S(1)}, u32[]{:S(2)}, u32[]{:S(2)}) collective-permute-start(f32[64,1792]{1,0:T(8,128)S(1)} %get-tuple-element.72), channel_id=1, source_target_pairs={{0,8},{8,0},{16,24},{24,16},{1,9},{9,1},{17,25},{25,17},{2,10},{10... | collective-permute-start | bytes 1376264 | tf_op jit(solution)/shard_map/ppermute | solution.py:400
  31.3 15.7 %collective-permute-start.5 = (f32[64,1792]{1,0:T(8,128)S(1)}, f32[64,1792]{1,0:T(8,128)S(1)}, u32[]{:S(2)}, u32[]{:S(2)}) collective-permute-start(f32[64,1792]{1,0:T(8,128)S(1)} %get-tuple-element.73), channel_id=1, source_target_pairs={{0,16},{8,24},{16,0},{24,8},{1,17},{9,25},{17,1},{25,9},{2,18},{10... | collective-permute-start | bytes 1376264 | tf_op jit(solution)/shard_map/ppermute | solution.py:400
  33.0 50.5 %all-to-all-start = ((f32[32,72,128]{2,1,0:T(8,128)}), f32[32,72,128]{2,1,0:T(8,128)S(1)}, u32[]{:S(2)}, u32[]{:S(2)}) async-start(f32[32,72,128]{2,1,0:T(8,128)} %events_part.1), calls=%async_computation | async-start | bytes 2359296 | tf_op jit(solution)/shard_map/all_to_all | solution.py:453
  48.3 13.6 %collective-permute-start.6 = (f32[2,16,1536]{2,1,0:T(8,128)S(1)}, f32[2,16,1536]{2,1,0:T(8,128)S(1)}, u32[]{:S(2)}, u32[]{:S(2)}) collective-permute-start(f32[2,16,1536]{2,1,0:T(8,128)S(1)} %get-tuple-element.77), channel_id=1, source_target_pairs={{0,2},{1,3},{2,0},{3,1},{4,6},{5,7},{6,4},{7,5},{8,10},{9,11},{10,... | collective-permute-start | bytes 589832 | tf_op jit(solution)/shard_map/ppermute | solution.py:401
  51.5 6.1 %collective-permute-start.7 = (f32[4,16,512]{2,1,0:T(8,128)S(1)}, f32[4,16,512]{2,1,0:T(8,128)S(1)}, u32[]{:S(2)}, u32[]{:S(2)}) collective-permute-start(f32[4,16,512]{2,1,0:T(8,128)S(1)} %get-tuple-element.80), channel_id=1, source_target_pairs={{0,8},{8,0},{16,24},{24,16},{1,9},{9,1},{17,25},{25,17},{2,10},{10... | collective-permute-start | bytes 393224 | tf_op jit(solution)/shard_map/ppermute | solution.py:400
  54.1 5.7 %collective-permute-start.8 = (f32[4,16,512]{2,1,0:T(8,128)S(1)}, f32[4,16,512]{2,1,0:T(8,128)S(1)}, u32[]{:S(2)}, u32[]{:S(2)}) collective-permute-start(f32[4,16,512]{2,1,0:T(8,128)S(1)} %get-tuple-element.81), channel_id=1, source_target_pairs={{0,16},{8,24},{16,0},{24,8},{1,17},{9,25},{17,1},{25,9},{2,18},{10... | collective-permute-start | bytes 393224 | tf_op jit(solution)/shard_map/ppermute | solution.py:400
  61.9 9.3 %collective-permute-start.10 = (f32[2,16,1024]{2,1,0:T(8,128)S(1)}, f32[2,16,1024]{2,1,0:T(8,128)S(1)}, u32[]{:S(2)}, u32[]{:S(2)}) collective-permute-start(f32[2,16,1024]{2,1,0:T(8,128)S(1)} %get-tuple-element.85), channel_id=1, source_target_pairs={{0,2},{1,3},{2,0},{3,1},{4,6},{5,7},{6,4},{7,5},{8,10},{9,11},{10,... | collective-permute-start | bytes 393224 | tf_op jit(solution)/shard_map/ppermute | solution.py:401
  64.5 5.8 %collective-permute-start.9 = (f32[1,16,1536]{2,1,0:T(8,128)S(1)}, f32[1,16,1536]{2,1,0:T(8,128)S(1)}, u32[]{:S(2)}, u32[]{:S(2)}) collective-permute-start(f32[1,16,1536]{2,1,0:T(8,128)S(1)} %get-tuple-element.83), channel_id=1, source_target_pairs={{0,4},{1,5},{2,6},{3,7},{4,0},{5,1},{6,2},{7,3},{8,12},{9,13},{10,... | collective-permute-start | bytes 294920 | tf_op jit(solution)/shard_map/ppermute | solution.py:401
  71.3 5.2 %collective-permute-start.11 = (f32[16,1536]{1,0:T(8,128)S(1)}, f32[16,1536]{1,0:T(8,128)S(1)}, u32[]{:S(2)}, u32[]{:S(2)}) collective-permute-start(f32[16,1536]{1,0:T(8,128)S(1)} %get-tuple-element.86.refs_0_), channel_id=1, source_target_pairs={{0,8},{8,0},{16,24},{24,16},{1,9},{9,1},{17,25},{25,17},{2,10},{10... | collective-permute-start | bytes 294920 | tf_op jit(solution)/shard_map/ppermute | solution.py:400
  72.8 5.7 %collective-permute-start.12 = (f32[16,1536]{1,0:T(8,128)S(1)}, f32[16,1536]{1,0:T(8,128)S(1)}, u32[]{:S(2)}, u32[]{:S(2)}) collective-permute-start(f32[16,1536]{1,0:T(8,128)S(1)} %get-tuple-element.86.refs_0_), channel_id=1, source_target_pairs={{0,16},{8,24},{16,0},{24,8},{1,17},{9,25},{17,1},{25,9},{2,18},{10... | collective-permute-start | bytes 294920 | tf_op jit(solution)/shard_map/ppermute | solution.py:400
  74.3 5.5 %collective-permute-start.13 = (f32[16,1536]{1,0:T(8,128)S(1)}, f32[16,1536]{1,0:T(8,128)S(1)}, u32[]{:S(2)}, u32[]{:S(2)}) collective-permute-start(f32[16,1536]{1,0:T(8,128)S(1)} %get-tuple-element.86.refs_0_), channel_id=1, source_target_pairs={{0,24},{8,16},{16,8},{24,0},{1,25},{9,17},{17,9},{25,1},{2,26},{10... | collective-permute-start | bytes 294920 | tf_op jit(solution)/shard_map/ppermute | solution.py:400
  74.8 5.2 %collective-permute-start.14 = (f32[1,16,1024]{2,1,0:T(8,128)S(1)}, f32[1,16,1024]{2,1,0:T(8,128)S(1)}, u32[]{:S(2)}, u32[]{:S(2)}) collective-permute-start(f32[1,16,1024]{2,1,0:T(8,128)S(1)} %get-tuple-element.89), channel_id=1, source_target_pairs={{0,4},{1,5},{2,6},{3,7},{4,0},{5,1},{6,2},{7,3},{8,12},{9,13},{10,... | collective-permute-start | bytes 196616 | tf_op jit(solution)/shard_map/ppermute | solution.py:401
  79.8 3.7 %copy-start.2 = (f32[512,512]{1,0:T(8,128)S(1)}, f32[512,512]{1,0:T(8,128)}, u32[]{:S(2)}) copy-start(f32[512,512]{1,0:T(8,128)} %table_ref.1) | copy-start | bytes 3145732
  79.8 3.7 %copy-start.3 = (f32[512]{0:T(512)S(1)}, f32[512]{0:T(512)}, u32[]{:S(2)}) copy-start(f32[512]{0:T(512)} %accum_ref.1) | copy-start | bytes 6148
  80.0 8.2 %collective-permute-start.15 = (f32[16,1024]{1,0:T(8,128)S(1)}, f32[16,1024]{1,0:T(8,128)S(1)}, u32[]{:S(2)}, u32[]{:S(2)}) collective-permute-start(f32[16,1024]{1,0:T(8,128)S(1)} %chip_sums.5.refs_4_), channel_id=1, source_target_pairs={{0,8},{8,0},{16,24},{24,16},{1,9},{9,1},{17,25},{25,17},{2,10},{10... | collective-permute-start | bytes 196616 | tf_op jit(solution)/shard_map/ppermute | solution.py:400
  81.6 6.6 %collective-permute-start.16 = (f32[16,1024]{1,0:T(8,128)S(1)}, f32[16,1024]{1,0:T(8,128)S(1)}, u32[]{:S(2)}, u32[]{:S(2)}) collective-permute-start(f32[16,1024]{1,0:T(8,128)S(1)} %chip_sums.5.refs_4_), channel_id=1, source_target_pairs={{0,16},{8,24},{16,0},{24,8},{1,17},{9,25},{17,1},{25,9},{2,18},{10... | collective-permute-start | bytes 196616 | tf_op jit(solution)/shard_map/ppermute | solution.py:400
  83.0 5.2 %collective-permute-start.17 = (f32[16,1024]{1,0:T(8,128)S(1)}, f32[16,1024]{1,0:T(8,128)S(1)}, u32[]{:S(2)}, u32[]{:S(2)}) collective-permute-start(f32[16,1024]{1,0:T(8,128)S(1)} %chip_sums.5.refs_4_), channel_id=1, source_target_pairs={{0,24},{8,16},{16,8},{24,0},{1,25},{9,17},{17,9},{25,1},{2,26},{10... | collective-permute-start | bytes 196616 | tf_op jit(solution)/shard_map/ppermute | solution.py:400

commit v9 on v1

--- a/solution.py
+++ b/solution.py
@@ -14,7 +14,7 @@
 learning_rate = 0.1
 
 f32, bf16 = jnp.float32, jnp.bfloat16
-VMEM_BYTES = 32 * 1024 * 1024
+MIB = 1024 * 1024
 STEP = 256
 LANES = 128
 ID_ROWS = 8
@@ -252,6 +252,72 @@
     table_new_ref[...] = table_ref[...] - learning_rate * grad / (jnp.sqrt(accum_new) + adagrad_eps)
 
 
+def place_on_dp():
+    d = lax.axis_index("dp")
+    return lax.rem(d, 2), d // 2
+
+
+def first_kernel(keep1_ref, recv1_ref, keep2_ref, recv2_ref, to_x_ref, to_y_ref, keep_a_ref, keep_b_ref):
+    x, y = place_on_dp()
+    start = 0
+    for keep_ref, recv_ref in ((keep1_ref, recv1_ref), (keep2_ref, recv2_ref)):
+        half = keep_ref.shape[-1] // 2
+        part = lambda i, j, cols: keep_ref[i, j, :, cols] + recv_ref[i, j, :, cols]
+        lo, hi, out = slice(0, half), slice(half, 2 * half), slice(start, start + half)
+        for s in range(2):
+            to_x_ref[s, :, out] = part(s, 1 - x, lo)
+            to_y_ref[s, :, out] = part(1 - y, s, hi)
+            keep_a_ref[s, :, out] = part(s, x, lo)
+            keep_b_ref[s, :, out] = part(y, s, hi)
+        start += half
+
+
+def second_kernel(keep_a_ref, from_x_ref, keep_b_ref, from_y_ref, to_y_ref, to_x_ref, next_a_ref, next_b_ref):
+    x, y = place_on_dp()
+    to_y_ref[...] = keep_a_ref[1 - y] + from_x_ref[1 - y]
+    to_x_ref[...] = keep_b_ref[1 - x] + from_y_ref[1 - x]
+    next_a_ref[...] = keep_a_ref[y] + from_x_ref[y]
+    next_b_ref[...] = keep_b_ref[x] + from_y_ref[x]
+
+
+def chip_bit(bit):
+    return (lax.axis_index("rows") // 2) // (1 << bit) % 2
+
+
+def halve(bit, send_ref, keep_ref, block):
+    mine = chip_bit(bit)
+    for i in range(send_ref.shape[0]):
+        send_ref[i] = block(2 * i + 1 - mine)
+        keep_ref[i] = block(2 * i + mine)
+
+
+def chip_first_kernel(next_a_ref, from_y_ref, next_b_ref, from_x_ref, send_ref, keep_ref):
+    halve(0, send_ref, keep_ref, lambda at: jnp.concatenate(
+        [next_a_ref[at] + from_y_ref[at], next_b_ref[at] + from_x_ref[at]], axis=1))
+
+
+def chip_kernel(bit, keep_in, recv_in, send_ref, keep_ref):
+    halve(bit, send_ref, keep_ref, lambda at: keep_in[at] + recv_in[at])
+
+
+def total_kernel(tokens, keep_ref, recv_ref, out_ref):
+    out_ref[...] = (keep_ref[0] + recv_ref[0]) * (1.0 / tokens)
+
+
+def gather_kernel(*refs):
+    *pieces, grad_in_ref, grad_out_ref = refs
+    d = lax.axis_index("dp")
+    width = grad_out_ref.shape[-1]
+    half = width // 2
+    for k, piece in enumerate(pieces):
+        at = jnp.bitwise_xor(d, k)
+        grad_out_ref[at] = piece[:, :width]
+        start = width
+        for cols, first in ((half, 0), (width, 2 * width), (half, half), (width, width), (width, 3 * width)):
+            grad_in_ref[at, :, first:first + cols] = piece[:, start:start + cols]
+            start += cols
+
+
 def vmem():
     return pl.BlockSpec(memory_space=pltpu.VMEM)
 
@@ -260,18 +326,19 @@
     return jax.ShapeDtypeStruct(dims, dtype)
 
 
-def call(kernel, name, out_shape, args, scalars=0, scratch=(), flops=0, far=0):
+def call(kernel, name, out_shape, args, scalars=0, scratch=(), far=0, long=False, grant=4, apart=(), either=()):
     place = [None] * scalars + [pltpu.HBM] * far + [pltpu.VMEM] * (len(args) - scalars - far)
-    args = [a if p is None else pltpu.with_memory_space_constraint(a, p) for a, p in zip(args, place)]
+    held = [None if i in either else pltpu.HBM if i in apart else p for i, p in enumerate(place)]
+    args = [a if p is None else pltpu.with_memory_space_constraint(a, p) for a, p in zip(args, held)]
     return pl.pallas_call(
         kernel,
         name=name,
         in_specs=[pl.BlockSpec(memory_space=p or pltpu.SMEM) for p in place],
         out_specs=[vmem()] * len(out_shape),
-        out_shape=out_shape,
+        out_shape=list(out_shape),
         scratch_shapes=[pltpu.VMEM(dims, dtype) for dims, dtype in scratch] + [pltpu.SemaphoreType.DMA((7,))] * (far > 0),
-        compiler_params=pltpu.CompilerParams(vmem_limit_bytes=VMEM_BYTES),
-        cost_estimate=pl.CostEstimate(flops=flops, bytes_accessed=1 << 20, transcendentals=0),
+        compiler_params=pltpu.CompilerParams(vmem_limit_bytes=grant * MIB),
+        cost_estimate=pl.CostEstimate(flops=100_000_000_000 if long else 1_000_000_000, bytes_accessed=1 << 16, transcendentals=0),
     )(*args)
 
 
@@ -281,24 +348,18 @@
     chips = rows_size // 2
     piece = width // (rows_size * dp_size)
     cores = [(i, i ^ 1) for i in range(rows_size)]
-    lines = [list(range(c, rows_size, 2)) for c in range(2)]
-
-    def exchange(v, axis, groups=None):
-        return lax.all_to_all(v, axis, split_axis=0, concat_axis=0, axis_index_groups=groups, tiled=True)
-
-    def after(value, *others):
-        return lax.optimization_barrier((value, *others))[0]
-
-    def over_dp(both):
-        return exchange(both.reshape(dp_size, chips * piece, both.shape[1]), "dp")
-
-    def over_chips(parts):
-        return exchange(jnp.sum(parts, axis=0).reshape(chips, piece, -1), "rows", lines)
-
-    def gathered(parts):
-        part = jnp.sum(parts, axis=0) * (1.0 / tokens)
-        return exchange(jnp.broadcast_to(part, (dp_size, *part.shape)), "dp").reshape(dp_size * piece, -1)
-
+    over_dp = lambda v, bit: lax.ppermute(v, "dp", [(i, i ^ bit) for i in range(dp_size)])
+    over_chips = lambda v, bit: lax.ppermute(v, "rows", [(i, i ^ (2 << bit)) for i in range(rows_size)])
+    after = lambda value, *others: lax.optimization_barrier((value, *others))[0]
+    strip = chips * piece
+
+    def gathered(total):
+        return [total] + [over_dp(total, k) for k in range(1, dp_size)]
+
+    by_dp = lambda v: v.reshape(2, 2, strip, v.shape[-1])
+    by_chip = lambda v: v.reshape(*v.shape[:-2], chips, piece, v.shape[-1])
+    bits = chips.bit_length() - 1
+    far_off = lambda *dims, dtype=f32: pltpu.HBM(dims, dtype)
     local = lambda *dims, dtype=f32: pltpu.VMEM(dims, dtype)
     sides = lambda cols: [local(width // 2, cols)] * 2
     keep1, send1, hid, dsilu, gatt, gpre_uv, normed_t, events, cotangent, w_in = call(
@@ -316,35 +377,46 @@
         (lengths, events, cotangent, w_in, w_out), 1,
         [((tokens, width), bf16), ((tokens, width), bf16), ((tokens, width), f32), ((tokens, width), f32),
          ((tokens, width), bf16), ((tokens, width), bf16), ((tokens, width), f32), ((HEADS, tokens, tokens), bf16),
-         (w_out.shape, bf16)],
-        flops=100_000_000_000, far=4)
+         (w_out.shape, bf16)], far=4, long=True, grant=16)
     recv1 = lax.ppermute(send1, "rows", cores)
     keep2, send2, gpre_qk = call(
         attention_kernel, "attention_part", sides(2 * width) + [local(tokens, 2 * width, dtype=bf16)],
-        (lengths, hid, dsilu, gatt, normed_t), 1, flops=100_000_000_000)
+        (lengths, hid, dsilu, gatt, normed_t), 1, long=True, grant=10)
     recv2 = lax.ppermute(send2, "rows", cores)
     pay_rows = capacity * (width // LANES) + ID_ROWS
-    both1 = keep1 + recv1
-    gpre_uv = after(gpre_uv, both1)
-    parts1 = over_dp(both1)
     (send,) = call(
         events_kernel, "events_part", [local(owners, pay_rows, LANES)],
         (lengths, events, cotangent, w_in, event_slot, slot_row[0].T, gpre_uv, gpre_qk), 1,
-        [((tokens, width), bf16), ((tokens, width), bf16), ((owners * capacity, width), f32)], flops=100_000_000_000)
-    recv = exchange(send, ("dp", "rows"))
-    both2 = after(keep2, send) + recv2
-    parts2 = over_dp(both2)
-    parts1 = over_chips(after(parts1, both2))
-    parts2 = over_chips(after(parts2, parts1))
-    first = gathered(parts1)
-    second = gathered(parts2)
-    grad_in = jnp.concatenate([first[:, width:], second], axis=1)
+        [((tokens, width), bf16), ((tokens, width), bf16), ((owners * capacity, width), f32)], grant=10)
+    cols = w_in.shape[1] + width
+    to_x, to_y, keep_a, keep_b = call(
+        first_kernel, "first_sums", [local(2, strip, cols // 2)] * 2 + [far_off(2, strip, cols // 2)] * 2,
+        [by_dp(v) for v in (after(keep1, send), recv1, keep2, recv2)])
+    recv = lax.all_to_all(after(send, to_x, to_y), ("dp", "rows"), split_axis=0, concat_axis=0, tiled=True)
+    from_x, from_y = over_dp(to_x, 1), over_dp(to_y, 2)
+    to_y, to_x, next_a, next_b = call(
+        second_kernel, "second_sums", [local(strip, cols // 2)] * 4, (keep_a, from_x, keep_b, from_y),
+        long=True, grant=10, apart=(0, 2), either=(1, 3))
+    from_y, from_x = over_dp(to_y, 2), over_dp(to_x, 1)
+    send, keep = call(
+        chip_first_kernel, "chip_sums", [local(chips // 2, piece, cols)] * 2,
+        [by_chip(v) for v in (next_a, from_y, next_b, from_x)])
+    for bit in range(1, bits):
+        send, keep = call(
+            functools.partial(chip_kernel, bit), "chip_sums", [local(chips >> (bit + 1), piece, cols)] * 2,
+            (keep, over_chips(send, bit - 1)))
+    (total,) = call(
+        functools.partial(total_kernel, tokens), "total", [local(piece, cols)], (keep, over_chips(send, bits - 1)))
+    pieces = gathered(total)
     slots = owners * capacity
     table_new, accum_new = call(
         table_kernel, "table_part", [shape(*item_table.shape), shape(*accumulator.shape)],
         (recv, item_table, accumulator), 0,
-        [((slots, width), f32), ((slots, width), bf16), ((slots, width), bf16)], flops=10_000_000_000)
-    return grad_in, first[:, :width], table_new, accum_new
+        [((slots, width), f32), ((slots, width), bf16), ((slots, width), bf16)], grant=10)
+    pieces[-1] = after(pieces[-1], accum_new)
+    grad_in, grad_out = call(
+        gather_kernel, "gather", [shape(dp_size, piece, 4 * width), shape(dp_size, piece, width)], pieces)
+    return grad_in.reshape(-1, 4 * width), grad_out.reshape(-1, width), table_new, accum_new
 
 
 def solution(mesh):

time: 140 us -> 85.4 us (0.61)
  blocking collectives: 26.6 us -> 0 us
  waiting for transfers between devices: 60.8 us -> 43 us
  local copies, waits for them, and re-layouts: 7.11 us -> 0.01 us
  other arithmetic: 6.19 us -> 0 us
  Pallas kernels: 18 us -> 22.1 us
    all_to_all x5 -> x1, waiting for transfers between devices: 60.8 us -> 0.01 us  [body(): lax.all_to_all(after(send, to_x, to_y), ('dp', 'rows'), split_axis=0, con...]
    ppermute x0 -> x9, waiting for transfers between devices: none -> 43 us  [the longest x7 29.4 us: body(): lax.ppermute(v, 'dp', [(i, i ^ bit) for i in range(dp_size)])]
    all_to_all x2 -> x0, blocking collectives: 26.6 us -> none  [exchange(): lax.all_to_all(v, axis, split_axis=0, concat_axis=0, axis_index_groups=gr...]
    all_to_all x5 -> x1, starting transfers between devices: 18.6 us -> 3.97 us  [body(): lax.all_to_all(after(send, to_x, to_y), ('dp', 'rows'), split_axis=0, con...]
    ppermute x0 -> x9, starting transfers between devices: none -> 14.1 us  [the longest x7 10.7 us: body(): lax.ppermute(v, 'dp', [(i, i ^ bit) for i in range(dp_size)])]
    unnamed x24 -> x8, local copies, waits for them, and re-layouts: 4.93 us -> 0.01 us
    pallas_call x4 -> x10, Pallas kernels: 18 us -> 22.1 us  [call(): pl.pallas_call(kernel, name=name, in_specs=[pl.BlockSpec(memory_space=p o...]
    add x2 -> x0, other arithmetic: 3.7 us -> none  [the longest x1 2.33 us: body(): both2 = after(keep2, send) + recv2]
  transfers between devices with their start and end apart: 7 -> 12, of which waited for: 5 -> 8; matrix products, arithmetic and copies ran while one was open for 3% -> 0% of each run, Pallas kernels for 7% -> 13%
where the time goes in v9:
time: 85.4 us; the launch traced here: 85.2 us
  waiting for transfers between devices  43 us (50%)
  Pallas kernels  22.1 us (26%)
  starting transfers between devices  18.7 us (22%)
  between operations  1.34 us (2%)
    ppermute x7, waiting for transfers between devices, body(): lax.ppermute(v, 'dp', [(i, i ^ bit) for i in range(dp_size)])  29.4 us
    pallas_call x10, Pallas kernels, call(): pl.pallas_call(kernel, name=name, in_specs=[pl.BlockSpec(memory_space=p o...  22.1 us
    ppermute x2, waiting for transfers between devices, body(): lax.ppermute(v, 'rows', [(i, i ^ 2 << bit) for i in range(rows_size)])  13.5 us
    ppermute x7, starting transfers between devices, body(): lax.ppermute(v, 'dp', [(i, i ^ bit) for i in range(dp_size)])  10.7 us
    all_to_all x1, starting transfers between devices, body(): lax.all_to_all(after(send, to_x, to_y), ('dp', 'rows'), split_axis=0, con...  3.97 us
    ppermute x2, starting transfers between devices, body(): lax.ppermute(v, 'rows', [(i, i ^ 2 << bit) for i in range(rows_size)])  3.39 us
  transfers between devices with their start and end apart: 12, of which 8 were waited for; matrix products, arithmetic and copies ran while one was open for 0% of the time, Pallas kernels for 13%

profile of v9, /device:TPU:0, one launch (start us, length us, event | category | flops | bytes accessed | tf_op | source)
XLA Modules:
  0.0 85.2 jit_solution(918720057290856494)
XLA Ops:
  1.3 8.3 %forward_part.1 = (f32[256,1536]{1,0:T(8,128)S(1)}, f32[256,1536]{1,0:T(8,128)S(1)}, bf16[512,1536]{1,0:T(8,128)(2,1)S(1)}, bf16[512,1024]{1,0:T(8,128)(2,1)S(1)...) custom-call(s32[1]{0:T(128)S(6)} %copy.13.len_ref, ...), custom_call_target="tpu_custom_call" | custom-call | flops 99999997952 | bytes 65536 | tf_op jit(solution)/shard_map/forward_part/pallas_call | solution.py:333
  9.5 0.5 collective-permute-start
  10.1 0.0 copy-start
  10.1 0.0 copy-start.1
  10.1 4.1 %attention_part.1 = (f32[256,1024]{1,0:T(8,128)S(1)}, f32[256,1024]{1,0:T(8,128)S(1)}, bf16[512,1024]{1,0:T(8,128)(2,1)S(1)}) custom-call(s32[1]{0:T(128)S(6)} %copy.13.len_ref, bf16[512,1536]{1,0:T(8,128)(2,1)S(1)} %get-tuple-element.41.hid_ref, bf16[512,1024]{1,0:T(8,128)(2,1)S(1)} %get-tuple-element.42.dsilu_ref, ...), custom_call_target="tpu_custom_call" | custom-call | flops 99999997952 | bytes 65536 | tf_op jit(solution)/shard_map/attention_part/pallas_call | solution.py:333
  14.2 0.1 collective-permute-start.1
  14.3 0.0 copy-done
  14.3 0.0 copy-done.1
  14.3 3.4 %events_part.1 = f32[32,72,128]{2,1,0:T(8,128)} custom-call(s32[1]{0:T(128)S(6)} %copy.13.len_ref, bf16[512,512]{1,0:T(8,128)(2,1)S(1)} %get-tuple-element.37.ev_ref, bf16[512,512]{1,0:T(8,128)(2,1)S(1)} %get-tuple-element.38.cot_ref, bf16[512,2048]{1,0:T(8,128)(2,1)S(1)} %get-tuple-element.39.win_ref, s32[1,512]{1,0:T(1,128)S(1)} %copy-done.1, ...), custom_call_target="tpu_custom_call" | custom-call | flops 1000000000 | bytes 65536 | tf_op jit(solution)/shard_map/events_part/pallas_call | solution.py:333
  17.7 0.0 collective-permute-done.1
  17.7 0.0 collective-permute-done
  17.7 1.5 %first_sums.1 = (f32[2,64,1280]{2,1,0:T(8,128)}, f32[2,64,1280]{2,1,0:T(8,128)S(1)}, f32[2,64,1280]{2,1,0:T(8,128)}, f32[2,64,1280]{2,1,0:T(8,128)}) custom-call(f32[2,2,64,1536]{3,2,1,0:T(8,128)S(1)} %bitcast.13, f32[2,2,64,1536]{3,2,1,0:T(8,128)S(1)} %bitcast.14, f32[2,2,64,1024]{3,2,1,0:T(8,128)S(1)} %bitcast.15, f32[2,2,64,1024]{3,2,1,0:T(8,128)S(1)} %bitcast.16), custom_call_target="tpu_custom_call" | custom-call | flops 1000000000 | bytes 65536 | tf_op jit(solution)/shard_map/first_sums/pallas_call | solution.py:333
  19.2 2.9 %collective-permute-start.2 = (f32[2,64,1280]{2,1,0:T(8,128)}, f32[2,64,1280]{2,1,0:T(8,128)S(1)}, u32[]{:S(2)}, u32[]{:S(2)}) collective-permute-start(f32[2,64,1280]{2,1,0:T(8,128)} %get-tuple-element.51), channel_id=1, source_target_pairs={{0,8},{8,0},{16,24},{24,16},{1,9},{9,1},{17,25},{25,17},{2,10},{10... | collective-permute-start | bytes 1966088 | tf_op jit(solution)/shard_map/ppermute | solution.py:351
  22.2 1.5 %collective-permute-start.3 = (f32[2,64,1280]{2,1,0:T(8,128)S(1)}, f32[2,64,1280]{2,1,0:T(8,128)S(1)}, u32[]{:S(2)}, u32[]{:S(2)}) collective-permute-start(f32[2,64,1280]{2,1,0:T(8,128)S(1)} %get-tuple-element.53), channel_id=1, source_target_pairs={{0,16},{8,24},{16,0},{24,8},{1,17},{9,25},{17,1},{25,9},{2,18},{10... | collective-permute-start | bytes 1966088 | tf_op jit(solution)/shard_map/ppermute | solution.py:351
  23.7 4.0 %all-to-all-start = ((f32[32,72,128]{2,1,0:T(8,128)}), f32[32,72,128]{2,1,0:T(8,128)S(1)}, u32[]{:S(2)}, u32[]{:S(2)}) async-start(f32[32,72,128]{2,1,0:T(8,128)} %events_part.1), calls=%async_computation | async-start | bytes 2359296 | tf_op jit(solution)/shard_map/all_to_all | solution.py:395
  27.7 15.4 %collective-permute-done.2.from_x_ref = f32[2,64,1280]{2,1,0:T(8,128)S(1)} collective-permute-done((f32[2,64,1280]{2,1,0:T(8,128)}, f32[2,64,1280]{2,1,0:T(8,128)S(1)}, u32[]{:S(2)}, u32[]{:S(2)}) %collective-permute-start.2) | collective-permute-done | bytes 655392 | tf_op jit(solution)/shard_map/ppermute | solution.py:351
  43.1 4.9 %collective-permute-done.3.from_y_ref = f32[2,64,1280]{2,1,0:T(8,128)S(1)} collective-permute-done((f32[2,64,1280]{2,1,0:T(8,128)S(1)}, f32[2,64,1280]{2,1,0:T(8,128)S(1)}, u32[]{:S(2)}, u32[]{:S(2)}) %collective-permute-start.3) | collective-permute-done | bytes 655392 | tf_op jit(solution)/shard_map/ppermute | solution.py:351
  47.9 1.4 %second_sums.1 = (f32[64,1280]{1,0:T(8,128)S(1)}, f32[64,1280]{1,0:T(8,128)S(1)}, f32[64,1280]{1,0:T(8,128)S(1)}, f32[64,1280]{1,0:T(8,128)S(1)}) custom-call(f32[2,64,1280]{2,1,0:T(8,128)} %get-tuple-element.50.keep_a_ref, f32[2,64,1280]{2,1,0:T(8,128)S(1)} %collective-permute-done.2.from_x_ref, f32[2,64,1280]{2,1,0:T(8,128)} %get-tuple-element.52.keep_b_ref, ...), custom_call_target="tpu_custom_call" | custom-call | flops 99999997952 | bytes 65536 | tf_op jit(solution)/shard_map/second_sums/pallas_call | solution.py:333
  49.4 2.7 %collective-permute-start.4 = (f32[64,1280]{1,0:T(8,128)S(1)}, f32[64,1280]{1,0:T(8,128)S(1)}, u32[]{:S(2)}, u32[]{:S(2)}) collective-permute-start(f32[64,1280]{1,0:T(8,128)S(1)} %get-tuple-element.55), channel_id=1, source_target_pairs={{0,16},{8,24},{16,0},{24,8},{1,17},{9,25},{17,1},{25,9},{2,18},{10... | collective-permute-start | bytes 983048 | tf_op jit(solution)/shard_map/ppermute | solution.py:351
  52.1 0.0 collective-permute-start.5
  52.1 6.2 %collective-permute-done.4 = f32[64,1280]{1,0:T(8,128)S(1)} collective-permute-done((f32[64,1280]{1,0:T(8,128)S(1)}, f32[64,1280]{1,0:T(8,128)S(1)}, u32[]{:S(2)}, u32[]{:S(2)}) %collective-permute-start.4) | collective-permute-done | bytes 327712 | tf_op jit(solution)/shard_map/ppermute | solution.py:351
  58.3 1.7 %collective-permute-done.5 = f32[64,1280]{1,0:T(8,128)S(1)} collective-permute-done((f32[64,1280]{1,0:T(8,128)S(1)}, f32[64,1280]{1,0:T(8,128)S(1)}, u32[]{:S(2)}, u32[]{:S(2)}) %collective-permute-start.5) | collective-permute-done | bytes 327712 | tf_op jit(solution)/shard_map/ppermute | solution.py:351
  60.0 0.1 chip_sums.2
  60.1 1.0 %collective-permute-start.6 = (f32[2,16,2560]{2,1,0:T(8,128)S(1)}, f32[2,16,2560]{2,1,0:T(8,128)S(1)}, u32[]{:S(2)}, u32[]{:S(2)}) collective-permute-start(f32[2,16,2560]{2,1,0:T(8,128)S(1)} %get-tuple-element.59), channel_id=1, source_target_pairs={{0,2},{1,3},{2,0},{3,1},{4,6},{5,7},{6,4},{7,5},{8,10},{9,11},{10,... | collective-permute-start | bytes 983048 | tf_op jit(solution)/shard_map/ppermute | solution.py:352
  61.1 7.9 %collective-permute-done.6.recv_in = f32[2,16,2560]{2,1,0:T(8,128)S(1)} collective-permute-done((f32[2,16,2560]{2,1,0:T(8,128)S(1)}, f32[2,16,2560]{2,1,0:T(8,128)S(1)}, u32[]{:S(2)}, u32[]{:S(2)}) %collective-permute-start.6) | collective-permute-done | bytes 327712 | tf_op jit(solution)/shard_map/ppermute | solution.py:352
  69.0 2.4 %collective-permute-start.7 = (f32[1,16,2560]{2,1,0:T(8,128)S(1)}, f32[1,16,2560]{2,1,0:T(8,128)S(1)}, u32[]{:S(2)}, u32[]{:S(2)}) collective-permute-start(f32[1,16,2560]{2,1,0:T(8,128)S(1)} %get-tuple-element.61), channel_id=1, source_target_pairs={{0,4},{1,5},{2,6},{3,7},{4,0},{5,1},{6,2},{7,3},{8,12},{9,13},{10,... | collective-permute-start | bytes 491528 | tf_op jit(solution)/shard_map/ppermute | solution.py:352
  71.4 5.7 %collective-permute-done.7.recv_ref = f32[1,16,2560]{2,1,0:T(8,128)S(1)} collective-permute-done((f32[1,16,2560]{2,1,0:T(8,128)S(1)}, f32[1,16,2560]{2,1,0:T(8,128)S(1)}, u32[]{:S(2)}, u32[]{:S(2)}) %collective-permute-start.7) | collective-permute-done | bytes 163872 | tf_op jit(solution)/shard_map/ppermute | solution.py:352
  77.0 0.0 copy-start.2
  77.0 0.0 copy-start.3
  77.1 0.1 collective-permute-start.10
  77.1 1.4 %collective-permute-start.9 = (f32[16,2560]{1,0:T(8,128)S(1)}, f32[16,2560]{1,0:T(8,128)S(1)}, u32[]{:S(2)}, u32[]{:S(2)}) collective-permute-start(f32[16,2560]{1,0:T(8,128)S(1)} %total.1.refs_0_), channel_id=1, source_target_pairs={{0,16},{8,24},{16,0},{24,8},{1,17},{9,25},{17,1},{25,9},{2,18},{10... | collective-permute-start | bytes 491528 | tf_op jit(solution)/shard_map/ppermute | solution.py:351
  78.6 2.0 %collective-permute-start.8 = (f32[16,2560]{1,0:T(8,128)S(1)}, f32[16,2560]{1,0:T(8,128)S(1)}, u32[]{:S(2)}, u32[]{:S(2)}) collective-permute-start(f32[16,2560]{1,0:T(8,128)S(1)} %total.1.refs_0_), channel_id=1, source_target_pairs={{0,8},{8,0},{16,24},{24,16},{1,9},{9,1},{17,25},{25,17},{2,10},{10... | collective-permute-start | bytes 491528 | tf_op jit(solution)/shard_map/ppermute | solution.py:351
  80.6 0.0 all-to-all-done.recv_ref
  80.6 0.0 copy-done.2
  80.6 0.0 copy-done.3
  80.6 2.4 %table_part.1 = (f32[512,512]{1,0:T(8,128)}, f32[512]{0:T(512)}) custom-call(f32[32,72,128]{2,1,0:T(8,128)S(1)} %all-to-all-done.recv_ref, f32[512,512]{1,0:T(8,128)S(1)} %copy-done.2, f32[512]{0:T(512)S(1)} %copy-done.3), custom_call_target="tpu_custom_call" | custom-call | flops 1000000000 | bytes 65536 | tf_op jit(solution)/shard_map/table_part/pallas_call | solution.py:333
  83.0 0.4 collective-permute-done.10.refs_3_
  83.5 0.8 collective-permute-done.9.refs_2_
  84.3 0.0 collective-permute-done.8.refs_1_
  84.3 0.9 %gather.1 = (f32[4,16,2048]{2,1,0:T(8,128)}, f32[4,16,512]{2,1,0:T(8,128)}) custom-call(f32[16,2560]{1,0:T(8,128)S(1)} %total.1.refs_0_, f32[16,2560]{1,0:T(8,128)S(1)} %collective-permute-done.8.refs_1_, f32[16,2560]{1,0:T(8,128)S(1)} %collective-permute-done.9.refs_2_, f32[16,2560]{1,0:T(8,128)S(1)} %collective-permute-done.10.refs_3_), custom_call_target="tpu_custom_call" | custom-call | flops 1000000000 | bytes 65536 | tf_op jit(solution)/shard_map/gather/pallas_call | solution.py:333
  (2 shorter events, 0.1 us)
Async XLA Ops:
  9.5 8.2 %collective-permute-start = (f32[256,1536]{1,0:T(8,128)S(1)}, f32[256,1536]{1,0:T(8,128)S(1)}, u32[]{:S(2)}, u32[]{:S(2)}) collective-permute-start(f32[256,1536]{1,0:T(8,128)S(1)} %get-tuple-element.47), channel_id=1, source_target_pairs={{0,1},{1,0},{2,3},{3,2},{4,5},{5,4},{6,7},{7,6},{8,9},{9,8},{10,11... | collective-permute-start | bytes 4718600 | tf_op jit(solution)/shard_map/ppermute | solution.py:381
  10.1 4.3 %copy-start = (s32[1,32,16]{1,2,0:T(8,128)S(1)}, s32[1,32,16]{1,2,0:T(8,128)}, u32[]{:S(2)}) copy-start(s32[1,32,16]{1,2,0:T(8,128)} %param.14) | copy-start | bytes 6148
  10.1 4.3 %copy-start.1 = (s32[1,512]{1,0:T(1,128)S(1)}, s32[1,512]{1,0:T(1,128)}, u32[]{:S(2)}) copy-start(s32[1,512]{1,0:T(1,128)} %slot_ref.1) | copy-start | bytes 6148
  14.2 3.5 %collective-permute-start.1 = (f32[256,1024]{1,0:T(8,128)S(1)}, f32[256,1024]{1,0:T(8,128)S(1)}, u32[]{:S(2)}, u32[]{:S(2)}) collective-permute-start(f32[256,1024]{1,0:T(8,128)S(1)} %get-tuple-element.49), channel_id=1, source_target_pairs={{0,1},{1,0},{2,3},{3,2},{4,5},{5,4},{6,7},{7,6},{8,9},{9,8},{10,11... | collective-permute-start | bytes 3145736 | tf_op jit(solution)/shard_map/ppermute | solution.py:385
  19.2 23.8 %collective-permute-start.2 = (f32[2,64,1280]{2,1,0:T(8,128)}, f32[2,64,1280]{2,1,0:T(8,128)S(1)}, u32[]{:S(2)}, u32[]{:S(2)}) collective-permute-start(f32[2,64,1280]{2,1,0:T(8,128)} %get-tuple-element.51), channel_id=1, source_target_pairs={{0,8},{8,0},{16,24},{24,16},{1,9},{9,1},{17,25},{25,17},{2,10},{10... | collective-permute-start | bytes 1966088 | tf_op jit(solution)/shard_map/ppermute | solution.py:351
  22.2 25.8 %collective-permute-start.3 = (f32[2,64,1280]{2,1,0:T(8,128)S(1)}, f32[2,64,1280]{2,1,0:T(8,128)S(1)}, u32[]{:S(2)}, u32[]{:S(2)}) collective-permute-start(f32[2,64,1280]{2,1,0:T(8,128)S(1)} %get-tuple-element.53), channel_id=1, source_target_pairs={{0,16},{8,24},{16,0},{24,8},{1,17},{9,25},{17,1},{25,9},{2,18},{10... | collective-permute-start | bytes 1966088 | tf_op jit(solution)/shard_map/ppermute | solution.py:351
  23.7 56.9 %all-to-all-start = ((f32[32,72,128]{2,1,0:T(8,128)}), f32[32,72,128]{2,1,0:T(8,128)S(1)}, u32[]{:S(2)}, u32[]{:S(2)}) async-start(f32[32,72,128]{2,1,0:T(8,128)} %events_part.1), calls=%async_computation | async-start | bytes 2359296 | tf_op jit(solution)/shard_map/all_to_all | solution.py:395
  49.4 9.0 %collective-permute-start.4 = (f32[64,1280]{1,0:T(8,128)S(1)}, f32[64,1280]{1,0:T(8,128)S(1)}, u32[]{:S(2)}, u32[]{:S(2)}) collective-permute-start(f32[64,1280]{1,0:T(8,128)S(1)} %get-tuple-element.55), channel_id=1, source_target_pairs={{0,16},{8,24},{16,0},{24,8},{1,17},{9,25},{17,1},{25,9},{2,18},{10... | collective-permute-start | bytes 983048 | tf_op jit(solution)/shard_map/ppermute | solution.py:351
  52.1 7.9 %collective-permute-start.5 = (f32[64,1280]{1,0:T(8,128)S(1)}, f32[64,1280]{1,0:T(8,128)S(1)}, u32[]{:S(2)}, u32[]{:S(2)}) collective-permute-start(f32[64,1280]{1,0:T(8,128)S(1)} %get-tuple-element.57), channel_id=1, source_target_pairs={{0,8},{8,0},{16,24},{24,16},{1,9},{9,1},{17,25},{25,17},{2,10},{10... | collective-permute-start | bytes 983048 | tf_op jit(solution)/shard_map/ppermute | solution.py:351
  60.1 8.9 %collective-permute-start.6 = (f32[2,16,2560]{2,1,0:T(8,128)S(1)}, f32[2,16,2560]{2,1,0:T(8,128)S(1)}, u32[]{:S(2)}, u32[]{:S(2)}) collective-permute-start(f32[2,16,2560]{2,1,0:T(8,128)S(1)} %get-tuple-element.59), channel_id=1, source_target_pairs={{0,2},{1,3},{2,0},{3,1},{4,6},{5,7},{6,4},{7,5},{8,10},{9,11},{10,... | collective-permute-start | bytes 983048 | tf_op jit(solution)/shard_map/ppermute | solution.py:352
  69.0 8.0 %collective-permute-start.7 = (f32[1,16,2560]{2,1,0:T(8,128)S(1)}, f32[1,16,2560]{2,1,0:T(8,128)S(1)}, u32[]{:S(2)}, u32[]{:S(2)}) collective-permute-start(f32[1,16,2560]{2,1,0:T(8,128)S(1)} %get-tuple-element.61), channel_id=1, source_target_pairs={{0,4},{1,5},{2,6},{3,7},{4,0},{5,1},{6,2},{7,3},{8,12},{9,13},{10,... | collective-permute-start | bytes 491528 | tf_op jit(solution)/shard_map/ppermute | solution.py:352
  77.0 3.6 %copy-start.2 = (f32[512,512]{1,0:T(8,128)S(1)}, f32[512,512]{1,0:T(8,128)}, u32[]{:S(2)}) copy-start(f32[512,512]{1,0:T(8,128)} %table_ref.1) | copy-start | bytes 3145732
  77.0 3.6 %copy-start.3 = (f32[512]{0:T(512)S(1)}, f32[512]{0:T(512)}, u32[]{:S(2)}) copy-start(f32[512]{0:T(512)} %accum_ref.1) | copy-start | bytes 6148
  77.1 6.4 %collective-permute-start.10 = (f32[16,2560]{1,0:T(8,128)S(1)}, f32[16,2560]{1,0:T(8,128)S(1)}, u32[]{:S(2)}, u32[]{:S(2)}) collective-permute-start(f32[16,2560]{1,0:T(8,128)S(1)} %total.1.refs_0_), channel_id=1, source_target_pairs={{0,24},{8,16},{16,8},{24,0},{1,25},{9,17},{17,9},{25,1},{2,26},{10... | collective-permute-start | bytes 491528 | tf_op jit(solution)/shard_map/ppermute | solution.py:351
  77.1 7.1 %collective-permute-start.9 = (f32[16,2560]{1,0:T(8,128)S(1)}, f32[16,2560]{1,0:T(8,128)S(1)}, u32[]{:S(2)}, u32[]{:S(2)}) collective-permute-start(f32[16,2560]{1,0:T(8,128)S(1)} %total.1.refs_0_), channel_id=1, source_target_pairs={{0,16},{8,24},{16,0},{24,8},{1,17},{9,25},{17,1},{25,9},{2,18},{10... | collective-permute-start | bytes 491528 | tf_op jit(solution)/shard_map/ppermute | solution.py:351
  78.6 5.7 %collective-permute-start.8 = (f32[16,2560]{1,0:T(8,128)S(1)}, f32[16,2560]{1,0:T(8,128)S(1)}, u32[]{:S(2)}, u32[]{:S(2)}) collective-permute-start(f32[16,2560]{1,0:T(8,128)S(1)} %total.1.refs_0_), channel_id=1, source_target_pairs={{0,8},{8,0},{16,24},{24,16},{1,9},{9,1},{17,25},{25,17},{2,10},{10... | collective-permute-start | bytes 491528 | tf_op jit(solution)/shard_map/ppermute | solution.py:351

commit v10 on v9

--- a/solution.py
+++ b/solution.py
@@ -195,8 +195,16 @@
         ref[...] = dot_nn(normed_t_ref[start:start + half, :], gpre_ref[...])
 
 
-def events_kernel(len_ref, ev_ref, cot_ref, win_ref, slot_ref, slot_row_ref, gpre_uv_ref, gpre_qk_ref,
-                  send_ref, hi_ref, lo_ref, rows_ref):
+def slots_in_order(position, capacity, dp, rows):
+    chips = rows // 2
+    owner, place = position // capacity, position % capacity
+    ahead, core, part = owner // (2 * dp), (owner // dp) % 2, owner % dp
+    chip = (lax.axis_index("rows") // 2 + ahead) % chips
+    return part * rows + chip * 2 + core, place
+
+
+def events_kernel(rows_size, dp_size, len_ref, ev_ref, cot_ref, win_ref, slot_ref, slot_row_ref, gpre_uv_ref, gpre_qk_ref, *refs):
+    *send_refs, hi_ref, lo_ref, rows_ref = refs
     tokens, width = ev_ref.shape
     capacity, owners = slot_row_ref.shape
     length = len_ref[0]
@@ -211,41 +219,92 @@
         hi_ref[rows, :] = high
         lo_ref[rows, :] = (grad - high.astype(f32)).astype(bf16)
 
-    rows_ref[...] = one_hot_rows(slot_ref[...], rows_ref.shape[0], hi_ref, lo_ref)
-    me = lax.axis_index(("dp", "rows"))
-    lane = lax.broadcasted_iota(jnp.int32, (capacity, LANES), 1)
-    place = lax.broadcasted_iota(jnp.int32, (capacity, LANES), 0) + lax.rem(me, LANES // capacity) * capacity
-    spread = jnp.where(lane == place, 1.0, 0.0).astype(bf16)
-    ids = slot_row_ref[...]
-    ids = 16.0 * dot_tn((ids // 16).astype(bf16), spread) + dot_tn((ids % 16).astype(bf16), spread)
+    slots = rows_ref.shape[0]
+    owner, place = slots_in_order(lax.broadcasted_iota(jnp.int32, (slots, 1), 0), capacity, dp_size, rows_size)
+    rows_ref[...] = one_hot_rows(slot_ref[...], owner * capacity + place, hi_ref, lo_ref)
+    owner, place = slots_in_order(lax.broadcasted_iota(jnp.int32, (1, slots), 1), capacity, dp_size, rows_size)
+    chosen = lax.broadcasted_iota(jnp.int32, (owners, slots), 0) == owner
+    mine = lax.broadcasted_iota(jnp.int32, (capacity, slots), 0) == place
+    ids = whole_numbers(slot_row_ref[...], chosen, mine)
     tiles = width // LANES
-    for o in range(owners):
-        for t in range(tiles):
-            send_ref[o, t * capacity:(t + 1) * capacity, :] = rows_ref[o * capacity:(o + 1) * capacity, t * LANES:(t + 1) * LANES]
-        send_ref[o, tiles * capacity:, :] = jnp.broadcast_to(ids[o:o + 1, :], (ID_ROWS, LANES))
-
-
-def one_hot_rows(ids, rows, hi_ref, lo_ref):
-    named = lax.broadcasted_iota(jnp.int32, (rows, ids.shape[1]), 0) == ids
-    onehot = jnp.where(named, 1.0, 0.0).astype(bf16)
+    blocks = 2 * dp_size
+    for k, send_ref in enumerate(send_refs):
+        for i in range(blocks):
+            at = (k * blocks + i) * capacity
+            for t in range(tiles):
+                send_ref[(i * tiles + t) * capacity:(i * tiles + t + 1) * capacity, :] = rows_ref[at:at + capacity, t * LANES:(t + 1) * LANES]
+        tile = k * blocks * capacity // LANES * LANES
+        send_ref[blocks * tiles * capacity:, :] = jnp.broadcast_to(ids[:, tile:tile + LANES], (ID_ROWS, LANES))
+
+
+def whole_numbers(values, chosen, mine):
+    pick = jnp.where(chosen, 1.0, 0.0).astype(bf16)
+    found = 16.0 * dot_nn((values // 16).astype(bf16), pick) + dot_nn((values % 16).astype(bf16), pick)
+    return jnp.sum(jnp.where(mine, found, 0.0), axis=0, keepdims=True)
+
+
+def id_rows(chips):
+    return max(ID_ROWS, chips)
+
+
+def by_part_kernel(dp, block, *refs):
+    ins, outs = refs[:-dp], refs[-dp:]
+    d = lax.axis_index("dp")
+    for j, out_ref in enumerate(outs):
+        part = jnp.bitwise_xor(d, j)
+        for k, in_ref in enumerate(ins):
+            for core in range(2):
+                start = pl.multiple_of((core * dp + part) * block, block)
+                out_ref[(k * 2 + core) * block:(k * 2 + core + 1) * block, :] = in_ref[pl.ds(start, block), :]
+        ids = [in_ref[2 * dp * block:2 * dp * block + 1, :] for in_ref in ins]
+        ids += [jnp.zeros((1, LANES), f32)] * (id_rows(len(ins)) - len(ins))
+        out_ref[2 * len(ins) * block:, :] = jnp.concatenate(ids, axis=0)
+
+
+def by_core_kernel(chips, block, *refs):
+    *ins, keep_ref, send_ref = refs
+    core = lax.rem(lax.axis_index("rows"), 2)
+    for out_ref, to in ((send_ref, 1 - core), (keep_ref, core)):
+        for j, in_ref in enumerate(ins):
+            for k in range(chips):
+                start = pl.multiple_of((k * 2 + to) * block, block)
+                out_ref[(j * chips + k) * block:(j * chips + k + 1) * block, :] = in_ref[pl.ds(start, block), :]
+            at = len(ins) * chips * block + j * id_rows(chips)
+            out_ref[at:at + id_rows(chips), :] = in_ref[2 * chips * block:, :]
+
+
+def one_hot_rows(ids, wanted, hi_ref, lo_ref):
+    onehot = jnp.where(wanted == ids, 1.0, 0.0).astype(bf16)
     return dot_nn(onehot, hi_ref[...]) + dot_nn(onehot, lo_ref[...])
 
 
-def table_kernel(recv_ref, table_ref, accum_ref, table_new_ref, accum_new_ref, rows_ref, hi_ref, lo_ref):
-    owners = recv_ref.shape[0]
+def table_kernel(dp, chips, keep_ref, recv_ref, table_ref, accum_ref, table_new_ref, accum_new_ref, rows_ref, hi_ref, lo_ref):
     rows, width = table_ref.shape
     tiles = width // LANES
-    capacity = (recv_ref.shape[1] - ID_ROWS) // tiles
-    for o in range(owners):
-        for t in range(tiles):
-            rows_ref[o * capacity:(o + 1) * capacity, t * LANES:(t + 1) * LANES] = recv_ref[o, t * capacity:(t + 1) * capacity, :]
-    group = LANES // capacity
-    ids = [sum(recv_ref[o, tiles * capacity:, :] for o in range(g, g + group)) for g in range(0, owners, group)]
-    ids = jnp.concatenate(ids, axis=1)[:1, :].astype(jnp.int32)
+    sources = dp * chips
+    capacity = rows_ref.shape[0] // (2 * sources)
+    count = sources * capacity
+    r = lax.axis_index("rows")
+    block = lax.rem(r, 2) * dp + lax.axis_index("dp")
+    ids = []
+    for side, ref in enumerate((keep_ref, recv_ref)):
+        for i in range(sources):
+            at = side * count + i * capacity
+            for t in range(tiles):
+                rows_ref[at:at + capacity, t * LANES:(t + 1) * LANES] = ref[(i * tiles + t) * capacity:(i * tiles + t + 1) * capacity, :]
+        values = ref[sources * tiles * capacity:, :].astype(jnp.int32)
+        position = lax.broadcasted_iota(jnp.int32, (1, count), 1)
+        source, place = position // capacity, position % capacity
+        part, ahead = source // chips, source % chips
+        lane = ahead * (2 * dp * capacity) % LANES + block * capacity + place
+        chosen = lax.broadcasted_iota(jnp.int32, (LANES, count), 0) == lane
+        mine = lax.broadcasted_iota(jnp.int32, (values.shape[0], count), 0) == part * id_rows(chips) + ahead
+        ids.append(whole_numbers(values, chosen, mine))
+    ids = jnp.concatenate(ids, axis=1).astype(jnp.int32)
     high = rows_ref[...].astype(bf16)
     hi_ref[...] = high
     lo_ref[...] = (rows_ref[...] - high.astype(f32)).astype(bf16)
-    grad = one_hot_rows(ids, rows, hi_ref, lo_ref)
+    grad = one_hot_rows(ids, lax.broadcasted_iota(jnp.int32, (rows, 1), 0), hi_ref, lo_ref)
     accum = jnp.transpose(jnp.broadcast_to(accum_ref[...].reshape(1, rows), (8, rows)))[:, :1]
     accum_new = accum + jnp.mean(grad * grad, axis=-1, keepdims=True)
     accum_new_ref[...] = jnp.transpose(jnp.broadcast_to(accum_new, (rows, LANES)))[:1, :].reshape(rows)
@@ -383,35 +442,48 @@
         attention_kernel, "attention_part", sides(2 * width) + [local(tokens, 2 * width, dtype=bf16)],
         (lengths, hid, dsilu, gatt, normed_t), 1, long=True, grant=10)
     recv2 = lax.ppermute(send2, "rows", cores)
-    pay_rows = capacity * (width // LANES) + ID_ROWS
-    (send,) = call(
-        events_kernel, "events_part", [local(owners, pay_rows, LANES)],
+    block = capacity * (width // LANES)
+    sends = call(
+        functools.partial(events_kernel, rows_size, dp_size), "events_part",
+        [local(2 * dp_size * block + ID_ROWS, LANES)] * chips,
         (lengths, events, cotangent, w_in, event_slot, slot_row[0].T, gpre_uv, gpre_qk), 1,
-        [((tokens, width), bf16), ((tokens, width), bf16), ((owners * capacity, width), f32)], grant=10)
+        [((tokens, width), bf16), ((tokens, width), bf16), ((owners * capacity, width), f32)], grant=10, long=True)
+    ahead = lambda v, k: lax.ppermute(v, "rows", [(i, (i + 2 * k) % rows_size) for i in range(rows_size)])
+    came = [sends[0]] + [ahead(sends[k], k) for k in range(1, chips)]
     cols = w_in.shape[1] + width
     to_x, to_y, keep_a, keep_b = call(
-        first_kernel, "first_sums", [local(2, strip, cols // 2)] * 2 + [far_off(2, strip, cols // 2)] * 2,
-        [by_dp(v) for v in (after(keep1, send), recv1, keep2, recv2)])
-    recv = lax.all_to_all(after(send, to_x, to_y), ("dp", "rows"), split_axis=0, concat_axis=0, tiled=True)
+        first_kernel, "first_sums", [local(2, strip, cols // 2)] * 4,
+        [by_dp(v) for v in (after(keep1, *sends), recv1, keep2, recv2)])
     from_x, from_y = over_dp(to_x, 1), over_dp(to_y, 2)
     to_y, to_x, next_a, next_b = call(
         second_kernel, "second_sums", [local(strip, cols // 2)] * 4, (keep_a, from_x, keep_b, from_y),
-        long=True, grant=10, apart=(0, 2), either=(1, 3))
+        long=True)
     from_y, from_x = over_dp(to_y, 2), over_dp(to_x, 1)
+    came[0] = after(came[0], to_y, to_x)
+    parts = call(
+        functools.partial(by_part_kernel, dp_size, block), "by_part",
+        [local(2 * chips * block + id_rows(chips), LANES)] * dp_size, came, long=True)
+    next_a = after(next_a, *parts)
     send, keep = call(
         chip_first_kernel, "chip_sums", [local(chips // 2, piece, cols)] * 2,
         [by_chip(v) for v in (next_a, from_y, next_b, from_x)])
+    parts = [parts[0]] + [over_dp(parts[k], k) for k in range(1, dp_size)]
     for bit in range(1, bits):
         send, keep = call(
             functools.partial(chip_kernel, bit), "chip_sums", [local(chips >> (bit + 1), piece, cols)] * 2,
-            (keep, over_chips(send, bit - 1)))
+            (keep, over_chips(send, bit - 1)), long=bit == 1)
     (total,) = call(
         functools.partial(total_kernel, tokens), "total", [local(piece, cols)], (keep, over_chips(send, bits - 1)))
     pieces = gathered(total)
+    parts[0] = after(parts[0], total)
+    keep, send = call(
+        functools.partial(by_core_kernel, chips, block), "by_core",
+        [local(dp_size * (chips * block + id_rows(chips)), LANES)] * 2, parts, long=True)
+    recv = lax.ppermute(send, "rows", cores)
     slots = owners * capacity
     table_new, accum_new = call(
-        table_kernel, "table_part", [shape(*item_table.shape), shape(*accumulator.shape)],
-        (recv, item_table, accumulator), 0,
+        functools.partial(table_kernel, dp_size, chips), "table_part", [shape(*item_table.shape), shape(*accumulator.shape)],
+        (keep, recv, item_table, accumulator), 0,
         [((slots, width), f32), ((slots, width), bf16), ((slots, width), bf16)], grant=10)
     pieces[-1] = after(pieces[-1], accum_new)
     grad_in, grad_out = call(

time: 85.4 us -> 81.4 us (0.953)
  waiting for transfers between devices: 43 us -> 34.9 us
  starting transfers between devices: 18.7 us -> 23.4 us
    ppermute x7 -> x10, waiting for transfers between devices: 29.4 us -> 17.1 us  [body(): lax.ppermute(v, 'dp', [(i, i ^ bit) for i in range(dp_size)])]
    ppermute x0 -> x4, starting transfers between devices: none -> 5.59 us  [the longest x3 5.52 us: body(): lax.ppermute(v, 'rows', [(i, (i + 2 * k) % rows_size) for i in range(rows...]
    ppermute x0 -> x4, waiting for transfers between devices: none -> 4.05 us  [the longest x3 4.05 us: body(): lax.ppermute(v, 'rows', [(i, (i + 2 * k) % rows_size) for i in range(rows...]
    all_to_all x1 -> x0, starting transfers between devices: 3.97 us -> none  [body(): lax.all_to_all(after(send, to_x, to_y), ('dp', 'rows'), split_axis=0, con...]
    ppermute x7 -> x10, starting transfers between devices: 10.7 us -> 13.7 us  [body(): lax.ppermute(v, 'dp', [(i, i ^ bit) for i in range(dp_size)])]
    pallas_call x10 -> x12, Pallas kernels: 22.1 us -> 21.4 us  [call(): pl.pallas_call(kernel, name=name, in_specs=[pl.BlockSpec(memory_space=p o...]
  transfers between devices with their start and end apart: 12 -> 18, of which waited for: 8 -> 9; matrix products, arithmetic and copies ran while one was open for 0% -> 0% of each run, Pallas kernels for 13% -> 12%
where the time goes in v10:
time: 81.4 us; the launch traced here: 81.2 us
  waiting for transfers between devices  34.9 us (43%)
  starting transfers between devices  23.4 us (29%)
  Pallas kernels  21.4 us (26%)
  between operations  1.41 us (2%)
    pallas_call x12, Pallas kernels, call(): pl.pallas_call(kernel, name=name, in_specs=[pl.BlockSpec(memory_space=p o...  21.4 us
    ppermute x10, waiting for transfers between devices, body(): lax.ppermute(v, 'dp', [(i, i ^ bit) for i in range(dp_size)])  17.1 us
    ppermute x10, starting transfers between devices, body(): lax.ppermute(v, 'dp', [(i, i ^ bit) for i in range(dp_size)])  13.7 us
    ppermute x2, waiting for transfers between devices, body(): lax.ppermute(v, 'rows', [(i, i ^ 2 << bit) for i in range(rows_size)])  13.7 us
    ppermute x3, starting transfers between devices, body(): lax.ppermute(v, 'rows', [(i, (i + 2 * k) % rows_size) for i in range(rows...  5.52 us
    ppermute x3, waiting for transfers between devices, body(): lax.ppermute(v, 'rows', [(i, (i + 2 * k) % rows_size) for i in range(rows...  4.05 us
    ppermute x2, starting transfers between devices, body(): lax.ppermute(v, 'rows', [(i, i ^ 2 << bit) for i in range(rows_size)])  3.53 us
  transfers between devices with their start and end apart: 18, of which 9 were waited for; matrix products, arithmetic and copies ran while one was open for 0% of the time, Pallas kernels for 12%

profile of v10, /device:TPU:0, one launch (start us, length us, event | category | flops | bytes accessed | tf_op | source)
XLA Modules:
  0.0 81.2 jit_solution(5341380907406614373)
XLA Ops:
  1.3 9.2 %forward_part.1 = (f32[256,1536]{1,0:T(8,128)S(1)}, f32[256,1536]{1,0:T(8,128)}, bf16[512,1536]{1,0:T(8,128)(2,1)S(1)}, bf16[512,1024]{1,0:T(8,128)(2,1)S(1)}, b...) custom-call(s32[1]{0:T(128)S(6)} %copy.13.len_ref, ...), custom_call_target="tpu_custom_call" | custom-call | flops 99999997952 | bytes 65536 | tf_op jit(solution)/shard_map/forward_part/pallas_call | solution.py:392
  10.5 0.5 collective-permute-start
  11.0 0.0 copy-start.1
  11.0 0.0 copy-start.2
  11.0 4.1 %attention_part.1 = (f32[256,1024]{1,0:T(8,128)S(1)}, f32[256,1024]{1,0:T(8,128)S(1)}, bf16[512,1024]{1,0:T(8,128)(2,1)S(1)}) custom-call(s32[1]{0:T(128)S(6)} %copy.13.len_ref, bf16[512,1536]{1,0:T(8,128)(2,1)S(1)} %get-tuple-element.53.hid_ref, bf16[512,1024]{1,0:T(8,128)(2,1)S(1)} %get-tuple-element.54.dsilu_ref, ...), custom_call_target="tpu_custom_call" | custom-call | flops 99999997952 | bytes 65536 | tf_op jit(solution)/shard_map/attention_part/pallas_call | solution.py:392
  15.2 0.1 collective-permute-start.1
  15.3 0.0 copy-done.1
  15.3 0.0 copy-done.2
  15.3 2.6 %events_part.1 = (f32[520,128]{1,0:T(8,128)S(1)}, f32[520,128]{1,0:T(8,128)S(1)}, f32[520,128]{1,0:T(8,128)S(1)}, f32[520,128]{1,0:T(8,128)S(1)}) custom-call(s32[1]{0:T(128)S(6)} %copy.13.len_ref, bf16[512,512]{1,0:T(8,128)(2,1)S(1)} %get-tuple-element.49.ev_ref, bf16[512,512]{1,0:T(8,128)(2,1)S(1)} %get-tuple-element.50.cot_ref, ...), custom_call_target="tpu_custom_call" | custom-call | flops 99999997952 | bytes 65536 | tf_op jit(solution)/shard_map/events_part/pallas_call | solution.py:392
  17.9 0.0 collective-permute-done.1
  17.9 0.0 collective-permute-done
  17.9 1.7 %first_sums.1 = (f32[2,64,1280]{2,1,0:T(8,128)S(1)}, f32[2,64,1280]{2,1,0:T(8,128)S(1)}, f32[2,64,1280]{2,1,0:T(8,128)S(1)}, f32[2,64,1280]{2,1,0:T(8,128)S(1)}) custom-call(f32[2,2,64,1536]{3,2,1,0:T(8,128)S(1)} %bitcast.13, f32[2,2,64,1536]{3,2,1,0:T(8,128)} %bitcast.3.recv1_ref, f32[2,2,64,1024]{3,2,1,0:T(8,128)S(1)} %bitcast.14, ...), custom_call_target="tpu_custom_call" | custom-call | flops 1000000000 | bytes 65536 | tf_op jit(solution)/shard_map/first_sums/pallas_call | solution.py:392
  19.6 3.0 %collective-permute-start.2 = (f32[2,64,1280]{2,1,0:T(8,128)S(1)}, f32[2,64,1280]{2,1,0:T(8,128)S(1)}, u32[]{:S(2)}, u32[]{:S(2)}) collective-permute-start(f32[2,64,1280]{2,1,0:T(8,128)S(1)} %get-tuple-element.67), channel_id=1, source_target_pairs={{0,8},{8,0},{16,24},{24,16},{1,9},{9,1},{17,25},{25,17},{2,10},{10... | collective-permute-start | bytes 1966088 | tf_op jit(solution)/shard_map/ppermute | solution.py:410
  22.6 1.5 %collective-permute-start.3 = (f32[2,64,1280]{2,1,0:T(8,128)S(1)}, f32[2,64,1280]{2,1,0:T(8,128)S(1)}, u32[]{:S(2)}, u32[]{:S(2)}) collective-permute-start(f32[2,64,1280]{2,1,0:T(8,128)S(1)} %get-tuple-element.69), channel_id=1, source_target_pairs={{0,16},{8,24},{16,0},{24,8},{1,17},{9,25},{17,1},{25,9},{2,18},{10... | collective-permute-start | bytes 1966088 | tf_op jit(solution)/shard_map/ppermute | solution.py:410
  24.1 1.6 %collective-permute-start.4 = (f32[520,128]{1,0:T(8,128)S(1)}, f32[520,128]{1,0:T(8,128)S(1)}, u32[]{:S(2)}, u32[]{:S(2)}) collective-permute-start(f32[520,128]{1,0:T(8,128)S(1)} %get-tuple-element.59), channel_id=1, source_target_pairs={{0,2},{1,3},{2,4},{3,5},{4,6},{5,7},{6,0},{7,1},{8,10},{9,11},{10,... | collective-permute-start | bytes 798728 | tf_op jit(solution)/shard_map/ppermute | solution.py:451
  25.7 2.6 %collective-permute-start.5 = (f32[520,128]{1,0:T(8,128)S(1)}, f32[520,128]{1,0:T(8,128)S(1)}, u32[]{:S(2)}, u32[]{:S(2)}) collective-permute-start(f32[520,128]{1,0:T(8,128)S(1)} %get-tuple-element.60), channel_id=1, source_target_pairs={{0,4},{1,5},{2,6},{3,7},{4,0},{5,1},{6,2},{7,3},{8,12},{9,13},{10,... | collective-permute-start | bytes 798728 | tf_op jit(solution)/shard_map/ppermute | solution.py:451
  28.3 1.3 %collective-permute-start.6 = (f32[520,128]{1,0:T(8,128)S(1)}, f32[520,128]{1,0:T(8,128)S(1)}, u32[]{:S(2)}, u32[]{:S(2)}) collective-permute-start(f32[520,128]{1,0:T(8,128)S(1)} %get-tuple-element.61), channel_id=1, source_target_pairs={{0,6},{1,7},{2,0},{3,1},{4,2},{5,3},{6,4},{7,5},{8,14},{9,15},{10,... | collective-permute-start | bytes 798728 | tf_op jit(solution)/shard_map/ppermute | solution.py:451
  29.6 7.9 %collective-permute-done.2.from_x_ref = f32[2,64,1280]{2,1,0:T(8,128)S(1)} collective-permute-done((f32[2,64,1280]{2,1,0:T(8,128)S(1)}, f32[2,64,1280]{2,1,0:T(8,128)S(1)}, u32[]{:S(2)}, u32[]{:S(2)}) %collective-permute-start.2) | collective-permute-done | bytes 655392 | tf_op jit(solution)/shard_map/ppermute | solution.py:410
  37.5 1.5 %collective-permute-done.3.from_y_ref = f32[2,64,1280]{2,1,0:T(8,128)S(1)} collective-permute-done((f32[2,64,1280]{2,1,0:T(8,128)S(1)}, f32[2,64,1280]{2,1,0:T(8,128)S(1)}, u32[]{:S(2)}, u32[]{:S(2)}) %collective-permute-start.3) | collective-permute-done | bytes 655392 | tf_op jit(solution)/shard_map/ppermute | solution.py:410
  39.0 0.1 second_sums.1
  39.1 1.6 %collective-permute-start.7 = (f32[64,1280]{1,0:T(8,128)S(1)}, f32[64,1280]{1,0:T(8,128)S(1)}, u32[]{:S(2)}, u32[]{:S(2)}) collective-permute-start(f32[64,1280]{1,0:T(8,128)S(1)} %get-tuple-element.71), channel_id=1, source_target_pairs={{0,16},{8,24},{16,0},{24,8},{1,17},{9,25},{17,1},{25,9},{2,18},{10... | collective-permute-start | bytes 983048 | tf_op jit(solution)/shard_map/ppermute | solution.py:410
  40.7 0.5 collective-permute-start.8
  41.2 0.0 collective-permute-done.4.refs_1_
  41.3 4.0 %collective-permute-done.5.refs_2_ = f32[520,128]{1,0:T(8,128)S(1)} collective-permute-done((f32[520,128]{1,0:T(8,128)S(1)}, f32[520,128]{1,0:T(8,128)S(1)}, u32[]{:S(2)}, u32[]{:S(2)}) %collective-permute-start.5) | collective-permute-done | bytes 266272 | tf_op jit(solution)/shard_map/ppermute | solution.py:451
  45.3 0.0 collective-permute-done.6.refs_3_
  45.3 0.1 by_part.1
  45.4 2.3 %collective-permute-done.7 = f32[64,1280]{1,0:T(8,128)S(1)} collective-permute-done((f32[64,1280]{1,0:T(8,128)S(1)}, f32[64,1280]{1,0:T(8,128)S(1)}, u32[]{:S(2)}, u32[]{:S(2)}) %collective-permute-start.7) | collective-permute-done | bytes 327712 | tf_op jit(solution)/shard_map/ppermute | solution.py:410
  47.7 1.2 %collective-permute-done.8 = f32[64,1280]{1,0:T(8,128)S(1)} collective-permute-done((f32[64,1280]{1,0:T(8,128)S(1)}, f32[64,1280]{1,0:T(8,128)S(1)}, u32[]{:S(2)}, u32[]{:S(2)}) %collective-permute-start.8) | collective-permute-done | bytes 327712 | tf_op jit(solution)/shard_map/ppermute | solution.py:410
  48.9 0.1 chip_sums.2
  49.0 2.7 %collective-permute-start.9 = (f32[2,16,2560]{2,1,0:T(8,128)S(1)}, f32[2,16,2560]{2,1,0:T(8,128)S(1)}, u32[]{:S(2)}, u32[]{:S(2)}) collective-permute-start(f32[2,16,2560]{2,1,0:T(8,128)S(1)} %get-tuple-element.81), channel_id=1, source_target_pairs={{0,2},{1,3},{2,0},{3,1},{4,6},{5,7},{6,4},{7,5},{8,10},{9,11},{10,... | collective-permute-start | bytes 983048 | tf_op jit(solution)/shard_map/ppermute | solution.py:411
  51.7 0.5 collective-permute-start.14
  52.3 0.5 collective-permute-start.15
  52.8 2.4 %collective-permute-start.16 = (f32[520,128]{1,0:T(8,128)S(1)}, f32[520,128]{1,0:T(8,128)S(1)}, u32[]{:S(2)}, u32[]{:S(2)}) collective-permute-start(f32[520,128]{1,0:T(8,128)S(1)} %get-tuple-element.77), channel_id=1, source_target_pairs={{0,24},{8,16},{16,8},{24,0},{1,25},{9,17},{17,9},{25,1},{2,26},{10... | collective-permute-start | bytes 798728 | tf_op jit(solution)/shard_map/ppermute | solution.py:410
  55.2 4.4 %collective-permute-done.9.recv_in = f32[2,16,2560]{2,1,0:T(8,128)S(1)} collective-permute-done((f32[2,16,2560]{2,1,0:T(8,128)S(1)}, f32[2,16,2560]{2,1,0:T(8,128)S(1)}, u32[]{:S(2)}, u32[]{:S(2)}) %collective-permute-start.9) | collective-permute-done | bytes 327712 | tf_op jit(solution)/shard_map/ppermute | solution.py:411
  59.7 0.8 collective-permute-start.10
  60.5 9.3 %collective-permute-done.10.recv_ref = f32[1,16,2560]{2,1,0:T(8,128)S(1)} collective-permute-done((f32[1,16,2560]{2,1,0:T(8,128)S(1)}, f32[1,16,2560]{2,1,0:T(8,128)S(1)}, u32[]{:S(2)}, u32[]{:S(2)}) %collective-permute-start.10) | collective-permute-done | bytes 163872 | tf_op jit(solution)/shard_map/ppermute | solution.py:411
  69.8 0.0 copy-start
  69.8 0.0 copy-start.3
  69.8 0.0 collective-permute-done.14.refs_1_
  69.8 0.0 collective-permute-done.15.refs_2_
  69.8 0.0 collective-permute-done.16.refs_3_
  69.8 0.1 by_core.1
  69.9 0.1 collective-permute-start.17
  70.0 0.5 collective-permute-start.13
  70.5 1.5 %collective-permute-start.12 = (f32[16,2560]{1,0:T(8,128)S(1)}, f32[16,2560]{1,0:T(8,128)S(1)}, u32[]{:S(2)}, u32[]{:S(2)}) collective-permute-start(f32[16,2560]{1,0:T(8,128)S(1)} %total.1.refs_0_), channel_id=1, source_target_pairs={{0,16},{8,24},{16,0},{24,8},{1,17},{9,25},{17,1},{25,9},{2,18},{10... | collective-permute-start | bytes 491528 | tf_op jit(solution)/shard_map/ppermute | solution.py:410
  72.1 1.5 %collective-permute-start.11 = (f32[16,2560]{1,0:T(8,128)S(1)}, f32[16,2560]{1,0:T(8,128)S(1)}, u32[]{:S(2)}, u32[]{:S(2)}) collective-permute-start(f32[16,2560]{1,0:T(8,128)S(1)} %total.1.refs_0_), channel_id=1, source_target_pairs={{0,8},{8,0},{16,24},{24,16},{1,9},{9,1},{17,25},{25,17},{2,10},{10... | collective-permute-start | bytes 491528 | tf_op jit(solution)/shard_map/ppermute | solution.py:410
  73.5 0.0 collective-permute-done.17.recv_ref
  73.6 0.0 copy-done
  73.6 0.0 copy-done.3
  73.6 2.5 %table_part.1 = (f32[512,512]{1,0:T(8,128)}, f32[512]{0:T(512)}) custom-call(f32[1056,128]{1,0:T(8,128)S(1)} %get-tuple-element.85.keep_ref, f32[1056,128]{1,0:T(8,128)S(1)} %collective-permute-done.17.recv_ref, f32[512,512]{1,0:T(8,128)S(1)} %copy-done, f32[512]{0:T(512)S(1)} %copy-done.3), custom_call_target="tpu_custom_call" | custom-call | flops 1000000000 | bytes 65536 | tf_op jit(solution)/shard_map/table_part/pallas_call | solution.py:392
  76.1 1.9 %collective-permute-done.13.refs_3_ = f32[16,2560]{1,0:T(8,128)S(1)} collective-permute-done((f32[16,2560]{1,0:T(8,128)S(1)}, f32[16,2560]{1,0:T(8,128)S(1)}, u32[]{:S(2)}, u32[]{:S(2)}) %collective-permute-start.13) | collective-permute-done | bytes 163872 | tf_op jit(solution)/shard_map/ppermute | solution.py:410
  78.0 2.3 %collective-permute-done.12.refs_2_ = f32[16,2560]{1,0:T(8,128)S(1)} collective-permute-done((f32[16,2560]{1,0:T(8,128)S(1)}, f32[16,2560]{1,0:T(8,128)S(1)}, u32[]{:S(2)}, u32[]{:S(2)}) %collective-permute-start.12) | collective-permute-done | bytes 163872 | tf_op jit(solution)/shard_map/ppermute | solution.py:410
  80.3 0.0 collective-permute-done.11.refs_1_
  80.3 0.9 %gather.1 = (f32[4,16,2048]{2,1,0:T(8,128)}, f32[4,16,512]{2,1,0:T(8,128)}) custom-call(f32[16,2560]{1,0:T(8,128)S(1)} %total.1.refs_0_, f32[16,2560]{1,0:T(8,128)S(1)} %collective-permute-done.11.refs_1_, f32[16,2560]{1,0:T(8,128)S(1)} %collective-permute-done.12.refs_2_, f32[16,2560]{1,0:T(8,128)S(1)} %collective-permute-done.13.refs_3_), custom_call_target="tpu_custom_call" | custom-call | flops 1000000000 | bytes 65536 | tf_op jit(solution)/shard_map/gather/pallas_call | solution.py:392
  (2 shorter events, 0.1 us)
Async XLA Ops:
  10.5 7.4 %collective-permute-start = (f32[256,1536]{1,0:T(8,128)}, f32[256,1536]{1,0:T(8,128)}, u32[]{:S(2)}, u32[]{:S(2)}) collective-permute-start(f32[256,1536]{1,0:T(8,128)} %get-tuple-element.63), channel_id=1, source_target_pairs={{0,1},{1,0},{2,3},{3,2},{4,5},{5,4},{6,7},{7,6},{8,9},{9,8},{10,11... | collective-permute-start | bytes 4718600 | tf_op jit(solution)/shard_map/ppermute | solution.py:440
  11.0 4.3 %copy-start.1 = (s32[1,32,16]{1,2,0:T(8,128)S(1)}, s32[1,32,16]{1,2,0:T(8,128)}, u32[]{:S(2)}) copy-start(s32[1,32,16]{1,2,0:T(8,128)} %param.14) | copy-start | bytes 6148
  11.0 4.3 %copy-start.2 = (s32[1,512]{1,0:T(1,128)S(1)}, s32[1,512]{1,0:T(1,128)}, u32[]{:S(2)}) copy-start(s32[1,512]{1,0:T(1,128)} %slot_ref.1) | copy-start | bytes 6148
  15.2 2.7 %collective-permute-start.1 = (f32[256,1024]{1,0:T(8,128)S(1)}, f32[256,1024]{1,0:T(8,128)S(1)}, u32[]{:S(2)}, u32[]{:S(2)}) collective-permute-start(f32[256,1024]{1,0:T(8,128)S(1)} %get-tuple-element.65), channel_id=1, source_target_pairs={{0,1},{1,0},{2,3},{3,2},{4,5},{5,4},{6,7},{7,6},{8,9},{9,8},{10,11... | collective-permute-start | bytes 3145736 | tf_op jit(solution)/shard_map/ppermute | solution.py:444
  19.6 17.9 %collective-permute-start.2 = (f32[2,64,1280]{2,1,0:T(8,128)S(1)}, f32[2,64,1280]{2,1,0:T(8,128)S(1)}, u32[]{:S(2)}, u32[]{:S(2)}) collective-permute-start(f32[2,64,1280]{2,1,0:T(8,128)S(1)} %get-tuple-element.67), channel_id=1, source_target_pairs={{0,8},{8,0},{16,24},{24,16},{1,9},{9,1},{17,25},{25,17},{2,10},{10... | collective-permute-start | bytes 1966088 | tf_op jit(solution)/shard_map/ppermute | solution.py:410
  22.6 16.4 %collective-permute-start.3 = (f32[2,64,1280]{2,1,0:T(8,128)S(1)}, f32[2,64,1280]{2,1,0:T(8,128)S(1)}, u32[]{:S(2)}, u32[]{:S(2)}) collective-permute-start(f32[2,64,1280]{2,1,0:T(8,128)S(1)} %get-tuple-element.69), channel_id=1, source_target_pairs={{0,16},{8,24},{16,0},{24,8},{1,17},{9,25},{17,1},{25,9},{2,18},{10... | collective-permute-start | bytes 1966088 | tf_op jit(solution)/shard_map/ppermute | solution.py:410
  24.1 17.1 %collective-permute-start.4 = (f32[520,128]{1,0:T(8,128)S(1)}, f32[520,128]{1,0:T(8,128)S(1)}, u32[]{:S(2)}, u32[]{:S(2)}) collective-permute-start(f32[520,128]{1,0:T(8,128)S(1)} %get-tuple-element.59), channel_id=1, source_target_pairs={{0,2},{1,3},{2,4},{3,5},{4,6},{5,7},{6,0},{7,1},{8,10},{9,11},{10,... | collective-permute-start | bytes 798728 | tf_op jit(solution)/shard_map/ppermute | solution.py:451
  25.7 19.6 %collective-permute-start.5 = (f32[520,128]{1,0:T(8,128)S(1)}, f32[520,128]{1,0:T(8,128)S(1)}, u32[]{:S(2)}, u32[]{:S(2)}) collective-permute-start(f32[520,128]{1,0:T(8,128)S(1)} %get-tuple-element.60), channel_id=1, source_target_pairs={{0,4},{1,5},{2,6},{3,7},{4,0},{5,1},{6,2},{7,3},{8,12},{9,13},{10,... | collective-permute-start | bytes 798728 | tf_op jit(solution)/shard_map/ppermute | solution.py:451
  28.3 17.0 %collective-permute-start.6 = (f32[520,128]{1,0:T(8,128)S(1)}, f32[520,128]{1,0:T(8,128)S(1)}, u32[]{:S(2)}, u32[]{:S(2)}) collective-permute-start(f32[520,128]{1,0:T(8,128)S(1)} %get-tuple-element.61), channel_id=1, source_target_pairs={{0,6},{1,7},{2,0},{3,1},{4,2},{5,3},{6,4},{7,5},{8,14},{9,15},{10,... | collective-permute-start | bytes 798728 | tf_op jit(solution)/shard_map/ppermute | solution.py:451
  39.1 8.6 %collective-permute-start.7 = (f32[64,1280]{1,0:T(8,128)S(1)}, f32[64,1280]{1,0:T(8,128)S(1)}, u32[]{:S(2)}, u32[]{:S(2)}) collective-permute-start(f32[64,1280]{1,0:T(8,128)S(1)} %get-tuple-element.71), channel_id=1, source_target_pairs={{0,16},{8,24},{16,0},{24,8},{1,17},{9,25},{17,1},{25,9},{2,18},{10... | collective-permute-start | bytes 983048 | tf_op jit(solution)/shard_map/ppermute | solution.py:410
  40.7 8.2 %collective-permute-start.8 = (f32[64,1280]{1,0:T(8,128)S(1)}, f32[64,1280]{1,0:T(8,128)S(1)}, u32[]{:S(2)}, u32[]{:S(2)}) collective-permute-start(f32[64,1280]{1,0:T(8,128)S(1)} %get-tuple-element.72), channel_id=1, source_target_pairs={{0,8},{8,0},{16,24},{24,16},{1,9},{9,1},{17,25},{25,17},{2,10},{10... | collective-permute-start | bytes 983048 | tf_op jit(solution)/shard_map/ppermute | solution.py:410
  49.0 10.6 %collective-permute-start.9 = (f32[2,16,2560]{2,1,0:T(8,128)S(1)}, f32[2,16,2560]{2,1,0:T(8,128)S(1)}, u32[]{:S(2)}, u32[]{:S(2)}) collective-permute-start(f32[2,16,2560]{2,1,0:T(8,128)S(1)} %get-tuple-element.81), channel_id=1, source_target_pairs={{0,2},{1,3},{2,0},{3,1},{4,6},{5,7},{6,4},{7,5},{8,10},{9,11},{10,... | collective-permute-start | bytes 983048 | tf_op jit(solution)/shard_map/ppermute | solution.py:411
  51.7 18.1 %collective-permute-start.14 = (f32[520,128]{1,0:T(8,128)S(1)}, f32[520,128]{1,0:T(8,128)S(1)}, u32[]{:S(2)}, u32[]{:S(2)}) collective-permute-start(f32[520,128]{1,0:T(8,128)S(1)} %get-tuple-element.75), channel_id=1, source_target_pairs={{0,8},{8,0},{16,24},{24,16},{1,9},{9,1},{17,25},{25,17},{2,10},{10... | collective-permute-start | bytes 798728 | tf_op jit(solution)/shard_map/ppermute | solution.py:410
  52.3 17.5 %collective-permute-start.15 = (f32[520,128]{1,0:T(8,128)S(1)}, f32[520,128]{1,0:T(8,128)S(1)}, u32[]{:S(2)}, u32[]{:S(2)}) collective-permute-start(f32[520,128]{1,0:T(8,128)S(1)} %get-tuple-element.76), channel_id=1, source_target_pairs={{0,16},{8,24},{16,0},{24,8},{1,17},{9,25},{17,1},{25,9},{2,18},{10... | collective-permute-start | bytes 798728 | tf_op jit(solution)/shard_map/ppermute | solution.py:410
  52.8 17.0 %collective-permute-start.16 = (f32[520,128]{1,0:T(8,128)S(1)}, f32[520,128]{1,0:T(8,128)S(1)}, u32[]{:S(2)}, u32[]{:S(2)}) collective-permute-start(f32[520,128]{1,0:T(8,128)S(1)} %get-tuple-element.77), channel_id=1, source_target_pairs={{0,24},{8,16},{16,8},{24,0},{1,25},{9,17},{17,9},{25,1},{2,26},{10... | collective-permute-start | bytes 798728 | tf_op jit(solution)/shard_map/ppermute | solution.py:410
  59.7 10.1 %collective-permute-start.10 = (f32[1,16,2560]{2,1,0:T(8,128)S(1)}, f32[1,16,2560]{2,1,0:T(8,128)S(1)}, u32[]{:S(2)}, u32[]{:S(2)}) collective-permute-start(f32[1,16,2560]{2,1,0:T(8,128)S(1)} %get-tuple-element.83), channel_id=1, source_target_pairs={{0,4},{1,5},{2,6},{3,7},{4,0},{5,1},{6,2},{7,3},{8,12},{9,13},{10,... | collective-permute-start | bytes 491528 | tf_op jit(solution)/shard_map/ppermute | solution.py:411
  69.8 3.8 %copy-start = (f32[512,512]{1,0:T(8,128)S(1)}, f32[512,512]{1,0:T(8,128)}, u32[]{:S(2)}) copy-start(f32[512,512]{1,0:T(8,128)} %table_ref.1) | copy-start | bytes 3145732
  69.8 3.8 %copy-start.3 = (f32[512]{0:T(512)S(1)}, f32[512]{0:T(512)}, u32[]{:S(2)}) copy-start(f32[512]{0:T(512)} %accum_ref.1) | copy-start | bytes 6148
  69.9 3.6 %collective-permute-start.17 = (f32[1056,128]{1,0:T(8,128)S(1)}, f32[1056,128]{1,0:T(8,128)S(1)}, u32[]{:S(2)}, u32[]{:S(2)}) collective-permute-start(f32[1056,128]{1,0:T(8,128)S(1)} %get-tuple-element.86), channel_id=1, source_target_pairs={{0,1},{1,0},{2,3},{3,2},{4,5},{5,4},{6,7},{7,6},{8,9},{9,8},{10,11... | collective-permute-start | bytes 1622024 | tf_op jit(solution)/shard_map/ppermute | solution.py:482
  70.0 8.0 %collective-permute-start.13 = (f32[16,2560]{1,0:T(8,128)S(1)}, f32[16,2560]{1,0:T(8,128)S(1)}, u32[]{:S(2)}, u32[]{:S(2)}) collective-permute-start(f32[16,2560]{1,0:T(8,128)S(1)} %total.1.refs_0_), channel_id=1, source_target_pairs={{0,24},{8,16},{16,8},{24,0},{1,25},{9,17},{17,9},{25,1},{2,26},{10... | collective-permute-start | bytes 491528 | tf_op jit(solution)/shard_map/ppermute | solution.py:410
  70.5 9.8 %collective-permute-start.12 = (f32[16,2560]{1,0:T(8,128)S(1)}, f32[16,2560]{1,0:T(8,128)S(1)}, u32[]{:S(2)}, u32[]{:S(2)}) collective-permute-start(f32[16,2560]{1,0:T(8,128)S(1)} %total.1.refs_0_), channel_id=1, source_target_pairs={{0,16},{8,24},{16,0},{24,8},{1,17},{9,25},{17,1},{25,9},{2,18},{10... | collective-permute-start | bytes 491528 | tf_op jit(solution)/shard_map/ppermute | solution.py:410
  72.1 8.3 %collective-permute-start.11 = (f32[16,2560]{1,0:T(8,128)S(1)}, f32[16,2560]{1,0:T(8,128)S(1)}, u32[]{:S(2)}, u32[]{:S(2)}) collective-permute-start(f32[16,2560]{1,0:T(8,128)S(1)} %total.1.refs_0_), channel_id=1, source_target_pairs={{0,8},{8,0},{16,24},{24,16},{1,9},{9,1},{17,25},{25,17},{2,10},{10... | collective-permute-start | bytes 491528 | tf_op jit(solution)/shard_map/ppermute | solution.py:410

commit v11 on v10

--- a/solution.py
+++ b/solution.py
@@ -339,28 +339,21 @@
     next_b_ref[...] = keep_b_ref[x] + from_y_ref[x]
 
 
-def chip_bit(bit):
-    return (lax.axis_index("rows") // 2) // (1 << bit) % 2
-
-
-def halve(bit, send_ref, keep_ref, block):
-    mine = chip_bit(bit)
-    for i in range(send_ref.shape[0]):
-        send_ref[i] = block(2 * i + 1 - mine)
-        keep_ref[i] = block(2 * i + mine)
-
-
-def chip_first_kernel(next_a_ref, from_y_ref, next_b_ref, from_x_ref, send_ref, keep_ref):
-    halve(0, send_ref, keep_ref, lambda at: jnp.concatenate(
-        [next_a_ref[at] + from_y_ref[at], next_b_ref[at] + from_x_ref[at]], axis=1))
-
-
-def chip_kernel(bit, keep_in, recv_in, send_ref, keep_ref):
-    halve(bit, send_ref, keep_ref, lambda at: keep_in[at] + recv_in[at])
-
-
-def total_kernel(tokens, keep_ref, recv_ref, out_ref):
-    out_ref[...] = (keep_ref[0] + recv_ref[0]) * (1.0 / tokens)
+def chips_kernel(next_a_ref, from_y_ref, next_b_ref, from_x_ref, *out_refs):
+    chips = len(out_refs)
+    chip = lax.axis_index("rows") // 2
+    half = next_a_ref.shape[-1]
+    for k, out_ref in enumerate(out_refs):
+        at = lax.rem(chip + k, chips)
+        out_ref[:, :half] = next_a_ref[at] + from_y_ref[at]
+        out_ref[:, half:] = next_b_ref[at] + from_x_ref[at]
+
+
+def total_kernel(tokens, *refs):
+    total = refs[0][...]
+    for ref in refs[1:-1]:
+        total = total + ref[...]
+    refs[-1][...] = total * (1.0 / tokens)
 
 
 def gather_kernel(*refs):
@@ -408,7 +401,6 @@
     piece = width // (rows_size * dp_size)
     cores = [(i, i ^ 1) for i in range(rows_size)]
     over_dp = lambda v, bit: lax.ppermute(v, "dp", [(i, i ^ bit) for i in range(dp_size)])
-    over_chips = lambda v, bit: lax.ppermute(v, "rows", [(i, i ^ (2 << bit)) for i in range(rows_size)])
     after = lambda value, *others: lax.optimization_barrier((value, *others))[0]
     strip = chips * piece
 
@@ -417,8 +409,6 @@
 
     by_dp = lambda v: v.reshape(2, 2, strip, v.shape[-1])
     by_chip = lambda v: v.reshape(*v.shape[:-2], chips, piece, v.shape[-1])
-    bits = chips.bit_length() - 1
-    far_off = lambda *dims, dtype=f32: pltpu.HBM(dims, dtype)
     local = lambda *dims, dtype=f32: pltpu.VMEM(dims, dtype)
     sides = lambda cols: [local(width // 2, cols)] * 2
     keep1, send1, hid, dsilu, gatt, gpre_uv, normed_t, events, cotangent, w_in = call(
@@ -443,6 +433,7 @@
         (lengths, hid, dsilu, gatt, normed_t), 1, long=True, grant=10)
     recv2 = lax.ppermute(send2, "rows", cores)
     block = capacity * (width // LANES)
+    gpre_uv = after(gpre_uv, recv1)
     sends = call(
         functools.partial(events_kernel, rows_size, dp_size), "events_part",
         [local(2 * dp_size * block + ID_ROWS, LANES)] * chips,
@@ -464,16 +455,13 @@
         functools.partial(by_part_kernel, dp_size, block), "by_part",
         [local(2 * chips * block + id_rows(chips), LANES)] * dp_size, came, long=True)
     next_a = after(next_a, *parts)
-    send, keep = call(
-        chip_first_kernel, "chip_sums", [local(chips // 2, piece, cols)] * 2,
+    sums = call(
+        chips_kernel, "chip_sums", [local(piece, cols)] * chips,
         [by_chip(v) for v in (next_a, from_y, next_b, from_x)])
     parts = [parts[0]] + [over_dp(parts[k], k) for k in range(1, dp_size)]
-    for bit in range(1, bits):
-        send, keep = call(
-            functools.partial(chip_kernel, bit), "chip_sums", [local(chips >> (bit + 1), piece, cols)] * 2,
-            (keep, over_chips(send, bit - 1)), long=bit == 1)
+    sums = [sums[0]] + [ahead(sums[k], k) for k in range(1, chips)]
     (total,) = call(
-        functools.partial(total_kernel, tokens), "total", [local(piece, cols)], (keep, over_chips(send, bits - 1)))
+        functools.partial(total_kernel, tokens), "total", [local(piece, cols)], sums, long=True)
     pieces = gathered(total)
     parts[0] = after(parts[0], total)
     keep, send = call(

time: 81.4 us -> 77.8 us (0.956)
  Pallas kernels: 21.4 us -> 19.1 us
  waiting for transfers between devices: 34.9 us -> 33.3 us
    ppermute x2 -> x0, waiting for transfers between devices: 13.7 us -> none  [body(): lax.ppermute(v, 'rows', [(i, i ^ 2 << bit) for i in range(rows_size)])]
    ppermute x3 -> x6, waiting for transfers between devices: 4.05 us -> 10.9 us  [body(): lax.ppermute(v, 'rows', [(i, (i + 2 * k) % rows_size) for i in range(rows...]
    ppermute x3 -> x6, starting transfers between devices: 5.52 us -> 11.1 us  [body(): lax.ppermute(v, 'rows', [(i, (i + 2 * k) % rows_size) for i in range(rows...]
    ppermute x10, waiting for transfers between devices: 17.1 us -> 22.4 us  [body(): lax.ppermute(v, 'dp', [(i, i ^ bit) for i in range(dp_size)])]
    ppermute x2 -> x0, starting transfers between devices: 3.53 us -> none  [body(): lax.ppermute(v, 'rows', [(i, i ^ 2 << bit) for i in range(rows_size)])]
    pallas_call x12 -> x11, Pallas kernels: 21.4 us -> 19.1 us  [call(): pl.pallas_call(kernel, name=name, in_specs=[pl.BlockSpec(memory_space=p o...]
    ppermute x10, starting transfers between devices: 13.7 us -> 12.1 us  [body(): lax.ppermute(v, 'dp', [(i, i ^ bit) for i in range(dp_size)])]
  transfers between devices with their start and end apart: 18 -> 19, of which waited for: 9 -> 11; matrix products, arithmetic and copies ran while one was open for 0% -> 0% of each run, Pallas kernels for 12% -> 12%
where the time goes in v11:
time: 77.8 us; the launch traced here: 77.6 us
  waiting for transfers between devices  33.3 us (43%)
  starting transfers between devices  23.9 us (31%)
  Pallas kernels  19.1 us (25%)
  between operations  1.38 us (2%)
    ppermute x10, waiting for transfers between devices, body(): lax.ppermute(v, 'dp', [(i, i ^ bit) for i in range(dp_size)])  22.4 us
    pallas_call x11, Pallas kernels, call(): pl.pallas_call(kernel, name=name, in_specs=[pl.BlockSpec(memory_space=p o...  19.1 us
    ppermute x10, starting transfers between devices, body(): lax.ppermute(v, 'dp', [(i, i ^ bit) for i in range(dp_size)])  12.1 us
    ppermute x6, starting transfers between devices, body(): lax.ppermute(v, 'rows', [(i, (i + 2 * k) % rows_size) for i in range(rows...  11.1 us
    ppermute x6, waiting for transfers between devices, body(): lax.ppermute(v, 'rows', [(i, (i + 2 * k) % rows_size) for i in range(rows...  10.9 us
  transfers between devices with their start and end apart: 19, of which 11 were waited for; matrix products, arithmetic and copies ran while one was open for 0% of the time, Pallas kernels for 12%

profile of v11, /device:TPU:0, one launch (start us, length us, event | category | flops | bytes accessed | tf_op | source)
XLA Modules:
  0.0 77.6 jit_solution(49989510768659432)
XLA Ops:
  1.3 8.3 %forward_part.1 = (f32[256,1536]{1,0:T(8,128)S(1)}, f32[256,1536]{1,0:T(8,128)S(1)}, bf16[512,1536]{1,0:T(8,128)(2,1)S(1)}, bf16[512,1024]{1,0:T(8,128)(2,1)S(1)...) custom-call(s32[1]{0:T(128)S(6)} %copy.13.len_ref, ...), custom_call_target="tpu_custom_call" | custom-call | flops 99999997952 | bytes 65536 | tf_op jit(solution)/shard_map/forward_part/pallas_call | solution.py:385
  9.5 0.5 collective-permute-start
  10.1 0.0 copy-start.1
  10.1 0.0 copy-start.2
  10.1 4.1 %attention_part.1 = (f32[256,1024]{1,0:T(8,128)S(1)}, f32[256,1024]{1,0:T(8,128)S(1)}, bf16[512,1024]{1,0:T(8,128)(2,1)S(1)}) custom-call(s32[1]{0:T(128)S(6)} %copy.13.len_ref, bf16[512,1536]{1,0:T(8,128)(2,1)S(1)} %get-tuple-element.56.hid_ref, bf16[512,1024]{1,0:T(8,128)(2,1)S(1)} %get-tuple-element.57.dsilu_ref, ...), custom_call_target="tpu_custom_call" | custom-call | flops 99999997952 | bytes 65536 | tf_op jit(solution)/shard_map/attention_part/pallas_call | solution.py:385
  14.2 0.1 collective-permute-start.1
  14.3 0.0 collective-permute-done
  14.3 0.0 copy-done.1
  14.3 0.0 copy-done.2
  14.3 2.6 %events_part.1 = (f32[520,128]{1,0:T(8,128)S(1)}, f32[520,128]{1,0:T(8,128)S(1)}, f32[520,128]{1,0:T(8,128)S(1)}, f32[520,128]{1,0:T(8,128)S(1)}) custom-call(s32[1]{0:T(128)S(6)} %copy.13.len_ref, bf16[512,512]{1,0:T(8,128)(2,1)S(1)} %get-tuple-element.50.ev_ref, bf16[512,512]{1,0:T(8,128)(2,1)S(1)} %get-tuple-element.51.cot_ref, ...), custom_call_target="tpu_custom_call" | custom-call | flops 99999997952 | bytes 65536 | tf_op jit(solution)/shard_map/events_part/pallas_call | solution.py:385
  16.9 0.0 collective-permute-done.1
  16.9 0.3 first_sums.1
  17.2 3.0 %collective-permute-start.2 = (f32[2,64,1280]{2,1,0:T(8,128)S(1)}, f32[2,64,1280]{2,1,0:T(8,128)S(1)}, u32[]{:S(2)}, u32[]{:S(2)}) collective-permute-start(f32[2,64,1280]{2,1,0:T(8,128)S(1)} %get-tuple-element.69), channel_id=1, source_target_pairs={{0,8},{8,0},{16,24},{24,16},{1,9},{9,1},{17,25},{25,17},{2,10},{10... | collective-permute-start | bytes 1966088 | tf_op jit(solution)/shard_map/ppermute | solution.py:403
  20.2 1.5 %collective-permute-start.3 = (f32[2,64,1280]{2,1,0:T(8,128)S(1)}, f32[2,64,1280]{2,1,0:T(8,128)S(1)}, u32[]{:S(2)}, u32[]{:S(2)}) collective-permute-start(f32[2,64,1280]{2,1,0:T(8,128)S(1)} %get-tuple-element.71), channel_id=1, source_target_pairs={{0,16},{8,24},{16,0},{24,8},{1,17},{9,25},{17,1},{25,9},{2,18},{10... | collective-permute-start | bytes 1966088 | tf_op jit(solution)/shard_map/ppermute | solution.py:403
  21.8 1.6 %collective-permute-start.4 = (f32[520,128]{1,0:T(8,128)S(1)}, f32[520,128]{1,0:T(8,128)S(1)}, u32[]{:S(2)}, u32[]{:S(2)}) collective-permute-start(f32[520,128]{1,0:T(8,128)S(1)} %get-tuple-element.62), channel_id=1, source_target_pairs={{0,2},{1,3},{2,4},{3,5},{4,6},{5,7},{6,0},{7,1},{8,10},{9,11},{10,... | collective-permute-start | bytes 798728 | tf_op jit(solution)/shard_map/ppermute | solution.py:442
  23.3 2.6 %collective-permute-start.5 = (f32[520,128]{1,0:T(8,128)S(1)}, f32[520,128]{1,0:T(8,128)S(1)}, u32[]{:S(2)}, u32[]{:S(2)}) collective-permute-start(f32[520,128]{1,0:T(8,128)S(1)} %get-tuple-element.63), channel_id=1, source_target_pairs={{0,4},{1,5},{2,6},{3,7},{4,0},{5,1},{6,2},{7,3},{8,12},{9,13},{10,... | collective-permute-start | bytes 798728 | tf_op jit(solution)/shard_map/ppermute | solution.py:442
  25.9 1.3 %collective-permute-start.6 = (f32[520,128]{1,0:T(8,128)S(1)}, f32[520,128]{1,0:T(8,128)S(1)}, u32[]{:S(2)}, u32[]{:S(2)}) collective-permute-start(f32[520,128]{1,0:T(8,128)S(1)} %get-tuple-element.64), channel_id=1, source_target_pairs={{0,6},{1,7},{2,0},{3,1},{4,2},{5,3},{6,4},{7,5},{8,14},{9,15},{10,... | collective-permute-start | bytes 798728 | tf_op jit(solution)/shard_map/ppermute | solution.py:442
  27.3 7.9 %collective-permute-done.2.from_x_ref = f32[2,64,1280]{2,1,0:T(8,128)S(1)} collective-permute-done((f32[2,64,1280]{2,1,0:T(8,128)S(1)}, f32[2,64,1280]{2,1,0:T(8,128)S(1)}, u32[]{:S(2)}, u32[]{:S(2)}) %collective-permute-start.2) | collective-permute-done | bytes 655392 | tf_op jit(solution)/shard_map/ppermute | solution.py:403
  35.2 1.5 %collective-permute-done.3.from_y_ref = f32[2,64,1280]{2,1,0:T(8,128)S(1)} collective-permute-done((f32[2,64,1280]{2,1,0:T(8,128)S(1)}, f32[2,64,1280]{2,1,0:T(8,128)S(1)}, u32[]{:S(2)}, u32[]{:S(2)}) %collective-permute-start.3) | collective-permute-done | bytes 655392 | tf_op jit(solution)/shard_map/ppermute | solution.py:403
  36.6 0.1 second_sums.1
  36.8 1.6 %collective-permute-start.7 = (f32[64,1280]{1,0:T(8,128)S(1)}, f32[64,1280]{1,0:T(8,128)S(1)}, u32[]{:S(2)}, u32[]{:S(2)}) collective-permute-start(f32[64,1280]{1,0:T(8,128)S(1)} %get-tuple-element.73), channel_id=1, source_target_pairs={{0,16},{8,24},{16,0},{24,8},{1,17},{9,25},{17,1},{25,9},{2,18},{10... | collective-permute-start | bytes 983048 | tf_op jit(solution)/shard_map/ppermute | solution.py:403
  38.4 0.5 collective-permute-start.8
  38.9 0.0 collective-permute-done.4.refs_1_
  38.9 4.0 %collective-permute-done.5.refs_2_ = f32[520,128]{1,0:T(8,128)S(1)} collective-permute-done((f32[520,128]{1,0:T(8,128)S(1)}, f32[520,128]{1,0:T(8,128)S(1)}, u32[]{:S(2)}, u32[]{:S(2)}) %collective-permute-start.5) | collective-permute-done | bytes 266272 | tf_op jit(solution)/shard_map/ppermute | solution.py:442
  42.9 0.0 collective-permute-done.6.refs_3_
  42.9 0.1 by_part.1
  43.0 2.3 %collective-permute-done.7 = f32[64,1280]{1,0:T(8,128)S(1)} collective-permute-done((f32[64,1280]{1,0:T(8,128)S(1)}, f32[64,1280]{1,0:T(8,128)S(1)}, u32[]{:S(2)}, u32[]{:S(2)}) %collective-permute-start.7) | collective-permute-done | bytes 327712 | tf_op jit(solution)/shard_map/ppermute | solution.py:403
  45.3 1.2 %collective-permute-done.8 = f32[64,1280]{1,0:T(8,128)S(1)} collective-permute-done((f32[64,1280]{1,0:T(8,128)S(1)}, f32[64,1280]{1,0:T(8,128)S(1)}, u32[]{:S(2)}, u32[]{:S(2)}) %collective-permute-start.8) | collective-permute-done | bytes 327712 | tf_op jit(solution)/shard_map/ppermute | solution.py:403
  46.6 0.1 chip_sums.1
  46.6 2.7 %collective-permute-start.9 = (f32[16,2560]{1,0:T(8,128)S(1)}, f32[16,2560]{1,0:T(8,128)S(1)}, u32[]{:S(2)}, u32[]{:S(2)}) collective-permute-start(f32[16,2560]{1,0:T(8,128)S(1)} %get-tuple-element.83), channel_id=1, source_target_pairs={{0,2},{1,3},{2,4},{3,5},{4,6},{5,7},{6,0},{7,1},{8,10},{9,11},{10,... | collective-permute-start | bytes 491528 | tf_op jit(solution)/shard_map/ppermute | solution.py:442
  49.4 1.6 %collective-permute-start.10 = (f32[16,2560]{1,0:T(8,128)S(1)}, f32[16,2560]{1,0:T(8,128)S(1)}, u32[]{:S(2)}, u32[]{:S(2)}) collective-permute-start(f32[16,2560]{1,0:T(8,128)S(1)} %get-tuple-element.84), channel_id=1, source_target_pairs={{0,4},{1,5},{2,6},{3,7},{4,0},{5,1},{6,2},{7,3},{8,12},{9,13},{10,... | collective-permute-start | bytes 491528 | tf_op jit(solution)/shard_map/ppermute | solution.py:442
  51.0 1.3 %collective-permute-start.11 = (f32[16,2560]{1,0:T(8,128)S(1)}, f32[16,2560]{1,0:T(8,128)S(1)}, u32[]{:S(2)}, u32[]{:S(2)}) collective-permute-start(f32[16,2560]{1,0:T(8,128)S(1)} %get-tuple-element.85), channel_id=1, source_target_pairs={{0,6},{1,7},{2,0},{3,1},{4,2},{5,3},{6,4},{7,5},{8,14},{9,15},{10,... | collective-permute-start | bytes 491528 | tf_op jit(solution)/shard_map/ppermute | solution.py:442
  52.2 0.6 collective-permute-start.15
  52.8 0.5 collective-permute-start.16
  53.3 2.0 %collective-permute-done.9.refs_1_ = f32[16,2560]{1,0:T(8,128)S(1)} collective-permute-done((f32[16,2560]{1,0:T(8,128)S(1)}, f32[16,2560]{1,0:T(8,128)S(1)}, u32[]{:S(2)}, u32[]{:S(2)}) %collective-permute-start.9) | collective-permute-done | bytes 163872 | tf_op jit(solution)/shard_map/ppermute | solution.py:442
  55.3 0.7 collective-permute-start.17
  56.1 4.8 %collective-permute-done.10.refs_2_ = f32[16,2560]{1,0:T(8,128)S(1)} collective-permute-done((f32[16,2560]{1,0:T(8,128)S(1)}, f32[16,2560]{1,0:T(8,128)S(1)}, u32[]{:S(2)}, u32[]{:S(2)}) %collective-permute-start.10) | collective-permute-done | bytes 163872 | tf_op jit(solution)/shard_map/ppermute | solution.py:442
  60.9 0.0 collective-permute-done.11.refs_3_
  61.0 0.0 copy-start
  61.0 0.0 copy-start.3
  61.0 0.6 collective-permute-done.15.refs_1_
  61.6 4.0 %collective-permute-done.16.refs_2_ = f32[520,128]{1,0:T(8,128)S(1)} collective-permute-done((f32[520,128]{1,0:T(8,128)S(1)}, f32[520,128]{1,0:T(8,128)S(1)}, u32[]{:S(2)}, u32[]{:S(2)}) %collective-permute-start.16) | collective-permute-done | bytes 266272 | tf_op jit(solution)/shard_map/ppermute | solution.py:403
  65.5 0.0 collective-permute-done.17.refs_3_
  65.5 0.1 by_core.1
  65.6 0.1 collective-permute-start.18
  65.7 1.5 %collective-permute-start.14 = (f32[16,2560]{1,0:T(8,128)S(1)}, f32[16,2560]{1,0:T(8,128)S(1)}, u32[]{:S(2)}, u32[]{:S(2)}) collective-permute-start(f32[16,2560]{1,0:T(8,128)S(1)} %total.1.refs_0_), channel_id=1, source_target_pairs={{0,24},{8,16},{16,8},{24,0},{1,25},{9,17},{17,9},{25,1},{2,26},{10... | collective-permute-start | bytes 491528 | tf_op jit(solution)/shard_map/ppermute | solution.py:403
  67.2 1.5 %collective-permute-start.13 = (f32[16,2560]{1,0:T(8,128)S(1)}, f32[16,2560]{1,0:T(8,128)S(1)}, u32[]{:S(2)}, u32[]{:S(2)}) collective-permute-start(f32[16,2560]{1,0:T(8,128)S(1)} %total.1.refs_0_), channel_id=1, source_target_pairs={{0,16},{8,24},{16,0},{24,8},{1,17},{9,25},{17,1},{25,9},{2,18},{10... | collective-permute-start | bytes 491528 | tf_op jit(solution)/shard_map/ppermute | solution.py:403
  68.7 0.5 collective-permute-start.12
  69.2 0.0 collective-permute-done.18.recv_ref
  69.2 0.0 copy-done
  69.2 0.0 copy-done.3
  69.3 2.5 %table_part.1 = (f32[512,512]{1,0:T(8,128)}, f32[512]{0:T(512)}) custom-call(f32[1056,128]{1,0:T(8,128)S(1)} %get-tuple-element.87.keep_ref, f32[1056,128]{1,0:T(8,128)S(1)} %collective-permute-done.18.recv_ref, f32[512,512]{1,0:T(8,128)S(1)} %copy-done, f32[512]{0:T(512)S(1)} %copy-done.3), custom_call_target="tpu_custom_call" | custom-call | flops 1000000000 | bytes 65536 | tf_op jit(solution)/shard_map/table_part/pallas_call | solution.py:385
  71.8 1.9 %collective-permute-done.14.refs_3_ = f32[16,2560]{1,0:T(8,128)S(1)} collective-permute-done((f32[16,2560]{1,0:T(8,128)S(1)}, f32[16,2560]{1,0:T(8,128)S(1)}, u32[]{:S(2)}, u32[]{:S(2)}) %collective-permute-start.14) | collective-permute-done | bytes 163872 | tf_op jit(solution)/shard_map/ppermute | solution.py:403
  73.7 3.0 %collective-permute-done.13.refs_2_ = f32[16,2560]{1,0:T(8,128)S(1)} collective-permute-done((f32[16,2560]{1,0:T(8,128)S(1)}, f32[16,2560]{1,0:T(8,128)S(1)}, u32[]{:S(2)}, u32[]{:S(2)}) %collective-permute-start.13) | collective-permute-done | bytes 163872 | tf_op jit(solution)/shard_map/ppermute | solution.py:403
  76.7 0.0 collective-permute-done.12.refs_1_
  76.7 0.9 %gather.1 = (f32[4,16,2048]{2,1,0:T(8,128)}, f32[4,16,512]{2,1,0:T(8,128)}) custom-call(f32[16,2560]{1,0:T(8,128)S(1)} %total.1.refs_0_, f32[16,2560]{1,0:T(8,128)S(1)} %collective-permute-done.12.refs_1_, f32[16,2560]{1,0:T(8,128)S(1)} %collective-permute-done.13.refs_2_, f32[16,2560]{1,0:T(8,128)S(1)} %collective-permute-done.14.refs_3_), custom_call_target="tpu_custom_call" | custom-call | flops 1000000000 | bytes 65536 | tf_op jit(solution)/shard_map/gather/pallas_call | solution.py:385
  (1 shorter events, 0.0 us)
Async XLA Ops:
  9.5 4.8 %collective-permute-start = (f32[256,1536]{1,0:T(8,128)S(1)}, f32[256,1536]{1,0:T(8,128)S(1)}, u32[]{:S(2)}, u32[]{:S(2)}) collective-permute-start(f32[256,1536]{1,0:T(8,128)S(1)} %get-tuple-element.54), channel_id=1, source_target_pairs={{0,1},{1,0},{2,3},{3,2},{4,5},{5,4},{6,7},{7,6},{8,9},{9,8},{10,11... | collective-permute-start | bytes 4718600 | tf_op jit(solution)/shard_map/ppermute | solution.py:430
  10.1 4.3 %copy-start.1 = (s32[1,32,16]{1,2,0:T(8,128)S(1)}, s32[1,32,16]{1,2,0:T(8,128)}, u32[]{:S(2)}) copy-start(s32[1,32,16]{1,2,0:T(8,128)} %param.14) | copy-start | bytes 6148
  10.1 4.3 %copy-start.2 = (s32[1,512]{1,0:T(1,128)S(1)}, s32[1,512]{1,0:T(1,128)}, u32[]{:S(2)}) copy-start(s32[1,512]{1,0:T(1,128)} %slot_ref.1) | copy-start | bytes 6148
  14.2 2.7 %collective-permute-start.1 = (f32[256,1024]{1,0:T(8,128)S(1)}, f32[256,1024]{1,0:T(8,128)S(1)}, u32[]{:S(2)}, u32[]{:S(2)}) collective-permute-start(f32[256,1024]{1,0:T(8,128)S(1)} %get-tuple-element.67), channel_id=1, source_target_pairs={{0,1},{1,0},{2,3},{3,2},{4,5},{5,4},{6,7},{7,6},{8,9},{9,8},{10,11... | collective-permute-start | bytes 3145736 | tf_op jit(solution)/shard_map/ppermute | solution.py:434
  17.2 17.9 %collective-permute-start.2 = (f32[2,64,1280]{2,1,0:T(8,128)S(1)}, f32[2,64,1280]{2,1,0:T(8,128)S(1)}, u32[]{:S(2)}, u32[]{:S(2)}) collective-permute-start(f32[2,64,1280]{2,1,0:T(8,128)S(1)} %get-tuple-element.69), channel_id=1, source_target_pairs={{0,8},{8,0},{16,24},{24,16},{1,9},{9,1},{17,25},{25,17},{2,10},{10... | collective-permute-start | bytes 1966088 | tf_op jit(solution)/shard_map/ppermute | solution.py:403
  20.2 16.4 %collective-permute-start.3 = (f32[2,64,1280]{2,1,0:T(8,128)S(1)}, f32[2,64,1280]{2,1,0:T(8,128)S(1)}, u32[]{:S(2)}, u32[]{:S(2)}) collective-permute-start(f32[2,64,1280]{2,1,0:T(8,128)S(1)} %get-tuple-element.71), channel_id=1, source_target_pairs={{0,16},{8,24},{16,0},{24,8},{1,17},{9,25},{17,1},{25,9},{2,18},{10... | collective-permute-start | bytes 1966088 | tf_op jit(solution)/shard_map/ppermute | solution.py:403
  21.8 17.1 %collective-permute-start.4 = (f32[520,128]{1,0:T(8,128)S(1)}, f32[520,128]{1,0:T(8,128)S(1)}, u32[]{:S(2)}, u32[]{:S(2)}) collective-permute-start(f32[520,128]{1,0:T(8,128)S(1)} %get-tuple-element.62), channel_id=1, source_target_pairs={{0,2},{1,3},{2,4},{3,5},{4,6},{5,7},{6,0},{7,1},{8,10},{9,11},{10,... | collective-permute-start | bytes 798728 | tf_op jit(solution)/shard_map/ppermute | solution.py:442
  23.3 19.6 %collective-permute-start.5 = (f32[520,128]{1,0:T(8,128)S(1)}, f32[520,128]{1,0:T(8,128)S(1)}, u32[]{:S(2)}, u32[]{:S(2)}) collective-permute-start(f32[520,128]{1,0:T(8,128)S(1)} %get-tuple-element.63), channel_id=1, source_target_pairs={{0,4},{1,5},{2,6},{3,7},{4,0},{5,1},{6,2},{7,3},{8,12},{9,13},{10,... | collective-permute-start | bytes 798728 | tf_op jit(solution)/shard_map/ppermute | solution.py:442
  25.9 17.0 %collective-permute-start.6 = (f32[520,128]{1,0:T(8,128)S(1)}, f32[520,128]{1,0:T(8,128)S(1)}, u32[]{:S(2)}, u32[]{:S(2)}) collective-permute-start(f32[520,128]{1,0:T(8,128)S(1)} %get-tuple-element.64), channel_id=1, source_target_pairs={{0,6},{1,7},{2,0},{3,1},{4,2},{5,3},{6,4},{7,5},{8,14},{9,15},{10,... | collective-permute-start | bytes 798728 | tf_op jit(solution)/shard_map/ppermute | solution.py:442
  36.8 8.6 %collective-permute-start.7 = (f32[64,1280]{1,0:T(8,128)S(1)}, f32[64,1280]{1,0:T(8,128)S(1)}, u32[]{:S(2)}, u32[]{:S(2)}) collective-permute-start(f32[64,1280]{1,0:T(8,128)S(1)} %get-tuple-element.73), channel_id=1, source_target_pairs={{0,16},{8,24},{16,0},{24,8},{1,17},{9,25},{17,1},{25,9},{2,18},{10... | collective-permute-start | bytes 983048 | tf_op jit(solution)/shard_map/ppermute | solution.py:403
  38.4 8.2 %collective-permute-start.8 = (f32[64,1280]{1,0:T(8,128)S(1)}, f32[64,1280]{1,0:T(8,128)S(1)}, u32[]{:S(2)}, u32[]{:S(2)}) collective-permute-start(f32[64,1280]{1,0:T(8,128)S(1)} %get-tuple-element.74), channel_id=1, source_target_pairs={{0,8},{8,0},{16,24},{24,16},{1,9},{9,1},{17,25},{25,17},{2,10},{10... | collective-permute-start | bytes 983048 | tf_op jit(solution)/shard_map/ppermute | solution.py:403
  46.6 8.7 %collective-permute-start.9 = (f32[16,2560]{1,0:T(8,128)S(1)}, f32[16,2560]{1,0:T(8,128)S(1)}, u32[]{:S(2)}, u32[]{:S(2)}) collective-permute-start(f32[16,2560]{1,0:T(8,128)S(1)} %get-tuple-element.83), channel_id=1, source_target_pairs={{0,2},{1,3},{2,4},{3,5},{4,6},{5,7},{6,0},{7,1},{8,10},{9,11},{10,... | collective-permute-start | bytes 491528 | tf_op jit(solution)/shard_map/ppermute | solution.py:442
  49.4 11.6 %collective-permute-start.10 = (f32[16,2560]{1,0:T(8,128)S(1)}, f32[16,2560]{1,0:T(8,128)S(1)}, u32[]{:S(2)}, u32[]{:S(2)}) collective-permute-start(f32[16,2560]{1,0:T(8,128)S(1)} %get-tuple-element.84), channel_id=1, source_target_pairs={{0,4},{1,5},{2,6},{3,7},{4,0},{5,1},{6,2},{7,3},{8,12},{9,13},{10,... | collective-permute-start | bytes 491528 | tf_op jit(solution)/shard_map/ppermute | solution.py:442
  51.0 10.0 %collective-permute-start.11 = (f32[16,2560]{1,0:T(8,128)S(1)}, f32[16,2560]{1,0:T(8,128)S(1)}, u32[]{:S(2)}, u32[]{:S(2)}) collective-permute-start(f32[16,2560]{1,0:T(8,128)S(1)} %get-tuple-element.85), channel_id=1, source_target_pairs={{0,6},{1,7},{2,0},{3,1},{4,2},{5,3},{6,4},{7,5},{8,14},{9,15},{10,... | collective-permute-start | bytes 491528 | tf_op jit(solution)/shard_map/ppermute | solution.py:442
  52.2 9.3 %collective-permute-start.15 = (f32[520,128]{1,0:T(8,128)S(1)}, f32[520,128]{1,0:T(8,128)S(1)}, u32[]{:S(2)}, u32[]{:S(2)}) collective-permute-start(f32[520,128]{1,0:T(8,128)S(1)} %get-tuple-element.77), channel_id=1, source_target_pairs={{0,8},{8,0},{16,24},{24,16},{1,9},{9,1},{17,25},{25,17},{2,10},{10... | collective-permute-start | bytes 798728 | tf_op jit(solution)/shard_map/ppermute | solution.py:403
  52.8 12.7 %collective-permute-start.16 = (f32[520,128]{1,0:T(8,128)S(1)}, f32[520,128]{1,0:T(8,128)S(1)}, u32[]{:S(2)}, u32[]{:S(2)}) collective-permute-start(f32[520,128]{1,0:T(8,128)S(1)} %get-tuple-element.78), channel_id=1, source_target_pairs={{0,16},{8,24},{16,0},{24,8},{1,17},{9,25},{17,1},{25,9},{2,18},{10... | collective-permute-start | bytes 798728 | tf_op jit(solution)/shard_map/ppermute | solution.py:403
  55.3 10.2 %collective-permute-start.17 = (f32[520,128]{1,0:T(8,128)S(1)}, f32[520,128]{1,0:T(8,128)S(1)}, u32[]{:S(2)}, u32[]{:S(2)}) collective-permute-start(f32[520,128]{1,0:T(8,128)S(1)} %get-tuple-element.79), channel_id=1, source_target_pairs={{0,24},{8,16},{16,8},{24,0},{1,25},{9,17},{17,9},{25,1},{2,26},{10... | collective-permute-start | bytes 798728 | tf_op jit(solution)/shard_map/ppermute | solution.py:403
  61.0 8.3 %copy-start = (f32[512,512]{1,0:T(8,128)S(1)}, f32[512,512]{1,0:T(8,128)}, u32[]{:S(2)}) copy-start(f32[512,512]{1,0:T(8,128)} %table_ref.1) | copy-start | bytes 3145732
  61.0 8.3 %copy-start.3 = (f32[512]{0:T(512)S(1)}, f32[512]{0:T(512)}, u32[]{:S(2)}) copy-start(f32[512]{0:T(512)} %accum_ref.1) | copy-start | bytes 6148
  65.6 3.6 %collective-permute-start.18 = (f32[1056,128]{1,0:T(8,128)S(1)}, f32[1056,128]{1,0:T(8,128)S(1)}, u32[]{:S(2)}, u32[]{:S(2)}) collective-permute-start(f32[1056,128]{1,0:T(8,128)S(1)} %get-tuple-element.88), channel_id=1, source_target_pairs={{0,1},{1,0},{2,3},{3,2},{4,5},{5,4},{6,7},{7,6},{8,9},{9,8},{10,11... | collective-permute-start | bytes 1622024 | tf_op jit(solution)/shard_map/ppermute | solution.py:470
  65.7 8.0 %collective-permute-start.14 = (f32[16,2560]{1,0:T(8,128)S(1)}, f32[16,2560]{1,0:T(8,128)S(1)}, u32[]{:S(2)}, u32[]{:S(2)}) collective-permute-start(f32[16,2560]{1,0:T(8,128)S(1)} %total.1.refs_0_), channel_id=1, source_target_pairs={{0,24},{8,16},{16,8},{24,0},{1,25},{9,17},{17,9},{25,1},{2,26},{10... | collective-permute-start | bytes 491528 | tf_op jit(solution)/shard_map/ppermute | solution.py:403
  67.2 9.5 %collective-permute-start.13 = (f32[16,2560]{1,0:T(8,128)S(1)}, f32[16,2560]{1,0:T(8,128)S(1)}, u32[]{:S(2)}, u32[]{:S(2)}) collective-permute-start(f32[16,2560]{1,0:T(8,128)S(1)} %total.1.refs_0_), channel_id=1, source_target_pairs={{0,16},{8,24},{16,0},{24,8},{1,17},{9,25},{17,1},{25,9},{2,18},{10... | collective-permute-start | bytes 491528 | tf_op jit(solution)/shard_map/ppermute | solution.py:403
  68.7 8.0 %collective-permute-start.12 = (f32[16,2560]{1,0:T(8,128)S(1)}, f32[16,2560]{1,0:T(8,128)S(1)}, u32[]{:S(2)}, u32[]{:S(2)}) collective-permute-start(f32[16,2560]{1,0:T(8,128)S(1)} %total.1.refs_0_), channel_id=1, source_target_pairs={{0,8},{8,0},{16,24},{24,16},{1,9},{9,1},{17,25},{25,17},{2,10},{10... | collective-permute-start | bytes 491528 | tf_op jit(solution)/shard_map/ppermute | solution.py:403

commit v12 on v11

--- a/solution.py
+++ b/solution.py
@@ -32,6 +32,14 @@
     return lax.dot_general(a, b, (((0,), (0,)), ((), ())), preferred_element_type=f32)
 
 
+def over(value, n):
+    return value >> (n.bit_length() - 1) if n & (n - 1) == 0 else value // n
+
+
+def rest(value, n):
+    return value & (n - 1) if n & (n - 1) == 0 else value % n
+
+
 def standardize(x):
     centered = x - jnp.mean(x, axis=-1, keepdims=True)
     inv = lax.rsqrt(jnp.mean(centered * centered, axis=-1, keepdims=True) + norm_eps)
@@ -47,9 +55,8 @@
     chips = rows // 2
     piece = width // (rows * dp)
     at = lax.broadcasted_iota(jnp.int32, (width, 1), 0)
-    side, rest = at // (width // 2), at % (width // 2)
-    part, rest = rest // (chips * piece), rest % (chips * piece)
-    chip, row = rest // piece, rest % piece
+    side, part = over(at, width // 2), rest(over(at, chips * piece), dp)
+    chip, row = rest(over(at, piece), chips), rest(at, piece)
     core = lax.rem(lax.axis_index("rows"), 2)
     core = jnp.where(side == 0, core, 1 - core)
     wanted = ((chip * 2 + core) * dp + part) * piece + row
@@ -59,7 +66,7 @@
 def forward_kernel(rows_size, dp_size, len_ref, ev_hbm, cot_hbm, win_hbm, wout_hbm,
                    keep_ref, send_ref, hid_ref, dsilu_ref, gatt_ref, gpre_ref, normed_t_ref,
                    ev_ref, cot_ref, win_ref, normed_ref, user_ref, duser_ref, att_ref, mixed_ref, masked_ref, dval_ref, weights_ref,
-                   wout_ref, arrived):
+                   wout_ref, order_ref, arrived):
     tokens, width = ev_ref.shape
     copies = [pltpu.make_async_copy(ev_hbm, ev_ref, arrived.at[0])]
     for c in range(4):
@@ -69,6 +76,7 @@
     copies.append(pltpu.make_async_copy(wout_hbm, wout_ref, arrived.at[6]))
     for copy in copies:
         copy.start()
+    order_ref[...] = owner_order(width, rows_size, dp_size)
     hd = width // HEADS
     length = len_ref[0]
     inv_len = 1.0 / length.astype(f32)
@@ -145,7 +153,7 @@
             grad_v = dot_tn(weights_ref[h, rest, keys], gatt_ref[rest, v_cols])
             gpre_ref[keys, width + h * hd:width + (h + 1) * hd] = (grad_v * dval_ref[keys, v_cols]).astype(bf16)
 
-    order = owner_order(width, rows_size, dp_size)
+    order = order_ref[...]
     normed_t_ref[...] = dot_nt(order, normed_ref[...]).astype(bf16)
     mixed_t = dot_nt(order, mixed_ref[...]).astype(bf16)
     half = width // 2
@@ -161,6 +169,7 @@
     scale = hd ** -0.5
     steps = tokens // STEP
 
+    factor = 0.5 * inv_len * scale
     tri = lax.broadcasted_iota(jnp.int32, (STEP, STEP), 0) <= lax.broadcasted_iota(jnp.int32, (STEP, STEP), 1)
     for h in range(HEADS):
         v_cols = slice(h * hd, (h + 1) * hd)
@@ -175,20 +184,19 @@
                 rows = pl.ds(i * STEP, STEP)
                 query, gatt = hid_ref[rows, q_cols], gatt_ref[rows, v_cols]
                 half = dot_nt(key, query) * (0.5 * scale)
-                sig2 = 1.0 + jnp.tanh(half)
-                silu = half * sig2
-                dsilu = sig2 * ((1.0 + half) + (half - silu))
-                gscore = dot_nt(value, gatt) * dsilu * (0.5 * inv_len * scale)
+                gate = jnp.tanh(half)
+                dsilu = (1.0 + gate) * (1.0 + half * (1.0 - gate))
+                gscore = dot_nt(value, gatt) * dsilu
                 if i == j:
                     gscore = jnp.where(tri, gscore, 0.0)
                 gscore = gscore.astype(bf16)
                 pk, pq = dot_nn(gscore, query), dot_tn(gscore, key)
                 grad_k = pk if grad_k is None else grad_k + pk
                 grad_q[i] = pq if grad_q[i] is None else grad_q[i] + pq
-            gpre_ref[keys, q_cols] = (grad_k * dsilu_ref[keys, q_cols].astype(f32)).astype(bf16)
+            gpre_ref[keys, q_cols] = (grad_k * (dsilu_ref[keys, q_cols].astype(f32) * factor)).astype(bf16)
         for i in range(steps):
             rows = pl.ds(i * STEP, STEP)
-            gpre_ref[rows, v_cols] = (grad_q[i] * dsilu_ref[rows, v_cols].astype(f32)).astype(bf16)
+            gpre_ref[rows, v_cols] = (grad_q[i] * (dsilu_ref[rows, v_cols].astype(f32) * factor)).astype(bf16)
 
     half = width // 2
     for ref, start in ((send_ref, half), (keep_ref, 0)):
@@ -197,9 +205,9 @@
 
 def slots_in_order(position, capacity, dp, rows):
     chips = rows // 2
-    owner, place = position // capacity, position % capacity
-    ahead, core, part = owner // (2 * dp), (owner // dp) % 2, owner % dp
-    chip = (lax.axis_index("rows") // 2 + ahead) % chips
+    owner, place = over(position, capacity), rest(position, capacity)
+    ahead, core, part = over(owner, 2 * dp), rest(over(owner, dp), 2), rest(owner, dp)
+    chip = rest(lax.axis_index("rows") // 2 + ahead, chips)
     return part * rows + chip * 2 + core, place
 
 
@@ -239,7 +247,7 @@
 
 def whole_numbers(values, chosen, mine):
     pick = jnp.where(chosen, 1.0, 0.0).astype(bf16)
-    found = 16.0 * dot_nn((values // 16).astype(bf16), pick) + dot_nn((values % 16).astype(bf16), pick)
+    found = 16.0 * dot_nn(over(values, 16).astype(bf16), pick) + dot_nn(rest(values, 16).astype(bf16), pick)
     return jnp.sum(jnp.where(mine, found, 0.0), axis=0, keepdims=True)
 
 
@@ -294,9 +302,9 @@
                 rows_ref[at:at + capacity, t * LANES:(t + 1) * LANES] = ref[(i * tiles + t) * capacity:(i * tiles + t + 1) * capacity, :]
         values = ref[sources * tiles * capacity:, :].astype(jnp.int32)
         position = lax.broadcasted_iota(jnp.int32, (1, count), 1)
-        source, place = position // capacity, position % capacity
-        part, ahead = source // chips, source % chips
-        lane = ahead * (2 * dp * capacity) % LANES + block * capacity + place
+        source, place = over(position, capacity), rest(position, capacity)
+        part, ahead = over(source, chips), rest(source, chips)
+        lane = rest(ahead * (2 * dp * capacity), LANES) + block * capacity + place
         chosen = lax.broadcasted_iota(jnp.int32, (LANES, count), 0) == lane
         mine = lax.broadcasted_iota(jnp.int32, (values.shape[0], count), 0) == part * id_rows(chips) + ahead
         ids.append(whole_numbers(values, chosen, mine))
@@ -426,7 +434,7 @@
         (lengths, events, cotangent, w_in, w_out), 1,
         [((tokens, width), bf16), ((tokens, width), bf16), ((tokens, width), f32), ((tokens, width), f32),
          ((tokens, width), bf16), ((tokens, width), bf16), ((tokens, width), f32), ((HEADS, tokens, tokens), bf16),
-         (w_out.shape, bf16)], far=4, long=True, grant=16)
+         (w_out.shape, bf16), ((width, width), bf16)], far=4, long=True, grant=16)
     recv1 = lax.ppermute(send1, "rows", cores)
     keep2, send2, gpre_qk = call(
         attention_kernel, "attention_part", sides(2 * width) + [local(tokens, 2 * width, dtype=bf16)],

time: 77.8 us -> 78 us (level)
  transfers between devices with their start and end apart: 19 -> 19, of which waited for: 11 -> 12; matrix products, arithmetic and copies ran while one was open for 0% -> 0% of each run, Pallas kernels for 12% -> 12%
where the time goes in v12:
time: 78 us; the launch traced here: 77.2 us
  waiting for transfers between devices  33.5 us (43%)
  starting transfers between devices  23.8 us (31%)
  Pallas kernels  18.5 us (24%)
  between operations  1.37 us (2%)
    ppermute x10, waiting for transfers between devices, body(): lax.ppermute(v, 'dp', [(i, i ^ bit) for i in range(dp_size)])  22.5 us
    pallas_call x11, Pallas kernels, call(): pl.pallas_call(kernel, name=name, in_specs=[pl.BlockSpec(memory_space=p o...  18.5 us
    ppermute x10, starting transfers between devices, body(): lax.ppermute(v, 'dp', [(i, i ^ bit) for i in range(dp_size)])  12 us
    ppermute x6, starting transfers between devices, body(): lax.ppermute(v, 'rows', [(i, (i + 2 * k) % rows_size) for i in range(rows...  11.1 us
    ppermute x6, waiting for transfers between devices, body(): lax.ppermute(v, 'rows', [(i, (i + 2 * k) % rows_size) for i in range(rows...  10.9 us
  transfers between devices with their start and end apart: 19, of which 12 were waited for; matrix products, arithmetic and copies ran while one was open for 0% of the time, Pallas kernels for 12%

profile of v12, /device:TPU:0, one launch (start us, length us, event | category | flops | bytes accessed | tf_op | source)
XLA Modules:
  0.0 77.2 jit_solution(10846506373232884836)
XLA Ops:
  1.3 8.2 %forward_part.1 = (f32[256,1536]{1,0:T(8,128)S(1)}, f32[256,1536]{1,0:T(8,128)S(1)}, bf16[512,1536]{1,0:T(8,128)(2,1)S(1)}, bf16[512,1024]{1,0:T(8,128)(2,1)S(1)...) custom-call(s32[1]{0:T(128)S(6)} %copy.13.len_ref, ...), custom_call_target="tpu_custom_call" | custom-call | flops 99999997952 | bytes 65536 | tf_op jit(solution)/shard_map/forward_part/pallas_call | solution.py:393
  9.5 0.5 collective-permute-start
  10.0 0.0 copy-start.1
  10.0 0.0 copy-start.2
  10.0 3.8 %attention_part.1 = (f32[256,1024]{1,0:T(8,128)S(1)}, f32[256,1024]{1,0:T(8,128)S(1)}, bf16[512,1024]{1,0:T(8,128)(2,1)S(1)}) custom-call(s32[1]{0:T(128)S(6)} %copy.13.len_ref, bf16[512,1536]{1,0:T(8,128)(2,1)S(1)} %get-tuple-element.56.hid_ref, bf16[512,1024]{1,0:T(8,128)(2,1)S(1)} %get-tuple-element.57.dsilu_ref, ...), custom_call_target="tpu_custom_call" | custom-call | flops 99999997952 | bytes 65536 | tf_op jit(solution)/shard_map/attention_part/pallas_call | solution.py:393
  13.8 0.1 collective-permute-start.1
  13.9 0.0 collective-permute-done
  13.9 0.0 copy-done.1
  13.9 0.0 copy-done.2
  13.9 2.5 %events_part.1 = (f32[520,128]{1,0:T(8,128)S(1)}, f32[520,128]{1,0:T(8,128)S(1)}, f32[520,128]{1,0:T(8,128)S(1)}, f32[520,128]{1,0:T(8,128)S(1)}) custom-call(s32[1]{0:T(128)S(6)} %copy.13.len_ref, bf16[512,512]{1,0:T(8,128)(2,1)S(1)} %get-tuple-element.50.ev_ref, bf16[512,512]{1,0:T(8,128)(2,1)S(1)} %get-tuple-element.51.cot_ref, ...), custom_call_target="tpu_custom_call" | custom-call | flops 99999997952 | bytes 65536 | tf_op jit(solution)/shard_map/events_part/pallas_call | solution.py:393
  16.4 0.1 collective-permute-done.1
  16.5 0.3 first_sums.1
  16.8 2.9 %collective-permute-start.2 = (f32[2,64,1280]{2,1,0:T(8,128)S(1)}, f32[2,64,1280]{2,1,0:T(8,128)S(1)}, u32[]{:S(2)}, u32[]{:S(2)}) collective-permute-start(f32[2,64,1280]{2,1,0:T(8,128)S(1)} %get-tuple-element.69), channel_id=1, source_target_pairs={{0,8},{8,0},{16,24},{24,16},{1,9},{9,1},{17,25},{25,17},{2,10},{10... | collective-permute-start | bytes 1966088 | tf_op jit(solution)/shard_map/ppermute | solution.py:411
  19.7 1.5 %collective-permute-start.3 = (f32[2,64,1280]{2,1,0:T(8,128)S(1)}, f32[2,64,1280]{2,1,0:T(8,128)S(1)}, u32[]{:S(2)}, u32[]{:S(2)}) collective-permute-start(f32[2,64,1280]{2,1,0:T(8,128)S(1)} %get-tuple-element.71), channel_id=1, source_target_pairs={{0,16},{8,24},{16,0},{24,8},{1,17},{9,25},{17,1},{25,9},{2,18},{10... | collective-permute-start | bytes 1966088 | tf_op jit(solution)/shard_map/ppermute | solution.py:411
  21.2 1.6 %collective-permute-start.4 = (f32[520,128]{1,0:T(8,128)S(1)}, f32[520,128]{1,0:T(8,128)S(1)}, u32[]{:S(2)}, u32[]{:S(2)}) collective-permute-start(f32[520,128]{1,0:T(8,128)S(1)} %get-tuple-element.62), channel_id=1, source_target_pairs={{0,2},{1,3},{2,4},{3,5},{4,6},{5,7},{6,0},{7,1},{8,10},{9,11},{10,... | collective-permute-start | bytes 798728 | tf_op jit(solution)/shard_map/ppermute | solution.py:450
  22.8 2.6 %collective-permute-start.5 = (f32[520,128]{1,0:T(8,128)S(1)}, f32[520,128]{1,0:T(8,128)S(1)}, u32[]{:S(2)}, u32[]{:S(2)}) collective-permute-start(f32[520,128]{1,0:T(8,128)S(1)} %get-tuple-element.63), channel_id=1, source_target_pairs={{0,4},{1,5},{2,6},{3,7},{4,0},{5,1},{6,2},{7,3},{8,12},{9,13},{10,... | collective-permute-start | bytes 798728 | tf_op jit(solution)/shard_map/ppermute | solution.py:450
  25.4 1.3 %collective-permute-start.6 = (f32[520,128]{1,0:T(8,128)S(1)}, f32[520,128]{1,0:T(8,128)S(1)}, u32[]{:S(2)}, u32[]{:S(2)}) collective-permute-start(f32[520,128]{1,0:T(8,128)S(1)} %get-tuple-element.64), channel_id=1, source_target_pairs={{0,6},{1,7},{2,0},{3,1},{4,2},{5,3},{6,4},{7,5},{8,14},{9,15},{10,... | collective-permute-start | bytes 798728 | tf_op jit(solution)/shard_map/ppermute | solution.py:450
  26.8 8.0 %collective-permute-done.2.from_x_ref = f32[2,64,1280]{2,1,0:T(8,128)S(1)} collective-permute-done((f32[2,64,1280]{2,1,0:T(8,128)S(1)}, f32[2,64,1280]{2,1,0:T(8,128)S(1)}, u32[]{:S(2)}, u32[]{:S(2)}) %collective-permute-start.2) | collective-permute-done | bytes 655392 | tf_op jit(solution)/shard_map/ppermute | solution.py:411
  34.8 1.5 %collective-permute-done.3.from_y_ref = f32[2,64,1280]{2,1,0:T(8,128)S(1)} collective-permute-done((f32[2,64,1280]{2,1,0:T(8,128)S(1)}, f32[2,64,1280]{2,1,0:T(8,128)S(1)}, u32[]{:S(2)}, u32[]{:S(2)}) %collective-permute-start.3) | collective-permute-done | bytes 655392 | tf_op jit(solution)/shard_map/ppermute | solution.py:411
  36.2 0.1 second_sums.1
  36.4 1.6 %collective-permute-start.7 = (f32[64,1280]{1,0:T(8,128)S(1)}, f32[64,1280]{1,0:T(8,128)S(1)}, u32[]{:S(2)}, u32[]{:S(2)}) collective-permute-start(f32[64,1280]{1,0:T(8,128)S(1)} %get-tuple-element.73), channel_id=1, source_target_pairs={{0,16},{8,24},{16,0},{24,8},{1,17},{9,25},{17,1},{25,9},{2,18},{10... | collective-permute-start | bytes 983048 | tf_op jit(solution)/shard_map/ppermute | solution.py:411
  37.9 0.5 collective-permute-start.8
  38.5 0.0 collective-permute-done.4.refs_1_
  38.5 4.0 %collective-permute-done.5.refs_2_ = f32[520,128]{1,0:T(8,128)S(1)} collective-permute-done((f32[520,128]{1,0:T(8,128)S(1)}, f32[520,128]{1,0:T(8,128)S(1)}, u32[]{:S(2)}, u32[]{:S(2)}) %collective-permute-start.5) | collective-permute-done | bytes 266272 | tf_op jit(solution)/shard_map/ppermute | solution.py:450
  42.5 0.0 collective-permute-done.6.refs_3_
  42.5 0.1 by_part.1
  42.6 2.4 %collective-permute-done.7 = f32[64,1280]{1,0:T(8,128)S(1)} collective-permute-done((f32[64,1280]{1,0:T(8,128)S(1)}, f32[64,1280]{1,0:T(8,128)S(1)}, u32[]{:S(2)}, u32[]{:S(2)}) %collective-permute-start.7) | collective-permute-done | bytes 327712 | tf_op jit(solution)/shard_map/ppermute | solution.py:411
  45.0 1.2 %collective-permute-done.8 = f32[64,1280]{1,0:T(8,128)S(1)} collective-permute-done((f32[64,1280]{1,0:T(8,128)S(1)}, f32[64,1280]{1,0:T(8,128)S(1)}, u32[]{:S(2)}, u32[]{:S(2)}) %collective-permute-start.8) | collective-permute-done | bytes 327712 | tf_op jit(solution)/shard_map/ppermute | solution.py:411
  46.3 0.1 chip_sums.1
  46.4 2.6 %collective-permute-start.9 = (f32[16,2560]{1,0:T(8,128)S(1)}, f32[16,2560]{1,0:T(8,128)S(1)}, u32[]{:S(2)}, u32[]{:S(2)}) collective-permute-start(f32[16,2560]{1,0:T(8,128)S(1)} %get-tuple-element.83), channel_id=1, source_target_pairs={{0,2},{1,3},{2,4},{3,5},{4,6},{5,7},{6,0},{7,1},{8,10},{9,11},{10,... | collective-permute-start | bytes 491528 | tf_op jit(solution)/shard_map/ppermute | solution.py:450
  49.0 1.6 %collective-permute-start.10 = (f32[16,2560]{1,0:T(8,128)S(1)}, f32[16,2560]{1,0:T(8,128)S(1)}, u32[]{:S(2)}, u32[]{:S(2)}) collective-permute-start(f32[16,2560]{1,0:T(8,128)S(1)} %get-tuple-element.84), channel_id=1, source_target_pairs={{0,4},{1,5},{2,6},{3,7},{4,0},{5,1},{6,2},{7,3},{8,12},{9,13},{10,... | collective-permute-start | bytes 491528 | tf_op jit(solution)/shard_map/ppermute | solution.py:450
  50.6 1.3 %collective-permute-start.11 = (f32[16,2560]{1,0:T(8,128)S(1)}, f32[16,2560]{1,0:T(8,128)S(1)}, u32[]{:S(2)}, u32[]{:S(2)}) collective-permute-start(f32[16,2560]{1,0:T(8,128)S(1)} %get-tuple-element.85), channel_id=1, source_target_pairs={{0,6},{1,7},{2,0},{3,1},{4,2},{5,3},{6,4},{7,5},{8,14},{9,15},{10,... | collective-permute-start | bytes 491528 | tf_op jit(solution)/shard_map/ppermute | solution.py:450
  51.9 0.6 collective-permute-start.15
  52.5 0.5 collective-permute-start.16
  53.0 2.1 %collective-permute-done.9.refs_1_ = f32[16,2560]{1,0:T(8,128)S(1)} collective-permute-done((f32[16,2560]{1,0:T(8,128)S(1)}, f32[16,2560]{1,0:T(8,128)S(1)}, u32[]{:S(2)}, u32[]{:S(2)}) %collective-permute-start.9) | collective-permute-done | bytes 163872 | tf_op jit(solution)/shard_map/ppermute | solution.py:450
  55.2 0.8 collective-permute-start.17
  56.0 4.7 %collective-permute-done.10.refs_2_ = f32[16,2560]{1,0:T(8,128)S(1)} collective-permute-done((f32[16,2560]{1,0:T(8,128)S(1)}, f32[16,2560]{1,0:T(8,128)S(1)}, u32[]{:S(2)}, u32[]{:S(2)}) %collective-permute-start.10) | collective-permute-done | bytes 163872 | tf_op jit(solution)/shard_map/ppermute | solution.py:450
  60.7 0.0 collective-permute-done.11.refs_3_
  60.7 0.0 copy-start
  60.7 0.0 copy-start.3
  60.7 0.6 collective-permute-done.15.refs_1_
  61.3 3.8 %collective-permute-done.16.refs_2_ = f32[520,128]{1,0:T(8,128)S(1)} collective-permute-done((f32[520,128]{1,0:T(8,128)S(1)}, f32[520,128]{1,0:T(8,128)S(1)}, u32[]{:S(2)}, u32[]{:S(2)}) %collective-permute-start.16) | collective-permute-done | bytes 266272 | tf_op jit(solution)/shard_map/ppermute | solution.py:411
  65.1 0.0 collective-permute-done.17.refs_3_
  65.1 0.1 by_core.1
  65.2 0.1 collective-permute-start.18
  65.3 1.5 %collective-permute-start.14 = (f32[16,2560]{1,0:T(8,128)S(1)}, f32[16,2560]{1,0:T(8,128)S(1)}, u32[]{:S(2)}, u32[]{:S(2)}) collective-permute-start(f32[16,2560]{1,0:T(8,128)S(1)} %total.1.refs_0_), channel_id=1, source_target_pairs={{0,24},{8,16},{16,8},{24,0},{1,25},{9,17},{17,9},{25,1},{2,26},{10... | collective-permute-start | bytes 491528 | tf_op jit(solution)/shard_map/ppermute | solution.py:411
  66.8 1.5 %collective-permute-start.13 = (f32[16,2560]{1,0:T(8,128)S(1)}, f32[16,2560]{1,0:T(8,128)S(1)}, u32[]{:S(2)}, u32[]{:S(2)}) collective-permute-start(f32[16,2560]{1,0:T(8,128)S(1)} %total.1.refs_0_), channel_id=1, source_target_pairs={{0,16},{8,24},{16,0},{24,8},{1,17},{9,25},{17,1},{25,9},{2,18},{10... | collective-permute-start | bytes 491528 | tf_op jit(solution)/shard_map/ppermute | solution.py:411
  68.3 0.5 collective-permute-start.12
  68.8 0.0 collective-permute-done.18.recv_ref
  68.8 0.0 copy-done
  68.8 0.0 copy-done.3
  68.8 2.5 %table_part.1 = (f32[512,512]{1,0:T(8,128)}, f32[512]{0:T(512)}) custom-call(f32[1056,128]{1,0:T(8,128)S(1)} %get-tuple-element.87.keep_ref, f32[1056,128]{1,0:T(8,128)S(1)} %collective-permute-done.18.recv_ref, f32[512,512]{1,0:T(8,128)S(1)} %copy-done, f32[512]{0:T(512)S(1)} %copy-done.3), custom_call_target="tpu_custom_call" | custom-call | flops 1000000000 | bytes 65536 | tf_op jit(solution)/shard_map/table_part/pallas_call | solution.py:393
  71.3 1.9 %collective-permute-done.14.refs_3_ = f32[16,2560]{1,0:T(8,128)S(1)} collective-permute-done((f32[16,2560]{1,0:T(8,128)S(1)}, f32[16,2560]{1,0:T(8,128)S(1)}, u32[]{:S(2)}, u32[]{:S(2)}) %collective-permute-start.14) | collective-permute-done | bytes 163872 | tf_op jit(solution)/shard_map/ppermute | solution.py:411
  73.3 3.0 %collective-permute-done.13.refs_2_ = f32[16,2560]{1,0:T(8,128)S(1)} collective-permute-done((f32[16,2560]{1,0:T(8,128)S(1)}, f32[16,2560]{1,0:T(8,128)S(1)}, u32[]{:S(2)}, u32[]{:S(2)}) %collective-permute-start.13) | collective-permute-done | bytes 163872 | tf_op jit(solution)/shard_map/ppermute | solution.py:411
  76.3 0.0 collective-permute-done.12.refs_1_
  76.3 0.9 %gather.1 = (f32[4,16,2048]{2,1,0:T(8,128)}, f32[4,16,512]{2,1,0:T(8,128)}) custom-call(f32[16,2560]{1,0:T(8,128)S(1)} %total.1.refs_0_, f32[16,2560]{1,0:T(8,128)S(1)} %collective-permute-done.12.refs_1_, f32[16,2560]{1,0:T(8,128)S(1)} %collective-permute-done.13.refs_2_, f32[16,2560]{1,0:T(8,128)S(1)} %collective-permute-done.14.refs_3_), custom_call_target="tpu_custom_call" | custom-call | flops 1000000000 | bytes 65536 | tf_op jit(solution)/shard_map/gather/pallas_call | solution.py:393
  (1 shorter events, 0.0 us)
Async XLA Ops:
  9.5 4.5 %collective-permute-start = (f32[256,1536]{1,0:T(8,128)S(1)}, f32[256,1536]{1,0:T(8,128)S(1)}, u32[]{:S(2)}, u32[]{:S(2)}) collective-permute-start(f32[256,1536]{1,0:T(8,128)S(1)} %get-tuple-element.54), channel_id=1, source_target_pairs={{0,1},{1,0},{2,3},{3,2},{4,5},{5,4},{6,7},{7,6},{8,9},{9,8},{10,11... | collective-permute-start | bytes 4718600 | tf_op jit(solution)/shard_map/ppermute | solution.py:438
  10.0 4.0 %copy-start.1 = (s32[1,32,16]{1,2,0:T(8,128)S(1)}, s32[1,32,16]{1,2,0:T(8,128)}, u32[]{:S(2)}) copy-start(s32[1,32,16]{1,2,0:T(8,128)} %param.14) | copy-start | bytes 6148
  10.0 4.0 %copy-start.2 = (s32[1,512]{1,0:T(1,128)S(1)}, s32[1,512]{1,0:T(1,128)}, u32[]{:S(2)}) copy-start(s32[1,512]{1,0:T(1,128)} %slot_ref.1) | copy-start | bytes 6148
  13.8 2.7 %collective-permute-start.1 = (f32[256,1024]{1,0:T(8,128)S(1)}, f32[256,1024]{1,0:T(8,128)S(1)}, u32[]{:S(2)}, u32[]{:S(2)}) collective-permute-start(f32[256,1024]{1,0:T(8,128)S(1)} %get-tuple-element.67), channel_id=1, source_target_pairs={{0,1},{1,0},{2,3},{3,2},{4,5},{5,4},{6,7},{7,6},{8,9},{9,8},{10,11... | collective-permute-start | bytes 3145736 | tf_op jit(solution)/shard_map/ppermute | solution.py:442
  16.8 18.0 %collective-permute-start.2 = (f32[2,64,1280]{2,1,0:T(8,128)S(1)}, f32[2,64,1280]{2,1,0:T(8,128)S(1)}, u32[]{:S(2)}, u32[]{:S(2)}) collective-permute-start(f32[2,64,1280]{2,1,0:T(8,128)S(1)} %get-tuple-element.69), channel_id=1, source_target_pairs={{0,8},{8,0},{16,24},{24,16},{1,9},{9,1},{17,25},{25,17},{2,10},{10... | collective-permute-start | bytes 1966088 | tf_op jit(solution)/shard_map/ppermute | solution.py:411
  19.7 16.5 %collective-permute-start.3 = (f32[2,64,1280]{2,1,0:T(8,128)S(1)}, f32[2,64,1280]{2,1,0:T(8,128)S(1)}, u32[]{:S(2)}, u32[]{:S(2)}) collective-permute-start(f32[2,64,1280]{2,1,0:T(8,128)S(1)} %get-tuple-element.71), channel_id=1, source_target_pairs={{0,16},{8,24},{16,0},{24,8},{1,17},{9,25},{17,1},{25,9},{2,18},{10... | collective-permute-start | bytes 1966088 | tf_op jit(solution)/shard_map/ppermute | solution.py:411
  21.2 17.3 %collective-permute-start.4 = (f32[520,128]{1,0:T(8,128)S(1)}, f32[520,128]{1,0:T(8,128)S(1)}, u32[]{:S(2)}, u32[]{:S(2)}) collective-permute-start(f32[520,128]{1,0:T(8,128)S(1)} %get-tuple-element.62), channel_id=1, source_target_pairs={{0,2},{1,3},{2,4},{3,5},{4,6},{5,7},{6,0},{7,1},{8,10},{9,11},{10,... | collective-permute-start | bytes 798728 | tf_op jit(solution)/shard_map/ppermute | solution.py:450
  22.8 19.7 %collective-permute-start.5 = (f32[520,128]{1,0:T(8,128)S(1)}, f32[520,128]{1,0:T(8,128)S(1)}, u32[]{:S(2)}, u32[]{:S(2)}) collective-permute-start(f32[520,128]{1,0:T(8,128)S(1)} %get-tuple-element.63), channel_id=1, source_target_pairs={{0,4},{1,5},{2,6},{3,7},{4,0},{5,1},{6,2},{7,3},{8,12},{9,13},{10,... | collective-permute-start | bytes 798728 | tf_op jit(solution)/shard_map/ppermute | solution.py:450
  25.4 17.1 %collective-permute-start.6 = (f32[520,128]{1,0:T(8,128)S(1)}, f32[520,128]{1,0:T(8,128)S(1)}, u32[]{:S(2)}, u32[]{:S(2)}) collective-permute-start(f32[520,128]{1,0:T(8,128)S(1)} %get-tuple-element.64), channel_id=1, source_target_pairs={{0,6},{1,7},{2,0},{3,1},{4,2},{5,3},{6,4},{7,5},{8,14},{9,15},{10,... | collective-permute-start | bytes 798728 | tf_op jit(solution)/shard_map/ppermute | solution.py:450
  36.4 8.7 %collective-permute-start.7 = (f32[64,1280]{1,0:T(8,128)S(1)}, f32[64,1280]{1,0:T(8,128)S(1)}, u32[]{:S(2)}, u32[]{:S(2)}) collective-permute-start(f32[64,1280]{1,0:T(8,128)S(1)} %get-tuple-element.73), channel_id=1, source_target_pairs={{0,16},{8,24},{16,0},{24,8},{1,17},{9,25},{17,1},{25,9},{2,18},{10... | collective-permute-start | bytes 983048 | tf_op jit(solution)/shard_map/ppermute | solution.py:411
  37.9 8.3 %collective-permute-start.8 = (f32[64,1280]{1,0:T(8,128)S(1)}, f32[64,1280]{1,0:T(8,128)S(1)}, u32[]{:S(2)}, u32[]{:S(2)}) collective-permute-start(f32[64,1280]{1,0:T(8,128)S(1)} %get-tuple-element.74), channel_id=1, source_target_pairs={{0,8},{8,0},{16,24},{24,16},{1,9},{9,1},{17,25},{25,17},{2,10},{10... | collective-permute-start | bytes 983048 | tf_op jit(solution)/shard_map/ppermute | solution.py:411
  46.4 8.8 %collective-permute-start.9 = (f32[16,2560]{1,0:T(8,128)S(1)}, f32[16,2560]{1,0:T(8,128)S(1)}, u32[]{:S(2)}, u32[]{:S(2)}) collective-permute-start(f32[16,2560]{1,0:T(8,128)S(1)} %get-tuple-element.83), channel_id=1, source_target_pairs={{0,2},{1,3},{2,4},{3,5},{4,6},{5,7},{6,0},{7,1},{8,10},{9,11},{10,... | collective-permute-start | bytes 491528 | tf_op jit(solution)/shard_map/ppermute | solution.py:450
  49.0 11.7 %collective-permute-start.10 = (f32[16,2560]{1,0:T(8,128)S(1)}, f32[16,2560]{1,0:T(8,128)S(1)}, u32[]{:S(2)}, u32[]{:S(2)}) collective-permute-start(f32[16,2560]{1,0:T(8,128)S(1)} %get-tuple-element.84), channel_id=1, source_target_pairs={{0,4},{1,5},{2,6},{3,7},{4,0},{5,1},{6,2},{7,3},{8,12},{9,13},{10,... | collective-permute-start | bytes 491528 | tf_op jit(solution)/shard_map/ppermute | solution.py:450
  50.6 10.1 %collective-permute-start.11 = (f32[16,2560]{1,0:T(8,128)S(1)}, f32[16,2560]{1,0:T(8,128)S(1)}, u32[]{:S(2)}, u32[]{:S(2)}) collective-permute-start(f32[16,2560]{1,0:T(8,128)S(1)} %get-tuple-element.85), channel_id=1, source_target_pairs={{0,6},{1,7},{2,0},{3,1},{4,2},{5,3},{6,4},{7,5},{8,14},{9,15},{10,... | collective-permute-start | bytes 491528 | tf_op jit(solution)/shard_map/ppermute | solution.py:450
  51.9 9.3 %collective-permute-start.15 = (f32[520,128]{1,0:T(8,128)S(1)}, f32[520,128]{1,0:T(8,128)S(1)}, u32[]{:S(2)}, u32[]{:S(2)}) collective-permute-start(f32[520,128]{1,0:T(8,128)S(1)} %get-tuple-element.77), channel_id=1, source_target_pairs={{0,8},{8,0},{16,24},{24,16},{1,9},{9,1},{17,25},{25,17},{2,10},{10... | collective-permute-start | bytes 798728 | tf_op jit(solution)/shard_map/ppermute | solution.py:411
  52.5 12.6 %collective-permute-start.16 = (f32[520,128]{1,0:T(8,128)S(1)}, f32[520,128]{1,0:T(8,128)S(1)}, u32[]{:S(2)}, u32[]{:S(2)}) collective-permute-start(f32[520,128]{1,0:T(8,128)S(1)} %get-tuple-element.78), channel_id=1, source_target_pairs={{0,16},{8,24},{16,0},{24,8},{1,17},{9,25},{17,1},{25,9},{2,18},{10... | collective-permute-start | bytes 798728 | tf_op jit(solution)/shard_map/ppermute | solution.py:411
  55.2 9.9 %collective-permute-start.17 = (f32[520,128]{1,0:T(8,128)S(1)}, f32[520,128]{1,0:T(8,128)S(1)}, u32[]{:S(2)}, u32[]{:S(2)}) collective-permute-start(f32[520,128]{1,0:T(8,128)S(1)} %get-tuple-element.79), channel_id=1, source_target_pairs={{0,24},{8,16},{16,8},{24,0},{1,25},{9,17},{17,9},{25,1},{2,26},{10... | collective-permute-start | bytes 798728 | tf_op jit(solution)/shard_map/ppermute | solution.py:411
  60.7 8.1 %copy-start = (f32[512,512]{1,0:T(8,128)S(1)}, f32[512,512]{1,0:T(8,128)}, u32[]{:S(2)}) copy-start(f32[512,512]{1,0:T(8,128)} %table_ref.1) | copy-start | bytes 3145732
  60.7 8.1 %copy-start.3 = (f32[512]{0:T(512)S(1)}, f32[512]{0:T(512)}, u32[]{:S(2)}) copy-start(f32[512]{0:T(512)} %accum_ref.1) | copy-start | bytes 6148
  65.2 3.6 %collective-permute-start.18 = (f32[1056,128]{1,0:T(8,128)S(1)}, f32[1056,128]{1,0:T(8,128)S(1)}, u32[]{:S(2)}, u32[]{:S(2)}) collective-permute-start(f32[1056,128]{1,0:T(8,128)S(1)} %get-tuple-element.88), channel_id=1, source_target_pairs={{0,1},{1,0},{2,3},{3,2},{4,5},{5,4},{6,7},{7,6},{8,9},{9,8},{10,11... | collective-permute-start | bytes 1622024 | tf_op jit(solution)/shard_map/ppermute | solution.py:478
  65.3 8.0 %collective-permute-start.14 = (f32[16,2560]{1,0:T(8,128)S(1)}, f32[16,2560]{1,0:T(8,128)S(1)}, u32[]{:S(2)}, u32[]{:S(2)}) collective-permute-start(f32[16,2560]{1,0:T(8,128)S(1)} %total.1.refs_0_), channel_id=1, source_target_pairs={{0,24},{8,16},{16,8},{24,0},{1,25},{9,17},{17,9},{25,1},{2,26},{10... | collective-permute-start | bytes 491528 | tf_op jit(solution)/shard_map/ppermute | solution.py:411
  66.8 9.5 %collective-permute-start.13 = (f32[16,2560]{1,0:T(8,128)S(1)}, f32[16,2560]{1,0:T(8,128)S(1)}, u32[]{:S(2)}, u32[]{:S(2)}) collective-permute-start(f32[16,2560]{1,0:T(8,128)S(1)} %total.1.refs_0_), channel_id=1, source_target_pairs={{0,16},{8,24},{16,0},{24,8},{1,17},{9,25},{17,1},{25,9},{2,18},{10... | collective-permute-start | bytes 491528 | tf_op jit(solution)/shard_map/ppermute | solution.py:411
  68.3 8.0 %collective-permute-start.12 = (f32[16,2560]{1,0:T(8,128)S(1)}, f32[16,2560]{1,0:T(8,128)S(1)}, u32[]{:S(2)}, u32[]{:S(2)}) collective-permute-start(f32[16,2560]{1,0:T(8,128)S(1)} %total.1.refs_0_), channel_id=1, source_target_pairs={{0,8},{8,0},{16,24},{24,16},{1,9},{9,1},{17,25},{25,17},{2,10},{10... | collective-permute-start | bytes 491528 | tf_op jit(solution)/shard_map/ppermute | solution.py:411

commit v13 on v12

--- a/solution.py
+++ b/solution.py
@@ -66,7 +66,7 @@
 def forward_kernel(rows_size, dp_size, len_ref, ev_hbm, cot_hbm, win_hbm, wout_hbm,
                    keep_ref, send_ref, hid_ref, dsilu_ref, gatt_ref, gpre_ref, normed_t_ref,
                    ev_ref, cot_ref, win_ref, normed_ref, user_ref, duser_ref, att_ref, mixed_ref, masked_ref, dval_ref, weights_ref,
-                   wout_ref, order_ref, arrived):
+                   wout_ref, order_ref, grad_mixed_ref, arrived):
     tokens, width = ev_ref.shape
     copies = [pltpu.make_async_copy(ev_hbm, ev_ref, arrived.at[0])]
     for c in range(4):
@@ -111,6 +111,8 @@
         for i in range(steps):
             project(i, c)
 
+    copies[5].wait()
+    copies[6].wait()
     tri = lax.broadcasted_iota(jnp.int32, (STEP, STEP), 0) >= lax.broadcasted_iota(jnp.int32, (STEP, STEP), 1)
     for h in range(HEADS):
         v_cols = slice(h * hd, (h + 1) * hd)
@@ -131,16 +133,21 @@
                 part = dot_nn(weights, hid_ref[keys, v_cols])
                 total = part if total is None else total + part
             att_ref[rows, v_cols] = total
-
-    copies[5].wait()
-    copies[6].wait()
+        for i in range(h, steps, HEADS):
+            rows = pl.ds(i * STEP, STEP)
+            normed_t_ref[rows, :] = dot_nt(order_ref[rows, :], normed_ref[...]).astype(bf16)
+        for i in range(h - HEADS // 2, steps, HEADS):
+            if i >= 0:
+                rows = pl.ds(i * STEP, STEP)
+                masked_ref[rows, :] = masked_rows(cot_ref[rows, :], i * STEP, length).astype(bf16)
+                grad_mixed_ref[rows, :] = dot_nt(masked_ref[rows, :], wout_ref[...])
+
     for i in range(steps):
         rows = pl.ds(i * STEP, STEP)
-        masked_ref[rows, :] = masked_rows(cot_ref[rows, :], i * STEP, length).astype(bf16)
         ahat, inv = standardize(att_ref[rows, :])
         user = user_ref[rows, :].astype(f32)
         mixed_ref[rows, :] = (ahat * user).astype(bf16)
-        grad_mixed = dot_nt(masked_ref[rows, :], wout_ref[...])
+        grad_mixed = grad_mixed_ref[rows, :]
         gpre_ref[rows, :width] = (grad_mixed * ahat * duser_ref[rows, :]).astype(bf16)
         e = grad_mixed * user
         gatt_ref[rows, :] = (inv * (e - jnp.mean(e, axis=-1, keepdims=True)
@@ -153,9 +160,7 @@
             grad_v = dot_tn(weights_ref[h, rest, keys], gatt_ref[rest, v_cols])
             gpre_ref[keys, width + h * hd:width + (h + 1) * hd] = (grad_v * dval_ref[keys, v_cols]).astype(bf16)
 
-    order = order_ref[...]
-    normed_t_ref[...] = dot_nt(order, normed_ref[...]).astype(bf16)
-    mixed_t = dot_nt(order, mixed_ref[...]).astype(bf16)
+    mixed_t = dot_nt(order_ref[...], mixed_ref[...]).astype(bf16)
     half = width // 2
     for ref, start in ((send_ref, half), (keep_ref, 0)):
         ref[:, :width] = dot_nn(mixed_t[start:start + half], masked_ref[...])
@@ -347,21 +352,26 @@
     next_b_ref[...] = keep_b_ref[x] + from_y_ref[x]
 
 
-def chips_kernel(next_a_ref, from_y_ref, next_b_ref, from_x_ref, *out_refs):
-    chips = len(out_refs)
-    chip = lax.axis_index("rows") // 2
-    half = next_a_ref.shape[-1]
-    for k, out_ref in enumerate(out_refs):
-        at = lax.rem(chip + k, chips)
-        out_ref[:, :half] = next_a_ref[at] + from_y_ref[at]
-        out_ref[:, half:] = next_b_ref[at] + from_x_ref[at]
-
-
-def total_kernel(tokens, *refs):
-    total = refs[0][...]
-    for ref in refs[1:-1]:
-        total = total + ref[...]
-    refs[-1][...] = total * (1.0 / tokens)
+def halve(bit, send_ref, keep_ref, keep_in, recv_in):
+    mine = rest(lax.axis_index("rows") // 2 >> bit, 2)
+    for i in range(send_ref.shape[0]):
+        send_ref[i] = keep_in[2 * i + 1 - mine] + recv_in[2 * i + 1 - mine]
+        keep_ref[i] = keep_in[2 * i + mine] + recv_in[2 * i + mine]
+
+
+def chip_first_kernel(next_a_ref, from_y_ref, next_b_ref, from_x_ref, send_a_ref, keep_a_ref, send_b_ref, keep_b_ref):
+    halve(0, send_a_ref, keep_a_ref, next_a_ref, from_y_ref)
+    halve(0, send_b_ref, keep_b_ref, next_b_ref, from_x_ref)
+
+
+def chip_kernel(bit, keep_in, recv_in, send_ref, keep_ref):
+    halve(bit, send_ref, keep_ref, keep_in, recv_in)
+
+
+def total_kernel(tokens, keep_a_ref, recv_a_ref, keep_b_ref, recv_b_ref, out_ref):
+    half = keep_a_ref.shape[-1]
+    out_ref[:, :half] = (keep_a_ref[0] + recv_a_ref[0]) * (1.0 / tokens)
+    out_ref[:, half:] = (keep_b_ref[0] + recv_b_ref[0]) * (1.0 / tokens)
 
 
 def gather_kernel(*refs):
@@ -434,7 +444,7 @@
         (lengths, events, cotangent, w_in, w_out), 1,
         [((tokens, width), bf16), ((tokens, width), bf16), ((tokens, width), f32), ((tokens, width), f32),
          ((tokens, width), bf16), ((tokens, width), bf16), ((tokens, width), f32), ((HEADS, tokens, tokens), bf16),
-         (w_out.shape, bf16), ((width, width), bf16)], far=4, long=True, grant=16)
+         (w_out.shape, bf16), ((width, width), bf16), ((tokens, width), f32)], far=4, long=True, grant=16)
     recv1 = lax.ppermute(send1, "rows", cores)
     keep2, send2, gpre_qk = call(
         attention_kernel, "attention_part", sides(2 * width) + [local(tokens, 2 * width, dtype=bf16)],
@@ -463,18 +473,28 @@
         functools.partial(by_part_kernel, dp_size, block), "by_part",
         [local(2 * chips * block + id_rows(chips), LANES)] * dp_size, came, long=True)
     next_a = after(next_a, *parts)
-    sums = call(
-        chips_kernel, "chip_sums", [local(piece, cols)] * chips,
+    bits = chips.bit_length() - 1
+    over_chips = lambda v, bit: lax.ppermute(v, "rows", [(i, i ^ (2 << bit)) for i in range(rows_size)])
+    send_a, keep_a, send_b, keep_b = call(
+        chip_first_kernel, "chip_sums", [local(chips // 2, piece, cols // 2)] * 4,
         [by_chip(v) for v in (next_a, from_y, next_b, from_x)])
+    halves = [[keep_a, over_chips(send_a, 0)], [keep_b, over_chips(send_b, 0)]]
     parts = [parts[0]] + [over_dp(parts[k], k) for k in range(1, dp_size)]
-    sums = [sums[0]] + [ahead(sums[k], k) for k in range(1, chips)]
+    for bit in range(1, bits):
+        for i in range(2):
+            if i == 1:
+                halves[1][0] = after(halves[1][0], send, keep)
+            send, keep = call(
+                functools.partial(chip_kernel, bit), "chip_sums", [local(chips >> (bit + 1), piece, cols // 2)] * 2,
+                halves[i], long=False)
+            halves[i] = [keep, over_chips(send, bit)]
     (total,) = call(
-        functools.partial(total_kernel, tokens), "total", [local(piece, cols)], sums, long=True)
+        functools.partial(total_kernel, tokens), "total", [local(piece, cols)], halves[0] + halves[1], long=False)
     pieces = gathered(total)
     parts[0] = after(parts[0], total)
     keep, send = call(
         functools.partial(by_core_kernel, chips, block), "by_core",
-        [local(dp_size * (chips * block + id_rows(chips)), LANES)] * 2, parts, long=True)
+        [local(dp_size * (chips * block + id_rows(chips)), LANES)] * 2, parts, long=False)
     recv = lax.ppermute(send, "rows", cores)
     slots = owners * capacity
     table_new, accum_new = call(

time: 78 us -> 75.5 us (0.968)
  waiting for transfers between devices: 33.5 us -> 30.9 us
    ppermute x0 -> x4, waiting for transfers between devices: none -> 8.86 us  [body(): lax.ppermute(v, 'rows', [(i, i ^ 2 << bit) for i in range(rows_size)])]
    ppermute x6 -> x3, waiting for transfers between devices: 10.9 us -> 4.05 us  [body(): lax.ppermute(v, 'rows', [(i, (i + 2 * k) % rows_size) for i in range(rows...]
    ppermute x6 -> x3, starting transfers between devices: 11.1 us -> 5.51 us  [body(): lax.ppermute(v, 'rows', [(i, (i + 2 * k) % rows_size) for i in range(rows...]
    ppermute x0 -> x4, starting transfers between devices: none -> 4.67 us  [body(): lax.ppermute(v, 'rows', [(i, i ^ 2 << bit) for i in range(rows_size)])]
    ppermute x10, waiting for transfers between devices: 22.5 us -> 17.9 us  [body(): lax.ppermute(v, 'dp', [(i, i ^ bit) for i in range(dp_size)])]
    ppermute x10, starting transfers between devices: 12 us -> 13.6 us  [body(): lax.ppermute(v, 'dp', [(i, i ^ bit) for i in range(dp_size)])]
    pallas_call x11 -> x13, Pallas kernels: 18.5 us -> 18.5 us  [call(): pl.pallas_call(kernel, name=name, in_specs=[pl.BlockSpec(memory_space=p o...]
  transfers between devices with their start and end apart: 19 -> 20, of which waited for: 12 -> 12; matrix products, arithmetic and copies ran while one was open for 0% -> 0% of each run, Pallas kernels for 12% -> 12%
where the time goes in v13:
time: 75.5 us; the launch traced here: 75.4 us
  waiting for transfers between devices  30.9 us (41%)
  starting transfers between devices  24.5 us (32%)
  Pallas kernels  18.5 us (25%)
  between operations  1.41 us (2%)
    pallas_call x13, Pallas kernels, call(): pl.pallas_call(kernel, name=name, in_specs=[pl.BlockSpec(memory_space=p o...  18.5 us
    ppermute x10, waiting for transfers between devices, body(): lax.ppermute(v, 'dp', [(i, i ^ bit) for i in range(dp_size)])  17.9 us
    ppermute x10, starting transfers between devices, body(): lax.ppermute(v, 'dp', [(i, i ^ bit) for i in range(dp_size)])  13.6 us
    ppermute x4, waiting for transfers between devices, body(): lax.ppermute(v, 'rows', [(i, i ^ 2 << bit) for i in range(rows_size)])  8.86 us
    ppermute x3, starting transfers between devices, body(): lax.ppermute(v, 'rows', [(i, (i + 2 * k) % rows_size) for i in range(rows...  5.51 us
    ppermute x4, starting transfers between devices, body(): lax.ppermute(v, 'rows', [(i, i ^ 2 << bit) for i in range(rows_size)])  4.67 us
    ppermute x3, waiting for transfers between devices, body(): lax.ppermute(v, 'rows', [(i, (i + 2 * k) % rows_size) for i in range(rows...  4.05 us
  transfers between devices with their start and end apart: 20, of which 12 were waited for; matrix products, arithmetic and copies ran while one was open for 0% of the time, Pallas kernels for 12%

profile of v13, /device:TPU:0, one launch (start us, length us, event | category | flops | bytes accessed | tf_op | source)
XLA Modules:
  0.0 75.4 jit_solution(3502027671814849083)
XLA Ops:
  1.3 8.1 %forward_part.1 = (f32[256,1536]{1,0:T(8,128)S(1)}, f32[256,1536]{1,0:T(8,128)S(1)}, bf16[512,1536]{1,0:T(8,128)(2,1)S(1)}, bf16[512,1024]{1,0:T(8,128)(2,1)S(1)...) custom-call(s32[1]{0:T(128)S(6)} %copy.13.len_ref, ...), custom_call_target="tpu_custom_call" | custom-call | flops 99999997952 | bytes 65536 | tf_op jit(solution)/shard_map/forward_part/pallas_call | solution.py:403
  9.4 0.5 collective-permute-start
  10.0 0.0 copy-start.1
  10.0 0.0 copy-start.2
  10.0 3.8 %attention_part.1 = (f32[256,1024]{1,0:T(8,128)S(1)}, f32[256,1024]{1,0:T(8,128)S(1)}, bf16[512,1024]{1,0:T(8,128)(2,1)S(1)}) custom-call(s32[1]{0:T(128)S(6)} %copy.13.len_ref, bf16[512,1536]{1,0:T(8,128)(2,1)S(1)} %get-tuple-element.61.hid_ref, bf16[512,1024]{1,0:T(8,128)(2,1)S(1)} %get-tuple-element.62.dsilu_ref, ...), custom_call_target="tpu_custom_call" | custom-call | flops 99999997952 | bytes 65536 | tf_op jit(solution)/shard_map/attention_part/pallas_call | solution.py:403
  13.8 0.1 collective-permute-start.1
  13.9 0.0 collective-permute-done
  13.9 0.0 copy-done.1
  13.9 0.0 copy-done.2
  13.9 2.5 %events_part.1 = (f32[520,128]{1,0:T(8,128)S(1)}, f32[520,128]{1,0:T(8,128)S(1)}, f32[520,128]{1,0:T(8,128)S(1)}, f32[520,128]{1,0:T(8,128)S(1)}) custom-call(s32[1]{0:T(128)S(6)} %copy.13.len_ref, bf16[512,512]{1,0:T(8,128)(2,1)S(1)} %get-tuple-element.55.ev_ref, bf16[512,512]{1,0:T(8,128)(2,1)S(1)} %get-tuple-element.56.cot_ref, ...), custom_call_target="tpu_custom_call" | custom-call | flops 99999997952 | bytes 65536 | tf_op jit(solution)/shard_map/events_part/pallas_call | solution.py:403
  16.4 0.1 collective-permute-done.1
  16.5 0.3 first_sums.1
  16.8 2.9 %collective-permute-start.2 = (f32[2,64,1280]{2,1,0:T(8,128)S(1)}, f32[2,64,1280]{2,1,0:T(8,128)S(1)}, u32[]{:S(2)}, u32[]{:S(2)}) collective-permute-start(f32[2,64,1280]{2,1,0:T(8,128)S(1)} %get-tuple-element.74), channel_id=1, source_target_pairs={{0,8},{8,0},{16,24},{24,16},{1,9},{9,1},{17,25},{25,17},{2,10},{10... | collective-permute-start | bytes 1966088 | tf_op jit(solution)/shard_map/ppermute | solution.py:421
  19.7 1.5 %collective-permute-start.3 = (f32[2,64,1280]{2,1,0:T(8,128)S(1)}, f32[2,64,1280]{2,1,0:T(8,128)S(1)}, u32[]{:S(2)}, u32[]{:S(2)}) collective-permute-start(f32[2,64,1280]{2,1,0:T(8,128)S(1)} %get-tuple-element.76), channel_id=1, source_target_pairs={{0,16},{8,24},{16,0},{24,8},{1,17},{9,25},{17,1},{25,9},{2,18},{10... | collective-permute-start | bytes 1966088 | tf_op jit(solution)/shard_map/ppermute | solution.py:421
  21.2 1.6 %collective-permute-start.4 = (f32[520,128]{1,0:T(8,128)S(1)}, f32[520,128]{1,0:T(8,128)S(1)}, u32[]{:S(2)}, u32[]{:S(2)}) collective-permute-start(f32[520,128]{1,0:T(8,128)S(1)} %get-tuple-element.67), channel_id=1, source_target_pairs={{0,2},{1,3},{2,4},{3,5},{4,6},{5,7},{6,0},{7,1},{8,10},{9,11},{10,... | collective-permute-start | bytes 798728 | tf_op jit(solution)/shard_map/ppermute | solution.py:460
  22.8 2.6 %collective-permute-start.5 = (f32[520,128]{1,0:T(8,128)S(1)}, f32[520,128]{1,0:T(8,128)S(1)}, u32[]{:S(2)}, u32[]{:S(2)}) collective-permute-start(f32[520,128]{1,0:T(8,128)S(1)} %get-tuple-element.68), channel_id=1, source_target_pairs={{0,4},{1,5},{2,6},{3,7},{4,0},{5,1},{6,2},{7,3},{8,12},{9,13},{10,... | collective-permute-start | bytes 798728 | tf_op jit(solution)/shard_map/ppermute | solution.py:460
  25.4 1.3 %collective-permute-start.6 = (f32[520,128]{1,0:T(8,128)S(1)}, f32[520,128]{1,0:T(8,128)S(1)}, u32[]{:S(2)}, u32[]{:S(2)}) collective-permute-start(f32[520,128]{1,0:T(8,128)S(1)} %get-tuple-element.69), channel_id=1, source_target_pairs={{0,6},{1,7},{2,0},{3,1},{4,2},{5,3},{6,4},{7,5},{8,14},{9,15},{10,... | collective-permute-start | bytes 798728 | tf_op jit(solution)/shard_map/ppermute | solution.py:460
  26.7 8.0 %collective-permute-done.2.from_x_ref = f32[2,64,1280]{2,1,0:T(8,128)S(1)} collective-permute-done((f32[2,64,1280]{2,1,0:T(8,128)S(1)}, f32[2,64,1280]{2,1,0:T(8,128)S(1)}, u32[]{:S(2)}, u32[]{:S(2)}) %collective-permute-start.2) | collective-permute-done | bytes 655392 | tf_op jit(solution)/shard_map/ppermute | solution.py:421
  34.7 1.5 %collective-permute-done.3.from_y_ref = f32[2,64,1280]{2,1,0:T(8,128)S(1)} collective-permute-done((f32[2,64,1280]{2,1,0:T(8,128)S(1)}, f32[2,64,1280]{2,1,0:T(8,128)S(1)}, u32[]{:S(2)}, u32[]{:S(2)}) %collective-permute-start.3) | collective-permute-done | bytes 655392 | tf_op jit(solution)/shard_map/ppermute | solution.py:421
  36.2 0.1 second_sums.1
  36.3 1.6 %collective-permute-start.7 = (f32[64,1280]{1,0:T(8,128)S(1)}, f32[64,1280]{1,0:T(8,128)S(1)}, u32[]{:S(2)}, u32[]{:S(2)}) collective-permute-start(f32[64,1280]{1,0:T(8,128)S(1)} %get-tuple-element.78), channel_id=1, source_target_pairs={{0,16},{8,24},{16,0},{24,8},{1,17},{9,25},{17,1},{25,9},{2,18},{10... | collective-permute-start | bytes 983048 | tf_op jit(solution)/shard_map/ppermute | solution.py:421
  37.9 0.5 collective-permute-start.8
  38.4 0.0 collective-permute-done.4.refs_1_
  38.5 4.0 %collective-permute-done.5.refs_2_ = f32[520,128]{1,0:T(8,128)S(1)} collective-permute-done((f32[520,128]{1,0:T(8,128)S(1)}, f32[520,128]{1,0:T(8,128)S(1)}, u32[]{:S(2)}, u32[]{:S(2)}) %collective-permute-start.5) | collective-permute-done | bytes 266272 | tf_op jit(solution)/shard_map/ppermute | solution.py:460
  42.5 0.0 collective-permute-done.6.refs_3_
  42.5 0.1 by_part.1
  42.6 2.4 %collective-permute-done.7 = f32[64,1280]{1,0:T(8,128)S(1)} collective-permute-done((f32[64,1280]{1,0:T(8,128)S(1)}, f32[64,1280]{1,0:T(8,128)S(1)}, u32[]{:S(2)}, u32[]{:S(2)}) %collective-permute-start.7) | collective-permute-done | bytes 327712 | tf_op jit(solution)/shard_map/ppermute | solution.py:421
  45.0 1.2 %collective-permute-done.8 = f32[64,1280]{1,0:T(8,128)S(1)} collective-permute-done((f32[64,1280]{1,0:T(8,128)S(1)}, f32[64,1280]{1,0:T(8,128)S(1)}, u32[]{:S(2)}, u32[]{:S(2)}) %collective-permute-start.8) | collective-permute-done | bytes 327712 | tf_op jit(solution)/shard_map/ppermute | solution.py:421
  46.3 0.1 chip_sums.3
  46.3 2.6 %collective-permute-start.9 = (f32[2,16,1280]{2,1,0:T(8,128)S(1)}, f32[2,16,1280]{2,1,0:T(8,128)S(1)}, u32[]{:S(2)}, u32[]{:S(2)}) collective-permute-start(f32[2,16,1280]{2,1,0:T(8,128)S(1)} %get-tuple-element.88), channel_id=1, source_target_pairs={{0,2},{1,3},{2,0},{3,1},{4,6},{5,7},{6,4},{7,5},{8,10},{9,11},{10,... | collective-permute-start | bytes 491528 | tf_op jit(solution)/shard_map/ppermute | solution.py:477
  48.9 0.1 collective-permute-start.11
  49.0 0.5 collective-permute-start.16
  49.6 0.5 collective-permute-start.17
  50.1 2.4 %collective-permute-start.18 = (f32[520,128]{1,0:T(8,128)S(1)}, f32[520,128]{1,0:T(8,128)S(1)}, u32[]{:S(2)}, u32[]{:S(2)}) collective-permute-start(f32[520,128]{1,0:T(8,128)S(1)} %get-tuple-element.84), channel_id=1, source_target_pairs={{0,24},{8,16},{16,8},{24,0},{1,25},{9,17},{17,9},{25,1},{2,26},{10... | collective-permute-start | bytes 798728 | tf_op jit(solution)/shard_map/ppermute | solution.py:421
  52.5 1.4 %collective-permute-done.9.recv_in = f32[2,16,1280]{2,1,0:T(8,128)S(1)} collective-permute-done((f32[2,16,1280]{2,1,0:T(8,128)S(1)}, f32[2,16,1280]{2,1,0:T(8,128)S(1)}, u32[]{:S(2)}, u32[]{:S(2)}) %collective-permute-start.9) | collective-permute-done | bytes 163872 | tf_op jit(solution)/shard_map/ppermute | solution.py:477
  54.0 1.9 %collective-permute-start.10 = (f32[1,16,1280]{2,1,0:T(8,128)S(1)}, f32[1,16,1280]{2,1,0:T(8,128)S(1)}, u32[]{:S(2)}, u32[]{:S(2)}) collective-permute-start(f32[1,16,1280]{2,1,0:T(8,128)S(1)} %get-tuple-element.90), channel_id=1, source_target_pairs={{0,4},{1,5},{2,6},{3,7},{4,0},{5,1},{6,2},{7,3},{8,12},{9,13},{10,... | collective-permute-start | bytes 245768 | tf_op jit(solution)/shard_map/ppermute | solution.py:477
  55.9 1.8 %collective-permute-done.11.recv_in = f32[2,16,1280]{2,1,0:T(8,128)S(1)} collective-permute-done((f32[2,16,1280]{2,1,0:T(8,128)S(1)}, f32[2,16,1280]{2,1,0:T(8,128)S(1)}, u32[]{:S(2)}, u32[]{:S(2)}) %collective-permute-start.11) | collective-permute-done | bytes 163872 | tf_op jit(solution)/shard_map/ppermute | solution.py:477
  57.7 0.1 collective-permute-start.12
  57.8 1.6 %collective-permute-done.10.recv_a_ref = f32[1,16,1280]{2,1,0:T(8,128)S(1)} collective-permute-done((f32[1,16,1280]{2,1,0:T(8,128)S(1)}, f32[1,16,1280]{2,1,0:T(8,128)S(1)}, u32[]{:S(2)}, u32[]{:S(2)}) %collective-permute-start.10) | collective-permute-done | bytes 81952 | tf_op jit(solution)/shard_map/ppermute | solution.py:477
  59.4 4.0 %collective-permute-done.12.recv_b_ref = f32[1,16,1280]{2,1,0:T(8,128)S(1)} collective-permute-done((f32[1,16,1280]{2,1,0:T(8,128)S(1)}, f32[1,16,1280]{2,1,0:T(8,128)S(1)}, u32[]{:S(2)}, u32[]{:S(2)}) %collective-permute-start.12) | collective-permute-done | bytes 81952 | tf_op jit(solution)/shard_map/ppermute | solution.py:477
  63.4 0.0 copy-start
  63.5 0.0 copy-start.3
  63.5 0.0 collective-permute-done.16.refs_1_
  63.5 0.0 collective-permute-done.17.refs_2_
  63.5 0.0 collective-permute-done.18.refs_3_
  63.5 0.1 by_core.1
  63.6 0.1 collective-permute-start.19
  63.7 1.0 %collective-permute-start.15 = (f32[16,2560]{1,0:T(8,128)S(1)}, f32[16,2560]{1,0:T(8,128)S(1)}, u32[]{:S(2)}, u32[]{:S(2)}) collective-permute-start(f32[16,2560]{1,0:T(8,128)S(1)} %total.1.refs_0_), channel_id=1, source_target_pairs={{0,24},{8,16},{16,8},{24,0},{1,25},{9,17},{17,9},{25,1},{2,26},{10... | collective-permute-start | bytes 491528 | tf_op jit(solution)/shard_map/ppermute | solution.py:421
  64.7 1.5 %collective-permute-start.14 = (f32[16,2560]{1,0:T(8,128)S(1)}, f32[16,2560]{1,0:T(8,128)S(1)}, u32[]{:S(2)}, u32[]{:S(2)}) collective-permute-start(f32[16,2560]{1,0:T(8,128)S(1)} %total.1.refs_0_), channel_id=1, source_target_pairs={{0,16},{8,24},{16,0},{24,8},{1,17},{9,25},{17,1},{25,9},{2,18},{10... | collective-permute-start | bytes 491528 | tf_op jit(solution)/shard_map/ppermute | solution.py:421
  66.2 1.0 %collective-permute-start.13 = (f32[16,2560]{1,0:T(8,128)S(1)}, f32[16,2560]{1,0:T(8,128)S(1)}, u32[]{:S(2)}, u32[]{:S(2)}) collective-permute-start(f32[16,2560]{1,0:T(8,128)S(1)} %total.1.refs_0_), channel_id=1, source_target_pairs={{0,8},{8,0},{16,24},{24,16},{1,9},{9,1},{17,25},{25,17},{2,10},{10... | collective-permute-start | bytes 491528 | tf_op jit(solution)/shard_map/ppermute | solution.py:421
  67.2 0.0 collective-permute-done.19.recv_ref
  67.2 0.0 copy-done
  67.2 0.0 copy-done.3
  67.2 2.5 %table_part.1 = (f32[512,512]{1,0:T(8,128)}, f32[512]{0:T(512)}) custom-call(f32[1056,128]{1,0:T(8,128)S(1)} %get-tuple-element.97.keep_ref, f32[1056,128]{1,0:T(8,128)S(1)} %collective-permute-done.19.recv_ref, f32[512,512]{1,0:T(8,128)S(1)} %copy-done, f32[512]{0:T(512)S(1)} %copy-done.3), custom_call_target="tpu_custom_call" | custom-call | flops 1000000000 | bytes 65536 | tf_op jit(solution)/shard_map/table_part/pallas_call | solution.py:403
  69.7 2.0 %collective-permute-done.15.refs_3_ = f32[16,2560]{1,0:T(8,128)S(1)} collective-permute-done((f32[16,2560]{1,0:T(8,128)S(1)}, f32[16,2560]{1,0:T(8,128)S(1)}, u32[]{:S(2)}, u32[]{:S(2)}) %collective-permute-start.15) | collective-permute-done | bytes 163872 | tf_op jit(solution)/shard_map/ppermute | solution.py:421
  71.7 2.8 %collective-permute-done.14.refs_2_ = f32[16,2560]{1,0:T(8,128)S(1)} collective-permute-done((f32[16,2560]{1,0:T(8,128)S(1)}, f32[16,2560]{1,0:T(8,128)S(1)}, u32[]{:S(2)}, u32[]{:S(2)}) %collective-permute-start.14) | collective-permute-done | bytes 163872 | tf_op jit(solution)/shard_map/ppermute | solution.py:421
  74.5 0.0 collective-permute-done.13.refs_1_
  74.5 0.9 %gather.1 = (f32[4,16,2048]{2,1,0:T(8,128)}, f32[4,16,512]{2,1,0:T(8,128)}) custom-call(f32[16,2560]{1,0:T(8,128)S(1)} %total.1.refs_0_, f32[16,2560]{1,0:T(8,128)S(1)} %collective-permute-done.13.refs_1_, f32[16,2560]{1,0:T(8,128)S(1)} %collective-permute-done.14.refs_2_, f32[16,2560]{1,0:T(8,128)S(1)} %collective-permute-done.15.refs_3_), custom_call_target="tpu_custom_call" | custom-call | flops 1000000000 | bytes 65536 | tf_op jit(solution)/shard_map/gather/pallas_call | solution.py:403
  (3 shorter events, 0.1 us)
Async XLA Ops:
  9.4 4.5 %collective-permute-start = (f32[256,1536]{1,0:T(8,128)S(1)}, f32[256,1536]{1,0:T(8,128)S(1)}, u32[]{:S(2)}, u32[]{:S(2)}) collective-permute-start(f32[256,1536]{1,0:T(8,128)S(1)} %get-tuple-element.59), channel_id=1, source_target_pairs={{0,1},{1,0},{2,3},{3,2},{4,5},{5,4},{6,7},{7,6},{8,9},{9,8},{10,11... | collective-permute-start | bytes 4718600 | tf_op jit(solution)/shard_map/ppermute | solution.py:448
  10.0 3.9 %copy-start.1 = (s32[1,32,16]{1,2,0:T(8,128)S(1)}, s32[1,32,16]{1,2,0:T(8,128)}, u32[]{:S(2)}) copy-start(s32[1,32,16]{1,2,0:T(8,128)} %param.14) | copy-start | bytes 6148
  10.0 3.9 %copy-start.2 = (s32[1,512]{1,0:T(1,128)S(1)}, s32[1,512]{1,0:T(1,128)}, u32[]{:S(2)}) copy-start(s32[1,512]{1,0:T(1,128)} %slot_ref.1) | copy-start | bytes 6148
  13.8 2.7 %collective-permute-start.1 = (f32[256,1024]{1,0:T(8,128)S(1)}, f32[256,1024]{1,0:T(8,128)S(1)}, u32[]{:S(2)}, u32[]{:S(2)}) collective-permute-start(f32[256,1024]{1,0:T(8,128)S(1)} %get-tuple-element.72), channel_id=1, source_target_pairs={{0,1},{1,0},{2,3},{3,2},{4,5},{5,4},{6,7},{7,6},{8,9},{9,8},{10,11... | collective-permute-start | bytes 3145736 | tf_op jit(solution)/shard_map/ppermute | solution.py:452
  16.8 18.0 %collective-permute-start.2 = (f32[2,64,1280]{2,1,0:T(8,128)S(1)}, f32[2,64,1280]{2,1,0:T(8,128)S(1)}, u32[]{:S(2)}, u32[]{:S(2)}) collective-permute-start(f32[2,64,1280]{2,1,0:T(8,128)S(1)} %get-tuple-element.74), channel_id=1, source_target_pairs={{0,8},{8,0},{16,24},{24,16},{1,9},{9,1},{17,25},{25,17},{2,10},{10... | collective-permute-start | bytes 1966088 | tf_op jit(solution)/shard_map/ppermute | solution.py:421
  19.7 16.5 %collective-permute-start.3 = (f32[2,64,1280]{2,1,0:T(8,128)S(1)}, f32[2,64,1280]{2,1,0:T(8,128)S(1)}, u32[]{:S(2)}, u32[]{:S(2)}) collective-permute-start(f32[2,64,1280]{2,1,0:T(8,128)S(1)} %get-tuple-element.76), channel_id=1, source_target_pairs={{0,16},{8,24},{16,0},{24,8},{1,17},{9,25},{17,1},{25,9},{2,18},{10... | collective-permute-start | bytes 1966088 | tf_op jit(solution)/shard_map/ppermute | solution.py:421
  21.2 17.2 %collective-permute-start.4 = (f32[520,128]{1,0:T(8,128)S(1)}, f32[520,128]{1,0:T(8,128)S(1)}, u32[]{:S(2)}, u32[]{:S(2)}) collective-permute-start(f32[520,128]{1,0:T(8,128)S(1)} %get-tuple-element.67), channel_id=1, source_target_pairs={{0,2},{1,3},{2,4},{3,5},{4,6},{5,7},{6,0},{7,1},{8,10},{9,11},{10,... | collective-permute-start | bytes 798728 | tf_op jit(solution)/shard_map/ppermute | solution.py:460
  22.8 19.7 %collective-permute-start.5 = (f32[520,128]{1,0:T(8,128)S(1)}, f32[520,128]{1,0:T(8,128)S(1)}, u32[]{:S(2)}, u32[]{:S(2)}) collective-permute-start(f32[520,128]{1,0:T(8,128)S(1)} %get-tuple-element.68), channel_id=1, source_target_pairs={{0,4},{1,5},{2,6},{3,7},{4,0},{5,1},{6,2},{7,3},{8,12},{9,13},{10,... | collective-permute-start | bytes 798728 | tf_op jit(solution)/shard_map/ppermute | solution.py:460
  25.4 17.1 %collective-permute-start.6 = (f32[520,128]{1,0:T(8,128)S(1)}, f32[520,128]{1,0:T(8,128)S(1)}, u32[]{:S(2)}, u32[]{:S(2)}) collective-permute-start(f32[520,128]{1,0:T(8,128)S(1)} %get-tuple-element.69), channel_id=1, source_target_pairs={{0,6},{1,7},{2,0},{3,1},{4,2},{5,3},{6,4},{7,5},{8,14},{9,15},{10,... | collective-permute-start | bytes 798728 | tf_op jit(solution)/shard_map/ppermute | solution.py:460
  36.3 8.7 %collective-permute-start.7 = (f32[64,1280]{1,0:T(8,128)S(1)}, f32[64,1280]{1,0:T(8,128)S(1)}, u32[]{:S(2)}, u32[]{:S(2)}) collective-permute-start(f32[64,1280]{1,0:T(8,128)S(1)} %get-tuple-element.78), channel_id=1, source_target_pairs={{0,16},{8,24},{16,0},{24,8},{1,17},{9,25},{17,1},{25,9},{2,18},{10... | collective-permute-start | bytes 983048 | tf_op jit(solution)/shard_map/ppermute | solution.py:421
  37.9 8.3 %collective-permute-start.8 = (f32[64,1280]{1,0:T(8,128)S(1)}, f32[64,1280]{1,0:T(8,128)S(1)}, u32[]{:S(2)}, u32[]{:S(2)}) collective-permute-start(f32[64,1280]{1,0:T(8,128)S(1)} %get-tuple-element.79), channel_id=1, source_target_pairs={{0,8},{8,0},{16,24},{24,16},{1,9},{9,1},{17,25},{25,17},{2,10},{10... | collective-permute-start | bytes 983048 | tf_op jit(solution)/shard_map/ppermute | solution.py:421
  46.3 7.6 %collective-permute-start.9 = (f32[2,16,1280]{2,1,0:T(8,128)S(1)}, f32[2,16,1280]{2,1,0:T(8,128)S(1)}, u32[]{:S(2)}, u32[]{:S(2)}) collective-permute-start(f32[2,16,1280]{2,1,0:T(8,128)S(1)} %get-tuple-element.88), channel_id=1, source_target_pairs={{0,2},{1,3},{2,0},{3,1},{4,6},{5,7},{6,4},{7,5},{8,10},{9,11},{10,... | collective-permute-start | bytes 491528 | tf_op jit(solution)/shard_map/ppermute | solution.py:477
  48.9 8.8 %collective-permute-start.11 = (f32[2,16,1280]{2,1,0:T(8,128)S(1)}, f32[2,16,1280]{2,1,0:T(8,128)S(1)}, u32[]{:S(2)}, u32[]{:S(2)}) collective-permute-start(f32[2,16,1280]{2,1,0:T(8,128)S(1)} %get-tuple-element.93), channel_id=1, source_target_pairs={{0,2},{1,3},{2,0},{3,1},{4,6},{5,7},{6,4},{7,5},{8,10},{9,11},{10,... | collective-permute-start | bytes 491528 | tf_op jit(solution)/shard_map/ppermute | solution.py:477
  49.0 14.4 %collective-permute-start.16 = (f32[520,128]{1,0:T(8,128)S(1)}, f32[520,128]{1,0:T(8,128)S(1)}, u32[]{:S(2)}, u32[]{:S(2)}) collective-permute-start(f32[520,128]{1,0:T(8,128)S(1)} %get-tuple-element.82), channel_id=1, source_target_pairs={{0,8},{8,0},{16,24},{24,16},{1,9},{9,1},{17,25},{25,17},{2,10},{10... | collective-permute-start | bytes 798728 | tf_op jit(solution)/shard_map/ppermute | solution.py:421
  49.6 13.9 %collective-permute-start.17 = (f32[520,128]{1,0:T(8,128)S(1)}, f32[520,128]{1,0:T(8,128)S(1)}, u32[]{:S(2)}, u32[]{:S(2)}) collective-permute-start(f32[520,128]{1,0:T(8,128)S(1)} %get-tuple-element.83), channel_id=1, source_target_pairs={{0,16},{8,24},{16,0},{24,8},{1,17},{9,25},{17,1},{25,9},{2,18},{10... | collective-permute-start | bytes 798728 | tf_op jit(solution)/shard_map/ppermute | solution.py:421
  50.1 13.4 %collective-permute-start.18 = (f32[520,128]{1,0:T(8,128)S(1)}, f32[520,128]{1,0:T(8,128)S(1)}, u32[]{:S(2)}, u32[]{:S(2)}) collective-permute-start(f32[520,128]{1,0:T(8,128)S(1)} %get-tuple-element.84), channel_id=1, source_target_pairs={{0,24},{8,16},{16,8},{24,0},{1,25},{9,17},{17,9},{25,1},{2,26},{10... | collective-permute-start | bytes 798728 | tf_op jit(solution)/shard_map/ppermute | solution.py:421
  54.0 5.4 %collective-permute-start.10 = (f32[1,16,1280]{2,1,0:T(8,128)S(1)}, f32[1,16,1280]{2,1,0:T(8,128)S(1)}, u32[]{:S(2)}, u32[]{:S(2)}) collective-permute-start(f32[1,16,1280]{2,1,0:T(8,128)S(1)} %get-tuple-element.90), channel_id=1, source_target_pairs={{0,4},{1,5},{2,6},{3,7},{4,0},{5,1},{6,2},{7,3},{8,12},{9,13},{10,... | collective-permute-start | bytes 245768 | tf_op jit(solution)/shard_map/ppermute | solution.py:477
  57.7 5.7 %collective-permute-start.12 = (f32[1,16,1280]{2,1,0:T(8,128)S(1)}, f32[1,16,1280]{2,1,0:T(8,128)S(1)}, u32[]{:S(2)}, u32[]{:S(2)}) collective-permute-start(f32[1,16,1280]{2,1,0:T(8,128)S(1)} %get-tuple-element.95), channel_id=1, source_target_pairs={{0,4},{1,5},{2,6},{3,7},{4,0},{5,1},{6,2},{7,3},{8,12},{9,13},{10,... | collective-permute-start | bytes 245768 | tf_op jit(solution)/shard_map/ppermute | solution.py:477
  63.4 3.8 %copy-start = (f32[512,512]{1,0:T(8,128)S(1)}, f32[512,512]{1,0:T(8,128)}, u32[]{:S(2)}) copy-start(f32[512,512]{1,0:T(8,128)} %table_ref.1) | copy-start | bytes 3145732
  63.5 3.8 %copy-start.3 = (f32[512]{0:T(512)S(1)}, f32[512]{0:T(512)}, u32[]{:S(2)}) copy-start(f32[512]{0:T(512)} %accum_ref.1) | copy-start | bytes 6148
  63.6 3.6 %collective-permute-start.19 = (f32[1056,128]{1,0:T(8,128)S(1)}, f32[1056,128]{1,0:T(8,128)S(1)}, u32[]{:S(2)}, u32[]{:S(2)}) collective-permute-start(f32[1056,128]{1,0:T(8,128)S(1)} %get-tuple-element.98), channel_id=1, source_target_pairs={{0,1},{1,0},{2,3},{3,2},{4,5},{5,4},{6,7},{7,6},{8,9},{9,8},{10,11... | collective-permute-start | bytes 1622024 | tf_op jit(solution)/shard_map/ppermute | solution.py:498
  63.7 8.0 %collective-permute-start.15 = (f32[16,2560]{1,0:T(8,128)S(1)}, f32[16,2560]{1,0:T(8,128)S(1)}, u32[]{:S(2)}, u32[]{:S(2)}) collective-permute-start(f32[16,2560]{1,0:T(8,128)S(1)} %total.1.refs_0_), channel_id=1, source_target_pairs={{0,24},{8,16},{16,8},{24,0},{1,25},{9,17},{17,9},{25,1},{2,26},{10... | collective-permute-start | bytes 491528 | tf_op jit(solution)/shard_map/ppermute | solution.py:421
  64.7 9.8 %collective-permute-start.14 = (f32[16,2560]{1,0:T(8,128)S(1)}, f32[16,2560]{1,0:T(8,128)S(1)}, u32[]{:S(2)}, u32[]{:S(2)}) collective-permute-start(f32[16,2560]{1,0:T(8,128)S(1)} %total.1.refs_0_), channel_id=1, source_target_pairs={{0,16},{8,24},{16,0},{24,8},{1,17},{9,25},{17,1},{25,9},{2,18},{10... | collective-permute-start | bytes 491528 | tf_op jit(solution)/shard_map/ppermute | solution.py:421
  66.2 8.3 %collective-permute-start.13 = (f32[16,2560]{1,0:T(8,128)S(1)}, f32[16,2560]{1,0:T(8,128)S(1)}, u32[]{:S(2)}, u32[]{:S(2)}) collective-permute-start(f32[16,2560]{1,0:T(8,128)S(1)} %total.1.refs_0_), channel_id=1, source_target_pairs={{0,8},{8,0},{16,24},{24,16},{1,9},{9,1},{17,25},{25,17},{2,10},{10... | collective-permute-start | bytes 491528 | tf_op jit(solution)/shard_map/ppermute | solution.py:421

commit v14 on v13

--- a/solution.py
+++ b/solution.py
@@ -368,24 +368,24 @@
     halve(bit, send_ref, keep_ref, keep_in, recv_in)
 
 
-def total_kernel(tokens, keep_a_ref, recv_a_ref, keep_b_ref, recv_b_ref, out_ref):
-    half = keep_a_ref.shape[-1]
-    out_ref[:, :half] = (keep_a_ref[0] + recv_a_ref[0]) * (1.0 / tokens)
-    out_ref[:, half:] = (keep_b_ref[0] + recv_b_ref[0]) * (1.0 / tokens)
+def total_kernel(tokens, keep_ref, recv_ref, out_ref):
+    out_ref[...] = (keep_ref[0] + recv_ref[0]) * (1.0 / tokens)
 
 
 def gather_kernel(*refs):
     *pieces, grad_in_ref, grad_out_ref = refs
+    dp = len(pieces) // 2
     d = lax.axis_index("dp")
     width = grad_out_ref.shape[-1]
     half = width // 2
-    for k, piece in enumerate(pieces):
+    for k in range(dp):
         at = jnp.bitwise_xor(d, k)
+        piece, piece_b = pieces[k], pieces[dp + k]
         grad_out_ref[at] = piece[:, :width]
-        start = width
-        for cols, first in ((half, 0), (width, 2 * width), (half, half), (width, width), (width, 3 * width)):
-            grad_in_ref[at, :, first:first + cols] = piece[:, start:start + cols]
-            start += cols
+        grad_in_ref[at, :, :half] = piece[:, width:width + half]
+        grad_in_ref[at, :, half:2 * width] = piece_b[:, :width + half]
+        grad_in_ref[at, :, 2 * width:3 * width] = piece[:, width + half:]
+        grad_in_ref[at, :, 3 * width:] = piece_b[:, width + half:]
 
 
 def vmem():
@@ -488,13 +488,15 @@
                 functools.partial(chip_kernel, bit), "chip_sums", [local(chips >> (bit + 1), piece, cols // 2)] * 2,
                 halves[i], long=False)
             halves[i] = [keep, over_chips(send, bit)]
-    (total,) = call(
-        functools.partial(total_kernel, tokens), "total", [local(piece, cols)], halves[0] + halves[1], long=False)
-    pieces = gathered(total)
-    parts[0] = after(parts[0], total)
+    total = lambda half, **how: call(
+        functools.partial(total_kernel, tokens), "total", [local(piece, cols // 2)], half, **how)[0]
+    pieces = gathered(total(halves[0]))
+    parts[0] = after(parts[0], pieces[0])
     keep, send = call(
         functools.partial(by_core_kernel, chips, block), "by_core",
-        [local(dp_size * (chips * block + id_rows(chips)), LANES)] * 2, parts, long=False)
+        [local(dp_size * (chips * block + id_rows(chips)), LANES)] * 2, parts)
+    halves[1][0] = after(halves[1][0], keep, send, *pieces)
+    pieces += gathered(total(halves[1], long=True))
     recv = lax.ppermute(send, "rows", cores)
     slots = owners * capacity
     table_new, accum_new = call(

time: 75.5 us -> 79.4 us (1.052)
  starting transfers between devices: 24.5 us -> 30.1 us
  waiting for transfers between devices: 30.9 us -> 29.3 us
    ppermute x10 -> x13, starting transfers between devices: 13.6 us -> 19.2 us  [body(): lax.ppermute(v, 'dp', [(i, i ^ bit) for i in range(dp_size)])]
    ppermute x4, waiting for transfers between devices: 8.86 us -> 4.81 us  [body(): lax.ppermute(v, 'rows', [(i, i ^ 2 << bit) for i in range(rows_size)])]
    ppermute x10 -> x13, waiting for transfers between devices: 17.9 us -> 20.3 us  [body(): lax.ppermute(v, 'dp', [(i, i ^ bit) for i in range(dp_size)])]
    pallas_call x13 -> x14, Pallas kernels: 18.5 us -> 18.5 us  [call(): pl.pallas_call(kernel, name=name, in_specs=[pl.BlockSpec(memory_space=p o...]
  transfers between devices with their start and end apart: 20 -> 23, of which waited for: 12 -> 12; matrix products, arithmetic and copies ran while one was open for 0% -> 0% of each run, Pallas kernels for 12% -> 12%
where the time goes in v14:
time: 79.4 us; the launch traced here: 79.2 us
  starting transfers between devices  30.1 us (38%)
  waiting for transfers between devices  29.3 us (37%)
  Pallas kernels  18.5 us (23%)
  between operations  1.39 us (2%)
    ppermute x13, waiting for transfers between devices, body(): lax.ppermute(v, 'dp', [(i, i ^ bit) for i in range(dp_size)])  20.3 us
    ppermute x13, starting transfers between devices, body(): lax.ppermute(v, 'dp', [(i, i ^ bit) for i in range(dp_size)])  19.2 us
    pallas_call x14, Pallas kernels, call(): pl.pallas_call(kernel, name=name, in_specs=[pl.BlockSpec(memory_space=p o...  18.5 us
    ppermute x3, starting transfers between devices, body(): lax.ppermute(v, 'rows', [(i, (i + 2 * k) % rows_size) for i in range(rows...  5.51 us
    ppermute x4, waiting for transfers between devices, body(): lax.ppermute(v, 'rows', [(i, i ^ 2 << bit) for i in range(rows_size)])  4.81 us
    ppermute x4, starting transfers between devices, body(): lax.ppermute(v, 'rows', [(i, i ^ 2 << bit) for i in range(rows_size)])  4.67 us
    ppermute x3, waiting for transfers between devices, body(): lax.ppermute(v, 'rows', [(i, (i + 2 * k) % rows_size) for i in range(rows...  4.05 us
  transfers between devices with their start and end apart: 23, of which 12 were waited for; matrix products, arithmetic and copies ran while one was open for 0% of the time, Pallas kernels for 12%

profile of v14, /device:TPU:0, one launch (start us, length us, event | category | flops | bytes accessed | tf_op | source)
XLA Modules:
  0.0 79.2 jit_solution(13382243530840156314)
XLA Ops:
  1.3 8.1 %forward_part.1 = (f32[256,1536]{1,0:T(8,128)S(1)}, f32[256,1536]{1,0:T(8,128)S(1)}, bf16[512,1536]{1,0:T(8,128)(2,1)S(1)}, bf16[512,1024]{1,0:T(8,128)(2,1)S(1)...) custom-call(s32[1]{0:T(128)S(6)} %copy.13.len_ref, ...), custom_call_target="tpu_custom_call" | custom-call | flops 99999997952 | bytes 65536 | tf_op jit(solution)/shard_map/forward_part/pallas_call | solution.py:403
  9.4 0.5 collective-permute-start
  10.0 0.0 copy-start.1
  10.0 0.0 copy-start.2
  10.0 3.8 %attention_part.1 = (f32[256,1024]{1,0:T(8,128)S(1)}, f32[256,1024]{1,0:T(8,128)S(1)}, bf16[512,1024]{1,0:T(8,128)(2,1)S(1)}) custom-call(s32[1]{0:T(128)S(6)} %copy.13.len_ref, bf16[512,1536]{1,0:T(8,128)(2,1)S(1)} %get-tuple-element.62.hid_ref, bf16[512,1024]{1,0:T(8,128)(2,1)S(1)} %get-tuple-element.63.dsilu_ref, ...), custom_call_target="tpu_custom_call" | custom-call | flops 99999997952 | bytes 65536 | tf_op jit(solution)/shard_map/attention_part/pallas_call | solution.py:403
  13.8 0.1 collective-permute-start.1
  13.9 0.0 collective-permute-done
  13.9 0.0 copy-done.1
  13.9 0.0 copy-done.2
  13.9 2.5 %events_part.1 = (f32[520,128]{1,0:T(8,128)S(1)}, f32[520,128]{1,0:T(8,128)S(1)}, f32[520,128]{1,0:T(8,128)S(1)}, f32[520,128]{1,0:T(8,128)S(1)}) custom-call(s32[1]{0:T(128)S(6)} %copy.13.len_ref, bf16[512,512]{1,0:T(8,128)(2,1)S(1)} %get-tuple-element.56.ev_ref, bf16[512,512]{1,0:T(8,128)(2,1)S(1)} %get-tuple-element.57.cot_ref, ...), custom_call_target="tpu_custom_call" | custom-call | flops 99999997952 | bytes 65536 | tf_op jit(solution)/shard_map/events_part/pallas_call | solution.py:403
  16.4 0.1 collective-permute-done.1
  16.5 0.3 first_sums.1
  16.8 2.9 %collective-permute-start.2 = (f32[2,64,1280]{2,1,0:T(8,128)S(1)}, f32[2,64,1280]{2,1,0:T(8,128)S(1)}, u32[]{:S(2)}, u32[]{:S(2)}) collective-permute-start(f32[2,64,1280]{2,1,0:T(8,128)S(1)} %get-tuple-element.75), channel_id=1, source_target_pairs={{0,8},{8,0},{16,24},{24,16},{1,9},{9,1},{17,25},{25,17},{2,10},{10... | collective-permute-start | bytes 1966088 | tf_op jit(solution)/shard_map/ppermute | solution.py:421
  19.7 1.5 %collective-permute-start.3 = (f32[2,64,1280]{2,1,0:T(8,128)S(1)}, f32[2,64,1280]{2,1,0:T(8,128)S(1)}, u32[]{:S(2)}, u32[]{:S(2)}) collective-permute-start(f32[2,64,1280]{2,1,0:T(8,128)S(1)} %get-tuple-element.77), channel_id=1, source_target_pairs={{0,16},{8,24},{16,0},{24,8},{1,17},{9,25},{17,1},{25,9},{2,18},{10... | collective-permute-start | bytes 1966088 | tf_op jit(solution)/shard_map/ppermute | solution.py:421
  21.2 1.6 %collective-permute-start.4 = (f32[520,128]{1,0:T(8,128)S(1)}, f32[520,128]{1,0:T(8,128)S(1)}, u32[]{:S(2)}, u32[]{:S(2)}) collective-permute-start(f32[520,128]{1,0:T(8,128)S(1)} %get-tuple-element.68), channel_id=1, source_target_pairs={{0,2},{1,3},{2,4},{3,5},{4,6},{5,7},{6,0},{7,1},{8,10},{9,11},{10,... | collective-permute-start | bytes 798728 | tf_op jit(solution)/shard_map/ppermute | solution.py:460
  22.8 2.6 %collective-permute-start.5 = (f32[520,128]{1,0:T(8,128)S(1)}, f32[520,128]{1,0:T(8,128)S(1)}, u32[]{:S(2)}, u32[]{:S(2)}) collective-permute-start(f32[520,128]{1,0:T(8,128)S(1)} %get-tuple-element.69), channel_id=1, source_target_pairs={{0,4},{1,5},{2,6},{3,7},{4,0},{5,1},{6,2},{7,3},{8,12},{9,13},{10,... | collective-permute-start | bytes 798728 | tf_op jit(solution)/shard_map/ppermute | solution.py:460
  25.4 1.3 %collective-permute-start.6 = (f32[520,128]{1,0:T(8,128)S(1)}, f32[520,128]{1,0:T(8,128)S(1)}, u32[]{:S(2)}, u32[]{:S(2)}) collective-permute-start(f32[520,128]{1,0:T(8,128)S(1)} %get-tuple-element.70), channel_id=1, source_target_pairs={{0,6},{1,7},{2,0},{3,1},{4,2},{5,3},{6,4},{7,5},{8,14},{9,15},{10,... | collective-permute-start | bytes 798728 | tf_op jit(solution)/shard_map/ppermute | solution.py:460
  26.7 8.0 %collective-permute-done.2.from_x_ref = f32[2,64,1280]{2,1,0:T(8,128)S(1)} collective-permute-done((f32[2,64,1280]{2,1,0:T(8,128)S(1)}, f32[2,64,1280]{2,1,0:T(8,128)S(1)}, u32[]{:S(2)}, u32[]{:S(2)}) %collective-permute-start.2) | collective-permute-done | bytes 655392 | tf_op jit(solution)/shard_map/ppermute | solution.py:421
  34.7 1.5 %collective-permute-done.3.from_y_ref = f32[2,64,1280]{2,1,0:T(8,128)S(1)} collective-permute-done((f32[2,64,1280]{2,1,0:T(8,128)S(1)}, f32[2,64,1280]{2,1,0:T(8,128)S(1)}, u32[]{:S(2)}, u32[]{:S(2)}) %collective-permute-start.3) | collective-permute-done | bytes 655392 | tf_op jit(solution)/shard_map/ppermute | solution.py:421
  36.2 0.1 second_sums.1
  36.3 1.6 %collective-permute-start.7 = (f32[64,1280]{1,0:T(8,128)S(1)}, f32[64,1280]{1,0:T(8,128)S(1)}, u32[]{:S(2)}, u32[]{:S(2)}) collective-permute-start(f32[64,1280]{1,0:T(8,128)S(1)} %get-tuple-element.79), channel_id=1, source_target_pairs={{0,16},{8,24},{16,0},{24,8},{1,17},{9,25},{17,1},{25,9},{2,18},{10... | collective-permute-start | bytes 983048 | tf_op jit(solution)/shard_map/ppermute | solution.py:421
  37.9 0.5 collective-permute-start.8
  38.4 0.0 collective-permute-done.4.refs_1_
  38.5 4.0 %collective-permute-done.5.refs_2_ = f32[520,128]{1,0:T(8,128)S(1)} collective-permute-done((f32[520,128]{1,0:T(8,128)S(1)}, f32[520,128]{1,0:T(8,128)S(1)}, u32[]{:S(2)}, u32[]{:S(2)}) %collective-permute-start.5) | collective-permute-done | bytes 266272 | tf_op jit(solution)/shard_map/ppermute | solution.py:460
  42.5 0.0 collective-permute-done.6.refs_3_
  42.5 0.1 by_part.1
  42.6 2.4 %collective-permute-done.7 = f32[64,1280]{1,0:T(8,128)S(1)} collective-permute-done((f32[64,1280]{1,0:T(8,128)S(1)}, f32[64,1280]{1,0:T(8,128)S(1)}, u32[]{:S(2)}, u32[]{:S(2)}) %collective-permute-start.7) | collective-permute-done | bytes 327712 | tf_op jit(solution)/shard_map/ppermute | solution.py:421
  45.0 1.2 %collective-permute-done.8 = f32[64,1280]{1,0:T(8,128)S(1)} collective-permute-done((f32[64,1280]{1,0:T(8,128)S(1)}, f32[64,1280]{1,0:T(8,128)S(1)}, u32[]{:S(2)}, u32[]{:S(2)}) %collective-permute-start.8) | collective-permute-done | bytes 327712 | tf_op jit(solution)/shard_map/ppermute | solution.py:421
  46.3 0.1 chip_sums.3
  46.3 2.6 %collective-permute-start.9 = (f32[2,16,1280]{2,1,0:T(8,128)S(1)}, f32[2,16,1280]{2,1,0:T(8,128)S(1)}, u32[]{:S(2)}, u32[]{:S(2)}) collective-permute-start(f32[2,16,1280]{2,1,0:T(8,128)S(1)} %get-tuple-element.89), channel_id=1, source_target_pairs={{0,2},{1,3},{2,0},{3,1},{4,6},{5,7},{6,4},{7,5},{8,10},{9,11},{10,... | collective-permute-start | bytes 491528 | tf_op jit(solution)/shard_map/ppermute | solution.py:477
  48.9 0.1 collective-permute-start.14
  49.0 0.5 collective-permute-start.15
  49.6 0.5 collective-permute-start.16
  50.1 2.4 %collective-permute-start.17 = (f32[520,128]{1,0:T(8,128)S(1)}, f32[520,128]{1,0:T(8,128)S(1)}, u32[]{:S(2)}, u32[]{:S(2)}) collective-permute-start(f32[520,128]{1,0:T(8,128)S(1)} %get-tuple-element.85), channel_id=1, source_target_pairs={{0,24},{8,16},{16,8},{24,0},{1,25},{9,17},{17,9},{25,1},{2,26},{10... | collective-permute-start | bytes 798728 | tf_op jit(solution)/shard_map/ppermute | solution.py:421
  52.5 1.4 %collective-permute-done.9.recv_in = f32[2,16,1280]{2,1,0:T(8,128)S(1)} collective-permute-done((f32[2,16,1280]{2,1,0:T(8,128)S(1)}, f32[2,16,1280]{2,1,0:T(8,128)S(1)}, u32[]{:S(2)}, u32[]{:S(2)}) %collective-permute-start.9) | collective-permute-done | bytes 163872 | tf_op jit(solution)/shard_map/ppermute | solution.py:477
  54.0 1.9 %collective-permute-start.10 = (f32[1,16,1280]{2,1,0:T(8,128)S(1)}, f32[1,16,1280]{2,1,0:T(8,128)S(1)}, u32[]{:S(2)}, u32[]{:S(2)}) collective-permute-start(f32[1,16,1280]{2,1,0:T(8,128)S(1)} %get-tuple-element.91), channel_id=1, source_target_pairs={{0,4},{1,5},{2,6},{3,7},{4,0},{5,1},{6,2},{7,3},{8,12},{9,13},{10,... | collective-permute-start | bytes 245768 | tf_op jit(solution)/shard_map/ppermute | solution.py:477
  55.9 1.8 %collective-permute-done.14.recv_in = f32[2,16,1280]{2,1,0:T(8,128)S(1)} collective-permute-done((f32[2,16,1280]{2,1,0:T(8,128)S(1)}, f32[2,16,1280]{2,1,0:T(8,128)S(1)}, u32[]{:S(2)}, u32[]{:S(2)}) %collective-permute-start.14) | collective-permute-done | bytes 163872 | tf_op jit(solution)/shard_map/ppermute | solution.py:477
  57.7 0.1 collective-permute-start.18
  57.8 1.6 %collective-permute-done.10.recv_ref = f32[1,16,1280]{2,1,0:T(8,128)S(1)} collective-permute-done((f32[1,16,1280]{2,1,0:T(8,128)S(1)}, f32[1,16,1280]{2,1,0:T(8,128)S(1)}, u32[]{:S(2)}, u32[]{:S(2)}) %collective-permute-start.10) | collective-permute-done | bytes 81952 | tf_op jit(solution)/shard_map/ppermute | solution.py:477
  59.4 0.5 collective-permute-start.13
  59.9 0.0 collective-permute-done.15.refs_1_
  59.9 1.5 %collective-permute-start.12 = (f32[16,1280]{1,0:T(8,128)S(1)}, f32[16,1280]{1,0:T(8,128)S(1)}, u32[]{:S(2)}, u32[]{:S(2)}) collective-permute-start(f32[16,1280]{1,0:T(8,128)S(1)} %total.2.refs_0_), channel_id=1, source_target_pairs={{0,16},{8,24},{16,0},{24,8},{1,17},{9,25},{17,1},{25,9},{2,18},{10... | collective-permute-start | bytes 245768 | tf_op jit(solution)/shard_map/ppermute | solution.py:421
  61.5 2.6 %collective-permute-done.16.refs_2_ = f32[520,128]{1,0:T(8,128)S(1)} collective-permute-done((f32[520,128]{1,0:T(8,128)S(1)}, f32[520,128]{1,0:T(8,128)S(1)}, u32[]{:S(2)}, u32[]{:S(2)}) %collective-permute-start.16) | collective-permute-done | bytes 266272 | tf_op jit(solution)/shard_map/ppermute | solution.py:421
  64.1 3.1 %collective-permute-start.11 = (f32[16,1280]{1,0:T(8,128)S(1)}, f32[16,1280]{1,0:T(8,128)S(1)}, u32[]{:S(2)}, u32[]{:S(2)}) collective-permute-start(f32[16,1280]{1,0:T(8,128)S(1)} %total.2.refs_0_), channel_id=1, source_target_pairs={{0,8},{8,0},{16,24},{24,16},{1,9},{9,1},{17,25},{25,17},{2,10},{10... | collective-permute-start | bytes 245768 | tf_op jit(solution)/shard_map/ppermute | solution.py:421
  67.1 0.0 collective-permute-done.17.refs_3_
  67.1 0.1 by_core.1
  67.2 0.1 collective-permute-start.22
  67.3 0.0 collective-permute-done.13.refs_3_
  67.3 0.0 collective-permute-done.12.refs_2_
  67.3 2.5 %collective-permute-done.11.refs_1_ = f32[16,1280]{1,0:T(8,128)S(1)} collective-permute-done((f32[16,1280]{1,0:T(8,128)S(1)}, f32[16,1280]{1,0:T(8,128)S(1)}, u32[]{:S(2)}, u32[]{:S(2)}) %collective-permute-start.11) | collective-permute-done | bytes 81952 | tf_op jit(solution)/shard_map/ppermute | solution.py:421
  69.9 0.0 copy-start
  69.9 0.0 copy-start.3
  69.9 0.0 collective-permute-done.18.recv_ref
  69.9 0.8 collective-permute-start.21
  70.7 3.2 %collective-permute-start.20 = (f32[16,1280]{1,0:T(8,128)S(1)}, f32[16,1280]{1,0:T(8,128)S(1)}, u32[]{:S(2)}, u32[]{:S(2)}) collective-permute-start(f32[16,1280]{1,0:T(8,128)S(1)} %total.3.refs_4_), channel_id=1, source_target_pairs={{0,16},{8,24},{16,0},{24,8},{1,17},{9,25},{17,1},{25,9},{2,18},{10... | collective-permute-start | bytes 245768 | tf_op jit(solution)/shard_map/ppermute | solution.py:421
  73.9 0.0 collective-permute-start.19
  73.9 0.0 collective-permute-done.22.recv_ref
  73.9 0.0 copy-done
  73.9 0.0 copy-done.3
  73.9 2.5 %table_part.1 = (f32[512,512]{1,0:T(8,128)}, f32[512]{0:T(512)}) custom-call(f32[1056,128]{1,0:T(8,128)S(1)} %get-tuple-element.97.keep_ref, f32[1056,128]{1,0:T(8,128)S(1)} %collective-permute-done.22.recv_ref, f32[512,512]{1,0:T(8,128)S(1)} %copy-done, f32[512]{0:T(512)S(1)} %copy-done.3), custom_call_target="tpu_custom_call" | custom-call | flops 1000000000 | bytes 65536 | tf_op jit(solution)/shard_map/table_part/pallas_call | solution.py:403
  76.4 0.0 collective-permute-done.21.refs_7_
  76.4 0.0 collective-permute-done.20.refs_6_
  76.4 1.9 %collective-permute-done.19.refs_5_ = f32[16,1280]{1,0:T(8,128)S(1)} collective-permute-done((f32[16,1280]{1,0:T(8,128)S(1)}, f32[16,1280]{1,0:T(8,128)S(1)}, u32[]{:S(2)}, u32[]{:S(2)}) %collective-permute-start.19) | collective-permute-done | bytes 81952 | tf_op jit(solution)/shard_map/ppermute | solution.py:421
  78.3 0.9 %gather.1 = (f32[4,16,2048]{2,1,0:T(8,128)}, f32[4,16,512]{2,1,0:T(8,128)}) custom-call(f32[16,1280]{1,0:T(8,128)S(1)} %total.2.refs_0_, f32[16,1280]{1,0:T(8,128)S(1)} %collective-permute-done.11.refs_1_, f32[16,1280]{1,0:T(8,128)S(1)} %collective-permute-done.12.refs_2_, f32[16,1280]{1,0:T(8,128)S(1)} %collective-permute-done.13.refs_3_, ...), custom_call_target="tpu_custom_call" | custom-call | flops 1000000000 | bytes 65536 | tf_op jit(solution)/shard_map/gather/pallas_call | solution.py:403
  (4 shorter events, 0.1 us)
Async XLA Ops:
  9.4 4.5 %collective-permute-start = (f32[256,1536]{1,0:T(8,128)S(1)}, f32[256,1536]{1,0:T(8,128)S(1)}, u32[]{:S(2)}, u32[]{:S(2)}) collective-permute-start(f32[256,1536]{1,0:T(8,128)S(1)} %get-tuple-element.60), channel_id=1, source_target_pairs={{0,1},{1,0},{2,3},{3,2},{4,5},{5,4},{6,7},{7,6},{8,9},{9,8},{10,11... | collective-permute-start | bytes 4718600 | tf_op jit(solution)/shard_map/ppermute | solution.py:448
  10.0 3.9 %copy-start.1 = (s32[1,32,16]{1,2,0:T(8,128)S(1)}, s32[1,32,16]{1,2,0:T(8,128)}, u32[]{:S(2)}) copy-start(s32[1,32,16]{1,2,0:T(8,128)} %param.14) | copy-start | bytes 6148
  10.0 3.9 %copy-start.2 = (s32[1,512]{1,0:T(1,128)S(1)}, s32[1,512]{1,0:T(1,128)}, u32[]{:S(2)}) copy-start(s32[1,512]{1,0:T(1,128)} %slot_ref.1) | copy-start | bytes 6148
  13.8 2.7 %collective-permute-start.1 = (f32[256,1024]{1,0:T(8,128)S(1)}, f32[256,1024]{1,0:T(8,128)S(1)}, u32[]{:S(2)}, u32[]{:S(2)}) collective-permute-start(f32[256,1024]{1,0:T(8,128)S(1)} %get-tuple-element.73), channel_id=1, source_target_pairs={{0,1},{1,0},{2,3},{3,2},{4,5},{5,4},{6,7},{7,6},{8,9},{9,8},{10,11... | collective-permute-start | bytes 3145736 | tf_op jit(solution)/shard_map/ppermute | solution.py:452
  16.8 18.0 %collective-permute-start.2 = (f32[2,64,1280]{2,1,0:T(8,128)S(1)}, f32[2,64,1280]{2,1,0:T(8,128)S(1)}, u32[]{:S(2)}, u32[]{:S(2)}) collective-permute-start(f32[2,64,1280]{2,1,0:T(8,128)S(1)} %get-tuple-element.75), channel_id=1, source_target_pairs={{0,8},{8,0},{16,24},{24,16},{1,9},{9,1},{17,25},{25,17},{2,10},{10... | collective-permute-start | bytes 1966088 | tf_op jit(solution)/shard_map/ppermute | solution.py:421
  19.7 16.5 %collective-permute-start.3 = (f32[2,64,1280]{2,1,0:T(8,128)S(1)}, f32[2,64,1280]{2,1,0:T(8,128)S(1)}, u32[]{:S(2)}, u32[]{:S(2)}) collective-permute-start(f32[2,64,1280]{2,1,0:T(8,128)S(1)} %get-tuple-element.77), channel_id=1, source_target_pairs={{0,16},{8,24},{16,0},{24,8},{1,17},{9,25},{17,1},{25,9},{2,18},{10... | collective-permute-start | bytes 1966088 | tf_op jit(solution)/shard_map/ppermute | solution.py:421
  21.2 17.2 %collective-permute-start.4 = (f32[520,128]{1,0:T(8,128)S(1)}, f32[520,128]{1,0:T(8,128)S(1)}, u32[]{:S(2)}, u32[]{:S(2)}) collective-permute-start(f32[520,128]{1,0:T(8,128)S(1)} %get-tuple-element.68), channel_id=1, source_target_pairs={{0,2},{1,3},{2,4},{3,5},{4,6},{5,7},{6,0},{7,1},{8,10},{9,11},{10,... | collective-permute-start | bytes 798728 | tf_op jit(solution)/shard_map/ppermute | solution.py:460
  22.8 19.7 %collective-permute-start.5 = (f32[520,128]{1,0:T(8,128)S(1)}, f32[520,128]{1,0:T(8,128)S(1)}, u32[]{:S(2)}, u32[]{:S(2)}) collective-permute-start(f32[520,128]{1,0:T(8,128)S(1)} %get-tuple-element.69), channel_id=1, source_target_pairs={{0,4},{1,5},{2,6},{3,7},{4,0},{5,1},{6,2},{7,3},{8,12},{9,13},{10,... | collective-permute-start | bytes 798728 | tf_op jit(solution)/shard_map/ppermute | solution.py:460
  25.4 17.1 %collective-permute-start.6 = (f32[520,128]{1,0:T(8,128)S(1)}, f32[520,128]{1,0:T(8,128)S(1)}, u32[]{:S(2)}, u32[]{:S(2)}) collective-permute-start(f32[520,128]{1,0:T(8,128)S(1)} %get-tuple-element.70), channel_id=1, source_target_pairs={{0,6},{1,7},{2,0},{3,1},{4,2},{5,3},{6,4},{7,5},{8,14},{9,15},{10,... | collective-permute-start | bytes 798728 | tf_op jit(solution)/shard_map/ppermute | solution.py:460
  36.3 8.7 %collective-permute-start.7 = (f32[64,1280]{1,0:T(8,128)S(1)}, f32[64,1280]{1,0:T(8,128)S(1)}, u32[]{:S(2)}, u32[]{:S(2)}) collective-permute-start(f32[64,1280]{1,0:T(8,128)S(1)} %get-tuple-element.79), channel_id=1, source_target_pairs={{0,16},{8,24},{16,0},{24,8},{1,17},{9,25},{17,1},{25,9},{2,18},{10... | collective-permute-start | bytes 983048 | tf_op jit(solution)/shard_map/ppermute | solution.py:421
  37.9 8.3 %collective-permute-start.8 = (f32[64,1280]{1,0:T(8,128)S(1)}, f32[64,1280]{1,0:T(8,128)S(1)}, u32[]{:S(2)}, u32[]{:S(2)}) collective-permute-start(f32[64,1280]{1,0:T(8,128)S(1)} %get-tuple-element.80), channel_id=1, source_target_pairs={{0,8},{8,0},{16,24},{24,16},{1,9},{9,1},{17,25},{25,17},{2,10},{10... | collective-permute-start | bytes 983048 | tf_op jit(solution)/shard_map/ppermute | solution.py:421
  46.3 7.6 %collective-permute-start.9 = (f32[2,16,1280]{2,1,0:T(8,128)S(1)}, f32[2,16,1280]{2,1,0:T(8,128)S(1)}, u32[]{:S(2)}, u32[]{:S(2)}) collective-permute-start(f32[2,16,1280]{2,1,0:T(8,128)S(1)} %get-tuple-element.89), channel_id=1, source_target_pairs={{0,2},{1,3},{2,0},{3,1},{4,6},{5,7},{6,4},{7,5},{8,10},{9,11},{10,... | collective-permute-start | bytes 491528 | tf_op jit(solution)/shard_map/ppermute | solution.py:477
  48.9 8.8 %collective-permute-start.14 = (f32[2,16,1280]{2,1,0:T(8,128)S(1)}, f32[2,16,1280]{2,1,0:T(8,128)S(1)}, u32[]{:S(2)}, u32[]{:S(2)}) collective-permute-start(f32[2,16,1280]{2,1,0:T(8,128)S(1)} %get-tuple-element.94), channel_id=1, source_target_pairs={{0,2},{1,3},{2,0},{3,1},{4,6},{5,7},{6,4},{7,5},{8,10},{9,11},{10,... | collective-permute-start | bytes 491528 | tf_op jit(solution)/shard_map/ppermute | solution.py:477
  49.0 10.9 %collective-permute-start.15 = (f32[520,128]{1,0:T(8,128)S(1)}, f32[520,128]{1,0:T(8,128)S(1)}, u32[]{:S(2)}, u32[]{:S(2)}) collective-permute-start(f32[520,128]{1,0:T(8,128)S(1)} %get-tuple-element.83), channel_id=1, source_target_pairs={{0,8},{8,0},{16,24},{24,16},{1,9},{9,1},{17,25},{25,17},{2,10},{10... | collective-permute-start | bytes 798728 | tf_op jit(solution)/shard_map/ppermute | solution.py:421
  49.6 14.5 %collective-permute-start.16 = (f32[520,128]{1,0:T(8,128)S(1)}, f32[520,128]{1,0:T(8,128)S(1)}, u32[]{:S(2)}, u32[]{:S(2)}) collective-permute-start(f32[520,128]{1,0:T(8,128)S(1)} %get-tuple-element.84), channel_id=1, source_target_pairs={{0,16},{8,24},{16,0},{24,8},{1,17},{9,25},{17,1},{25,9},{2,18},{10... | collective-permute-start | bytes 798728 | tf_op jit(solution)/shard_map/ppermute | solution.py:421
  50.1 17.1 %collective-permute-start.17 = (f32[520,128]{1,0:T(8,128)S(1)}, f32[520,128]{1,0:T(8,128)S(1)}, u32[]{:S(2)}, u32[]{:S(2)}) collective-permute-start(f32[520,128]{1,0:T(8,128)S(1)} %get-tuple-element.85), channel_id=1, source_target_pairs={{0,24},{8,16},{16,8},{24,0},{1,25},{9,17},{17,9},{25,1},{2,26},{10... | collective-permute-start | bytes 798728 | tf_op jit(solution)/shard_map/ppermute | solution.py:421
  54.0 5.4 %collective-permute-start.10 = (f32[1,16,1280]{2,1,0:T(8,128)S(1)}, f32[1,16,1280]{2,1,0:T(8,128)S(1)}, u32[]{:S(2)}, u32[]{:S(2)}) collective-permute-start(f32[1,16,1280]{2,1,0:T(8,128)S(1)} %get-tuple-element.91), channel_id=1, source_target_pairs={{0,4},{1,5},{2,6},{3,7},{4,0},{5,1},{6,2},{7,3},{8,12},{9,13},{10,... | collective-permute-start | bytes 245768 | tf_op jit(solution)/shard_map/ppermute | solution.py:477
  57.7 12.1 %collective-permute-start.18 = (f32[1,16,1280]{2,1,0:T(8,128)S(1)}, f32[1,16,1280]{2,1,0:T(8,128)S(1)}, u32[]{:S(2)}, u32[]{:S(2)}) collective-permute-start(f32[1,16,1280]{2,1,0:T(8,128)S(1)} %get-tuple-element.100), channel_id=1, source_target_pairs={{0,4},{1,5},{2,6},{3,7},{4,0},{5,1},{6,2},{7,3},{8,12},{9,13},{10,... | collective-permute-start | bytes 245768 | tf_op jit(solution)/shard_map/ppermute | solution.py:477
  59.4 7.9 %collective-permute-start.13 = (f32[16,1280]{1,0:T(8,128)S(1)}, f32[16,1280]{1,0:T(8,128)S(1)}, u32[]{:S(2)}, u32[]{:S(2)}) collective-permute-start(f32[16,1280]{1,0:T(8,128)S(1)} %total.2.refs_0_), channel_id=1, source_target_pairs={{0,24},{8,16},{16,8},{24,0},{1,25},{9,17},{17,9},{25,1},{2,26},{10... | collective-permute-start | bytes 245768 | tf_op jit(solution)/shard_map/ppermute | solution.py:421
  59.9 7.4 %collective-permute-start.12 = (f32[16,1280]{1,0:T(8,128)S(1)}, f32[16,1280]{1,0:T(8,128)S(1)}, u32[]{:S(2)}, u32[]{:S(2)}) collective-permute-start(f32[16,1280]{1,0:T(8,128)S(1)} %total.2.refs_0_), channel_id=1, source_target_pairs={{0,16},{8,24},{16,0},{24,8},{1,17},{9,25},{17,1},{25,9},{2,18},{10... | collective-permute-start | bytes 245768 | tf_op jit(solution)/shard_map/ppermute | solution.py:421
  64.1 5.8 %collective-permute-start.11 = (f32[16,1280]{1,0:T(8,128)S(1)}, f32[16,1280]{1,0:T(8,128)S(1)}, u32[]{:S(2)}, u32[]{:S(2)}) collective-permute-start(f32[16,1280]{1,0:T(8,128)S(1)} %total.2.refs_0_), channel_id=1, source_target_pairs={{0,8},{8,0},{16,24},{24,16},{1,9},{9,1},{17,25},{25,17},{2,10},{10... | collective-permute-start | bytes 245768 | tf_op jit(solution)/shard_map/ppermute | solution.py:421
  67.2 6.7 %collective-permute-start.22 = (f32[1056,128]{1,0:T(8,128)S(1)}, f32[1056,128]{1,0:T(8,128)S(1)}, u32[]{:S(2)}, u32[]{:S(2)}) collective-permute-start(f32[1056,128]{1,0:T(8,128)S(1)} %get-tuple-element.98), channel_id=1, source_target_pairs={{0,1},{1,0},{2,3},{3,2},{4,5},{5,4},{6,7},{7,6},{8,9},{9,8},{10,11... | collective-permute-start | bytes 1622024 | tf_op jit(solution)/shard_map/ppermute | solution.py:500
  69.9 4.0 %copy-start = (f32[512,512]{1,0:T(8,128)S(1)}, f32[512,512]{1,0:T(8,128)}, u32[]{:S(2)}) copy-start(f32[512,512]{1,0:T(8,128)} %table_ref.1) | copy-start | bytes 3145732
  69.9 4.0 %copy-start.3 = (f32[512]{0:T(512)S(1)}, f32[512]{0:T(512)}, u32[]{:S(2)}) copy-start(f32[512]{0:T(512)} %accum_ref.1) | copy-start | bytes 6148
  69.9 6.5 %collective-permute-start.21 = (f32[16,1280]{1,0:T(8,128)S(1)}, f32[16,1280]{1,0:T(8,128)S(1)}, u32[]{:S(2)}, u32[]{:S(2)}) collective-permute-start(f32[16,1280]{1,0:T(8,128)S(1)} %total.3.refs_4_), channel_id=1, source_target_pairs={{0,24},{8,16},{16,8},{24,0},{1,25},{9,17},{17,9},{25,1},{2,26},{10... | collective-permute-start | bytes 245768 | tf_op jit(solution)/shard_map/ppermute | solution.py:421
  70.7 5.8 %collective-permute-start.20 = (f32[16,1280]{1,0:T(8,128)S(1)}, f32[16,1280]{1,0:T(8,128)S(1)}, u32[]{:S(2)}, u32[]{:S(2)}) collective-permute-start(f32[16,1280]{1,0:T(8,128)S(1)} %total.3.refs_4_), channel_id=1, source_target_pairs={{0,16},{8,24},{16,0},{24,8},{1,17},{9,25},{17,1},{25,9},{2,18},{10... | collective-permute-start | bytes 245768 | tf_op jit(solution)/shard_map/ppermute | solution.py:421
  73.9 4.4 %collective-permute-start.19 = (f32[16,1280]{1,0:T(8,128)S(1)}, f32[16,1280]{1,0:T(8,128)S(1)}, u32[]{:S(2)}, u32[]{:S(2)}) collective-permute-start(f32[16,1280]{1,0:T(8,128)S(1)} %total.3.refs_4_), channel_id=1, source_target_pairs={{0,8},{8,0},{16,24},{24,16},{1,9},{9,1},{17,25},{25,17},{2,10},{10... | collective-permute-start | bytes 245768 | tf_op jit(solution)/shard_map/ppermute | solution.py:421

commit v15 on v13

--- a/solution.py
+++ b/solution.py
@@ -16,6 +16,7 @@
 f32, bf16 = jnp.float32, jnp.bfloat16
 MIB = 1024 * 1024
 STEP = 256
+TILE = 32
 LANES = 128
 ID_ROWS = 8
 
@@ -63,10 +64,14 @@
     return jnp.where(lax.broadcasted_iota(jnp.int32, (width, width), 1) == wanted, 1.0, 0.0).astype(bf16)
 
 
+def tiles_of(start, count, size):
+    return [pl.ds(start + at, size) for at in range(0, count, size)]
+
+
 def forward_kernel(rows_size, dp_size, len_ref, ev_hbm, cot_hbm, win_hbm, wout_hbm,
                    keep_ref, send_ref, hid_ref, dsilu_ref, gatt_ref, gpre_ref, normed_t_ref,
-                   ev_ref, cot_ref, win_ref, normed_ref, user_ref, duser_ref, att_ref, mixed_ref, masked_ref, dval_ref, weights_ref,
-                   wout_ref, order_ref, grad_mixed_ref, arrived):
+                   ev_ref, masked_ref, win_ref, inv_ref, normed_ref, user_ref, duser_ref, att_ref, mixed_ref, dval_ref,
+                   weights_ref, wout_ref, order_ref, grad_mixed_ref, cot_ref, pre_ref, raw_ref, arrived):
     tokens, width = ev_ref.shape
     copies = [pltpu.make_async_copy(ev_hbm, ev_ref, arrived.at[0])]
     for c in range(4):
@@ -78,86 +83,88 @@
         copy.start()
     order_ref[...] = owner_order(width, rows_size, dp_size)
     hd = width // HEADS
-    length = len_ref[0]
-    inv_len = 1.0 / length.astype(f32)
     scale = hd ** -0.5
     steps = tokens // STEP
 
     copies[0].wait()
-    for i in range(steps):
-        rows = pl.ds(i * STEP, STEP)
-        xhat, _ = standardize(ev_ref[rows, :].astype(f32))
-        normed_ref[rows, :] = xhat.astype(bf16)
+    for tile in tiles_of(0, tokens, TILE):
+        xhat, _ = standardize(ev_ref[tile, :].astype(f32))
+        normed_ref[tile, :] = xhat.astype(bf16)
 
     def project(i, c):
         rows = pl.ds(i * STEP, STEP)
-        pre = dot_nn(normed_ref[rows, :], win_ref[:, c * width:(c + 1) * width])
-        sig = 0.5 + 0.5 * jnp.tanh(0.5 * pre)
-        hid = pre * sig
-        dsilu = sig * (1.0 + (pre - hid))
-        if c == 0:
-            user_ref[rows, :] = hid.astype(bf16)
-            duser_ref[rows, :] = dsilu
-        else:
-            cols = slice((c - 1) * width, c * width)
-            hid_ref[rows, cols] = hid.astype(bf16)
-            if c == 1:
-                dval_ref[rows, :] = dsilu
+        slot = (c * steps + i) % pre_ref.shape[0]
+        pre_ref[slot] = dot_nn(normed_ref[rows, :], win_ref[:, c * width:(c + 1) * width])
+        for at in range(0, STEP, TILE):
+            tile = pl.ds(i * STEP + at, TILE)
+            pre = pre_ref[slot, at:at + TILE, :]
+            sig = 0.5 + 0.5 * jnp.tanh(0.5 * pre)
+            hid = pre * sig
+            dsilu = sig * (1.0 + (pre - hid))
+            if c == 0:
+                user_ref[tile, :] = hid.astype(bf16)
+                duser_ref[tile, :] = dsilu
             else:
-                dsilu_ref[rows, (c - 2) * width:(c - 1) * width] = dsilu.astype(bf16)
+                hid_ref[tile, (c - 1) * width:c * width] = hid.astype(bf16)
+                if c == 1:
+                    dval_ref[tile, :] = dsilu
+                else:
+                    dsilu_ref[tile, (c - 2) * width:(c - 1) * width] = dsilu.astype(bf16)
 
     for c in range(4):
         copies[1 + c].wait()
         for i in range(steps):
             project(i, c)
 
-    copies[5].wait()
-    copies[6].wait()
-    tri = lax.broadcasted_iota(jnp.int32, (STEP, STEP), 0) >= lax.broadcasted_iota(jnp.int32, (STEP, STEP), 1)
+    for copy in copies[5:]:
+        copy.wait()
+    length = len_ref[0]
+    inv_len = 1.0 / length.astype(f32)
+    inv_ref[...] = jnp.full(inv_ref.shape, inv_len, f32)
     for h in range(HEADS):
         v_cols = slice(h * hd, (h + 1) * hd)
         q_cols = slice(width + h * hd, width + (h + 1) * hd)
         k_cols = slice(2 * width + h * hd, 2 * width + (h + 1) * hd)
         for i in range(steps):
             rows = pl.ds(i * STEP, STEP)
-            query = hid_ref[rows, q_cols]
-            total = None
             for j in range(i + 1):
                 keys = pl.ds(j * STEP, STEP)
-                half = dot_nt(query, hid_ref[keys, k_cols]) * (0.5 * scale)
-                weights = (half + half * jnp.tanh(half)) * inv_len
-                if i == j:
-                    weights = jnp.where(tri, weights, 0.0)
-                weights = weights.astype(bf16)
-                weights_ref[h, rows, keys] = weights
-                part = dot_nn(weights, hid_ref[keys, v_cols])
-                total = part if total is None else total + part
-            att_ref[rows, v_cols] = total
+                slot = (h * 3 + i + j) % raw_ref.shape[0]
+                raw_ref[slot] = dot_nt(hid_ref[rows, q_cols], hid_ref[keys, k_cols])
+                for at in range(0, STEP, 2 * TILE):
+                    half = raw_ref[slot, at:at + 2 * TILE, :] * (0.5 * scale)
+                    weights = (half + half * jnp.tanh(half)) * inv_len
+                    if i == j:
+                        row = at + lax.broadcasted_iota(jnp.int32, weights.shape, 0)
+                        weights = jnp.where(row >= lax.broadcasted_iota(jnp.int32, weights.shape, 1), weights, 0.0)
+                    weights_ref[h, pl.ds(i * STEP + at, 2 * TILE), keys] = weights.astype(bf16)
+            seen = pl.ds(0, (i + 1) * STEP)
+            att_ref[rows, v_cols] = dot_nn(weights_ref[h, rows, seen], hid_ref[seen, v_cols])
         for i in range(h, steps, HEADS):
             rows = pl.ds(i * STEP, STEP)
             normed_t_ref[rows, :] = dot_nt(order_ref[rows, :], normed_ref[...]).astype(bf16)
         for i in range(h - HEADS // 2, steps, HEADS):
             if i >= 0:
                 rows = pl.ds(i * STEP, STEP)
-                masked_ref[rows, :] = masked_rows(cot_ref[rows, :], i * STEP, length).astype(bf16)
+                for tile in tiles_of(i * STEP, STEP, TILE):
+                    masked_ref[tile, :] = masked_rows(cot_ref[tile, :], tile.start, length).astype(bf16)
                 grad_mixed_ref[rows, :] = dot_nt(masked_ref[rows, :], wout_ref[...])
 
-    for i in range(steps):
-        rows = pl.ds(i * STEP, STEP)
-        ahat, inv = standardize(att_ref[rows, :])
-        user = user_ref[rows, :].astype(f32)
-        mixed_ref[rows, :] = (ahat * user).astype(bf16)
-        grad_mixed = grad_mixed_ref[rows, :]
-        gpre_ref[rows, :width] = (grad_mixed * ahat * duser_ref[rows, :]).astype(bf16)
+    for tile in tiles_of(0, tokens, TILE // 2):
+        ahat, inv = standardize(att_ref[tile, :])
+        user = user_ref[tile, :].astype(f32)
+        mixed_ref[tile, :] = (ahat * user).astype(bf16)
+        grad_mixed = grad_mixed_ref[tile, :]
+        gpre_ref[tile, :width] = (grad_mixed * ahat * duser_ref[tile, :]).astype(bf16)
         e = grad_mixed * user
-        gatt_ref[rows, :] = (inv * (e - jnp.mean(e, axis=-1, keepdims=True)
+        gatt_ref[tile, :] = (inv * (e - jnp.mean(e, axis=-1, keepdims=True)
                                     - ahat * jnp.mean(e * ahat, axis=-1, keepdims=True))).astype(bf16)
 
     for h in range(HEADS):
         v_cols = slice(h * hd, (h + 1) * hd)
         for j in range(steps):
-            keys, rest = pl.ds(j * STEP, STEP), pl.ds(j * STEP, tokens - j * STEP)
-            grad_v = dot_tn(weights_ref[h, rest, keys], gatt_ref[rest, v_cols])
+            keys, later = pl.ds(j * STEP, STEP), pl.ds(j * STEP, tokens - j * STEP)
+            grad_v = dot_tn(weights_ref[h, later, keys], gatt_ref[later, v_cols])
             gpre_ref[keys, width + h * hd:width + (h + 1) * hd] = (grad_v * dval_ref[keys, v_cols]).astype(bf16)
 
     mixed_t = dot_nt(order_ref[...], mixed_ref[...]).astype(bf16)
@@ -167,41 +174,39 @@
         ref[:, width:] = dot_nn(normed_t_ref[start:start + half, :], gpre_ref[...])
 
 
-def attention_kernel(len_ref, hid_ref, dsilu_ref, gatt_ref, normed_t_ref, keep_ref, send_ref, gpre_ref):
+def attention_kernel(inv_ref, hid_ref, dsilu_ref, gatt_ref, normed_t_ref, keep_ref, send_ref, gpre_ref,
+                     raw_ref, weight_ref, score_ref):
     tokens, width = gatt_ref.shape
     hd = width // HEADS
-    inv_len = 1.0 / len_ref[0].astype(f32)
     scale = hd ** -0.5
     steps = tokens // STEP
-
-    factor = 0.5 * inv_len * scale
-    tri = lax.broadcasted_iota(jnp.int32, (STEP, STEP), 0) <= lax.broadcasted_iota(jnp.int32, (STEP, STEP), 1)
+    factor = inv_ref[:1, :hd] * (0.5 * scale)
+
     for h in range(HEADS):
         v_cols = slice(h * hd, (h + 1) * hd)
         q_cols = slice(width + h * hd, width + (h + 1) * hd)
         k_cols = slice(2 * width + h * hd, 2 * width + (h + 1) * hd)
-        grad_q = [None] * steps
         for j in range(steps):
             keys = pl.ds(j * STEP, STEP)
-            key, value = hid_ref[keys, k_cols], hid_ref[keys, v_cols]
-            grad_k = None
             for i in range(j, steps):
                 rows = pl.ds(i * STEP, STEP)
-                query, gatt = hid_ref[rows, q_cols], gatt_ref[rows, v_cols]
-                half = dot_nt(key, query) * (0.5 * scale)
-                gate = jnp.tanh(half)
-                dsilu = (1.0 + gate) * (1.0 + half * (1.0 - gate))
-                gscore = dot_nt(value, gatt) * dsilu
-                if i == j:
-                    gscore = jnp.where(tri, gscore, 0.0)
-                gscore = gscore.astype(bf16)
-                pk, pq = dot_nn(gscore, query), dot_tn(gscore, key)
-                grad_k = pk if grad_k is None else grad_k + pk
-                grad_q[i] = pq if grad_q[i] is None else grad_q[i] + pq
+                slot = (h * 3 + i + j) % raw_ref.shape[0]
+                raw_ref[slot] = dot_nt(hid_ref[keys, k_cols], hid_ref[rows, q_cols])
+                weight_ref[slot] = dot_nt(hid_ref[keys, v_cols], gatt_ref[rows, v_cols])
+                for at in range(0, STEP, TILE):
+                    half = raw_ref[slot, at:at + TILE, :] * (0.5 * scale)
+                    gate = jnp.tanh(half)
+                    gscore = weight_ref[slot, at:at + TILE, :] * ((1.0 + gate) * (1.0 + half * (1.0 - gate)))
+                    if i == j:
+                        row = at + lax.broadcasted_iota(jnp.int32, gscore.shape, 0)
+                        gscore = jnp.where(row <= lax.broadcasted_iota(jnp.int32, gscore.shape, 1), gscore, 0.0)
+                    score_ref[h % 2, pl.ds(j * STEP + at, TILE), rows] = gscore.astype(bf16)
+        for j in range(steps):
+            keys, later, seen = pl.ds(j * STEP, STEP), pl.ds(j * STEP, tokens - j * STEP), pl.ds(0, (j + 1) * STEP)
+            grad_k = dot_nn(score_ref[h % 2, keys, later], hid_ref[later, q_cols])
             gpre_ref[keys, q_cols] = (grad_k * (dsilu_ref[keys, q_cols].astype(f32) * factor)).astype(bf16)
-        for i in range(steps):
-            rows = pl.ds(i * STEP, STEP)
-            gpre_ref[rows, v_cols] = (grad_q[i] * (dsilu_ref[rows, v_cols].astype(f32) * factor)).astype(bf16)
+            grad_q = dot_tn(score_ref[h % 2, seen, keys], hid_ref[seen, k_cols])
+            gpre_ref[keys, v_cols] = (grad_q * (dsilu_ref[keys, v_cols].astype(f32) * factor)).astype(bf16)
 
     half = width // 2
     for ref, start in ((send_ref, half), (keep_ref, 0)):
@@ -216,25 +221,29 @@
     return part * rows + chip * 2 + core, place
 
 
-def events_kernel(rows_size, dp_size, len_ref, ev_ref, cot_ref, win_ref, slot_ref, slot_row_ref, gpre_uv_ref, gpre_qk_ref, *refs):
-    *send_refs, hi_ref, lo_ref, rows_ref = refs
+def events_kernel(rows_size, dp_size, ev_ref, masked_ref, win_ref, slot_ref, slot_row_ref, gpre_uv_ref, gpre_qk_ref, *refs):
+    *send_refs, hi_ref, lo_ref, rows_ref, grad_ref, onehot_ref = refs
     tokens, width = ev_ref.shape
     capacity, owners = slot_row_ref.shape
-    length = len_ref[0]
     for i in range(tokens // STEP):
         rows = pl.ds(i * STEP, STEP)
-        xhat, inv = standardize(ev_ref[rows, :].astype(f32))
-        grad_normed = dot_nt(gpre_uv_ref[rows, :], win_ref[:, :2 * width]) + dot_nt(gpre_qk_ref[rows, :], win_ref[:, 2 * width:])
-        grad = masked_rows(cot_ref[rows, :], i * STEP, length) + inv * (
-            grad_normed - jnp.mean(grad_normed, axis=-1, keepdims=True)
-            - xhat * jnp.mean(grad_normed * xhat, axis=-1, keepdims=True))
-        high = grad.astype(bf16)
-        hi_ref[rows, :] = high
-        lo_ref[rows, :] = (grad - high.astype(f32)).astype(bf16)
+        grad_ref[rows, :] = dot_nt(gpre_uv_ref[rows, :], win_ref[:, :2 * width]) + dot_nt(gpre_qk_ref[rows, :], win_ref[:, 2 * width:])
+        for tile in tiles_of(i * STEP, STEP, TILE // 2):
+            xhat, inv = standardize(ev_ref[tile, :].astype(f32))
+            grad_normed = grad_ref[tile, :]
+            grad = masked_ref[tile, :].astype(f32) + inv * (
+                grad_normed - jnp.mean(grad_normed, axis=-1, keepdims=True)
+                - xhat * jnp.mean(grad_normed * xhat, axis=-1, keepdims=True))
+            high = grad.astype(bf16)
+            hi_ref[tile, :] = high
+            lo_ref[tile, :] = (grad - high.astype(f32)).astype(bf16)
 
     slots = rows_ref.shape[0]
     owner, place = slots_in_order(lax.broadcasted_iota(jnp.int32, (slots, 1), 0), capacity, dp_size, rows_size)
-    rows_ref[...] = one_hot_rows(slot_ref[...], owner * capacity + place, hi_ref, lo_ref)
+    wanted = owner * capacity + place
+    for at in range(0, slots, 2 * TILE):
+        onehot_ref[at:at + 2 * TILE, :] = jnp.where(wanted[at:at + 2 * TILE] == slot_ref[...], 1.0, 0.0).astype(bf16)
+    rows_ref[...] = dot_nn(onehot_ref[...], hi_ref[...]) + dot_nn(onehot_ref[...], lo_ref[...])
     owner, place = slots_in_order(lax.broadcasted_iota(jnp.int32, (1, slots), 1), capacity, dp_size, rows_size)
     chosen = lax.broadcasted_iota(jnp.int32, (owners, slots), 0) == owner
     mine = lax.broadcasted_iota(jnp.int32, (capacity, slots), 0) == place
@@ -396,17 +405,17 @@
     return jax.ShapeDtypeStruct(dims, dtype)
 
 
-def call(kernel, name, out_shape, args, scalars=0, scratch=(), far=0, long=False, grant=4, apart=(), either=()):
-    place = [None] * scalars + [pltpu.HBM] * far + [pltpu.VMEM] * (len(args) - scalars - far)
-    held = [None if i in either else pltpu.HBM if i in apart else p for i, p in enumerate(place)]
-    args = [a if p is None else pltpu.with_memory_space_constraint(a, p) for a, p in zip(args, held)]
+def call(kernel, name, out_shape, args, scratch=(), far=0, long=False, grant=4):
+    place = [pltpu.SMEM if a.size == 1 else pltpu.HBM if i < far else pltpu.VMEM for i, a in enumerate(args)]
+    args = [a if p is pltpu.SMEM else pltpu.with_memory_space_constraint(a, p) for a, p in zip(args, place)]
     return pl.pallas_call(
         kernel,
         name=name,
-        in_specs=[pl.BlockSpec(memory_space=p or pltpu.SMEM) for p in place],
+        in_specs=[pl.BlockSpec(memory_space=p) for p in place],
         out_specs=[vmem()] * len(out_shape),
         out_shape=list(out_shape),
-        scratch_shapes=[pltpu.VMEM(dims, dtype) for dims, dtype in scratch] + [pltpu.SemaphoreType.DMA((7,))] * (far > 0),
+        scratch_shapes=[pltpu.VMEM(dims, dtype) for dims, dtype in scratch]
+        + [pltpu.SemaphoreType.DMA((7,))] * (far > 0),
         compiler_params=pltpu.CompilerParams(vmem_limit_bytes=grant * MIB),
         cost_estimate=pl.CostEstimate(flops=100_000_000_000 if long else 1_000_000_000, bytes_accessed=1 << 16, transcendentals=0),
     )(*args)
@@ -429,7 +438,7 @@
     by_chip = lambda v: v.reshape(*v.shape[:-2], chips, piece, v.shape[-1])
     local = lambda *dims, dtype=f32: pltpu.VMEM(dims, dtype)
     sides = lambda cols: [local(width // 2, cols)] * 2
-    keep1, send1, hid, dsilu, gatt, gpre_uv, normed_t, events, cotangent, w_in = call(
+    keep1, send1, hid, dsilu, gatt, gpre_uv, normed_t, events, masked, w_in, inv_len = call(
         functools.partial(forward_kernel, rows_size, dp_size), "forward_part",
         sides(3 * width) + [
             local(tokens, 3 * width, dtype=bf16),
@@ -440,23 +449,27 @@
             local(tokens, width, dtype=bf16),
             local(tokens, width, dtype=bf16),
             local(*w_in.shape, dtype=bf16),
+            local(8, LANES),
         ],
-        (lengths, events, cotangent, w_in, w_out), 1,
+        (lengths, events, cotangent, w_in, w_out),
         [((tokens, width), bf16), ((tokens, width), bf16), ((tokens, width), f32), ((tokens, width), f32),
-         ((tokens, width), bf16), ((tokens, width), bf16), ((tokens, width), f32), ((HEADS, tokens, tokens), bf16),
-         (w_out.shape, bf16), ((width, width), bf16), ((tokens, width), f32)], far=4, long=True, grant=16)
+         ((tokens, width), bf16), ((tokens, width), f32), ((HEADS, tokens, tokens), bf16),
+         (w_out.shape, bf16), ((width, width), bf16), ((tokens, width), f32), ((tokens, width), bf16),
+         ((4, STEP, width), f32), ((4, STEP, STEP), f32)], far=5, long=True, grant=22)
     recv1 = lax.ppermute(send1, "rows", cores)
     keep2, send2, gpre_qk = call(
         attention_kernel, "attention_part", sides(2 * width) + [local(tokens, 2 * width, dtype=bf16)],
-        (lengths, hid, dsilu, gatt, normed_t), 1, long=True, grant=10)
+        (inv_len, hid, dsilu, gatt, normed_t),
+        [((4, STEP, STEP), f32), ((4, STEP, STEP), f32), ((2, tokens, tokens), bf16)], long=True, grant=12)
     recv2 = lax.ppermute(send2, "rows", cores)
     block = capacity * (width // LANES)
     gpre_uv = after(gpre_uv, recv1)
     sends = call(
         functools.partial(events_kernel, rows_size, dp_size), "events_part",
         [local(2 * dp_size * block + ID_ROWS, LANES)] * chips,
-        (lengths, events, cotangent, w_in, event_slot, slot_row[0].T, gpre_uv, gpre_qk), 1,
-        [((tokens, width), bf16), ((tokens, width), bf16), ((owners * capacity, width), f32)], grant=10, long=True)
+        (events, masked, w_in, event_slot, slot_row[0].T, gpre_uv, gpre_qk),
+        [((tokens, width), bf16), ((tokens, width), bf16), ((owners * capacity, width), f32), ((tokens, width), f32),
+         ((owners * capacity, tokens), bf16)], grant=12, long=True)
     ahead = lambda v, k: lax.ppermute(v, "rows", [(i, (i + 2 * k) % rows_size) for i in range(rows_size)])
     came = [sends[0]] + [ahead(sends[k], k) for k in range(1, chips)]
     cols = w_in.shape[1] + width
@@ -499,7 +512,7 @@
     slots = owners * capacity
     table_new, accum_new = call(
         functools.partial(table_kernel, dp_size, chips), "table_part", [shape(*item_table.shape), shape(*accumulator.shape)],
-        (keep, recv, item_table, accumulator), 0,
+        (keep, recv, item_table, accumulator),
         [((slots, width), f32), ((slots, width), bf16), ((slots, width), bf16)], grant=10)
     pieces[-1] = after(pieces[-1], accum_new)
     grad_in, grad_out = call(

time: 75.5 us -> 74 us (0.980)
  Pallas kernels: 18.5 us -> 16.8 us
    pallas_call x13, Pallas kernels: 18.5 us -> 16.8 us  [call(): pl.pallas_call(kernel, name=name, in_specs=[pl.BlockSpec(memory_space=p)...]
  transfers between devices with their start and end apart: 20 -> 20, of which waited for: 12 -> 12; matrix products, arithmetic and copies ran while one was open for 0% -> 0% of each run, Pallas kernels for 12% -> 10%
where the time goes in v15:
time: 74 us; the launch traced here: 73.9 us
  waiting for transfers between devices  31.1 us (42%)
  starting transfers between devices  24.5 us (33%)
  Pallas kernels  16.8 us (23%)
  between operations  1.41 us (2%)
    ppermute x10, waiting for transfers between devices, body(): lax.ppermute(v, 'dp', [(i, i ^ bit) for i in range(dp_size)])  17.8 us
    pallas_call x13, Pallas kernels, call(): pl.pallas_call(kernel, name=name, in_specs=[pl.BlockSpec(memory_space=p)...  16.8 us
    ppermute x10, starting transfers between devices, body(): lax.ppermute(v, 'dp', [(i, i ^ bit) for i in range(dp_size)])  13.6 us
    ppermute x4, waiting for transfers between devices, body(): lax.ppermute(v, 'rows', [(i, i ^ 2 << bit) for i in range(rows_size)])  8.86 us
    ppermute x3, starting transfers between devices, body(): lax.ppermute(v, 'rows', [(i, (i + 2 * k) % rows_size) for i in range(rows...  5.51 us
    ppermute x4, starting transfers between devices, body(): lax.ppermute(v, 'rows', [(i, i ^ 2 << bit) for i in range(rows_size)])  4.69 us
    ppermute x3, waiting for transfers between devices, body(): lax.ppermute(v, 'rows', [(i, (i + 2 * k) % rows_size) for i in range(rows...  4.05 us
  transfers between devices with their start and end apart: 20, of which 12 were waited for; matrix products, arithmetic and copies ran while one was open for 0% of the time, Pallas kernels for 10%

profile of v15, /device:TPU:0, one launch (start us, length us, event | category | flops | bytes accessed | tf_op | source)
XLA Modules:
  0.0 73.9 jit_solution(18081359255120723671)
XLA Ops:
  1.3 7.8 %forward_part.1 = (f32[256,1536]{1,0:T(8,128)S(1)}, f32[256,1536]{1,0:T(8,128)S(1)}, bf16[512,1536]{1,0:T(8,128)(2,1)S(1)}, bf16[512,1024]{1,0:T(8,128)(2,1)S(1)...) custom-call(s32[1]{0:T(128)S(6)} %copy.13.len_ref, ...), custom_call_target="tpu_custom_call" | custom-call | flops 99999997952 | bytes 65536 | tf_op jit(solution)/shard_map/forward_part/pallas_call | solution.py:411
  9.1 0.5 collective-permute-start
  9.6 0.0 copy-start.1
  9.6 0.0 copy-start.2
  9.7 2.6 %attention_part.1 = (f32[256,1024]{1,0:T(8,128)S(1)}, f32[256,1024]{1,0:T(8,128)S(1)}, bf16[512,1024]{1,0:T(8,128)(2,1)S(1)}) custom-call(f32[8,128]{1,0:T(8,128)S(1)} %get-tuple-element.62.inv_ref, bf16[512,1536]{1,0:T(8,128)(2,1)S(1)} %get-tuple-element.63.hid_ref, bf16[512,1024]{1,0:T(8,128)(2,1)S(1)} %get-tuple-element.64.dsilu_ref, ...), custom_call_target="tpu_custom_call" | custom-call | flops 99999997952 | bytes 65536 | tf_op jit(solution)/shard_map/attention_part/pallas_call | solution.py:411
  12.3 0.1 collective-permute-start.1
  12.4 0.3 collective-permute-done
  12.7 0.0 copy-done.1
  12.7 0.0 copy-done.2
  12.7 2.2 %events_part.1 = (f32[520,128]{1,0:T(8,128)S(1)}, f32[520,128]{1,0:T(8,128)S(1)}, f32[520,128]{1,0:T(8,128)S(1)}, f32[520,128]{1,0:T(8,128)S(1)}) custom-call(bf16[512,512]{1,0:T(8,128)(2,1)S(1)} %get-tuple-element.56.ev_ref, bf16[512,512]{1,0:T(8,128)(2,1)S(1)} %get-tuple-element.57.masked_ref, bf16[512,2048]{1,0:T(8,128)(2,1)S(1)} %get-tuple-element.58.win_ref, ...), custom_call_target="tpu_custom_call" | custom-call | flops 99999997952 | bytes 65536 | tf_op jit(solution)/shard_map/events_part/pallas_call | solution.py:411
  14.9 0.0 collective-permute-done.1
  15.0 0.3 first_sums.1
  15.3 2.9 %collective-permute-start.2 = (f32[2,64,1280]{2,1,0:T(8,128)S(1)}, f32[2,64,1280]{2,1,0:T(8,128)S(1)}, u32[]{:S(2)}, u32[]{:S(2)}) collective-permute-start(f32[2,64,1280]{2,1,0:T(8,128)S(1)} %get-tuple-element.76), channel_id=1, source_target_pairs={{0,8},{8,0},{16,24},{24,16},{1,9},{9,1},{17,25},{25,17},{2,10},{10... | collective-permute-start | bytes 1966088 | tf_op jit(solution)/shard_map/ppermute | solution.py:430
  18.2 1.5 %collective-permute-start.3 = (f32[2,64,1280]{2,1,0:T(8,128)S(1)}, f32[2,64,1280]{2,1,0:T(8,128)S(1)}, u32[]{:S(2)}, u32[]{:S(2)}) collective-permute-start(f32[2,64,1280]{2,1,0:T(8,128)S(1)} %get-tuple-element.78), channel_id=1, source_target_pairs={{0,16},{8,24},{16,0},{24,8},{1,17},{9,25},{17,1},{25,9},{2,18},{10... | collective-permute-start | bytes 1966088 | tf_op jit(solution)/shard_map/ppermute | solution.py:430
  19.7 1.6 %collective-permute-start.4 = (f32[520,128]{1,0:T(8,128)S(1)}, f32[520,128]{1,0:T(8,128)S(1)}, u32[]{:S(2)}, u32[]{:S(2)}) collective-permute-start(f32[520,128]{1,0:T(8,128)S(1)} %get-tuple-element.69), channel_id=1, source_target_pairs={{0,2},{1,3},{2,4},{3,5},{4,6},{5,7},{6,0},{7,1},{8,10},{9,11},{10,... | collective-permute-start | bytes 798728 | tf_op jit(solution)/shard_map/ppermute | solution.py:473
  21.3 2.6 %collective-permute-start.5 = (f32[520,128]{1,0:T(8,128)S(1)}, f32[520,128]{1,0:T(8,128)S(1)}, u32[]{:S(2)}, u32[]{:S(2)}) collective-permute-start(f32[520,128]{1,0:T(8,128)S(1)} %get-tuple-element.70), channel_id=1, source_target_pairs={{0,4},{1,5},{2,6},{3,7},{4,0},{5,1},{6,2},{7,3},{8,12},{9,13},{10,... | collective-permute-start | bytes 798728 | tf_op jit(solution)/shard_map/ppermute | solution.py:473
  23.9 1.3 %collective-permute-start.6 = (f32[520,128]{1,0:T(8,128)S(1)}, f32[520,128]{1,0:T(8,128)S(1)}, u32[]{:S(2)}, u32[]{:S(2)}) collective-permute-start(f32[520,128]{1,0:T(8,128)S(1)} %get-tuple-element.71), channel_id=1, source_target_pairs={{0,6},{1,7},{2,0},{3,1},{4,2},{5,3},{6,4},{7,5},{8,14},{9,15},{10,... | collective-permute-start | bytes 798728 | tf_op jit(solution)/shard_map/ppermute | solution.py:473
  25.3 8.0 %collective-permute-done.2.from_x_ref = f32[2,64,1280]{2,1,0:T(8,128)S(1)} collective-permute-done((f32[2,64,1280]{2,1,0:T(8,128)S(1)}, f32[2,64,1280]{2,1,0:T(8,128)S(1)}, u32[]{:S(2)}, u32[]{:S(2)}) %collective-permute-start.2) | collective-permute-done | bytes 655392 | tf_op jit(solution)/shard_map/ppermute | solution.py:430
  33.3 1.5 %collective-permute-done.3.from_y_ref = f32[2,64,1280]{2,1,0:T(8,128)S(1)} collective-permute-done((f32[2,64,1280]{2,1,0:T(8,128)S(1)}, f32[2,64,1280]{2,1,0:T(8,128)S(1)}, u32[]{:S(2)}, u32[]{:S(2)}) %collective-permute-start.3) | collective-permute-done | bytes 655392 | tf_op jit(solution)/shard_map/ppermute | solution.py:430
  34.7 0.1 second_sums.1
  34.9 1.6 %collective-permute-start.7 = (f32[64,1280]{1,0:T(8,128)S(1)}, f32[64,1280]{1,0:T(8,128)S(1)}, u32[]{:S(2)}, u32[]{:S(2)}) collective-permute-start(f32[64,1280]{1,0:T(8,128)S(1)} %get-tuple-element.80), channel_id=1, source_target_pairs={{0,16},{8,24},{16,0},{24,8},{1,17},{9,25},{17,1},{25,9},{2,18},{10... | collective-permute-start | bytes 983048 | tf_op jit(solution)/shard_map/ppermute | solution.py:430
  36.4 0.5 collective-permute-start.8
  37.0 0.0 collective-permute-done.4.refs_1_
  37.0 4.0 %collective-permute-done.5.refs_2_ = f32[520,128]{1,0:T(8,128)S(1)} collective-permute-done((f32[520,128]{1,0:T(8,128)S(1)}, f32[520,128]{1,0:T(8,128)S(1)}, u32[]{:S(2)}, u32[]{:S(2)}) %collective-permute-start.5) | collective-permute-done | bytes 266272 | tf_op jit(solution)/shard_map/ppermute | solution.py:473
  41.0 0.0 collective-permute-done.6.refs_3_
  41.0 0.1 by_part.1
  41.1 2.4 %collective-permute-done.7 = f32[64,1280]{1,0:T(8,128)S(1)} collective-permute-done((f32[64,1280]{1,0:T(8,128)S(1)}, f32[64,1280]{1,0:T(8,128)S(1)}, u32[]{:S(2)}, u32[]{:S(2)}) %collective-permute-start.7) | collective-permute-done | bytes 327712 | tf_op jit(solution)/shard_map/ppermute | solution.py:430
  43.5 1.2 %collective-permute-done.8 = f32[64,1280]{1,0:T(8,128)S(1)} collective-permute-done((f32[64,1280]{1,0:T(8,128)S(1)}, f32[64,1280]{1,0:T(8,128)S(1)}, u32[]{:S(2)}, u32[]{:S(2)}) %collective-permute-start.8) | collective-permute-done | bytes 327712 | tf_op jit(solution)/shard_map/ppermute | solution.py:430
  44.8 0.1 chip_sums.3
  44.9 2.6 %collective-permute-start.9 = (f32[2,16,1280]{2,1,0:T(8,128)S(1)}, f32[2,16,1280]{2,1,0:T(8,128)S(1)}, u32[]{:S(2)}, u32[]{:S(2)}) collective-permute-start(f32[2,16,1280]{2,1,0:T(8,128)S(1)} %get-tuple-element.90), channel_id=1, source_target_pairs={{0,2},{1,3},{2,0},{3,1},{4,6},{5,7},{6,4},{7,5},{8,10},{9,11},{10,... | collective-permute-start | bytes 491528 | tf_op jit(solution)/shard_map/ppermute | solution.py:490
  47.5 0.1 collective-permute-start.11
  47.6 0.5 collective-permute-start.16
  48.1 0.5 collective-permute-start.17
  48.6 2.5 %collective-permute-start.18 = (f32[520,128]{1,0:T(8,128)S(1)}, f32[520,128]{1,0:T(8,128)S(1)}, u32[]{:S(2)}, u32[]{:S(2)}) collective-permute-start(f32[520,128]{1,0:T(8,128)S(1)} %get-tuple-element.86), channel_id=1, source_target_pairs={{0,24},{8,16},{16,8},{24,0},{1,25},{9,17},{17,9},{25,1},{2,26},{10... | collective-permute-start | bytes 798728 | tf_op jit(solution)/shard_map/ppermute | solution.py:430
  51.0 1.4 %collective-permute-done.9.recv_in = f32[2,16,1280]{2,1,0:T(8,128)S(1)} collective-permute-done((f32[2,16,1280]{2,1,0:T(8,128)S(1)}, f32[2,16,1280]{2,1,0:T(8,128)S(1)}, u32[]{:S(2)}, u32[]{:S(2)}) %collective-permute-start.9) | collective-permute-done | bytes 163872 | tf_op jit(solution)/shard_map/ppermute | solution.py:490
  52.5 1.9 %collective-permute-start.10 = (f32[1,16,1280]{2,1,0:T(8,128)S(1)}, f32[1,16,1280]{2,1,0:T(8,128)S(1)}, u32[]{:S(2)}, u32[]{:S(2)}) collective-permute-start(f32[1,16,1280]{2,1,0:T(8,128)S(1)} %get-tuple-element.92), channel_id=1, source_target_pairs={{0,4},{1,5},{2,6},{3,7},{4,0},{5,1},{6,2},{7,3},{8,12},{9,13},{10,... | collective-permute-start | bytes 245768 | tf_op jit(solution)/shard_map/ppermute | solution.py:490
  54.4 1.8 %collective-permute-done.11.recv_in = f32[2,16,1280]{2,1,0:T(8,128)S(1)} collective-permute-done((f32[2,16,1280]{2,1,0:T(8,128)S(1)}, f32[2,16,1280]{2,1,0:T(8,128)S(1)}, u32[]{:S(2)}, u32[]{:S(2)}) %collective-permute-start.11) | collective-permute-done | bytes 163872 | tf_op jit(solution)/shard_map/ppermute | solution.py:490
  56.3 0.1 collective-permute-start.12
  56.3 1.6 %collective-permute-done.10.recv_a_ref = f32[1,16,1280]{2,1,0:T(8,128)S(1)} collective-permute-done((f32[1,16,1280]{2,1,0:T(8,128)S(1)}, f32[1,16,1280]{2,1,0:T(8,128)S(1)}, u32[]{:S(2)}, u32[]{:S(2)}) %collective-permute-start.10) | collective-permute-done | bytes 81952 | tf_op jit(solution)/shard_map/ppermute | solution.py:490
  57.9 4.0 %collective-permute-done.12.recv_b_ref = f32[1,16,1280]{2,1,0:T(8,128)S(1)} collective-permute-done((f32[1,16,1280]{2,1,0:T(8,128)S(1)}, f32[1,16,1280]{2,1,0:T(8,128)S(1)}, u32[]{:S(2)}, u32[]{:S(2)}) %collective-permute-start.12) | collective-permute-done | bytes 81952 | tf_op jit(solution)/shard_map/ppermute | solution.py:490
  62.0 0.0 copy-start
  62.0 0.0 copy-start.3
  62.0 0.0 collective-permute-done.16.refs_1_
  62.0 0.0 collective-permute-done.17.refs_2_
  62.0 0.0 collective-permute-done.18.refs_3_
  62.0 0.1 by_core.1
  62.1 0.1 collective-permute-start.19
  62.2 1.0 %collective-permute-start.15 = (f32[16,2560]{1,0:T(8,128)S(1)}, f32[16,2560]{1,0:T(8,128)S(1)}, u32[]{:S(2)}, u32[]{:S(2)}) collective-permute-start(f32[16,2560]{1,0:T(8,128)S(1)} %total.1.refs_0_), channel_id=1, source_target_pairs={{0,24},{8,16},{16,8},{24,0},{1,25},{9,17},{17,9},{25,1},{2,26},{10... | collective-permute-start | bytes 491528 | tf_op jit(solution)/shard_map/ppermute | solution.py:430
  63.2 1.5 %collective-permute-start.14 = (f32[16,2560]{1,0:T(8,128)S(1)}, f32[16,2560]{1,0:T(8,128)S(1)}, u32[]{:S(2)}, u32[]{:S(2)}) collective-permute-start(f32[16,2560]{1,0:T(8,128)S(1)} %total.1.refs_0_), channel_id=1, source_target_pairs={{0,16},{8,24},{16,0},{24,8},{1,17},{9,25},{17,1},{25,9},{2,18},{10... | collective-permute-start | bytes 491528 | tf_op jit(solution)/shard_map/ppermute | solution.py:430
  64.7 1.0 %collective-permute-start.13 = (f32[16,2560]{1,0:T(8,128)S(1)}, f32[16,2560]{1,0:T(8,128)S(1)}, u32[]{:S(2)}, u32[]{:S(2)}) collective-permute-start(f32[16,2560]{1,0:T(8,128)S(1)} %total.1.refs_0_), channel_id=1, source_target_pairs={{0,8},{8,0},{16,24},{24,16},{1,9},{9,1},{17,25},{25,17},{2,10},{10... | collective-permute-start | bytes 491528 | tf_op jit(solution)/shard_map/ppermute | solution.py:430
  65.8 0.0 collective-permute-done.19.recv_ref
  65.8 0.0 copy-done
  65.8 0.0 copy-done.3
  65.8 2.5 %table_part.1 = (f32[512,512]{1,0:T(8,128)}, f32[512]{0:T(512)}) custom-call(f32[1056,128]{1,0:T(8,128)S(1)} %get-tuple-element.99.keep_ref, f32[1056,128]{1,0:T(8,128)S(1)} %collective-permute-done.19.recv_ref, f32[512,512]{1,0:T(8,128)S(1)} %copy-done, f32[512]{0:T(512)S(1)} %copy-done.3), custom_call_target="tpu_custom_call" | custom-call | flops 1000000000 | bytes 65536 | tf_op jit(solution)/shard_map/table_part/pallas_call | solution.py:411
  68.3 1.9 %collective-permute-done.15.refs_3_ = f32[16,2560]{1,0:T(8,128)S(1)} collective-permute-done((f32[16,2560]{1,0:T(8,128)S(1)}, f32[16,2560]{1,0:T(8,128)S(1)}, u32[]{:S(2)}, u32[]{:S(2)}) %collective-permute-start.15) | collective-permute-done | bytes 163872 | tf_op jit(solution)/shard_map/ppermute | solution.py:430
  70.2 2.8 %collective-permute-done.14.refs_2_ = f32[16,2560]{1,0:T(8,128)S(1)} collective-permute-done((f32[16,2560]{1,0:T(8,128)S(1)}, f32[16,2560]{1,0:T(8,128)S(1)}, u32[]{:S(2)}, u32[]{:S(2)}) %collective-permute-start.14) | collective-permute-done | bytes 163872 | tf_op jit(solution)/shard_map/ppermute | solution.py:430
  73.0 0.0 collective-permute-done.13.refs_1_
  73.0 0.9 %gather.1 = (f32[4,16,2048]{2,1,0:T(8,128)}, f32[4,16,512]{2,1,0:T(8,128)}) custom-call(f32[16,2560]{1,0:T(8,128)S(1)} %total.1.refs_0_, f32[16,2560]{1,0:T(8,128)S(1)} %collective-permute-done.13.refs_1_, f32[16,2560]{1,0:T(8,128)S(1)} %collective-permute-done.14.refs_2_, f32[16,2560]{1,0:T(8,128)S(1)} %collective-permute-done.15.refs_3_), custom_call_target="tpu_custom_call" | custom-call | flops 1000000000 | bytes 65536 | tf_op jit(solution)/shard_map/gather/pallas_call | solution.py:411
  (3 shorter events, 0.1 us)
Async XLA Ops:
  9.1 3.6 %collective-permute-start = (f32[256,1536]{1,0:T(8,128)S(1)}, f32[256,1536]{1,0:T(8,128)S(1)}, u32[]{:S(2)}, u32[]{:S(2)}) collective-permute-start(f32[256,1536]{1,0:T(8,128)S(1)} %get-tuple-element.60), channel_id=1, source_target_pairs={{0,1},{1,0},{2,3},{3,2},{4,5},{5,4},{6,7},{7,6},{8,9},{9,8},{10,11... | collective-permute-start | bytes 4718600 | tf_op jit(solution)/shard_map/ppermute | solution.py:459
  9.6 3.0 %copy-start.1 = (s32[1,32,16]{1,2,0:T(8,128)S(1)}, s32[1,32,16]{1,2,0:T(8,128)}, u32[]{:S(2)}) copy-start(s32[1,32,16]{1,2,0:T(8,128)} %param.14) | copy-start | bytes 6148
  9.6 3.0 %copy-start.2 = (s32[1,512]{1,0:T(1,128)S(1)}, s32[1,512]{1,0:T(1,128)}, u32[]{:S(2)}) copy-start(s32[1,512]{1,0:T(1,128)} %slot_ref.1) | copy-start | bytes 6148
  12.3 2.7 %collective-permute-start.1 = (f32[256,1024]{1,0:T(8,128)S(1)}, f32[256,1024]{1,0:T(8,128)S(1)}, u32[]{:S(2)}, u32[]{:S(2)}) collective-permute-start(f32[256,1024]{1,0:T(8,128)S(1)} %get-tuple-element.74), channel_id=1, source_target_pairs={{0,1},{1,0},{2,3},{3,2},{4,5},{5,4},{6,7},{7,6},{8,9},{9,8},{10,11... | collective-permute-start | bytes 3145736 | tf_op jit(solution)/shard_map/ppermute | solution.py:464
  15.3 18.0 %collective-permute-start.2 = (f32[2,64,1280]{2,1,0:T(8,128)S(1)}, f32[2,64,1280]{2,1,0:T(8,128)S(1)}, u32[]{:S(2)}, u32[]{:S(2)}) collective-permute-start(f32[2,64,1280]{2,1,0:T(8,128)S(1)} %get-tuple-element.76), channel_id=1, source_target_pairs={{0,8},{8,0},{16,24},{24,16},{1,9},{9,1},{17,25},{25,17},{2,10},{10... | collective-permute-start | bytes 1966088 | tf_op jit(solution)/shard_map/ppermute | solution.py:430
  18.2 16.5 %collective-permute-start.3 = (f32[2,64,1280]{2,1,0:T(8,128)S(1)}, f32[2,64,1280]{2,1,0:T(8,128)S(1)}, u32[]{:S(2)}, u32[]{:S(2)}) collective-permute-start(f32[2,64,1280]{2,1,0:T(8,128)S(1)} %get-tuple-element.78), channel_id=1, source_target_pairs={{0,16},{8,24},{16,0},{24,8},{1,17},{9,25},{17,1},{25,9},{2,18},{10... | collective-permute-start | bytes 1966088 | tf_op jit(solution)/shard_map/ppermute | solution.py:430
  19.7 17.2 %collective-permute-start.4 = (f32[520,128]{1,0:T(8,128)S(1)}, f32[520,128]{1,0:T(8,128)S(1)}, u32[]{:S(2)}, u32[]{:S(2)}) collective-permute-start(f32[520,128]{1,0:T(8,128)S(1)} %get-tuple-element.69), channel_id=1, source_target_pairs={{0,2},{1,3},{2,4},{3,5},{4,6},{5,7},{6,0},{7,1},{8,10},{9,11},{10,... | collective-permute-start | bytes 798728 | tf_op jit(solution)/shard_map/ppermute | solution.py:473
  21.3 19.7 %collective-permute-start.5 = (f32[520,128]{1,0:T(8,128)S(1)}, f32[520,128]{1,0:T(8,128)S(1)}, u32[]{:S(2)}, u32[]{:S(2)}) collective-permute-start(f32[520,128]{1,0:T(8,128)S(1)} %get-tuple-element.70), channel_id=1, source_target_pairs={{0,4},{1,5},{2,6},{3,7},{4,0},{5,1},{6,2},{7,3},{8,12},{9,13},{10,... | collective-permute-start | bytes 798728 | tf_op jit(solution)/shard_map/ppermute | solution.py:473
  23.9 17.1 %collective-permute-start.6 = (f32[520,128]{1,0:T(8,128)S(1)}, f32[520,128]{1,0:T(8,128)S(1)}, u32[]{:S(2)}, u32[]{:S(2)}) collective-permute-start(f32[520,128]{1,0:T(8,128)S(1)} %get-tuple-element.71), channel_id=1, source_target_pairs={{0,6},{1,7},{2,0},{3,1},{4,2},{5,3},{6,4},{7,5},{8,14},{9,15},{10,... | collective-permute-start | bytes 798728 | tf_op jit(solution)/shard_map/ppermute | solution.py:473
  34.9 8.7 %collective-permute-start.7 = (f32[64,1280]{1,0:T(8,128)S(1)}, f32[64,1280]{1,0:T(8,128)S(1)}, u32[]{:S(2)}, u32[]{:S(2)}) collective-permute-start(f32[64,1280]{1,0:T(8,128)S(1)} %get-tuple-element.80), channel_id=1, source_target_pairs={{0,16},{8,24},{16,0},{24,8},{1,17},{9,25},{17,1},{25,9},{2,18},{10... | collective-permute-start | bytes 983048 | tf_op jit(solution)/shard_map/ppermute | solution.py:430
  36.4 8.3 %collective-permute-start.8 = (f32[64,1280]{1,0:T(8,128)S(1)}, f32[64,1280]{1,0:T(8,128)S(1)}, u32[]{:S(2)}, u32[]{:S(2)}) collective-permute-start(f32[64,1280]{1,0:T(8,128)S(1)} %get-tuple-element.81), channel_id=1, source_target_pairs={{0,8},{8,0},{16,24},{24,16},{1,9},{9,1},{17,25},{25,17},{2,10},{10... | collective-permute-start | bytes 983048 | tf_op jit(solution)/shard_map/ppermute | solution.py:430
  44.9 7.6 %collective-permute-start.9 = (f32[2,16,1280]{2,1,0:T(8,128)S(1)}, f32[2,16,1280]{2,1,0:T(8,128)S(1)}, u32[]{:S(2)}, u32[]{:S(2)}) collective-permute-start(f32[2,16,1280]{2,1,0:T(8,128)S(1)} %get-tuple-element.90), channel_id=1, source_target_pairs={{0,2},{1,3},{2,0},{3,1},{4,6},{5,7},{6,4},{7,5},{8,10},{9,11},{10,... | collective-permute-start | bytes 491528 | tf_op jit(solution)/shard_map/ppermute | solution.py:490
  47.5 8.8 %collective-permute-start.11 = (f32[2,16,1280]{2,1,0:T(8,128)S(1)}, f32[2,16,1280]{2,1,0:T(8,128)S(1)}, u32[]{:S(2)}, u32[]{:S(2)}) collective-permute-start(f32[2,16,1280]{2,1,0:T(8,128)S(1)} %get-tuple-element.95), channel_id=1, source_target_pairs={{0,2},{1,3},{2,0},{3,1},{4,6},{5,7},{6,4},{7,5},{8,10},{9,11},{10,... | collective-permute-start | bytes 491528 | tf_op jit(solution)/shard_map/ppermute | solution.py:490
  47.6 14.4 %collective-permute-start.16 = (f32[520,128]{1,0:T(8,128)S(1)}, f32[520,128]{1,0:T(8,128)S(1)}, u32[]{:S(2)}, u32[]{:S(2)}) collective-permute-start(f32[520,128]{1,0:T(8,128)S(1)} %get-tuple-element.84), channel_id=1, source_target_pairs={{0,8},{8,0},{16,24},{24,16},{1,9},{9,1},{17,25},{25,17},{2,10},{10... | collective-permute-start | bytes 798728 | tf_op jit(solution)/shard_map/ppermute | solution.py:430
  48.1 13.9 %collective-permute-start.17 = (f32[520,128]{1,0:T(8,128)S(1)}, f32[520,128]{1,0:T(8,128)S(1)}, u32[]{:S(2)}, u32[]{:S(2)}) collective-permute-start(f32[520,128]{1,0:T(8,128)S(1)} %get-tuple-element.85), channel_id=1, source_target_pairs={{0,16},{8,24},{16,0},{24,8},{1,17},{9,25},{17,1},{25,9},{2,18},{10... | collective-permute-start | bytes 798728 | tf_op jit(solution)/shard_map/ppermute | solution.py:430
  48.6 13.4 %collective-permute-start.18 = (f32[520,128]{1,0:T(8,128)S(1)}, f32[520,128]{1,0:T(8,128)S(1)}, u32[]{:S(2)}, u32[]{:S(2)}) collective-permute-start(f32[520,128]{1,0:T(8,128)S(1)} %get-tuple-element.86), channel_id=1, source_target_pairs={{0,24},{8,16},{16,8},{24,0},{1,25},{9,17},{17,9},{25,1},{2,26},{10... | collective-permute-start | bytes 798728 | tf_op jit(solution)/shard_map/ppermute | solution.py:430
  52.5 5.4 %collective-permute-start.10 = (f32[1,16,1280]{2,1,0:T(8,128)S(1)}, f32[1,16,1280]{2,1,0:T(8,128)S(1)}, u32[]{:S(2)}, u32[]{:S(2)}) collective-permute-start(f32[1,16,1280]{2,1,0:T(8,128)S(1)} %get-tuple-element.92), channel_id=1, source_target_pairs={{0,4},{1,5},{2,6},{3,7},{4,0},{5,1},{6,2},{7,3},{8,12},{9,13},{10,... | collective-permute-start | bytes 245768 | tf_op jit(solution)/shard_map/ppermute | solution.py:490
  56.3 5.7 %collective-permute-start.12 = (f32[1,16,1280]{2,1,0:T(8,128)S(1)}, f32[1,16,1280]{2,1,0:T(8,128)S(1)}, u32[]{:S(2)}, u32[]{:S(2)}) collective-permute-start(f32[1,16,1280]{2,1,0:T(8,128)S(1)} %get-tuple-element.97), channel_id=1, source_target_pairs={{0,4},{1,5},{2,6},{3,7},{4,0},{5,1},{6,2},{7,3},{8,12},{9,13},{10,... | collective-permute-start | bytes 245768 | tf_op jit(solution)/shard_map/ppermute | solution.py:490
  62.0 3.8 %copy-start = (f32[512,512]{1,0:T(8,128)S(1)}, f32[512,512]{1,0:T(8,128)}, u32[]{:S(2)}) copy-start(f32[512,512]{1,0:T(8,128)} %table_ref.1) | copy-start | bytes 3145732
  62.0 3.8 %copy-start.3 = (f32[512]{0:T(512)S(1)}, f32[512]{0:T(512)}, u32[]{:S(2)}) copy-start(f32[512]{0:T(512)} %accum_ref.1) | copy-start | bytes 6148
  62.1 3.6 %collective-permute-start.19 = (f32[1056,128]{1,0:T(8,128)S(1)}, f32[1056,128]{1,0:T(8,128)S(1)}, u32[]{:S(2)}, u32[]{:S(2)}) collective-permute-start(f32[1056,128]{1,0:T(8,128)S(1)} %get-tuple-element.100), channel_id=1, source_target_pairs={{0,1},{1,0},{2,3},{3,2},{4,5},{5,4},{6,7},{7,6},{8,9},{9,8},{10,11... | collective-permute-start | bytes 1622024 | tf_op jit(solution)/shard_map/ppermute | solution.py:511
  62.2 8.0 %collective-permute-start.15 = (f32[16,2560]{1,0:T(8,128)S(1)}, f32[16,2560]{1,0:T(8,128)S(1)}, u32[]{:S(2)}, u32[]{:S(2)}) collective-permute-start(f32[16,2560]{1,0:T(8,128)S(1)} %total.1.refs_0_), channel_id=1, source_target_pairs={{0,24},{8,16},{16,8},{24,0},{1,25},{9,17},{17,9},{25,1},{2,26},{10... | collective-permute-start | bytes 491528 | tf_op jit(solution)/shard_map/ppermute | solution.py:430
  63.2 9.8 %collective-permute-start.14 = (f32[16,2560]{1,0:T(8,128)S(1)}, f32[16,2560]{1,0:T(8,128)S(1)}, u32[]{:S(2)}, u32[]{:S(2)}) collective-permute-start(f32[16,2560]{1,0:T(8,128)S(1)} %total.1.refs_0_), channel_id=1, source_target_pairs={{0,16},{8,24},{16,0},{24,8},{1,17},{9,25},{17,1},{25,9},{2,18},{10... | collective-permute-start | bytes 491528 | tf_op jit(solution)/shard_map/ppermute | solution.py:430
  64.7 8.3 %collective-permute-start.13 = (f32[16,2560]{1,0:T(8,128)S(1)}, f32[16,2560]{1,0:T(8,128)S(1)}, u32[]{:S(2)}, u32[]{:S(2)}) collective-permute-start(f32[16,2560]{1,0:T(8,128)S(1)} %total.1.refs_0_), channel_id=1, source_target_pairs={{0,8},{8,0},{16,24},{24,16},{1,9},{9,1},{17,25},{25,17},{2,10},{10... | collective-permute-start | bytes 491528 | tf_op jit(solution)/shard_map/ppermute | solution.py:430

commit v16 on v15

--- a/solution.py
+++ b/solution.py
@@ -71,33 +71,36 @@
 def forward_kernel(rows_size, dp_size, len_ref, ev_hbm, cot_hbm, win_hbm, wout_hbm,
                    keep_ref, send_ref, hid_ref, dsilu_ref, gatt_ref, gpre_ref, normed_t_ref,
                    ev_ref, masked_ref, win_ref, inv_ref, normed_ref, user_ref, duser_ref, att_ref, mixed_ref, dval_ref,
-                   weights_ref, wout_ref, order_ref, grad_mixed_ref, cot_ref, pre_ref, raw_ref, arrived):
+                   weights_ref, wout_ref, order_ref, grad_mixed_ref, cot_ref, pre_ref, raw_ref, mixed_t_ref, arrived):
     tokens, width = ev_ref.shape
-    copies = [pltpu.make_async_copy(ev_hbm, ev_ref, arrived.at[0])]
+    parts = [pl.ds(i * STEP, STEP) for i in range(tokens // STEP)]
+    early = [pltpu.make_async_copy(ev_hbm.at[part, :], ev_ref.at[part, :], arrived.at[7 + i]) for i, part in enumerate(parts)]
+    copies = [None]
     for c in range(4):
         cols = pl.ds(c * width, width)
         copies.append(pltpu.make_async_copy(win_hbm.at[:, cols], win_ref.at[:, cols], arrived.at[1 + c]))
     copies.append(pltpu.make_async_copy(cot_hbm, cot_ref, arrived.at[5]))
     copies.append(pltpu.make_async_copy(wout_hbm, wout_ref, arrived.at[6]))
-    for copy in copies:
+    for copy in early + copies[1:]:
         copy.start()
     order_ref[...] = owner_order(width, rows_size, dp_size)
     hd = width // HEADS
     scale = hd ** -0.5
     steps = tokens // STEP
 
-    copies[0].wait()
-    for tile in tiles_of(0, tokens, TILE):
-        xhat, _ = standardize(ev_ref[tile, :].astype(f32))
-        normed_ref[tile, :] = xhat.astype(bf16)
+    for i in range(steps):
+        early[i].wait()
+        for tile in tiles_of(i * STEP, STEP, TILE // 2):
+            xhat, _ = standardize(ev_ref[tile, :].astype(f32))
+            normed_ref[tile, :] = xhat.astype(bf16)
 
     def project(i, c):
         rows = pl.ds(i * STEP, STEP)
         slot = (c * steps + i) % pre_ref.shape[0]
         pre_ref[slot] = dot_nn(normed_ref[rows, :], win_ref[:, c * width:(c + 1) * width])
-        for at in range(0, STEP, TILE):
-            tile = pl.ds(i * STEP + at, TILE)
-            pre = pre_ref[slot, at:at + TILE, :]
+        for at in range(0, STEP, TILE // 2):
+            tile = pl.ds(i * STEP + at, TILE // 2)
+            pre = pre_ref[slot, at:at + TILE // 2, :]
             sig = 0.5 + 0.5 * jnp.tanh(0.5 * pre)
             hid = pre * sig
             dsilu = sig * (1.0 + (pre - hid))
@@ -131,13 +134,13 @@
                 keys = pl.ds(j * STEP, STEP)
                 slot = (h * 3 + i + j) % raw_ref.shape[0]
                 raw_ref[slot] = dot_nt(hid_ref[rows, q_cols], hid_ref[keys, k_cols])
-                for at in range(0, STEP, 2 * TILE):
-                    half = raw_ref[slot, at:at + 2 * TILE, :] * (0.5 * scale)
+                for at in range(0, STEP, TILE):
+                    half = raw_ref[slot, at:at + TILE, :] * (0.5 * scale)
                     weights = (half + half * jnp.tanh(half)) * inv_len
                     if i == j:
                         row = at + lax.broadcasted_iota(jnp.int32, weights.shape, 0)
                         weights = jnp.where(row >= lax.broadcasted_iota(jnp.int32, weights.shape, 1), weights, 0.0)
-                    weights_ref[h, pl.ds(i * STEP + at, 2 * TILE), keys] = weights.astype(bf16)
+                    weights_ref[h, pl.ds(i * STEP + at, TILE), keys] = weights.astype(bf16)
             seen = pl.ds(0, (i + 1) * STEP)
             att_ref[rows, v_cols] = dot_nn(weights_ref[h, rows, seen], hid_ref[seen, v_cols])
         for i in range(h, steps, HEADS):
@@ -167,10 +170,10 @@
             grad_v = dot_tn(weights_ref[h, later, keys], gatt_ref[later, v_cols])
             gpre_ref[keys, width + h * hd:width + (h + 1) * hd] = (grad_v * dval_ref[keys, v_cols]).astype(bf16)
 
-    mixed_t = dot_nt(order_ref[...], mixed_ref[...]).astype(bf16)
     half = width // 2
     for ref, start in ((send_ref, half), (keep_ref, 0)):
-        ref[:, :width] = dot_nn(mixed_t[start:start + half], masked_ref[...])
+        mixed_t_ref[...] = dot_nt(order_ref[start:start + half, :], mixed_ref[...]).astype(bf16)
+        ref[:, :width] = dot_nn(mixed_t_ref[...], masked_ref[...])
         ref[:, width:] = dot_nn(normed_t_ref[start:start + half, :], gpre_ref[...])
 
 
@@ -415,7 +418,7 @@
         out_specs=[vmem()] * len(out_shape),
         out_shape=list(out_shape),
         scratch_shapes=[pltpu.VMEM(dims, dtype) for dims, dtype in scratch]
-        + [pltpu.SemaphoreType.DMA((7,))] * (far > 0),
+        + [pltpu.SemaphoreType.DMA((16,))] * (far > 0),
         compiler_params=pltpu.CompilerParams(vmem_limit_bytes=grant * MIB),
         cost_estimate=pl.CostEstimate(flops=100_000_000_000 if long else 1_000_000_000, bytes_accessed=1 << 16, transcendentals=0),
     )(*args)
@@ -455,7 +458,7 @@
         [((tokens, width), bf16), ((tokens, width), bf16), ((tokens, width), f32), ((tokens, width), f32),
          ((tokens, width), bf16), ((tokens, width), f32), ((HEADS, tokens, tokens), bf16),
          (w_out.shape, bf16), ((width, width), bf16), ((tokens, width), f32), ((tokens, width), bf16),
-         ((4, STEP, width), f32), ((4, STEP, STEP), f32)], far=5, long=True, grant=22)
+         ((4, STEP, width), f32), ((4, STEP, STEP), f32), ((width // 2, tokens), bf16)], far=5, long=True, grant=22)
     recv1 = lax.ppermute(send1, "rows", cores)
     keep2, send2, gpre_qk = call(
         attention_kernel, "attention_part", sides(2 * width) + [local(tokens, 2 * width, dtype=bf16)],

time: 74 us -> 74.3 us (level)
  no operation moved by 1% of the time
where the time goes in v16:
time: 74.3 us; the launch traced here: 74.1 us
  waiting for transfers between devices  31.1 us (42%)
  starting transfers between devices  24.5 us (33%)
  Pallas kernels  17.1 us (23%)
  between operations  1.41 us (2%)
    ppermute x10, waiting for transfers between devices, body(): lax.ppermute(v, 'dp', [(i, i ^ bit) for i in range(dp_size)])  17.8 us
    pallas_call x13, Pallas kernels, call(): pl.pallas_call(kernel, name=name, in_specs=[pl.BlockSpec(memory_space=p)...  17.1 us
    ppermute x10, starting transfers between devices, body(): lax.ppermute(v, 'dp', [(i, i ^ bit) for i in range(dp_size)])  13.6 us
    ppermute x4, waiting for transfers between devices, body(): lax.ppermute(v, 'rows', [(i, i ^ 2 << bit) for i in range(rows_size)])  8.86 us
    ppermute x3, starting transfers between devices, body(): lax.ppermute(v, 'rows', [(i, (i + 2 * k) % rows_size) for i in range(rows...  5.52 us
    ppermute x4, starting transfers between devices, body(): lax.ppermute(v, 'rows', [(i, i ^ 2 << bit) for i in range(rows_size)])  4.69 us
    ppermute x3, waiting for transfers between devices, body(): lax.ppermute(v, 'rows', [(i, (i + 2 * k) % rows_size) for i in range(rows...  4.06 us
  transfers between devices with their start and end apart: 20, of which 12 were waited for; matrix products, arithmetic and copies ran while one was open for 0% of the time, Pallas kernels for 10%

profile of v16, /device:TPU:0, one launch (start us, length us, event | category | flops | bytes accessed | tf_op | source)
XLA Modules:
  0.0 74.1 jit_solution(4650914878436939505)
XLA Ops:
  1.3 8.1 %forward_part.1 = (f32[256,1536]{1,0:T(8,128)S(1)}, f32[256,1536]{1,0:T(8,128)S(1)}, bf16[512,1536]{1,0:T(8,128)(2,1)S(1)}, bf16[512,1024]{1,0:T(8,128)(2,1)S(1)...) custom-call(s32[1]{0:T(128)S(6)} %copy.13.len_ref, ...), custom_call_target="tpu_custom_call" | custom-call | flops 99999997952 | bytes 65536 | tf_op jit(solution)/shard_map/forward_part/pallas_call | solution.py:414
  9.4 0.5 collective-permute-start
  9.9 0.0 copy-start.1
  9.9 0.0 copy-start.2
  9.9 2.6 %attention_part.1 = (f32[256,1024]{1,0:T(8,128)S(1)}, f32[256,1024]{1,0:T(8,128)S(1)}, bf16[512,1024]{1,0:T(8,128)(2,1)S(1)}) custom-call(f32[8,128]{1,0:T(8,128)S(1)} %get-tuple-element.62.inv_ref, bf16[512,1536]{1,0:T(8,128)(2,1)S(1)} %get-tuple-element.63.hid_ref, bf16[512,1024]{1,0:T(8,128)(2,1)S(1)} %get-tuple-element.64.dsilu_ref, ...), custom_call_target="tpu_custom_call" | custom-call | flops 99999997952 | bytes 65536 | tf_op jit(solution)/shard_map/attention_part/pallas_call | solution.py:414
  12.5 0.1 collective-permute-start.1
  12.6 0.3 collective-permute-done
  12.9 0.0 copy-done.1
  12.9 0.0 copy-done.2
  12.9 2.2 %events_part.1 = (f32[520,128]{1,0:T(8,128)S(1)}, f32[520,128]{1,0:T(8,128)S(1)}, f32[520,128]{1,0:T(8,128)S(1)}, f32[520,128]{1,0:T(8,128)S(1)}) custom-call(bf16[512,512]{1,0:T(8,128)(2,1)S(1)} %get-tuple-element.56.ev_ref, bf16[512,512]{1,0:T(8,128)(2,1)S(1)} %get-tuple-element.57.masked_ref, bf16[512,2048]{1,0:T(8,128)(2,1)S(1)} %get-tuple-element.58.win_ref, ...), custom_call_target="tpu_custom_call" | custom-call | flops 99999997952 | bytes 65536 | tf_op jit(solution)/shard_map/events_part/pallas_call | solution.py:414
  15.2 0.0 collective-permute-done.1
  15.2 0.3 first_sums.1
  15.5 2.9 %collective-permute-start.2 = (f32[2,64,1280]{2,1,0:T(8,128)S(1)}, f32[2,64,1280]{2,1,0:T(8,128)S(1)}, u32[]{:S(2)}, u32[]{:S(2)}) collective-permute-start(f32[2,64,1280]{2,1,0:T(8,128)S(1)} %get-tuple-element.76), channel_id=1, source_target_pairs={{0,8},{8,0},{16,24},{24,16},{1,9},{9,1},{17,25},{25,17},{2,10},{10... | collective-permute-start | bytes 1966088 | tf_op jit(solution)/shard_map/ppermute | solution.py:433
  18.5 1.5 %collective-permute-start.3 = (f32[2,64,1280]{2,1,0:T(8,128)S(1)}, f32[2,64,1280]{2,1,0:T(8,128)S(1)}, u32[]{:S(2)}, u32[]{:S(2)}) collective-permute-start(f32[2,64,1280]{2,1,0:T(8,128)S(1)} %get-tuple-element.78), channel_id=1, source_target_pairs={{0,16},{8,24},{16,0},{24,8},{1,17},{9,25},{17,1},{25,9},{2,18},{10... | collective-permute-start | bytes 1966088 | tf_op jit(solution)/shard_map/ppermute | solution.py:433
  20.0 1.6 %collective-permute-start.4 = (f32[520,128]{1,0:T(8,128)S(1)}, f32[520,128]{1,0:T(8,128)S(1)}, u32[]{:S(2)}, u32[]{:S(2)}) collective-permute-start(f32[520,128]{1,0:T(8,128)S(1)} %get-tuple-element.69), channel_id=1, source_target_pairs={{0,2},{1,3},{2,4},{3,5},{4,6},{5,7},{6,0},{7,1},{8,10},{9,11},{10,... | collective-permute-start | bytes 798728 | tf_op jit(solution)/shard_map/ppermute | solution.py:476
  21.6 2.6 %collective-permute-start.5 = (f32[520,128]{1,0:T(8,128)S(1)}, f32[520,128]{1,0:T(8,128)S(1)}, u32[]{:S(2)}, u32[]{:S(2)}) collective-permute-start(f32[520,128]{1,0:T(8,128)S(1)} %get-tuple-element.70), channel_id=1, source_target_pairs={{0,4},{1,5},{2,6},{3,7},{4,0},{5,1},{6,2},{7,3},{8,12},{9,13},{10,... | collective-permute-start | bytes 798728 | tf_op jit(solution)/shard_map/ppermute | solution.py:476
  24.2 1.3 %collective-permute-start.6 = (f32[520,128]{1,0:T(8,128)S(1)}, f32[520,128]{1,0:T(8,128)S(1)}, u32[]{:S(2)}, u32[]{:S(2)}) collective-permute-start(f32[520,128]{1,0:T(8,128)S(1)} %get-tuple-element.71), channel_id=1, source_target_pairs={{0,6},{1,7},{2,0},{3,1},{4,2},{5,3},{6,4},{7,5},{8,14},{9,15},{10,... | collective-permute-start | bytes 798728 | tf_op jit(solution)/shard_map/ppermute | solution.py:476
  25.5 8.0 %collective-permute-done.2.from_x_ref = f32[2,64,1280]{2,1,0:T(8,128)S(1)} collective-permute-done((f32[2,64,1280]{2,1,0:T(8,128)S(1)}, f32[2,64,1280]{2,1,0:T(8,128)S(1)}, u32[]{:S(2)}, u32[]{:S(2)}) %collective-permute-start.2) | collective-permute-done | bytes 655392 | tf_op jit(solution)/shard_map/ppermute | solution.py:433
  33.5 1.5 %collective-permute-done.3.from_y_ref = f32[2,64,1280]{2,1,0:T(8,128)S(1)} collective-permute-done((f32[2,64,1280]{2,1,0:T(8,128)S(1)}, f32[2,64,1280]{2,1,0:T(8,128)S(1)}, u32[]{:S(2)}, u32[]{:S(2)}) %collective-permute-start.3) | collective-permute-done | bytes 655392 | tf_op jit(solution)/shard_map/ppermute | solution.py:433
  35.0 0.1 second_sums.1
  35.1 1.6 %collective-permute-start.7 = (f32[64,1280]{1,0:T(8,128)S(1)}, f32[64,1280]{1,0:T(8,128)S(1)}, u32[]{:S(2)}, u32[]{:S(2)}) collective-permute-start(f32[64,1280]{1,0:T(8,128)S(1)} %get-tuple-element.80), channel_id=1, source_target_pairs={{0,16},{8,24},{16,0},{24,8},{1,17},{9,25},{17,1},{25,9},{2,18},{10... | collective-permute-start | bytes 983048 | tf_op jit(solution)/shard_map/ppermute | solution.py:433
  36.7 0.5 collective-permute-start.8
  37.2 0.0 collective-permute-done.4.refs_1_
  37.2 4.1 %collective-permute-done.5.refs_2_ = f32[520,128]{1,0:T(8,128)S(1)} collective-permute-done((f32[520,128]{1,0:T(8,128)S(1)}, f32[520,128]{1,0:T(8,128)S(1)}, u32[]{:S(2)}, u32[]{:S(2)}) %collective-permute-start.5) | collective-permute-done | bytes 266272 | tf_op jit(solution)/shard_map/ppermute | solution.py:476
  41.3 0.0 collective-permute-done.6.refs_3_
  41.3 0.1 by_part.1
  41.4 2.4 %collective-permute-done.7 = f32[64,1280]{1,0:T(8,128)S(1)} collective-permute-done((f32[64,1280]{1,0:T(8,128)S(1)}, f32[64,1280]{1,0:T(8,128)S(1)}, u32[]{:S(2)}, u32[]{:S(2)}) %collective-permute-start.7) | collective-permute-done | bytes 327712 | tf_op jit(solution)/shard_map/ppermute | solution.py:433
  43.8 1.2 %collective-permute-done.8 = f32[64,1280]{1,0:T(8,128)S(1)} collective-permute-done((f32[64,1280]{1,0:T(8,128)S(1)}, f32[64,1280]{1,0:T(8,128)S(1)}, u32[]{:S(2)}, u32[]{:S(2)}) %collective-permute-start.8) | collective-permute-done | bytes 327712 | tf_op jit(solution)/shard_map/ppermute | solution.py:433
  45.0 0.1 chip_sums.3
  45.1 2.6 %collective-permute-start.9 = (f32[2,16,1280]{2,1,0:T(8,128)S(1)}, f32[2,16,1280]{2,1,0:T(8,128)S(1)}, u32[]{:S(2)}, u32[]{:S(2)}) collective-permute-start(f32[2,16,1280]{2,1,0:T(8,128)S(1)} %get-tuple-element.90), channel_id=1, source_target_pairs={{0,2},{1,3},{2,0},{3,1},{4,6},{5,7},{6,4},{7,5},{8,10},{9,11},{10,... | collective-permute-start | bytes 491528 | tf_op jit(solution)/shard_map/ppermute | solution.py:493
  47.7 0.1 collective-permute-start.11
  47.8 0.5 collective-permute-start.16
  48.3 0.5 collective-permute-start.17
  48.8 2.4 %collective-permute-start.18 = (f32[520,128]{1,0:T(8,128)S(1)}, f32[520,128]{1,0:T(8,128)S(1)}, u32[]{:S(2)}, u32[]{:S(2)}) collective-permute-start(f32[520,128]{1,0:T(8,128)S(1)} %get-tuple-element.86), channel_id=1, source_target_pairs={{0,24},{8,16},{16,8},{24,0},{1,25},{9,17},{17,9},{25,1},{2,26},{10... | collective-permute-start | bytes 798728 | tf_op jit(solution)/shard_map/ppermute | solution.py:433
  51.3 1.4 %collective-permute-done.9.recv_in = f32[2,16,1280]{2,1,0:T(8,128)S(1)} collective-permute-done((f32[2,16,1280]{2,1,0:T(8,128)S(1)}, f32[2,16,1280]{2,1,0:T(8,128)S(1)}, u32[]{:S(2)}, u32[]{:S(2)}) %collective-permute-start.9) | collective-permute-done | bytes 163872 | tf_op jit(solution)/shard_map/ppermute | solution.py:493
  52.7 1.9 %collective-permute-start.10 = (f32[1,16,1280]{2,1,0:T(8,128)S(1)}, f32[1,16,1280]{2,1,0:T(8,128)S(1)}, u32[]{:S(2)}, u32[]{:S(2)}) collective-permute-start(f32[1,16,1280]{2,1,0:T(8,128)S(1)} %get-tuple-element.92), channel_id=1, source_target_pairs={{0,4},{1,5},{2,6},{3,7},{4,0},{5,1},{6,2},{7,3},{8,12},{9,13},{10,... | collective-permute-start | bytes 245768 | tf_op jit(solution)/shard_map/ppermute | solution.py:493
  54.7 1.8 %collective-permute-done.11.recv_in = f32[2,16,1280]{2,1,0:T(8,128)S(1)} collective-permute-done((f32[2,16,1280]{2,1,0:T(8,128)S(1)}, f32[2,16,1280]{2,1,0:T(8,128)S(1)}, u32[]{:S(2)}, u32[]{:S(2)}) %collective-permute-start.11) | collective-permute-done | bytes 163872 | tf_op jit(solution)/shard_map/ppermute | solution.py:493
  56.5 0.1 collective-permute-start.12
  56.6 1.6 %collective-permute-done.10.recv_a_ref = f32[1,16,1280]{2,1,0:T(8,128)S(1)} collective-permute-done((f32[1,16,1280]{2,1,0:T(8,128)S(1)}, f32[1,16,1280]{2,1,0:T(8,128)S(1)}, u32[]{:S(2)}, u32[]{:S(2)}) %collective-permute-start.10) | collective-permute-done | bytes 81952 | tf_op jit(solution)/shard_map/ppermute | solution.py:493
  58.1 4.0 %collective-permute-done.12.recv_b_ref = f32[1,16,1280]{2,1,0:T(8,128)S(1)} collective-permute-done((f32[1,16,1280]{2,1,0:T(8,128)S(1)}, f32[1,16,1280]{2,1,0:T(8,128)S(1)}, u32[]{:S(2)}, u32[]{:S(2)}) %collective-permute-start.12) | collective-permute-done | bytes 81952 | tf_op jit(solution)/shard_map/ppermute | solution.py:493
  62.2 0.0 copy-start
  62.2 0.0 copy-start.3
  62.2 0.0 collective-permute-done.16.refs_1_
  62.2 0.0 collective-permute-done.17.refs_2_
  62.3 0.0 collective-permute-done.18.refs_3_
  62.3 0.1 by_core.1
  62.4 0.1 collective-permute-start.19
  62.4 1.0 %collective-permute-start.15 = (f32[16,2560]{1,0:T(8,128)S(1)}, f32[16,2560]{1,0:T(8,128)S(1)}, u32[]{:S(2)}, u32[]{:S(2)}) collective-permute-start(f32[16,2560]{1,0:T(8,128)S(1)} %total.1.refs_0_), channel_id=1, source_target_pairs={{0,24},{8,16},{16,8},{24,0},{1,25},{9,17},{17,9},{25,1},{2,26},{10... | collective-permute-start | bytes 491528 | tf_op jit(solution)/shard_map/ppermute | solution.py:433
  63.4 1.5 %collective-permute-start.14 = (f32[16,2560]{1,0:T(8,128)S(1)}, f32[16,2560]{1,0:T(8,128)S(1)}, u32[]{:S(2)}, u32[]{:S(2)}) collective-permute-start(f32[16,2560]{1,0:T(8,128)S(1)} %total.1.refs_0_), channel_id=1, source_target_pairs={{0,16},{8,24},{16,0},{24,8},{1,17},{9,25},{17,1},{25,9},{2,18},{10... | collective-permute-start | bytes 491528 | tf_op jit(solution)/shard_map/ppermute | solution.py:433
  65.0 1.0 %collective-permute-start.13 = (f32[16,2560]{1,0:T(8,128)S(1)}, f32[16,2560]{1,0:T(8,128)S(1)}, u32[]{:S(2)}, u32[]{:S(2)}) collective-permute-start(f32[16,2560]{1,0:T(8,128)S(1)} %total.1.refs_0_), channel_id=1, source_target_pairs={{0,8},{8,0},{16,24},{24,16},{1,9},{9,1},{17,25},{25,17},{2,10},{10... | collective-permute-start | bytes 491528 | tf_op jit(solution)/shard_map/ppermute | solution.py:433
  66.0 0.0 collective-permute-done.19.recv_ref
  66.0 0.0 copy-done
  66.0 0.0 copy-done.3
  66.0 2.5 %table_part.1 = (f32[512,512]{1,0:T(8,128)}, f32[512]{0:T(512)}) custom-call(f32[1056,128]{1,0:T(8,128)S(1)} %get-tuple-element.99.keep_ref, f32[1056,128]{1,0:T(8,128)S(1)} %collective-permute-done.19.recv_ref, f32[512,512]{1,0:T(8,128)S(1)} %copy-done, f32[512]{0:T(512)S(1)} %copy-done.3), custom_call_target="tpu_custom_call" | custom-call | flops 1000000000 | bytes 65536 | tf_op jit(solution)/shard_map/table_part/pallas_call | solution.py:414
  68.5 1.9 %collective-permute-done.15.refs_3_ = f32[16,2560]{1,0:T(8,128)S(1)} collective-permute-done((f32[16,2560]{1,0:T(8,128)S(1)}, f32[16,2560]{1,0:T(8,128)S(1)}, u32[]{:S(2)}, u32[]{:S(2)}) %collective-permute-start.15) | collective-permute-done | bytes 163872 | tf_op jit(solution)/shard_map/ppermute | solution.py:433
  70.4 2.8 %collective-permute-done.14.refs_2_ = f32[16,2560]{1,0:T(8,128)S(1)} collective-permute-done((f32[16,2560]{1,0:T(8,128)S(1)}, f32[16,2560]{1,0:T(8,128)S(1)}, u32[]{:S(2)}, u32[]{:S(2)}) %collective-permute-start.14) | collective-permute-done | bytes 163872 | tf_op jit(solution)/shard_map/ppermute | solution.py:433
  73.2 0.0 collective-permute-done.13.refs_1_
  73.2 0.9 %gather.1 = (f32[4,16,2048]{2,1,0:T(8,128)}, f32[4,16,512]{2,1,0:T(8,128)}) custom-call(f32[16,2560]{1,0:T(8,128)S(1)} %total.1.refs_0_, f32[16,2560]{1,0:T(8,128)S(1)} %collective-permute-done.13.refs_1_, f32[16,2560]{1,0:T(8,128)S(1)} %collective-permute-done.14.refs_2_, f32[16,2560]{1,0:T(8,128)S(1)} %collective-permute-done.15.refs_3_), custom_call_target="tpu_custom_call" | custom-call | flops 1000000000 | bytes 65536 | tf_op jit(solution)/shard_map/gather/pallas_call | solution.py:414
  (3 shorter events, 0.1 us)
Async XLA Ops:
  9.4 3.6 %collective-permute-start = (f32[256,1536]{1,0:T(8,128)S(1)}, f32[256,1536]{1,0:T(8,128)S(1)}, u32[]{:S(2)}, u32[]{:S(2)}) collective-permute-start(f32[256,1536]{1,0:T(8,128)S(1)} %get-tuple-element.60), channel_id=1, source_target_pairs={{0,1},{1,0},{2,3},{3,2},{4,5},{5,4},{6,7},{7,6},{8,9},{9,8},{10,11... | collective-permute-start | bytes 4718600 | tf_op jit(solution)/shard_map/ppermute | solution.py:462
  9.9 3.0 %copy-start.1 = (s32[1,32,16]{1,2,0:T(8,128)S(1)}, s32[1,32,16]{1,2,0:T(8,128)}, u32[]{:S(2)}) copy-start(s32[1,32,16]{1,2,0:T(8,128)} %param.14) | copy-start | bytes 6148
  9.9 3.0 %copy-start.2 = (s32[1,512]{1,0:T(1,128)S(1)}, s32[1,512]{1,0:T(1,128)}, u32[]{:S(2)}) copy-start(s32[1,512]{1,0:T(1,128)} %slot_ref.1) | copy-start | bytes 6148
  12.5 2.7 %collective-permute-start.1 = (f32[256,1024]{1,0:T(8,128)S(1)}, f32[256,1024]{1,0:T(8,128)S(1)}, u32[]{:S(2)}, u32[]{:S(2)}) collective-permute-start(f32[256,1024]{1,0:T(8,128)S(1)} %get-tuple-element.74), channel_id=1, source_target_pairs={{0,1},{1,0},{2,3},{3,2},{4,5},{5,4},{6,7},{7,6},{8,9},{9,8},{10,11... | collective-permute-start | bytes 3145736 | tf_op jit(solution)/shard_map/ppermute | solution.py:467
  15.5 18.0 %collective-permute-start.2 = (f32[2,64,1280]{2,1,0:T(8,128)S(1)}, f32[2,64,1280]{2,1,0:T(8,128)S(1)}, u32[]{:S(2)}, u32[]{:S(2)}) collective-permute-start(f32[2,64,1280]{2,1,0:T(8,128)S(1)} %get-tuple-element.76), channel_id=1, source_target_pairs={{0,8},{8,0},{16,24},{24,16},{1,9},{9,1},{17,25},{25,17},{2,10},{10... | collective-permute-start | bytes 1966088 | tf_op jit(solution)/shard_map/ppermute | solution.py:433
  18.5 16.5 %collective-permute-start.3 = (f32[2,64,1280]{2,1,0:T(8,128)S(1)}, f32[2,64,1280]{2,1,0:T(8,128)S(1)}, u32[]{:S(2)}, u32[]{:S(2)}) collective-permute-start(f32[2,64,1280]{2,1,0:T(8,128)S(1)} %get-tuple-element.78), channel_id=1, source_target_pairs={{0,16},{8,24},{16,0},{24,8},{1,17},{9,25},{17,1},{25,9},{2,18},{10... | collective-permute-start | bytes 1966088 | tf_op jit(solution)/shard_map/ppermute | solution.py:433
  20.0 17.2 %collective-permute-start.4 = (f32[520,128]{1,0:T(8,128)S(1)}, f32[520,128]{1,0:T(8,128)S(1)}, u32[]{:S(2)}, u32[]{:S(2)}) collective-permute-start(f32[520,128]{1,0:T(8,128)S(1)} %get-tuple-element.69), channel_id=1, source_target_pairs={{0,2},{1,3},{2,4},{3,5},{4,6},{5,7},{6,0},{7,1},{8,10},{9,11},{10,... | collective-permute-start | bytes 798728 | tf_op jit(solution)/shard_map/ppermute | solution.py:476
  21.6 19.7 %collective-permute-start.5 = (f32[520,128]{1,0:T(8,128)S(1)}, f32[520,128]{1,0:T(8,128)S(1)}, u32[]{:S(2)}, u32[]{:S(2)}) collective-permute-start(f32[520,128]{1,0:T(8,128)S(1)} %get-tuple-element.70), channel_id=1, source_target_pairs={{0,4},{1,5},{2,6},{3,7},{4,0},{5,1},{6,2},{7,3},{8,12},{9,13},{10,... | collective-permute-start | bytes 798728 | tf_op jit(solution)/shard_map/ppermute | solution.py:476
  24.2 17.1 %collective-permute-start.6 = (f32[520,128]{1,0:T(8,128)S(1)}, f32[520,128]{1,0:T(8,128)S(1)}, u32[]{:S(2)}, u32[]{:S(2)}) collective-permute-start(f32[520,128]{1,0:T(8,128)S(1)} %get-tuple-element.71), channel_id=1, source_target_pairs={{0,6},{1,7},{2,0},{3,1},{4,2},{5,3},{6,4},{7,5},{8,14},{9,15},{10,... | collective-permute-start | bytes 798728 | tf_op jit(solution)/shard_map/ppermute | solution.py:476
  35.1 8.7 %collective-permute-start.7 = (f32[64,1280]{1,0:T(8,128)S(1)}, f32[64,1280]{1,0:T(8,128)S(1)}, u32[]{:S(2)}, u32[]{:S(2)}) collective-permute-start(f32[64,1280]{1,0:T(8,128)S(1)} %get-tuple-element.80), channel_id=1, source_target_pairs={{0,16},{8,24},{16,0},{24,8},{1,17},{9,25},{17,1},{25,9},{2,18},{10... | collective-permute-start | bytes 983048 | tf_op jit(solution)/shard_map/ppermute | solution.py:433
  36.7 8.3 %collective-permute-start.8 = (f32[64,1280]{1,0:T(8,128)S(1)}, f32[64,1280]{1,0:T(8,128)S(1)}, u32[]{:S(2)}, u32[]{:S(2)}) collective-permute-start(f32[64,1280]{1,0:T(8,128)S(1)} %get-tuple-element.81), channel_id=1, source_target_pairs={{0,8},{8,0},{16,24},{24,16},{1,9},{9,1},{17,25},{25,17},{2,10},{10... | collective-permute-start | bytes 983048 | tf_op jit(solution)/shard_map/ppermute | solution.py:433
  45.1 7.6 %collective-permute-start.9 = (f32[2,16,1280]{2,1,0:T(8,128)S(1)}, f32[2,16,1280]{2,1,0:T(8,128)S(1)}, u32[]{:S(2)}, u32[]{:S(2)}) collective-permute-start(f32[2,16,1280]{2,1,0:T(8,128)S(1)} %get-tuple-element.90), channel_id=1, source_target_pairs={{0,2},{1,3},{2,0},{3,1},{4,6},{5,7},{6,4},{7,5},{8,10},{9,11},{10,... | collective-permute-start | bytes 491528 | tf_op jit(solution)/shard_map/ppermute | solution.py:493
  47.7 8.8 %collective-permute-start.11 = (f32[2,16,1280]{2,1,0:T(8,128)S(1)}, f32[2,16,1280]{2,1,0:T(8,128)S(1)}, u32[]{:S(2)}, u32[]{:S(2)}) collective-permute-start(f32[2,16,1280]{2,1,0:T(8,128)S(1)} %get-tuple-element.95), channel_id=1, source_target_pairs={{0,2},{1,3},{2,0},{3,1},{4,6},{5,7},{6,4},{7,5},{8,10},{9,11},{10,... | collective-permute-start | bytes 491528 | tf_op jit(solution)/shard_map/ppermute | solution.py:493
  47.8 14.4 %collective-permute-start.16 = (f32[520,128]{1,0:T(8,128)S(1)}, f32[520,128]{1,0:T(8,128)S(1)}, u32[]{:S(2)}, u32[]{:S(2)}) collective-permute-start(f32[520,128]{1,0:T(8,128)S(1)} %get-tuple-element.84), channel_id=1, source_target_pairs={{0,8},{8,0},{16,24},{24,16},{1,9},{9,1},{17,25},{25,17},{2,10},{10... | collective-permute-start | bytes 798728 | tf_op jit(solution)/shard_map/ppermute | solution.py:433
  48.3 13.9 %collective-permute-start.17 = (f32[520,128]{1,0:T(8,128)S(1)}, f32[520,128]{1,0:T(8,128)S(1)}, u32[]{:S(2)}, u32[]{:S(2)}) collective-permute-start(f32[520,128]{1,0:T(8,128)S(1)} %get-tuple-element.85), channel_id=1, source_target_pairs={{0,16},{8,24},{16,0},{24,8},{1,17},{9,25},{17,1},{25,9},{2,18},{10... | collective-permute-start | bytes 798728 | tf_op jit(solution)/shard_map/ppermute | solution.py:433
  48.8 13.4 %collective-permute-start.18 = (f32[520,128]{1,0:T(8,128)S(1)}, f32[520,128]{1,0:T(8,128)S(1)}, u32[]{:S(2)}, u32[]{:S(2)}) collective-permute-start(f32[520,128]{1,0:T(8,128)S(1)} %get-tuple-element.86), channel_id=1, source_target_pairs={{0,24},{8,16},{16,8},{24,0},{1,25},{9,17},{17,9},{25,1},{2,26},{10... | collective-permute-start | bytes 798728 | tf_op jit(solution)/shard_map/ppermute | solution.py:433
  52.7 5.4 %collective-permute-start.10 = (f32[1,16,1280]{2,1,0:T(8,128)S(1)}, f32[1,16,1280]{2,1,0:T(8,128)S(1)}, u32[]{:S(2)}, u32[]{:S(2)}) collective-permute-start(f32[1,16,1280]{2,1,0:T(8,128)S(1)} %get-tuple-element.92), channel_id=1, source_target_pairs={{0,4},{1,5},{2,6},{3,7},{4,0},{5,1},{6,2},{7,3},{8,12},{9,13},{10,... | collective-permute-start | bytes 245768 | tf_op jit(solution)/shard_map/ppermute | solution.py:493
  56.5 5.7 %collective-permute-start.12 = (f32[1,16,1280]{2,1,0:T(8,128)S(1)}, f32[1,16,1280]{2,1,0:T(8,128)S(1)}, u32[]{:S(2)}, u32[]{:S(2)}) collective-permute-start(f32[1,16,1280]{2,1,0:T(8,128)S(1)} %get-tuple-element.97), channel_id=1, source_target_pairs={{0,4},{1,5},{2,6},{3,7},{4,0},{5,1},{6,2},{7,3},{8,12},{9,13},{10,... | collective-permute-start | bytes 245768 | tf_op jit(solution)/shard_map/ppermute | solution.py:493
  62.2 3.8 %copy-start = (f32[512,512]{1,0:T(8,128)S(1)}, f32[512,512]{1,0:T(8,128)}, u32[]{:S(2)}) copy-start(f32[512,512]{1,0:T(8,128)} %table_ref.1) | copy-start | bytes 3145732
  62.2 3.8 %copy-start.3 = (f32[512]{0:T(512)S(1)}, f32[512]{0:T(512)}, u32[]{:S(2)}) copy-start(f32[512]{0:T(512)} %accum_ref.1) | copy-start | bytes 6148
  62.4 3.6 %collective-permute-start.19 = (f32[1056,128]{1,0:T(8,128)S(1)}, f32[1056,128]{1,0:T(8,128)S(1)}, u32[]{:S(2)}, u32[]{:S(2)}) collective-permute-start(f32[1056,128]{1,0:T(8,128)S(1)} %get-tuple-element.100), channel_id=1, source_target_pairs={{0,1},{1,0},{2,3},{3,2},{4,5},{5,4},{6,7},{7,6},{8,9},{9,8},{10,11... | collective-permute-start | bytes 1622024 | tf_op jit(solution)/shard_map/ppermute | solution.py:514
  62.4 8.0 %collective-permute-start.15 = (f32[16,2560]{1,0:T(8,128)S(1)}, f32[16,2560]{1,0:T(8,128)S(1)}, u32[]{:S(2)}, u32[]{:S(2)}) collective-permute-start(f32[16,2560]{1,0:T(8,128)S(1)} %total.1.refs_0_), channel_id=1, source_target_pairs={{0,24},{8,16},{16,8},{24,0},{1,25},{9,17},{17,9},{25,1},{2,26},{10... | collective-permute-start | bytes 491528 | tf_op jit(solution)/shard_map/ppermute | solution.py:433
  63.4 9.8 %collective-permute-start.14 = (f32[16,2560]{1,0:T(8,128)S(1)}, f32[16,2560]{1,0:T(8,128)S(1)}, u32[]{:S(2)}, u32[]{:S(2)}) collective-permute-start(f32[16,2560]{1,0:T(8,128)S(1)} %total.1.refs_0_), channel_id=1, source_target_pairs={{0,16},{8,24},{16,0},{24,8},{1,17},{9,25},{17,1},{25,9},{2,18},{10... | collective-permute-start | bytes 491528 | tf_op jit(solution)/shard_map/ppermute | solution.py:433
  65.0 8.3 %collective-permute-start.13 = (f32[16,2560]{1,0:T(8,128)S(1)}, f32[16,2560]{1,0:T(8,128)S(1)}, u32[]{:S(2)}, u32[]{:S(2)}) collective-permute-start(f32[16,2560]{1,0:T(8,128)S(1)} %total.1.refs_0_), channel_id=1, source_target_pairs={{0,8},{8,0},{16,24},{24,16},{1,9},{9,1},{17,25},{25,17},{2,10},{10... | collective-permute-start | bytes 491528 | tf_op jit(solution)/shard_map/ppermute | solution.py:433

commit v17 on v15

--- a/solution.py
+++ b/solution.py
@@ -91,13 +91,17 @@
         xhat, _ = standardize(ev_ref[tile, :].astype(f32))
         normed_ref[tile, :] = xhat.astype(bf16)
 
-    def project(i, c):
-        rows = pl.ds(i * STEP, STEP)
-        slot = (c * steps + i) % pre_ref.shape[0]
-        pre_ref[slot] = dot_nn(normed_ref[rows, :], win_ref[:, c * width:(c + 1) * width])
+    def project(n):
+        c, i = n // steps, n % steps
+        if i == 0:
+            copies[1 + c].wait()
+        pre_ref[n % pre_ref.shape[0]] = dot_nn(normed_ref[pl.ds(i * STEP, STEP), :], win_ref[:, c * width:(c + 1) * width])
+
+    def gate(n):
+        c, i = n // steps, n % steps
         for at in range(0, STEP, TILE):
             tile = pl.ds(i * STEP + at, TILE)
-            pre = pre_ref[slot, at:at + TILE, :]
+            pre = pre_ref[n % pre_ref.shape[0], at:at + TILE, :]
             sig = 0.5 + 0.5 * jnp.tanh(0.5 * pre)
             hid = pre * sig
             dsilu = sig * (1.0 + (pre - hid))
@@ -111,35 +115,41 @@
                 else:
                     dsilu_ref[tile, (c - 2) * width:(c - 1) * width] = dsilu.astype(bf16)
 
-    for c in range(4):
-        copies[1 + c].wait()
-        for i in range(steps):
-            project(i, c)
+    project(0)
+    for n in range(4 * steps):
+        if n + 1 < 4 * steps:
+            project(n + 1)
+        gate(n)
 
     for copy in copies[5:]:
         copy.wait()
     length = len_ref[0]
     inv_len = 1.0 / length.astype(f32)
     inv_ref[...] = jnp.full(inv_ref.shape, inv_len, f32)
-    for h in range(HEADS):
-        v_cols = slice(h * hd, (h + 1) * hd)
-        q_cols = slice(width + h * hd, width + (h + 1) * hd)
-        k_cols = slice(2 * width + h * hd, 2 * width + (h + 1) * hd)
-        for i in range(steps):
-            rows = pl.ds(i * STEP, STEP)
-            for j in range(i + 1):
-                keys = pl.ds(j * STEP, STEP)
-                slot = (h * 3 + i + j) % raw_ref.shape[0]
-                raw_ref[slot] = dot_nt(hid_ref[rows, q_cols], hid_ref[keys, k_cols])
-                for at in range(0, STEP, 2 * TILE):
-                    half = raw_ref[slot, at:at + 2 * TILE, :] * (0.5 * scale)
-                    weights = (half + half * jnp.tanh(half)) * inv_len
-                    if i == j:
-                        row = at + lax.broadcasted_iota(jnp.int32, weights.shape, 0)
-                        weights = jnp.where(row >= lax.broadcasted_iota(jnp.int32, weights.shape, 1), weights, 0.0)
-                    weights_ref[h, pl.ds(i * STEP + at, 2 * TILE), keys] = weights.astype(bf16)
-            seen = pl.ds(0, (i + 1) * STEP)
+    blocks = [(h, i, j) for h in range(HEADS) for i in range(steps) for j in range(i + 1)]
+
+    def score(n):
+        h, i, j = blocks[n]
+        query = hid_ref[pl.ds(i * STEP, STEP), width + h * hd:width + (h + 1) * hd]
+        key = hid_ref[pl.ds(j * STEP, STEP), 2 * width + h * hd:2 * width + (h + 1) * hd]
+        raw_ref[n % raw_ref.shape[0]] = dot_nt(query, key)
+
+    score(0)
+    for n, (h, i, j) in enumerate(blocks):
+        if n + 1 < len(blocks):
+            score(n + 1)
+        for at in range(0, STEP, 2 * TILE):
+            half = raw_ref[n % raw_ref.shape[0], at:at + 2 * TILE, :] * (0.5 * scale)
+            weights = (half + half * jnp.tanh(half)) * inv_len
+            if i == j:
+                row = at + lax.broadcasted_iota(jnp.int32, weights.shape, 0)
+                weights = jnp.where(row >= lax.broadcasted_iota(jnp.int32, weights.shape, 1), weights, 0.0)
+            weights_ref[h, pl.ds(i * STEP + at, 2 * TILE), pl.ds(j * STEP, STEP)] = weights.astype(bf16)
+        if j == i:
+            rows, seen, v_cols = pl.ds(i * STEP, STEP), pl.ds(0, (i + 1) * STEP), slice(h * hd, (h + 1) * hd)
             att_ref[rows, v_cols] = dot_nn(weights_ref[h, rows, seen], hid_ref[seen, v_cols])
+        if i < steps - 1 or j < i:
+            continue
         for i in range(h, steps, HEADS):
             rows = pl.ds(i * STEP, STEP)
             normed_t_ref[rows, :] = dot_nt(order_ref[rows, :], normed_ref[...]).astype(bf16)
@@ -182,25 +192,33 @@
     steps = tokens // STEP
     factor = inv_ref[:1, :hd] * (0.5 * scale)
 
-    for h in range(HEADS):
+    blocks = [(h, j, i) for h in range(HEADS) for j in range(steps) for i in range(j, steps)]
+    slots = raw_ref.shape[0]
+
+    def score(n):
+        h, j, i = blocks[n]
+        keys, rows, v_cols = pl.ds(j * STEP, STEP), pl.ds(i * STEP, STEP), slice(h * hd, (h + 1) * hd)
+        raw_ref[n % slots] = dot_nt(
+            hid_ref[keys, 2 * width + h * hd:2 * width + (h + 1) * hd], hid_ref[rows, width + h * hd:width + (h + 1) * hd])
+        weight_ref[n % slots] = dot_nt(hid_ref[keys, v_cols], gatt_ref[rows, v_cols])
+
+    score(0)
+    for n, (h, j, i) in enumerate(blocks):
+        if n + 1 < len(blocks):
+            score(n + 1)
+        for at in range(0, STEP, TILE):
+            half = raw_ref[n % slots, at:at + TILE, :] * (0.5 * scale)
+            gate = jnp.tanh(half)
+            gscore = weight_ref[n % slots, at:at + TILE, :] * ((1.0 + gate) * (1.0 + half * (1.0 - gate)))
+            if i == j:
+                row = at + lax.broadcasted_iota(jnp.int32, gscore.shape, 0)
+                gscore = jnp.where(row <= lax.broadcasted_iota(jnp.int32, gscore.shape, 1), gscore, 0.0)
+            score_ref[h % 2, pl.ds(j * STEP + at, TILE), pl.ds(i * STEP, STEP)] = gscore.astype(bf16)
+        if j < steps - 1:
+            continue
         v_cols = slice(h * hd, (h + 1) * hd)
         q_cols = slice(width + h * hd, width + (h + 1) * hd)
         k_cols = slice(2 * width + h * hd, 2 * width + (h + 1) * hd)
-        for j in range(steps):
-            keys = pl.ds(j * STEP, STEP)
-            for i in range(j, steps):
-                rows = pl.ds(i * STEP, STEP)
-                slot = (h * 3 + i + j) % raw_ref.shape[0]
-                raw_ref[slot] = dot_nt(hid_ref[keys, k_cols], hid_ref[rows, q_cols])
-                weight_ref[slot] = dot_nt(hid_ref[keys, v_cols], gatt_ref[rows, v_cols])
-                for at in range(0, STEP, TILE):
-                    half = raw_ref[slot, at:at + TILE, :] * (0.5 * scale)
-                    gate = jnp.tanh(half)
-                    gscore = weight_ref[slot, at:at + TILE, :] * ((1.0 + gate) * (1.0 + half * (1.0 - gate)))
-                    if i == j:
-                        row = at + lax.broadcasted_iota(jnp.int32, gscore.shape, 0)
-                        gscore = jnp.where(row <= lax.broadcasted_iota(jnp.int32, gscore.shape, 1), gscore, 0.0)
-                    score_ref[h % 2, pl.ds(j * STEP + at, TILE), rows] = gscore.astype(bf16)
         for j in range(steps):
             keys, later, seen = pl.ds(j * STEP, STEP), pl.ds(j * STEP, tokens - j * STEP), pl.ds(0, (j + 1) * STEP)
             grad_k = dot_nn(score_ref[h % 2, keys, later], hid_ref[later, q_cols])

time: 74 us -> 73.9 us (level)
  no operation moved by 1% of the time
where the time goes in v17:
time: 73.9 us; the launch traced here: 73.8 us
  waiting for transfers between devices  31.2 us (42%)
  starting transfers between devices  24.5 us (33%)
  Pallas kernels  16.7 us (23%)
  between operations  1.41 us (2%)
    ppermute x10, waiting for transfers between devices, body(): lax.ppermute(v, 'dp', [(i, i ^ bit) for i in range(dp_size)])  17.9 us
    pallas_call x13, Pallas kernels, call(): pl.pallas_call(kernel, name=name, in_specs=[pl.BlockSpec(memory_space=p)...  16.7 us
    ppermute x10, starting transfers between devices, body(): lax.ppermute(v, 'dp', [(i, i ^ bit) for i in range(dp_size)])  13.6 us
    ppermute x4, waiting for transfers between devices, body(): lax.ppermute(v, 'rows', [(i, i ^ 2 << bit) for i in range(rows_size)])  8.86 us
    ppermute x3, starting transfers between devices, body(): lax.ppermute(v, 'rows', [(i, (i + 2 * k) % rows_size) for i in range(rows...  5.5 us
    ppermute x4, starting transfers between devices, body(): lax.ppermute(v, 'rows', [(i, i ^ 2 << bit) for i in range(rows_size)])  4.67 us
    ppermute x3, waiting for transfers between devices, body(): lax.ppermute(v, 'rows', [(i, (i + 2 * k) % rows_size) for i in range(rows...  4.05 us
  transfers between devices with their start and end apart: 20, of which 12 were waited for; matrix products, arithmetic and copies ran while one was open for 0% of the time, Pallas kernels for 10%

profile of v17, /device:TPU:0, one launch (start us, length us, event | category | flops | bytes accessed | tf_op | source)
XLA Modules:
  0.0 73.8 jit_solution(16996759539999545892)
XLA Ops:
  1.3 7.7 %forward_part.1 = (f32[256,1536]{1,0:T(8,128)S(1)}, f32[256,1536]{1,0:T(8,128)S(1)}, bf16[512,1536]{1,0:T(8,128)(2,1)S(1)}, bf16[512,1024]{1,0:T(8,128)(2,1)S(1)...) custom-call(s32[1]{0:T(128)S(6)} %copy.13.len_ref, ...), custom_call_target="tpu_custom_call" | custom-call | flops 99999997952 | bytes 65536 | tf_op jit(solution)/shard_map/forward_part/pallas_call | solution.py:429
  9.0 0.5 collective-permute-start
  9.5 0.0 copy-start.1
  9.5 0.0 copy-start.2
  9.6 2.6 %attention_part.1 = (f32[256,1024]{1,0:T(8,128)S(1)}, f32[256,1024]{1,0:T(8,128)S(1)}, bf16[512,1024]{1,0:T(8,128)(2,1)S(1)}) custom-call(f32[8,128]{1,0:T(8,128)S(1)} %get-tuple-element.62.inv_ref, bf16[512,1536]{1,0:T(8,128)(2,1)S(1)} %get-tuple-element.63.hid_ref, bf16[512,1024]{1,0:T(8,128)(2,1)S(1)} %get-tuple-element.64.dsilu_ref, ...), custom_call_target="tpu_custom_call" | custom-call | flops 99999997952 | bytes 65536 | tf_op jit(solution)/shard_map/attention_part/pallas_call | solution.py:429
  12.2 0.1 collective-permute-start.1
  12.3 0.3 collective-permute-done
  12.6 0.0 copy-done.1
  12.6 0.0 copy-done.2
  12.6 2.2 %events_part.1 = (f32[520,128]{1,0:T(8,128)S(1)}, f32[520,128]{1,0:T(8,128)S(1)}, f32[520,128]{1,0:T(8,128)S(1)}, f32[520,128]{1,0:T(8,128)S(1)}) custom-call(bf16[512,512]{1,0:T(8,128)(2,1)S(1)} %get-tuple-element.56.ev_ref, bf16[512,512]{1,0:T(8,128)(2,1)S(1)} %get-tuple-element.57.masked_ref, bf16[512,2048]{1,0:T(8,128)(2,1)S(1)} %get-tuple-element.58.win_ref, ...), custom_call_target="tpu_custom_call" | custom-call | flops 99999997952 | bytes 65536 | tf_op jit(solution)/shard_map/events_part/pallas_call | solution.py:429
  14.8 0.0 collective-permute-done.1
  14.9 0.3 first_sums.1
  15.2 2.9 %collective-permute-start.2 = (f32[2,64,1280]{2,1,0:T(8,128)S(1)}, f32[2,64,1280]{2,1,0:T(8,128)S(1)}, u32[]{:S(2)}, u32[]{:S(2)}) collective-permute-start(f32[2,64,1280]{2,1,0:T(8,128)S(1)} %get-tuple-element.76), channel_id=1, source_target_pairs={{0,8},{8,0},{16,24},{24,16},{1,9},{9,1},{17,25},{25,17},{2,10},{10... | collective-permute-start | bytes 1966088 | tf_op jit(solution)/shard_map/ppermute | solution.py:448
  18.1 1.5 %collective-permute-start.3 = (f32[2,64,1280]{2,1,0:T(8,128)S(1)}, f32[2,64,1280]{2,1,0:T(8,128)S(1)}, u32[]{:S(2)}, u32[]{:S(2)}) collective-permute-start(f32[2,64,1280]{2,1,0:T(8,128)S(1)} %get-tuple-element.78), channel_id=1, source_target_pairs={{0,16},{8,24},{16,0},{24,8},{1,17},{9,25},{17,1},{25,9},{2,18},{10... | collective-permute-start | bytes 1966088 | tf_op jit(solution)/shard_map/ppermute | solution.py:448
  19.6 1.6 %collective-permute-start.4 = (f32[520,128]{1,0:T(8,128)S(1)}, f32[520,128]{1,0:T(8,128)S(1)}, u32[]{:S(2)}, u32[]{:S(2)}) collective-permute-start(f32[520,128]{1,0:T(8,128)S(1)} %get-tuple-element.69), channel_id=1, source_target_pairs={{0,2},{1,3},{2,4},{3,5},{4,6},{5,7},{6,0},{7,1},{8,10},{9,11},{10,... | collective-permute-start | bytes 798728 | tf_op jit(solution)/shard_map/ppermute | solution.py:491
  21.2 2.6 %collective-permute-start.5 = (f32[520,128]{1,0:T(8,128)S(1)}, f32[520,128]{1,0:T(8,128)S(1)}, u32[]{:S(2)}, u32[]{:S(2)}) collective-permute-start(f32[520,128]{1,0:T(8,128)S(1)} %get-tuple-element.70), channel_id=1, source_target_pairs={{0,4},{1,5},{2,6},{3,7},{4,0},{5,1},{6,2},{7,3},{8,12},{9,13},{10,... | collective-permute-start | bytes 798728 | tf_op jit(solution)/shard_map/ppermute | solution.py:491
  23.8 1.3 %collective-permute-start.6 = (f32[520,128]{1,0:T(8,128)S(1)}, f32[520,128]{1,0:T(8,128)S(1)}, u32[]{:S(2)}, u32[]{:S(2)}) collective-permute-start(f32[520,128]{1,0:T(8,128)S(1)} %get-tuple-element.71), channel_id=1, source_target_pairs={{0,6},{1,7},{2,0},{3,1},{4,2},{5,3},{6,4},{7,5},{8,14},{9,15},{10,... | collective-permute-start | bytes 798728 | tf_op jit(solution)/shard_map/ppermute | solution.py:491
  25.1 8.0 %collective-permute-done.2.from_x_ref = f32[2,64,1280]{2,1,0:T(8,128)S(1)} collective-permute-done((f32[2,64,1280]{2,1,0:T(8,128)S(1)}, f32[2,64,1280]{2,1,0:T(8,128)S(1)}, u32[]{:S(2)}, u32[]{:S(2)}) %collective-permute-start.2) | collective-permute-done | bytes 655392 | tf_op jit(solution)/shard_map/ppermute | solution.py:448
  33.2 1.5 %collective-permute-done.3.from_y_ref = f32[2,64,1280]{2,1,0:T(8,128)S(1)} collective-permute-done((f32[2,64,1280]{2,1,0:T(8,128)S(1)}, f32[2,64,1280]{2,1,0:T(8,128)S(1)}, u32[]{:S(2)}, u32[]{:S(2)}) %collective-permute-start.3) | collective-permute-done | bytes 655392 | tf_op jit(solution)/shard_map/ppermute | solution.py:448
  34.6 0.1 second_sums.1
  34.8 1.6 %collective-permute-start.7 = (f32[64,1280]{1,0:T(8,128)S(1)}, f32[64,1280]{1,0:T(8,128)S(1)}, u32[]{:S(2)}, u32[]{:S(2)}) collective-permute-start(f32[64,1280]{1,0:T(8,128)S(1)} %get-tuple-element.80), channel_id=1, source_target_pairs={{0,16},{8,24},{16,0},{24,8},{1,17},{9,25},{17,1},{25,9},{2,18},{10... | collective-permute-start | bytes 983048 | tf_op jit(solution)/shard_map/ppermute | solution.py:448
  36.4 0.5 collective-permute-start.8
  36.9 0.0 collective-permute-done.4.refs_1_
  36.9 4.0 %collective-permute-done.5.refs_2_ = f32[520,128]{1,0:T(8,128)S(1)} collective-permute-done((f32[520,128]{1,0:T(8,128)S(1)}, f32[520,128]{1,0:T(8,128)S(1)}, u32[]{:S(2)}, u32[]{:S(2)}) %collective-permute-start.5) | collective-permute-done | bytes 266272 | tf_op jit(solution)/shard_map/ppermute | solution.py:491
  40.9 0.0 collective-permute-done.6.refs_3_
  40.9 0.1 by_part.1
  41.0 2.4 %collective-permute-done.7 = f32[64,1280]{1,0:T(8,128)S(1)} collective-permute-done((f32[64,1280]{1,0:T(8,128)S(1)}, f32[64,1280]{1,0:T(8,128)S(1)}, u32[]{:S(2)}, u32[]{:S(2)}) %collective-permute-start.7) | collective-permute-done | bytes 327712 | tf_op jit(solution)/shard_map/ppermute | solution.py:448
  43.4 1.3 %collective-permute-done.8 = f32[64,1280]{1,0:T(8,128)S(1)} collective-permute-done((f32[64,1280]{1,0:T(8,128)S(1)}, f32[64,1280]{1,0:T(8,128)S(1)}, u32[]{:S(2)}, u32[]{:S(2)}) %collective-permute-start.8) | collective-permute-done | bytes 327712 | tf_op jit(solution)/shard_map/ppermute | solution.py:448
  44.7 0.1 chip_sums.3
  44.8 2.6 %collective-permute-start.9 = (f32[2,16,1280]{2,1,0:T(8,128)S(1)}, f32[2,16,1280]{2,1,0:T(8,128)S(1)}, u32[]{:S(2)}, u32[]{:S(2)}) collective-permute-start(f32[2,16,1280]{2,1,0:T(8,128)S(1)} %get-tuple-element.90), channel_id=1, source_target_pairs={{0,2},{1,3},{2,0},{3,1},{4,6},{5,7},{6,4},{7,5},{8,10},{9,11},{10,... | collective-permute-start | bytes 491528 | tf_op jit(solution)/shard_map/ppermute | solution.py:508
  47.4 0.1 collective-permute-start.11
  47.4 0.5 collective-permute-start.16
  48.0 0.5 collective-permute-start.17
  48.5 2.4 %collective-permute-start.18 = (f32[520,128]{1,0:T(8,128)S(1)}, f32[520,128]{1,0:T(8,128)S(1)}, u32[]{:S(2)}, u32[]{:S(2)}) collective-permute-start(f32[520,128]{1,0:T(8,128)S(1)} %get-tuple-element.86), channel_id=1, source_target_pairs={{0,24},{8,16},{16,8},{24,0},{1,25},{9,17},{17,9},{25,1},{2,26},{10... | collective-permute-start | bytes 798728 | tf_op jit(solution)/shard_map/ppermute | solution.py:448
  50.9 1.4 %collective-permute-done.9.recv_in = f32[2,16,1280]{2,1,0:T(8,128)S(1)} collective-permute-done((f32[2,16,1280]{2,1,0:T(8,128)S(1)}, f32[2,16,1280]{2,1,0:T(8,128)S(1)}, u32[]{:S(2)}, u32[]{:S(2)}) %collective-permute-start.9) | collective-permute-done | bytes 163872 | tf_op jit(solution)/shard_map/ppermute | solution.py:508
  52.4 1.9 %collective-permute-start.10 = (f32[1,16,1280]{2,1,0:T(8,128)S(1)}, f32[1,16,1280]{2,1,0:T(8,128)S(1)}, u32[]{:S(2)}, u32[]{:S(2)}) collective-permute-start(f32[1,16,1280]{2,1,0:T(8,128)S(1)} %get-tuple-element.92), channel_id=1, source_target_pairs={{0,4},{1,5},{2,6},{3,7},{4,0},{5,1},{6,2},{7,3},{8,12},{9,13},{10,... | collective-permute-start | bytes 245768 | tf_op jit(solution)/shard_map/ppermute | solution.py:508
  54.3 1.8 %collective-permute-done.11.recv_in = f32[2,16,1280]{2,1,0:T(8,128)S(1)} collective-permute-done((f32[2,16,1280]{2,1,0:T(8,128)S(1)}, f32[2,16,1280]{2,1,0:T(8,128)S(1)}, u32[]{:S(2)}, u32[]{:S(2)}) %collective-permute-start.11) | collective-permute-done | bytes 163872 | tf_op jit(solution)/shard_map/ppermute | solution.py:508
  56.2 0.1 collective-permute-start.12
  56.2 1.6 %collective-permute-done.10.recv_a_ref = f32[1,16,1280]{2,1,0:T(8,128)S(1)} collective-permute-done((f32[1,16,1280]{2,1,0:T(8,128)S(1)}, f32[1,16,1280]{2,1,0:T(8,128)S(1)}, u32[]{:S(2)}, u32[]{:S(2)}) %collective-permute-start.10) | collective-permute-done | bytes 81952 | tf_op jit(solution)/shard_map/ppermute | solution.py:508
  57.8 4.0 %collective-permute-done.12.recv_b_ref = f32[1,16,1280]{2,1,0:T(8,128)S(1)} collective-permute-done((f32[1,16,1280]{2,1,0:T(8,128)S(1)}, f32[1,16,1280]{2,1,0:T(8,128)S(1)}, u32[]{:S(2)}, u32[]{:S(2)}) %collective-permute-start.12) | collective-permute-done | bytes 81952 | tf_op jit(solution)/shard_map/ppermute | solution.py:508
  61.9 0.0 copy-start
  61.9 0.0 copy-start.3
  61.9 0.0 collective-permute-done.16.refs_1_
  61.9 0.0 collective-permute-done.17.refs_2_
  61.9 0.0 collective-permute-done.18.refs_3_
  61.9 0.1 by_core.1
  62.0 0.1 collective-permute-start.19
  62.1 1.0 %collective-permute-start.15 = (f32[16,2560]{1,0:T(8,128)S(1)}, f32[16,2560]{1,0:T(8,128)S(1)}, u32[]{:S(2)}, u32[]{:S(2)}) collective-permute-start(f32[16,2560]{1,0:T(8,128)S(1)} %total.1.refs_0_), channel_id=1, source_target_pairs={{0,24},{8,16},{16,8},{24,0},{1,25},{9,17},{17,9},{25,1},{2,26},{10... | collective-permute-start | bytes 491528 | tf_op jit(solution)/shard_map/ppermute | solution.py:448
  63.1 1.5 %collective-permute-start.14 = (f32[16,2560]{1,0:T(8,128)S(1)}, f32[16,2560]{1,0:T(8,128)S(1)}, u32[]{:S(2)}, u32[]{:S(2)}) collective-permute-start(f32[16,2560]{1,0:T(8,128)S(1)} %total.1.refs_0_), channel_id=1, source_target_pairs={{0,16},{8,24},{16,0},{24,8},{1,17},{9,25},{17,1},{25,9},{2,18},{10... | collective-permute-start | bytes 491528 | tf_op jit(solution)/shard_map/ppermute | solution.py:448
  64.6 1.0 %collective-permute-start.13 = (f32[16,2560]{1,0:T(8,128)S(1)}, f32[16,2560]{1,0:T(8,128)S(1)}, u32[]{:S(2)}, u32[]{:S(2)}) collective-permute-start(f32[16,2560]{1,0:T(8,128)S(1)} %total.1.refs_0_), channel_id=1, source_target_pairs={{0,8},{8,0},{16,24},{24,16},{1,9},{9,1},{17,25},{25,17},{2,10},{10... | collective-permute-start | bytes 491528 | tf_op jit(solution)/shard_map/ppermute | solution.py:448
  65.6 0.0 collective-permute-done.19.recv_ref
  65.7 0.0 copy-done
  65.7 0.0 copy-done.3
  65.7 2.5 %table_part.1 = (f32[512,512]{1,0:T(8,128)}, f32[512]{0:T(512)}) custom-call(f32[1056,128]{1,0:T(8,128)S(1)} %get-tuple-element.99.keep_ref, f32[1056,128]{1,0:T(8,128)S(1)} %collective-permute-done.19.recv_ref, f32[512,512]{1,0:T(8,128)S(1)} %copy-done, f32[512]{0:T(512)S(1)} %copy-done.3), custom_call_target="tpu_custom_call" | custom-call | flops 1000000000 | bytes 65536 | tf_op jit(solution)/shard_map/table_part/pallas_call | solution.py:429
  68.2 2.0 %collective-permute-done.15.refs_3_ = f32[16,2560]{1,0:T(8,128)S(1)} collective-permute-done((f32[16,2560]{1,0:T(8,128)S(1)}, f32[16,2560]{1,0:T(8,128)S(1)}, u32[]{:S(2)}, u32[]{:S(2)}) %collective-permute-start.15) | collective-permute-done | bytes 163872 | tf_op jit(solution)/shard_map/ppermute | solution.py:448
  70.1 2.8 %collective-permute-done.14.refs_2_ = f32[16,2560]{1,0:T(8,128)S(1)} collective-permute-done((f32[16,2560]{1,0:T(8,128)S(1)}, f32[16,2560]{1,0:T(8,128)S(1)}, u32[]{:S(2)}, u32[]{:S(2)}) %collective-permute-start.14) | collective-permute-done | bytes 163872 | tf_op jit(solution)/shard_map/ppermute | solution.py:448
  72.9 0.0 collective-permute-done.13.refs_1_
  72.9 0.9 %gather.1 = (f32[4,16,2048]{2,1,0:T(8,128)}, f32[4,16,512]{2,1,0:T(8,128)}) custom-call(f32[16,2560]{1,0:T(8,128)S(1)} %total.1.refs_0_, f32[16,2560]{1,0:T(8,128)S(1)} %collective-permute-done.13.refs_1_, f32[16,2560]{1,0:T(8,128)S(1)} %collective-permute-done.14.refs_2_, f32[16,2560]{1,0:T(8,128)S(1)} %collective-permute-done.15.refs_3_), custom_call_target="tpu_custom_call" | custom-call | flops 1000000000 | bytes 65536 | tf_op jit(solution)/shard_map/gather/pallas_call | solution.py:429
  (3 shorter events, 0.1 us)
Async XLA Ops:
  9.0 3.6 %collective-permute-start = (f32[256,1536]{1,0:T(8,128)S(1)}, f32[256,1536]{1,0:T(8,128)S(1)}, u32[]{:S(2)}, u32[]{:S(2)}) collective-permute-start(f32[256,1536]{1,0:T(8,128)S(1)} %get-tuple-element.60), channel_id=1, source_target_pairs={{0,1},{1,0},{2,3},{3,2},{4,5},{5,4},{6,7},{7,6},{8,9},{9,8},{10,11... | collective-permute-start | bytes 4718600 | tf_op jit(solution)/shard_map/ppermute | solution.py:477
  9.5 3.0 %copy-start.1 = (s32[1,32,16]{1,2,0:T(8,128)S(1)}, s32[1,32,16]{1,2,0:T(8,128)}, u32[]{:S(2)}) copy-start(s32[1,32,16]{1,2,0:T(8,128)} %param.14) | copy-start | bytes 6148
  9.5 3.0 %copy-start.2 = (s32[1,512]{1,0:T(1,128)S(1)}, s32[1,512]{1,0:T(1,128)}, u32[]{:S(2)}) copy-start(s32[1,512]{1,0:T(1,128)} %slot_ref.1) | copy-start | bytes 6148
  12.2 2.7 %collective-permute-start.1 = (f32[256,1024]{1,0:T(8,128)S(1)}, f32[256,1024]{1,0:T(8,128)S(1)}, u32[]{:S(2)}, u32[]{:S(2)}) collective-permute-start(f32[256,1024]{1,0:T(8,128)S(1)} %get-tuple-element.74), channel_id=1, source_target_pairs={{0,1},{1,0},{2,3},{3,2},{4,5},{5,4},{6,7},{7,6},{8,9},{9,8},{10,11... | collective-permute-start | bytes 3145736 | tf_op jit(solution)/shard_map/ppermute | solution.py:482
  15.2 18.0 %collective-permute-start.2 = (f32[2,64,1280]{2,1,0:T(8,128)S(1)}, f32[2,64,1280]{2,1,0:T(8,128)S(1)}, u32[]{:S(2)}, u32[]{:S(2)}) collective-permute-start(f32[2,64,1280]{2,1,0:T(8,128)S(1)} %get-tuple-element.76), channel_id=1, source_target_pairs={{0,8},{8,0},{16,24},{24,16},{1,9},{9,1},{17,25},{25,17},{2,10},{10... | collective-permute-start | bytes 1966088 | tf_op jit(solution)/shard_map/ppermute | solution.py:448
  18.1 16.5 %collective-permute-start.3 = (f32[2,64,1280]{2,1,0:T(8,128)S(1)}, f32[2,64,1280]{2,1,0:T(8,128)S(1)}, u32[]{:S(2)}, u32[]{:S(2)}) collective-permute-start(f32[2,64,1280]{2,1,0:T(8,128)S(1)} %get-tuple-element.78), channel_id=1, source_target_pairs={{0,16},{8,24},{16,0},{24,8},{1,17},{9,25},{17,1},{25,9},{2,18},{10... | collective-permute-start | bytes 1966088 | tf_op jit(solution)/shard_map/ppermute | solution.py:448
  19.6 17.2 %collective-permute-start.4 = (f32[520,128]{1,0:T(8,128)S(1)}, f32[520,128]{1,0:T(8,128)S(1)}, u32[]{:S(2)}, u32[]{:S(2)}) collective-permute-start(f32[520,128]{1,0:T(8,128)S(1)} %get-tuple-element.69), channel_id=1, source_target_pairs={{0,2},{1,3},{2,4},{3,5},{4,6},{5,7},{6,0},{7,1},{8,10},{9,11},{10,... | collective-permute-start | bytes 798728 | tf_op jit(solution)/shard_map/ppermute | solution.py:491
  21.2 19.7 %collective-permute-start.5 = (f32[520,128]{1,0:T(8,128)S(1)}, f32[520,128]{1,0:T(8,128)S(1)}, u32[]{:S(2)}, u32[]{:S(2)}) collective-permute-start(f32[520,128]{1,0:T(8,128)S(1)} %get-tuple-element.70), channel_id=1, source_target_pairs={{0,4},{1,5},{2,6},{3,7},{4,0},{5,1},{6,2},{7,3},{8,12},{9,13},{10,... | collective-permute-start | bytes 798728 | tf_op jit(solution)/shard_map/ppermute | solution.py:491
  23.8 17.1 %collective-permute-start.6 = (f32[520,128]{1,0:T(8,128)S(1)}, f32[520,128]{1,0:T(8,128)S(1)}, u32[]{:S(2)}, u32[]{:S(2)}) collective-permute-start(f32[520,128]{1,0:T(8,128)S(1)} %get-tuple-element.71), channel_id=1, source_target_pairs={{0,6},{1,7},{2,0},{3,1},{4,2},{5,3},{6,4},{7,5},{8,14},{9,15},{10,... | collective-permute-start | bytes 798728 | tf_op jit(solution)/shard_map/ppermute | solution.py:491
  34.8 8.7 %collective-permute-start.7 = (f32[64,1280]{1,0:T(8,128)S(1)}, f32[64,1280]{1,0:T(8,128)S(1)}, u32[]{:S(2)}, u32[]{:S(2)}) collective-permute-start(f32[64,1280]{1,0:T(8,128)S(1)} %get-tuple-element.80), channel_id=1, source_target_pairs={{0,16},{8,24},{16,0},{24,8},{1,17},{9,25},{17,1},{25,9},{2,18},{10... | collective-permute-start | bytes 983048 | tf_op jit(solution)/shard_map/ppermute | solution.py:448
  36.4 8.3 %collective-permute-start.8 = (f32[64,1280]{1,0:T(8,128)S(1)}, f32[64,1280]{1,0:T(8,128)S(1)}, u32[]{:S(2)}, u32[]{:S(2)}) collective-permute-start(f32[64,1280]{1,0:T(8,128)S(1)} %get-tuple-element.81), channel_id=1, source_target_pairs={{0,8},{8,0},{16,24},{24,16},{1,9},{9,1},{17,25},{25,17},{2,10},{10... | collective-permute-start | bytes 983048 | tf_op jit(solution)/shard_map/ppermute | solution.py:448
  44.8 7.6 %collective-permute-start.9 = (f32[2,16,1280]{2,1,0:T(8,128)S(1)}, f32[2,16,1280]{2,1,0:T(8,128)S(1)}, u32[]{:S(2)}, u32[]{:S(2)}) collective-permute-start(f32[2,16,1280]{2,1,0:T(8,128)S(1)} %get-tuple-element.90), channel_id=1, source_target_pairs={{0,2},{1,3},{2,0},{3,1},{4,6},{5,7},{6,4},{7,5},{8,10},{9,11},{10,... | collective-permute-start | bytes 491528 | tf_op jit(solution)/shard_map/ppermute | solution.py:508
  47.4 8.8 %collective-permute-start.11 = (f32[2,16,1280]{2,1,0:T(8,128)S(1)}, f32[2,16,1280]{2,1,0:T(8,128)S(1)}, u32[]{:S(2)}, u32[]{:S(2)}) collective-permute-start(f32[2,16,1280]{2,1,0:T(8,128)S(1)} %get-tuple-element.95), channel_id=1, source_target_pairs={{0,2},{1,3},{2,0},{3,1},{4,6},{5,7},{6,4},{7,5},{8,10},{9,11},{10,... | collective-permute-start | bytes 491528 | tf_op jit(solution)/shard_map/ppermute | solution.py:508
  47.4 14.4 %collective-permute-start.16 = (f32[520,128]{1,0:T(8,128)S(1)}, f32[520,128]{1,0:T(8,128)S(1)}, u32[]{:S(2)}, u32[]{:S(2)}) collective-permute-start(f32[520,128]{1,0:T(8,128)S(1)} %get-tuple-element.84), channel_id=1, source_target_pairs={{0,8},{8,0},{16,24},{24,16},{1,9},{9,1},{17,25},{25,17},{2,10},{10... | collective-permute-start | bytes 798728 | tf_op jit(solution)/shard_map/ppermute | solution.py:448
  48.0 13.9 %collective-permute-start.17 = (f32[520,128]{1,0:T(8,128)S(1)}, f32[520,128]{1,0:T(8,128)S(1)}, u32[]{:S(2)}, u32[]{:S(2)}) collective-permute-start(f32[520,128]{1,0:T(8,128)S(1)} %get-tuple-element.85), channel_id=1, source_target_pairs={{0,16},{8,24},{16,0},{24,8},{1,17},{9,25},{17,1},{25,9},{2,18},{10... | collective-permute-start | bytes 798728 | tf_op jit(solution)/shard_map/ppermute | solution.py:448
  48.5 13.4 %collective-permute-start.18 = (f32[520,128]{1,0:T(8,128)S(1)}, f32[520,128]{1,0:T(8,128)S(1)}, u32[]{:S(2)}, u32[]{:S(2)}) collective-permute-start(f32[520,128]{1,0:T(8,128)S(1)} %get-tuple-element.86), channel_id=1, source_target_pairs={{0,24},{8,16},{16,8},{24,0},{1,25},{9,17},{17,9},{25,1},{2,26},{10... | collective-permute-start | bytes 798728 | tf_op jit(solution)/shard_map/ppermute | solution.py:448
  52.4 5.4 %collective-permute-start.10 = (f32[1,16,1280]{2,1,0:T(8,128)S(1)}, f32[1,16,1280]{2,1,0:T(8,128)S(1)}, u32[]{:S(2)}, u32[]{:S(2)}) collective-permute-start(f32[1,16,1280]{2,1,0:T(8,128)S(1)} %get-tuple-element.92), channel_id=1, source_target_pairs={{0,4},{1,5},{2,6},{3,7},{4,0},{5,1},{6,2},{7,3},{8,12},{9,13},{10,... | collective-permute-start | bytes 245768 | tf_op jit(solution)/shard_map/ppermute | solution.py:508
  56.2 5.7 %collective-permute-start.12 = (f32[1,16,1280]{2,1,0:T(8,128)S(1)}, f32[1,16,1280]{2,1,0:T(8,128)S(1)}, u32[]{:S(2)}, u32[]{:S(2)}) collective-permute-start(f32[1,16,1280]{2,1,0:T(8,128)S(1)} %get-tuple-element.97), channel_id=1, source_target_pairs={{0,4},{1,5},{2,6},{3,7},{4,0},{5,1},{6,2},{7,3},{8,12},{9,13},{10,... | collective-permute-start | bytes 245768 | tf_op jit(solution)/shard_map/ppermute | solution.py:508
  61.9 3.8 %copy-start = (f32[512,512]{1,0:T(8,128)S(1)}, f32[512,512]{1,0:T(8,128)}, u32[]{:S(2)}) copy-start(f32[512,512]{1,0:T(8,128)} %table_ref.1) | copy-start | bytes 3145732
  61.9 3.8 %copy-start.3 = (f32[512]{0:T(512)S(1)}, f32[512]{0:T(512)}, u32[]{:S(2)}) copy-start(f32[512]{0:T(512)} %accum_ref.1) | copy-start | bytes 6148
  62.0 3.6 %collective-permute-start.19 = (f32[1056,128]{1,0:T(8,128)S(1)}, f32[1056,128]{1,0:T(8,128)S(1)}, u32[]{:S(2)}, u32[]{:S(2)}) collective-permute-start(f32[1056,128]{1,0:T(8,128)S(1)} %get-tuple-element.100), channel_id=1, source_target_pairs={{0,1},{1,0},{2,3},{3,2},{4,5},{5,4},{6,7},{7,6},{8,9},{9,8},{10,11... | collective-permute-start | bytes 1622024 | tf_op jit(solution)/shard_map/ppermute | solution.py:529
  62.1 8.0 %collective-permute-start.15 = (f32[16,2560]{1,0:T(8,128)S(1)}, f32[16,2560]{1,0:T(8,128)S(1)}, u32[]{:S(2)}, u32[]{:S(2)}) collective-permute-start(f32[16,2560]{1,0:T(8,128)S(1)} %total.1.refs_0_), channel_id=1, source_target_pairs={{0,24},{8,16},{16,8},{24,0},{1,25},{9,17},{17,9},{25,1},{2,26},{10... | collective-permute-start | bytes 491528 | tf_op jit(solution)/shard_map/ppermute | solution.py:448
  63.1 9.8 %collective-permute-start.14 = (f32[16,2560]{1,0:T(8,128)S(1)}, f32[16,2560]{1,0:T(8,128)S(1)}, u32[]{:S(2)}, u32[]{:S(2)}) collective-permute-start(f32[16,2560]{1,0:T(8,128)S(1)} %total.1.refs_0_), channel_id=1, source_target_pairs={{0,16},{8,24},{16,0},{24,8},{1,17},{9,25},{17,1},{25,9},{2,18},{10... | collective-permute-start | bytes 491528 | tf_op jit(solution)/shard_map/ppermute | solution.py:448
  64.6 8.3 %collective-permute-start.13 = (f32[16,2560]{1,0:T(8,128)S(1)}, f32[16,2560]{1,0:T(8,128)S(1)}, u32[]{:S(2)}, u32[]{:S(2)}) collective-permute-start(f32[16,2560]{1,0:T(8,128)S(1)} %total.1.refs_0_), channel_id=1, source_target_pairs={{0,8},{8,0},{16,24},{24,16},{1,9},{9,1},{17,25},{25,17},{2,10},{10... | collective-permute-start | bytes 491528 | tf_op jit(solution)/shard_map/ppermute | solution.py:448

commit v18 on v15

--- a/solution.py
+++ b/solution.py
@@ -64,13 +64,21 @@
     return jnp.where(lax.broadcasted_iota(jnp.int32, (width, width), 1) == wanted, 1.0, 0.0).astype(bf16)
 
 
+def at_block(index, size):
+    return pl.ds(pl.multiple_of(index * size, size), size)
+
+
+def repeat(count, body, unroll=1):
+    lax.fori_loop(0, count, lambda i, _: (body(i), None)[1], None, unroll=unroll)
+
+
 def tiles_of(start, count, size):
     return [pl.ds(start + at, size) for at in range(0, count, size)]
 
 
 def forward_kernel(rows_size, dp_size, len_ref, ev_hbm, cot_hbm, win_hbm, wout_hbm,
                    keep_ref, send_ref, hid_ref, dsilu_ref, gatt_ref, gpre_ref, normed_t_ref,
-                   ev_ref, masked_ref, win_ref, inv_ref, normed_ref, user_ref, duser_ref, att_ref, mixed_ref, dval_ref,
+                   ev_ref, masked_ref, win_ref, inv_ref, normed_ref, att_ref, mixed_ref,
                    weights_ref, wout_ref, order_ref, grad_mixed_ref, cot_ref, pre_ref, raw_ref, arrived):
     tokens, width = ev_ref.shape
     copies = [pltpu.make_async_copy(ev_hbm, ev_ref, arrived.at[0])]
@@ -87,85 +95,83 @@
     steps = tokens // STEP
 
     copies[0].wait()
-    for tile in tiles_of(0, tokens, TILE):
+
+    def normalize(t):
+        tile = at_block(t, TILE // 2)
         xhat, _ = standardize(ev_ref[tile, :].astype(f32))
         normed_ref[tile, :] = xhat.astype(bf16)
 
-    def project(i, c):
-        rows = pl.ds(i * STEP, STEP)
-        slot = (c * steps + i) % pre_ref.shape[0]
-        pre_ref[slot] = dot_nn(normed_ref[rows, :], win_ref[:, c * width:(c + 1) * width])
-        for at in range(0, STEP, TILE):
-            tile = pl.ds(i * STEP + at, TILE)
-            pre = pre_ref[slot, at:at + TILE, :]
-            sig = 0.5 + 0.5 * jnp.tanh(0.5 * pre)
-            hid = pre * sig
-            dsilu = sig * (1.0 + (pre - hid))
-            if c == 0:
-                user_ref[tile, :] = hid.astype(bf16)
-                duser_ref[tile, :] = dsilu
-            else:
-                hid_ref[tile, (c - 1) * width:c * width] = hid.astype(bf16)
-                if c == 1:
-                    dval_ref[tile, :] = dsilu
-                else:
-                    dsilu_ref[tile, (c - 2) * width:(c - 1) * width] = dsilu.astype(bf16)
-
-    for c in range(4):
-        copies[1 + c].wait()
+    repeat(tokens // (TILE // 2), normalize, unroll=4)
+
+    def project(c):
+        cols = at_block(c, width)
+        pltpu.make_async_copy(win_hbm.at[:, cols], win_ref.at[:, cols], arrived.at[1 + c]).wait()
         for i in range(steps):
-            project(i, c)
+            pre_ref[i] = dot_nn(normed_ref[pl.ds(i * STEP, STEP), :], win_ref[:, cols])
+            for at in range(0, STEP, TILE):
+                tile = pl.ds(i * STEP + at, TILE)
+                pre = pre_ref[i, at:at + TILE, :]
+                sig = 0.5 + 0.5 * jnp.tanh(0.5 * pre)
+                hid = pre * sig
+                hid_ref[tile, cols] = hid.astype(bf16)
+                dsilu_ref[tile, cols] = (sig * (1.0 + (pre - hid))).astype(bf16)
+
+    repeat(4, project)
 
     for copy in copies[5:]:
         copy.wait()
     length = len_ref[0]
     inv_len = 1.0 / length.astype(f32)
     inv_ref[...] = jnp.full(inv_ref.shape, inv_len, f32)
-    for h in range(HEADS):
-        v_cols = slice(h * hd, (h + 1) * hd)
-        q_cols = slice(width + h * hd, width + (h + 1) * hd)
-        k_cols = slice(2 * width + h * hd, 2 * width + (h + 1) * hd)
+
+    def attend(h):
+        v_cols, q_cols, k_cols = (at_block(part * HEADS + h, hd) for part in (1, 2, 3))
         for i in range(steps):
             rows = pl.ds(i * STEP, STEP)
             for j in range(i + 1):
                 keys = pl.ds(j * STEP, STEP)
-                slot = (h * 3 + i + j) % raw_ref.shape[0]
-                raw_ref[slot] = dot_nt(hid_ref[rows, q_cols], hid_ref[keys, k_cols])
+                raw_ref[i + j] = dot_nt(hid_ref[rows, q_cols], hid_ref[keys, k_cols])
                 for at in range(0, STEP, 2 * TILE):
-                    half = raw_ref[slot, at:at + 2 * TILE, :] * (0.5 * scale)
+                    half = raw_ref[i + j, at:at + 2 * TILE, :] * (0.5 * scale)
                     weights = (half + half * jnp.tanh(half)) * inv_len
                     if i == j:
                         row = at + lax.broadcasted_iota(jnp.int32, weights.shape, 0)
                         weights = jnp.where(row >= lax.broadcasted_iota(jnp.int32, weights.shape, 1), weights, 0.0)
                     weights_ref[h, pl.ds(i * STEP + at, 2 * TILE), keys] = weights.astype(bf16)
             seen = pl.ds(0, (i + 1) * STEP)
-            att_ref[rows, v_cols] = dot_nn(weights_ref[h, rows, seen], hid_ref[seen, v_cols])
-        for i in range(h, steps, HEADS):
-            rows = pl.ds(i * STEP, STEP)
-            normed_t_ref[rows, :] = dot_nt(order_ref[rows, :], normed_ref[...]).astype(bf16)
-        for i in range(h - HEADS // 2, steps, HEADS):
-            if i >= 0:
-                rows = pl.ds(i * STEP, STEP)
-                for tile in tiles_of(i * STEP, STEP, TILE):
-                    masked_ref[tile, :] = masked_rows(cot_ref[tile, :], tile.start, length).astype(bf16)
-                grad_mixed_ref[rows, :] = dot_nt(masked_ref[rows, :], wout_ref[...])
-
-    for tile in tiles_of(0, tokens, TILE // 2):
+            att_ref[rows, at_block(h, hd)] = dot_nn(weights_ref[h, rows, seen], hid_ref[seen, v_cols])
+
+    repeat(HEADS, attend)
+
+    def mask(t):
+        tile = at_block(t, TILE)
+        masked_ref[tile, :] = masked_rows(cot_ref[tile, :], t * TILE, length).astype(bf16)
+
+    repeat(tokens // TILE, mask, unroll=4)
+    normed_t_ref[...] = dot_nt(order_ref[...], normed_ref[...]).astype(bf16)
+    grad_mixed_ref[...] = dot_nt(masked_ref[...], wout_ref[...])
+
+    def gate(t):
+        tile = at_block(t, TILE // 2)
         ahat, inv = standardize(att_ref[tile, :])
-        user = user_ref[tile, :].astype(f32)
+        user = hid_ref[tile, :width].astype(f32)
         mixed_ref[tile, :] = (ahat * user).astype(bf16)
         grad_mixed = grad_mixed_ref[tile, :]
-        gpre_ref[tile, :width] = (grad_mixed * ahat * duser_ref[tile, :]).astype(bf16)
+        gpre_ref[tile, :width] = (grad_mixed * ahat * dsilu_ref[tile, :width].astype(f32)).astype(bf16)
         e = grad_mixed * user
         gatt_ref[tile, :] = (inv * (e - jnp.mean(e, axis=-1, keepdims=True)
                                     - ahat * jnp.mean(e * ahat, axis=-1, keepdims=True))).astype(bf16)
 
-    for h in range(HEADS):
-        v_cols = slice(h * hd, (h + 1) * hd)
+    repeat(tokens // (TILE // 2), gate, unroll=4)
+
+    def value_grads(h):
+        v_cols, out_cols = at_block(h, hd), at_block(HEADS + h, hd)
         for j in range(steps):
             keys, later = pl.ds(j * STEP, STEP), pl.ds(j * STEP, tokens - j * STEP)
             grad_v = dot_tn(weights_ref[h, later, keys], gatt_ref[later, v_cols])
-            gpre_ref[keys, width + h * hd:width + (h + 1) * hd] = (grad_v * dval_ref[keys, v_cols]).astype(bf16)
+            gpre_ref[keys, out_cols] = (grad_v * dsilu_ref[keys, out_cols].astype(f32)).astype(bf16)
+
+    repeat(HEADS, value_grads)
 
     mixed_t = dot_nt(order_ref[...], mixed_ref[...]).astype(bf16)
     half = width // 2
@@ -182,31 +188,30 @@
     steps = tokens // STEP
     factor = inv_ref[:1, :hd] * (0.5 * scale)
 
-    for h in range(HEADS):
-        v_cols = slice(h * hd, (h + 1) * hd)
-        q_cols = slice(width + h * hd, width + (h + 1) * hd)
-        k_cols = slice(2 * width + h * hd, 2 * width + (h + 1) * hd)
+    def attend(h):
+        a_cols, v_cols, q_cols, k_cols = (at_block(part * HEADS + h, hd) for part in range(4))
         for j in range(steps):
             keys = pl.ds(j * STEP, STEP)
             for i in range(j, steps):
                 rows = pl.ds(i * STEP, STEP)
-                slot = (h * 3 + i + j) % raw_ref.shape[0]
-                raw_ref[slot] = dot_nt(hid_ref[keys, k_cols], hid_ref[rows, q_cols])
-                weight_ref[slot] = dot_nt(hid_ref[keys, v_cols], gatt_ref[rows, v_cols])
+                raw_ref[i + j] = dot_nt(hid_ref[keys, k_cols], hid_ref[rows, q_cols])
+                weight_ref[i + j] = dot_nt(hid_ref[keys, v_cols], gatt_ref[rows, a_cols])
                 for at in range(0, STEP, TILE):
-                    half = raw_ref[slot, at:at + TILE, :] * (0.5 * scale)
+                    half = raw_ref[i + j, at:at + TILE, :] * (0.5 * scale)
                     gate = jnp.tanh(half)
-                    gscore = weight_ref[slot, at:at + TILE, :] * ((1.0 + gate) * (1.0 + half * (1.0 - gate)))
+                    gscore = weight_ref[i + j, at:at + TILE, :] * ((1.0 + gate) * (1.0 + half * (1.0 - gate)))
                     if i == j:
                         row = at + lax.broadcasted_iota(jnp.int32, gscore.shape, 0)
                         gscore = jnp.where(row <= lax.broadcasted_iota(jnp.int32, gscore.shape, 1), gscore, 0.0)
-                    score_ref[h % 2, pl.ds(j * STEP + at, TILE), rows] = gscore.astype(bf16)
+                    score_ref[pl.ds(j * STEP + at, TILE), rows] = gscore.astype(bf16)
         for j in range(steps):
             keys, later, seen = pl.ds(j * STEP, STEP), pl.ds(j * STEP, tokens - j * STEP), pl.ds(0, (j + 1) * STEP)
-            grad_k = dot_nn(score_ref[h % 2, keys, later], hid_ref[later, q_cols])
-            gpre_ref[keys, q_cols] = (grad_k * (dsilu_ref[keys, q_cols].astype(f32) * factor)).astype(bf16)
-            grad_q = dot_tn(score_ref[h % 2, seen, keys], hid_ref[seen, k_cols])
-            gpre_ref[keys, v_cols] = (grad_q * (dsilu_ref[keys, v_cols].astype(f32) * factor)).astype(bf16)
+            grad_k = dot_nn(score_ref[keys, later], hid_ref[later, q_cols])
+            gpre_ref[keys, v_cols] = (grad_k * (dsilu_ref[keys, k_cols].astype(f32) * factor)).astype(bf16)
+            grad_q = dot_tn(score_ref[seen, keys], hid_ref[seen, k_cols])
+            gpre_ref[keys, a_cols] = (grad_q * (dsilu_ref[keys, q_cols].astype(f32) * factor)).astype(bf16)
+
+    repeat(HEADS, attend)
 
     half = width // 2
     for ref, start in ((send_ref, half), (keep_ref, 0)):
@@ -228,15 +233,19 @@
     for i in range(tokens // STEP):
         rows = pl.ds(i * STEP, STEP)
         grad_ref[rows, :] = dot_nt(gpre_uv_ref[rows, :], win_ref[:, :2 * width]) + dot_nt(gpre_qk_ref[rows, :], win_ref[:, 2 * width:])
-        for tile in tiles_of(i * STEP, STEP, TILE // 2):
-            xhat, inv = standardize(ev_ref[tile, :].astype(f32))
-            grad_normed = grad_ref[tile, :]
-            grad = masked_ref[tile, :].astype(f32) + inv * (
-                grad_normed - jnp.mean(grad_normed, axis=-1, keepdims=True)
-                - xhat * jnp.mean(grad_normed * xhat, axis=-1, keepdims=True))
-            high = grad.astype(bf16)
-            hi_ref[tile, :] = high
-            lo_ref[tile, :] = (grad - high.astype(f32)).astype(bf16)
+
+    def event_grads(t):
+        tile = at_block(t, TILE // 2)
+        xhat, inv = standardize(ev_ref[tile, :].astype(f32))
+        grad_normed = grad_ref[tile, :]
+        grad = masked_ref[tile, :].astype(f32) + inv * (
+            grad_normed - jnp.mean(grad_normed, axis=-1, keepdims=True)
+            - xhat * jnp.mean(grad_normed * xhat, axis=-1, keepdims=True))
+        high = grad.astype(bf16)
+        hi_ref[tile, :] = high
+        lo_ref[tile, :] = (grad - high.astype(f32)).astype(bf16)
+
+    repeat(tokens // (TILE // 2), event_grads, unroll=4)
 
     slots = rows_ref.shape[0]
     owner, place = slots_in_order(lax.broadcasted_iota(jnp.int32, (slots, 1), 0), capacity, dp_size, rows_size)
@@ -441,8 +450,8 @@
     keep1, send1, hid, dsilu, gatt, gpre_uv, normed_t, events, masked, w_in, inv_len = call(
         functools.partial(forward_kernel, rows_size, dp_size), "forward_part",
         sides(3 * width) + [
-            local(tokens, 3 * width, dtype=bf16),
-            local(tokens, 2 * width, dtype=bf16),
+            local(tokens, 4 * width, dtype=bf16),
+            local(tokens, 4 * width, dtype=bf16),
             local(tokens, width, dtype=bf16),
             local(tokens, 2 * width, dtype=bf16),
             local(width, tokens, dtype=bf16),
@@ -452,15 +461,14 @@
             local(8, LANES),
         ],
         (lengths, events, cotangent, w_in, w_out),
-        [((tokens, width), bf16), ((tokens, width), bf16), ((tokens, width), f32), ((tokens, width), f32),
-         ((tokens, width), bf16), ((tokens, width), f32), ((HEADS, tokens, tokens), bf16),
+        [((tokens, width), bf16), ((tokens, width), f32), ((tokens, width), bf16), ((HEADS, tokens, tokens), bf16),
          (w_out.shape, bf16), ((width, width), bf16), ((tokens, width), f32), ((tokens, width), bf16),
          ((4, STEP, width), f32), ((4, STEP, STEP), f32)], far=5, long=True, grant=22)
     recv1 = lax.ppermute(send1, "rows", cores)
     keep2, send2, gpre_qk = call(
         attention_kernel, "attention_part", sides(2 * width) + [local(tokens, 2 * width, dtype=bf16)],
         (inv_len, hid, dsilu, gatt, normed_t),
-        [((4, STEP, STEP), f32), ((4, STEP, STEP), f32), ((2, tokens, tokens), bf16)], long=True, grant=12)
+        [((4, STEP, STEP), f32), ((4, STEP, STEP), f32), ((tokens, tokens), bf16)], long=True, grant=12)
     recv2 = lax.ppermute(send2, "rows", cores)
     block = capacity * (width // LANES)
     gpre_uv = after(gpre_uv, recv1)

time: 74 us -> 82 us (1.11)
  Pallas kernels: 16.8 us -> 25.1 us
    pallas_call x13, Pallas kernels: 16.8 us -> 25.1 us  [call(): pl.pallas_call(kernel, name=name, in_specs=[pl.BlockSpec(memory_space=p)...]
  transfers between devices with their start and end apart: 20 -> 20, of which waited for: 12 -> 11; matrix products, arithmetic and copies ran while one was open for 0% -> 0% of each run, Pallas kernels for 10% -> 13%
where the time goes in v18:
time: 82 us; the launch traced here: 81.8 us
  waiting for transfers between devices  30.5 us (37%)
  Pallas kernels  25.1 us (31%)
  starting transfers between devices  24.7 us (30%)
  between operations  1.42 us (2%)
    pallas_call x13, Pallas kernels, call(): pl.pallas_call(kernel, name=name, in_specs=[pl.BlockSpec(memory_space=p)...  25.1 us
    ppermute x10, waiting for transfers between devices, body(): lax.ppermute(v, 'dp', [(i, i ^ bit) for i in range(dp_size)])  17.6 us
    ppermute x10, starting transfers between devices, body(): lax.ppermute(v, 'dp', [(i, i ^ bit) for i in range(dp_size)])  13.7 us
    ppermute x4, waiting for transfers between devices, body(): lax.ppermute(v, 'rows', [(i, i ^ 2 << bit) for i in range(rows_size)])  8.86 us
    ppermute x3, starting transfers between devices, body(): lax.ppermute(v, 'rows', [(i, (i + 2 * k) % rows_size) for i in range(rows...  5.52 us
    ppermute x4, starting transfers between devices, body(): lax.ppermute(v, 'rows', [(i, i ^ 2 << bit) for i in range(rows_size)])  4.81 us
    ppermute x3, waiting for transfers between devices, body(): lax.ppermute(v, 'rows', [(i, (i + 2 * k) % rows_size) for i in range(rows...  4.05 us
  transfers between devices with their start and end apart: 20, of which 11 were waited for; matrix products, arithmetic and copies ran while one was open for 0% of the time, Pallas kernels for 13%

profile of v18, /device:TPU:0, one launch (start us, length us, event | category | flops | bytes accessed | tf_op | source)
XLA Modules:
  0.0 81.8 jit_solution(17718620094986214924)
XLA Ops:
  1.3 13.1 %forward_part.1 = (f32[256,1536]{1,0:T(8,128)S(1)}, f32[256,1536]{1,0:T(8,128)S(1)}, bf16[512,2048]{1,0:T(8,128)(2,1)S(1)}, bf16[512,2048]{1,0:T(8,128)(2,1)S(1)...) custom-call(s32[1]{0:T(128)S(6)} %copy.13.len_ref, ...), custom_call_target="tpu_custom_call" | custom-call | flops 99999997952 | bytes 65536 | tf_op jit(solution)/shard_map/forward_part/pallas_call | solution.py:420
  14.4 0.5 collective-permute-start
  14.9 0.0 copy-start.1
  14.9 0.0 copy-start.2
  14.9 3.5 %attention_part.1 = (f32[256,1024]{1,0:T(8,128)S(1)}, f32[256,1024]{1,0:T(8,128)S(1)}, bf16[512,1024]{1,0:T(8,128)(2,1)S(1)}) custom-call(f32[8,128]{1,0:T(8,128)S(1)} %get-tuple-element.62.inv_ref, bf16[512,2048]{1,0:T(8,128)(2,1)S(1)} %get-tuple-element.63.hid_ref, bf16[512,2048]{1,0:T(8,128)(2,1)S(1)} %get-tuple-element.64.dsilu_ref, ...), custom_call_target="tpu_custom_call" | custom-call | flops 99999997952 | bytes 65536 | tf_op jit(solution)/shard_map/attention_part/pallas_call | solution.py:420
  18.4 0.1 collective-permute-start.1
  18.5 0.0 collective-permute-done
  18.5 0.0 copy-done.1
  18.5 0.0 copy-done.2
  18.5 4.4 %events_part.1 = (f32[520,128]{1,0:T(8,128)S(1)}, f32[520,128]{1,0:T(8,128)S(1)}, f32[520,128]{1,0:T(8,128)S(1)}, f32[520,128]{1,0:T(8,128)S(1)}) custom-call(bf16[512,512]{1,0:T(8,128)(2,1)S(1)} %get-tuple-element.56.ev_ref, bf16[512,512]{1,0:T(8,128)(2,1)S(1)} %get-tuple-element.57.masked_ref, bf16[512,2048]{1,0:T(8,128)(2,1)S(1)} %get-tuple-element.58.win_ref, ...), custom_call_target="tpu_custom_call" | custom-call | flops 99999997952 | bytes 65536 | tf_op jit(solution)/shard_map/events_part/pallas_call | solution.py:420
  22.9 0.0 collective-permute-done.1
  22.9 0.3 first_sums.1
  23.2 3.0 %collective-permute-start.2 = (f32[2,64,1280]{2,1,0:T(8,128)S(1)}, f32[2,64,1280]{2,1,0:T(8,128)S(1)}, u32[]{:S(2)}, u32[]{:S(2)}) collective-permute-start(f32[2,64,1280]{2,1,0:T(8,128)S(1)} %get-tuple-element.76), channel_id=1, source_target_pairs={{0,8},{8,0},{16,24},{24,16},{1,9},{9,1},{17,25},{25,17},{2,10},{10... | collective-permute-start | bytes 1966088 | tf_op jit(solution)/shard_map/ppermute | solution.py:439
  26.3 1.5 %collective-permute-start.3 = (f32[2,64,1280]{2,1,0:T(8,128)S(1)}, f32[2,64,1280]{2,1,0:T(8,128)S(1)}, u32[]{:S(2)}, u32[]{:S(2)}) collective-permute-start(f32[2,64,1280]{2,1,0:T(8,128)S(1)} %get-tuple-element.78), channel_id=1, source_target_pairs={{0,16},{8,24},{16,0},{24,8},{1,17},{9,25},{17,1},{25,9},{2,18},{10... | collective-permute-start | bytes 1966088 | tf_op jit(solution)/shard_map/ppermute | solution.py:439
  27.8 1.6 %collective-permute-start.4 = (f32[520,128]{1,0:T(8,128)S(1)}, f32[520,128]{1,0:T(8,128)S(1)}, u32[]{:S(2)}, u32[]{:S(2)}) collective-permute-start(f32[520,128]{1,0:T(8,128)S(1)} %get-tuple-element.69), channel_id=1, source_target_pairs={{0,2},{1,3},{2,4},{3,5},{4,6},{5,7},{6,0},{7,1},{8,10},{9,11},{10,... | collective-permute-start | bytes 798728 | tf_op jit(solution)/shard_map/ppermute | solution.py:481
  29.3 2.6 %collective-permute-start.5 = (f32[520,128]{1,0:T(8,128)S(1)}, f32[520,128]{1,0:T(8,128)S(1)}, u32[]{:S(2)}, u32[]{:S(2)}) collective-permute-start(f32[520,128]{1,0:T(8,128)S(1)} %get-tuple-element.70), channel_id=1, source_target_pairs={{0,4},{1,5},{2,6},{3,7},{4,0},{5,1},{6,2},{7,3},{8,12},{9,13},{10,... | collective-permute-start | bytes 798728 | tf_op jit(solution)/shard_map/ppermute | solution.py:481
  31.9 1.3 %collective-permute-start.6 = (f32[520,128]{1,0:T(8,128)S(1)}, f32[520,128]{1,0:T(8,128)S(1)}, u32[]{:S(2)}, u32[]{:S(2)}) collective-permute-start(f32[520,128]{1,0:T(8,128)S(1)} %get-tuple-element.71), channel_id=1, source_target_pairs={{0,6},{1,7},{2,0},{3,1},{4,2},{5,3},{6,4},{7,5},{8,14},{9,15},{10,... | collective-permute-start | bytes 798728 | tf_op jit(solution)/shard_map/ppermute | solution.py:481
  33.3 7.9 %collective-permute-done.2.from_x_ref = f32[2,64,1280]{2,1,0:T(8,128)S(1)} collective-permute-done((f32[2,64,1280]{2,1,0:T(8,128)S(1)}, f32[2,64,1280]{2,1,0:T(8,128)S(1)}, u32[]{:S(2)}, u32[]{:S(2)}) %collective-permute-start.2) | collective-permute-done | bytes 655392 | tf_op jit(solution)/shard_map/ppermute | solution.py:439
  41.2 1.5 %collective-permute-done.3.from_y_ref = f32[2,64,1280]{2,1,0:T(8,128)S(1)} collective-permute-done((f32[2,64,1280]{2,1,0:T(8,128)S(1)}, f32[2,64,1280]{2,1,0:T(8,128)S(1)}, u32[]{:S(2)}, u32[]{:S(2)}) %collective-permute-start.3) | collective-permute-done | bytes 655392 | tf_op jit(solution)/shard_map/ppermute | solution.py:439
  42.6 0.1 second_sums.1
  42.8 1.6 %collective-permute-start.7 = (f32[64,1280]{1,0:T(8,128)S(1)}, f32[64,1280]{1,0:T(8,128)S(1)}, u32[]{:S(2)}, u32[]{:S(2)}) collective-permute-start(f32[64,1280]{1,0:T(8,128)S(1)} %get-tuple-element.80), channel_id=1, source_target_pairs={{0,16},{8,24},{16,0},{24,8},{1,17},{9,25},{17,1},{25,9},{2,18},{10... | collective-permute-start | bytes 983048 | tf_op jit(solution)/shard_map/ppermute | solution.py:439
  44.4 0.5 collective-permute-start.8
  44.9 0.0 collective-permute-done.4.refs_1_
  44.9 4.0 %collective-permute-done.5.refs_2_ = f32[520,128]{1,0:T(8,128)S(1)} collective-permute-done((f32[520,128]{1,0:T(8,128)S(1)}, f32[520,128]{1,0:T(8,128)S(1)}, u32[]{:S(2)}, u32[]{:S(2)}) %collective-permute-start.5) | collective-permute-done | bytes 266272 | tf_op jit(solution)/shard_map/ppermute | solution.py:481
  49.0 0.0 collective-permute-done.6.refs_3_
  49.0 0.1 by_part.1
  49.0 2.3 %collective-permute-done.7 = f32[64,1280]{1,0:T(8,128)S(1)} collective-permute-done((f32[64,1280]{1,0:T(8,128)S(1)}, f32[64,1280]{1,0:T(8,128)S(1)}, u32[]{:S(2)}, u32[]{:S(2)}) %collective-permute-start.7) | collective-permute-done | bytes 327712 | tf_op jit(solution)/shard_map/ppermute | solution.py:439
  51.3 1.2 %collective-permute-done.8 = f32[64,1280]{1,0:T(8,128)S(1)} collective-permute-done((f32[64,1280]{1,0:T(8,128)S(1)}, f32[64,1280]{1,0:T(8,128)S(1)}, u32[]{:S(2)}, u32[]{:S(2)}) %collective-permute-start.8) | collective-permute-done | bytes 327712 | tf_op jit(solution)/shard_map/ppermute | solution.py:439
  52.6 0.1 chip_sums.3
  52.7 2.7 %collective-permute-start.9 = (f32[2,16,1280]{2,1,0:T(8,128)S(1)}, f32[2,16,1280]{2,1,0:T(8,128)S(1)}, u32[]{:S(2)}, u32[]{:S(2)}) collective-permute-start(f32[2,16,1280]{2,1,0:T(8,128)S(1)} %get-tuple-element.90), channel_id=1, source_target_pairs={{0,2},{1,3},{2,0},{3,1},{4,6},{5,7},{6,4},{7,5},{8,10},{9,11},{10,... | collective-permute-start | bytes 491528 | tf_op jit(solution)/shard_map/ppermute | solution.py:498
  55.4 0.1 collective-permute-start.11
  55.5 0.5 collective-permute-start.16
  56.0 0.5 collective-permute-start.17
  56.5 2.4 %collective-permute-start.18 = (f32[520,128]{1,0:T(8,128)S(1)}, f32[520,128]{1,0:T(8,128)S(1)}, u32[]{:S(2)}, u32[]{:S(2)}) collective-permute-start(f32[520,128]{1,0:T(8,128)S(1)} %get-tuple-element.86), channel_id=1, source_target_pairs={{0,24},{8,16},{16,8},{24,0},{1,25},{9,17},{17,9},{25,1},{2,26},{10... | collective-permute-start | bytes 798728 | tf_op jit(solution)/shard_map/ppermute | solution.py:439
  59.0 1.4 %collective-permute-done.9.recv_in = f32[2,16,1280]{2,1,0:T(8,128)S(1)} collective-permute-done((f32[2,16,1280]{2,1,0:T(8,128)S(1)}, f32[2,16,1280]{2,1,0:T(8,128)S(1)}, u32[]{:S(2)}, u32[]{:S(2)}) %collective-permute-start.9) | collective-permute-done | bytes 163872 | tf_op jit(solution)/shard_map/ppermute | solution.py:498
  60.4 1.9 %collective-permute-start.10 = (f32[1,16,1280]{2,1,0:T(8,128)S(1)}, f32[1,16,1280]{2,1,0:T(8,128)S(1)}, u32[]{:S(2)}, u32[]{:S(2)}) collective-permute-start(f32[1,16,1280]{2,1,0:T(8,128)S(1)} %get-tuple-element.92), channel_id=1, source_target_pairs={{0,4},{1,5},{2,6},{3,7},{4,0},{5,1},{6,2},{7,3},{8,12},{9,13},{10,... | collective-permute-start | bytes 245768 | tf_op jit(solution)/shard_map/ppermute | solution.py:498
  62.3 1.8 %collective-permute-done.11.recv_in = f32[2,16,1280]{2,1,0:T(8,128)S(1)} collective-permute-done((f32[2,16,1280]{2,1,0:T(8,128)S(1)}, f32[2,16,1280]{2,1,0:T(8,128)S(1)}, u32[]{:S(2)}, u32[]{:S(2)}) %collective-permute-start.11) | collective-permute-done | bytes 163872 | tf_op jit(solution)/shard_map/ppermute | solution.py:498
  64.2 0.1 collective-permute-start.12
  64.3 1.6 %collective-permute-done.10.recv_a_ref = f32[1,16,1280]{2,1,0:T(8,128)S(1)} collective-permute-done((f32[1,16,1280]{2,1,0:T(8,128)S(1)}, f32[1,16,1280]{2,1,0:T(8,128)S(1)}, u32[]{:S(2)}, u32[]{:S(2)}) %collective-permute-start.10) | collective-permute-done | bytes 81952 | tf_op jit(solution)/shard_map/ppermute | solution.py:498
  65.8 4.0 %collective-permute-done.12.recv_b_ref = f32[1,16,1280]{2,1,0:T(8,128)S(1)} collective-permute-done((f32[1,16,1280]{2,1,0:T(8,128)S(1)}, f32[1,16,1280]{2,1,0:T(8,128)S(1)}, u32[]{:S(2)}, u32[]{:S(2)}) %collective-permute-start.12) | collective-permute-done | bytes 81952 | tf_op jit(solution)/shard_map/ppermute | solution.py:498
  69.9 0.0 copy-start
  69.9 0.0 copy-start.3
  69.9 0.0 collective-permute-done.16.refs_1_
  69.9 0.0 collective-permute-done.17.refs_2_
  69.9 0.0 collective-permute-done.18.refs_3_
  70.0 0.1 by_core.1
  70.0 0.1 collective-permute-start.19
  70.1 1.0 %collective-permute-start.15 = (f32[16,2560]{1,0:T(8,128)S(1)}, f32[16,2560]{1,0:T(8,128)S(1)}, u32[]{:S(2)}, u32[]{:S(2)}) collective-permute-start(f32[16,2560]{1,0:T(8,128)S(1)} %total.1.refs_0_), channel_id=1, source_target_pairs={{0,24},{8,16},{16,8},{24,0},{1,25},{9,17},{17,9},{25,1},{2,26},{10... | collective-permute-start | bytes 491528 | tf_op jit(solution)/shard_map/ppermute | solution.py:439
  71.1 1.5 %collective-permute-start.14 = (f32[16,2560]{1,0:T(8,128)S(1)}, f32[16,2560]{1,0:T(8,128)S(1)}, u32[]{:S(2)}, u32[]{:S(2)}) collective-permute-start(f32[16,2560]{1,0:T(8,128)S(1)} %total.1.refs_0_), channel_id=1, source_target_pairs={{0,16},{8,24},{16,0},{24,8},{1,17},{9,25},{17,1},{25,9},{2,18},{10... | collective-permute-start | bytes 491528 | tf_op jit(solution)/shard_map/ppermute | solution.py:439
  72.6 1.0 %collective-permute-start.13 = (f32[16,2560]{1,0:T(8,128)S(1)}, f32[16,2560]{1,0:T(8,128)S(1)}, u32[]{:S(2)}, u32[]{:S(2)}) collective-permute-start(f32[16,2560]{1,0:T(8,128)S(1)} %total.1.refs_0_), channel_id=1, source_target_pairs={{0,8},{8,0},{16,24},{24,16},{1,9},{9,1},{17,25},{25,17},{2,10},{10... | collective-permute-start | bytes 491528 | tf_op jit(solution)/shard_map/ppermute | solution.py:439
  73.7 0.0 collective-permute-done.19.recv_ref
  73.7 0.0 copy-done
  73.7 0.0 copy-done.3
  73.7 2.5 %table_part.1 = (f32[512,512]{1,0:T(8,128)}, f32[512]{0:T(512)}) custom-call(f32[1056,128]{1,0:T(8,128)S(1)} %get-tuple-element.99.keep_ref, f32[1056,128]{1,0:T(8,128)S(1)} %collective-permute-done.19.recv_ref, f32[512,512]{1,0:T(8,128)S(1)} %copy-done, f32[512]{0:T(512)S(1)} %copy-done.3), custom_call_target="tpu_custom_call" | custom-call | flops 1000000000 | bytes 65536 | tf_op jit(solution)/shard_map/table_part/pallas_call | solution.py:420
  76.2 2.0 %collective-permute-done.15.refs_3_ = f32[16,2560]{1,0:T(8,128)S(1)} collective-permute-done((f32[16,2560]{1,0:T(8,128)S(1)}, f32[16,2560]{1,0:T(8,128)S(1)}, u32[]{:S(2)}, u32[]{:S(2)}) %collective-permute-start.15) | collective-permute-done | bytes 163872 | tf_op jit(solution)/shard_map/ppermute | solution.py:439
  78.1 2.8 %collective-permute-done.14.refs_2_ = f32[16,2560]{1,0:T(8,128)S(1)} collective-permute-done((f32[16,2560]{1,0:T(8,128)S(1)}, f32[16,2560]{1,0:T(8,128)S(1)}, u32[]{:S(2)}, u32[]{:S(2)}) %collective-permute-start.14) | collective-permute-done | bytes 163872 | tf_op jit(solution)/shard_map/ppermute | solution.py:439
  80.9 0.0 collective-permute-done.13.refs_1_
  80.9 0.9 %gather.1 = (f32[4,16,2048]{2,1,0:T(8,128)}, f32[4,16,512]{2,1,0:T(8,128)}) custom-call(f32[16,2560]{1,0:T(8,128)S(1)} %total.1.refs_0_, f32[16,2560]{1,0:T(8,128)S(1)} %collective-permute-done.13.refs_1_, f32[16,2560]{1,0:T(8,128)S(1)} %collective-permute-done.14.refs_2_, f32[16,2560]{1,0:T(8,128)S(1)} %collective-permute-done.15.refs_3_), custom_call_target="tpu_custom_call" | custom-call | flops 1000000000 | bytes 65536 | tf_op jit(solution)/shard_map/gather/pallas_call | solution.py:420
  (3 shorter events, 0.1 us)
Async XLA Ops:
  14.4 4.1 %collective-permute-start = (f32[256,1536]{1,0:T(8,128)S(1)}, f32[256,1536]{1,0:T(8,128)S(1)}, u32[]{:S(2)}, u32[]{:S(2)}) collective-permute-start(f32[256,1536]{1,0:T(8,128)S(1)} %get-tuple-element.60), channel_id=1, source_target_pairs={{0,1},{1,0},{2,3},{3,2},{4,5},{5,4},{6,7},{7,6},{8,9},{9,8},{10,11... | collective-permute-start | bytes 4718600 | tf_op jit(solution)/shard_map/ppermute | solution.py:467
  14.9 3.6 %copy-start.1 = (s32[1,32,16]{1,2,0:T(8,128)S(1)}, s32[1,32,16]{1,2,0:T(8,128)}, u32[]{:S(2)}) copy-start(s32[1,32,16]{1,2,0:T(8,128)} %param.14) | copy-start | bytes 6148
  14.9 3.6 %copy-start.2 = (s32[1,512]{1,0:T(1,128)S(1)}, s32[1,512]{1,0:T(1,128)}, u32[]{:S(2)}) copy-start(s32[1,512]{1,0:T(1,128)} %slot_ref.1) | copy-start | bytes 6148
  18.4 4.5 %collective-permute-start.1 = (f32[256,1024]{1,0:T(8,128)S(1)}, f32[256,1024]{1,0:T(8,128)S(1)}, u32[]{:S(2)}, u32[]{:S(2)}) collective-permute-start(f32[256,1024]{1,0:T(8,128)S(1)} %get-tuple-element.74), channel_id=1, source_target_pairs={{0,1},{1,0},{2,3},{3,2},{4,5},{5,4},{6,7},{7,6},{8,9},{9,8},{10,11... | collective-permute-start | bytes 3145736 | tf_op jit(solution)/shard_map/ppermute | solution.py:472
  23.2 17.9 %collective-permute-start.2 = (f32[2,64,1280]{2,1,0:T(8,128)S(1)}, f32[2,64,1280]{2,1,0:T(8,128)S(1)}, u32[]{:S(2)}, u32[]{:S(2)}) collective-permute-start(f32[2,64,1280]{2,1,0:T(8,128)S(1)} %get-tuple-element.76), channel_id=1, source_target_pairs={{0,8},{8,0},{16,24},{24,16},{1,9},{9,1},{17,25},{25,17},{2,10},{10... | collective-permute-start | bytes 1966088 | tf_op jit(solution)/shard_map/ppermute | solution.py:439
  26.3 16.4 %collective-permute-start.3 = (f32[2,64,1280]{2,1,0:T(8,128)S(1)}, f32[2,64,1280]{2,1,0:T(8,128)S(1)}, u32[]{:S(2)}, u32[]{:S(2)}) collective-permute-start(f32[2,64,1280]{2,1,0:T(8,128)S(1)} %get-tuple-element.78), channel_id=1, source_target_pairs={{0,16},{8,24},{16,0},{24,8},{1,17},{9,25},{17,1},{25,9},{2,18},{10... | collective-permute-start | bytes 1966088 | tf_op jit(solution)/shard_map/ppermute | solution.py:439
  27.8 17.1 %collective-permute-start.4 = (f32[520,128]{1,0:T(8,128)S(1)}, f32[520,128]{1,0:T(8,128)S(1)}, u32[]{:S(2)}, u32[]{:S(2)}) collective-permute-start(f32[520,128]{1,0:T(8,128)S(1)} %get-tuple-element.69), channel_id=1, source_target_pairs={{0,2},{1,3},{2,4},{3,5},{4,6},{5,7},{6,0},{7,1},{8,10},{9,11},{10,... | collective-permute-start | bytes 798728 | tf_op jit(solution)/shard_map/ppermute | solution.py:481
  29.3 19.6 %collective-permute-start.5 = (f32[520,128]{1,0:T(8,128)S(1)}, f32[520,128]{1,0:T(8,128)S(1)}, u32[]{:S(2)}, u32[]{:S(2)}) collective-permute-start(f32[520,128]{1,0:T(8,128)S(1)} %get-tuple-element.70), channel_id=1, source_target_pairs={{0,4},{1,5},{2,6},{3,7},{4,0},{5,1},{6,2},{7,3},{8,12},{9,13},{10,... | collective-permute-start | bytes 798728 | tf_op jit(solution)/shard_map/ppermute | solution.py:481
  31.9 17.0 %collective-permute-start.6 = (f32[520,128]{1,0:T(8,128)S(1)}, f32[520,128]{1,0:T(8,128)S(1)}, u32[]{:S(2)}, u32[]{:S(2)}) collective-permute-start(f32[520,128]{1,0:T(8,128)S(1)} %get-tuple-element.71), channel_id=1, source_target_pairs={{0,6},{1,7},{2,0},{3,1},{4,2},{5,3},{6,4},{7,5},{8,14},{9,15},{10,... | collective-permute-start | bytes 798728 | tf_op jit(solution)/shard_map/ppermute | solution.py:481
  42.8 8.6 %collective-permute-start.7 = (f32[64,1280]{1,0:T(8,128)S(1)}, f32[64,1280]{1,0:T(8,128)S(1)}, u32[]{:S(2)}, u32[]{:S(2)}) collective-permute-start(f32[64,1280]{1,0:T(8,128)S(1)} %get-tuple-element.80), channel_id=1, source_target_pairs={{0,16},{8,24},{16,0},{24,8},{1,17},{9,25},{17,1},{25,9},{2,18},{10... | collective-permute-start | bytes 983048 | tf_op jit(solution)/shard_map/ppermute | solution.py:439
  44.4 8.2 %collective-permute-start.8 = (f32[64,1280]{1,0:T(8,128)S(1)}, f32[64,1280]{1,0:T(8,128)S(1)}, u32[]{:S(2)}, u32[]{:S(2)}) collective-permute-start(f32[64,1280]{1,0:T(8,128)S(1)} %get-tuple-element.81), channel_id=1, source_target_pairs={{0,8},{8,0},{16,24},{24,16},{1,9},{9,1},{17,25},{25,17},{2,10},{10... | collective-permute-start | bytes 983048 | tf_op jit(solution)/shard_map/ppermute | solution.py:439
  52.7 7.7 %collective-permute-start.9 = (f32[2,16,1280]{2,1,0:T(8,128)S(1)}, f32[2,16,1280]{2,1,0:T(8,128)S(1)}, u32[]{:S(2)}, u32[]{:S(2)}) collective-permute-start(f32[2,16,1280]{2,1,0:T(8,128)S(1)} %get-tuple-element.90), channel_id=1, source_target_pairs={{0,2},{1,3},{2,0},{3,1},{4,6},{5,7},{6,4},{7,5},{8,10},{9,11},{10,... | collective-permute-start | bytes 491528 | tf_op jit(solution)/shard_map/ppermute | solution.py:498
  55.4 8.8 %collective-permute-start.11 = (f32[2,16,1280]{2,1,0:T(8,128)S(1)}, f32[2,16,1280]{2,1,0:T(8,128)S(1)}, u32[]{:S(2)}, u32[]{:S(2)}) collective-permute-start(f32[2,16,1280]{2,1,0:T(8,128)S(1)} %get-tuple-element.95), channel_id=1, source_target_pairs={{0,2},{1,3},{2,0},{3,1},{4,6},{5,7},{6,4},{7,5},{8,10},{9,11},{10,... | collective-permute-start | bytes 491528 | tf_op jit(solution)/shard_map/ppermute | solution.py:498
  55.5 14.4 %collective-permute-start.16 = (f32[520,128]{1,0:T(8,128)S(1)}, f32[520,128]{1,0:T(8,128)S(1)}, u32[]{:S(2)}, u32[]{:S(2)}) collective-permute-start(f32[520,128]{1,0:T(8,128)S(1)} %get-tuple-element.84), channel_id=1, source_target_pairs={{0,8},{8,0},{16,24},{24,16},{1,9},{9,1},{17,25},{25,17},{2,10},{10... | collective-permute-start | bytes 798728 | tf_op jit(solution)/shard_map/ppermute | solution.py:439
  56.0 13.9 %collective-permute-start.17 = (f32[520,128]{1,0:T(8,128)S(1)}, f32[520,128]{1,0:T(8,128)S(1)}, u32[]{:S(2)}, u32[]{:S(2)}) collective-permute-start(f32[520,128]{1,0:T(8,128)S(1)} %get-tuple-element.85), channel_id=1, source_target_pairs={{0,16},{8,24},{16,0},{24,8},{1,17},{9,25},{17,1},{25,9},{2,18},{10... | collective-permute-start | bytes 798728 | tf_op jit(solution)/shard_map/ppermute | solution.py:439
  56.5 13.4 %collective-permute-start.18 = (f32[520,128]{1,0:T(8,128)S(1)}, f32[520,128]{1,0:T(8,128)S(1)}, u32[]{:S(2)}, u32[]{:S(2)}) collective-permute-start(f32[520,128]{1,0:T(8,128)S(1)} %get-tuple-element.86), channel_id=1, source_target_pairs={{0,24},{8,16},{16,8},{24,0},{1,25},{9,17},{17,9},{25,1},{2,26},{10... | collective-permute-start | bytes 798728 | tf_op jit(solution)/shard_map/ppermute | solution.py:439
  60.4 5.4 %collective-permute-start.10 = (f32[1,16,1280]{2,1,0:T(8,128)S(1)}, f32[1,16,1280]{2,1,0:T(8,128)S(1)}, u32[]{:S(2)}, u32[]{:S(2)}) collective-permute-start(f32[1,16,1280]{2,1,0:T(8,128)S(1)} %get-tuple-element.92), channel_id=1, source_target_pairs={{0,4},{1,5},{2,6},{3,7},{4,0},{5,1},{6,2},{7,3},{8,12},{9,13},{10,... | collective-permute-start | bytes 245768 | tf_op jit(solution)/shard_map/ppermute | solution.py:498
  64.2 5.7 %collective-permute-start.12 = (f32[1,16,1280]{2,1,0:T(8,128)S(1)}, f32[1,16,1280]{2,1,0:T(8,128)S(1)}, u32[]{:S(2)}, u32[]{:S(2)}) collective-permute-start(f32[1,16,1280]{2,1,0:T(8,128)S(1)} %get-tuple-element.97), channel_id=1, source_target_pairs={{0,4},{1,5},{2,6},{3,7},{4,0},{5,1},{6,2},{7,3},{8,12},{9,13},{10,... | collective-permute-start | bytes 245768 | tf_op jit(solution)/shard_map/ppermute | solution.py:498
  69.9 3.8 %copy-start = (f32[512,512]{1,0:T(8,128)S(1)}, f32[512,512]{1,0:T(8,128)}, u32[]{:S(2)}) copy-start(f32[512,512]{1,0:T(8,128)} %table_ref.1) | copy-start | bytes 3145732
  69.9 3.8 %copy-start.3 = (f32[512]{0:T(512)S(1)}, f32[512]{0:T(512)}, u32[]{:S(2)}) copy-start(f32[512]{0:T(512)} %accum_ref.1) | copy-start | bytes 6148
  70.0 3.6 %collective-permute-start.19 = (f32[1056,128]{1,0:T(8,128)S(1)}, f32[1056,128]{1,0:T(8,128)S(1)}, u32[]{:S(2)}, u32[]{:S(2)}) collective-permute-start(f32[1056,128]{1,0:T(8,128)S(1)} %get-tuple-element.100), channel_id=1, source_target_pairs={{0,1},{1,0},{2,3},{3,2},{4,5},{5,4},{6,7},{7,6},{8,9},{9,8},{10,11... | collective-permute-start | bytes 1622024 | tf_op jit(solution)/shard_map/ppermute | solution.py:519
  70.1 8.0 %collective-permute-start.15 = (f32[16,2560]{1,0:T(8,128)S(1)}, f32[16,2560]{1,0:T(8,128)S(1)}, u32[]{:S(2)}, u32[]{:S(2)}) collective-permute-start(f32[16,2560]{1,0:T(8,128)S(1)} %total.1.refs_0_), channel_id=1, source_target_pairs={{0,24},{8,16},{16,8},{24,0},{1,25},{9,17},{17,9},{25,1},{2,26},{10... | collective-permute-start | bytes 491528 | tf_op jit(solution)/shard_map/ppermute | solution.py:439
  71.1 9.8 %collective-permute-start.14 = (f32[16,2560]{1,0:T(8,128)S(1)}, f32[16,2560]{1,0:T(8,128)S(1)}, u32[]{:S(2)}, u32[]{:S(2)}) collective-permute-start(f32[16,2560]{1,0:T(8,128)S(1)} %total.1.refs_0_), channel_id=1, source_target_pairs={{0,16},{8,24},{16,0},{24,8},{1,17},{9,25},{17,1},{25,9},{2,18},{10... | collective-permute-start | bytes 491528 | tf_op jit(solution)/shard_map/ppermute | solution.py:439
  72.6 8.3 %collective-permute-start.13 = (f32[16,2560]{1,0:T(8,128)S(1)}, f32[16,2560]{1,0:T(8,128)S(1)}, u32[]{:S(2)}, u32[]{:S(2)}) collective-permute-start(f32[16,2560]{1,0:T(8,128)S(1)} %total.1.refs_0_), channel_id=1, source_target_pairs={{0,8},{8,0},{16,24},{24,16},{1,9},{9,1},{17,25},{25,17},{2,10},{10... | collective-permute-start | bytes 491528 | tf_op jit(solution)/shard_map/ppermute | solution.py:439

commit v19 on v15

--- a/solution.py
+++ b/solution.py
@@ -501,13 +501,14 @@
                 functools.partial(chip_kernel, bit), "chip_sums", [local(chips >> (bit + 1), piece, cols // 2)] * 2,
                 halves[i], long=False)
             halves[i] = [keep, over_chips(send, bit)]
-    (total,) = call(
-        functools.partial(total_kernel, tokens), "total", [local(piece, cols)], halves[0] + halves[1], long=False)
-    pieces = gathered(total)
-    parts[0] = after(parts[0], total)
+    parts[0] = after(parts[0], halves[1][0])
     keep, send = call(
         functools.partial(by_core_kernel, chips, block), "by_core",
-        [local(dp_size * (chips * block + id_rows(chips)), LANES)] * 2, parts, long=False)
+        [local(dp_size * (chips * block + id_rows(chips)), LANES)] * 2, parts, long=True)
+    halves[1][0] = after(halves[1][0], keep, send)
+    (total,) = call(
+        functools.partial(total_kernel, tokens), "total", [local(piece, cols)], halves[0] + halves[1], long=True)
+    pieces = gathered(total)
     recv = lax.ppermute(send, "rows", cores)
     slots = owners * capacity
     table_new, accum_new = call(

time: 74 us -> 73.8 us (level)
  no operation moved by 1% of the time
where the time goes in v19:
time: 73.8 us; the launch traced here: 73.6 us
  waiting for transfers between devices  31.3 us (42%)
  starting transfers between devices  24.1 us (33%)
  Pallas kernels  16.8 us (23%)
  between operations  1.38 us (2%)
    ppermute x10, waiting for transfers between devices, body(): lax.ppermute(v, 'dp', [(i, i ^ bit) for i in range(dp_size)])  18.4 us
    pallas_call x13, Pallas kernels, call(): pl.pallas_call(kernel, name=name, in_specs=[pl.BlockSpec(memory_space=p)...  16.8 us
    ppermute x10, starting transfers between devices, body(): lax.ppermute(v, 'dp', [(i, i ^ bit) for i in range(dp_size)])  13.6 us
    ppermute x4, waiting for transfers between devices, body(): lax.ppermute(v, 'rows', [(i, i ^ 2 << bit) for i in range(rows_size)])  8.52 us
    ppermute x3, starting transfers between devices, body(): lax.ppermute(v, 'rows', [(i, (i + 2 * k) % rows_size) for i in range(rows...  5.51 us
    ppermute x4, starting transfers between devices, body(): lax.ppermute(v, 'rows', [(i, i ^ 2 << bit) for i in range(rows_size)])  4.26 us
    ppermute x3, waiting for transfers between devices, body(): lax.ppermute(v, 'rows', [(i, (i + 2 * k) % rows_size) for i in range(rows...  4.05 us
  transfers between devices with their start and end apart: 20, of which 12 were waited for; matrix products, arithmetic and copies ran while one was open for 0% of the time, Pallas kernels for 10%

profile of v19, /device:TPU:0, one launch (start us, length us, event | category | flops | bytes accessed | tf_op | source)
XLA Modules:
  0.0 73.6 jit_solution(6490836613381111012)
XLA Ops:
  1.3 7.8 %forward_part.1 = (f32[256,1536]{1,0:T(8,128)S(1)}, f32[256,1536]{1,0:T(8,128)S(1)}, bf16[512,1536]{1,0:T(8,128)(2,1)S(1)}, bf16[512,1024]{1,0:T(8,128)(2,1)S(1)...) custom-call(s32[1]{0:T(128)S(6)} %copy.13.len_ref, ...), custom_call_target="tpu_custom_call" | custom-call | flops 99999997952 | bytes 65536 | tf_op jit(solution)/shard_map/forward_part/pallas_call | solution.py:411
  9.1 0.5 collective-permute-start
  9.6 0.0 copy-start.1
  9.6 0.0 copy-start.2
  9.7 2.6 %attention_part.1 = (f32[256,1024]{1,0:T(8,128)S(1)}, f32[256,1024]{1,0:T(8,128)S(1)}, bf16[512,1024]{1,0:T(8,128)(2,1)S(1)}) custom-call(f32[8,128]{1,0:T(8,128)S(1)} %get-tuple-element.63.inv_ref, bf16[512,1536]{1,0:T(8,128)(2,1)S(1)} %get-tuple-element.64.hid_ref, bf16[512,1024]{1,0:T(8,128)(2,1)S(1)} %get-tuple-element.65.dsilu_ref, ...), custom_call_target="tpu_custom_call" | custom-call | flops 99999997952 | bytes 65536 | tf_op jit(solution)/shard_map/attention_part/pallas_call | solution.py:411
  12.3 0.1 collective-permute-start.1
  12.4 0.3 collective-permute-done
  12.7 0.0 copy-done.1
  12.7 0.0 copy-done.2
  12.7 2.2 %events_part.1 = (f32[520,128]{1,0:T(8,128)S(1)}, f32[520,128]{1,0:T(8,128)S(1)}, f32[520,128]{1,0:T(8,128)S(1)}, f32[520,128]{1,0:T(8,128)S(1)}) custom-call(bf16[512,512]{1,0:T(8,128)(2,1)S(1)} %get-tuple-element.57.ev_ref, bf16[512,512]{1,0:T(8,128)(2,1)S(1)} %get-tuple-element.58.masked_ref, bf16[512,2048]{1,0:T(8,128)(2,1)S(1)} %get-tuple-element.59.win_ref, ...), custom_call_target="tpu_custom_call" | custom-call | flops 99999997952 | bytes 65536 | tf_op jit(solution)/shard_map/events_part/pallas_call | solution.py:411
  14.9 0.0 collective-permute-done.1
  15.0 0.3 first_sums.1
  15.3 2.9 %collective-permute-start.2 = (f32[2,64,1280]{2,1,0:T(8,128)S(1)}, f32[2,64,1280]{2,1,0:T(8,128)S(1)}, u32[]{:S(2)}, u32[]{:S(2)}) collective-permute-start(f32[2,64,1280]{2,1,0:T(8,128)S(1)} %get-tuple-element.77), channel_id=1, source_target_pairs={{0,8},{8,0},{16,24},{24,16},{1,9},{9,1},{17,25},{25,17},{2,10},{10... | collective-permute-start | bytes 1966088 | tf_op jit(solution)/shard_map/ppermute | solution.py:430
  18.2 1.5 %collective-permute-start.3 = (f32[2,64,1280]{2,1,0:T(8,128)S(1)}, f32[2,64,1280]{2,1,0:T(8,128)S(1)}, u32[]{:S(2)}, u32[]{:S(2)}) collective-permute-start(f32[2,64,1280]{2,1,0:T(8,128)S(1)} %get-tuple-element.79), channel_id=1, source_target_pairs={{0,16},{8,24},{16,0},{24,8},{1,17},{9,25},{17,1},{25,9},{2,18},{10... | collective-permute-start | bytes 1966088 | tf_op jit(solution)/shard_map/ppermute | solution.py:430
  19.7 1.6 %collective-permute-start.4 = (f32[520,128]{1,0:T(8,128)S(1)}, f32[520,128]{1,0:T(8,128)S(1)}, u32[]{:S(2)}, u32[]{:S(2)}) collective-permute-start(f32[520,128]{1,0:T(8,128)S(1)} %get-tuple-element.70), channel_id=1, source_target_pairs={{0,2},{1,3},{2,4},{3,5},{4,6},{5,7},{6,0},{7,1},{8,10},{9,11},{10,... | collective-permute-start | bytes 798728 | tf_op jit(solution)/shard_map/ppermute | solution.py:473
  21.3 2.6 %collective-permute-start.5 = (f32[520,128]{1,0:T(8,128)S(1)}, f32[520,128]{1,0:T(8,128)S(1)}, u32[]{:S(2)}, u32[]{:S(2)}) collective-permute-start(f32[520,128]{1,0:T(8,128)S(1)} %get-tuple-element.71), channel_id=1, source_target_pairs={{0,4},{1,5},{2,6},{3,7},{4,0},{5,1},{6,2},{7,3},{8,12},{9,13},{10,... | collective-permute-start | bytes 798728 | tf_op jit(solution)/shard_map/ppermute | solution.py:473
  23.9 1.3 %collective-permute-start.6 = (f32[520,128]{1,0:T(8,128)S(1)}, f32[520,128]{1,0:T(8,128)S(1)}, u32[]{:S(2)}, u32[]{:S(2)}) collective-permute-start(f32[520,128]{1,0:T(8,128)S(1)} %get-tuple-element.72), channel_id=1, source_target_pairs={{0,6},{1,7},{2,0},{3,1},{4,2},{5,3},{6,4},{7,5},{8,14},{9,15},{10,... | collective-permute-start | bytes 798728 | tf_op jit(solution)/shard_map/ppermute | solution.py:473
  25.3 8.0 %collective-permute-done.2.from_x_ref = f32[2,64,1280]{2,1,0:T(8,128)S(1)} collective-permute-done((f32[2,64,1280]{2,1,0:T(8,128)S(1)}, f32[2,64,1280]{2,1,0:T(8,128)S(1)}, u32[]{:S(2)}, u32[]{:S(2)}) %collective-permute-start.2) | collective-permute-done | bytes 655392 | tf_op jit(solution)/shard_map/ppermute | solution.py:430
  33.3 1.5 %collective-permute-done.3.from_y_ref = f32[2,64,1280]{2,1,0:T(8,128)S(1)} collective-permute-done((f32[2,64,1280]{2,1,0:T(8,128)S(1)}, f32[2,64,1280]{2,1,0:T(8,128)S(1)}, u32[]{:S(2)}, u32[]{:S(2)}) %collective-permute-start.3) | collective-permute-done | bytes 655392 | tf_op jit(solution)/shard_map/ppermute | solution.py:430
  34.7 0.1 second_sums.1
  34.9 1.6 %collective-permute-start.7 = (f32[64,1280]{1,0:T(8,128)S(1)}, f32[64,1280]{1,0:T(8,128)S(1)}, u32[]{:S(2)}, u32[]{:S(2)}) collective-permute-start(f32[64,1280]{1,0:T(8,128)S(1)} %get-tuple-element.81), channel_id=1, source_target_pairs={{0,16},{8,24},{16,0},{24,8},{1,17},{9,25},{17,1},{25,9},{2,18},{10... | collective-permute-start | bytes 983048 | tf_op jit(solution)/shard_map/ppermute | solution.py:430
  36.4 0.5 collective-permute-start.8
  37.0 0.0 collective-permute-done.4.refs_1_
  37.0 4.0 %collective-permute-done.5.refs_2_ = f32[520,128]{1,0:T(8,128)S(1)} collective-permute-done((f32[520,128]{1,0:T(8,128)S(1)}, f32[520,128]{1,0:T(8,128)S(1)}, u32[]{:S(2)}, u32[]{:S(2)}) %collective-permute-start.5) | collective-permute-done | bytes 266272 | tf_op jit(solution)/shard_map/ppermute | solution.py:473
  41.0 0.0 collective-permute-done.6.refs_3_
  41.0 0.1 by_part.1
  41.1 2.4 %collective-permute-done.7 = f32[64,1280]{1,0:T(8,128)S(1)} collective-permute-done((f32[64,1280]{1,0:T(8,128)S(1)}, f32[64,1280]{1,0:T(8,128)S(1)}, u32[]{:S(2)}, u32[]{:S(2)}) %collective-permute-start.7) | collective-permute-done | bytes 327712 | tf_op jit(solution)/shard_map/ppermute | solution.py:430
  43.5 1.2 %collective-permute-done.8 = f32[64,1280]{1,0:T(8,128)S(1)} collective-permute-done((f32[64,1280]{1,0:T(8,128)S(1)}, f32[64,1280]{1,0:T(8,128)S(1)}, u32[]{:S(2)}, u32[]{:S(2)}) %collective-permute-start.8) | collective-permute-done | bytes 327712 | tf_op jit(solution)/shard_map/ppermute | solution.py:430
  44.8 0.1 chip_sums.3
  44.9 2.6 %collective-permute-start.9 = (f32[2,16,1280]{2,1,0:T(8,128)S(1)}, f32[2,16,1280]{2,1,0:T(8,128)S(1)}, u32[]{:S(2)}, u32[]{:S(2)}) collective-permute-start(f32[2,16,1280]{2,1,0:T(8,128)S(1)} %get-tuple-element.91), channel_id=1, source_target_pairs={{0,2},{1,3},{2,0},{3,1},{4,6},{5,7},{6,4},{7,5},{8,10},{9,11},{10,... | collective-permute-start | bytes 491528 | tf_op jit(solution)/shard_map/ppermute | solution.py:490
  47.5 0.5 collective-permute-start.12
  48.0 0.5 collective-permute-start.13
  48.5 2.5 %collective-permute-start.14 = (f32[520,128]{1,0:T(8,128)S(1)}, f32[520,128]{1,0:T(8,128)S(1)}, u32[]{:S(2)}, u32[]{:S(2)}) collective-permute-start(f32[520,128]{1,0:T(8,128)S(1)} %get-tuple-element.87), channel_id=1, source_target_pairs={{0,24},{8,16},{16,8},{24,0},{1,25},{9,17},{17,9},{25,1},{2,26},{10... | collective-permute-start | bytes 798728 | tf_op jit(solution)/shard_map/ppermute | solution.py:430
  51.0 0.1 collective-permute-start.11
  51.0 0.8 %collective-permute-done.9.recv_in = f32[2,16,1280]{2,1,0:T(8,128)S(1)} collective-permute-done((f32[2,16,1280]{2,1,0:T(8,128)S(1)}, f32[2,16,1280]{2,1,0:T(8,128)S(1)}, u32[]{:S(2)}, u32[]{:S(2)}) %collective-permute-start.9) | collective-permute-done | bytes 163872 | tf_op jit(solution)/shard_map/ppermute | solution.py:490
  51.9 1.2 %collective-permute-start.10 = (f32[1,16,1280]{2,1,0:T(8,128)S(1)}, f32[1,16,1280]{2,1,0:T(8,128)S(1)}, u32[]{:S(2)}, u32[]{:S(2)}) collective-permute-start(f32[1,16,1280]{2,1,0:T(8,128)S(1)} %get-tuple-element.93), channel_id=1, source_target_pairs={{0,4},{1,5},{2,6},{3,7},{4,0},{5,1},{6,2},{7,3},{8,12},{9,13},{10,... | collective-permute-start | bytes 245768 | tf_op jit(solution)/shard_map/ppermute | solution.py:490
  53.1 5.4 %collective-permute-done.11.recv_in = f32[2,16,1280]{2,1,0:T(8,128)S(1)} collective-permute-done((f32[2,16,1280]{2,1,0:T(8,128)S(1)}, f32[2,16,1280]{2,1,0:T(8,128)S(1)}, u32[]{:S(2)}, u32[]{:S(2)}) %collective-permute-start.11) | collective-permute-done | bytes 163872 | tf_op jit(solution)/shard_map/ppermute | solution.py:490
  58.6 0.3 collective-permute-start.15
  58.9 0.0 collective-permute-done.12.refs_1_
  58.9 2.6 %collective-permute-done.13.refs_2_ = f32[520,128]{1,0:T(8,128)S(1)} collective-permute-done((f32[520,128]{1,0:T(8,128)S(1)}, f32[520,128]{1,0:T(8,128)S(1)}, u32[]{:S(2)}, u32[]{:S(2)}) %collective-permute-start.13) | collective-permute-done | bytes 266272 | tf_op jit(solution)/shard_map/ppermute | solution.py:430
  61.5 0.0 collective-permute-done.14.refs_3_
  61.5 0.1 by_core.1
  61.5 0.1 collective-permute-start.19
  61.6 0.0 copy-start
  61.6 0.0 copy-start.3
  61.6 0.0 collective-permute-done.10.recv_a_ref
  61.7 2.3 %collective-permute-done.15.recv_b_ref = f32[1,16,1280]{2,1,0:T(8,128)S(1)} collective-permute-done((f32[1,16,1280]{2,1,0:T(8,128)S(1)}, f32[1,16,1280]{2,1,0:T(8,128)S(1)}, u32[]{:S(2)}, u32[]{:S(2)}) %collective-permute-start.15) | collective-permute-done | bytes 81952 | tf_op jit(solution)/shard_map/ppermute | solution.py:490
  64.0 0.5 collective-permute-start.18
  64.5 1.5 %collective-permute-start.17 = (f32[16,2560]{1,0:T(8,128)S(1)}, f32[16,2560]{1,0:T(8,128)S(1)}, u32[]{:S(2)}, u32[]{:S(2)}) collective-permute-start(f32[16,2560]{1,0:T(8,128)S(1)} %total.1.refs_0_), channel_id=1, source_target_pairs={{0,16},{8,24},{16,0},{24,8},{1,17},{9,25},{17,1},{25,9},{2,18},{10... | collective-permute-start | bytes 491528 | tf_op jit(solution)/shard_map/ppermute | solution.py:430
  66.0 1.5 %collective-permute-start.16 = (f32[16,2560]{1,0:T(8,128)S(1)}, f32[16,2560]{1,0:T(8,128)S(1)}, u32[]{:S(2)}, u32[]{:S(2)}) collective-permute-start(f32[16,2560]{1,0:T(8,128)S(1)} %total.1.refs_0_), channel_id=1, source_target_pairs={{0,8},{8,0},{16,24},{24,16},{1,9},{9,1},{17,25},{25,17},{2,10},{10... | collective-permute-start | bytes 491528 | tf_op jit(solution)/shard_map/ppermute | solution.py:430
  67.5 0.0 collective-permute-done.19.recv_ref
  67.5 0.0 copy-done
  67.5 0.0 copy-done.3
  67.6 2.5 %table_part.1 = (f32[512,512]{1,0:T(8,128)}, f32[512]{0:T(512)}) custom-call(f32[1056,128]{1,0:T(8,128)S(1)} %get-tuple-element.99.keep_ref, f32[1056,128]{1,0:T(8,128)S(1)} %collective-permute-done.19.recv_ref, f32[512,512]{1,0:T(8,128)S(1)} %copy-done, f32[512]{0:T(512)S(1)} %copy-done.3), custom_call_target="tpu_custom_call" | custom-call | flops 1000000000 | bytes 65536 | tf_op jit(solution)/shard_map/table_part/pallas_call | solution.py:411
  70.0 1.0 %collective-permute-done.18.refs_3_ = f32[16,2560]{1,0:T(8,128)S(1)} collective-permute-done((f32[16,2560]{1,0:T(8,128)S(1)}, f32[16,2560]{1,0:T(8,128)S(1)}, u32[]{:S(2)}, u32[]{:S(2)}) %collective-permute-start.18) | collective-permute-done | bytes 163872 | tf_op jit(solution)/shard_map/ppermute | solution.py:430
  71.1 1.7 %collective-permute-done.17.refs_2_ = f32[16,2560]{1,0:T(8,128)S(1)} collective-permute-done((f32[16,2560]{1,0:T(8,128)S(1)}, f32[16,2560]{1,0:T(8,128)S(1)}, u32[]{:S(2)}, u32[]{:S(2)}) %collective-permute-start.17) | collective-permute-done | bytes 163872 | tf_op jit(solution)/shard_map/ppermute | solution.py:430
  72.7 0.0 collective-permute-done.16.refs_1_
  72.7 0.9 %gather.1 = (f32[4,16,2048]{2,1,0:T(8,128)}, f32[4,16,512]{2,1,0:T(8,128)}) custom-call(f32[16,2560]{1,0:T(8,128)S(1)} %total.1.refs_0_, f32[16,2560]{1,0:T(8,128)S(1)} %collective-permute-done.16.refs_1_, f32[16,2560]{1,0:T(8,128)S(1)} %collective-permute-done.17.refs_2_, f32[16,2560]{1,0:T(8,128)S(1)} %collective-permute-done.18.refs_3_), custom_call_target="tpu_custom_call" | custom-call | flops 1000000000 | bytes 65536 | tf_op jit(solution)/shard_map/gather/pallas_call | solution.py:411
  (3 shorter events, 0.1 us)
Async XLA Ops:
  9.1 3.6 %collective-permute-start = (f32[256,1536]{1,0:T(8,128)S(1)}, f32[256,1536]{1,0:T(8,128)S(1)}, u32[]{:S(2)}, u32[]{:S(2)}) collective-permute-start(f32[256,1536]{1,0:T(8,128)S(1)} %get-tuple-element.61), channel_id=1, source_target_pairs={{0,1},{1,0},{2,3},{3,2},{4,5},{5,4},{6,7},{7,6},{8,9},{9,8},{10,11... | collective-permute-start | bytes 4718600 | tf_op jit(solution)/shard_map/ppermute | solution.py:459
  9.6 3.0 %copy-start.1 = (s32[1,32,16]{1,2,0:T(8,128)S(1)}, s32[1,32,16]{1,2,0:T(8,128)}, u32[]{:S(2)}) copy-start(s32[1,32,16]{1,2,0:T(8,128)} %param.14) | copy-start | bytes 6148
  9.6 3.0 %copy-start.2 = (s32[1,512]{1,0:T(1,128)S(1)}, s32[1,512]{1,0:T(1,128)}, u32[]{:S(2)}) copy-start(s32[1,512]{1,0:T(1,128)} %slot_ref.1) | copy-start | bytes 6148
  12.3 2.7 %collective-permute-start.1 = (f32[256,1024]{1,0:T(8,128)S(1)}, f32[256,1024]{1,0:T(8,128)S(1)}, u32[]{:S(2)}, u32[]{:S(2)}) collective-permute-start(f32[256,1024]{1,0:T(8,128)S(1)} %get-tuple-element.75), channel_id=1, source_target_pairs={{0,1},{1,0},{2,3},{3,2},{4,5},{5,4},{6,7},{7,6},{8,9},{9,8},{10,11... | collective-permute-start | bytes 3145736 | tf_op jit(solution)/shard_map/ppermute | solution.py:464
  15.3 18.0 %collective-permute-start.2 = (f32[2,64,1280]{2,1,0:T(8,128)S(1)}, f32[2,64,1280]{2,1,0:T(8,128)S(1)}, u32[]{:S(2)}, u32[]{:S(2)}) collective-permute-start(f32[2,64,1280]{2,1,0:T(8,128)S(1)} %get-tuple-element.77), channel_id=1, source_target_pairs={{0,8},{8,0},{16,24},{24,16},{1,9},{9,1},{17,25},{25,17},{2,10},{10... | collective-permute-start | bytes 1966088 | tf_op jit(solution)/shard_map/ppermute | solution.py:430
  18.2 16.5 %collective-permute-start.3 = (f32[2,64,1280]{2,1,0:T(8,128)S(1)}, f32[2,64,1280]{2,1,0:T(8,128)S(1)}, u32[]{:S(2)}, u32[]{:S(2)}) collective-permute-start(f32[2,64,1280]{2,1,0:T(8,128)S(1)} %get-tuple-element.79), channel_id=1, source_target_pairs={{0,16},{8,24},{16,0},{24,8},{1,17},{9,25},{17,1},{25,9},{2,18},{10... | collective-permute-start | bytes 1966088 | tf_op jit(solution)/shard_map/ppermute | solution.py:430
  19.7 17.2 %collective-permute-start.4 = (f32[520,128]{1,0:T(8,128)S(1)}, f32[520,128]{1,0:T(8,128)S(1)}, u32[]{:S(2)}, u32[]{:S(2)}) collective-permute-start(f32[520,128]{1,0:T(8,128)S(1)} %get-tuple-element.70), channel_id=1, source_target_pairs={{0,2},{1,3},{2,4},{3,5},{4,6},{5,7},{6,0},{7,1},{8,10},{9,11},{10,... | collective-permute-start | bytes 798728 | tf_op jit(solution)/shard_map/ppermute | solution.py:473
  21.3 19.7 %collective-permute-start.5 = (f32[520,128]{1,0:T(8,128)S(1)}, f32[520,128]{1,0:T(8,128)S(1)}, u32[]{:S(2)}, u32[]{:S(2)}) collective-permute-start(f32[520,128]{1,0:T(8,128)S(1)} %get-tuple-element.71), channel_id=1, source_target_pairs={{0,4},{1,5},{2,6},{3,7},{4,0},{5,1},{6,2},{7,3},{8,12},{9,13},{10,... | collective-permute-start | bytes 798728 | tf_op jit(solution)/shard_map/ppermute | solution.py:473
  23.9 17.1 %collective-permute-start.6 = (f32[520,128]{1,0:T(8,128)S(1)}, f32[520,128]{1,0:T(8,128)S(1)}, u32[]{:S(2)}, u32[]{:S(2)}) collective-permute-start(f32[520,128]{1,0:T(8,128)S(1)} %get-tuple-element.72), channel_id=1, source_target_pairs={{0,6},{1,7},{2,0},{3,1},{4,2},{5,3},{6,4},{7,5},{8,14},{9,15},{10,... | collective-permute-start | bytes 798728 | tf_op jit(solution)/shard_map/ppermute | solution.py:473
  34.9 8.7 %collective-permute-start.7 = (f32[64,1280]{1,0:T(8,128)S(1)}, f32[64,1280]{1,0:T(8,128)S(1)}, u32[]{:S(2)}, u32[]{:S(2)}) collective-permute-start(f32[64,1280]{1,0:T(8,128)S(1)} %get-tuple-element.81), channel_id=1, source_target_pairs={{0,16},{8,24},{16,0},{24,8},{1,17},{9,25},{17,1},{25,9},{2,18},{10... | collective-permute-start | bytes 983048 | tf_op jit(solution)/shard_map/ppermute | solution.py:430
  36.4 8.3 %collective-permute-start.8 = (f32[64,1280]{1,0:T(8,128)S(1)}, f32[64,1280]{1,0:T(8,128)S(1)}, u32[]{:S(2)}, u32[]{:S(2)}) collective-permute-start(f32[64,1280]{1,0:T(8,128)S(1)} %get-tuple-element.82), channel_id=1, source_target_pairs={{0,8},{8,0},{16,24},{24,16},{1,9},{9,1},{17,25},{25,17},{2,10},{10... | collective-permute-start | bytes 983048 | tf_op jit(solution)/shard_map/ppermute | solution.py:430
  44.9 7.0 %collective-permute-start.9 = (f32[2,16,1280]{2,1,0:T(8,128)S(1)}, f32[2,16,1280]{2,1,0:T(8,128)S(1)}, u32[]{:S(2)}, u32[]{:S(2)}) collective-permute-start(f32[2,16,1280]{2,1,0:T(8,128)S(1)} %get-tuple-element.91), channel_id=1, source_target_pairs={{0,2},{1,3},{2,0},{3,1},{4,6},{5,7},{6,4},{7,5},{8,10},{9,11},{10,... | collective-permute-start | bytes 491528 | tf_op jit(solution)/shard_map/ppermute | solution.py:490
  47.5 11.4 %collective-permute-start.12 = (f32[520,128]{1,0:T(8,128)S(1)}, f32[520,128]{1,0:T(8,128)S(1)}, u32[]{:S(2)}, u32[]{:S(2)}) collective-permute-start(f32[520,128]{1,0:T(8,128)S(1)} %get-tuple-element.85), channel_id=1, source_target_pairs={{0,8},{8,0},{16,24},{24,16},{1,9},{9,1},{17,25},{25,17},{2,10},{10... | collective-permute-start | bytes 798728 | tf_op jit(solution)/shard_map/ppermute | solution.py:430
  48.0 13.5 %collective-permute-start.13 = (f32[520,128]{1,0:T(8,128)S(1)}, f32[520,128]{1,0:T(8,128)S(1)}, u32[]{:S(2)}, u32[]{:S(2)}) collective-permute-start(f32[520,128]{1,0:T(8,128)S(1)} %get-tuple-element.86), channel_id=1, source_target_pairs={{0,16},{8,24},{16,0},{24,8},{1,17},{9,25},{17,1},{25,9},{2,18},{10... | collective-permute-start | bytes 798728 | tf_op jit(solution)/shard_map/ppermute | solution.py:430
  48.5 13.0 %collective-permute-start.14 = (f32[520,128]{1,0:T(8,128)S(1)}, f32[520,128]{1,0:T(8,128)S(1)}, u32[]{:S(2)}, u32[]{:S(2)}) collective-permute-start(f32[520,128]{1,0:T(8,128)S(1)} %get-tuple-element.87), channel_id=1, source_target_pairs={{0,24},{8,16},{16,8},{24,0},{1,25},{9,17},{17,9},{25,1},{2,26},{10... | collective-permute-start | bytes 798728 | tf_op jit(solution)/shard_map/ppermute | solution.py:430
  51.0 7.6 %collective-permute-start.11 = (f32[2,16,1280]{2,1,0:T(8,128)S(1)}, f32[2,16,1280]{2,1,0:T(8,128)S(1)}, u32[]{:S(2)}, u32[]{:S(2)}) collective-permute-start(f32[2,16,1280]{2,1,0:T(8,128)S(1)} %get-tuple-element.96), channel_id=1, source_target_pairs={{0,2},{1,3},{2,0},{3,1},{4,6},{5,7},{6,4},{7,5},{8,10},{9,11},{10,... | collective-permute-start | bytes 491528 | tf_op jit(solution)/shard_map/ppermute | solution.py:490
  51.9 9.8 %collective-permute-start.10 = (f32[1,16,1280]{2,1,0:T(8,128)S(1)}, f32[1,16,1280]{2,1,0:T(8,128)S(1)}, u32[]{:S(2)}, u32[]{:S(2)}) collective-permute-start(f32[1,16,1280]{2,1,0:T(8,128)S(1)} %get-tuple-element.93), channel_id=1, source_target_pairs={{0,4},{1,5},{2,6},{3,7},{4,0},{5,1},{6,2},{7,3},{8,12},{9,13},{10,... | collective-permute-start | bytes 245768 | tf_op jit(solution)/shard_map/ppermute | solution.py:490
  58.6 5.4 %collective-permute-start.15 = (f32[1,16,1280]{2,1,0:T(8,128)S(1)}, f32[1,16,1280]{2,1,0:T(8,128)S(1)}, u32[]{:S(2)}, u32[]{:S(2)}) collective-permute-start(f32[1,16,1280]{2,1,0:T(8,128)S(1)} %get-tuple-element.102), channel_id=1, source_target_pairs={{0,4},{1,5},{2,6},{3,7},{4,0},{5,1},{6,2},{7,3},{8,12},{9,13},{10,... | collective-permute-start | bytes 245768 | tf_op jit(solution)/shard_map/ppermute | solution.py:490
  61.5 6.0 %collective-permute-start.19 = (f32[1056,128]{1,0:T(8,128)S(1)}, f32[1056,128]{1,0:T(8,128)S(1)}, u32[]{:S(2)}, u32[]{:S(2)}) collective-permute-start(f32[1056,128]{1,0:T(8,128)S(1)} %get-tuple-element.100), channel_id=1, source_target_pairs={{0,1},{1,0},{2,3},{3,2},{4,5},{5,4},{6,7},{7,6},{8,9},{9,8},{10,11... | collective-permute-start | bytes 1622024 | tf_op jit(solution)/shard_map/ppermute | solution.py:512
  61.6 5.9 %copy-start = (f32[512,512]{1,0:T(8,128)S(1)}, f32[512,512]{1,0:T(8,128)}, u32[]{:S(2)}) copy-start(f32[512,512]{1,0:T(8,128)} %table_ref.1) | copy-start | bytes 3145732
  61.6 5.9 %copy-start.3 = (f32[512]{0:T(512)S(1)}, f32[512]{0:T(512)}, u32[]{:S(2)}) copy-start(f32[512]{0:T(512)} %accum_ref.1) | copy-start | bytes 6148
  64.0 7.1 %collective-permute-start.18 = (f32[16,2560]{1,0:T(8,128)S(1)}, f32[16,2560]{1,0:T(8,128)S(1)}, u32[]{:S(2)}, u32[]{:S(2)}) collective-permute-start(f32[16,2560]{1,0:T(8,128)S(1)} %total.1.refs_0_), channel_id=1, source_target_pairs={{0,24},{8,16},{16,8},{24,0},{1,25},{9,17},{17,9},{25,1},{2,26},{10... | collective-permute-start | bytes 491528 | tf_op jit(solution)/shard_map/ppermute | solution.py:430
  64.5 8.2 %collective-permute-start.17 = (f32[16,2560]{1,0:T(8,128)S(1)}, f32[16,2560]{1,0:T(8,128)S(1)}, u32[]{:S(2)}, u32[]{:S(2)}) collective-permute-start(f32[16,2560]{1,0:T(8,128)S(1)} %total.1.refs_0_), channel_id=1, source_target_pairs={{0,16},{8,24},{16,0},{24,8},{1,17},{9,25},{17,1},{25,9},{2,18},{10... | collective-permute-start | bytes 491528 | tf_op jit(solution)/shard_map/ppermute | solution.py:430
  66.0 6.7 %collective-permute-start.16 = (f32[16,2560]{1,0:T(8,128)S(1)}, f32[16,2560]{1,0:T(8,128)S(1)}, u32[]{:S(2)}, u32[]{:S(2)}) collective-permute-start(f32[16,2560]{1,0:T(8,128)S(1)} %total.1.refs_0_), channel_id=1, source_target_pairs={{0,8},{8,0},{16,24},{24,16},{1,9},{9,1},{17,25},{25,17},{2,10},{10... | collective-permute-start | bytes 491528 | tf_op jit(solution)/shard_map/ppermute | solution.py:430
